TPU v7x, 32 devices: a whole 2x2x4 slice. The times are simulated.
32 devices in a mesh: groups: 2 (over y), ctx: 16 (over z, x, core).
Axes of the slice: x: 2, y: 2, z: 4, core: 2. Of those that a mesh axis runs over, the one named last changes fastest.
Arguments:
- normed_input: bfloat16 [2048, 8192], P(('groups', 'ctx')), parts along dimension 0, may hold values from -5 to 5
- query_base: bfloat16 [2048, 4096], P(('groups', 'ctx')), parts along dimension 0, may hold values from -6 to 6
- key_base: bfloat16 [2048, 512], P(('groups', 'ctx')), parts along dimension 0, may hold values from -6 to 6
- value_base: bfloat16 [2048, 512], P(('groups', 'ctx')), parts along dimension 0, may hold values from -4 to 4
- adapter_pool: bfloat16 [16, 2686976], P('ctx'), may hold values from -1 to 1
- stretch_adapter: int32 [4], P('groups'), parts along dimension 0, may hold values from 0 to 15
- adapter_owner: int32 [16], replicated, may hold values from 0 to 15, each once
Outputs:
- attended: bfloat16 [2048, 4096], P(('groups', 'ctx')), parts along dimension 0
- out_delta: bfloat16 [2048, 8192], P(('groups', 'ctx')), parts along dimension 0
There are 2 independent parts, one for each index of `groups`. A program takes and returns all parts, laid end to end along the dimension named above; an argument that names none is the same for every part. Nothing has to cross between parts.
All inputs are finite; a program needn't handle non-finite values.
Results may differ from a plain program's by a relative error of at most 0.018.
Values may be sent and summed in bfloat16 or wider, within the bound.
No kernel may reach another device: no remote copies, remote signals or barrier semaphores. Data moves between devices by JAX's collectives and lax.ppermute only.
A program may use at most 192 MiB of HBM per device.

v0:
```python
from functools import partial
import math

import jax
import jax.numpy as jnp
from jax import lax
from jax.experimental import pallas as pl
from jax.experimental.pallas import tpu as pltpu
from jax.sharding import PartitionSpec as P

D = 8192
QH = 32
KEYVALUE_HEADS = 4
HEAD_SIZE = 128
ADAPTER_RANK = 64
BLOCK_TOKENS = 512
QKV_POOL = 1900544


adapter_scale = 2.0
rope_base = 500000.0
mask_floor = -1e30


def from_partner(block, axis, apart):
    count = lax.axis_size(axis)
    route = []
    for low in range(count):
        high = low | 1 << apart
        if high != low and high < count:
            route += [(low, high), (high, low)]
    return lax.ppermute(block, axis, route)


def rotate(delta, token_positions, heads):
    half_dim = HEAD_SIZE // 2
    frequency = rope_base ** (-(jnp.arange(half_dim, dtype=jnp.float32) * 2.0) / HEAD_SIZE)
    angle = token_positions.astype(jnp.float32)[:, None] * frequency[None, :]
    cosine = jnp.cos(angle)[:, None, :]
    sine_part = jnp.sin(angle)[:, None, :]
    shaped = delta.reshape(delta.shape[0], heads, HEAD_SIZE)
    first_half = shaped[..., :half_dim]
    second_half = shaped[..., half_dim:]
    joined = jnp.concatenate(
        [
            first_half * cosine - second_half * sine_part,
            second_half * cosine + first_half * sine_part,
        ],
        -1,
    )
    return joined.reshape(delta.shape[0], heads * HEAD_SIZE)


def project_heads(
    narrow_product, query_row_block, key_row_block, value_row_block, upper_part, token_positions
):
    query_up_weight = upper_part[: ADAPTER_RANK * QH * HEAD_SIZE].reshape(
        ADAPTER_RANK, QH * HEAD_SIZE
    )
    keyvalue_up_weight = upper_part[ADAPTER_RANK * QH * HEAD_SIZE :].reshape(
        ADAPTER_RANK, 2 * KEYVALUE_HEADS * HEAD_SIZE
    )
    query_correction = adapter_scale * jnp.dot(
        narrow_product[:, :ADAPTER_RANK], query_up_weight, preferred_element_type=jnp.float32
    )
    key_correction = adapter_scale * jnp.dot(
        narrow_product[:, ADAPTER_RANK : 2 * ADAPTER_RANK],
        keyvalue_up_weight[:, : KEYVALUE_HEADS * HEAD_SIZE],
        preferred_element_type=jnp.float32,
    )
    value_correction = adapter_scale * jnp.dot(
        narrow_product[:, 2 * ADAPTER_RANK :],
        keyvalue_up_weight[:, KEYVALUE_HEADS * HEAD_SIZE :],
        preferred_element_type=jnp.float32,
    )
    queries = (
        query_row_block.astype(jnp.float32) + rotate(query_correction, token_positions, QH)
    ).astype(jnp.bfloat16)
    new_keys = (
        key_row_block.astype(jnp.float32) + rotate(key_correction, token_positions, KEYVALUE_HEADS)
    ).astype(jnp.bfloat16)
    new_values = (value_row_block.astype(jnp.float32) + value_correction).astype(jnp.bfloat16)
    return (queries, new_keys, new_values)


def output_delta(attended_rows, out_part):
    down_out = out_part[: QH * HEAD_SIZE * ADAPTER_RANK].reshape(QH * HEAD_SIZE, ADAPTER_RANK)
    raised_output = out_part[QH * HEAD_SIZE * ADAPTER_RANK :].reshape(ADAPTER_RANK, D)
    narrow_product = jnp.dot(attended_rows, down_out, preferred_element_type=jnp.float32).astype(
        jnp.bfloat16
    )
    return (
        adapter_scale * jnp.dot(narrow_product, raised_output, preferred_element_type=jnp.float32)
    ).astype(jnp.bfloat16)


def head_major(query_row_block):
    count_rows = query_row_block.shape[0]
    group_size = QH // KEYVALUE_HEADS
    return (
        query_row_block.reshape(count_rows, KEYVALUE_HEADS, group_size, HEAD_SIZE)
        .transpose(1, 2, 0, 3)
        .reshape(KEYVALUE_HEADS, group_size * count_rows, HEAD_SIZE)
    )


def row_major(head_rows, count_rows):
    group_size = QH // KEYVALUE_HEADS
    return (
        head_rows.reshape(KEYVALUE_HEADS, group_size, count_rows, HEAD_SIZE)
        .transpose(2, 0, 1, 3)
        .reshape(count_rows, QH * HEAD_SIZE)
    )


def online_update(current, queries, query_pos, key_slice, value_slice, key_start):
    run_max, run_sum, run_acc = current
    scores = jnp.einsum(
        "hqd,khd->hqk", queries, key_slice, preferred_element_type=jnp.float32
    ) * HEAD_SIZE ** (-0.5)
    key_pos = key_start + jnp.arange(key_slice.shape[0], dtype=jnp.int32)
    allowed = (query_pos[:, None] >= key_pos[None, :])[None]
    new_max = jnp.maximum(run_max, jnp.max(jnp.where(allowed, scores, mask_floor), axis=-1))
    weights = jnp.where(allowed, jnp.exp(scores - new_max[..., None]), 0.0)
    rescale = jnp.exp(run_max - new_max)
    new_sum = run_sum * rescale + jnp.sum(weights, axis=-1)
    new_acc = run_acc * rescale[..., None] + jnp.einsum(
        "hqk,khd->hqd",
        weights.astype(jnp.bfloat16),
        value_slice,
        preferred_element_type=jnp.float32,
    )
    return (new_max, new_sum, new_acc)


def unchanged(current):
    return current


def fold_keys(carry_state, shard_part, prepared):
    key_row_block, value_row_block = shard_part
    key_count = key_row_block.shape[0]
    sub_width = math.gcd(key_count, 1024)
    key_heads = key_row_block.reshape(key_count // sub_width, sub_width, KEYVALUE_HEADS, HEAD_SIZE)
    value_heads = value_row_block.reshape(
        key_count // sub_width, sub_width, KEYVALUE_HEADS, HEAD_SIZE
    )

    def one_step(sub_index, carried):
        key_start = sub_index * sub_width
        key_slice = lax.dynamic_index_in_dim(key_heads, sub_index, 0, keepdims=False)
        value_slice = lax.dynamic_index_in_dim(value_heads, sub_index, 0, keepdims=False)
        updated = []
        for (queries, query_pos), running in zip(prepared, carried):
            advance = partial(
                online_update,
                queries=queries,
                query_pos=query_pos,
                key_slice=key_slice,
                value_slice=value_slice,
                key_start=key_start,
            )
            updated.append(lax.cond(key_start <= jnp.max(query_pos), advance, unchanged, running))
        return tuple(updated)

    return lax.fori_loop(0, key_count // sub_width, one_step, carry_state)


def finish_block(result, count_rows):
    run_max, run_sum, run_acc = result
    divisor = jnp.where(run_sum > 0.0, run_sum, 1.0)
    return row_major(run_acc / divisor[..., None], count_rows).astype(jnp.bfloat16)


def spread_shards(
    normed_input, query_base, key_base, value_base, adapter_pool, stretch_adapter, adapter_owner
):
    cycle_size = lax.axis_size("ctx")
    my_index = lax.axis_index("ctx")
    tok_rows = normed_input.shape[0]
    token_positions = my_index * tok_rows + jnp.arange(tok_rows, dtype=jnp.int32)
    device_ids = jnp.arange(cycle_size, dtype=jnp.int32)
    stretch_of = device_ids * tok_rows // BLOCK_TOKENS
    stretch_ids = jnp.arange(stretch_adapter.shape[0], dtype=jnp.int32)
    adapter_of = jnp.sum(
        jnp.where(stretch_of[:, None] == stretch_ids[None, :], stretch_adapter[None, :], 0), axis=1
    )
    adapter_ids = jnp.arange(adapter_owner.shape[0], dtype=jnp.int32)
    slot_of = jnp.sum(
        jnp.where(adapter_of[:, None] == adapter_ids[None, :], adapter_owner[None, :], 0), axis=1
    )
    down_size = 3 * ADAPTER_RANK * D
    group_count = BLOCK_TOKENS // tok_rows
    levels = group_count.bit_length() - 1
    local_index = my_index % group_count
    col_width = D // group_count
    piece_len = down_size // (group_count * cycle_size)
    pool_rows = adapter_pool.shape[0]
    down_shaped = adapter_pool[:, :down_size].reshape(pool_rows, group_count, cycle_size, piece_len)
    spread_down = lax.all_to_all(down_shaped, "ctx", split_axis=2, concat_axis=0, tiled=True)
    flat_down = spread_down.reshape(-1, piece_len)
    wanted = jnp.take(flat_down, slot_of * group_count + device_ids % group_count, axis=0)[
        :, None, :
    ]
    down_slice = lax.all_to_all(wanted, "ctx", split_axis=0, concat_axis=1, tiled=True).reshape(
        col_width, 3 * ADAPTER_RANK
    )
    spread_rest = lax.all_to_all(
        adapter_pool[:, down_size:], "ctx", split_axis=1, concat_axis=0, tiled=True
    )
    rest_row = lax.all_to_all(
        jnp.take(spread_rest, slot_of, axis=0), "ctx", split_axis=0, concat_axis=1, tiled=True
    )[0]
    upper_part = rest_row[: QKV_POOL - down_size]
    out_part = rest_row[QKV_POOL - down_size :]
    pieces = normed_input.reshape(tok_rows, group_count, col_width)
    slice_order = jnp.bitwise_xor(local_index, jnp.arange(group_count, dtype=jnp.int32))
    moving = jnp.take(pieces, slice_order, axis=1).transpose(1, 0, 2)
    for level in range(levels):
        shaped = moving.reshape(group_count >> level + 1, 2, 1 << level, tok_rows, col_width)
        arrived = from_partner(shaped[:, 1], "ctx", level)
        moving = jnp.stack([shaped[:, 0], arrived], 1).reshape(group_count, tok_rows, col_width)
    partial_rows = jnp.dot(
        moving.reshape(group_count * tok_rows, col_width),
        down_slice,
        preferred_element_type=jnp.float32,
    ).reshape(group_count, tok_rows, 3 * ADAPTER_RANK)
    for level in reversed(range(levels)):
        halves = partial_rows.reshape(2, partial_rows.shape[0] // 2, tok_rows, 3 * ADAPTER_RANK)
        partial_rows = halves[0] + from_partner(
            halves[1].astype(jnp.bfloat16), "ctx", level
        ).astype(jnp.float32)
    narrow_product = partial_rows[0].astype(jnp.bfloat16)
    queries, new_keys, new_values = project_heads(
        narrow_product, query_base, key_base, value_base, upper_part, token_positions
    )
    group_size = QH // KEYVALUE_HEADS
    blocks = [(queries, token_positions)]
    prepared = [
        (head_major(block_q), jnp.tile(block_pos, group_size)) for block_q, block_pos in blocks
    ]
    initial = tuple(
        (
            (
                jnp.full((KEYVALUE_HEADS, head_q.shape[1]), mask_floor, jnp.float32),
                jnp.zeros((KEYVALUE_HEADS, head_q.shape[1]), jnp.float32),
                jnp.zeros((KEYVALUE_HEADS, head_q.shape[1], HEAD_SIZE), jnp.float32),
            )
            for head_q, block_pos in prepared
        )
    )
    finals = fold_keys(
        initial,
        (
            lax.all_gather(new_keys, "ctx", axis=0, tiled=True),
            lax.all_gather(new_values, "ctx", axis=0, tiled=True),
        ),
        prepared,
    )
    attended = finish_block(finals[0], tok_rows)
    out_delta = output_delta(attended, out_part)
    return (attended, out_delta)


PIECES = 8
GROUP = QH // KEYVALUE_HEADS
DOWN = ((0, 12288),)
REST = ((12288, 2048), (14336, 512), (14848, 2048), (16896, 4096))


def pack_kernel(sections, pool, *refs):
    out, buffers, sems = refs[-3:]
    plane = lax.axis_index("groups")
    slabs, slab_rows = out.shape[:2]

    def copies(slab, slot):
        listed = []
        offset = 0
        for number, (first, rows) in enumerate(sections):
            share = rows // (4 * PIECES)
            quarter = 2 * plane + slab // PIECES
            begin = first + (lax.rem(slab, PIECES) * 4 + quarter) * share
            listed.append(
                pltpu.make_async_copy(
                    pool.at[:, pl.ds(pl.multiple_of(begin * 128, 2048), share * 128)],
                    buffers.at[slot, :, pl.ds(offset, share * 128)],
                    sems.at[slot, number],
                )
            )
            offset += share * 128
        return listed

    for copy in copies(0, 0):
        copy.start()

    def step(slab, carried):
        slot = lax.rem(slab, 2)

        @pl.when(slab < slabs - 1)
        def _():
            for copy in copies(slab + 1, 1 - slot):
                copy.start()

        for copy in copies(slab, slot):
            copy.wait()

        def chunk(index, inner):
            line = buffers[slot, :, pl.ds(pl.multiple_of(index * 2048, 2048), 2048)]
            block = line.astype(jnp.float32).reshape(16, 128).astype(jnp.bfloat16)
            out[slab, pl.ds(pl.multiple_of(index * 16, 16), 16), :] = block
            return inner

        lax.fori_loop(0, slab_rows // 16, chunk, 0, unroll=8)
        return carried

    lax.fori_loop(0, slabs, step, 0)


def pack_row(pool, sections, *after):
    slab_rows = sum(rows for _, rows in sections) // (4 * PIECES)
    return pl.pallas_call(
        partial(pack_kernel, sections),
        out_shape=jax.ShapeDtypeStruct((2 * PIECES, slab_rows, 128), jnp.bfloat16),
        in_specs=[pl.BlockSpec(memory_space=pl.ANY)] * (1 + len(after)),
        out_specs=pl.BlockSpec(memory_space=pltpu.VMEM),
        scratch_shapes=[
            pltpu.VMEM((2, 1, slab_rows * 128), jnp.bfloat16),
            pltpu.SemaphoreType.DMA((2, len(sections))),
        ],
        compiler_params=pltpu.CompilerParams(vmem_limit_bytes=60 << 20),
        cost_estimate=pl.CostEstimate(flops=0, bytes_accessed=8 << 20, transcendentals=0),
    )(pool, *after)


def attend_kernel(
    query_block,
    key_block,
    value_block,
    own_rank,
    all_rank,
    query_up,
    key_up,
    value_up,
    cosines,
    sines,
    down_out,
    up_out,
    attended,
    out_delta,
    total,
):
    step = pl.program_id(0)
    rows = query_block.shape[0]
    base = lax.axis_index("ctx") * rows
    dot = partial(jnp.dot, preferred_element_type=jnp.float32)

    def turned(delta, cosine, sine):
        return delta * cosine + pltpu.roll(delta, HEAD_SIZE // 2, 1) * sine

    keys = []
    values = []
    half = lax.axis_index("ctx") * rows // BLOCK_TOKENS
    for block in range(key_up.shape[0]):
        span = slice(block * BLOCK_TOKENS, (block + 1) * BLOCK_TOKENS)
        delta = adapter_scale * dot(all_rank[span, :ADAPTER_RANK], key_up[block ^ half])
        delta = turned(delta, cosines[span, :], sines[span, :])
        keys.append((key_block[span, :].astype(jnp.float32) + delta).astype(jnp.bfloat16))
        delta = adapter_scale * dot(all_rank[span, ADAPTER_RANK:], value_up[block ^ half])
        values.append((value_block[span, :].astype(jnp.float32) + delta).astype(jnp.bfloat16))
    keys = jnp.concatenate(keys, 0)
    values = jnp.concatenate(values, 0)
    here = pl.ds(pl.multiple_of(base, rows), rows)
    cosine = cosines[here, :]
    sine = sines[here, :]
    delta = adapter_scale * dot(own_rank[:, :ADAPTER_RANK], query_up[...])
    added = jnp.zeros((rows, ADAPTER_RANK), jnp.float32)
    taken = GROUP // 2
    for first in range(0, GROUP, taken):
        queries = []
        for head in range(first, first + taken):
            span = slice(head * HEAD_SIZE, (head + 1) * HEAD_SIZE)
            moved = turned(delta[:, span], cosine, sine)
            queries.append(
                (query_block[:, span].astype(jnp.float32) + moved).astype(jnp.bfloat16)
            )
        queries = jnp.concatenate(queries, 0)
        scores = lax.dot_general(
            queries, keys, (((1,), (1,)), ((), ())), preferred_element_type=jnp.float32
        ) * HEAD_SIZE ** (-0.5)
        row = lax.broadcasted_iota(jnp.int32, scores.shape, 0)
        column = lax.broadcasted_iota(jnp.int32, scores.shape, 1)
        scores = jnp.where(column <= base + lax.rem(row, rows), scores, mask_floor)
        weights = jnp.exp(scores - jnp.max(scores, axis=-1, keepdims=True))
        divisor = jnp.sum(weights, axis=-1, keepdims=True)
        result = (dot(weights.astype(jnp.bfloat16), values) / divisor).astype(jnp.bfloat16)
        for place, head in enumerate(range(first, first + taken)):
            span = slice(head * HEAD_SIZE, (head + 1) * HEAD_SIZE)
            part = result[place * rows : (place + 1) * rows]
            attended[:, span] = part
            added += dot(part, down_out[span, :])

    @pl.when(step == 0)
    def _():
        total[...] = jnp.zeros_like(total)

    total[...] += added

    @pl.when(step == pl.num_programs(0) - 1)
    def _():
        narrow = total[...].astype(jnp.bfloat16)
        out_delta[...] = (adapter_scale * dot(narrow, up_out[...])).astype(jnp.bfloat16)


def attend(
    query_base,
    base_rows,
    own_rank,
    all_rank,
    query_up,
    keyval_up,
    cosines,
    sines,
    down_out,
    up_out,
):
    rows = query_base.shape[0]
    seq = base_rows.shape[0]
    blocks = keyval_up.shape[0]
    width = GROUP * HEAD_SIZE

    def whole(shape):
        return pl.BlockSpec(shape, lambda h: (0,) * len(shape))

    return pl.pallas_call(
        attend_kernel,
        grid=(KEYVALUE_HEADS,),
        out_shape=(
            jax.ShapeDtypeStruct((rows, QH * HEAD_SIZE), jnp.bfloat16),
            jax.ShapeDtypeStruct((rows, D), jnp.bfloat16),
        ),
        in_specs=[
            pl.BlockSpec((rows, width), lambda h: (0, h)),
            pl.BlockSpec((seq, HEAD_SIZE), lambda h: (0, h)),
            pl.BlockSpec((seq, HEAD_SIZE), lambda h: (0, h + KEYVALUE_HEADS)),
            whole(own_rank.shape),
            whole(all_rank.shape),
            pl.BlockSpec((ADAPTER_RANK, width), lambda h: (0, h)),
            pl.BlockSpec((blocks, ADAPTER_RANK, HEAD_SIZE), lambda h: (0, 0, h)),
            pl.BlockSpec((blocks, ADAPTER_RANK, HEAD_SIZE), lambda h: (0, 0, h + KEYVALUE_HEADS)),
            whole(cosines.shape),
            whole(sines.shape),
            pl.BlockSpec((width, ADAPTER_RANK), lambda h: (h, 0)),
            whole(up_out.shape),
        ],
        out_specs=(
            pl.BlockSpec((rows, width), lambda h: (0, h)),
            whole((rows, D)),
        ),
        scratch_shapes=[pltpu.VMEM((rows, ADAPTER_RANK), jnp.float32)],
        compiler_params=pltpu.CompilerParams(vmem_limit_bytes=60 << 20),
        cost_estimate=pl.CostEstimate(
            flops=4 * rows * QH * seq * HEAD_SIZE,
            bytes_accessed=10 << 20,
            transcendentals=rows * QH * seq,
        ),
    )(
        query_base,
        base_rows,
        base_rows,
        own_rank,
        all_rank,
        query_up,
        keyval_up,
        keyval_up,
        cosines,
        sines,
        down_out,
        up_out,
    )


def swap(block, mask):
    return lax.ppermute(block, ("groups", "ctx"), [(i, i ^ mask) for i in range(4 * PIECES)])


def fetch_piece(packed, slots, corner, mirrored=None):
    spread = lax.all_to_all(packed, "ctx", 0, 0)
    arrived = []
    for flip, mask in enumerate((0, PIECES, 2 * PIECES, 3 * PIECES)):
        row = lax.dynamic_index_in_dim(slots, corner ^ flip, 0, keepdims=False)
        block = lax.dynamic_index_in_dim(spread, row, 0, keepdims=False)
        if mirrored is not None:
            row = lax.dynamic_index_in_dim(slots, corner ^ flip ^ 1, 0, keepdims=False)
            other = lax.dynamic_index_in_dim(spread, row, 0, keepdims=False)
            block = jnp.concatenate([block, other[mirrored]])
        arrived.append(swap(block, mask) if mask else block)
    low = corner % 2 == 0
    arrived = [jnp.where(low, arrived[q], arrived[q ^ 1]) for q in range(4)]
    high = corner < 2
    return jnp.stack([jnp.where(high, arrived[q], arrived[q ^ 2]) for q in range(4)])


def direct_shards(
    normed_input, query_base, key_base, value_base, adapter_pool, stretch_adapter, adapter_owner
):
    plane = lax.axis_index("groups")
    index = lax.axis_index("ctx")
    tok_rows = normed_input.shape[0]
    ctx = lax.axis_size("ctx")
    seq = ctx * tok_rows
    blocks = [list(range(PIECES)), list(range(PIECES, 2 * PIECES))]
    corner = 2 * plane + index // PIECES

    elsewhere = swap(stretch_adapter, 2 * PIECES)
    wanted = jnp.where(
        plane == 0,
        jnp.concatenate([stretch_adapter, elsewhere]),
        jnp.concatenate([elsewhere, stretch_adapter]),
    )
    ids = jnp.arange(adapter_owner.shape[0], dtype=jnp.int32)
    slots = jnp.sum(jnp.where(wanted[:, None] == ids[None, :], adapter_owner[None, :], 0), axis=1)

    moving = normed_input.reshape(tok_rows, PIECES, D // PIECES).transpose(1, 0, 2)
    moving = lax.all_to_all(moving, "ctx", 0, 0, axis_index_groups=blocks)
    base_rows = lax.all_gather(
        jnp.concatenate([key_base, value_base], 1), "ctx", axis=0, tiled=True
    )

    packed_rest = pack_row(adapter_pool, REST)
    packed_down = pack_row(adapter_pool, DOWN, packed_rest)
    rest = fetch_piece(packed_rest, slots, corner, slice(64, 80))
    rest, base_rows = lax.optimization_barrier((rest, base_rows))
    rest = lax.all_gather(rest, "ctx", axis_index_groups=blocks)
    query_up = rest[:, :, :64].reshape(ADAPTER_RANK, QH * HEAD_SIZE)
    keyval_up = jnp.stack([rest[:, :, 64:80], rest[:, :, 272:]])
    keyval_up = keyval_up.reshape(2, ADAPTER_RANK, 2 * KEYVALUE_HEADS * HEAD_SIZE)
    down_out = rest[:, :, 80:144].reshape(QH * HEAD_SIZE, ADAPTER_RANK)
    up_out = rest[:, :, 144:272].reshape(ADAPTER_RANK, D)

    down_slice = fetch_piece(packed_down, slots, corner)
    down_slice = down_slice.reshape(D // PIECES, 3 * ADAPTER_RANK)
    partial_rows = jnp.dot(
        moving.reshape(BLOCK_TOKENS, D // PIECES), down_slice, preferred_element_type=jnp.float32
    ).astype(jnp.bfloat16)
    partial_rows = lax.all_to_all(
        partial_rows.reshape(PIECES, tok_rows, 3 * ADAPTER_RANK),
        "ctx",
        0,
        0,
        axis_index_groups=blocks,
    )
    own_rank = jnp.sum(partial_rows.astype(jnp.float32), axis=0).astype(jnp.bfloat16)
    all_rank = jnp.broadcast_to(own_rank[None, :, ADAPTER_RANK:], (ctx, tok_rows, 2 * ADAPTER_RANK))
    all_rank = lax.all_to_all(all_rank, "ctx", 0, 0).reshape(seq, 2 * ADAPTER_RANK)

    half_dim = HEAD_SIZE // 2
    frequency = rope_base ** (-(jnp.arange(half_dim, dtype=jnp.float32) * 2.0) / HEAD_SIZE)
    angle = jnp.arange(seq, dtype=jnp.int32).astype(jnp.float32)[:, None] * frequency[None, :]
    cosine = jnp.cos(angle)
    sine = jnp.sin(angle)
    cosines = jnp.concatenate([cosine, cosine], 1)
    sines = jnp.concatenate([-sine, sine], 1)
    return attend(
        query_base,
        base_rows,
        own_rank,
        all_rank,
        query_up,
        keyval_up,
        cosines,
        sines,
        down_out,
        up_out,
    )


def shards(normed_input, query_base, key_base, value_base, adapter_pool, stretch_adapter, owner):
    fits = (
        lax.axis_size("groups") == 2
        and lax.axis_size("ctx") == 2 * PIECES
        and normed_input.shape[0] * PIECES == BLOCK_TOKENS
        and adapter_pool.shape[0] == 1
    )
    plan = direct_shards if fits else spread_shards
    return plan(
        normed_input, query_base, key_base, value_base, adapter_pool, stretch_adapter, owner
    )


def solution(mesh):
    placed = (
        P(("groups", "ctx"), None),
        P(("groups", "ctx"), None),
        P(("groups", "ctx"), None),
        P(("groups", "ctx"), None),
        P("ctx", None),
        P("groups"),
        P(),
    )
    return jax.shard_map(
        shards,
        mesh=mesh,
        in_specs=placed,
        out_specs=(P(("groups", "ctx"), None), P(("groups", "ctx"), None)),
        check_vma=False,
    )
```

profile of v0, /device:TPU:0, one launch (start us, length us, event | category | flops | bytes accessed | tf_op | source)
XLA Modules:
  0.0 191.6 jit_solution(4455928861911986624)
XLA Ops:
  7.2 0.0 all-gather.4.cloned.1.call-start
  7.2 1.5 pad_maximum_fusion.5
  8.7 0.0 all-gather.4.cloned.1.call-update
  8.8 8.9 %shard_map.86.refs_0_ = bf16[16,272,128]{2,1,0:T(8,128)(2,1)} custom-call(bf16[1,2686976]{1,0:T(2,128)(2,1)} %pool.3), custom_call_target="tpu_custom_call" | custom-call | bytes 8388608 | tf_op jit(solution)/shard_map/pallas_call | solution.py:321
  17.7 7.4 %all-to-all-start = ((bf16[16,272,128]{2,1,0:T(8,128)(2,1)}), bf16[16,272,128]{2,1,0:T(8,128)(2,1)S(1)}, u32[]{:S(2)}, u32[]{:S(2)}) async-start(bf16[16,272,128]{2,1,0:T(8,128)(2,1)} %shard_map.86.refs_0_), calls=%async_computation | async-start | bytes 2228224 | tf_op jit(solution)/shard_map/all_to_all | solution.py:487
  25.1 9.6 %shard_map.87 = bf16[16,384,128]{2,1,0:T(8,128)(2,1)} custom-call(bf16[1,2686976]{1,0:T(2,128)(2,1)} %pool.3, bf16[16,272,128]{2,1,0:T(8,128)(2,1)} %shard_map.86.refs_0_), custom_call_target="tpu_custom_call" | custom-call | bytes 8388608 | tf_op jit(solution)/shard_map/pallas_call | solution.py:321
  34.6 0.0 copy-start.3
  34.6 0.0 copy-start.4
  34.7 20.4 %all-to-all-done = bf16[16,272,128]{2,1,0:T(8,128)(2,1)S(1)} async-done(((bf16[16,272,128]{2,1,0:T(8,128)(2,1)}), bf16[16,272,128]{2,1,0:T(8,128)(2,1)S(1)}, u32[]{:S(2)}, u32[]{:S(2)}) %all-to-all-start) | async-done | bytes 1114144 | tf_op jit(solution)/shard_map/all_to_all | solution.py:487
  55.1 12.1 %all-to-all-start.1 = ((bf16[16,384,128]{2,1,0:T(8,128)(2,1)}), bf16[16,384,128]{2,1,0:T(8,128)(2,1)S(1)}, u32[]{:S(2)}, u32[]{:S(2)}) async-start(bf16[16,384,128]{2,1,0:T(8,128)(2,1)} %shard_map.87), calls=%async_computation.1 | async-start | bytes 3145728 | tf_op jit(solution)/shard_map/all_to_all | solution.py:487
  67.1 0.0 all-gather.6.cloned.1.call-start
  67.2 0.0 copy-done.3
  67.2 1.6 collective-permute-start
  68.8 2.0 %collective-permute-done = s32[2]{0:T(128)S(1)} collective-permute-done((s32[2]{0:T(128)S(1)}, s32[2]{0:T(128)S(1)}, u32[]{:S(2)}, u32[]{:S(2)}) %collective-permute-start) | collective-permute-done | bytes 40 | tf_op jit(solution)/shard_map/ppermute | solution.py:483
  70.8 0.1 broadcast_select_fusion.6
  70.9 0.0 copy-done.4
  70.9 0.2 select_reduce_fusion
  71.1 0.7 fusion.4
  84.9 0.0 copy-start.1
  84.9 2.9 %collective-permute-start.1 = (bf16[288,128]{1,0:T(8,128)(2,1)S(1)}, bf16[288,128]{1,0:T(8,128)(2,1)S(1)}, u32[]{:S(2)}, u32[]{:S(2)}) collective-permute-start(bf16[288,128]{1,0:T(8,128)(2,1)S(1)} %pad_maximum_fusion.7), channel_id=1, source_target_pairs={{0,8},{1,9},{2,10},{3,11},{4,12},{5,13},{6,14},{7,15},{8,0},{9,1},... | collective-permute-start | bytes 221192 | tf_op jit(solution)/shard_map/ppermute | solution.py:483
  87.8 1.1 collective-permute-start.3
  88.9 0.5 collective-permute-start.2
  89.5 20.7 %collective-permute-done.1 = bf16[288,128]{1,0:T(8,128)(2,1)S(1)} collective-permute-done((bf16[288,128]{1,0:T(8,128)(2,1)S(1)}, bf16[288,128]{1,0:T(8,128)(2,1)S(1)}, u32[]{:S(2)}, u32[]{:S(2)}) %collective-permute-start.1) | collective-permute-done | bytes 73760 | tf_op jit(solution)/shard_map/ppermute | solution.py:483
  110.2 2.1 %collective-permute-done.3 = bf16[288,128]{1,0:T(8,128)(2,1)S(1)} collective-permute-done((bf16[288,128]{1,0:T(8,128)(2,1)S(1)}, bf16[288,128]{1,0:T(8,128)(2,1)S(1)}, u32[]{:S(2)}, u32[]{:S(2)}) %collective-permute-start.3) | collective-permute-done | bytes 73760 | tf_op jit(solution)/shard_map/ppermute | solution.py:483
  112.2 0.0 collective-permute-done.2
  112.2 0.1 select_bitcast_fusion.7
  112.3 0.8 pad_maximum_fusion.3
  113.1 0.0 all-gather.6.cloned.1.call-update
  113.1 0.6 copy.16
  113.7 1.5 copy.14
  115.3 0.0 all-to-all-done.1
  115.3 3.6 %all-to-all-start.2 = ((bf16[8,64,1024]{2,1,0:T(8,128)(2,1)}), bf16[8,64,1024]{2,1,0:T(8,128)(2,1)S(1)}, u32[]{:S(2)}, u32[]{:S(2)}) async-start(bf16[8,64,1024]{2,1,0:T(8,128)(2,1)} %copy.14), calls=%async_computation.2 | async-start | bytes 2097152 | tf_op jit(solution)/shard_map/all_to_all | solution.py:524
  118.9 0.6 collective-permute-start.4
  119.5 0.5 collective-permute-start.5
  120.1 3.3 %collective-permute-start.6 = (bf16[384,128]{1,0:T(8,128)(2,1)S(1)}, bf16[384,128]{1,0:T(8,128)(2,1)S(1)}, u32[]{:S(2)}, u32[]{:S(2)}) collective-permute-start(bf16[384,128]{1,0:T(8,128)(2,1)S(1)} %get-tuple-element.15), channel_id=1, source_target_pairs={{0,24},{1,25},{2,26},{3,27},{4,28},{5,29},{6,30},{7,31},{8,16},{9,... | collective-permute-start | bytes 294920 | tf_op jit(solution)/shard_map/ppermute | solution.py:483
  123.4 19.0 %collective-permute-done.4 = bf16[384,128]{1,0:T(8,128)(2,1)S(1)} collective-permute-done((bf16[384,128]{1,0:T(8,128)(2,1)S(1)}, bf16[384,128]{1,0:T(8,128)(2,1)S(1)}, u32[]{:S(2)}, u32[]{:S(2)}) %collective-permute-start.4) | collective-permute-done | bytes 98336 | tf_op jit(solution)/shard_map/ppermute | solution.py:483
  142.4 0.0 collective-permute-done.5
  142.4 2.1 %collective-permute-done.6 = bf16[384,128]{1,0:T(8,128)(2,1)S(1)} collective-permute-done((bf16[384,128]{1,0:T(8,128)(2,1)S(1)}, bf16[384,128]{1,0:T(8,128)(2,1)S(1)}, u32[]{:S(2)}, u32[]{:S(2)}) %collective-permute-start.6) | collective-permute-done | bytes 98336 | tf_op jit(solution)/shard_map/ppermute | solution.py:483
  144.5 0.1 pad_maximum_fusion.2
  144.6 0.3 reshape.79
  145.0 1.6 all-to-all-done.2
  146.5 0.5 fusion
  147.0 0.8 copy.15
  147.9 3.7 %all-to-all-start.3 = ((bf16[8,64,192]{2,1,0:T(8,128)(2,1)}), bf16[8,64,192]{2,1,0:T(8,128)(2,1)S(1)}, u32[]{:S(2)}, u32[]{:S(2)}) async-start(bf16[8,64,192]{2,1,0:T(8,128)(2,1)} %bitcast.30), calls=%async_computation.3 | async-start | bytes 524288 | tf_op jit(solution)/shard_map/all_to_all | solution.py:545
  151.6 1.9 fusion.1
  153.5 1.3 pad_maximum_fusion
  154.8 2.8 %all-to-all-done.3 = bf16[8,64,192]{2,1,0:T(8,128)(2,1)S(1)} async-done(((bf16[8,64,192]{2,1,0:T(8,128)(2,1)}), bf16[8,64,192]{2,1,0:T(8,128)(2,1)S(1)}, u32[]{:S(2)}, u32[]{:S(2)}) %all-to-all-start.3) | async-done | bytes 196640 | tf_op jit(solution)/shard_map/all_to_all | solution.py:545
  157.7 0.0 copy-start.2
  157.7 0.1 slice.56
  157.7 0.8 broadcast_in_dim.16
  158.5 4.1 %all-to-all-start.4 = ((bf16[16,64,128]{2,1,0:T(8,128)(2,1)}), bf16[16,64,128]{2,1,0:T(8,128)(2,1)S(1)}, u32[]{:S(2)}, u32[]{:S(2)}) async-start(bf16[16,64,128]{2,1,0:T(8,128)(2,1)} %broadcast_in_dim.16), calls=%async_computation.4 | async-start | bytes 524288 | tf_op jit(solution)/shard_map/all_to_all | solution.py:554
  162.6 0.0 all-gather.6.cloned.1.call-done
  162.6 1.0 fusion.3
  163.6 1.3 slice.61
  164.9 0.1 stack.49
  165.0 0.1 stack.50
  165.0 1.3 fusion.2
  166.4 1.4 reshape.85.down_out
  167.8 1.3 reshape.86.up_out
  169.0 1.0 reshape.84.query_up
  170.1 0.7 pad_maximum_fusion.4.key_up.value_up
  170.8 1.8 all-to-all-done.4
  172.6 0.7 copy-done
  173.3 11.4 %shard_map.88 = (bf16[64,4096]{1,0:T(8,128)(2,1)}, bf16[64,8192]{1,0:T(8,128)(2,1)}) custom-call(bf16[64,4096]{1,0:T(8,128)(2,1)} %query_block.1, bf16[1024,1024]{1,0:T(8,128)(2,1)} %all-gather.4.cloned.1.call-done.key_block.value_block, bf16[1024,1024]{1,0:T(8,128)(2,1)} %all-gather.4.cloned.1.call-done.key_block.value_block, bf16[64,192]{1,0:T(8,128)(2,1)} %copy-done.2, ...), custom_call_target="tpu_custom_call" | custom-call | flops 1073741824 | bytes 10485760 | tf_op jit(solution)/shard_map/pallas_call | solution.py:434
  (14 shorter events, 0.2 us)
Async XLA Ops:
  7.2 105.9 %all-gather.4.cloned.1.call-start = ((), (), s32[]{:S(2)}) async-start(), calls=%async_computation.5 | async-start | bytes 2228224 | tf_op jit(solution)/shard_map/all_gather | solution.py:525
  17.7 37.4 %all-to-all-start = ((bf16[16,272,128]{2,1,0:T(8,128)(2,1)}), bf16[16,272,128]{2,1,0:T(8,128)(2,1)S(1)}, u32[]{:S(2)}, u32[]{:S(2)}) async-start(bf16[16,272,128]{2,1,0:T(8,128)(2,1)} %shard_map.86.refs_0_), calls=%async_computation | async-start | bytes 2228224 | tf_op jit(solution)/shard_map/all_to_all | solution.py:487
  34.6 32.6 %copy-start.3 = (s32[2]{0:T(128)S(1)}, s32[2]{0:T(128)}, u32[]{:S(2)}) copy-start(s32[2]{0:T(128)} %param.12) | copy-start | bytes 28
  34.6 36.2 %copy-start.4 = (s32[16]{0:T(128)S(1)}, s32[16]{0:T(128)}, u32[]{:S(2)}) copy-start(s32[16]{0:T(128)} %param.13) | copy-start | bytes 196
  55.1 60.2 %all-to-all-start.1 = ((bf16[16,384,128]{2,1,0:T(8,128)(2,1)}), bf16[16,384,128]{2,1,0:T(8,128)(2,1)S(1)}, u32[]{:S(2)}, u32[]{:S(2)}) async-start(bf16[16,384,128]{2,1,0:T(8,128)(2,1)} %shard_map.87), calls=%async_computation.1 | async-start | bytes 3145728 | tf_op jit(solution)/shard_map/all_to_all | solution.py:487
  67.1 95.4 %all-gather.6.cloned.1.call-start = ((), (), s32[]{:S(2)}) async-start(), calls=%async_computation.6 | async-start | bytes 2654208 | tf_op jit(solution)/shard_map/all_gather | solution.py:533
  67.2 3.6 %collective-permute-start = (s32[2]{0:T(128)S(1)}, s32[2]{0:T(128)S(1)}, u32[]{:S(2)}, u32[]{:S(2)}) collective-permute-start(s32[2]{0:T(128)S(1)} %copy-done.3), channel_id=1, source_target_pairs={{0,16},{1,17},{2,18},{3,19},{4,20},{5,21},{6,22},{7,23},{8,24},{9,... | collective-permute-start | bytes 32 | tf_op jit(solution)/shard_map/ppermute | solution.py:483
  84.9 28.2 %copy-start.1 = (bf16[64,8192]{1,0:T(8,128)(2,1)S(1)}, bf16[64,8192]{1,0:T(8,128)(2,1)}, u32[]{:S(2)}) copy-start(bf16[64,8192]{1,0:T(8,128)(2,1)} %param.7) | copy-start | bytes 3145732
  84.9 25.2 %collective-permute-start.1 = (bf16[288,128]{1,0:T(8,128)(2,1)S(1)}, bf16[288,128]{1,0:T(8,128)(2,1)S(1)}, u32[]{:S(2)}, u32[]{:S(2)}) collective-permute-start(bf16[288,128]{1,0:T(8,128)(2,1)S(1)} %pad_maximum_fusion.7), channel_id=1, source_target_pairs={{0,8},{1,9},{2,10},{3,11},{4,12},{5,13},{6,14},{7,15},{8,0},{9,1},... | collective-permute-start | bytes 221192 | tf_op jit(solution)/shard_map/ppermute | solution.py:483
  87.8 24.4 %collective-permute-start.3 = (bf16[288,128]{1,0:T(8,128)(2,1)S(1)}, bf16[288,128]{1,0:T(8,128)(2,1)S(1)}, u32[]{:S(2)}, u32[]{:S(2)}) collective-permute-start(bf16[288,128]{1,0:T(8,128)(2,1)S(1)} %pad_maximum_fusion.9), channel_id=1, source_target_pairs={{0,24},{1,25},{2,26},{3,27},{4,28},{5,29},{6,30},{7,31},{8,16},{9,... | collective-permute-start | bytes 221192 | tf_op jit(solution)/shard_map/ppermute | solution.py:483
  88.9 23.3 %collective-permute-start.2 = (bf16[288,128]{1,0:T(8,128)(2,1)S(1)}, bf16[288,128]{1,0:T(8,128)(2,1)S(1)}, u32[]{:S(2)}, u32[]{:S(2)}) collective-permute-start(bf16[288,128]{1,0:T(8,128)(2,1)S(1)} %pad_maximum_fusion.8), channel_id=1, source_target_pairs={{0,16},{1,17},{2,18},{3,19},{4,20},{5,21},{6,22},{7,23},{8,24},{9,... | collective-permute-start | bytes 221192 | tf_op jit(solution)/shard_map/ppermute | solution.py:483
  115.3 31.2 %all-to-all-start.2 = ((bf16[8,64,1024]{2,1,0:T(8,128)(2,1)}), bf16[8,64,1024]{2,1,0:T(8,128)(2,1)S(1)}, u32[]{:S(2)}, u32[]{:S(2)}) async-start(bf16[8,64,1024]{2,1,0:T(8,128)(2,1)} %copy.14), calls=%async_computation.2 | async-start | bytes 2097152 | tf_op jit(solution)/shard_map/all_to_all | solution.py:524
  118.9 23.5 %collective-permute-start.4 = (bf16[384,128]{1,0:T(8,128)(2,1)S(1)}, bf16[384,128]{1,0:T(8,128)(2,1)S(1)}, u32[]{:S(2)}, u32[]{:S(2)}) collective-permute-start(bf16[384,128]{1,0:T(8,128)(2,1)S(1)} %get-tuple-element.14), channel_id=1, source_target_pairs={{0,8},{1,9},{2,10},{3,11},{4,12},{5,13},{6,14},{7,15},{8,0},{9,1},... | collective-permute-start | bytes 294920 | tf_op jit(solution)/shard_map/ppermute | solution.py:483
  119.5 22.8 %collective-permute-start.5 = (bf16[384,128]{1,0:T(8,128)(2,1)S(1)}, bf16[384,128]{1,0:T(8,128)(2,1)S(1)}, u32[]{:S(2)}, u32[]{:S(2)}) collective-permute-start(bf16[384,128]{1,0:T(8,128)(2,1)S(1)} %get-tuple-element.16), channel_id=1, source_target_pairs={{0,16},{1,17},{2,18},{3,19},{4,20},{5,21},{6,22},{7,23},{8,24},{9,... | collective-permute-start | bytes 294920 | tf_op jit(solution)/shard_map/ppermute | solution.py:483
  120.1 24.4 %collective-permute-start.6 = (bf16[384,128]{1,0:T(8,128)(2,1)S(1)}, bf16[384,128]{1,0:T(8,128)(2,1)S(1)}, u32[]{:S(2)}, u32[]{:S(2)}) collective-permute-start(bf16[384,128]{1,0:T(8,128)(2,1)S(1)} %get-tuple-element.15), channel_id=1, source_target_pairs={{0,24},{1,25},{2,26},{3,27},{4,28},{5,29},{6,30},{7,31},{8,16},{9,... | collective-permute-start | bytes 294920 | tf_op jit(solution)/shard_map/ppermute | solution.py:483
  147.9 9.7 %all-to-all-start.3 = ((bf16[8,64,192]{2,1,0:T(8,128)(2,1)}), bf16[8,64,192]{2,1,0:T(8,128)(2,1)S(1)}, u32[]{:S(2)}, u32[]{:S(2)}) async-start(bf16[8,64,192]{2,1,0:T(8,128)(2,1)} %bitcast.30), calls=%async_computation.3 | async-start | bytes 524288 | tf_op jit(solution)/shard_map/all_to_all | solution.py:545
  157.7 7.2 %copy-start.2 = (bf16[64,192]{1,0:T(8,128)(2,1)}, bf16[64,192]{1,0:T(8,128)(2,1)S(1)}, u32[]{:S(2)}) copy-start(bf16[64,192]{1,0:T(8,128)(2,1)S(1)} %reduce_sum.22.own_rank) | copy-start | bytes 73732
  158.5 14.1 %all-to-all-start.4 = ((bf16[16,64,128]{2,1,0:T(8,128)(2,1)}), bf16[16,64,128]{2,1,0:T(8,128)(2,1)S(1)}, u32[]{:S(2)}, u32[]{:S(2)}) async-start(bf16[16,64,128]{2,1,0:T(8,128)(2,1)} %broadcast_in_dim.16), calls=%async_computation.4 | async-start | bytes 524288 | tf_op jit(solution)/shard_map/all_to_all | solution.py:554
  172.6 0.7 copy-start
Sparse Core Ops, SparseCore 0:
  10.7 52.6 all-gather.3
  113.2 32.9 all-gather.5
where the time goes:
time: 193 us; the launch traced here: 192 us
  waiting for transfers between devices  72.6 us (38%)
  starting transfers between devices  41.4 us (21%)
  Pallas kernels  29.9 us (15%)
  between operations  27.4 us (14%)
  local copies, waits for them, and re-layouts  13.1 us (7%)
  other arithmetic  6.77 us (4%)
    ppermute x7, waiting for transfers between devices, swap(): lax.ppermute(block, ('groups', 'ctx'), [(i, i ^ mask) for i in range(4 *...  45.9 us
    all_to_all x2, waiting for transfers between devices, fetch_piece(): spread = lax.all_to_all(packed, 'ctx', 0, 0)  20.4 us
    all_to_all x2, starting transfers between devices, fetch_piece(): spread = lax.all_to_all(packed, 'ctx', 0, 0)  19.4 us
    pallas_call x2, Pallas kernels, pack_row(): pl.pallas_call(partial(pack_kernel, sections), out_shape=jax.ShapeDtypeSt...  18.5 us
    pallas_call x1, Pallas kernels, attend(): pl.pallas_call(attend_kernel, grid=(KEYVALUE_HEADS,), out_shape=(jax.Shap...  11.4 us
    ppermute x7, starting transfers between devices, swap(): lax.ppermute(block, ('groups', 'ctx'), [(i, i ^ mask) for i in range(4 *...  10.6 us
    all_to_all x1, starting transfers between devices, direct_shards(): lax.all_to_all(all_rank, 'ctx', 0, 0).reshape(seq, 2 * ADAPTER_RANK)  4.06 us
  transfers between devices with their start and end apart: 14, of which 9 were waited for; matrix products, arithmetic and copies ran while one was open for 9% of the time, Pallas kernels for 10%

commit v1 on v0

--- a/solution.py
+++ b/solution.py
@@ -273,39 +273,32 @@
     plane = lax.axis_index("groups")
     slabs, slab_rows = out.shape[:2]
 
-    def copies(slab, slot):
+    def copies(slab):
         listed = []
         offset = 0
-        for number, (first, rows) in enumerate(sections):
-            share = rows // (4 * PIECES)
-            quarter = 2 * plane + slab // PIECES
-            begin = first + (lax.rem(slab, PIECES) * 4 + quarter) * share
+        for first, rows in sections:
+            share = rows // (2 * PIECES)
+            begin = first + (slab * 2 + plane) * share
             listed.append(
                 pltpu.make_async_copy(
                     pool.at[:, pl.ds(pl.multiple_of(begin * 128, 2048), share * 128)],
-                    buffers.at[slot, :, pl.ds(offset, share * 128)],
-                    sems.at[slot, number],
+                    buffers.at[slab, :, pl.ds(offset, share * 128)],
+                    sems.at[slab, len(listed)],
                 )
             )
             offset += share * 128
         return listed
 
-    for copy in copies(0, 0):
-        copy.start()
+    for slab in range(slabs):
+        for copy in copies(slab):
+            copy.start()
 
     def step(slab, carried):
-        slot = lax.rem(slab, 2)
-
-        @pl.when(slab < slabs - 1)
-        def _():
-            for copy in copies(slab + 1, 1 - slot):
-                copy.start()
-
-        for copy in copies(slab, slot):
+        for copy in copies(slab):
             copy.wait()
 
         def chunk(index, inner):
-            line = buffers[slot, :, pl.ds(pl.multiple_of(index * 2048, 2048), 2048)]
+            line = buffers[slab, :, pl.ds(pl.multiple_of(index * 2048, 2048), 2048)]
             block = line.astype(jnp.float32).reshape(16, 128).astype(jnp.bfloat16)
             out[slab, pl.ds(pl.multiple_of(index * 16, 16), 16), :] = block
             return inner
@@ -317,25 +310,68 @@
 
 
 def pack_row(pool, sections, *after):
-    slab_rows = sum(rows for _, rows in sections) // (4 * PIECES)
+    slab_rows = sum(rows for _, rows in sections) // (2 * PIECES)
     return pl.pallas_call(
         partial(pack_kernel, sections),
-        out_shape=jax.ShapeDtypeStruct((2 * PIECES, slab_rows, 128), jnp.bfloat16),
+        out_shape=jax.ShapeDtypeStruct((PIECES, slab_rows, 128), jnp.bfloat16),
         in_specs=[pl.BlockSpec(memory_space=pl.ANY)] * (1 + len(after)),
         out_specs=pl.BlockSpec(memory_space=pltpu.VMEM),
         scratch_shapes=[
-            pltpu.VMEM((2, 1, slab_rows * 128), jnp.bfloat16),
-            pltpu.SemaphoreType.DMA((2, len(sections))),
+            pltpu.VMEM((PIECES, 1, slab_rows * 128), jnp.bfloat16),
+            pltpu.SemaphoreType.DMA((PIECES, len(sections))),
         ],
         compiler_params=pltpu.CompilerParams(vmem_limit_bytes=60 << 20),
         cost_estimate=pl.CostEstimate(flops=0, bytes_accessed=8 << 20, transcendentals=0),
     )(pool, *after)
 
 
+def pick_kernel(mirrored, here, there, owner, spread, *refs):
+    outs, sems = refs[:4], refs[4]
+    half = lax.axis_index("ctx") // PIECES
+    rows = spread.shape[1]
+    copies = []
+    for flip, out in enumerate(outs):
+        wishes = there if flip >= 2 else here
+        block = half ^ (flip & 1)
+        row = lax.rem(owner[wishes[block]], PIECES)
+        copies.append(
+            pltpu.make_async_copy(spread.at[row], out.at[pl.ds(0, rows)], sems.at[flip, 0])
+        )
+        if mirrored is not None:
+            first, count = mirrored
+            row = lax.rem(owner[wishes[1 - block]], PIECES)
+            copies.append(
+                pltpu.make_async_copy(
+                    spread.at[row, pl.ds(first, count)],
+                    out.at[pl.ds(rows, count)],
+                    sems.at[flip, 1],
+                )
+            )
+    for copy in copies:
+        copy.start()
+    for copy in copies:
+        copy.wait()
+
+
+def pick(spread, here, there, owner, mirrored):
+    rows = spread.shape[1] + (mirrored[1] if mirrored else 0)
+    slab = jax.ShapeDtypeStruct((rows, 128), jnp.bfloat16)
+    return pl.pallas_call(
+        partial(pick_kernel, mirrored),
+        out_shape=(slab,) * 4,
+        in_specs=[pl.BlockSpec(memory_space=pltpu.SMEM)] * 3 + [pl.BlockSpec(memory_space=pl.ANY)],
+        out_specs=(pl.BlockSpec(memory_space=pl.ANY),) * 4,
+        scratch_shapes=[pltpu.SemaphoreType.DMA((4, 2))],
+        cost_estimate=pl.CostEstimate(flops=0, bytes_accessed=2 << 20, transcendentals=0),
+    )(here, there, owner, spread)
+
+
 def attend_kernel(
     query_block,
-    key_block,
-    value_block,
+    key_same,
+    key_other,
+    value_same,
+    value_other,
     own_rank,
     all_rank,
     query_up,
@@ -348,6 +384,8 @@
     attended,
     out_delta,
     total,
+    keys,
+    values,
 ):
     step = pl.program_id(0)
     rows = query_block.shape[0]
@@ -357,18 +395,20 @@
     def turned(delta, cosine, sine):
         return delta * cosine + pltpu.roll(delta, HEAD_SIZE // 2, 1) * sine
 
-    keys = []
-    values = []
     half = lax.axis_index("ctx") * rows // BLOCK_TOKENS
+    core = lax.rem(lax.axis_index("ctx"), 2)
     for block in range(key_up.shape[0]):
-        span = slice(block * BLOCK_TOKENS, (block + 1) * BLOCK_TOKENS)
-        delta = adapter_scale * dot(all_rank[span, :ADAPTER_RANK], key_up[block ^ half])
-        delta = turned(delta, cosines[span, :], sines[span, :])
-        keys.append((key_block[span, :].astype(jnp.float32) + delta).astype(jnp.bfloat16))
-        delta = adapter_scale * dot(all_rank[span, ADAPTER_RANK:], value_up[block ^ half])
-        values.append((value_block[span, :].astype(jnp.float32) + delta).astype(jnp.bfloat16))
-    keys = jnp.concatenate(keys, 0)
-    values = jnp.concatenate(values, 0)
+        for chip in range(block * PIECES // 2, (block + 1) * PIECES // 2):
+            for apart in range(2):
+                first = (2 * chip + (core ^ apart)) * rows
+                span = pl.ds(pl.multiple_of(first, rows), rows)
+                key_base = (key_other if apart else key_same)[chip]
+                value_base = (value_other if apart else value_same)[chip]
+                delta = adapter_scale * dot(all_rank[span, :ADAPTER_RANK], key_up[block ^ half])
+                delta = turned(delta, cosines[span, :], sines[span, :])
+                keys[span, :] = (key_base.astype(jnp.float32) + delta).astype(jnp.bfloat16)
+                delta = adapter_scale * dot(all_rank[span, ADAPTER_RANK:], value_up[block ^ half])
+                values[span, :] = (value_base.astype(jnp.float32) + delta).astype(jnp.bfloat16)
     here = pl.ds(pl.multiple_of(base, rows), rows)
     cosine = cosines[here, :]
     sine = sines[here, :]
@@ -385,14 +425,14 @@
             )
         queries = jnp.concatenate(queries, 0)
         scores = lax.dot_general(
-            queries, keys, (((1,), (1,)), ((), ())), preferred_element_type=jnp.float32
+            queries, keys[...], (((1,), (1,)), ((), ())), preferred_element_type=jnp.float32
         ) * HEAD_SIZE ** (-0.5)
         row = lax.broadcasted_iota(jnp.int32, scores.shape, 0)
         column = lax.broadcasted_iota(jnp.int32, scores.shape, 1)
         scores = jnp.where(column <= base + lax.rem(row, rows), scores, mask_floor)
         weights = jnp.exp(scores - jnp.max(scores, axis=-1, keepdims=True))
         divisor = jnp.sum(weights, axis=-1, keepdims=True)
-        result = (dot(weights.astype(jnp.bfloat16), values) / divisor).astype(jnp.bfloat16)
+        result = (dot(weights.astype(jnp.bfloat16), values[...]) / divisor).astype(jnp.bfloat16)
         for place, head in enumerate(range(first, first + taken)):
             span = slice(head * HEAD_SIZE, (head + 1) * HEAD_SIZE)
             part = result[place * rows : (place + 1) * rows]
@@ -414,6 +454,7 @@
 def attend(
     query_base,
     base_rows,
+    base_other,
     own_rank,
     all_rank,
     query_up,
@@ -424,7 +465,8 @@
     up_out,
 ):
     rows = query_base.shape[0]
-    seq = base_rows.shape[0]
+    chips = base_rows.shape[0]
+    seq = 2 * chips * rows
     blocks = keyval_up.shape[0]
     width = GROUP * HEAD_SIZE
 
@@ -440,8 +482,10 @@
         ),
         in_specs=[
             pl.BlockSpec((rows, width), lambda h: (0, h)),
-            pl.BlockSpec((seq, HEAD_SIZE), lambda h: (0, h)),
-            pl.BlockSpec((seq, HEAD_SIZE), lambda h: (0, h + KEYVALUE_HEADS)),
+            pl.BlockSpec((chips, rows, HEAD_SIZE), lambda h: (0, 0, h)),
+            pl.BlockSpec((chips, rows, HEAD_SIZE), lambda h: (0, 0, h)),
+            pl.BlockSpec((chips, rows, HEAD_SIZE), lambda h: (0, 0, h + KEYVALUE_HEADS)),
+            pl.BlockSpec((chips, rows, HEAD_SIZE), lambda h: (0, 0, h + KEYVALUE_HEADS)),
             whole(own_rank.shape),
             whole(all_rank.shape),
             pl.BlockSpec((ADAPTER_RANK, width), lambda h: (0, h)),
@@ -456,7 +500,11 @@
             pl.BlockSpec((rows, width), lambda h: (0, h)),
             whole((rows, D)),
         ),
-        scratch_shapes=[pltpu.VMEM((rows, ADAPTER_RANK), jnp.float32)],
+        scratch_shapes=[
+            pltpu.VMEM((rows, ADAPTER_RANK), jnp.float32),
+            pltpu.VMEM((seq, HEAD_SIZE), jnp.bfloat16),
+            pltpu.VMEM((seq, HEAD_SIZE), jnp.bfloat16),
+        ],
         compiler_params=pltpu.CompilerParams(vmem_limit_bytes=60 << 20),
         cost_estimate=pl.CostEstimate(
             flops=4 * rows * QH * seq * HEAD_SIZE,
@@ -466,7 +514,9 @@
     )(
         query_base,
         base_rows,
+        base_other,
         base_rows,
+        base_other,
         own_rank,
         all_rank,
         query_up,
@@ -483,62 +533,70 @@
     return lax.ppermute(block, ("groups", "ctx"), [(i, i ^ mask) for i in range(4 * PIECES)])
 
 
-def fetch_piece(packed, slots, corner, mirrored=None):
-    spread = lax.all_to_all(packed, "ctx", 0, 0)
-    arrived = []
-    for flip, mask in enumerate((0, PIECES, 2 * PIECES, 3 * PIECES)):
-        row = lax.dynamic_index_in_dim(slots, corner ^ flip, 0, keepdims=False)
-        block = lax.dynamic_index_in_dim(spread, row, 0, keepdims=False)
-        if mirrored is not None:
-            row = lax.dynamic_index_in_dim(slots, corner ^ flip ^ 1, 0, keepdims=False)
-            other = lax.dynamic_index_in_dim(spread, row, 0, keepdims=False)
-            block = jnp.concatenate([block, other[mirrored]])
-        arrived.append(swap(block, mask) if mask else block)
-    low = corner % 2 == 0
-    arrived = [jnp.where(low, arrived[q], arrived[q ^ 1]) for q in range(4)]
-    high = corner < 2
-    return jnp.stack([jnp.where(high, arrived[q], arrived[q ^ 2]) for q in range(4)])
-
-
 def direct_shards(
     normed_input, query_base, key_base, value_base, adapter_pool, stretch_adapter, adapter_owner
 ):
     plane = lax.axis_index("groups")
     index = lax.axis_index("ctx")
+    core = index % 2
+    half = index // PIECES
     tok_rows = normed_input.shape[0]
     ctx = lax.axis_size("ctx")
     seq = ctx * tok_rows
     blocks = [list(range(PIECES)), list(range(PIECES, 2 * PIECES))]
-    corner = 2 * plane + index // PIECES
-
-    elsewhere = swap(stretch_adapter, 2 * PIECES)
-    wanted = jnp.where(
-        plane == 0,
-        jnp.concatenate([stretch_adapter, elsewhere]),
-        jnp.concatenate([elsewhere, stretch_adapter]),
-    )
-    ids = jnp.arange(adapter_owner.shape[0], dtype=jnp.int32)
-    slots = jnp.sum(jnp.where(wanted[:, None] == ids[None, :], adapter_owner[None, :], 0), axis=1)
+    same_core = [list(range(c, ctx, 2)) for c in range(2)]
+    block_core = [list(range(s + c, s + PIECES, 2)) for s in (0, PIECES) for c in range(2)]
 
     moving = normed_input.reshape(tok_rows, PIECES, D // PIECES).transpose(1, 0, 2)
     moving = lax.all_to_all(moving, "ctx", 0, 0, axis_index_groups=blocks)
+    elsewhere = swap(stretch_adapter, 2 * PIECES)
     base_rows = lax.all_gather(
-        jnp.concatenate([key_base, value_base], 1), "ctx", axis=0, tiled=True
-    )
-
-    packed_rest = pack_row(adapter_pool, REST)
-    packed_down = pack_row(adapter_pool, DOWN, packed_rest)
-    rest = fetch_piece(packed_rest, slots, corner, slice(64, 80))
+        jnp.concatenate([key_base, value_base], 1), "ctx", axis_index_groups=same_core
+    )
+
+    packed_rest = pack_row(adapter_pool, REST, elsewhere)
+    packed_down = pack_row(adapter_pool, DOWN, packed_rest, moving)
+    ids = jnp.arange(adapter_owner.shape[0], dtype=jnp.int32)
+    slots = jnp.sum(
+        jnp.where(stretch_adapter[:, None] == ids[None, :], adapter_owner[None, :], 0), axis=1
+    )
+    near = (slots // PIECES) == half
+
+    def fetch(packed, mirrored=None):
+        spread = lax.all_to_all(packed, "ctx", 0, 0, axis_index_groups=blocks)
+        sent = pick(spread, stretch_adapter, elsewhere, adapter_owner, mirrored)
+        return [swap(block, flip * PIECES) if flip else block for flip, block in enumerate(sent)]
+
+    def settle(arrived, close):
+        own = jnp.where(close, arrived[0], arrived[1])
+        other = jnp.where(close, arrived[2], arrived[3])
+        low = plane == 0
+        return jnp.stack([jnp.where(low, own, other), jnp.where(low, other, own)])
+
+    close = jnp.where(half == 0, near[0], near[1])
+    far_close = jnp.where(half == 0, near[1], near[0])
+    rest = fetch(packed_rest, (128, 32))
+    mine = jnp.arange(rest[0].shape[0], dtype=jnp.int32)[:, None] < 544
+    rest = settle(rest, jnp.where(mine, close, far_close))
     rest, base_rows = lax.optimization_barrier((rest, base_rows))
-    rest = lax.all_gather(rest, "ctx", axis_index_groups=blocks)
-    query_up = rest[:, :, :64].reshape(ADAPTER_RANK, QH * HEAD_SIZE)
-    keyval_up = jnp.stack([rest[:, :, 64:80], rest[:, :, 272:]])
+    base_other = swap(base_rows, 1)
+    rest = lax.all_gather(rest, "ctx", axis_index_groups=block_core)
+    rest_other = swap(rest, 1)
+
+    def section(first, last):
+        same = rest[:, :, first:last]
+        other = rest_other[:, :, first:last]
+        return jnp.stack(
+            [jnp.where(core == 0, same, other), jnp.where(core == 0, other, same)], 1
+        )
+
+    query_up = section(0, 128).reshape(ADAPTER_RANK, QH * HEAD_SIZE)
+    keyval_up = jnp.stack([section(128, 160), section(544, 576)])
     keyval_up = keyval_up.reshape(2, ADAPTER_RANK, 2 * KEYVALUE_HEADS * HEAD_SIZE)
-    down_out = rest[:, :, 80:144].reshape(QH * HEAD_SIZE, ADAPTER_RANK)
-    up_out = rest[:, :, 144:272].reshape(ADAPTER_RANK, D)
-
-    down_slice = fetch_piece(packed_down, slots, corner)
-    down_slice = down_slice.reshape(D // PIECES, 3 * ADAPTER_RANK)
+    down_out = section(160, 288).reshape(QH * HEAD_SIZE, ADAPTER_RANK)
+    up_out = section(288, 544).reshape(ADAPTER_RANK, D)
+
+    down_slice = settle(fetch(packed_down), close).reshape(D // PIECES, 3 * ADAPTER_RANK)
     partial_rows = jnp.dot(
         moving.reshape(BLOCK_TOKENS, D // PIECES), down_slice, preferred_element_type=jnp.float32
     ).astype(jnp.bfloat16)
@@ -563,6 +621,7 @@
     return attend(
         query_base,
         base_rows,
+        base_other,
         own_rank,
         all_rank,
         query_up,

time: 193 us -> 225 us (1.17)
  Pallas kernels: 29.9 us -> 63.8 us
  waiting for transfers between devices: 72.6 us -> 84.1 us
  between operations: 27.4 us -> 16.9 us
  starting transfers between devices: 41.4 us -> 32.8 us
  other arithmetic: 6.77 us -> 11.4 us
    pallas_call x0 -> x2, Pallas kernels: none -> 45.4 us  [pick(): pl.pallas_call(partial(pick_kernel, mirrored), out_shape=(slab,) * 4, in_...]
    all_gather x2, waiting for transfers between devices: 0.02 us -> 28.9 us  [the longest x1 28.9 us: direct_shards(): rest = lax.all_gather(rest, 'ctx', axis_index_groups=block_core)]
    ppermute x7 -> x9, waiting for transfers between devices: 45.9 us -> 30.7 us  [swap(): lax.ppermute(block, ('groups', 'ctx'), [(i, i ^ mask) for i in range(4 *...]
    all_to_all x2, starting transfers between devices: 19.4 us -> 7.14 us  [fetch(): spread = lax.all_to_all(packed, 'ctx', 0, 0, axis_index_groups=blocks)]
    pallas_call x2, Pallas kernels: 18.5 us -> 6.72 us  [pack_row(): pl.pallas_call(partial(pack_kernel, sections), out_shape=jax.ShapeDtypeSt...]
    all_to_all x2, waiting for transfers between devices: 20.4 us -> 10.7 us  [fetch(): spread = lax.all_to_all(packed, 'ctx', 0, 0, axis_index_groups=blocks)]
    all_to_all x1, waiting for transfers between devices: 1.56 us -> 7.03 us  [direct_shards(): moving = lax.all_to_all(moving, 'ctx', 0, 0, axis_index_groups=blocks)]
    another operation x5 -> x12, other arithmetic: 1.65 us -> 6.35 us  [the longest x7 3.74 us: section(): jnp.stack([jnp.where(core == 0, same, other), jnp.where(core == 0, other,...]
  transfers between devices with their start and end apart: 14 -> 16, of which waited for: 9 -> 10; matrix products, arithmetic and copies ran while one was open for 9% -> 9% of each run, Pallas kernels for 10% -> 23%
where the time goes in v1:
time: 225 us
  waiting for transfers between devices  84.1 us (37%)
  Pallas kernels  63.8 us (28%)
  starting transfers between devices  32.8 us (15%)
  between operations  16.9 us (8%)
  local copies, waits for them, and re-layouts  14.6 us (6%)
  other arithmetic  11.4 us (5%)
    pallas_call x2, Pallas kernels, pick(): pl.pallas_call(partial(pick_kernel, mirrored), out_shape=(slab,) * 4, in_...  45.4 us
    ppermute x9, waiting for transfers between devices, swap(): lax.ppermute(block, ('groups', 'ctx'), [(i, i ^ mask) for i in range(4 *...  30.7 us
    all_gather x1, waiting for transfers between devices, direct_shards(): rest = lax.all_gather(rest, 'ctx', axis_index_groups=block_core)  28.9 us
    pallas_call x1, Pallas kernels, attend(): pl.pallas_call(attend_kernel, grid=(KEYVALUE_HEADS,), out_shape=(jax.Shap...  11.6 us
    all_to_all x2, waiting for transfers between devices, fetch(): spread = lax.all_to_all(packed, 'ctx', 0, 0, axis_index_groups=blocks)  10.7 us
    ppermute x9, starting transfers between devices, swap(): lax.ppermute(block, ('groups', 'ctx'), [(i, i ^ mask) for i in range(4 *...  10.5 us
    all_to_all x2, starting transfers between devices, fetch(): spread = lax.all_to_all(packed, 'ctx', 0, 0, axis_index_groups=blocks)  7.14 us
    all_to_all x1, waiting for transfers between devices, direct_shards(): moving = lax.all_to_all(moving, 'ctx', 0, 0, axis_index_groups=blocks)  7.03 us
  transfers between devices with their start and end apart: 16, of which 10 were waited for; matrix products, arithmetic and copies ran while one was open for 9% of the time, Pallas kernels for 23%

profile of v1, /device:TPU:0, one launch (start us, length us, event | category | flops | bytes accessed | tf_op | source)
XLA Modules:
  0.0 225.1 jit_solution(11313530729012235850)
XLA Ops:
  7.2 2.3 %copy.37 = bf16[8,8,8,1024]{3,2,0,1:T(8,128)(2,1)} copy(bf16[8,8,8,1024]{3,2,1,0:T(8,128)(2,1)} %bitcast.67) | data formatting | bytes 2097152 | tf_op jit(solution)/shard_map/reshape | solution.py:550
  9.5 5.4 %all-to-all-start.1 = ((bf16[8,64,1024]{2,1,0:T(8,128)(2,1)}), bf16[8,64,1024]{2,1,0:T(8,128)(2,1)S(1)}, u32[]{:S(2)}, u32[]{:S(2)}) async-start(bf16[8,64,1024]{2,1,0:T(8,128)(2,1)} %bitcast.57), calls=%async_computation.1 | async-start | bytes 2097152 | tf_op jit(solution)/shard_map/all_to_all | solution.py:551
  14.8 1.6 collective-permute-start
  16.4 2.0 collective-permute-done.refs_0_.there
  18.4 0.5 copy-done.13
  18.9 3.3 %shard_map.86.refs_0_ = bf16[8,544,128]{2,1,0:T(8,128)(2,1)} custom-call(bf16[1,2686976]{1,0:T(2,128)(2,1)} %pool.3, s32[2]{0:T(128)} %copy-done.13), custom_call_target="tpu_custom_call" | custom-call | bytes 8388608 | tf_op jit(solution)/shard_map/pallas_call | solution.py:314
  22.2 0.0 copy-start.12
  22.2 7.0 %all-to-all-done.1.refs_1_ = bf16[8,64,1024]{2,1,0:T(8,128)(2,1)S(1)} async-done(((bf16[8,64,1024]{2,1,0:T(8,128)(2,1)}), bf16[8,64,1024]{2,1,0:T(8,128)(2,1)S(1)}, u32[]{:S(2)}, u32[]{:S(2)}) %all-to-all-start.1) | async-done | bytes 1048608 | tf_op jit(solution)/shard_map/all_to_all | solution.py:551
  29.3 3.6 %all-to-all-start = ((bf16[8,544,128]{2,1,0:T(8,128)(2,1)}), bf16[8,544,128]{2,1,0:T(8,128)(2,1)S(1)}, u32[]{:S(2)}, u32[]{:S(2)}) async-start(bf16[8,544,128]{2,1,0:T(8,128)(2,1)} %shard_map.86.refs_0_), calls=%async_computation | async-start | bytes 2228224 | tf_op jit(solution)/shard_map/all_to_all | solution.py:566
  32.8 0.0 all-gather.5.cloned.1.call-start
  32.9 0.7 pad_maximum_fusion.8
  33.6 0.0 all-gather.5.cloned.1.call-update
  33.6 0.2 fusion.3
  33.8 3.5 %shard_map.88 = bf16[8,768,128]{2,1,0:T(8,128)(2,1)} custom-call(bf16[1,2686976]{1,0:T(2,128)(2,1)} %pool.3, bf16[8,544,128]{2,1,0:T(8,128)(2,1)} %shard_map.86.refs_0_, bf16[8,64,1024]{2,1,0:T(8,128)(2,1)} %copy-done), custom_call_target="tpu_custom_call" | custom-call | bytes 8388608 | tf_op jit(solution)/shard_map/pallas_call | solution.py:314
  37.3 10.7 %all-to-all-done.spread = bf16[8,544,128]{2,1,0:T(8,128)(2,1)S(1)} async-done(((bf16[8,544,128]{2,1,0:T(8,128)(2,1)}), bf16[8,544,128]{2,1,0:T(8,128)(2,1)S(1)}, u32[]{:S(2)}, u32[]{:S(2)}) %all-to-all-start) | async-done | bytes 1114144 | tf_op jit(solution)/shard_map/all_to_all | solution.py:566
  47.9 1.0 copy-done.3
  48.9 3.6 %all-to-all-start.2 = ((bf16[8,768,128]{2,1,0:T(8,128)(2,1)}), bf16[8,768,128]{2,1,0:T(8,128)(2,1)S(1)}, u32[]{:S(2)}, u32[]{:S(2)}) async-start(bf16[8,768,128]{2,1,0:T(8,128)(2,1)} %shard_map.88), calls=%async_computation.2 | async-start | bytes 3145728 | tf_op jit(solution)/shard_map/all_to_all | solution.py:566
  52.5 0.0 all-gather.7.cloned.1.call-start
  52.6 19.7 %shard_map.87 = (bf16[576,128]{1,0:T(8,128)(2,1)}, bf16[576,128]{1,0:T(8,128)(2,1)}, bf16[576,128]{1,0:T(8,128)(2,1)}, bf16[576,128]{1,0:T(8,128)(2,1)}) custom-call(s32[2]{0:T(128)} %here.3, s32[2]{0:T(128)} %copy-done.13, s32[16]{0:T(128)} %owner.3, bf16[8,544,128]{2,1,0:T(8,128)(2,1)} %copy-done.3), custom_call_target="tpu_custom_call" | custom-call | bytes 2097152 | tf_op jit(solution)/shard_map/pallas_call | solution.py:359
  72.3 2.7 %collective-permute-start.1 = (bf16[576,128]{1,0:T(8,128)(2,1)}, bf16[576,128]{1,0:T(8,128)(2,1)S(1)}, u32[]{:S(2)}, u32[]{:S(2)}) collective-permute-start(bf16[576,128]{1,0:T(8,128)(2,1)} %get-tuple-element.13), channel_id=1, source_target_pairs={{0,8},{1,9},{2,10},{3,11},{4,12},{5,13},{6,14},{7,15},{8,0},{9,1},... | collective-permute-start | bytes 442376 | tf_op jit(solution)/shard_map/ppermute | solution.py:533
  75.0 1.6 collective-permute-start.2
  76.6 0.2 collective-permute-start.3
  76.8 0.7 fusion.5
  79.9 9.7 %collective-permute-done.1 = bf16[576,128]{1,0:T(8,128)(2,1)S(1)} collective-permute-done((bf16[576,128]{1,0:T(8,128)(2,1)}, bf16[576,128]{1,0:T(8,128)(2,1)S(1)}, u32[]{:S(2)}, u32[]{:S(2)}) %collective-permute-start.1) | collective-permute-done | bytes 147488 | tf_op jit(solution)/shard_map/ppermute | solution.py:533
  89.7 4.6 %collective-permute-done.3 = bf16[576,128]{1,0:T(8,128)(2,1)S(1)} collective-permute-done((bf16[576,128]{1,0:T(8,128)(2,1)}, bf16[576,128]{1,0:T(8,128)(2,1)S(1)}, u32[]{:S(2)}, u32[]{:S(2)}) %collective-permute-start.3) | collective-permute-done | bytes 147488 | tf_op jit(solution)/shard_map/ppermute | solution.py:533
  94.3 1.1 select_bitcast_fusion.9
  95.4 0.7 pad_maximum_fusion.6
  96.1 0.0 all-gather.7.cloned.1.call-update
  96.1 28.9 %all-gather.7.cloned.1.call-done = bf16[8,576,128]{2,1,0:T(8,128)(2,1)} async-done(((bf16[2,576,128]{2,1,0:T(8,128)(2,1)}), bf16[8,576,128]{2,1,0:T(8,128)(2,1)}) %all-gather.7.cloned.1.call-update) | async-done | bytes 1179664 | tf_op jit(solution)/shard_map/all_gather | solution.py:583
  125.0 1.2 copy-done.2
  126.2 25.7 %shard_map.89 = (bf16[768,128]{1,0:T(8,128)(2,1)}, bf16[768,128]{1,0:T(8,128)(2,1)}, bf16[768,128]{1,0:T(8,128)(2,1)}, bf16[768,128]{1,0:T(8,128)(2,1)}) custom-call(s32[2]{0:T(128)} %here.3, s32[2]{0:T(128)} %copy-done.13, s32[16]{0:T(128)} %owner.3, bf16[8,768,128]{2,1,0:T(8,128)(2,1)} %copy-done.2), custom_call_target="tpu_custom_call" | custom-call | bytes 2097152 | tf_op jit(solution)/shard_map/pallas_call | solution.py:359
  151.9 2.5 %collective-permute-start.5 = (bf16[768,128]{1,0:T(8,128)(2,1)}, bf16[768,128]{1,0:T(8,128)(2,1)S(1)}, u32[]{:S(2)}, u32[]{:S(2)}) collective-permute-start(bf16[768,128]{1,0:T(8,128)(2,1)} %get-tuple-element.18), channel_id=1, source_target_pairs={{0,8},{1,9},{2,10},{3,11},{4,12},{5,13},{6,14},{7,15},{8,0},{9,1},... | collective-permute-start | bytes 589832 | tf_op jit(solution)/shard_map/ppermute | solution.py:533
  154.4 1.5 collective-permute-start.6
  155.9 0.5 collective-permute-start.7
  156.4 1.9 fusion.1
  158.3 1.3 pad_maximum_fusion.2
  159.6 9.6 %collective-permute-done.5 = bf16[768,128]{1,0:T(8,128)(2,1)S(1)} collective-permute-done((bf16[768,128]{1,0:T(8,128)(2,1)}, bf16[768,128]{1,0:T(8,128)(2,1)S(1)}, u32[]{:S(2)}, u32[]{:S(2)}) %collective-permute-start.5) | collective-permute-done | bytes 196640 | tf_op jit(solution)/shard_map/ppermute | solution.py:533
  169.2 4.7 %collective-permute-done.7 = bf16[768,128]{1,0:T(8,128)(2,1)S(1)} collective-permute-done((bf16[768,128]{1,0:T(8,128)(2,1)}, bf16[768,128]{1,0:T(8,128)(2,1)S(1)}, u32[]{:S(2)}, u32[]{:S(2)}) %collective-permute-start.7) | collective-permute-done | bytes 196640 | tf_op jit(solution)/shard_map/ppermute | solution.py:533
  173.9 0.7 copy-done.10
  174.7 1.2 reshape.55
  175.9 1.5 fusion
  177.4 0.8 copy.29
  178.3 4.0 %all-to-all-start.3 = ((bf16[8,64,192]{2,1,0:T(8,128)(2,1)}), bf16[8,64,192]{2,1,0:T(8,128)(2,1)}, u32[]{:S(2)}, u32[]{:S(2)}) async-start(bf16[8,64,192]{2,1,0:T(8,128)(2,1)} %bitcast.10), calls=%async_computation.3 | async-start | bytes 524288 | tf_op jit(solution)/shard_map/all_to_all | solution.py:603
  182.3 1.3 select_bitcast_fusion.1
  183.6 0.1 pad_maximum_fusion
  183.7 0.1 copy.34
  183.8 1.3 reshape.61.up_out
  185.1 1.3 select_bitcast_fusion.3
  186.4 0.1 pad_maximum_fusion.4
  186.4 1.4 reshape.60.down_out
  187.9 0.5 all-to-all-done.3
  188.4 1.0 reduce_sum.22.own_rank
  189.4 0.1 slice.54
  189.5 0.8 broadcast_in_dim.48
  190.2 5.6 %all-to-all-start.4 = ((bf16[16,64,128]{2,1,0:T(8,128)(2,1)}), bf16[16,64,128]{2,1,0:T(8,128)(2,1)S(1)}, u32[]{:S(2)}, u32[]{:S(2)}) async-start(bf16[16,64,128]{2,1,0:T(8,128)(2,1)} %broadcast_in_dim.48), calls=%async_computation.4 | async-start | bytes 524288 | tf_op jit(solution)/shard_map/all_to_all | solution.py:612
  195.9 1.0 select_bitcast_fusion.13
  196.9 0.1 stack.84
  197.0 0.7 stack.88
  197.7 0.1 pad_maximum_fusion.1
  197.8 1.0 reshape.59.query_up
  198.8 0.7 pad_maximum_fusion.7.key_up.value_up
  199.6 6.4 %all-to-all-done.4 = bf16[16,64,128]{2,1,0:T(8,128)(2,1)S(1)} async-done(((bf16[16,64,128]{2,1,0:T(8,128)(2,1)}), bf16[16,64,128]{2,1,0:T(8,128)(2,1)S(1)}, u32[]{:S(2)}, u32[]{:S(2)}) %all-to-all-start.4) | async-done | bytes 262176 | tf_op jit(solution)/shard_map/all_to_all | solution.py:612
  205.9 0.7 copy-done.6
  206.6 11.6 %shard_map.90 = (bf16[64,4096]{1,0:T(8,128)(2,1)}, bf16[64,8192]{1,0:T(8,128)(2,1)}) custom-call(bf16[64,4096]{1,0:T(8,128)(2,1)} %query_block.1, bf16[8,64,1024]{2,1,0:T(8,128)(2,1)} %bitcast.59, bf16[8,64,1024]{2,1,0:T(8,128)(2,1)} %copy-done.5, bf16[8,64,1024]{2,1,0:T(8,128)(2,1)} %bitcast.60, bf16[8,64,1024]{2,1,0:T(8,128)(2,1)} %copy-done.5, ...), custom_call_target="tpu_custom_call" | custom-call | flops 1073741824 | bytes 10485760 | tf_op jit(solution)/shard_map/pallas_call | solution.py:476
  (44 shorter events, 0.3 us)
Async XLA Ops:
  9.4 5.4 %copy-start.14 = (s32[2]{0:T(128)S(1)}, s32[2]{0:T(128)}, u32[]{:S(2)}) copy-start(s32[2]{0:T(128)} %here.3) | copy-start | bytes 28
  9.5 19.8 %all-to-all-start.1 = ((bf16[8,64,1024]{2,1,0:T(8,128)(2,1)}), bf16[8,64,1024]{2,1,0:T(8,128)(2,1)S(1)}, u32[]{:S(2)}, u32[]{:S(2)}) async-start(bf16[8,64,1024]{2,1,0:T(8,128)(2,1)} %bitcast.57), calls=%async_computation.1 | async-start | bytes 2097152 | tf_op jit(solution)/shard_map/all_to_all | solution.py:551
  14.8 3.6 %collective-permute-start = (s32[2]{0:T(128)S(1)}, s32[2]{0:T(128)S(1)}, u32[]{:S(2)}, u32[]{:S(2)}) collective-permute-start(s32[2]{0:T(128)S(1)} %copy-done.14), channel_id=1, source_target_pairs={{0,16},{1,17},{2,18},{3,19},{4,20},{5,21},{6,22},{7,23},{8,24},{9,... | collective-permute-start | bytes 32 | tf_op jit(solution)/shard_map/ppermute | solution.py:533
  18.4 0.5 copy-start.13
  22.2 10.7 %copy-start.11 = (bf16[64,512]{1,0:T(8,128)(2,1)S(1)}, bf16[64,512]{1,0:T(8,128)(2,1)}, u32[]{:S(2)}) copy-start(bf16[64,512]{1,0:T(8,128)(2,1)} %param.10) | copy-start | bytes 196612
  22.2 10.7 %copy-start.12 = (bf16[64,512]{1,0:T(8,128)(2,1)S(1)}, bf16[64,512]{1,0:T(8,128)(2,1)}, u32[]{:S(2)}) copy-start(bf16[64,512]{1,0:T(8,128)(2,1)} %param.9) | copy-start | bytes 196612
  22.2 11.4 %copy-start.15 = (s32[16]{0:T(128)S(1)}, s32[16]{0:T(128)}, u32[]{:S(2)}) copy-start(s32[16]{0:T(128)} %owner.3) | copy-start | bytes 196
  29.3 4.3 %copy-start = (bf16[8,64,1024]{2,1,0:T(8,128)(2,1)}, bf16[8,64,1024]{2,1,0:T(8,128)(2,1)S(1)}, u32[]{:S(2)}) copy-start(bf16[8,64,1024]{2,1,0:T(8,128)(2,1)S(1)} %all-to-all-done.1.refs_1_) | copy-start | bytes 3145732
  29.3 18.7 %all-to-all-start = ((bf16[8,544,128]{2,1,0:T(8,128)(2,1)}), bf16[8,544,128]{2,1,0:T(8,128)(2,1)S(1)}, u32[]{:S(2)}, u32[]{:S(2)}) async-start(bf16[8,544,128]{2,1,0:T(8,128)(2,1)} %shard_map.86.refs_0_), calls=%async_computation | async-start | bytes 2228224 | tf_op jit(solution)/shard_map/all_to_all | solution.py:566
  32.8 63.3 %all-gather.5.cloned.1.call-start = ((), (), s32[]{:S(2)}) async-start(), calls=%async_computation.5 | async-start | bytes 1179648 | tf_op jit(solution)/shard_map/all_gather | solution.py:553
  47.9 1.0 copy-start.3
  48.9 76.1 %all-to-all-start.2 = ((bf16[8,768,128]{2,1,0:T(8,128)(2,1)}), bf16[8,768,128]{2,1,0:T(8,128)(2,1)S(1)}, u32[]{:S(2)}, u32[]{:S(2)}) async-start(bf16[8,768,128]{2,1,0:T(8,128)(2,1)} %shard_map.88), calls=%async_computation.2 | async-start | bytes 3145728 | tf_op jit(solution)/shard_map/all_to_all | solution.py:566
  52.5 72.5 %all-gather.7.cloned.1.call-start = ((), (), s32[]{:S(2)}) async-start(), calls=%async_computation.6 | async-start | bytes 1474560 | tf_op jit(solution)/shard_map/all_gather | solution.py:583
  72.3 17.3 %collective-permute-start.1 = (bf16[576,128]{1,0:T(8,128)(2,1)}, bf16[576,128]{1,0:T(8,128)(2,1)S(1)}, u32[]{:S(2)}, u32[]{:S(2)}) collective-permute-start(bf16[576,128]{1,0:T(8,128)(2,1)} %get-tuple-element.13), channel_id=1, source_target_pairs={{0,8},{1,9},{2,10},{3,11},{4,12},{5,13},{6,14},{7,15},{8,0},{9,1},... | collective-permute-start | bytes 442376 | tf_op jit(solution)/shard_map/ppermute | solution.py:533
  75.0 14.7 %collective-permute-start.2 = (bf16[576,128]{1,0:T(8,128)(2,1)}, bf16[576,128]{1,0:T(8,128)(2,1)S(1)}, u32[]{:S(2)}, u32[]{:S(2)}) collective-permute-start(bf16[576,128]{1,0:T(8,128)(2,1)} %get-tuple-element.14), channel_id=1, source_target_pairs={{0,16},{1,17},{2,18},{3,19},{4,20},{5,21},{6,22},{7,23},{8,24},{9,... | collective-permute-start | bytes 442376 | tf_op jit(solution)/shard_map/ppermute | solution.py:533
  76.6 17.7 %collective-permute-start.3 = (bf16[576,128]{1,0:T(8,128)(2,1)}, bf16[576,128]{1,0:T(8,128)(2,1)S(1)}, u32[]{:S(2)}, u32[]{:S(2)}) collective-permute-start(bf16[576,128]{1,0:T(8,128)(2,1)} %get-tuple-element.15), channel_id=1, source_target_pairs={{0,24},{1,25},{2,26},{3,27},{4,28},{5,29},{6,30},{7,31},{8,16},{9,... | collective-permute-start | bytes 442376 | tf_op jit(solution)/shard_map/ppermute | solution.py:533
  125.0 57.3 %collective-permute-start.8 = (bf16[4,2,576,128]{3,2,1,0:T(8,128)(2,1)}, bf16[4,2,576,128]{3,2,1,0:T(8,128)(2,1)}, u32[]{:S(2)}, u32[]{:S(2)}) collective-permute-start(bf16[4,2,576,128]{3,2,1,0:T(8,128)(2,1)} %bitcast.62), channel_id=1, source_target_pairs={{0,1},{1,0},{2,3},{3,2},{4,5},{5,4},{6,7},{7,6},{8,9},{9,8},{10,11... | collective-permute-start | bytes 3538952 | tf_op jit(solution)/shard_map/ppermute | solution.py:533
  125.0 1.2 copy-start.2
  151.9 17.3 %collective-permute-start.5 = (bf16[768,128]{1,0:T(8,128)(2,1)}, bf16[768,128]{1,0:T(8,128)(2,1)S(1)}, u32[]{:S(2)}, u32[]{:S(2)}) collective-permute-start(bf16[768,128]{1,0:T(8,128)(2,1)} %get-tuple-element.18), channel_id=1, source_target_pairs={{0,8},{1,9},{2,10},{3,11},{4,12},{5,13},{6,14},{7,15},{8,0},{9,1},... | collective-permute-start | bytes 589832 | tf_op jit(solution)/shard_map/ppermute | solution.py:533
  154.4 14.8 %collective-permute-start.6 = (bf16[768,128]{1,0:T(8,128)(2,1)}, bf16[768,128]{1,0:T(8,128)(2,1)S(1)}, u32[]{:S(2)}, u32[]{:S(2)}) collective-permute-start(bf16[768,128]{1,0:T(8,128)(2,1)} %get-tuple-element.19), channel_id=1, source_target_pairs={{0,16},{1,17},{2,18},{3,19},{4,20},{5,21},{6,22},{7,23},{8,24},{9,... | collective-permute-start | bytes 589832 | tf_op jit(solution)/shard_map/ppermute | solution.py:533
  155.9 18.1 %collective-permute-start.7 = (bf16[768,128]{1,0:T(8,128)(2,1)}, bf16[768,128]{1,0:T(8,128)(2,1)S(1)}, u32[]{:S(2)}, u32[]{:S(2)}) collective-permute-start(bf16[768,128]{1,0:T(8,128)(2,1)} %get-tuple-element.20), channel_id=1, source_target_pairs={{0,24},{1,25},{2,26},{3,27},{4,28},{5,29},{6,30},{7,31},{8,16},{9,... | collective-permute-start | bytes 589832 | tf_op jit(solution)/shard_map/ppermute | solution.py:533
  158.3 1.3 copy-start.4
  158.3 16.3 %copy-start.9 = (bf16[768,128]{1,0:T(8,128)(2,1)S(1)}, bf16[768,128]{1,0:T(8,128)(2,1)}, u32[]{:S(2)}) copy-start(bf16[768,128]{1,0:T(8,128)(2,1)} %get-tuple-element.17) | copy-start | bytes 589828
  159.6 40.0 %collective-permute-start.4 = (bf16[8,64,1024]{2,1,0:T(8,128)(2,1)S(1)}, bf16[8,64,1024]{2,1,0:T(8,128)(2,1)S(1)}, u32[]{:S(2)}, u32[]{:S(2)}) collective-permute-start(bf16[8,64,1024]{2,1,0:T(8,128)(2,1)S(1)} %bitcast.61), channel_id=1, source_target_pairs={{0,1},{1,0},{2,3},{3,2},{4,5},{5,4},{6,7},{7,6},{8,9},{9,8},{10,11... | collective-permute-start | bytes 3145736 | tf_op jit(solution)/shard_map/ppermute | solution.py:533
  173.9 0.7 copy-start.10
  174.6 1.3 copy-start.1
  178.3 10.1 %all-to-all-start.3 = ((bf16[8,64,192]{2,1,0:T(8,128)(2,1)}), bf16[8,64,192]{2,1,0:T(8,128)(2,1)}, u32[]{:S(2)}, u32[]{:S(2)}) async-start(bf16[8,64,192]{2,1,0:T(8,128)(2,1)} %bitcast.10), calls=%async_computation.3 | async-start | bytes 524288 | tf_op jit(solution)/shard_map/all_to_all | solution.py:603
  189.4 0.8 copy-start.8
  190.2 15.7 %all-to-all-start.4 = ((bf16[16,64,128]{2,1,0:T(8,128)(2,1)}), bf16[16,64,128]{2,1,0:T(8,128)(2,1)S(1)}, u32[]{:S(2)}, u32[]{:S(2)}) async-start(bf16[16,64,128]{2,1,0:T(8,128)(2,1)} %broadcast_in_dim.48), calls=%async_computation.4 | async-start | bytes 524288 | tf_op jit(solution)/shard_map/all_to_all | solution.py:612
  197.8 1.1 copy-start.7
  199.6 6.4 %copy-start.5 = (bf16[8,64,1024]{2,1,0:T(8,128)(2,1)}, bf16[8,64,1024]{2,1,0:T(8,128)(2,1)S(1)}, u32[]{:S(2)}) copy-start(bf16[8,64,1024]{2,1,0:T(8,128)(2,1)S(1)} %collective-permute-done.4.key_other.value_other) | copy-start | bytes 3145732
  205.9 0.7 copy-start.6
Sparse Core Ops, SparseCore 0:
  35.8 56.1 all-gather.4
  96.3 28.6 all-gather.6

commit v2 on v1

--- a/solution.py
+++ b/solution.py
@@ -360,10 +360,36 @@
         partial(pick_kernel, mirrored),
         out_shape=(slab,) * 4,
         in_specs=[pl.BlockSpec(memory_space=pltpu.SMEM)] * 3 + [pl.BlockSpec(memory_space=pl.ANY)],
-        out_specs=(pl.BlockSpec(memory_space=pl.ANY),) * 4,
+        out_specs=(pl.BlockSpec(memory_space=pltpu.VMEM),) * 4,
         scratch_shapes=[pltpu.SemaphoreType.DMA((4, 2))],
+        compiler_params=pltpu.CompilerParams(vmem_limit_bytes=16 << 20),
         cost_estimate=pl.CostEstimate(flops=0, bytes_accessed=2 << 20, transcendentals=0),
     )(here, there, owner, spread)
+
+
+def assemble_kernel(*refs):
+    pieces, out, sems = refs[:PIECES], refs[PIECES], refs[PIECES + 1]
+    seat = lax.rem(lax.axis_index("ctx"), PIECES)
+    copies = [
+        pltpu.make_async_copy(piece, out.at[seat ^ apart], sems.at[apart])
+        for apart, piece in enumerate(pieces)
+    ]
+    for copy in copies:
+        copy.start()
+    for copy in copies:
+        copy.wait()
+
+
+def assemble(pieces):
+    return pl.pallas_call(
+        assemble_kernel,
+        out_shape=jax.ShapeDtypeStruct((PIECES,) + pieces[0].shape, jnp.bfloat16),
+        in_specs=[pl.BlockSpec(memory_space=pl.ANY)] * PIECES,
+        out_specs=pl.BlockSpec(memory_space=pltpu.VMEM),
+        scratch_shapes=[pltpu.SemaphoreType.DMA((PIECES,))],
+        compiler_params=pltpu.CompilerParams(vmem_limit_bytes=16 << 20),
+        cost_estimate=pl.CostEstimate(flops=0, bytes_accessed=6 << 20, transcendentals=0),
+    )(*pieces)
 
 
 def attend_kernel(
@@ -545,25 +571,20 @@
     seq = ctx * tok_rows
     blocks = [list(range(PIECES)), list(range(PIECES, 2 * PIECES))]
     same_core = [list(range(c, ctx, 2)) for c in range(2)]
-    block_core = [list(range(s + c, s + PIECES, 2)) for s in (0, PIECES) for c in range(2)]
-
-    moving = normed_input.reshape(tok_rows, PIECES, D // PIECES).transpose(1, 0, 2)
-    moving = lax.all_to_all(moving, "ctx", 0, 0, axis_index_groups=blocks)
-    elsewhere = swap(stretch_adapter, 2 * PIECES)
+
     base_rows = lax.all_gather(
         jnp.concatenate([key_base, value_base], 1), "ctx", axis_index_groups=same_core
     )
-
-    packed_rest = pack_row(adapter_pool, REST, elsewhere)
-    packed_down = pack_row(adapter_pool, DOWN, packed_rest, moving)
+    elsewhere = swap(stretch_adapter, 2 * PIECES)
+    packed_rest = pack_row(adapter_pool, REST)
+    packed_down = pack_row(adapter_pool, DOWN, packed_rest, elsewhere)
     ids = jnp.arange(adapter_owner.shape[0], dtype=jnp.int32)
     slots = jnp.sum(
         jnp.where(stretch_adapter[:, None] == ids[None, :], adapter_owner[None, :], 0), axis=1
     )
     near = (slots // PIECES) == half
 
-    def fetch(packed, mirrored=None):
-        spread = lax.all_to_all(packed, "ctx", 0, 0, axis_index_groups=blocks)
+    def fetch(spread, mirrored=None):
         sent = pick(spread, stretch_adapter, elsewhere, adapter_owner, mirrored)
         return [swap(block, flip * PIECES) if flip else block for flip, block in enumerate(sent)]
 
@@ -575,28 +596,27 @@
 
     close = jnp.where(half == 0, near[0], near[1])
     far_close = jnp.where(half == 0, near[1], near[0])
-    rest = fetch(packed_rest, (128, 32))
+    spread_rest = lax.all_to_all(packed_rest, "ctx", 0, 0, axis_index_groups=blocks)
+    spread_down = lax.all_to_all(packed_down, "ctx", 0, 0, axis_index_groups=blocks)
+    moving = normed_input.reshape(tok_rows, PIECES, D // PIECES).transpose(1, 0, 2)
+    moving, spread_down = lax.optimization_barrier((moving, spread_down))
+    moving = lax.all_to_all(moving, "ctx", 0, 0, axis_index_groups=blocks)
+
+    rest = fetch(spread_rest, (128, 32))
     mine = jnp.arange(rest[0].shape[0], dtype=jnp.int32)[:, None] < 544
     rest = settle(rest, jnp.where(mine, close, far_close))
-    rest, base_rows = lax.optimization_barrier((rest, base_rows))
+    rest = [swap(rest, apart) if apart else rest for apart in (0, 2, 4, 6)]
+    rest = assemble([piece for block in rest for piece in (block, swap(block, 1))])
+    query_up = rest[:, :, :128].reshape(ADAPTER_RANK, QH * HEAD_SIZE)
+    keyval_up = jnp.stack([rest[:, :, 128:160], rest[:, :, 544:]])
+    keyval_up = keyval_up.reshape(2, ADAPTER_RANK, 2 * KEYVALUE_HEADS * HEAD_SIZE)
+    down_out = rest[:, :, 160:288].reshape(QH * HEAD_SIZE, ADAPTER_RANK)
+    up_out = rest[:, :, 288:544].reshape(ADAPTER_RANK, D)
+
+    arrived = fetch(spread_down)
+    arrived, base_rows = lax.optimization_barrier((arrived, base_rows))
     base_other = swap(base_rows, 1)
-    rest = lax.all_gather(rest, "ctx", axis_index_groups=block_core)
-    rest_other = swap(rest, 1)
-
-    def section(first, last):
-        same = rest[:, :, first:last]
-        other = rest_other[:, :, first:last]
-        return jnp.stack(
-            [jnp.where(core == 0, same, other), jnp.where(core == 0, other, same)], 1
-        )
-
-    query_up = section(0, 128).reshape(ADAPTER_RANK, QH * HEAD_SIZE)
-    keyval_up = jnp.stack([section(128, 160), section(544, 576)])
-    keyval_up = keyval_up.reshape(2, ADAPTER_RANK, 2 * KEYVALUE_HEADS * HEAD_SIZE)
-    down_out = section(160, 288).reshape(QH * HEAD_SIZE, ADAPTER_RANK)
-    up_out = section(288, 544).reshape(ADAPTER_RANK, D)
-
-    down_slice = settle(fetch(packed_down), close).reshape(D // PIECES, 3 * ADAPTER_RANK)
+    down_slice = settle(arrived, close).reshape(D // PIECES, 3 * ADAPTER_RANK)
     partial_rows = jnp.dot(
         moving.reshape(BLOCK_TOKENS, D // PIECES), down_slice, preferred_element_type=jnp.float32
     ).astype(jnp.bfloat16)

time: 225 us -> 177 us (0.79)
  waiting for transfers between devices: 84.1 us -> 41.2 us
  Pallas kernels: 63.8 us -> 22 us
  blocking collectives: 0 us -> 24.2 us
  local copies, waits for them, and re-layouts: 14.6 us -> 23.2 us
  starting transfers between devices: 32.8 us -> 40 us
  other arithmetic: 11.4 us -> 7.05 us
    pallas_call x2, Pallas kernels: 45.4 us -> 3.1 us  [pick(): pl.pallas_call(partial(pick_kernel, mirrored), out_shape=(slab,) * 4, in_...]
    all_gather x1 -> x0, waiting for transfers between devices: 28.9 us -> none  [direct_shards(): rest = lax.all_gather(rest, 'ctx', axis_index_groups=block_core)]
    all_to_all x0 -> x1, blocking collectives: none -> 24.2 us  [direct_shards(): lax.all_to_all(packed_down, 'ctx', 0, 0, axis_index_groups=blocks)]
    ppermute x9 -> x15, starting transfers between devices: 10.5 us -> 20.6 us  [swap(): lax.ppermute(block, ('groups', 'ctx'), [(i, i ^ mask) for i in range(4 *...]
    all_to_all x1, waiting for transfers between devices: 7.03 us -> 0.01 us  [direct_shards(): moving = lax.all_to_all(moving, 'ctx', 0, 0, axis_index_groups=blocks)]
    all_to_all x1, waiting for transfers between devices: 6.35 us -> 0.12 us  [direct_shards(): lax.all_to_all(all_rank, 'ctx', 0, 0).reshape(seq, 2 * ADAPTER_RANK)]
    unnamed x32 -> x37, local copies, waits for them, and re-layouts: 4.11 us -> 9.79 us
    another operation x8 -> x1, other arithmetic: 4.46 us -> 0.74 us  [direct_shards(): keyval_up = jnp.stack([rest[:, :, 128:160], rest[:, :, 544:]])]
  transfers between devices with their start and end apart: 16 -> 20, of which waited for: 10 -> 6; matrix products, arithmetic and copies ran while one was open for 9% -> 14% of each run, Pallas kernels for 23% -> 4%
where the time goes in v2:
time: 177 us; the launch traced here: 176 us
  waiting for transfers between devices  41.2 us (23%)
  starting transfers between devices  40 us (23%)
  blocking collectives  24.2 us (14%)
  local copies, waits for them, and re-layouts  23.2 us (13%)
  Pallas kernels  22 us (12%)
  between operations  16.9 us (10%)
  other arithmetic  7.05 us (4%)
    ppermute x15, waiting for transfers between devices, swap(): lax.ppermute(block, ('groups', 'ctx'), [(i, i ^ mask) for i in range(4 *...  29.7 us
    all_to_all x1, blocking collectives, direct_shards(): lax.all_to_all(packed_down, 'ctx', 0, 0, axis_index_groups=blocks)  24.2 us
    ppermute x15, starting transfers between devices, swap(): lax.ppermute(block, ('groups', 'ctx'), [(i, i ^ mask) for i in range(4 *...  20.6 us
    pallas_call x1, Pallas kernels, attend(): pl.pallas_call(attend_kernel, grid=(KEYVALUE_HEADS,), out_shape=(jax.Shap...  11.6 us
    all_to_all x1, waiting for transfers between devices, direct_shards(): lax.all_to_all(packed_rest, 'ctx', 0, 0, axis_index_groups=blocks)  11.4 us
    unnamed x37, local copies, waits for them, and re-layouts  9.79 us
    pallas_call x2, Pallas kernels, pack_row(): pl.pallas_call(partial(pack_kernel, sections), out_shape=jax.ShapeDtypeSt...  6.7 us
    all_to_all x1, starting transfers between devices, direct_shards(): lax.all_to_all(all_rank, 'ctx', 0, 0).reshape(seq, 2 * ADAPTER_RANK)  6.43 us
  transfers between devices with their start and end apart: 20, of which 6 were waited for; matrix products, arithmetic and copies ran while one was open for 14% of the time, Pallas kernels for 4%

profile of v2, /device:TPU:0, one launch (start us, length us, event | category | flops | bytes accessed | tf_op | source)
XLA Modules:
  0.0 176.3 jit_solution(14267439967556823105)
XLA Ops:
  7.2 3.0 %collective-permute-start = (s32[2]{0:T(128)}, s32[2]{0:T(128)S(1)}, u32[]{:S(2)}, u32[]{:S(2)}) collective-permute-start(s32[2]{0:T(128)} %here.3), channel_id=1, source_target_pairs={{0,16},{1,17},{2,18},{3,19},{4,20},{5,21},{6,22},{7,23},{8,24},{9,... | collective-permute-start | bytes 32 | tf_op jit(solution)/shard_map/ppermute | solution.py:559
  10.2 3.2 %shard_map.86.refs_0_ = bf16[8,544,128]{2,1,0:T(8,128)(2,1)} custom-call(bf16[1,2686976]{1,0:T(2,128)(2,1)} %pool.3), custom_call_target="tpu_custom_call" | custom-call | bytes 8388608 | tf_op jit(solution)/shard_map/pallas_call | solution.py:314
  13.5 0.5 copy-done.8
  14.0 3.5 %shard_map.87 = bf16[8,768,128]{2,1,0:T(8,128)(2,1)} custom-call(bf16[1,2686976]{1,0:T(2,128)(2,1)} %pool.3, bf16[8,544,128]{2,1,0:T(8,128)(2,1)} %shard_map.86.refs_0_, s32[2]{0:T(128)} %copy-done.8), custom_call_target="tpu_custom_call" | custom-call | bytes 8388608 | tf_op jit(solution)/shard_map/pallas_call | solution.py:314
  17.5 24.2 %all_to_all.25.spread = bf16[8,768,128]{2,1,0:T(8,128)(2,1)S(1)} all-to-all(bf16[8,768,128]{2,1,0:T(8,128)(2,1)} %shard_map.87), channel_id=1, replica_groups={{0,1,2,3,4,5,6,7},{8,9,10,11,12,13,14,15},{16,17,18,19,20,21,22,23},{24..., dimensions={0} | all-to-all | bytes 3145728 | tf_op jit(solution)/shard_map/all_to_all | solution.py:600
  41.7 3.6 %all-to-all-start.4 = ((bf16[8,544,128]{2,1,0:T(8,128)(2,1)}), bf16[8,544,128]{2,1,0:T(8,128)(2,1)S(1)}, u32[]{:S(2)}, u32[]{:S(2)}) async-start(bf16[8,544,128]{2,1,0:T(8,128)(2,1)} %shard_map.86.refs_0_), calls=%async_computation.4 | async-start | bytes 2228224 | tf_op jit(solution)/shard_map/all_to_all | solution.py:599
  45.3 0.0 all-gather.3.cloned.1.call-start
  45.3 0.7 pad_maximum_fusion.5
  46.0 0.0 all-gather.3.cloned.1.call-update
  46.0 1.8 %copy.16 = bf16[8,8,8,1024]{3,2,1,0:T(8,128)(2,1)S(1)} copy(bf16[8,8,8,1024]{3,1,2,0:T(8,128)(2,1)} %bitcast.34) | data formatting | bytes 2097152
  47.9 1.5 copy.14
  49.4 11.4 %all-to-all-done.4.spread = bf16[8,544,128]{2,1,0:T(8,128)(2,1)S(1)} async-done(((bf16[8,544,128]{2,1,0:T(8,128)(2,1)}), bf16[8,544,128]{2,1,0:T(8,128)(2,1)S(1)}, u32[]{:S(2)}, u32[]{:S(2)}) %all-to-all-start.4) | async-done | bytes 1114144 | tf_op jit(solution)/shard_map/all_to_all | solution.py:599
  60.8 4.2 %all-to-all-start.1 = ((bf16[8,64,1024]{2,1,0:T(8,128)(2,1)}), bf16[8,64,1024]{2,1,0:T(8,128)(2,1)}, u32[]{:S(2)}, u32[]{:S(2)}) async-start(bf16[8,64,1024]{2,1,0:T(8,128)(2,1)} %copy.14), calls=%async_computation.1 | async-start | bytes 2097152 | tf_op jit(solution)/shard_map/all_to_all | solution.py:603
  65.1 0.2 fusion.2
  65.3 1.4 shard_map.89
  66.8 3.0 %collective-permute-start.5 = (bf16[576,128]{1,0:T(8,128)(2,1)S(1)}, bf16[576,128]{1,0:T(8,128)(2,1)S(1)}, u32[]{:S(2)}, u32[]{:S(2)}) collective-permute-start(bf16[576,128]{1,0:T(8,128)(2,1)S(1)} %get-tuple-element.29), channel_id=1, source_target_pairs={{0,8},{1,9},{2,10},{3,11},{4,12},{5,13},{6,14},{7,15},{8,0},{9,1},... | collective-permute-start | bytes 442376 | tf_op jit(solution)/shard_map/ppermute | solution.py:559
  69.8 1.5 collective-permute-start.7
  71.3 0.6 fusion.6
  74.4 12.3 %collective-permute-done.5 = bf16[576,128]{1,0:T(8,128)(2,1)S(1)} collective-permute-done((bf16[576,128]{1,0:T(8,128)(2,1)S(1)}, bf16[576,128]{1,0:T(8,128)(2,1)S(1)}, u32[]{:S(2)}, u32[]{:S(2)}) %collective-permute-start.5) | collective-permute-done | bytes 147488 | tf_op jit(solution)/shard_map/ppermute | solution.py:559
  86.7 6.0 %collective-permute-done.7 = bf16[576,128]{1,0:T(8,128)(2,1)S(1)} collective-permute-done((bf16[576,128]{1,0:T(8,128)(2,1)S(1)}, bf16[576,128]{1,0:T(8,128)(2,1)S(1)}, u32[]{:S(2)}, u32[]{:S(2)}) %collective-permute-start.7) | collective-permute-done | bytes 147488 | tf_op jit(solution)/shard_map/ppermute | solution.py:559
  92.7 0.1 select_bitcast_fusion.3
  92.9 2.1 %collective-permute-start.9 = (bf16[2,576,128]{2,1,0:T(8,128)(2,1)S(1)}, bf16[2,576,128]{2,1,0:T(8,128)(2,1)S(1)}, u32[]{:S(2)}, u32[]{:S(2)}) collective-permute-start(bf16[2,576,128]{2,1,0:T(8,128)(2,1)S(1)} %pad_maximum_fusion.3.refs_0_), channel_id=1, source_target_pairs={{0,2},{1,3},{2,0},{3,1},{4,6},{5,7},{6,4},{7,5},{8,10},{9,11},{10,... | collective-permute-start | bytes 884744 | tf_op jit(solution)/shard_map/ppermute | solution.py:559
  95.1 2.4 %collective-permute-start.11 = (bf16[2,576,128]{2,1,0:T(8,128)(2,1)S(1)}, bf16[2,576,128]{2,1,0:T(8,128)(2,1)S(1)}, u32[]{:S(2)}, u32[]{:S(2)}) collective-permute-start(bf16[2,576,128]{2,1,0:T(8,128)(2,1)S(1)} %pad_maximum_fusion.3.refs_0_), channel_id=1, source_target_pairs={{0,4},{1,5},{2,6},{3,7},{4,0},{5,1},{6,2},{7,3},{8,12},{9,13},{10,... | collective-permute-start | bytes 884744 | tf_op jit(solution)/shard_map/ppermute | solution.py:559
  97.5 1.7 shard_map.88
  99.1 1.0 collective-permute-start.1
  100.1 3.0 %collective-permute-start.2 = (bf16[768,128]{1,0:T(8,128)(2,1)S(1)}, bf16[768,128]{1,0:T(8,128)(2,1)}, u32[]{:S(2)}, u32[]{:S(2)}) collective-permute-start(bf16[768,128]{1,0:T(8,128)(2,1)S(1)} %get-tuple-element.20), channel_id=1, source_target_pairs={{0,16},{1,17},{2,18},{3,19},{4,20},{5,21},{6,22},{7,23},{8,24},{9,... | collective-permute-start | bytes 589832 | tf_op jit(solution)/shard_map/ppermute | solution.py:559
  103.2 3.4 %collective-permute-start.3 = (bf16[768,128]{1,0:T(8,128)(2,1)S(1)}, bf16[768,128]{1,0:T(8,128)(2,1)S(1)}, u32[]{:S(2)}, u32[]{:S(2)}) collective-permute-start(bf16[768,128]{1,0:T(8,128)(2,1)S(1)} %get-tuple-element.21), channel_id=1, source_target_pairs={{0,24},{1,25},{2,26},{3,27},{4,28},{5,29},{6,30},{7,31},{8,16},{9,... | collective-permute-start | bytes 589832 | tf_op jit(solution)/shard_map/ppermute | solution.py:559
  106.6 7.2 %collective-permute-done.11.refs_4_ = bf16[2,576,128]{2,1,0:T(8,128)(2,1)S(1)} collective-permute-done((bf16[2,576,128]{2,1,0:T(8,128)(2,1)S(1)}, bf16[2,576,128]{2,1,0:T(8,128)(2,1)S(1)}, u32[]{:S(2)}, u32[]{:S(2)}) %collective-permute-start.11) | collective-permute-done | bytes 294944 | tf_op jit(solution)/shard_map/ppermute | solution.py:559
  113.8 4.1 %collective-permute-done.13.refs_6_ = bf16[2,576,128]{2,1,0:T(8,128)(2,1)S(1)} collective-permute-done((bf16[2,576,128]{2,1,0:T(8,128)(2,1)S(1)}, bf16[2,576,128]{2,1,0:T(8,128)(2,1)S(1)}, u32[]{:S(2)}, u32[]{:S(2)}) %collective-permute-start.13) | collective-permute-done | bytes 294944 | tf_op jit(solution)/shard_map/ppermute | solution.py:559
  117.9 0.5 collective-permute-start.12
  118.5 0.1 collective-permute-start.14
  118.5 0.7 copy-done.15
  119.2 1.0 select_bitcast_fusion.1
  120.2 0.3 reshape.56
  120.6 0.5 collective-permute-start.4
  121.1 1.7 convolution_convert_fusion
  122.8 0.8 copy.15
  123.7 5.2 %all-to-all-start.2 = ((bf16[8,64,192]{2,1,0:T(8,128)(2,1)}), bf16[8,64,192]{2,1,0:T(8,128)(2,1)}, u32[]{:S(2)}, u32[]{:S(2)}) async-start(bf16[8,64,192]{2,1,0:T(8,128)(2,1)} %bitcast.7), calls=%async_computation.2 | async-start | bytes 524288 | tf_op jit(solution)/shard_map/all_to_all | solution.py:623
  128.8 1.9 %fusion = (f32[1024,64]{1,0:T(8,128)S(1)}, f32[1024,64]{1,0:T(8,128)S(1)}, f32[1024,64]{1,0:T(8,128)S(1)}) fusion(f32[64]{0:T(128)S(1)} %multiply_power_fusion, f32[1024]{0:T(1024)S(1)} %iota_convert_fusion), kind=kLoop, calls=%fused_computation.12 | loop fusion | flops 131072 | bytes 790784 | tf_op jit(solution)/shard_map/neg | solution.py:640
  130.7 1.3 pad_maximum_fusion
  132.1 0.7 copy-done
  132.8 0.7 copy-done.2
  133.5 0.7 copy-done.4
  134.3 0.7 copy-done.6
  135.0 1.0 copy-done.1
  135.9 1.0 copy-done.3
  136.9 1.0 copy-done.5
  137.9 1.0 copy-done.7
  138.8 0.6 shard_map.90
  139.4 1.0 reduce_sum.22.own_rank
  140.4 0.1 slice.34
  140.5 0.8 broadcast_in_dim.45
  141.3 6.4 %all-to-all-start.3 = ((bf16[16,64,128]{2,1,0:T(8,128)(2,1)}), bf16[16,64,128]{2,1,0:T(8,128)(2,1)}, u32[]{:S(2)}, u32[]{:S(2)}) async-start(bf16[16,64,128]{2,1,0:T(8,128)(2,1)} %broadcast_in_dim.45), calls=%async_computation.3 | async-start | bytes 524288 | tf_op jit(solution)/shard_map/all_to_all | solution.py:632
  147.7 0.7 fusion.5
  148.4 0.1 slice.39
  148.5 1.0 stack.33
  149.5 1.6 stack.34
  151.1 1.1 fusion.4
  152.2 2.4 %reshape.60.down_out = bf16[4096,64]{1,0:T(8,128)(2,1)} reshape(bf16[8,2,128,128]{3,2,1,0:T(8,128)(2,1)} %get-tuple-element.32) | data formatting | bytes 1048576 | tf_op jit(solution)/shard_map/reshape | solution.py:613
  154.7 1.3 reshape.61.up_out
  155.9 1.0 reshape.59.query_up
  156.9 0.7 pad_maximum_fusion.4.key_up.value_up
  157.7 0.1 all-to-all-done.3
  157.8 11.6 %shard_map.91 = (bf16[64,4096]{1,0:T(8,128)(2,1)}, bf16[64,8192]{1,0:T(8,128)(2,1)}) custom-call(bf16[64,4096]{1,0:T(8,128)(2,1)} %query_block.1, bf16[8,64,1024]{2,1,0:T(8,128)(2,1)} %bitcast.31, bf16[8,64,1024]{2,1,0:T(8,128)(2,1)} %collective-permute-done.4.key_other.value_other, bf16[8,64,1024]{2,1,0:T(8,128)(2,1)} %bitcast.32, ...), custom_call_target="tpu_custom_call" | custom-call | flops 1073741824 | bytes 10485760 | tf_op jit(solution)/shard_map/pallas_call | solution.py:502
  (50 shorter events, 0.2 us)
Async XLA Ops:
  7.2 6.3 %collective-permute-start = (s32[2]{0:T(128)}, s32[2]{0:T(128)S(1)}, u32[]{:S(2)}, u32[]{:S(2)}) collective-permute-start(s32[2]{0:T(128)} %here.3), channel_id=1, source_target_pairs={{0,16},{1,17},{2,18},{3,19},{4,20},{5,21},{6,22},{7,23},{8,24},{9,... | collective-permute-start | bytes 32 | tf_op jit(solution)/shard_map/ppermute | solution.py:559
  13.5 0.5 copy-start.8
  17.5 27.9 %copy-start.16 = (bf16[64,512]{1,0:T(8,128)(2,1)S(1)}, bf16[64,512]{1,0:T(8,128)(2,1)}, u32[]{:S(2)}) copy-start(bf16[64,512]{1,0:T(8,128)(2,1)} %param.10) | copy-start | bytes 196612
  17.5 27.9 %copy-start.17 = (bf16[64,512]{1,0:T(8,128)(2,1)S(1)}, bf16[64,512]{1,0:T(8,128)(2,1)}, u32[]{:S(2)}) copy-start(bf16[64,512]{1,0:T(8,128)(2,1)} %param.9) | copy-start | bytes 196612
  41.7 19.1 %all-to-all-start.4 = ((bf16[8,544,128]{2,1,0:T(8,128)(2,1)}), bf16[8,544,128]{2,1,0:T(8,128)(2,1)S(1)}, u32[]{:S(2)}, u32[]{:S(2)}) async-start(bf16[8,544,128]{2,1,0:T(8,128)(2,1)} %shard_map.86.refs_0_), calls=%async_computation.4 | async-start | bytes 2228224 | tf_op jit(solution)/shard_map/all_to_all | solution.py:599
  45.3 73.3 %all-gather.3.cloned.1.call-start = ((), (), s32[]{:S(2)}) async-start(), calls=%async_computation.5 | async-start | bytes 1179648 | tf_op jit(solution)/shard_map/all_gather | solution.py:575
  47.9 17.2 %copy-start.10 = (s32[2]{0:T(128)S(1)}, s32[2]{0:T(128)}, u32[]{:S(2)}) copy-start(s32[2]{0:T(128)} %here.3) | copy-start | bytes 28
  47.9 17.2 %copy-start.11 = (s32[16]{0:T(128)S(1)}, s32[16]{0:T(128)}, u32[]{:S(2)}) copy-start(s32[16]{0:T(128)} %owner.3) | copy-start | bytes 196
  47.9 17.4 %copy-start.9 = (s32[2]{0:T(128)S(1)}, s32[2]{0:T(128)}, u32[]{:S(2)}) copy-start(s32[2]{0:T(128)} %copy-done.8) | copy-start | bytes 28
  60.8 60.3 %all-to-all-start.1 = ((bf16[8,64,1024]{2,1,0:T(8,128)(2,1)}), bf16[8,64,1024]{2,1,0:T(8,128)(2,1)}, u32[]{:S(2)}, u32[]{:S(2)}) async-start(bf16[8,64,1024]{2,1,0:T(8,128)(2,1)} %copy.14), calls=%async_computation.1 | async-start | bytes 2097152 | tf_op jit(solution)/shard_map/all_to_all | solution.py:603
  66.8 20.0 %collective-permute-start.5 = (bf16[576,128]{1,0:T(8,128)(2,1)S(1)}, bf16[576,128]{1,0:T(8,128)(2,1)S(1)}, u32[]{:S(2)}, u32[]{:S(2)}) collective-permute-start(bf16[576,128]{1,0:T(8,128)(2,1)S(1)} %get-tuple-element.29), channel_id=1, source_target_pairs={{0,8},{1,9},{2,10},{3,11},{4,12},{5,13},{6,14},{7,15},{8,0},{9,1},... | collective-permute-start | bytes 442376 | tf_op jit(solution)/shard_map/ppermute | solution.py:559
  69.8 17.0 %collective-permute-start.6 = (bf16[576,128]{1,0:T(8,128)(2,1)S(1)}, bf16[576,128]{1,0:T(8,128)(2,1)S(1)}, u32[]{:S(2)}, u32[]{:S(2)}) collective-permute-start(bf16[576,128]{1,0:T(8,128)(2,1)S(1)} %get-tuple-element.30), channel_id=1, source_target_pairs={{0,16},{1,17},{2,18},{3,19},{4,20},{5,21},{6,22},{7,23},{8,24},{9,... | collective-permute-start | bytes 442376 | tf_op jit(solution)/shard_map/ppermute | solution.py:559
  69.8 23.0 %collective-permute-start.7 = (bf16[576,128]{1,0:T(8,128)(2,1)S(1)}, bf16[576,128]{1,0:T(8,128)(2,1)S(1)}, u32[]{:S(2)}, u32[]{:S(2)}) collective-permute-start(bf16[576,128]{1,0:T(8,128)(2,1)S(1)} %get-tuple-element.31), channel_id=1, source_target_pairs={{0,24},{1,25},{2,26},{3,27},{4,28},{5,29},{6,30},{7,31},{8,16},{9,... | collective-permute-start | bytes 442376 | tf_op jit(solution)/shard_map/ppermute | solution.py:559
  92.9 10.2 %collective-permute-start.9 = (bf16[2,576,128]{2,1,0:T(8,128)(2,1)S(1)}, bf16[2,576,128]{2,1,0:T(8,128)(2,1)S(1)}, u32[]{:S(2)}, u32[]{:S(2)}) collective-permute-start(bf16[2,576,128]{2,1,0:T(8,128)(2,1)S(1)} %pad_maximum_fusion.3.refs_0_), channel_id=1, source_target_pairs={{0,2},{1,3},{2,0},{3,1},{4,6},{5,7},{6,4},{7,5},{8,10},{9,11},{10,... | collective-permute-start | bytes 884744 | tf_op jit(solution)/shard_map/ppermute | solution.py:559
  95.1 18.7 %collective-permute-start.11 = (bf16[2,576,128]{2,1,0:T(8,128)(2,1)S(1)}, bf16[2,576,128]{2,1,0:T(8,128)(2,1)S(1)}, u32[]{:S(2)}, u32[]{:S(2)}) collective-permute-start(bf16[2,576,128]{2,1,0:T(8,128)(2,1)S(1)} %pad_maximum_fusion.3.refs_0_), channel_id=1, source_target_pairs={{0,4},{1,5},{2,6},{3,7},{4,0},{5,1},{6,2},{7,3},{8,12},{9,13},{10,... | collective-permute-start | bytes 884744 | tf_op jit(solution)/shard_map/ppermute | solution.py:559
  97.5 20.5 %collective-permute-start.13 = (bf16[2,576,128]{2,1,0:T(8,128)(2,1)S(1)}, bf16[2,576,128]{2,1,0:T(8,128)(2,1)S(1)}, u32[]{:S(2)}, u32[]{:S(2)}) collective-permute-start(bf16[2,576,128]{2,1,0:T(8,128)(2,1)S(1)} %pad_maximum_fusion.3.refs_0_), channel_id=1, source_target_pairs={{0,6},{1,7},{2,4},{3,5},{4,2},{5,3},{6,0},{7,1},{8,14},{9,15},{10,... | collective-permute-start | bytes 884744 | tf_op jit(solution)/shard_map/ppermute | solution.py:559
  99.1 18.8 %collective-permute-start.1 = (bf16[768,128]{1,0:T(8,128)(2,1)S(1)}, bf16[768,128]{1,0:T(8,128)(2,1)S(1)}, u32[]{:S(2)}, u32[]{:S(2)}) collective-permute-start(bf16[768,128]{1,0:T(8,128)(2,1)S(1)} %get-tuple-element.19), channel_id=1, source_target_pairs={{0,8},{1,9},{2,10},{3,11},{4,12},{5,13},{6,14},{7,15},{8,0},{9,1},... | collective-permute-start | bytes 589832 | tf_op jit(solution)/shard_map/ppermute | solution.py:559
  100.1 18.3 %collective-permute-start.2 = (bf16[768,128]{1,0:T(8,128)(2,1)S(1)}, bf16[768,128]{1,0:T(8,128)(2,1)}, u32[]{:S(2)}, u32[]{:S(2)}) collective-permute-start(bf16[768,128]{1,0:T(8,128)(2,1)S(1)} %get-tuple-element.20), channel_id=1, source_target_pairs={{0,16},{1,17},{2,18},{3,19},{4,20},{5,21},{6,22},{7,23},{8,24},{9,... | collective-permute-start | bytes 589832 | tf_op jit(solution)/shard_map/ppermute | solution.py:559
  103.2 15.4 %collective-permute-start.3 = (bf16[768,128]{1,0:T(8,128)(2,1)S(1)}, bf16[768,128]{1,0:T(8,128)(2,1)S(1)}, u32[]{:S(2)}, u32[]{:S(2)}) collective-permute-start(bf16[768,128]{1,0:T(8,128)(2,1)S(1)} %get-tuple-element.21), channel_id=1, source_target_pairs={{0,24},{1,25},{2,26},{3,27},{4,28},{5,29},{6,30},{7,31},{8,16},{9,... | collective-permute-start | bytes 589832 | tf_op jit(solution)/shard_map/ppermute | solution.py:559
  113.8 18.3 %collective-permute-start.8 = (bf16[2,576,128]{2,1,0:T(8,128)(2,1)S(1)}, bf16[2,576,128]{2,1,0:T(8,128)(2,1)S(1)}, u32[]{:S(2)}, u32[]{:S(2)}) collective-permute-start(bf16[2,576,128]{2,1,0:T(8,128)(2,1)S(1)} %pad_maximum_fusion.3.refs_0_), channel_id=1, source_target_pairs={{0,1},{1,0},{2,3},{3,2},{4,5},{5,4},{6,7},{7,6},{8,9},{9,8},{10,11... | collective-permute-start | bytes 884744 | tf_op jit(solution)/shard_map/ppermute | solution.py:559
  117.9 14.9 %collective-permute-start.10 = (bf16[2,576,128]{2,1,0:T(8,128)(2,1)S(1)}, bf16[2,576,128]{2,1,0:T(8,128)(2,1)S(1)}, u32[]{:S(2)}, u32[]{:S(2)}) collective-permute-start(bf16[2,576,128]{2,1,0:T(8,128)(2,1)S(1)} %collective-permute-done.9.refs_2_), channel_id=1, source_target_pairs={{0,1},{1,0},{2,3},{3,2},{4,5},{5,4},{6,7},{7,6},{8,9},{9,8},{10,11... | collective-permute-start | bytes 884744 | tf_op jit(solution)/shard_map/ppermute | solution.py:559
  117.9 15.6 %collective-permute-start.12 = (bf16[2,576,128]{2,1,0:T(8,128)(2,1)S(1)}, bf16[2,576,128]{2,1,0:T(8,128)(2,1)S(1)}, u32[]{:S(2)}, u32[]{:S(2)}) collective-permute-start(bf16[2,576,128]{2,1,0:T(8,128)(2,1)S(1)} %collective-permute-done.11.refs_4_), channel_id=1, source_target_pairs={{0,1},{1,0},{2,3},{3,2},{4,5},{5,4},{6,7},{7,6},{8,9},{9,8},{10,11... | collective-permute-start | bytes 884744 | tf_op jit(solution)/shard_map/ppermute | solution.py:559
  118.5 15.8 %collective-permute-start.14 = (bf16[2,576,128]{2,1,0:T(8,128)(2,1)S(1)}, bf16[2,576,128]{2,1,0:T(8,128)(2,1)S(1)}, u32[]{:S(2)}, u32[]{:S(2)}) collective-permute-start(bf16[2,576,128]{2,1,0:T(8,128)(2,1)S(1)} %collective-permute-done.13.refs_6_), channel_id=1, source_target_pairs={{0,1},{1,0},{2,3},{3,2},{4,5},{5,4},{6,7},{7,6},{8,9},{9,8},{10,11... | collective-permute-start | bytes 884744 | tf_op jit(solution)/shard_map/ppermute | solution.py:559
  118.5 0.7 copy-start.15
  120.6 37.1 %collective-permute-start.4 = (bf16[8,64,1024]{2,1,0:T(8,128)(2,1)}, bf16[8,64,1024]{2,1,0:T(8,128)(2,1)}, u32[]{:S(2)}, u32[]{:S(2)}) collective-permute-start(bf16[8,64,1024]{2,1,0:T(8,128)(2,1)} %bitcast.30), channel_id=1, source_target_pairs={{0,1},{1,0},{2,3},{3,2},{4,5},{5,4},{6,7},{7,6},{8,9},{9,8},{10,11... | collective-permute-start | bytes 3145736 | tf_op jit(solution)/shard_map/ppermute | solution.py:559
  123.7 15.7 %all-to-all-start.2 = ((bf16[8,64,192]{2,1,0:T(8,128)(2,1)}), bf16[8,64,192]{2,1,0:T(8,128)(2,1)}, u32[]{:S(2)}, u32[]{:S(2)}) async-start(bf16[8,64,192]{2,1,0:T(8,128)(2,1)} %bitcast.7), calls=%async_computation.2 | async-start | bytes 524288 | tf_op jit(solution)/shard_map/all_to_all | solution.py:623
  132.1 0.7 copy-start
  132.8 0.7 copy-start.2
  133.5 0.7 copy-start.4
  134.3 0.7 copy-start.6
  135.0 1.0 copy-start.1
  135.9 1.0 copy-start.3
  136.9 1.0 copy-start.5
  137.9 1.0 copy-start.7
  140.4 7.3 %copy-start.14 = (bf16[64,192]{1,0:T(8,128)(2,1)}, bf16[64,192]{1,0:T(8,128)(2,1)S(1)}, u32[]{:S(2)}) copy-start(bf16[64,192]{1,0:T(8,128)(2,1)S(1)} %reduce_sum.22.own_rank) | copy-start | bytes 73732
  141.3 16.5 %all-to-all-start.3 = ((bf16[16,64,128]{2,1,0:T(8,128)(2,1)}), bf16[16,64,128]{2,1,0:T(8,128)(2,1)}, u32[]{:S(2)}, u32[]{:S(2)}) async-start(bf16[16,64,128]{2,1,0:T(8,128)(2,1)} %broadcast_in_dim.45), calls=%async_computation.3 | async-start | bytes 524288 | tf_op jit(solution)/shard_map/all_to_all | solution.py:632
  152.2 3.7 %copy-start.12 = (bf16[8,2,128,128]{3,2,1,0:T(8,128)(2,1)S(1)}, bf16[8,2,128,128]{3,2,1,0:T(8,128)(2,1)}, u32[]{:S(2)}) copy-start(bf16[8,2,128,128]{3,2,1,0:T(8,128)(2,1)} %get-tuple-element.33) | copy-start | bytes 1572868
  152.2 4.7 %copy-start.13 = (bf16[1,64,1024]{2,1,0:T(8,128)(2,1)S(1)}, bf16[1,64,1024]{2,1,0:T(8,128)(2,1)}, u32[]{:S(2)}) copy-start(bf16[1,64,1024]{2,1,0:T(8,128)(2,1)} %stack.34) | copy-start | bytes 393220
Sparse Core Ops, SparseCore 0:
  48.8 46.8 all-gather.2

commit v3 on v2

--- a/solution.py
+++ b/solution.py
@@ -384,7 +384,7 @@
     return pl.pallas_call(
         assemble_kernel,
         out_shape=jax.ShapeDtypeStruct((PIECES,) + pieces[0].shape, jnp.bfloat16),
-        in_specs=[pl.BlockSpec(memory_space=pl.ANY)] * PIECES,
+        in_specs=[pl.BlockSpec(memory_space=pltpu.VMEM)] * PIECES,
         out_specs=pl.BlockSpec(memory_space=pltpu.VMEM),
         scratch_shapes=[pltpu.SemaphoreType.DMA((PIECES,))],
         compiler_params=pltpu.CompilerParams(vmem_limit_bytes=16 << 20),
@@ -394,10 +394,8 @@
 
 def attend_kernel(
     query_block,
-    key_same,
-    key_other,
-    value_same,
-    value_other,
+    key_base,
+    value_base,
     own_rank,
     all_rank,
     query_up,
@@ -422,19 +420,17 @@
         return delta * cosine + pltpu.roll(delta, HEAD_SIZE // 2, 1) * sine
 
     half = lax.axis_index("ctx") * rows // BLOCK_TOKENS
-    core = lax.rem(lax.axis_index("ctx"), 2)
-    for block in range(key_up.shape[0]):
-        for chip in range(block * PIECES // 2, (block + 1) * PIECES // 2):
-            for apart in range(2):
-                first = (2 * chip + (core ^ apart)) * rows
-                span = pl.ds(pl.multiple_of(first, rows), rows)
-                key_base = (key_other if apart else key_same)[chip]
-                value_base = (value_other if apart else value_same)[chip]
-                delta = adapter_scale * dot(all_rank[span, :ADAPTER_RANK], key_up[block ^ half])
-                delta = turned(delta, cosines[span, :], sines[span, :])
-                keys[span, :] = (key_base.astype(jnp.float32) + delta).astype(jnp.bfloat16)
-                delta = adapter_scale * dot(all_rank[span, ADAPTER_RANK:], value_up[block ^ half])
-                values[span, :] = (value_base.astype(jnp.float32) + delta).astype(jnp.bfloat16)
+    for apart in range(key_up.shape[0]):
+        for seat in range(PIECES):
+            first = ((half ^ apart) * PIECES + seat) * rows
+            span = pl.ds(pl.multiple_of(first, rows), rows)
+            delta = adapter_scale * dot(all_rank[span, :ADAPTER_RANK], key_up[apart])
+            delta = turned(delta, cosines[span, :], sines[span, :])
+            full = key_base[seat, apart].astype(jnp.float32) + delta
+            keys[span, :] = full.astype(jnp.bfloat16)
+            delta = adapter_scale * dot(all_rank[span, ADAPTER_RANK:], value_up[apart])
+            full = value_base[seat, apart].astype(jnp.float32) + delta
+            values[span, :] = full.astype(jnp.bfloat16)
     here = pl.ds(pl.multiple_of(base, rows), rows)
     cosine = cosines[here, :]
     sine = sines[here, :]
@@ -479,8 +475,7 @@
 
 def attend(
     query_base,
-    base_rows,
-    base_other,
+    base,
     own_rank,
     all_rank,
     query_up,
@@ -491,8 +486,7 @@
     up_out,
 ):
     rows = query_base.shape[0]
-    chips = base_rows.shape[0]
-    seq = 2 * chips * rows
+    seq = base.shape[0] * base.shape[1] * rows
     blocks = keyval_up.shape[0]
     width = GROUP * HEAD_SIZE
 
@@ -508,10 +502,8 @@
         ),
         in_specs=[
             pl.BlockSpec((rows, width), lambda h: (0, h)),
-            pl.BlockSpec((chips, rows, HEAD_SIZE), lambda h: (0, 0, h)),
-            pl.BlockSpec((chips, rows, HEAD_SIZE), lambda h: (0, 0, h)),
-            pl.BlockSpec((chips, rows, HEAD_SIZE), lambda h: (0, 0, h + KEYVALUE_HEADS)),
-            pl.BlockSpec((chips, rows, HEAD_SIZE), lambda h: (0, 0, h + KEYVALUE_HEADS)),
+            pl.BlockSpec((PIECES, 2, rows, HEAD_SIZE), lambda h: (0, 0, 0, h)),
+            pl.BlockSpec((PIECES, 2, rows, HEAD_SIZE), lambda h: (0, 0, 0, h + KEYVALUE_HEADS)),
             whole(own_rank.shape),
             whole(all_rank.shape),
             pl.BlockSpec((ADAPTER_RANK, width), lambda h: (0, h)),
@@ -539,10 +531,8 @@
         ),
     )(
         query_base,
-        base_rows,
-        base_other,
-        base_rows,
-        base_other,
+        base,
+        base,
         own_rank,
         all_rank,
         query_up,
@@ -570,23 +560,18 @@
     ctx = lax.axis_size("ctx")
     seq = ctx * tok_rows
     blocks = [list(range(PIECES)), list(range(PIECES, 2 * PIECES))]
-    same_core = [list(range(c, ctx, 2)) for c in range(2)]
-
-    base_rows = lax.all_gather(
-        jnp.concatenate([key_base, value_base], 1), "ctx", axis_index_groups=same_core
-    )
+    base = jnp.concatenate([key_base, value_base], 1)
+    base = jnp.stack([base, swap(base, PIECES)])
     elsewhere = swap(stretch_adapter, 2 * PIECES)
     packed_rest = pack_row(adapter_pool, REST)
-    packed_down = pack_row(adapter_pool, DOWN, packed_rest, elsewhere)
+    packed_down = pack_row(adapter_pool, DOWN, packed_rest)
     ids = jnp.arange(adapter_owner.shape[0], dtype=jnp.int32)
     slots = jnp.sum(
         jnp.where(stretch_adapter[:, None] == ids[None, :], adapter_owner[None, :], 0), axis=1
     )
     near = (slots // PIECES) == half
-
-    def fetch(spread, mirrored=None):
-        sent = pick(spread, stretch_adapter, elsewhere, adapter_owner, mirrored)
-        return [swap(block, flip * PIECES) if flip else block for flip, block in enumerate(sent)]
+    close = jnp.where(half == 0, near[0], near[1])
+    far_close = jnp.where(half == 0, near[1], near[0])
 
     def settle(arrived, close):
         own = jnp.where(close, arrived[0], arrived[1])
@@ -594,29 +579,35 @@
         low = plane == 0
         return jnp.stack([jnp.where(low, own, other), jnp.where(low, other, own)])
 
-    close = jnp.where(half == 0, near[0], near[1])
-    far_close = jnp.where(half == 0, near[1], near[0])
+    def exchange(sent):
+        return [swap(block, flip * PIECES) if flip else block for flip, block in enumerate(sent)]
+
+    def gather(block):
+        parts = [swap(block, apart) if apart else block for apart in (0, 2, 4, 6)]
+        return assemble([piece for part in parts for piece in (part, swap(part, 1))])
+
     spread_rest = lax.all_to_all(packed_rest, "ctx", 0, 0, axis_index_groups=blocks)
+    sent_rest = pick(spread_rest, stretch_adapter, elsewhere, adapter_owner, (128, 32))
+    sent_rest, packed_down = lax.optimization_barrier((sent_rest, packed_down))
     spread_down = lax.all_to_all(packed_down, "ctx", 0, 0, axis_index_groups=blocks)
+    mine = jnp.arange(sent_rest[0].shape[0], dtype=jnp.int32)[:, None] < 544
+    rest = settle(exchange(sent_rest), jnp.where(mine, close, far_close))
+
+    rest, spread_down = lax.optimization_barrier((rest, spread_down))
+    sent_down = pick(spread_down, stretch_adapter, elsewhere, adapter_owner, None)
     moving = normed_input.reshape(tok_rows, PIECES, D // PIECES).transpose(1, 0, 2)
-    moving, spread_down = lax.optimization_barrier((moving, spread_down))
+    moving, rest, base, sent_down = lax.optimization_barrier((moving, rest, base, sent_down))
     moving = lax.all_to_all(moving, "ctx", 0, 0, axis_index_groups=blocks)
-
-    rest = fetch(spread_rest, (128, 32))
-    mine = jnp.arange(rest[0].shape[0], dtype=jnp.int32)[:, None] < 544
-    rest = settle(rest, jnp.where(mine, close, far_close))
-    rest = [swap(rest, apart) if apart else rest for apart in (0, 2, 4, 6)]
-    rest = assemble([piece for block in rest for piece in (block, swap(block, 1))])
+    down_slice = settle(exchange(sent_down), close).reshape(D // PIECES, 3 * ADAPTER_RANK)
+
+    rest = gather(rest)
     query_up = rest[:, :, :128].reshape(ADAPTER_RANK, QH * HEAD_SIZE)
     keyval_up = jnp.stack([rest[:, :, 128:160], rest[:, :, 544:]])
     keyval_up = keyval_up.reshape(2, ADAPTER_RANK, 2 * KEYVALUE_HEADS * HEAD_SIZE)
     down_out = rest[:, :, 160:288].reshape(QH * HEAD_SIZE, ADAPTER_RANK)
     up_out = rest[:, :, 288:544].reshape(ADAPTER_RANK, D)
-
-    arrived = fetch(spread_down)
-    arrived, base_rows = lax.optimization_barrier((arrived, base_rows))
-    base_other = swap(base_rows, 1)
-    down_slice = settle(arrived, close).reshape(D // PIECES, 3 * ADAPTER_RANK)
+    base = gather(base)
+
     partial_rows = jnp.dot(
         moving.reshape(BLOCK_TOKENS, D // PIECES), down_slice, preferred_element_type=jnp.float32
     ).astype(jnp.bfloat16)
@@ -640,8 +631,7 @@
     sines = jnp.concatenate([-sine, sine], 1)
     return attend(
         query_base,
-        base_rows,
-        base_other,
+        base,
         own_rank,
         all_rank,
         query_up,

time: 177 us -> 150 us (0.85)
  blocking collectives: 24.2 us -> 0 us
  between operations: 16.9 us -> 3.54 us
  waiting for transfers between devices: 41.2 us -> 53.5 us
  local copies, waits for them, and re-layouts: 23.2 us -> 14 us
  starting transfers between devices: 40 us -> 48.3 us
    all_to_all x1 -> x0, blocking collectives: 24.2 us -> none  [direct_shards(): lax.all_to_all(packed_down, 'ctx', 0, 0, axis_index_groups=blocks)]
    ppermute x15 -> x22, waiting for transfers between devices: 29.7 us -> 36.9 us  [swap(): lax.ppermute(block, ('groups', 'ctx'), [(i, i ^ mask) for i in range(4 *...]
    unnamed x37 -> x20, local copies, waits for them, and re-layouts: 9.79 us -> 4.21 us
    ppermute x15 -> x22, starting transfers between devices: 20.6 us -> 25.3 us  [swap(): lax.ppermute(block, ('groups', 'ctx'), [(i, i ^ mask) for i in range(4 *...]
    all_to_all x1, waiting for transfers between devices: 0.12 us -> 4.61 us  [direct_shards(): lax.all_to_all(all_rank, 'ctx', 0, 0).reshape(seq, 2 * ADAPTER_RANK)]
    all_to_all x0 -> x1, starting transfers between devices: none -> 3.59 us  [direct_shards(): lax.all_to_all(packed_down, 'ctx', 0, 0, axis_index_groups=blocks)]
    all_to_all x1, starting transfers between devices: 6.43 us -> 4.2 us  [direct_shards(): lax.all_to_all(all_rank, 'ctx', 0, 0).reshape(seq, 2 * ADAPTER_RANK)]
    all_to_all x0 -> x1, waiting for transfers between devices: none -> 1.9 us  [direct_shards(): lax.all_to_all(packed_down, 'ctx', 0, 0, axis_index_groups=blocks)]
  transfers between devices with their start and end apart: 20 -> 27, of which waited for: 6 -> 11; matrix products, arithmetic and copies ran while one was open for 14% -> 11% of each run, Pallas kernels for 4% -> 3%
where the time goes in v3:
time: 150 us
  waiting for transfers between devices  53.5 us (36%)
  starting transfers between devices  48.3 us (32%)
  Pallas kernels  22.1 us (15%)
  local copies, waits for them, and re-layouts  14 us (9%)
  other arithmetic  5.68 us (4%)
  between operations  3.54 us (2%)
  matrix products  2.41 us (2%)
    ppermute x22, waiting for transfers between devices, swap(): lax.ppermute(block, ('groups', 'ctx'), [(i, i ^ mask) for i in range(4 *...  36.9 us
    ppermute x22, starting transfers between devices, swap(): lax.ppermute(block, ('groups', 'ctx'), [(i, i ^ mask) for i in range(4 *...  25.3 us
    pallas_call x1, Pallas kernels, attend(): pl.pallas_call(attend_kernel, grid=(KEYVALUE_HEADS,), out_shape=(jax.Shap...  11.5 us
    all_to_all x1, waiting for transfers between devices, direct_shards(): lax.all_to_all(packed_rest, 'ctx', 0, 0, axis_index_groups=blocks)  10.1 us
    pallas_call x2, Pallas kernels, pack_row(): pl.pallas_call(partial(pack_kernel, sections), out_shape=jax.ShapeDtypeSt...  6.72 us
    all_to_all x1, starting transfers between devices, direct_shards(): moving = lax.all_to_all(moving, 'ctx', 0, 0, axis_index_groups=blocks)  5.95 us
    all_to_all x1, starting transfers between devices, direct_shards(): lax.all_to_all(packed_rest, 'ctx', 0, 0, axis_index_groups=blocks)  5.24 us
    all_to_all x1, waiting for transfers between devices, direct_shards(): lax.all_to_all(all_rank, 'ctx', 0, 0).reshape(seq, 2 * ADAPTER_RANK)  4.61 us
  transfers between devices with their start and end apart: 27, of which 11 were waited for; matrix products, arithmetic and copies ran while one was open for 11% of the time, Pallas kernels for 3%

profile of v3, /device:TPU:0, one launch (start us, length us, event | category | flops | bytes accessed | tf_op | source)
XLA Modules:
  0.0 149.6 jit_solution(12360508130124457878)
XLA Ops:
  0.6 3.3 %shard_map.86.refs_0_ = bf16[8,544,128]{2,1,0:T(8,128)(2,1)} custom-call(bf16[1,2686976]{1,0:T(2,128)(2,1)} %pool.3), custom_call_target="tpu_custom_call" | custom-call | bytes 8388608 | tf_op jit(solution)/shard_map/pallas_call | solution.py:314
  3.9 5.2 %all-to-all-start = ((bf16[8,544,128]{2,1,0:T(8,128)(2,1)}), bf16[8,544,128]{2,1,0:T(8,128)(2,1)S(1)}, u32[]{:S(2)}, u32[]{:S(2)}) async-start(bf16[8,544,128]{2,1,0:T(8,128)(2,1)} %shard_map.86.refs_0_), calls=%async_computation | async-start | bytes 2228224 | tf_op jit(solution)/shard_map/all_to_all | solution.py:589
  9.2 1.6 %collective-permute-start = (s32[2]{0:T(128)S(1)}, s32[2]{0:T(128)S(1)}, u32[]{:S(2)}, u32[]{:S(2)}) collective-permute-start(s32[2]{0:T(128)S(1)} %copy-done.2), channel_id=1, source_target_pairs={{0,16},{1,17},{2,18},{3,19},{4,20},{5,21},{6,22},{7,23},{8,24},{9,... | collective-permute-start | bytes 32 | tf_op jit(solution)/shard_map/ppermute | solution.py:549
  10.8 3.5 %shard_map.88 = bf16[8,768,128]{2,1,0:T(8,128)(2,1)} custom-call(bf16[1,2686976]{1,0:T(2,128)(2,1)} %pool.3, bf16[8,544,128]{2,1,0:T(8,128)(2,1)} %shard_map.86.refs_0_), custom_call_target="tpu_custom_call" | custom-call | bytes 8388608 | tf_op jit(solution)/shard_map/pallas_call | solution.py:314
  14.2 0.0 copy-start.7
  14.3 10.1 %all-to-all-done.spread = bf16[8,544,128]{2,1,0:T(8,128)(2,1)S(1)} async-done(((bf16[8,544,128]{2,1,0:T(8,128)(2,1)}), bf16[8,544,128]{2,1,0:T(8,128)(2,1)S(1)}, u32[]{:S(2)}, u32[]{:S(2)}) %all-to-all-start) | async-done | bytes 1114144 | tf_op jit(solution)/shard_map/all_to_all | solution.py:589
  24.3 1.4 shard_map.87
  25.8 3.6 %all-to-all-start.1 = ((bf16[8,768,128]{2,1,0:T(8,128)(2,1)}), bf16[8,768,128]{2,1,0:T(8,128)(2,1)S(1)}, u32[]{:S(2)}, u32[]{:S(2)}) async-start(bf16[8,768,128]{2,1,0:T(8,128)(2,1)} %shard_map.88), calls=%async_computation.1 | async-start | bytes 3145728 | tf_op jit(solution)/shard_map/all_to_all | solution.py:592
  29.4 2.7 %collective-permute-start.4 = (bf16[64,1024]{1,0:T(8,128)(2,1)S(1)}, bf16[64,1024]{1,0:T(8,128)(2,1)S(1)}, u32[]{:S(2)}, u32[]{:S(2)}) collective-permute-start(bf16[64,1024]{1,0:T(8,128)(2,1)S(1)} %constant_dynamic-update-slice_fusion), channel_id=1, source_target_pairs={{0,8},{1,9},{2,10},{3,11},{4,12},{5,13},{6,14},{7,15},{8,0},{9,1},... | collective-permute-start | bytes 393224 | tf_op jit(solution)/shard_map/ppermute | solution.py:549
  32.1 0.2 fusion.2
  32.3 0.6 fusion.6
  35.5 0.4 collective-permute-start.1
  35.9 1.5 %collective-permute-start.2 = (bf16[576,128]{1,0:T(8,128)(2,1)S(1)}, bf16[576,128]{1,0:T(8,128)(2,1)S(1)}, u32[]{:S(2)}, u32[]{:S(2)}) collective-permute-start(bf16[576,128]{1,0:T(8,128)(2,1)S(1)} %get-tuple-element.30), channel_id=1, source_target_pairs={{0,16},{1,17},{2,18},{3,19},{4,20},{5,21},{6,22},{7,23},{8,24},{9,... | collective-permute-start | bytes 442376 | tf_op jit(solution)/shard_map/ppermute | solution.py:549
  37.4 2.5 %collective-permute-start.3 = (bf16[576,128]{1,0:T(8,128)(2,1)S(1)}, bf16[576,128]{1,0:T(8,128)(2,1)S(1)}, u32[]{:S(2)}, u32[]{:S(2)}) collective-permute-start(bf16[576,128]{1,0:T(8,128)(2,1)S(1)} %get-tuple-element.31), channel_id=1, source_target_pairs={{0,24},{1,25},{2,26},{3,27},{4,28},{5,29},{6,30},{7,31},{8,16},{9,... | collective-permute-start | bytes 442376 | tf_op jit(solution)/shard_map/ppermute | solution.py:549
  39.9 2.8 %copy.16 = bf16[8,8,8,1024]{3,2,1,0:T(8,128)(2,1)} copy(bf16[8,8,8,1024]{3,1,2,0:T(8,128)(2,1)} %bitcast.32) | data formatting | bytes 2097152
  42.7 7.6 %collective-permute-done.4 = bf16[64,1024]{1,0:T(8,128)(2,1)S(1)} collective-permute-done((bf16[64,1024]{1,0:T(8,128)(2,1)S(1)}, bf16[64,1024]{1,0:T(8,128)(2,1)S(1)}, u32[]{:S(2)}, u32[]{:S(2)}) %collective-permute-start.4) | collective-permute-done | bytes 131104 | tf_op jit(solution)/shard_map/ppermute | solution.py:549
  50.3 3.1 %collective-permute-done.1 = bf16[576,128]{1,0:T(8,128)(2,1)S(1)} collective-permute-done((bf16[576,128]{1,0:T(8,128)(2,1)S(1)}, bf16[576,128]{1,0:T(8,128)(2,1)S(1)}, u32[]{:S(2)}, u32[]{:S(2)}) %collective-permute-start.1) | collective-permute-done | bytes 147488 | tf_op jit(solution)/shard_map/ppermute | solution.py:549
  53.5 2.9 %collective-permute-done.3 = bf16[576,128]{1,0:T(8,128)(2,1)S(1)} collective-permute-done((bf16[576,128]{1,0:T(8,128)(2,1)S(1)}, bf16[576,128]{1,0:T(8,128)(2,1)S(1)}, u32[]{:S(2)}, u32[]{:S(2)}) %collective-permute-start.3) | collective-permute-done | bytes 147488 | tf_op jit(solution)/shard_map/ppermute | solution.py:549
  56.4 0.1 select_bitcast_fusion.3
  56.6 1.9 %all-to-all-done.1.spread = bf16[8,768,128]{2,1,0:T(8,128)(2,1)S(1)} async-done(((bf16[8,768,128]{2,1,0:T(8,128)(2,1)}), bf16[8,768,128]{2,1,0:T(8,128)(2,1)S(1)}, u32[]{:S(2)}, u32[]{:S(2)}) %all-to-all-start.1) | async-done | bytes 1572896 | tf_op jit(solution)/shard_map/all_to_all | solution.py:592
  58.5 1.7 %shard_map.89 = (bf16[768,128]{1,0:T(8,128)(2,1)S(1)}, bf16[768,128]{1,0:T(8,128)(2,1)S(1)}, bf16[768,128]{1,0:T(8,128)(2,1)S(1)}, bf16[768,128]{1,0:T(8,128)(2,1)S(1)}) custom-call(s32[2]{0:T(128)S(1)} %copy-done.2, s32[2]{0:T(128)S(1)} %collective-permute-done.there, s32[16]{0:T(128)S(1)} %copy-done.3, bf16[8,768,128]{2,1,0:T(8,128)(2,1)S(1)} %all-to-all-done.1.spread), custom_call_target="tpu_custom_call" | custom-call | bytes 2097152 | tf_op jit(solution)/shard_map/pallas_call | solution.py:359
  60.2 1.5 %copy.14 = bf16[8,64,1024]{2,1,0:T(8,128)(2,1)} copy(bf16[8,64,1024]{2,0,1:T(8,128)(2,1)S(1)} %bitcast.31) | data formatting | bytes 2097152 | tf_op jit(solution)/shard_map/optimization_barrier | solution.py:599
  61.7 6.0 %all-to-all-start.2 = ((bf16[8,64,1024]{2,1,0:T(8,128)(2,1)}), bf16[8,64,1024]{2,1,0:T(8,128)(2,1)}, u32[]{:S(2)}, u32[]{:S(2)}) async-start(bf16[8,64,1024]{2,1,0:T(8,128)(2,1)} %copy.14), calls=%async_computation.2 | async-start | bytes 2097152 | tf_op jit(solution)/shard_map/all_to_all | solution.py:600
  67.7 0.8 collective-permute-start.12
  68.5 0.5 collective-permute-start.13
  69.0 3.1 %collective-permute-start.14 = (bf16[768,128]{1,0:T(8,128)(2,1)S(1)}, bf16[768,128]{1,0:T(8,128)(2,1)S(1)}, u32[]{:S(2)}, u32[]{:S(2)}) collective-permute-start(bf16[768,128]{1,0:T(8,128)(2,1)S(1)} %get-tuple-element.44), channel_id=1, source_target_pairs={{0,24},{1,25},{2,26},{3,27},{4,28},{5,29},{6,30},{7,31},{8,16},{9,... | collective-permute-start | bytes 589832 | tf_op jit(solution)/shard_map/ppermute | solution.py:549
  72.1 3.0 %collective-permute-start.10 = (bf16[2,64,1024]{2,1,0:T(8,128)(2,1)S(1)}, bf16[2,64,1024]{2,1,0:T(8,128)(2,1)S(1)}, u32[]{:S(2)}, u32[]{:S(2)}) collective-permute-start(bf16[2,64,1024]{2,1,0:T(8,128)(2,1)S(1)} %pad_maximum_fusion.4.refs_0_), channel_id=1, source_target_pairs={{0,6},{1,7},{2,4},{3,5},{4,2},{5,3},{6,0},{7,1},{8,14},{9,15},{10,... | collective-permute-start | bytes 786440 | tf_op jit(solution)/shard_map/ppermute | solution.py:549
  75.1 0.6 collective-permute-start.6
  75.6 8.8 %collective-permute-done.12 = bf16[768,128]{1,0:T(8,128)(2,1)S(1)} collective-permute-done((bf16[768,128]{1,0:T(8,128)(2,1)S(1)}, bf16[768,128]{1,0:T(8,128)(2,1)S(1)}, u32[]{:S(2)}, u32[]{:S(2)}) %collective-permute-start.12) | collective-permute-done | bytes 196640 | tf_op jit(solution)/shard_map/ppermute | solution.py:549
  84.5 3.0 %collective-permute-start.8 = (bf16[2,64,1024]{2,1,0:T(8,128)(2,1)S(1)}, bf16[2,64,1024]{2,1,0:T(8,128)(2,1)S(1)}, u32[]{:S(2)}, u32[]{:S(2)}) collective-permute-start(bf16[2,64,1024]{2,1,0:T(8,128)(2,1)S(1)} %pad_maximum_fusion.4.refs_0_), channel_id=1, source_target_pairs={{0,4},{1,5},{2,6},{3,7},{4,0},{5,1},{6,2},{7,3},{8,12},{9,13},{10,... | collective-permute-start | bytes 786440 | tf_op jit(solution)/shard_map/ppermute | solution.py:549
  87.5 1.2 collective-permute-done.14
  88.7 1.9 %collective-permute-start.16 = (bf16[2,576,128]{2,1,0:T(8,128)(2,1)S(1)}, bf16[2,576,128]{2,1,0:T(8,128)(2,1)S(1)}, u32[]{:S(2)}, u32[]{:S(2)}) collective-permute-start(bf16[2,576,128]{2,1,0:T(8,128)(2,1)S(1)} %pad_maximum_fusion.3.refs_0_), channel_id=1, source_target_pairs={{0,2},{1,3},{2,0},{3,1},{4,6},{5,7},{6,4},{7,5},{8,10},{9,11},{10,... | collective-permute-start | bytes 884744 | tf_op jit(solution)/shard_map/ppermute | solution.py:549
  90.6 7.0 %collective-permute-done.10.refs_6_ = bf16[2,64,1024]{2,1,0:T(8,128)(2,1)S(1)} collective-permute-done((bf16[2,64,1024]{2,1,0:T(8,128)(2,1)S(1)}, bf16[2,64,1024]{2,1,0:T(8,128)(2,1)S(1)}, u32[]{:S(2)}, u32[]{:S(2)}) %collective-permute-start.10) | collective-permute-done | bytes 262176 | tf_op jit(solution)/shard_map/ppermute | solution.py:549
  97.6 0.5 collective-permute-start.18
  98.2 1.5 %collective-permute-start.20 = (bf16[2,576,128]{2,1,0:T(8,128)(2,1)S(1)}, bf16[2,576,128]{2,1,0:T(8,128)(2,1)S(1)}, u32[]{:S(2)}, u32[]{:S(2)}) collective-permute-start(bf16[2,576,128]{2,1,0:T(8,128)(2,1)S(1)} %pad_maximum_fusion.3.refs_0_), channel_id=1, source_target_pairs={{0,6},{1,7},{2,4},{3,5},{4,2},{5,3},{6,0},{7,1},{8,14},{9,15},{10,... | collective-permute-start | bytes 884744 | tf_op jit(solution)/shard_map/ppermute | solution.py:549
  99.7 0.3 reshape.56
  100.1 2.3 %collective-permute-done.8.refs_4_ = bf16[2,64,1024]{2,1,0:T(8,128)(2,1)S(1)} collective-permute-done((bf16[2,64,1024]{2,1,0:T(8,128)(2,1)S(1)}, bf16[2,64,1024]{2,1,0:T(8,128)(2,1)S(1)}, u32[]{:S(2)}, u32[]{:S(2)}) %collective-permute-start.8) | collective-permute-done | bytes 262176 | tf_op jit(solution)/shard_map/ppermute | solution.py:549
  102.4 0.5 collective-permute-start.7
  102.9 2.4 %convolution_convert_fusion = bf16[512,192]{0,1:T(8,128)(2,1)} fusion(bf16[512,1024]{1,0:T(8,128)(2,1)} %bitcast.7, bf16[1024,192]{1,0:T(8,128)(2,1)S(1)} %reshape.56), kind=kOutput, calls=%fused_computation | convolution fusion | flops 201424896 | bytes 1638400 | tf_op jit(solution)/shard_map/dot_general | solution.py:611
  105.3 1.8 %copy.15 = bf16[512,192]{1,0:T(8,128)(2,1)} copy(bf16[512,192]{0,1:T(8,128)(2,1)} %convolution_convert_fusion) | data formatting | bytes 393216 | tf_op jit(solution)/shard_map/convert_element_type | solution.py:613
  107.1 4.1 %all-to-all-start.3 = ((bf16[8,64,192]{2,1,0:T(8,128)(2,1)}), bf16[8,64,192]{2,1,0:T(8,128)(2,1)}, u32[]{:S(2)}, u32[]{:S(2)}) async-start(bf16[8,64,192]{2,1,0:T(8,128)(2,1)} %bitcast.10), calls=%async_computation.3 | async-start | bytes 524288 | tf_op jit(solution)/shard_map/all_to_all | solution.py:614
  111.1 0.4 collective-permute-start.15
  111.5 0.2 collective-permute-start.9
  111.7 3.9 %collective-permute-done.20.refs_6_ = bf16[2,576,128]{2,1,0:T(8,128)(2,1)S(1)} collective-permute-done((bf16[2,576,128]{2,1,0:T(8,128)(2,1)S(1)}, bf16[2,576,128]{2,1,0:T(8,128)(2,1)S(1)}, u32[]{:S(2)}, u32[]{:S(2)}) %collective-permute-start.20) | collective-permute-done | bytes 294944 | tf_op jit(solution)/shard_map/ppermute | solution.py:549
  115.7 0.5 collective-permute-start.19
  116.2 0.1 collective-permute-start.21
  116.2 1.9 %fusion = (f32[1024,64]{1,0:T(8,128)S(1)}, f32[1024,64]{1,0:T(8,128)S(1)}, f32[1024,64]{1,0:T(8,128)S(1)}) fusion(f32[64]{0:T(128)S(1)} %multiply_power_fusion, f32[1024]{0:T(1024)S(1)} %iota_convert_fusion), kind=kLoop, calls=%fused_computation.13 | loop fusion | flops 131072 | bytes 790784 | tf_op jit(solution)/shard_map/neg | solution.py:631
  118.1 1.3 pad_maximum_fusion
  119.5 0.2 shard_map.90.key_base.value_base
  119.7 1.4 copy-done
  121.1 0.6 shard_map.91
  121.7 1.2 reduce_sum.22.own_rank
  123.0 0.1 slice.34
  123.0 0.8 broadcast_in_dim.48
  123.8 4.2 %all-to-all-start.4 = ((bf16[16,64,128]{2,1,0:T(8,128)(2,1)}), bf16[16,64,128]{2,1,0:T(8,128)(2,1)}, u32[]{:S(2)}, u32[]{:S(2)}) async-start(bf16[16,64,128]{2,1,0:T(8,128)(2,1)} %broadcast_in_dim.48), calls=%async_computation.4 | async-start | bytes 524288 | tf_op jit(solution)/shard_map/all_to_all | solution.py:623
  128.0 0.1 stack.45
  128.1 0.7 stack.46
  128.8 0.1 fusion.4
  129.0 1.4 reshape.60.down_out
  130.4 1.3 reshape.61.up_out
  131.7 1.0 reshape.59.query_up
  132.7 0.7 pad_maximum_fusion.5.key_up.value_up
  133.4 4.6 %all-to-all-done.4 = bf16[16,64,128]{2,1,0:T(8,128)(2,1)} async-done(((bf16[16,64,128]{2,1,0:T(8,128)(2,1)}), bf16[16,64,128]{2,1,0:T(8,128)(2,1)}, u32[]{:S(2)}, u32[]{:S(2)}) %all-to-all-start.4) | async-done | bytes 262176 | tf_op jit(solution)/shard_map/all_to_all | solution.py:623
  138.1 11.5 %shard_map.92 = (bf16[64,4096]{1,0:T(8,128)(2,1)}, bf16[64,8192]{1,0:T(8,128)(2,1)}) custom-call(bf16[64,4096]{1,0:T(8,128)(2,1)} %query_block.1, bf16[8,2,64,1024]{3,2,1,0:T(8,128)(2,1)} %copy-done, bf16[8,2,64,1024]{3,2,1,0:T(8,128)(2,1)} %copy-done, bf16[64,192]{1,0:T(8,128)(2,1)} %copy-done.6, bf16[1024,128]{1,0:T(8,128)(2,1)} %bitcast.11.all_rank, ...), custom_call_target="tpu_custom_call" | custom-call | flops 1073741824 | bytes 10485760 | tf_op jit(solution)/shard_map/pallas_call | solution.py:496
  (48 shorter events, 0.3 us)
Async XLA Ops:
  3.9 5.3 %copy-start.2 = (s32[2]{0:T(128)S(1)}, s32[2]{0:T(128)}, u32[]{:S(2)}) copy-start(s32[2]{0:T(128)} %here.3) | copy-start | bytes 28
  3.9 20.4 %all-to-all-start = ((bf16[8,544,128]{2,1,0:T(8,128)(2,1)}), bf16[8,544,128]{2,1,0:T(8,128)(2,1)S(1)}, u32[]{:S(2)}, u32[]{:S(2)}) async-start(bf16[8,544,128]{2,1,0:T(8,128)(2,1)} %shard_map.86.refs_0_), calls=%async_computation | async-start | bytes 2228224 | tf_op jit(solution)/shard_map/all_to_all | solution.py:589
  9.2 15.2 %copy-start.3 = (s32[16]{0:T(128)S(1)}, s32[16]{0:T(128)}, u32[]{:S(2)}) copy-start(s32[16]{0:T(128)} %owner.3) | copy-start | bytes 196
  9.2 5.1 %collective-permute-start = (s32[2]{0:T(128)S(1)}, s32[2]{0:T(128)S(1)}, u32[]{:S(2)}, u32[]{:S(2)}) collective-permute-start(s32[2]{0:T(128)S(1)} %copy-done.2), channel_id=1, source_target_pairs={{0,16},{1,17},{2,18},{3,19},{4,20},{5,21},{6,22},{7,23},{8,24},{9,... | collective-permute-start | bytes 32 | tf_op jit(solution)/shard_map/ppermute | solution.py:549
  14.2 15.1 %copy-start.7 = (bf16[64,512]{1,0:T(8,128)(2,1)S(1)}, bf16[64,512]{1,0:T(8,128)(2,1)}, u32[]{:S(2)}) copy-start(bf16[64,512]{1,0:T(8,128)(2,1)} %param.9) | copy-start | bytes 196612
  14.2 15.2 %copy-start.8 = (bf16[64,512]{1,0:T(8,128)(2,1)S(1)}, bf16[64,512]{1,0:T(8,128)(2,1)}, u32[]{:S(2)}) copy-start(bf16[64,512]{1,0:T(8,128)(2,1)} %param.10) | copy-start | bytes 196612
  25.8 32.7 %all-to-all-start.1 = ((bf16[8,768,128]{2,1,0:T(8,128)(2,1)}), bf16[8,768,128]{2,1,0:T(8,128)(2,1)S(1)}, u32[]{:S(2)}, u32[]{:S(2)}) async-start(bf16[8,768,128]{2,1,0:T(8,128)(2,1)} %shard_map.88), calls=%async_computation.1 | async-start | bytes 3145728 | tf_op jit(solution)/shard_map/all_to_all | solution.py:592
  29.4 20.9 %collective-permute-start.4 = (bf16[64,1024]{1,0:T(8,128)(2,1)S(1)}, bf16[64,1024]{1,0:T(8,128)(2,1)S(1)}, u32[]{:S(2)}, u32[]{:S(2)}) collective-permute-start(bf16[64,1024]{1,0:T(8,128)(2,1)S(1)} %constant_dynamic-update-slice_fusion), channel_id=1, source_target_pairs={{0,8},{1,9},{2,10},{3,11},{4,12},{5,13},{6,14},{7,15},{8,0},{9,1},... | collective-permute-start | bytes 393224 | tf_op jit(solution)/shard_map/ppermute | solution.py:549
  35.5 18.0 %collective-permute-start.1 = (bf16[576,128]{1,0:T(8,128)(2,1)S(1)}, bf16[576,128]{1,0:T(8,128)(2,1)S(1)}, u32[]{:S(2)}, u32[]{:S(2)}) collective-permute-start(bf16[576,128]{1,0:T(8,128)(2,1)S(1)} %get-tuple-element.29), channel_id=1, source_target_pairs={{0,8},{1,9},{2,10},{3,11},{4,12},{5,13},{6,14},{7,15},{8,0},{9,1},... | collective-permute-start | bytes 442376 | tf_op jit(solution)/shard_map/ppermute | solution.py:549
  35.9 17.6 %collective-permute-start.2 = (bf16[576,128]{1,0:T(8,128)(2,1)S(1)}, bf16[576,128]{1,0:T(8,128)(2,1)S(1)}, u32[]{:S(2)}, u32[]{:S(2)}) collective-permute-start(bf16[576,128]{1,0:T(8,128)(2,1)S(1)} %get-tuple-element.30), channel_id=1, source_target_pairs={{0,16},{1,17},{2,18},{3,19},{4,20},{5,21},{6,22},{7,23},{8,24},{9,... | collective-permute-start | bytes 442376 | tf_op jit(solution)/shard_map/ppermute | solution.py:549
  37.4 19.0 %collective-permute-start.3 = (bf16[576,128]{1,0:T(8,128)(2,1)S(1)}, bf16[576,128]{1,0:T(8,128)(2,1)S(1)}, u32[]{:S(2)}, u32[]{:S(2)}) collective-permute-start(bf16[576,128]{1,0:T(8,128)(2,1)S(1)} %get-tuple-element.31), channel_id=1, source_target_pairs={{0,24},{1,25},{2,26},{3,27},{4,28},{5,29},{6,30},{7,31},{8,16},{9,... | collective-permute-start | bytes 442376 | tf_op jit(solution)/shard_map/ppermute | solution.py:549
  58.5 1.7 %copy-start.4 = (bf16[8,8,8,1024]{3,2,1,0:T(8,128)(2,1)S(1)}, bf16[8,8,8,1024]{3,2,1,0:T(8,128)(2,1)}, u32[]{:S(2)}) copy-start(bf16[8,8,8,1024]{3,2,1,0:T(8,128)(2,1)} %copy.16) | copy-start | bytes 3145732
  61.7 41.2 %all-to-all-start.2 = ((bf16[8,64,1024]{2,1,0:T(8,128)(2,1)}), bf16[8,64,1024]{2,1,0:T(8,128)(2,1)}, u32[]{:S(2)}, u32[]{:S(2)}) async-start(bf16[8,64,1024]{2,1,0:T(8,128)(2,1)} %copy.14), calls=%async_computation.2 | async-start | bytes 2097152 | tf_op jit(solution)/shard_map/all_to_all | solution.py:600
  67.7 16.8 %collective-permute-start.12 = (bf16[768,128]{1,0:T(8,128)(2,1)S(1)}, bf16[768,128]{1,0:T(8,128)(2,1)S(1)}, u32[]{:S(2)}, u32[]{:S(2)}) collective-permute-start(bf16[768,128]{1,0:T(8,128)(2,1)S(1)} %get-tuple-element.42), channel_id=1, source_target_pairs={{0,8},{1,9},{2,10},{3,11},{4,12},{5,13},{6,14},{7,15},{8,0},{9,1},... | collective-permute-start | bytes 589832 | tf_op jit(solution)/shard_map/ppermute | solution.py:549
  68.5 19.0 %collective-permute-start.13 = (bf16[768,128]{1,0:T(8,128)(2,1)S(1)}, bf16[768,128]{1,0:T(8,128)(2,1)S(1)}, u32[]{:S(2)}, u32[]{:S(2)}) collective-permute-start(bf16[768,128]{1,0:T(8,128)(2,1)S(1)} %get-tuple-element.43), channel_id=1, source_target_pairs={{0,16},{1,17},{2,18},{3,19},{4,20},{5,21},{6,22},{7,23},{8,24},{9,... | collective-permute-start | bytes 589832 | tf_op jit(solution)/shard_map/ppermute | solution.py:549
  69.0 19.7 %collective-permute-start.14 = (bf16[768,128]{1,0:T(8,128)(2,1)S(1)}, bf16[768,128]{1,0:T(8,128)(2,1)S(1)}, u32[]{:S(2)}, u32[]{:S(2)}) collective-permute-start(bf16[768,128]{1,0:T(8,128)(2,1)S(1)} %get-tuple-element.44), channel_id=1, source_target_pairs={{0,24},{1,25},{2,26},{3,27},{4,28},{5,29},{6,30},{7,31},{8,16},{9,... | collective-permute-start | bytes 589832 | tf_op jit(solution)/shard_map/ppermute | solution.py:549
  72.1 25.6 %collective-permute-start.10 = (bf16[2,64,1024]{2,1,0:T(8,128)(2,1)S(1)}, bf16[2,64,1024]{2,1,0:T(8,128)(2,1)S(1)}, u32[]{:S(2)}, u32[]{:S(2)}) collective-permute-start(bf16[2,64,1024]{2,1,0:T(8,128)(2,1)S(1)} %pad_maximum_fusion.4.refs_0_), channel_id=1, source_target_pairs={{0,6},{1,7},{2,4},{3,5},{4,2},{5,3},{6,0},{7,1},{8,14},{9,15},{10,... | collective-permute-start | bytes 786440 | tf_op jit(solution)/shard_map/ppermute | solution.py:549
  75.1 23.1 %collective-permute-start.6 = (bf16[2,64,1024]{2,1,0:T(8,128)(2,1)S(1)}, bf16[2,64,1024]{2,1,0:T(8,128)(2,1)S(1)}, u32[]{:S(2)}, u32[]{:S(2)}) collective-permute-start(bf16[2,64,1024]{2,1,0:T(8,128)(2,1)S(1)} %pad_maximum_fusion.4.refs_0_), channel_id=1, source_target_pairs={{0,2},{1,3},{2,0},{3,1},{4,6},{5,7},{6,4},{7,5},{8,10},{9,11},{10,... | collective-permute-start | bytes 786440 | tf_op jit(solution)/shard_map/ppermute | solution.py:549
  84.5 17.9 %collective-permute-start.8 = (bf16[2,64,1024]{2,1,0:T(8,128)(2,1)S(1)}, bf16[2,64,1024]{2,1,0:T(8,128)(2,1)S(1)}, u32[]{:S(2)}, u32[]{:S(2)}) collective-permute-start(bf16[2,64,1024]{2,1,0:T(8,128)(2,1)S(1)} %pad_maximum_fusion.4.refs_0_), channel_id=1, source_target_pairs={{0,4},{1,5},{2,6},{3,7},{4,0},{5,1},{6,2},{7,3},{8,12},{9,13},{10,... | collective-permute-start | bytes 786440 | tf_op jit(solution)/shard_map/ppermute | solution.py:549
  87.5 14.9 %collective-permute-start.5 = (bf16[2,64,1024]{2,1,0:T(8,128)(2,1)S(1)}, bf16[2,64,1024]{2,1,0:T(8,128)(2,1)S(1)}, u32[]{:S(2)}, u32[]{:S(2)}) collective-permute-start(bf16[2,64,1024]{2,1,0:T(8,128)(2,1)S(1)} %pad_maximum_fusion.4.refs_0_), channel_id=1, source_target_pairs={{0,1},{1,0},{2,3},{3,2},{4,5},{5,4},{6,7},{7,6},{8,9},{9,8},{10,11... | collective-permute-start | bytes 786440 | tf_op jit(solution)/shard_map/ppermute | solution.py:549
  88.7 22.5 %collective-permute-start.16 = (bf16[2,576,128]{2,1,0:T(8,128)(2,1)S(1)}, bf16[2,576,128]{2,1,0:T(8,128)(2,1)S(1)}, u32[]{:S(2)}, u32[]{:S(2)}) collective-permute-start(bf16[2,576,128]{2,1,0:T(8,128)(2,1)S(1)} %pad_maximum_fusion.3.refs_0_), channel_id=1, source_target_pairs={{0,2},{1,3},{2,0},{3,1},{4,6},{5,7},{6,4},{7,5},{8,10},{9,11},{10,... | collective-permute-start | bytes 884744 | tf_op jit(solution)/shard_map/ppermute | solution.py:549
  97.6 13.9 %collective-permute-start.18 = (bf16[2,576,128]{2,1,0:T(8,128)(2,1)S(1)}, bf16[2,576,128]{2,1,0:T(8,128)(2,1)S(1)}, u32[]{:S(2)}, u32[]{:S(2)}) collective-permute-start(bf16[2,576,128]{2,1,0:T(8,128)(2,1)S(1)} %pad_maximum_fusion.3.refs_0_), channel_id=1, source_target_pairs={{0,4},{1,5},{2,6},{3,7},{4,0},{5,1},{6,2},{7,3},{8,12},{9,13},{10,... | collective-permute-start | bytes 884744 | tf_op jit(solution)/shard_map/ppermute | solution.py:549
  98.2 17.5 %collective-permute-start.20 = (bf16[2,576,128]{2,1,0:T(8,128)(2,1)S(1)}, bf16[2,576,128]{2,1,0:T(8,128)(2,1)S(1)}, u32[]{:S(2)}, u32[]{:S(2)}) collective-permute-start(bf16[2,576,128]{2,1,0:T(8,128)(2,1)S(1)} %pad_maximum_fusion.3.refs_0_), channel_id=1, source_target_pairs={{0,6},{1,7},{2,4},{3,5},{4,2},{5,3},{6,0},{7,1},{8,14},{9,15},{10,... | collective-permute-start | bytes 884744 | tf_op jit(solution)/shard_map/ppermute | solution.py:549
  102.4 13.3 %collective-permute-start.11 = (bf16[2,64,1024]{2,1,0:T(8,128)(2,1)S(1)}, bf16[2,64,1024]{2,1,0:T(8,128)(2,1)S(1)}, u32[]{:S(2)}, u32[]{:S(2)}) collective-permute-start(bf16[2,64,1024]{2,1,0:T(8,128)(2,1)S(1)} %collective-permute-done.10.refs_6_), channel_id=1, source_target_pairs={{0,1},{1,0},{2,3},{3,2},{4,5},{5,4},{6,7},{7,6},{8,9},{9,8},{10,11... | collective-permute-start | bytes 786440 | tf_op jit(solution)/shard_map/ppermute | solution.py:549
  102.4 13.8 %collective-permute-start.7 = (bf16[2,64,1024]{2,1,0:T(8,128)(2,1)S(1)}, bf16[2,64,1024]{2,1,0:T(8,128)(2,1)S(1)}, u32[]{:S(2)}, u32[]{:S(2)}) collective-permute-start(bf16[2,64,1024]{2,1,0:T(8,128)(2,1)S(1)} %collective-permute-done.6.refs_2_), channel_id=1, source_target_pairs={{0,1},{1,0},{2,3},{3,2},{4,5},{5,4},{6,7},{7,6},{8,9},{9,8},{10,11... | collective-permute-start | bytes 786440 | tf_op jit(solution)/shard_map/ppermute | solution.py:549
  107.1 14.7 %all-to-all-start.3 = ((bf16[8,64,192]{2,1,0:T(8,128)(2,1)}), bf16[8,64,192]{2,1,0:T(8,128)(2,1)}, u32[]{:S(2)}, u32[]{:S(2)}) async-start(bf16[8,64,192]{2,1,0:T(8,128)(2,1)} %bitcast.10), calls=%async_computation.3 | async-start | bytes 524288 | tf_op jit(solution)/shard_map/all_to_all | solution.py:614
  111.1 10.0 %collective-permute-start.15 = (bf16[2,576,128]{2,1,0:T(8,128)(2,1)S(1)}, bf16[2,576,128]{2,1,0:T(8,128)(2,1)S(1)}, u32[]{:S(2)}, u32[]{:S(2)}) collective-permute-start(bf16[2,576,128]{2,1,0:T(8,128)(2,1)S(1)} %pad_maximum_fusion.3.refs_0_), channel_id=1, source_target_pairs={{0,1},{1,0},{2,3},{3,2},{4,5},{5,4},{6,7},{7,6},{8,9},{9,8},{10,11... | collective-permute-start | bytes 884744 | tf_op jit(solution)/shard_map/ppermute | solution.py:549
  111.5 8.0 %collective-permute-start.9 = (bf16[2,64,1024]{2,1,0:T(8,128)(2,1)S(1)}, bf16[2,64,1024]{2,1,0:T(8,128)(2,1)S(1)}, u32[]{:S(2)}, u32[]{:S(2)}) collective-permute-start(bf16[2,64,1024]{2,1,0:T(8,128)(2,1)S(1)} %collective-permute-done.8.refs_4_), channel_id=1, source_target_pairs={{0,1},{1,0},{2,3},{3,2},{4,5},{5,4},{6,7},{7,6},{8,9},{9,8},{10,11... | collective-permute-start | bytes 786440 | tf_op jit(solution)/shard_map/ppermute | solution.py:549
  115.7 5.5 %collective-permute-start.17 = (bf16[2,576,128]{2,1,0:T(8,128)(2,1)S(1)}, bf16[2,576,128]{2,1,0:T(8,128)(2,1)S(1)}, u32[]{:S(2)}, u32[]{:S(2)}) collective-permute-start(bf16[2,576,128]{2,1,0:T(8,128)(2,1)S(1)} %collective-permute-done.16.refs_2_), channel_id=1, source_target_pairs={{0,1},{1,0},{2,3},{3,2},{4,5},{5,4},{6,7},{7,6},{8,9},{9,8},{10,11... | collective-permute-start | bytes 884744 | tf_op jit(solution)/shard_map/ppermute | solution.py:549
  115.7 5.4 %collective-permute-start.19 = (bf16[2,576,128]{2,1,0:T(8,128)(2,1)S(1)}, bf16[2,576,128]{2,1,0:T(8,128)(2,1)S(1)}, u32[]{:S(2)}, u32[]{:S(2)}) collective-permute-start(bf16[2,576,128]{2,1,0:T(8,128)(2,1)S(1)} %collective-permute-done.18.refs_4_), channel_id=1, source_target_pairs={{0,1},{1,0},{2,3},{3,2},{4,5},{5,4},{6,7},{7,6},{8,9},{9,8},{10,11... | collective-permute-start | bytes 884744 | tf_op jit(solution)/shard_map/ppermute | solution.py:549
  116.2 4.9 %collective-permute-start.21 = (bf16[2,576,128]{2,1,0:T(8,128)(2,1)S(1)}, bf16[2,576,128]{2,1,0:T(8,128)(2,1)S(1)}, u32[]{:S(2)}, u32[]{:S(2)}) collective-permute-start(bf16[2,576,128]{2,1,0:T(8,128)(2,1)S(1)} %collective-permute-done.20.refs_6_), channel_id=1, source_target_pairs={{0,1},{1,0},{2,3},{3,2},{4,5},{5,4},{6,7},{7,6},{8,9},{9,8},{10,11... | collective-permute-start | bytes 884744 | tf_op jit(solution)/shard_map/ppermute | solution.py:549
  119.7 1.4 copy-start
  121.7 7.1 %copy-start.1 = (bf16[8,2,576,128]{3,2,1,0:T(8,128)(2,1)}, bf16[8,2,576,128]{3,2,1,0:T(8,128)(2,1)S(1)}, u32[]{:S(2)}) copy-start(bf16[8,2,576,128]{3,2,1,0:T(8,128)(2,1)S(1)} %shard_map.91) | copy-start | bytes 7077892
  123.0 0.8 copy-start.6
  123.8 14.3 %all-to-all-start.4 = ((bf16[16,64,128]{2,1,0:T(8,128)(2,1)}), bf16[16,64,128]{2,1,0:T(8,128)(2,1)}, u32[]{:S(2)}, u32[]{:S(2)}) async-start(bf16[16,64,128]{2,1,0:T(8,128)(2,1)} %broadcast_in_dim.48), calls=%async_computation.4 | async-start | bytes 524288 | tf_op jit(solution)/shard_map/all_to_all | solution.py:623
  128.9 1.4 slice-start
  129.0 3.8 %copy-start.5 = (bf16[1,64,1024]{2,1,0:T(8,128)(2,1)S(1)}, bf16[1,64,1024]{2,1,0:T(8,128)(2,1)}, u32[]{:S(2)}) copy-start(bf16[1,64,1024]{2,1,0:T(8,128)(2,1)} %stack.46) | copy-start | bytes 393220

commit v4 on v3

--- a/solution.py
+++ b/solution.py
@@ -367,6 +367,102 @@
     )(here, there, owner, spread)
 
 
+def deal_kernel(rows, even, odd, sems):
+    seat = lax.rem(lax.axis_index("ctx"), PIECES)
+    width = rows.shape[1] // PIECES
+    copies = []
+    for apart in range(PIECES):
+        first = pl.multiple_of((seat ^ apart) * width, width)
+        target = (odd if apart % 2 else even).at[apart // 2]
+        copies.append(
+            pltpu.make_async_copy(rows.at[:, pl.ds(first, width)], target, sems.at[apart])
+        )
+    for copy in copies:
+        copy.start()
+    for copy in copies:
+        copy.wait()
+
+
+def deal(rows, *after):
+    slab = jax.ShapeDtypeStruct((PIECES // 2, rows.shape[0], rows.shape[1] // PIECES), rows.dtype)
+
+    def kernel(rows, *refs):
+        deal_kernel(rows, *refs[-3:])
+
+    return pl.pallas_call(
+        kernel,
+        out_shape=(slab, slab),
+        in_specs=[pl.BlockSpec(memory_space=pl.ANY)] * (1 + len(after)),
+        out_specs=(pl.BlockSpec(memory_space=pltpu.VMEM),) * 2,
+        scratch_shapes=[pltpu.SemaphoreType.DMA((PIECES,))],
+        compiler_params=pltpu.CompilerParams(vmem_limit_bytes=16 << 20),
+        cost_estimate=pl.CostEstimate(flops=0, bytes_accessed=2 << 20, transcendentals=0),
+    )(rows, *after)
+
+
+def narrow_kernel(here, owner, own, mirror, across, both, *refs):
+    dealt, outs, (flat, left, right) = refs[:4], refs[4:8], refs[8:]
+    plane = lax.axis_index("groups")
+    half = lax.axis_index("ctx") // PIECES
+    close = owner[here[half]] // PIECES == half
+    count = own.shape[0]
+
+    def place(block, position):
+        flat[pl.ds(pl.multiple_of(position * count, count), count), :] = block[...].astype(
+            jnp.float32
+        )
+
+    @pl.when(close)
+    def _():
+        place(own, plane)
+        place(across, 1 - plane)
+
+    @pl.when(jnp.logical_not(close))
+    def _():
+        place(mirror, plane)
+        place(both, 1 - plane)
+
+    third = flat.shape[0] // 3
+    one = flat[pl.ds(0, third, stride=3), :]
+    two = flat[pl.ds(1, third, stride=3), :]
+    three = flat[pl.ds(2, third, stride=3), :]
+    lane = lax.broadcasted_iota(jnp.int32, one.shape, 1)
+    two = pltpu.roll(two, 64, 1)
+    three = pltpu.roll(three, 64, 1)
+    left[pl.ds(0, third, stride=2), :] = one
+    left[pl.ds(1, third, stride=2), :] = jnp.where(lane < 64, two, three)
+    right[pl.ds(0, third, stride=2), :] = pltpu.roll(two, 64, 1)
+    right[pl.ds(1, third, stride=2), :] = three
+    weight = jnp.concatenate([left[...], right[...]], 1).astype(jnp.bfloat16)
+    for block, out in zip(dealt, outs):
+        sides, rows, depth = block.shape
+        product = jnp.dot(
+            block[...].reshape(sides * rows, depth), weight, preferred_element_type=jnp.float32
+        )
+        out[...] = product[:, : 3 * ADAPTER_RANK].reshape(out.shape).astype(jnp.bfloat16)
+
+
+def narrow(here, owner, arrived, dealt):
+    sides, rows, depth = dealt[0].shape
+    partial_sums = jax.ShapeDtypeStruct((sides, rows, 3 * ADAPTER_RANK), jnp.bfloat16)
+    return pl.pallas_call(
+        narrow_kernel,
+        out_shape=(partial_sums,) * 4,
+        in_specs=[pl.BlockSpec(memory_space=pltpu.SMEM)] * 2
+        + [pl.BlockSpec(memory_space=pltpu.VMEM)] * 8,
+        out_specs=(pl.BlockSpec(memory_space=pltpu.VMEM),) * 4,
+        scratch_shapes=[
+            pltpu.VMEM((depth * 3 * ADAPTER_RANK // 128, 128), jnp.float32),
+            pltpu.VMEM((depth, 128), jnp.float32),
+            pltpu.VMEM((depth, 128), jnp.float32),
+        ],
+        compiler_params=pltpu.CompilerParams(vmem_limit_bytes=16 << 20),
+        cost_estimate=pl.CostEstimate(
+            flops=2 * 8 * rows * depth * 256, bytes_accessed=3 << 20, transcendentals=0
+        ),
+    )(here, owner, *arrived, *dealt)
+
+
 def assemble_kernel(*refs):
     pieces, out, sems = refs[:PIECES], refs[PIECES], refs[PIECES + 1]
     seat = lax.rem(lax.axis_index("ctx"), PIECES)
@@ -420,16 +516,19 @@
         return delta * cosine + pltpu.roll(delta, HEAD_SIZE // 2, 1) * sine
 
     half = lax.axis_index("ctx") * rows // BLOCK_TOKENS
-    for apart in range(key_up.shape[0]):
-        for seat in range(PIECES):
-            first = ((half ^ apart) * PIECES + seat) * rows
+    seat = lax.rem(lax.axis_index("ctx"), PIECES)
+    for side in range(key_up.shape[0]):
+        for apart in range(PIECES):
+            there = seat ^ apart
+            first = ((half ^ side) * PIECES + there) * rows
             span = pl.ds(pl.multiple_of(first, rows), rows)
-            delta = adapter_scale * dot(all_rank[span, :ADAPTER_RANK], key_up[apart])
+            rank = all_rank[apart % 2, apart // 2, side]
+            delta = adapter_scale * dot(rank[:, :ADAPTER_RANK], key_up[side])
             delta = turned(delta, cosines[span, :], sines[span, :])
-            full = key_base[seat, apart].astype(jnp.float32) + delta
+            full = key_base[there, side].astype(jnp.float32) + delta
             keys[span, :] = full.astype(jnp.bfloat16)
-            delta = adapter_scale * dot(all_rank[span, ADAPTER_RANK:], value_up[apart])
-            full = value_base[seat, apart].astype(jnp.float32) + delta
+            delta = adapter_scale * dot(rank[:, ADAPTER_RANK:], value_up[side])
+            full = value_base[there, side].astype(jnp.float32) + delta
             values[span, :] = full.astype(jnp.bfloat16)
     here = pl.ds(pl.multiple_of(base, rows), rows)
     cosine = cosines[here, :]
@@ -554,73 +653,80 @@
 ):
     plane = lax.axis_index("groups")
     index = lax.axis_index("ctx")
-    core = index % 2
     half = index // PIECES
     tok_rows = normed_input.shape[0]
     ctx = lax.axis_size("ctx")
     seq = ctx * tok_rows
     blocks = [list(range(PIECES)), list(range(PIECES, 2 * PIECES))]
-    base = jnp.concatenate([key_base, value_base], 1)
-    base = jnp.stack([base, swap(base, PIECES)])
+    def after(block, *others):
+        return lax.optimization_barrier((block, others))[0]
+
     elsewhere = swap(stretch_adapter, 2 * PIECES)
     packed_rest = pack_row(adapter_pool, REST)
     packed_down = pack_row(adapter_pool, DOWN, packed_rest)
-    ids = jnp.arange(adapter_owner.shape[0], dtype=jnp.int32)
+    even, odd = deal(normed_input, packed_rest)
+    sibling = swap(odd, 1)
+    base = jnp.concatenate([key_base, value_base], 1)
+    base = jnp.stack([base, swap(base, PIECES)])
     slots = jnp.sum(
-        jnp.where(stretch_adapter[:, None] == ids[None, :], adapter_owner[None, :], 0), axis=1
+        jnp.where(
+            stretch_adapter[:, None] == jnp.arange(adapter_owner.shape[0], dtype=jnp.int32)[None, :],
+            adapter_owner[None, :],
+            0,
+        ),
+        axis=1,
     )
     near = (slots // PIECES) == half
     close = jnp.where(half == 0, near[0], near[1])
     far_close = jnp.where(half == 0, near[1], near[0])
 
-    def settle(arrived, close):
-        own = jnp.where(close, arrived[0], arrived[1])
-        other = jnp.where(close, arrived[2], arrived[3])
-        low = plane == 0
-        return jnp.stack([jnp.where(low, own, other), jnp.where(low, other, own)])
-
     def exchange(sent):
         return [swap(block, flip * PIECES) if flip else block for flip, block in enumerate(sent)]
 
     def gather(block):
-        parts = [swap(block, apart) if apart else block for apart in (0, 2, 4, 6)]
+        four = swap(block, 4)
+        return [block, swap(block, 2), four, swap(four, 2)]
+
+    def complete(parts, *others):
+        parts = [after(part, *others) for part in parts]
         return assemble([piece for part in parts for piece in (part, swap(part, 1))])
 
     spread_rest = lax.all_to_all(packed_rest, "ctx", 0, 0, axis_index_groups=blocks)
     sent_rest = pick(spread_rest, stretch_adapter, elsewhere, adapter_owner, (128, 32))
-    sent_rest, packed_down = lax.optimization_barrier((sent_rest, packed_down))
+    packed_down = after(packed_down, sent_rest, sibling, base)
     spread_down = lax.all_to_all(packed_down, "ctx", 0, 0, axis_index_groups=blocks)
-    mine = jnp.arange(sent_rest[0].shape[0], dtype=jnp.int32)[:, None] < 544
-    rest = settle(exchange(sent_rest), jnp.where(mine, close, far_close))
-
-    rest, spread_down = lax.optimization_barrier((rest, spread_down))
+    arrived = exchange(sent_rest)
+    mine = jnp.arange(arrived[0].shape[0], dtype=jnp.int32)[:, None] < 544
+    wide_close = jnp.where(mine, close, far_close)
+    own = jnp.where(wide_close, arrived[0], arrived[1])
+    other = jnp.where(wide_close, arrived[2], arrived[3])
+    rest = jnp.stack([jnp.where(plane == 0, own, other), jnp.where(plane == 0, other, own)])
+
+    spread_down = after(spread_down, rest)
     sent_down = pick(spread_down, stretch_adapter, elsewhere, adapter_owner, None)
-    moving = normed_input.reshape(tok_rows, PIECES, D // PIECES).transpose(1, 0, 2)
-    moving, rest, base, sent_down = lax.optimization_barrier((moving, rest, base, sent_down))
-    moving = lax.all_to_all(moving, "ctx", 0, 0, axis_index_groups=blocks)
-    down_slice = settle(exchange(sent_down), close).reshape(D // PIECES, 3 * ADAPTER_RANK)
-
-    rest = gather(rest)
+    arrived = exchange(sent_down)
+    dealt = [jnp.stack([even[j], sibling[j]]) for j in range(PIECES // 2)]
+    dealt = [swap(after(block, arrived[2]), 2 * j) if j else block for j, block in enumerate(dealt)]
+    rest = gather(after(rest, arrived[2]))
+    partial_sums = narrow(stretch_adapter, adapter_owner, arrived, dealt)
+    base = gather(after(base, *partial_sums))
+
+    back = [swap(block, 2 * j) if j else block for j, block in enumerate(partial_sums)]
+    back = sum(block.astype(jnp.float32) for block in back)
+    own_rank = back[0] + swap(back[1].astype(jnp.bfloat16), 1).astype(jnp.float32)
+    own_rank = own_rank.astype(jnp.bfloat16)
+    all_rank = own_rank[:, ADAPTER_RANK:]
+    all_rank = jnp.stack([all_rank, swap(all_rank, PIECES)])
+    all_rank = jnp.stack([swap(all_rank, apart) if apart else all_rank for apart in (0, 2, 4, 6)])
+    all_rank = jnp.stack([all_rank, swap(all_rank, 1)])
+
+    rest = complete(rest, *partial_sums)
     query_up = rest[:, :, :128].reshape(ADAPTER_RANK, QH * HEAD_SIZE)
     keyval_up = jnp.stack([rest[:, :, 128:160], rest[:, :, 544:]])
     keyval_up = keyval_up.reshape(2, ADAPTER_RANK, 2 * KEYVALUE_HEADS * HEAD_SIZE)
     down_out = rest[:, :, 160:288].reshape(QH * HEAD_SIZE, ADAPTER_RANK)
     up_out = rest[:, :, 288:544].reshape(ADAPTER_RANK, D)
-    base = gather(base)
-
-    partial_rows = jnp.dot(
-        moving.reshape(BLOCK_TOKENS, D // PIECES), down_slice, preferred_element_type=jnp.float32
-    ).astype(jnp.bfloat16)
-    partial_rows = lax.all_to_all(
-        partial_rows.reshape(PIECES, tok_rows, 3 * ADAPTER_RANK),
-        "ctx",
-        0,
-        0,
-        axis_index_groups=blocks,
-    )
-    own_rank = jnp.sum(partial_rows.astype(jnp.float32), axis=0).astype(jnp.bfloat16)
-    all_rank = jnp.broadcast_to(own_rank[None, :, ADAPTER_RANK:], (ctx, tok_rows, 2 * ADAPTER_RANK))
-    all_rank = lax.all_to_all(all_rank, "ctx", 0, 0).reshape(seq, 2 * ADAPTER_RANK)
+    base = complete(base)
 
     half_dim = HEAD_SIZE // 2
     frequency = rope_base ** (-(jnp.arange(half_dim, dtype=jnp.float32) * 2.0) / HEAD_SIZE)

time: 150 us -> 172 us (1.15)
  waiting for transfers between devices: 53.5 us -> 72.9 us
  local copies, waits for them, and re-layouts: 14 us -> 18.2 us
  Pallas kernels: 22.1 us -> 25.8 us
  starting transfers between devices: 48.3 us -> 45.3 us
  matrix products: 2.41 us -> 0 us
    ppermute x22 -> x35, waiting for transfers between devices: 36.9 us -> 69 us  [swap(): lax.ppermute(block, ('groups', 'ctx'), [(i, i ^ mask) for i in range(4 *...]
    all_to_all x3 -> x0, starting transfers between devices: 14.2 us -> none  [the longest x1 5.95 us: direct_shards(): moving = lax.all_to_all(moving, 'ctx', 0, 0, axis_index_groups=blocks)]
    ppermute x22 -> x35, starting transfers between devices: 25.3 us -> 35.2 us  [swap(): lax.ppermute(block, ('groups', 'ctx'), [(i, i ^ mask) for i in range(4 *...]
    all_to_all x1, waiting for transfers between devices: 10.1 us -> 2.07 us  [direct_shards(): lax.all_to_all(packed_rest, 'ctx', 0, 0, axis_index_groups=blocks)]
    all_to_all x3 -> x0, waiting for transfers between devices: 4.62 us -> none  [the longest x1 4.61 us: direct_shards(): lax.all_to_all(all_rank, 'ctx', 0, 0).reshape(seq, 2 * ADAPTER_RANK)]
    slice x1 -> x2, local copies, waits for them, and re-layouts: 0.08 us -> 2.58 us  [direct_shards(): dealt = [jnp.stack([even[j], sibling[j]]) for j in range(PIECES // 2)]]
    pallas_call x0 -> x2, Pallas kernels: none -> 2.44 us  [the longest x1 1.36 us: narrow(): pl.pallas_call(narrow_kernel, out_shape=(partial_sums,) * 4, in_specs=[pl...]
    dot_general x1 -> x0, matrix products: 2.41 us -> none  [direct_shards(): jnp.dot(moving.reshape(BLOCK_TOKENS, D // PIECES), down_slice, preferred_...]
  transfers between devices with their start and end apart: 27 -> 37, of which waited for: 11 -> 17; matrix products, arithmetic and copies ran while one was open for 11% -> 11% of each run, Pallas kernels for 3% -> 4%
where the time goes in v4:
time: 172 us; the launch traced here: 171 us
  waiting for transfers between devices  72.9 us (42%)
  starting transfers between devices  45.3 us (26%)
  Pallas kernels  25.8 us (15%)
  local copies, waits for them, and re-layouts  18.2 us (11%)
  other arithmetic  5.33 us (3%)
  between operations  3.56 us (2%)
    ppermute x35, waiting for transfers between devices, swap(): lax.ppermute(block, ('groups', 'ctx'), [(i, i ^ mask) for i in range(4 *...  69 us
    ppermute x35, starting transfers between devices, swap(): lax.ppermute(block, ('groups', 'ctx'), [(i, i ^ mask) for i in range(4 *...  35.2 us
    pallas_call x1, Pallas kernels, attend(): pl.pallas_call(attend_kernel, grid=(KEYVALUE_HEADS,), out_shape=(jax.Shap...  11.5 us
    pallas_call x2, Pallas kernels, pack_row(): pl.pallas_call(partial(pack_kernel, sections), out_shape=jax.ShapeDtypeSt...  6.74 us
    all_to_all x1, starting transfers between devices, direct_shards(): lax.all_to_all(packed_rest, 'ctx', 0, 0, axis_index_groups=blocks)  5.37 us
    all_to_all x1, starting transfers between devices, direct_shards(): lax.all_to_all(packed_down, 'ctx', 0, 0, axis_index_groups=blocks)  4.79 us
    unnamed x41, local copies, waits for them, and re-layouts  4.29 us
  transfers between devices with their start and end apart: 37, of which 17 were waited for; matrix products, arithmetic and copies ran while one was open for 11% of the time, Pallas kernels for 4%

profile of v4, /device:TPU:0, one launch (start us, length us, event | category | flops | bytes accessed | tf_op | source)
XLA Modules:
  0.0 171.2 jit_solution(6420538007990418798)
XLA Ops:
  0.6 3.3 %shard_map.86.refs_0_ = bf16[8,544,128]{2,1,0:T(8,128)(2,1)} custom-call(bf16[1,2686976]{1,0:T(2,128)(2,1)} %pool.3), custom_call_target="tpu_custom_call" | custom-call | bytes 8388608 | tf_op jit(solution)/shard_map/pallas_call | solution.py:314
  4.0 5.4 %all-to-all-start = ((bf16[8,544,128]{2,1,0:T(8,128)(2,1)}), bf16[8,544,128]{2,1,0:T(8,128)(2,1)S(1)}, u32[]{:S(2)}, u32[]{:S(2)}) async-start(bf16[8,544,128]{2,1,0:T(8,128)(2,1)} %shard_map.86.refs_0_), calls=%async_computation | async-start | bytes 2228224 | tf_op jit(solution)/shard_map/all_to_all | solution.py:694
  9.4 1.1 shard_map.89
  10.5 0.8 copy-done.3
  11.8 2.7 %collective-permute-start = (bf16[64,1024]{1,0:T(8,128)(2,1)S(1)}, bf16[64,1024]{1,0:T(8,128)(2,1)S(1)}, u32[]{:S(2)}, u32[]{:S(2)}) collective-permute-start(bf16[64,1024]{1,0:T(8,128)(2,1)S(1)} %constant_dynamic-update-slice_fusion), channel_id=1, source_target_pairs={{0,8},{1,9},{2,10},{3,11},{4,12},{5,13},{6,14},{7,15},{8,0},{9,1},... | collective-permute-start | bytes 393224 | tf_op jit(solution)/shard_map/ppermute | solution.py:648
  14.4 1.5 collective-permute-start.1
  16.0 3.5 %shard_map.87 = bf16[8,768,128]{2,1,0:T(8,128)(2,1)} custom-call(bf16[1,2686976]{1,0:T(2,128)(2,1)} %pool.3, bf16[8,544,128]{2,1,0:T(8,128)(2,1)} %shard_map.86.refs_0_), custom_call_target="tpu_custom_call" | custom-call | bytes 8388608 | tf_op jit(solution)/shard_map/pallas_call | solution.py:314
  19.4 5.8 %collective-permute-done = bf16[64,1024]{1,0:T(8,128)(2,1)S(1)} collective-permute-done((bf16[64,1024]{1,0:T(8,128)(2,1)S(1)}, bf16[64,1024]{1,0:T(8,128)(2,1)S(1)}, u32[]{:S(2)}, u32[]{:S(2)}) %collective-permute-start) | collective-permute-done | bytes 131104 | tf_op jit(solution)/shard_map/ppermute | solution.py:648
  25.3 2.1 %all-to-all-done.spread = bf16[8,544,128]{2,1,0:T(8,128)(2,1)S(1)} async-done(((bf16[8,544,128]{2,1,0:T(8,128)(2,1)}), bf16[8,544,128]{2,1,0:T(8,128)(2,1)S(1)}, u32[]{:S(2)}, u32[]{:S(2)}) %all-to-all-start) | async-done | bytes 1114144 | tf_op jit(solution)/shard_map/all_to_all | solution.py:694
  27.4 1.4 shard_map.88
  28.8 0.7 copy-done.7
  29.5 0.7 copy-done.9
  30.2 0.8 copy-done.11
  30.9 4.8 %all-to-all-start.1 = ((bf16[8,768,128]{2,1,0:T(8,128)(2,1)}), bf16[8,768,128]{2,1,0:T(8,128)(2,1)S(1)}, u32[]{:S(2)}, u32[]{:S(2)}) async-start(bf16[8,768,128]{2,1,0:T(8,128)(2,1)} %shard_map.87), calls=%async_computation.1 | async-start | bytes 3145728 | tf_op jit(solution)/shard_map/all_to_all | solution.py:697
  35.9 0.6 fusion.13
  39.1 0.8 fusion.11
  40.4 1.5 collective-permute-start.4
  41.9 2.3 %collective-permute-start.5 = (bf16[576,128]{1,0:T(8,128)(2,1)S(1)}, bf16[576,128]{1,0:T(8,128)(2,1)S(1)}, u32[]{:S(2)}, u32[]{:S(2)}) collective-permute-start(bf16[576,128]{1,0:T(8,128)(2,1)S(1)} %get-tuple-element.30), channel_id=1, source_target_pairs={{0,24},{1,25},{2,26},{3,27},{4,28},{5,29},{6,30},{7,31},{8,16},{9,... | collective-permute-start | bytes 442376 | tf_op jit(solution)/shard_map/ppermute | solution.py:648
  44.2 1.8 %fusion.12 = (bf16[1,64,1024]{2,1,0:T(8,128)(2,1)}, bf16[1,64,1024]{2,1,0:T(8,128)(2,1)}, bf16[1,64,1024]{2,1,0:T(8,128)(2,1)}, bf16[1,64,1024]{2,1,0:T(8,128)(2,1)S(1)}) fusion(bf16[4,64,1024]{2,1,0:T(8,128)(2,1)} %copy-done.11), kind=kLoop, calls=%fused_computation.44 | loop fusion | bytes 1048576 | tf_op jit(solution)/shard_map/slice | solution.py:708
  46.1 11.0 %collective-permute-done.3 = bf16[576,128]{1,0:T(8,128)(2,1)S(1)} collective-permute-done((bf16[576,128]{1,0:T(8,128)(2,1)S(1)}, bf16[576,128]{1,0:T(8,128)(2,1)S(1)}, u32[]{:S(2)}, u32[]{:S(2)}) %collective-permute-start.3) | collective-permute-done | bytes 147488 | tf_op jit(solution)/shard_map/ppermute | solution.py:648
  57.1 3.0 %collective-permute-done.5 = bf16[576,128]{1,0:T(8,128)(2,1)S(1)} collective-permute-done((bf16[576,128]{1,0:T(8,128)(2,1)S(1)}, bf16[576,128]{1,0:T(8,128)(2,1)S(1)}, u32[]{:S(2)}, u32[]{:S(2)}) %collective-permute-start.5) | collective-permute-done | bytes 147488 | tf_op jit(solution)/shard_map/ppermute | solution.py:648
  60.3 1.9 %all-to-all-done.1.spread = bf16[8,768,128]{2,1,0:T(8,128)(2,1)S(1)} async-done(((bf16[8,768,128]{2,1,0:T(8,128)(2,1)}), bf16[8,768,128]{2,1,0:T(8,128)(2,1)S(1)}, u32[]{:S(2)}, u32[]{:S(2)}) %all-to-all-start.1) | async-done | bytes 1572896 | tf_op jit(solution)/shard_map/all_to_all | solution.py:697
  62.1 1.7 shard_map.90
  63.8 1.6 collective-permute-start.7
  65.5 4.8 %collective-permute-done.7.across = bf16[768,128]{1,0:T(8,128)(2,1)S(1)} collective-permute-done((bf16[768,128]{1,0:T(8,128)(2,1)S(1)}, bf16[768,128]{1,0:T(8,128)(2,1)S(1)}, u32[]{:S(2)}, u32[]{:S(2)}) %collective-permute-start.7) | collective-permute-done | bytes 196640 | tf_op jit(solution)/shard_map/ppermute | solution.py:648
  70.3 1.7 %collective-permute-start.10 = (bf16[2,64,1024]{2,1,0:T(8,128)(2,1)S(1)}, bf16[2,64,1024]{2,1,0:T(8,128)(2,1)S(1)}, u32[]{:S(2)}, u32[]{:S(2)}) collective-permute-start(bf16[2,64,1024]{2,1,0:T(8,128)(2,1)S(1)} %get-tuple-element.40), channel_id=1, source_target_pairs={{0,4},{1,5},{2,6},{3,7},{4,0},{5,1},{6,2},{7,3},{8,12},{9,13},{10,... | collective-permute-start | bytes 786440 | tf_op jit(solution)/shard_map/ppermute | solution.py:648
  72.0 1.5 collective-permute-start.9
  73.8 2.8 %collective-permute-start.6 = (bf16[768,128]{1,0:T(8,128)(2,1)S(1)}, bf16[768,128]{1,0:T(8,128)(2,1)S(1)}, u32[]{:S(2)}, u32[]{:S(2)}) collective-permute-start(bf16[768,128]{1,0:T(8,128)(2,1)S(1)} %get-tuple-element.35), channel_id=1, source_target_pairs={{0,8},{1,9},{2,10},{3,11},{4,12},{5,13},{6,14},{7,15},{8,0},{9,1},... | collective-permute-start | bytes 589832 | tf_op jit(solution)/shard_map/ppermute | solution.py:648
  76.6 1.1 collective-permute-start.8
  77.7 10.8 %collective-permute-done.6.mirror = bf16[768,128]{1,0:T(8,128)(2,1)S(1)} collective-permute-done((bf16[768,128]{1,0:T(8,128)(2,1)S(1)}, bf16[768,128]{1,0:T(8,128)(2,1)S(1)}, u32[]{:S(2)}, u32[]{:S(2)}) %collective-permute-start.6) | collective-permute-done | bytes 196640 | tf_op jit(solution)/shard_map/ppermute | solution.py:648
  88.5 2.1 %collective-permute-done.8.both = bf16[768,128]{1,0:T(8,128)(2,1)S(1)} collective-permute-done((bf16[768,128]{1,0:T(8,128)(2,1)S(1)}, bf16[768,128]{1,0:T(8,128)(2,1)S(1)}, u32[]{:S(2)}, u32[]{:S(2)}) %collective-permute-start.8) | collective-permute-done | bytes 196640 | tf_op jit(solution)/shard_map/ppermute | solution.py:648
  90.6 1.6 collective-permute-done.11.refs_3_
  92.2 1.4 shard_map.91
  93.6 0.6 collective-permute-start.19
  94.2 2.6 %collective-permute-start.20 = (bf16[2,64,192]{2,1,0:T(8,128)(2,1)S(1)}, bf16[2,64,192]{2,1,0:T(8,128)(2,1)S(1)}, u32[]{:S(2)}, u32[]{:S(2)}) collective-permute-start(bf16[2,64,192]{2,1,0:T(8,128)(2,1)S(1)} %get-tuple-element.44), channel_id=1, source_target_pairs={{0,4},{1,5},{2,6},{3,7},{4,0},{5,1},{6,2},{7,3},{8,12},{9,13},{10,... | collective-permute-start | bytes 147464 | tf_op jit(solution)/shard_map/ppermute | solution.py:648
  97.3 1.3 collective-permute-done.19
  99.1 2.9 %collective-permute-done.21 = bf16[2,64,192]{2,1,0:T(8,128)(2,1)S(1)} collective-permute-done((bf16[2,64,192]{2,1,0:T(8,128)(2,1)S(1)}, bf16[2,64,192]{2,1,0:T(8,128)(2,1)S(1)}, u32[]{:S(2)}, u32[]{:S(2)}) %collective-permute-start.21) | collective-permute-done | bytes 49184 | tf_op jit(solution)/shard_map/ppermute | solution.py:648
  102.4 0.9 collective-permute-done.22
  103.4 0.9 collective-permute-start.23
  104.3 5.3 %collective-permute-done.23 = bf16[64,128]{1,0:T(8,128)(2,1)S(1)} collective-permute-done((bf16[64,128]{1,0:T(8,128)(2,1)S(1)}, bf16[64,128]{1,0:T(8,128)(2,1)S(1)}, u32[]{:S(2)}, u32[]{:S(2)}) %collective-permute-start.23) | collective-permute-done | bytes 16416 | tf_op jit(solution)/shard_map/ppermute | solution.py:648
  109.7 3.0 %collective-permute-start.25 = (bf16[2,64,128]{2,1,0:T(8,128)(2,1)S(1)}, bf16[2,64,128]{2,1,0:T(8,128)(2,1)S(1)}, u32[]{:S(2)}, u32[]{:S(2)}) collective-permute-start(bf16[2,64,128]{2,1,0:T(8,128)(2,1)S(1)} %get-tuple-element.69), channel_id=1, source_target_pairs={{0,4},{1,5},{2,6},{3,7},{4,0},{5,1},{6,2},{7,3},{8,12},{9,13},{10,... | collective-permute-start | bytes 98312 | tf_op jit(solution)/shard_map/ppermute | solution.py:648
  112.7 1.0 collective-permute-start.24
  114.2 1.0 collective-permute-start.29
  115.2 2.0 %collective-permute-start.15 = (bf16[2,64,1024]{2,1,0:T(8,128)(2,1)S(1)}, bf16[2,64,1024]{2,1,0:T(8,128)(2,1)S(1)}, u32[]{:S(2)}, u32[]{:S(2)}) collective-permute-start(bf16[2,64,1024]{2,1,0:T(8,128)(2,1)S(1)} %pad_maximum_fusion.3.refs_0_), channel_id=1, source_target_pairs={{0,4},{1,5},{2,6},{3,7},{4,0},{5,1},{6,2},{7,3},{8,12},{9,13},{10,... | collective-permute-start | bytes 786440 | tf_op jit(solution)/shard_map/ppermute | solution.py:648
  117.2 1.0 collective-permute-start.13
  118.2 1.0 collective-permute-start.33
  119.4 5.2 %collective-permute-done.29.refs_2_ = bf16[2,576,128]{2,1,0:T(8,128)(2,1)S(1)} collective-permute-done((bf16[2,576,128]{2,1,0:T(8,128)(2,1)S(1)}, bf16[2,576,128]{2,1,0:T(8,128)(2,1)S(1)}, u32[]{:S(2)}, u32[]{:S(2)}) %collective-permute-start.29) | collective-permute-done | bytes 294944 | tf_op jit(solution)/shard_map/ppermute | solution.py:648
  124.5 10.4 %collective-permute-done.33.refs_6_ = bf16[2,576,128]{2,1,0:T(8,128)(2,1)S(1)} collective-permute-done((bf16[2,576,128]{2,1,0:T(8,128)(2,1)S(1)}, bf16[2,576,128]{2,1,0:T(8,128)(2,1)S(1)}, u32[]{:S(2)}, u32[]{:S(2)}) %collective-permute-start.33) | collective-permute-done | bytes 294944 | tf_op jit(solution)/shard_map/ppermute | solution.py:648
  135.5 1.0 collective-permute-start.17
  136.5 1.9 %fusion = (f32[1024,64]{1,0:T(8,128)S(1)}, f32[1024,64]{1,0:T(8,128)S(1)}, f32[1024,64]{1,0:T(8,128)S(1)}) fusion(f32[64]{0:T(128)S(1)} %multiply_power_fusion, f32[1024]{0:T(1024)S(1)} %iota_convert_fusion), kind=kLoop, calls=%fused_computation.12 | loop fusion | flops 131072 | bytes 790784 | tf_op jit(solution)/shard_map/neg | solution.py:737
  138.4 1.4 pad_maximum_fusion
  139.7 0.7 pad_maximum_fusion.8.all_rank
  140.5 3.4 %collective-permute-done.17.refs_6_ = bf16[2,64,1024]{2,1,0:T(8,128)(2,1)} collective-permute-done((bf16[2,64,1024]{2,1,0:T(8,128)(2,1)S(1)}, bf16[2,64,1024]{2,1,0:T(8,128)(2,1)}, u32[]{:S(2)}, u32[]{:S(2)}) %collective-permute-start.17) | collective-permute-done | bytes 262176 | tf_op jit(solution)/shard_map/ppermute | solution.py:648
  145.5 0.7 fusion.10
  146.1 1.0 slice.86
  147.2 1.0 stack.94
  148.2 2.3 %reshape.41.up_out = bf16[64,8192]{1,0:T(8,128)(2,1)} reshape(bf16[8,2,256,128]{3,2,1,0:T(8,128)(2,1)} %slice.86) | data formatting | bytes 2097152 | tf_op jit(solution)/shard_map/reshape | solution.py:728
  150.5 1.1 fusion.9
  151.6 2.4 %reshape.40.down_out = bf16[4096,64]{1,0:T(8,128)(2,1)} reshape(bf16[8,2,128,128]{3,2,1,0:T(8,128)(2,1)} %get-tuple-element.52) | data formatting | bytes 1048576 | tf_op jit(solution)/shard_map/reshape | solution.py:727
  154.0 2.1 %reshape.39.query_up = bf16[64,4096]{1,0:T(8,128)(2,1)} reshape(bf16[8,2,128,128]{3,2,1,0:T(8,128)(2,1)} %get-tuple-element.53) | data formatting | bytes 1048576 | tf_op jit(solution)/shard_map/reshape | solution.py:724
  156.1 0.8 pad_maximum_fusion.9.key_up.value_up
  156.8 1.5 shard_map.92.key_base.value_base
  158.4 1.3 copy-done
  159.7 11.5 %shard_map.94 = (bf16[64,4096]{1,0:T(8,128)(2,1)}, bf16[64,8192]{1,0:T(8,128)(2,1)}) custom-call(bf16[64,4096]{1,0:T(8,128)(2,1)} %query_block.1, bf16[8,2,64,1024]{3,2,1,0:T(8,128)(2,1)} %copy-done, bf16[8,2,64,1024]{3,2,1,0:T(8,128)(2,1)} %copy-done, bf16[64,192]{1,0:T(8,128)(2,1)} %copy-done.17, bf16[2,4,2,64,128]{4,3,2,1,0:T(8,128)(2,1)} %pad_maximum_fusion.8.all_rank, ...), custom_call_target="tpu_custom_call" | custom-call | flops 1073741824 | bytes 10485760 | tf_op jit(solution)/shard_map/pallas_call | solution.py:595
  (93 shorter events, 6.2 us)
Async XLA Ops:
  3.9 5.4 %copy-start.1 = (bf16[8,544,128]{2,1,0:T(8,128)(2,1)S(1)}, bf16[8,544,128]{2,1,0:T(8,128)(2,1)}, u32[]{:S(2)}) copy-start(bf16[8,544,128]{2,1,0:T(8,128)(2,1)} %shard_map.86.refs_0_) | copy-start | bytes 3342340
  3.9 5.4 %copy-start.2 = (bf16[64,8192]{1,0:T(8,128)(2,1)S(1)}, bf16[64,8192]{1,0:T(8,128)(2,1)}, u32[]{:S(2)}) copy-start(bf16[64,8192]{1,0:T(8,128)(2,1)} %rows.1) | copy-start | bytes 3145732
  3.9 7.8 %copy-start.18 = (bf16[64,512]{1,0:T(8,128)(2,1)S(1)}, bf16[64,512]{1,0:T(8,128)(2,1)}, u32[]{:S(2)}) copy-start(bf16[64,512]{1,0:T(8,128)(2,1)} %param.9) | copy-start | bytes 196612
  4.0 7.8 %copy-start.19 = (bf16[64,512]{1,0:T(8,128)(2,1)S(1)}, bf16[64,512]{1,0:T(8,128)(2,1)}, u32[]{:S(2)}) copy-start(bf16[64,512]{1,0:T(8,128)(2,1)} %param.10) | copy-start | bytes 196612
  4.0 10.5 %copy-start.5 = (s32[2]{0:T(128)S(1)}, s32[2]{0:T(128)}, u32[]{:S(2)}) copy-start(s32[2]{0:T(128)} %here.5) | copy-start | bytes 28
  4.0 23.4 %all-to-all-start = ((bf16[8,544,128]{2,1,0:T(8,128)(2,1)}), bf16[8,544,128]{2,1,0:T(8,128)(2,1)S(1)}, u32[]{:S(2)}, u32[]{:S(2)}) async-start(bf16[8,544,128]{2,1,0:T(8,128)(2,1)} %shard_map.86.refs_0_), calls=%async_computation | async-start | bytes 2228224 | tf_op jit(solution)/shard_map/all_to_all | solution.py:694
  10.4 0.8 copy-start.3
  11.2 18.9 %collective-permute-start.2 = (bf16[4,64,1024]{2,1,0:T(8,128)(2,1)}, bf16[4,64,1024]{2,1,0:T(8,128)(2,1)S(1)}, u32[]{:S(2)}, u32[]{:S(2)}) collective-permute-start(bf16[4,64,1024]{2,1,0:T(8,128)(2,1)} %get-tuple-element.31), channel_id=1, source_target_pairs={{0,1},{1,0},{2,3},{3,2},{4,5},{5,4},{6,7},{7,6},{8,9},{9,8},{10,11... | collective-permute-start | bytes 1572872 | tf_op jit(solution)/shard_map/ppermute | solution.py:648
  11.8 15.6 %copy-start.6 = (s32[16]{0:T(128)S(1)}, s32[16]{0:T(128)}, u32[]{:S(2)}) copy-start(s32[16]{0:T(128)} %owner.5) | copy-start | bytes 196
  11.8 13.5 %collective-permute-start = (bf16[64,1024]{1,0:T(8,128)(2,1)S(1)}, bf16[64,1024]{1,0:T(8,128)(2,1)S(1)}, u32[]{:S(2)}, u32[]{:S(2)}) collective-permute-start(bf16[64,1024]{1,0:T(8,128)(2,1)S(1)} %constant_dynamic-update-slice_fusion), channel_id=1, source_target_pairs={{0,8},{1,9},{2,10},{3,11},{4,12},{5,13},{6,14},{7,15},{8,0},{9,1},... | collective-permute-start | bytes 393224 | tf_op jit(solution)/shard_map/ppermute | solution.py:648
  14.4 10.8 %collective-permute-start.1 = (s32[2]{0:T(128)S(1)}, s32[2]{0:T(128)S(1)}, u32[]{:S(2)}, u32[]{:S(2)}) collective-permute-start(s32[2]{0:T(128)S(1)} %copy-done.5), channel_id=1, source_target_pairs={{0,16},{1,17},{2,18},{3,19},{4,20},{5,21},{6,22},{7,23},{8,24},{9,... | collective-permute-start | bytes 32 | tf_op jit(solution)/shard_map/ppermute | solution.py:648
  25.3 13.8 %copy-start.4 = (bf16[4,64,1024]{2,1,0:T(8,128)(2,1)S(1)}, bf16[4,64,1024]{2,1,0:T(8,128)(2,1)}, u32[]{:S(2)}) copy-start(bf16[4,64,1024]{2,1,0:T(8,128)(2,1)} %copy-done.3) | copy-start | bytes 1572868
  28.8 0.7 copy-start.7
  29.5 0.7 copy-start.9
  30.1 0.8 copy-start.11
  30.1 9.7 %copy-start.10 = (bf16[576,128]{1,0:T(8,128)(2,1)S(1)}, bf16[576,128]{1,0:T(8,128)(2,1)}, u32[]{:S(2)}) copy-start(bf16[576,128]{1,0:T(8,128)(2,1)} %copy-done.9) | copy-start | bytes 442372
  30.1 10.2 %copy-start.8 = (bf16[576,128]{1,0:T(8,128)(2,1)S(1)}, bf16[576,128]{1,0:T(8,128)(2,1)}, u32[]{:S(2)}) copy-start(bf16[576,128]{1,0:T(8,128)(2,1)} %copy-done.7) | copy-start | bytes 442372
  30.9 31.2 %all-to-all-start.1 = ((bf16[8,768,128]{2,1,0:T(8,128)(2,1)}), bf16[8,768,128]{2,1,0:T(8,128)(2,1)S(1)}, u32[]{:S(2)}, u32[]{:S(2)}) async-start(bf16[8,768,128]{2,1,0:T(8,128)(2,1)} %shard_map.87), calls=%async_computation.1 | async-start | bytes 3145728 | tf_op jit(solution)/shard_map/all_to_all | solution.py:697
  39.8 17.2 %collective-permute-start.3 = (bf16[576,128]{1,0:T(8,128)(2,1)S(1)}, bf16[576,128]{1,0:T(8,128)(2,1)S(1)}, u32[]{:S(2)}, u32[]{:S(2)}) collective-permute-start(bf16[576,128]{1,0:T(8,128)(2,1)S(1)} %copy-done.10), channel_id=1, source_target_pairs={{0,8},{1,9},{2,10},{3,11},{4,12},{5,13},{6,14},{7,15},{8,0},{9,1},... | collective-permute-start | bytes 442376 | tf_op jit(solution)/shard_map/ppermute | solution.py:648
  40.4 16.7 %collective-permute-start.4 = (bf16[576,128]{1,0:T(8,128)(2,1)S(1)}, bf16[576,128]{1,0:T(8,128)(2,1)S(1)}, u32[]{:S(2)}, u32[]{:S(2)}) collective-permute-start(bf16[576,128]{1,0:T(8,128)(2,1)S(1)} %copy-done.8), channel_id=1, source_target_pairs={{0,16},{1,17},{2,18},{3,19},{4,20},{5,21},{6,22},{7,23},{8,24},{9,... | collective-permute-start | bytes 442376 | tf_op jit(solution)/shard_map/ppermute | solution.py:648
  41.9 18.2 %collective-permute-start.5 = (bf16[576,128]{1,0:T(8,128)(2,1)S(1)}, bf16[576,128]{1,0:T(8,128)(2,1)S(1)}, u32[]{:S(2)}, u32[]{:S(2)}) collective-permute-start(bf16[576,128]{1,0:T(8,128)(2,1)S(1)} %get-tuple-element.30), channel_id=1, source_target_pairs={{0,24},{1,25},{2,26},{3,27},{4,28},{5,29},{6,30},{7,31},{8,16},{9,... | collective-permute-start | bytes 442376 | tf_op jit(solution)/shard_map/ppermute | solution.py:648
  57.1 8.3 %copy-start.12 = (bf16[1,64,1024]{2,1,0:T(8,128)(2,1)S(1)}, bf16[1,64,1024]{2,1,0:T(8,128)(2,1)}, u32[]{:S(2)}) copy-start(bf16[1,64,1024]{2,1,0:T(8,128)(2,1)} %get-tuple-element.62) | copy-start | bytes 393220
  57.1 8.3 %copy-start.13 = (bf16[1,64,1024]{2,1,0:T(8,128)(2,1)S(1)}, bf16[1,64,1024]{2,1,0:T(8,128)(2,1)}, u32[]{:S(2)}) copy-start(bf16[1,64,1024]{2,1,0:T(8,128)(2,1)} %get-tuple-element.59) | copy-start | bytes 393220
  60.2 5.2 %copy-start.14 = (bf16[1,64,1024]{2,1,0:T(8,128)(2,1)S(1)}, bf16[1,64,1024]{2,1,0:T(8,128)(2,1)}, u32[]{:S(2)}) copy-start(bf16[1,64,1024]{2,1,0:T(8,128)(2,1)} %get-tuple-element.60) | copy-start | bytes 393220
  62.1 3.3 %copy-start.15 = (bf16[1,64,1024]{2,1,0:T(8,128)(2,1)S(1)}, bf16[1,64,1024]{2,1,0:T(8,128)(2,1)}, u32[]{:S(2)}) copy-start(bf16[1,64,1024]{2,1,0:T(8,128)(2,1)} %get-tuple-element.63) | copy-start | bytes 393220
  62.1 3.3 %copy-start.16 = (bf16[1,64,1024]{2,1,0:T(8,128)(2,1)S(1)}, bf16[1,64,1024]{2,1,0:T(8,128)(2,1)}, u32[]{:S(2)}) copy-start(bf16[1,64,1024]{2,1,0:T(8,128)(2,1)} %get-tuple-element.64) | copy-start | bytes 393220
  63.8 6.5 %collective-permute-start.7 = (bf16[768,128]{1,0:T(8,128)(2,1)S(1)}, bf16[768,128]{1,0:T(8,128)(2,1)S(1)}, u32[]{:S(2)}, u32[]{:S(2)}) collective-permute-start(bf16[768,128]{1,0:T(8,128)(2,1)S(1)} %get-tuple-element.36), channel_id=1, source_target_pairs={{0,16},{1,17},{2,18},{3,19},{4,20},{5,21},{6,22},{7,23},{8,24},{9,... | collective-permute-start | bytes 589832 | tf_op jit(solution)/shard_map/ppermute | solution.py:648
  70.3 20.3 %collective-permute-start.10 = (bf16[2,64,1024]{2,1,0:T(8,128)(2,1)S(1)}, bf16[2,64,1024]{2,1,0:T(8,128)(2,1)S(1)}, u32[]{:S(2)}, u32[]{:S(2)}) collective-permute-start(bf16[2,64,1024]{2,1,0:T(8,128)(2,1)S(1)} %get-tuple-element.40), channel_id=1, source_target_pairs={{0,4},{1,5},{2,6},{3,7},{4,0},{5,1},{6,2},{7,3},{8,12},{9,13},{10,... | collective-permute-start | bytes 786440 | tf_op jit(solution)/shard_map/ppermute | solution.py:648
  72.0 18.6 %collective-permute-start.9 = (bf16[2,64,1024]{2,1,0:T(8,128)(2,1)S(1)}, bf16[2,64,1024]{2,1,0:T(8,128)(2,1)S(1)}, u32[]{:S(2)}, u32[]{:S(2)}) collective-permute-start(bf16[2,64,1024]{2,1,0:T(8,128)(2,1)S(1)} %get-tuple-element.39), channel_id=1, source_target_pairs={{0,2},{1,3},{2,0},{3,1},{4,6},{5,7},{6,4},{7,5},{8,10},{9,11},{10,... | collective-permute-start | bytes 786440 | tf_op jit(solution)/shard_map/ppermute | solution.py:648
  73.5 18.7 %collective-permute-start.11 = (bf16[2,64,1024]{2,1,0:T(8,128)(2,1)S(1)}, bf16[2,64,1024]{2,1,0:T(8,128)(2,1)S(1)}, u32[]{:S(2)}, u32[]{:S(2)}) collective-permute-start(bf16[2,64,1024]{2,1,0:T(8,128)(2,1)S(1)} %pad_maximum_fusion.7), channel_id=1, source_target_pairs={{0,6},{1,7},{2,4},{3,5},{4,2},{5,3},{6,0},{7,1},{8,14},{9,15},{10,... | collective-permute-start | bytes 786440 | tf_op jit(solution)/shard_map/ppermute | solution.py:648
  73.8 14.7 %collective-permute-start.6 = (bf16[768,128]{1,0:T(8,128)(2,1)S(1)}, bf16[768,128]{1,0:T(8,128)(2,1)S(1)}, u32[]{:S(2)}, u32[]{:S(2)}) collective-permute-start(bf16[768,128]{1,0:T(8,128)(2,1)S(1)} %get-tuple-element.35), channel_id=1, source_target_pairs={{0,8},{1,9},{2,10},{3,11},{4,12},{5,13},{6,14},{7,15},{8,0},{9,1},... | collective-permute-start | bytes 589832 | tf_op jit(solution)/shard_map/ppermute | solution.py:648
  76.6 14.0 %collective-permute-start.8 = (bf16[768,128]{1,0:T(8,128)(2,1)S(1)}, bf16[768,128]{1,0:T(8,128)(2,1)S(1)}, u32[]{:S(2)}, u32[]{:S(2)}) collective-permute-start(bf16[768,128]{1,0:T(8,128)(2,1)S(1)} %get-tuple-element.37), channel_id=1, source_target_pairs={{0,24},{1,25},{2,26},{3,27},{4,28},{5,29},{6,30},{7,31},{8,16},{9,... | collective-permute-start | bytes 589832 | tf_op jit(solution)/shard_map/ppermute | solution.py:648
  93.6 5.0 %collective-permute-start.19 = (bf16[2,64,192]{2,1,0:T(8,128)(2,1)S(1)}, bf16[2,64,192]{2,1,0:T(8,128)(2,1)S(1)}, u32[]{:S(2)}, u32[]{:S(2)}) collective-permute-start(bf16[2,64,192]{2,1,0:T(8,128)(2,1)S(1)} %get-tuple-element.43), channel_id=1, source_target_pairs={{0,2},{1,3},{2,0},{3,1},{4,6},{5,7},{6,4},{7,5},{8,10},{9,11},{10,... | collective-permute-start | bytes 147464 | tf_op jit(solution)/shard_map/ppermute | solution.py:648
  94.2 4.9 %collective-permute-start.20 = (bf16[2,64,192]{2,1,0:T(8,128)(2,1)S(1)}, bf16[2,64,192]{2,1,0:T(8,128)(2,1)S(1)}, u32[]{:S(2)}, u32[]{:S(2)}) collective-permute-start(bf16[2,64,192]{2,1,0:T(8,128)(2,1)S(1)} %get-tuple-element.44), channel_id=1, source_target_pairs={{0,4},{1,5},{2,6},{3,7},{4,0},{5,1},{6,2},{7,3},{8,12},{9,13},{10,... | collective-permute-start | bytes 147464 | tf_op jit(solution)/shard_map/ppermute | solution.py:648
  96.8 5.2 %collective-permute-start.21 = (bf16[2,64,192]{2,1,0:T(8,128)(2,1)S(1)}, bf16[2,64,192]{2,1,0:T(8,128)(2,1)S(1)}, u32[]{:S(2)}, u32[]{:S(2)}) collective-permute-start(bf16[2,64,192]{2,1,0:T(8,128)(2,1)S(1)} %get-tuple-element.45), channel_id=1, source_target_pairs={{0,6},{1,7},{2,4},{3,5},{4,2},{5,3},{6,0},{7,1},{8,14},{9,15},{10,... | collective-permute-start | bytes 147464 | tf_op jit(solution)/shard_map/ppermute | solution.py:648
  102.0 1.3 collective-permute-start.22
  102.1 13.1 %collective-permute-start.31 = (bf16[2,576,128]{2,1,0:T(8,128)(2,1)S(1)}, bf16[2,576,128]{2,1,0:T(8,128)(2,1)S(1)}, u32[]{:S(2)}, u32[]{:S(2)}) collective-permute-start(bf16[2,576,128]{2,1,0:T(8,128)(2,1)S(1)} %pad_maximum_fusion.2.refs_0_), channel_id=1, source_target_pairs={{0,4},{1,5},{2,6},{3,7},{4,0},{5,1},{6,2},{7,3},{8,12},{9,13},{10,... | collective-permute-start | bytes 884744 | tf_op jit(solution)/shard_map/ppermute | solution.py:648
  103.3 36.4 %copy-start.17 = (bf16[64,192]{1,0:T(8,128)(2,1)}, bf16[64,192]{1,0:T(8,128)(2,1)S(1)}, u32[]{:S(2)}) copy-start(bf16[64,192]{1,0:T(8,128)(2,1)S(1)} %fusion.2.own_rank) | copy-start | bytes 73732
  103.4 6.3 %collective-permute-start.23 = (bf16[64,128]{1,0:T(8,128)(2,1)S(1)}, bf16[64,128]{1,0:T(8,128)(2,1)S(1)}, u32[]{:S(2)}, u32[]{:S(2)}) collective-permute-start(bf16[64,128]{1,0:T(8,128)(2,1)S(1)} %get-tuple-element.71), channel_id=1, source_target_pairs={{0,8},{1,9},{2,10},{3,11},{4,12},{5,13},{6,14},{7,15},{8,0},{9,1},... | collective-permute-start | bytes 49160 | tf_op jit(solution)/shard_map/ppermute | solution.py:648
  109.7 7.5 %collective-permute-start.25 = (bf16[2,64,128]{2,1,0:T(8,128)(2,1)S(1)}, bf16[2,64,128]{2,1,0:T(8,128)(2,1)S(1)}, u32[]{:S(2)}, u32[]{:S(2)}) collective-permute-start(bf16[2,64,128]{2,1,0:T(8,128)(2,1)S(1)} %get-tuple-element.69), channel_id=1, source_target_pairs={{0,4},{1,5},{2,6},{3,7},{4,0},{5,1},{6,2},{7,3},{8,12},{9,13},{10,... | collective-permute-start | bytes 98312 | tf_op jit(solution)/shard_map/ppermute | solution.py:648
  112.7 5.5 %collective-permute-start.24 = (bf16[2,64,128]{2,1,0:T(8,128)(2,1)S(1)}, bf16[2,64,128]{2,1,0:T(8,128)(2,1)S(1)}, u32[]{:S(2)}, u32[]{:S(2)}) collective-permute-start(bf16[2,64,128]{2,1,0:T(8,128)(2,1)S(1)} %get-tuple-element.69), channel_id=1, source_target_pairs={{0,2},{1,3},{2,0},{3,1},{4,6},{5,7},{6,4},{7,5},{8,10},{9,11},{10,... | collective-permute-start | bytes 98312 | tf_op jit(solution)/shard_map/ppermute | solution.py:648
  113.7 5.5 %collective-permute-start.26 = (bf16[2,64,128]{2,1,0:T(8,128)(2,1)S(1)}, bf16[2,64,128]{2,1,0:T(8,128)(2,1)S(1)}, u32[]{:S(2)}, u32[]{:S(2)}) collective-permute-start(bf16[2,64,128]{2,1,0:T(8,128)(2,1)S(1)} %get-tuple-element.69), channel_id=1, source_target_pairs={{0,6},{1,7},{2,4},{3,5},{4,2},{5,3},{6,0},{7,1},{8,14},{9,15},{10,... | collective-permute-start | bytes 98312 | tf_op jit(solution)/shard_map/ppermute | solution.py:648
  114.2 10.3 %collective-permute-start.29 = (bf16[2,576,128]{2,1,0:T(8,128)(2,1)S(1)}, bf16[2,576,128]{2,1,0:T(8,128)(2,1)S(1)}, u32[]{:S(2)}, u32[]{:S(2)}) collective-permute-start(bf16[2,576,128]{2,1,0:T(8,128)(2,1)S(1)} %pad_maximum_fusion.2.refs_0_), channel_id=1, source_target_pairs={{0,2},{1,3},{2,0},{3,1},{4,6},{5,7},{6,4},{7,5},{8,10},{9,11},{10,... | collective-permute-start | bytes 884744 | tf_op jit(solution)/shard_map/ppermute | solution.py:648
  115.2 20.2 %collective-permute-start.15 = (bf16[2,64,1024]{2,1,0:T(8,128)(2,1)S(1)}, bf16[2,64,1024]{2,1,0:T(8,128)(2,1)S(1)}, u32[]{:S(2)}, u32[]{:S(2)}) collective-permute-start(bf16[2,64,1024]{2,1,0:T(8,128)(2,1)S(1)} %pad_maximum_fusion.3.refs_0_), channel_id=1, source_target_pairs={{0,4},{1,5},{2,6},{3,7},{4,0},{5,1},{6,2},{7,3},{8,12},{9,13},{10,... | collective-permute-start | bytes 786440 | tf_op jit(solution)/shard_map/ppermute | solution.py:648
  117.2 19.3 %collective-permute-start.13 = (bf16[2,64,1024]{2,1,0:T(8,128)(2,1)S(1)}, bf16[2,64,1024]{2,1,0:T(8,128)(2,1)S(1)}, u32[]{:S(2)}, u32[]{:S(2)}) collective-permute-start(bf16[2,64,1024]{2,1,0:T(8,128)(2,1)S(1)} %pad_maximum_fusion.3.refs_0_), channel_id=1, source_target_pairs={{0,2},{1,3},{2,0},{3,1},{4,6},{5,7},{6,4},{7,5},{8,10},{9,11},{10,... | collective-permute-start | bytes 786440 | tf_op jit(solution)/shard_map/ppermute | solution.py:648
  118.2 16.7 %collective-permute-start.33 = (bf16[2,576,128]{2,1,0:T(8,128)(2,1)S(1)}, bf16[2,576,128]{2,1,0:T(8,128)(2,1)S(1)}, u32[]{:S(2)}, u32[]{:S(2)}) collective-permute-start(bf16[2,576,128]{2,1,0:T(8,128)(2,1)S(1)} %collective-permute-done.31.refs_4_), channel_id=1, source_target_pairs={{0,2},{1,3},{2,0},{3,1},{4,6},{5,7},{6,4},{7,5},{8,10},{9,11},{10,... | collective-permute-start | bytes 884744 | tf_op jit(solution)/shard_map/ppermute | solution.py:648
  119.2 15.7 %collective-permute-start.27 = (bf16[4,2,64,128]{3,2,1,0:T(8,128)(2,1)S(1)}, bf16[4,2,64,128]{3,2,1,0:T(8,128)(2,1)S(1)}, u32[]{:S(2)}, u32[]{:S(2)}) collective-permute-start(bf16[4,2,64,128]{3,2,1,0:T(8,128)(2,1)S(1)} %get-tuple-element.67), channel_id=1, source_target_pairs={{0,1},{1,0},{2,3},{3,2},{4,5},{5,4},{6,7},{7,6},{8,9},{9,8},{10,11... | collective-permute-start | bytes 393224 | tf_op jit(solution)/shard_map/ppermute | solution.py:648
  124.5 19.3 %collective-permute-start.28 = (bf16[2,576,128]{2,1,0:T(8,128)(2,1)S(1)}, bf16[2,576,128]{2,1,0:T(8,128)(2,1)S(1)}, u32[]{:S(2)}, u32[]{:S(2)}) collective-permute-start(bf16[2,576,128]{2,1,0:T(8,128)(2,1)S(1)} %pad_maximum_fusion.2.refs_0_), channel_id=1, source_target_pairs={{0,1},{1,0},{2,3},{3,2},{4,5},{5,4},{6,7},{7,6},{8,9},{9,8},{10,11... | collective-permute-start | bytes 884744 | tf_op jit(solution)/shard_map/ppermute | solution.py:648
  134.9 9.4 %collective-permute-start.30 = (bf16[2,576,128]{2,1,0:T(8,128)(2,1)S(1)}, bf16[2,576,128]{2,1,0:T(8,128)(2,1)S(1)}, u32[]{:S(2)}, u32[]{:S(2)}) collective-permute-start(bf16[2,576,128]{2,1,0:T(8,128)(2,1)S(1)} %collective-permute-done.29.refs_2_), channel_id=1, source_target_pairs={{0,1},{1,0},{2,3},{3,2},{4,5},{5,4},{6,7},{7,6},{8,9},{9,8},{10,11... | collective-permute-start | bytes 884744 | tf_op jit(solution)/shard_map/ppermute | solution.py:648
  134.9 9.5 %collective-permute-start.32 = (bf16[2,576,128]{2,1,0:T(8,128)(2,1)S(1)}, bf16[2,576,128]{2,1,0:T(8,128)(2,1)S(1)}, u32[]{:S(2)}, u32[]{:S(2)}) collective-permute-start(bf16[2,576,128]{2,1,0:T(8,128)(2,1)S(1)} %collective-permute-done.31.refs_4_), channel_id=1, source_target_pairs={{0,1},{1,0},{2,3},{3,2},{4,5},{5,4},{6,7},{7,6},{8,9},{9,8},{10,11... | collective-permute-start | bytes 884744 | tf_op jit(solution)/shard_map/ppermute | solution.py:648
  135.5 8.4 %collective-permute-start.17 = (bf16[2,64,1024]{2,1,0:T(8,128)(2,1)S(1)}, bf16[2,64,1024]{2,1,0:T(8,128)(2,1)}, u32[]{:S(2)}, u32[]{:S(2)}) collective-permute-start(bf16[2,64,1024]{2,1,0:T(8,128)(2,1)S(1)} %collective-permute-done.15.refs_4_), channel_id=1, source_target_pairs={{0,2},{1,3},{2,0},{3,1},{4,6},{5,7},{6,4},{7,5},{8,10},{9,11},{10,... | collective-permute-start | bytes 786440 | tf_op jit(solution)/shard_map/ppermute | solution.py:648
  136.5 8.4 %collective-permute-start.34 = (bf16[2,576,128]{2,1,0:T(8,128)(2,1)S(1)}, bf16[2,576,128]{2,1,0:T(8,128)(2,1)S(1)}, u32[]{:S(2)}, u32[]{:S(2)}) collective-permute-start(bf16[2,576,128]{2,1,0:T(8,128)(2,1)S(1)} %collective-permute-done.33.refs_6_), channel_id=1, source_target_pairs={{0,1},{1,0},{2,3},{3,2},{4,5},{5,4},{6,7},{7,6},{8,9},{9,8},{10,11... | collective-permute-start | bytes 884744 | tf_op jit(solution)/shard_map/ppermute | solution.py:648
  143.8 13.0 %collective-permute-start.12 = (bf16[2,64,1024]{2,1,0:T(8,128)(2,1)S(1)}, bf16[2,64,1024]{2,1,0:T(8,128)(2,1)}, u32[]{:S(2)}, u32[]{:S(2)}) collective-permute-start(bf16[2,64,1024]{2,1,0:T(8,128)(2,1)S(1)} %pad_maximum_fusion.3.refs_0_), channel_id=1, source_target_pairs={{0,1},{1,0},{2,3},{3,2},{4,5},{5,4},{6,7},{7,6},{8,9},{9,8},{10,11... | collective-permute-start | bytes 786440 | tf_op jit(solution)/shard_map/ppermute | solution.py:648
  143.8 13.0 %collective-permute-start.16 = (bf16[2,64,1024]{2,1,0:T(8,128)(2,1)S(1)}, bf16[2,64,1024]{2,1,0:T(8,128)(2,1)}, u32[]{:S(2)}, u32[]{:S(2)}) collective-permute-start(bf16[2,64,1024]{2,1,0:T(8,128)(2,1)S(1)} %collective-permute-done.15.refs_4_), channel_id=1, source_target_pairs={{0,1},{1,0},{2,3},{3,2},{4,5},{5,4},{6,7},{7,6},{8,9},{9,8},{10,11... | collective-permute-start | bytes 786440 | tf_op jit(solution)/shard_map/ppermute | solution.py:648
  144.4 12.5 %collective-permute-start.14 = (bf16[2,64,1024]{2,1,0:T(8,128)(2,1)S(1)}, bf16[2,64,1024]{2,1,0:T(8,128)(2,1)}, u32[]{:S(2)}, u32[]{:S(2)}) collective-permute-start(bf16[2,64,1024]{2,1,0:T(8,128)(2,1)S(1)} %collective-permute-done.13.refs_2_), channel_id=1, source_target_pairs={{0,1},{1,0},{2,3},{3,2},{4,5},{5,4},{6,7},{7,6},{8,9},{9,8},{10,11... | collective-permute-start | bytes 786440 | tf_op jit(solution)/shard_map/ppermute | solution.py:648
  144.4 12.4 %collective-permute-start.18 = (bf16[2,64,1024]{2,1,0:T(8,128)(2,1)}, bf16[2,64,1024]{2,1,0:T(8,128)(2,1)}, u32[]{:S(2)}, u32[]{:S(2)}) collective-permute-start(bf16[2,64,1024]{2,1,0:T(8,128)(2,1)} %collective-permute-done.17.refs_6_), channel_id=1, source_target_pairs={{0,1},{1,0},{2,3},{3,2},{4,5},{5,4},{6,7},{7,6},{8,9},{9,8},{10,11... | collective-permute-start | bytes 786440 | tf_op jit(solution)/shard_map/ppermute | solution.py:648
  158.3 1.3 copy-start

commit v5 on v4

--- a/solution.py
+++ b/solution.py
@@ -264,8 +264,10 @@
 
 PIECES = 8
 GROUP = QH // KEYVALUE_HEADS
-DOWN = ((0, 12288),)
-REST = ((12288, 2048), (14336, 512), (14848, 2048), (16896, 4096))
+FIRST = ((0, 12288), (12288, 2048), (14336, 512))
+SECOND = ((14848, 2048), (16896, 4096))
+DOWN_ROWS, QUERY_ROWS, KEYVAL_ROWS, DOWN_OUT_ROWS, UP_OUT_ROWS = 768, 128, 32, 128, 256
+UP_ROWS = QUERY_ROWS + 2 * KEYVAL_ROWS
 
 
 def pack_kernel(sections, pool, *refs):
@@ -326,7 +328,8 @@
 
 
 def pick_kernel(mirrored, here, there, owner, spread, *refs):
-    outs, sems = refs[:4], refs[4]
+    sems = refs[-1]
+    outs = refs[:4] if len(refs) > 3 else [refs[flip % 2].at[flip // 2] for flip in range(4)]
     half = lax.axis_index("ctx") // PIECES
     rows = spread.shape[1]
     copies = []
@@ -355,12 +358,13 @@
 
 def pick(spread, here, there, owner, mirrored):
     rows = spread.shape[1] + (mirrored[1] if mirrored else 0)
-    slab = jax.ShapeDtypeStruct((rows, 128), jnp.bfloat16)
+    shape, count = ((rows, 128), 4) if mirrored else ((2, rows, 128), 2)
+    slab = jax.ShapeDtypeStruct(shape, jnp.bfloat16)
     return pl.pallas_call(
         partial(pick_kernel, mirrored),
-        out_shape=(slab,) * 4,
+        out_shape=(slab,) * count,
         in_specs=[pl.BlockSpec(memory_space=pltpu.SMEM)] * 3 + [pl.BlockSpec(memory_space=pl.ANY)],
-        out_specs=(pl.BlockSpec(memory_space=pltpu.VMEM),) * 4,
+        out_specs=(pl.BlockSpec(memory_space=pltpu.VMEM),) * count,
         scratch_shapes=[pltpu.SemaphoreType.DMA((4, 2))],
         compiler_params=pltpu.CompilerParams(vmem_limit_bytes=16 << 20),
         cost_estimate=pl.CostEstimate(flops=0, bytes_accessed=2 << 20, transcendentals=0),
@@ -400,248 +404,307 @@
     )(rows, *after)
 
 
-def narrow_kernel(here, owner, own, mirror, across, both, *refs):
-    dealt, outs, (flat, left, right) = refs[:4], refs[4:8], refs[8:]
+def nearest(here, owner, block):
+    half = lax.axis_index("ctx") // PIECES
+    return owner[here[block]] // PIECES == half
+
+
+def choose(close, arrived, put):
     plane = lax.axis_index("groups")
-    half = lax.axis_index("ctx") // PIECES
-    close = owner[here[half]] // PIECES == half
-    count = own.shape[0]
-
-    def place(block, position):
-        flat[pl.ds(pl.multiple_of(position * count, count), count), :] = block[...].astype(
-            jnp.float32
-        )
 
     @pl.when(close)
     def _():
-        place(own, plane)
-        place(across, 1 - plane)
+        put(arrived[0], plane)
+        put(arrived[2], 1 - plane)
 
     @pl.when(jnp.logical_not(close))
     def _():
-        place(mirror, plane)
-        place(both, 1 - plane)
+        put(arrived[1], plane)
+        put(arrived[3], 1 - plane)
+
+
+def join_kernel(here, owner, *refs):
+    arrived, (weight, ups), (flat, left, right) = refs[:4], refs[4:6], refs[6:]
+    half = lax.axis_index("ctx") // PIECES
+    split = DOWN_ROWS + QUERY_ROWS + KEYVAL_ROWS
+
+    def put_own(source, position):
+        first = pl.multiple_of(position * DOWN_ROWS, DOWN_ROWS)
+        flat[pl.ds(first, DOWN_ROWS), :] = source[:DOWN_ROWS, :].astype(jnp.float32)
+        ups[position, : UP_ROWS - KEYVAL_ROWS, :] = source[DOWN_ROWS:split, :]
+
+    def put_mirrored(source, position):
+        ups[position, UP_ROWS - KEYVAL_ROWS :, :] = source[split:, :]
+
+    choose(nearest(here, owner, half), arrived, put_own)
+    choose(nearest(here, owner, 1 - half), arrived, put_mirrored)
 
     third = flat.shape[0] // 3
     one = flat[pl.ds(0, third, stride=3), :]
-    two = flat[pl.ds(1, third, stride=3), :]
-    three = flat[pl.ds(2, third, stride=3), :]
+    two = pltpu.roll(flat[pl.ds(1, third, stride=3), :], 64, 1)
+    three = pltpu.roll(flat[pl.ds(2, third, stride=3), :], 64, 1)
     lane = lax.broadcasted_iota(jnp.int32, one.shape, 1)
-    two = pltpu.roll(two, 64, 1)
-    three = pltpu.roll(three, 64, 1)
     left[pl.ds(0, third, stride=2), :] = one
     left[pl.ds(1, third, stride=2), :] = jnp.where(lane < 64, two, three)
     right[pl.ds(0, third, stride=2), :] = pltpu.roll(two, 64, 1)
     right[pl.ds(1, third, stride=2), :] = three
-    weight = jnp.concatenate([left[...], right[...]], 1).astype(jnp.bfloat16)
-    for block, out in zip(dealt, outs):
+    weight[...] = jnp.concatenate([left[...], right[...]], 1).astype(jnp.bfloat16)
+
+
+def join(here, owner, arrived):
+    depth = D // PIECES
+    return pl.pallas_call(
+        join_kernel,
+        out_shape=(
+            jax.ShapeDtypeStruct((depth, 256), jnp.bfloat16),
+            jax.ShapeDtypeStruct((2, UP_ROWS, 128), jnp.bfloat16),
+        ),
+        in_specs=[pl.BlockSpec(memory_space=pltpu.SMEM)] * 2
+        + [pl.BlockSpec(memory_space=pltpu.VMEM)] * 4,
+        out_specs=(pl.BlockSpec(memory_space=pltpu.VMEM),) * 2,
+        scratch_shapes=[
+            pltpu.VMEM((2 * DOWN_ROWS, 128), jnp.float32),
+            pltpu.VMEM((depth, 128), jnp.float32),
+            pltpu.VMEM((depth, 128), jnp.float32),
+        ],
+        compiler_params=pltpu.CompilerParams(vmem_limit_bytes=16 << 20),
+        cost_estimate=pl.CostEstimate(flops=0, bytes_accessed=16 << 20, transcendentals=0),
+    )(here, owner, *arrived)
+
+
+def settle_kernel(here, there, owner, near, far, own, across):
+    half = lax.axis_index("ctx") // PIECES
+    for number, (wishes, out) in enumerate(((here, own), (there, across))):
+        close = nearest(wishes, owner, half)
+
+        @pl.when(close)
+        def _():
+            out[...] = near[number]
+
+        @pl.when(jnp.logical_not(close))
+        def _():
+            out[...] = far[number]
+
+
+def settle(here, there, owner, near, far):
+    slab = jax.ShapeDtypeStruct(near.shape[1:], jnp.bfloat16)
+    return pl.pallas_call(
+        settle_kernel,
+        out_shape=(slab, slab),
+        in_specs=[pl.BlockSpec(memory_space=pltpu.SMEM)] * 3
+        + [pl.BlockSpec(memory_space=pltpu.VMEM)] * 2,
+        out_specs=(pl.BlockSpec(memory_space=pltpu.VMEM),) * 2,
+        compiler_params=pltpu.CompilerParams(vmem_limit_bytes=16 << 20),
+        cost_estimate=pl.CostEstimate(flops=0, bytes_accessed=1 << 20, transcendentals=0),
+    )(here, there, owner, near, far)
+
+
+def narrow_kernel(weight, *refs):
+    for block, out in zip(refs[:4], refs[4:]):
         sides, rows, depth = block.shape
         product = jnp.dot(
-            block[...].reshape(sides * rows, depth), weight, preferred_element_type=jnp.float32
+            block[...].reshape(sides * rows, depth),
+            weight[...],
+            preferred_element_type=jnp.float32,
         )
         out[...] = product[:, : 3 * ADAPTER_RANK].reshape(out.shape).astype(jnp.bfloat16)
 
 
-def narrow(here, owner, arrived, dealt):
+def narrow(weight, dealt):
     sides, rows, depth = dealt[0].shape
     partial_sums = jax.ShapeDtypeStruct((sides, rows, 3 * ADAPTER_RANK), jnp.bfloat16)
     return pl.pallas_call(
         narrow_kernel,
         out_shape=(partial_sums,) * 4,
-        in_specs=[pl.BlockSpec(memory_space=pltpu.SMEM)] * 2
-        + [pl.BlockSpec(memory_space=pltpu.VMEM)] * 8,
+        in_specs=[pl.BlockSpec(memory_space=pltpu.VMEM)] * 5,
         out_specs=(pl.BlockSpec(memory_space=pltpu.VMEM),) * 4,
-        scratch_shapes=[
-            pltpu.VMEM((depth * 3 * ADAPTER_RANK // 128, 128), jnp.float32),
-            pltpu.VMEM((depth, 128), jnp.float32),
-            pltpu.VMEM((depth, 128), jnp.float32),
-        ],
         compiler_params=pltpu.CompilerParams(vmem_limit_bytes=16 << 20),
         cost_estimate=pl.CostEstimate(
-            flops=2 * 8 * rows * depth * 256, bytes_accessed=3 << 20, transcendentals=0
+            flops=2 * 8 * rows * depth * 256, bytes_accessed=2 << 20, transcendentals=0
         ),
-    )(here, owner, *arrived, *dealt)
-
-
-def assemble_kernel(*refs):
-    pieces, out, sems = refs[:PIECES], refs[PIECES], refs[PIECES + 1]
-    seat = lax.rem(lax.axis_index("ctx"), PIECES)
-    copies = [
-        pltpu.make_async_copy(piece, out.at[seat ^ apart], sems.at[apart])
-        for apart, piece in enumerate(pieces)
-    ]
-    for copy in copies:
-        copy.start()
-    for copy in copies:
-        copy.wait()
-
-
-def assemble(pieces):
-    return pl.pallas_call(
-        assemble_kernel,
-        out_shape=jax.ShapeDtypeStruct((PIECES,) + pieces[0].shape, jnp.bfloat16),
-        in_specs=[pl.BlockSpec(memory_space=pltpu.VMEM)] * PIECES,
-        out_specs=pl.BlockSpec(memory_space=pltpu.VMEM),
-        scratch_shapes=[pltpu.SemaphoreType.DMA((PIECES,))],
-        compiler_params=pltpu.CompilerParams(vmem_limit_bytes=16 << 20),
-        cost_estimate=pl.CostEstimate(flops=0, bytes_accessed=6 << 20, transcendentals=0),
-    )(*pieces)
+    )(weight, *dealt)
 
 
 def attend_kernel(
     query_block,
-    key_base,
-    value_base,
+    key_same,
+    key_other,
+    value_same,
+    value_other,
     own_rank,
     all_rank,
-    query_up,
-    key_up,
-    value_up,
+    up_same,
+    up_other,
     cosines,
     sines,
-    down_out,
-    up_out,
     attended,
-    out_delta,
-    total,
+    flat_query,
+    flat_keyval,
     keys,
     values,
 ):
     step = pl.program_id(0)
     rows = query_block.shape[0]
     base = lax.axis_index("ctx") * rows
+    half = lax.axis_index("ctx") // PIECES
+    seat = lax.rem(lax.axis_index("ctx"), PIECES)
     dot = partial(jnp.dot, preferred_element_type=jnp.float32)
+
+    @pl.when(step == 0)
+    def _():
+        for apart in range(PIECES):
+            ups = up_other if apart % 2 else up_same
+            for position in range(2):
+                piece = ups[apart // 2, position].astype(jnp.float32)
+                place = (seat ^ apart) * 2 + position
+                first = pl.multiple_of(place * QUERY_ROWS, QUERY_ROWS)
+                flat_query[pl.ds(first, QUERY_ROWS), :] = piece[:QUERY_ROWS]
+                first = pl.multiple_of(place * KEYVAL_ROWS, KEYVAL_ROWS)
+                for side in range(2):
+                    begin = QUERY_ROWS + side * KEYVAL_ROWS
+                    flat_keyval[side, pl.ds(first, KEYVAL_ROWS), :] = piece[
+                        begin : begin + KEYVAL_ROWS
+                    ]
 
     def turned(delta, cosine, sine):
         return delta * cosine + pltpu.roll(delta, HEAD_SIZE // 2, 1) * sine
 
-    half = lax.axis_index("ctx") * rows // BLOCK_TOKENS
-    seat = lax.rem(lax.axis_index("ctx"), PIECES)
-    for side in range(key_up.shape[0]):
-        for apart in range(PIECES):
-            there = seat ^ apart
-            first = ((half ^ side) * PIECES + there) * rows
-            span = pl.ds(pl.multiple_of(first, rows), rows)
-            rank = all_rank[apart % 2, apart // 2, side]
-            delta = adapter_scale * dot(rank[:, :ADAPTER_RANK], key_up[side])
-            delta = turned(delta, cosines[span, :], sines[span, :])
-            full = key_base[there, side].astype(jnp.float32) + delta
-            keys[span, :] = full.astype(jnp.bfloat16)
-            delta = adapter_scale * dot(rank[:, ADAPTER_RANK:], value_up[side])
-            full = value_base[there, side].astype(jnp.float32) + delta
-            values[span, :] = full.astype(jnp.bfloat16)
+    def up(flat, first, stride):
+        return flat[pl.ds(first, ADAPTER_RANK, stride=stride), :].astype(jnp.bfloat16)
+
+    for side in range(2):
+        heads = 2 * KEYVALUE_HEADS
+        key_up = up(flat_keyval.at[side], step, heads)
+        value_up = up(flat_keyval.at[side], step + KEYVALUE_HEADS, heads)
+        for core in range(2):
+            rank = all_rank[core, :, side].reshape(PIECES // 2 * rows, 2 * ADAPTER_RANK)
+            key_delta = adapter_scale * dot(rank[:, :ADAPTER_RANK], key_up)
+            value_delta = adapter_scale * dot(rank[:, ADAPTER_RANK:], value_up)
+            for chip in range(PIECES // 2):
+                there = seat ^ (2 * chip + core)
+                first = ((half ^ side) * PIECES + there) * rows
+                span = pl.ds(pl.multiple_of(first, rows), rows)
+                part = slice(chip * rows, (chip + 1) * rows)
+                delta = turned(key_delta[part], cosines[span, :], sines[span, :])
+                full = (key_other if core else key_same)[chip, side].astype(jnp.float32) + delta
+                keys[span, :] = full.astype(jnp.bfloat16)
+                full = (value_other if core else value_same)[chip, side].astype(jnp.float32)
+                values[span, :] = (full + value_delta[part]).astype(jnp.bfloat16)
     here = pl.ds(pl.multiple_of(base, rows), rows)
     cosine = cosines[here, :]
     sine = sines[here, :]
-    delta = adapter_scale * dot(own_rank[:, :ADAPTER_RANK], query_up[...])
-    added = jnp.zeros((rows, ADAPTER_RANK), jnp.float32)
     taken = GROUP // 2
     for first in range(0, GROUP, taken):
+        weight = [up(flat_query, step * GROUP + first + head, QH) for head in range(taken)]
+        deltas = adapter_scale * dot(own_rank[:, :ADAPTER_RANK], jnp.concatenate(weight, 1))
         queries = []
-        for head in range(first, first + taken):
-            span = slice(head * HEAD_SIZE, (head + 1) * HEAD_SIZE)
-            moved = turned(delta[:, span], cosine, sine)
+        for place in range(taken):
+            moved = turned(deltas[:, place * HEAD_SIZE : (place + 1) * HEAD_SIZE], cosine, sine)
+            span = slice((first + place) * HEAD_SIZE, (first + place + 1) * HEAD_SIZE)
             queries.append(
                 (query_block[:, span].astype(jnp.float32) + moved).astype(jnp.bfloat16)
             )
         queries = jnp.concatenate(queries, 0)
         scores = lax.dot_general(
             queries, keys[...], (((1,), (1,)), ((), ())), preferred_element_type=jnp.float32
-        ) * HEAD_SIZE ** (-0.5)
+        )
         row = lax.broadcasted_iota(jnp.int32, scores.shape, 0)
         column = lax.broadcasted_iota(jnp.int32, scores.shape, 1)
         scores = jnp.where(column <= base + lax.rem(row, rows), scores, mask_floor)
-        weights = jnp.exp(scores - jnp.max(scores, axis=-1, keepdims=True))
+        scores = scores - jnp.max(scores, axis=-1, keepdims=True)
+        weights = jnp.exp2(scores * (HEAD_SIZE ** (-0.5) * math.log2(math.e)))
         divisor = jnp.sum(weights, axis=-1, keepdims=True)
         result = (dot(weights.astype(jnp.bfloat16), values[...]) / divisor).astype(jnp.bfloat16)
-        for place, head in enumerate(range(first, first + taken)):
-            span = slice(head * HEAD_SIZE, (head + 1) * HEAD_SIZE)
-            part = result[place * rows : (place + 1) * rows]
-            attended[:, span] = part
-            added += dot(part, down_out[span, :])
-
-    @pl.when(step == 0)
-    def _():
-        total[...] = jnp.zeros_like(total)
-
-    total[...] += added
-
-    @pl.when(step == pl.num_programs(0) - 1)
-    def _():
-        narrow = total[...].astype(jnp.bfloat16)
-        out_delta[...] = (adapter_scale * dot(narrow, up_out[...])).astype(jnp.bfloat16)
-
-
-def attend(
-    query_base,
-    base,
-    own_rank,
-    all_rank,
-    query_up,
-    keyval_up,
-    cosines,
-    sines,
-    down_out,
-    up_out,
-):
+        for place in range(taken):
+            span = slice((first + place) * HEAD_SIZE, (first + place + 1) * HEAD_SIZE)
+            attended[:, span] = result[place * rows : (place + 1) * rows]
+
+
+def attend(query_base, base, own_rank, all_rank, ups, cosines, sines):
     rows = query_base.shape[0]
-    seq = base.shape[0] * base.shape[1] * rows
-    blocks = keyval_up.shape[0]
+    seq = 4 * PIECES // 2 * rows
     width = GROUP * HEAD_SIZE
 
     def whole(shape):
         return pl.BlockSpec(shape, lambda h: (0,) * len(shape))
 
+    key_spec = pl.BlockSpec((PIECES // 2, 2, rows, HEAD_SIZE), lambda h: (0, 0, 0, h))
+    value_spec = pl.BlockSpec(
+        (PIECES // 2, 2, rows, HEAD_SIZE), lambda h: (0, 0, 0, h + KEYVALUE_HEADS)
+    )
     return pl.pallas_call(
         attend_kernel,
         grid=(KEYVALUE_HEADS,),
-        out_shape=(
-            jax.ShapeDtypeStruct((rows, QH * HEAD_SIZE), jnp.bfloat16),
-            jax.ShapeDtypeStruct((rows, D), jnp.bfloat16),
-        ),
+        out_shape=jax.ShapeDtypeStruct((rows, QH * HEAD_SIZE), jnp.bfloat16),
         in_specs=[
             pl.BlockSpec((rows, width), lambda h: (0, h)),
-            pl.BlockSpec((PIECES, 2, rows, HEAD_SIZE), lambda h: (0, 0, 0, h)),
-            pl.BlockSpec((PIECES, 2, rows, HEAD_SIZE), lambda h: (0, 0, 0, h + KEYVALUE_HEADS)),
+            key_spec,
+            key_spec,
+            value_spec,
+            value_spec,
             whole(own_rank.shape),
             whole(all_rank.shape),
-            pl.BlockSpec((ADAPTER_RANK, width), lambda h: (0, h)),
-            pl.BlockSpec((blocks, ADAPTER_RANK, HEAD_SIZE), lambda h: (0, 0, h)),
-            pl.BlockSpec((blocks, ADAPTER_RANK, HEAD_SIZE), lambda h: (0, 0, h + KEYVALUE_HEADS)),
+            whole(ups[0].shape),
+            whole(ups[1].shape),
             whole(cosines.shape),
             whole(sines.shape),
-            pl.BlockSpec((width, ADAPTER_RANK), lambda h: (h, 0)),
-            whole(up_out.shape),
         ],
-        out_specs=(
-            pl.BlockSpec((rows, width), lambda h: (0, h)),
-            whole((rows, D)),
-        ),
+        out_specs=pl.BlockSpec((rows, width), lambda h: (0, h)),
         scratch_shapes=[
-            pltpu.VMEM((rows, ADAPTER_RANK), jnp.float32),
+            pltpu.VMEM((2 * PIECES * QUERY_ROWS, 128), jnp.float32),
+            pltpu.VMEM((2, 2 * PIECES * KEYVAL_ROWS, 128), jnp.float32),
             pltpu.VMEM((seq, HEAD_SIZE), jnp.bfloat16),
             pltpu.VMEM((seq, HEAD_SIZE), jnp.bfloat16),
         ],
         compiler_params=pltpu.CompilerParams(vmem_limit_bytes=60 << 20),
         cost_estimate=pl.CostEstimate(
-            flops=4 * rows * QH * seq * HEAD_SIZE,
+            flops=48 * rows * QH * seq * HEAD_SIZE,
             bytes_accessed=10 << 20,
             transcendentals=rows * QH * seq,
         ),
-    )(
-        query_base,
-        base,
-        base,
-        own_rank,
-        all_rank,
-        query_up,
-        keyval_up,
-        keyval_up,
-        cosines,
-        sines,
-        down_out,
-        up_out,
-    )
+    )(query_base, base[0], base[1], base[0], base[1], own_rank, all_rank, *ups, cosines, sines)
+
+
+def widen_kernel(attended, same, other, out_delta, down_out, up_out):
+    plane = lax.axis_index("groups")
+    seat = lax.rem(lax.axis_index("ctx"), PIECES)
+    for apart in range(PIECES):
+        pieces = other if apart % 2 else same
+        for position in range(2):
+            piece = pieces[apart // 2, position].astype(jnp.float32)
+            place = (seat ^ apart) * 2 + (position ^ plane)
+            first = place * 2 * DOWN_OUT_ROWS
+            block = piece[:DOWN_OUT_ROWS]
+            down_out[pl.ds(first, DOWN_OUT_ROWS, stride=2), :] = block
+            down_out[pl.ds(first + 1, DOWN_OUT_ROWS, stride=2), :] = pltpu.roll(block, 64, 1)
+            first = pl.multiple_of(place * UP_OUT_ROWS, UP_OUT_ROWS)
+            up_out[pl.ds(first, UP_OUT_ROWS), :] = piece[DOWN_OUT_ROWS:]
+    dot = partial(jnp.dot, preferred_element_type=jnp.float32)
+    rank = dot(attended[...], down_out[...].astype(jnp.bfloat16))[:, :ADAPTER_RANK]
+    rank = rank.astype(jnp.bfloat16)
+    blocks = D // 128
+    for first in range(0, blocks, 4):
+        weight = [
+            up_out[pl.ds(first + block, ADAPTER_RANK, stride=blocks), :].astype(jnp.bfloat16)
+            for block in range(4)
+        ]
+        delta = adapter_scale * dot(rank, jnp.concatenate(weight, 1))
+        out_delta[:, first * 128 : (first + 4) * 128] = delta.astype(jnp.bfloat16)
+
+
+def widen(attended, pieces):
+    return pl.pallas_call(
+        widen_kernel,
+        out_shape=jax.ShapeDtypeStruct((attended.shape[0], D), jnp.bfloat16),
+        in_specs=[pl.BlockSpec(memory_space=pltpu.VMEM)] * 3,
+        out_specs=pl.BlockSpec(memory_space=pltpu.VMEM),
+        scratch_shapes=[
+            pltpu.VMEM((QH * HEAD_SIZE, 128), jnp.float32),
+            pltpu.VMEM((ADAPTER_RANK * D // 128, 128), jnp.float32),
+        ],
+        compiler_params=pltpu.CompilerParams(vmem_limit_bytes=32 << 20),
+        cost_estimate=pl.CostEstimate(flops=1 << 27, bytes_accessed=4 << 20, transcendentals=0),
+    )(attended, *pieces)
 
 
 def swap(block, mask):
@@ -651,9 +714,6 @@
 def direct_shards(
     normed_input, query_base, key_base, value_base, adapter_pool, stretch_adapter, adapter_owner
 ):
-    plane = lax.axis_index("groups")
-    index = lax.axis_index("ctx")
-    half = index // PIECES
     tok_rows = normed_input.shape[0]
     ctx = lax.axis_size("ctx")
     seq = ctx * tok_rows
@@ -661,72 +721,62 @@
     def after(block, *others):
         return lax.optimization_barrier((block, others))[0]
 
+    def exchange(sent):
+        return [swap(block, flip * PIECES) if flip else block for flip, block in enumerate(sent)]
+
+    def along_z(block):
+        return jnp.stack([block, swap(block, 4)])
+
+    def along_x(pair):
+        quad = jnp.stack([pair, swap(pair, 2)], 1)
+        return quad.reshape((PIECES // 2,) + pair.shape[1:])
+
     elsewhere = swap(stretch_adapter, 2 * PIECES)
-    packed_rest = pack_row(adapter_pool, REST)
-    packed_down = pack_row(adapter_pool, DOWN, packed_rest)
-    even, odd = deal(normed_input, packed_rest)
+    packed = pack_row(adapter_pool, FIRST)
+    packed_second = pack_row(adapter_pool, SECOND, packed)
+    even, odd = deal(normed_input, packed)
     sibling = swap(odd, 1)
     base = jnp.concatenate([key_base, value_base], 1)
     base = jnp.stack([base, swap(base, PIECES)])
-    slots = jnp.sum(
-        jnp.where(
-            stretch_adapter[:, None] == jnp.arange(adapter_owner.shape[0], dtype=jnp.int32)[None, :],
-            adapter_owner[None, :],
-            0,
-        ),
-        axis=1,
-    )
-    near = (slots // PIECES) == half
-    close = jnp.where(half == 0, near[0], near[1])
-    far_close = jnp.where(half == 0, near[1], near[0])
-
-    def exchange(sent):
-        return [swap(block, flip * PIECES) if flip else block for flip, block in enumerate(sent)]
-
-    def gather(block):
-        four = swap(block, 4)
-        return [block, swap(block, 2), four, swap(four, 2)]
-
-    def complete(parts, *others):
-        parts = [after(part, *others) for part in parts]
-        return assemble([piece for part in parts for piece in (part, swap(part, 1))])
-
-    spread_rest = lax.all_to_all(packed_rest, "ctx", 0, 0, axis_index_groups=blocks)
-    sent_rest = pick(spread_rest, stretch_adapter, elsewhere, adapter_owner, (128, 32))
-    packed_down = after(packed_down, sent_rest, sibling, base)
-    spread_down = lax.all_to_all(packed_down, "ctx", 0, 0, axis_index_groups=blocks)
-    arrived = exchange(sent_rest)
-    mine = jnp.arange(arrived[0].shape[0], dtype=jnp.int32)[:, None] < 544
-    wide_close = jnp.where(mine, close, far_close)
-    own = jnp.where(wide_close, arrived[0], arrived[1])
-    other = jnp.where(wide_close, arrived[2], arrived[3])
-    rest = jnp.stack([jnp.where(plane == 0, own, other), jnp.where(plane == 0, other, own)])
-
-    spread_down = after(spread_down, rest)
-    sent_down = pick(spread_down, stretch_adapter, elsewhere, adapter_owner, None)
-    arrived = exchange(sent_down)
-    dealt = [jnp.stack([even[j], sibling[j]]) for j in range(PIECES // 2)]
-    dealt = [swap(after(block, arrived[2]), 2 * j) if j else block for j, block in enumerate(dealt)]
-    rest = gather(after(rest, arrived[2]))
-    partial_sums = narrow(stretch_adapter, adapter_owner, arrived, dealt)
-    base = gather(after(base, *partial_sums))
-
+
+    spread = lax.all_to_all(packed, "ctx", 0, 0, axis_index_groups=blocks)
+    spread = after(spread, packed_second, sibling, base)
+    sent = pick(spread, stretch_adapter, elsewhere, adapter_owner, (896, KEYVAL_ROWS))
+    arrived = exchange(sent)
+    dealt = [after(jnp.stack([even[j], sibling[j]]), sent) for j in range(PIECES // 2)]
+    dealt = [swap(block, 2 * j) if j else block for j, block in enumerate(dealt)]
+    base = along_z(after(base, arrived[2]))
+    packed_second = after(packed_second, arrived[2])
+    spread = lax.all_to_all(packed_second, "ctx", 0, 0, axis_index_groups=blocks)
+
+    near, far = pick(
+        after(spread, arrived[1]), stretch_adapter, elsewhere, adapter_owner, None
+    )
+    far = swap(far, PIECES)
+
+    weight, ups = join(stretch_adapter, adapter_owner, arrived)
+    partial_sums = narrow(after(weight, near), dealt)
     back = [swap(block, 2 * j) if j else block for j, block in enumerate(partial_sums)]
     back = sum(block.astype(jnp.float32) for block in back)
     own_rank = back[0] + swap(back[1].astype(jnp.bfloat16), 1).astype(jnp.float32)
     own_rank = own_rank.astype(jnp.bfloat16)
     all_rank = own_rank[:, ADAPTER_RANK:]
+    ups = along_z(after(ups, *partial_sums))
+    base = along_x(after(base, own_rank))
     all_rank = jnp.stack([all_rank, swap(all_rank, PIECES)])
+    far = after(far, all_rank)
+    own, across = settle(stretch_adapter, elsewhere, adapter_owner, near, far)
+    ends = jnp.stack([own, swap(across, 2 * PIECES)])
+    ups = along_x(after(ups, all_rank))
     all_rank = jnp.stack([swap(all_rank, apart) if apart else all_rank for apart in (0, 2, 4, 6)])
+    ends = along_z(after(ends, all_rank))
+    base = after(base, all_rank)
+    ups = after(ups, all_rank)
     all_rank = jnp.stack([all_rank, swap(all_rank, 1)])
-
-    rest = complete(rest, *partial_sums)
-    query_up = rest[:, :, :128].reshape(ADAPTER_RANK, QH * HEAD_SIZE)
-    keyval_up = jnp.stack([rest[:, :, 128:160], rest[:, :, 544:]])
-    keyval_up = keyval_up.reshape(2, ADAPTER_RANK, 2 * KEYVALUE_HEADS * HEAD_SIZE)
-    down_out = rest[:, :, 160:288].reshape(QH * HEAD_SIZE, ADAPTER_RANK)
-    up_out = rest[:, :, 288:544].reshape(ADAPTER_RANK, D)
-    base = complete(base)
+    base = (base, swap(base, 1))
+    ups = (ups, swap(ups, 1))
+    ends = along_x(after(ends, all_rank))
+    ends = (ends, swap(ends, 1))
 
     half_dim = HEAD_SIZE // 2
     frequency = rope_base ** (-(jnp.arange(half_dim, dtype=jnp.float32) * 2.0) / HEAD_SIZE)
@@ -735,18 +785,8 @@
     sine = jnp.sin(angle)
     cosines = jnp.concatenate([cosine, cosine], 1)
     sines = jnp.concatenate([-sine, sine], 1)
-    return attend(
-        query_base,
-        base,
-        own_rank,
-        all_rank,
-        query_up,
-        keyval_up,
-        cosines,
-        sines,
-        down_out,
-        up_out,
-    )
+    attended = attend(query_base, base, own_rank, all_rank, ups, cosines, sines)
+    return attended, widen(attended, ends)
 
 
 def shards(normed_input, query_base, key_base, value_base, adapter_pool, stretch_adapter, owner):

time: 172 us -> 155 us (0.901)
  local copies, waits for them, and re-layouts: 18.2 us -> 2.51 us
  between operations: 3.56 us -> 1.06 us
  other arithmetic: 5.33 us -> 7.6 us
    reshape x3 -> x0, local copies, waits for them, and re-layouts: 6.73 us -> none  [the longest x1 2.36 us: direct_shards(): down_out = rest[:, :, 160:288].reshape(QH * HEAD_SIZE, ADAPTER_RANK)]
    slice x6 -> x2, local copies, waits for them, and re-layouts: 6.03 us -> 0.07 us  [the longest x1 0.04 us: direct_shards(): sibling[j]]
    ppermute x35 -> x29, waiting for transfers between devices: 69 us -> 71.5 us  [swap(): lax.ppermute(block, ('groups', 'ctx'), [(i, i ^ mask) for i in range(4 *...]
    all_to_all x2, waiting for transfers between devices: 3.94 us -> 1.5 us  [the longest x1 1.5 us: direct_shards(): spread = lax.all_to_all(packed, 'ctx', 0, 0, axis_index_groups=blocks)]
    unnamed x41 -> x27, local copies, waits for them, and re-layouts: 4.29 us -> 2.17 us
    another operation x6 -> x9, other arithmetic: 1.03 us -> 2.81 us  [the longest x2 1.53 us: direct_shards(): jnp.stack([even[j], sibling[j]])]
    pallas_call x5 -> x6, Pallas kernels: 16.7 us -> 18.4 us  [the longest x1 10.7 us: attend(): pl.pallas_call(attend_kernel, grid=(KEYVALUE_HEADS,), out_shape=jax.Shape...]
    ppermute x35 -> x29, starting transfers between devices: 35.2 us -> 33.5 us  [swap(): lax.ppermute(block, ('groups', 'ctx'), [(i, i ^ mask) for i in range(4 *...]
  transfers between devices with their start and end apart: 37 -> 31, of which waited for: 17 -> 16; matrix products, arithmetic and copies ran while one was open for 11% -> 5% of each run, Pallas kernels for 4% -> 11%
where the time goes in v5:
time: 155 us
  waiting for transfers between devices  73 us (47%)
  starting transfers between devices  44.6 us (29%)
  Pallas kernels  25.8 us (17%)
  other arithmetic  7.6 us (5%)
  local copies, waits for them, and re-layouts  2.51 us (2%)
    ppermute x29, waiting for transfers between devices, swap(): lax.ppermute(block, ('groups', 'ctx'), [(i, i ^ mask) for i in range(4 *...  71.5 us
    ppermute x29, starting transfers between devices, swap(): lax.ppermute(block, ('groups', 'ctx'), [(i, i ^ mask) for i in range(4 *...  33.5 us
    pallas_call x1, Pallas kernels, attend(): pl.pallas_call(attend_kernel, grid=(KEYVALUE_HEADS,), out_shape=jax.Shape...  10.7 us
    pallas_call x2, Pallas kernels, pack_row(): pl.pallas_call(partial(pack_kernel, sections), out_shape=jax.ShapeDtypeSt...  6.66 us
    all_to_all x1, starting transfers between devices, direct_shards(): lax.all_to_all(packed_second, 'ctx', 0, 0, axis_index_groups=blocks)  5.59 us
    all_to_all x1, starting transfers between devices, direct_shards(): spread = lax.all_to_all(packed, 'ctx', 0, 0, axis_index_groups=blocks)  5.5 us
    pallas_call x2, Pallas kernels, pick(): pl.pallas_call(partial(pick_kernel, mirrored), out_shape=(slab,) * count,...  3.16 us
  transfers between devices with their start and end apart: 31, of which 16 were waited for; matrix products, arithmetic and copies ran while one was open for 5% of the time, Pallas kernels for 11%

profile of v5, /device:TPU:0, one launch (start us, length us, event | category | flops | bytes accessed | tf_op | source)
XLA Modules:
  0.0 154.6 jit_solution(3811866270258760254)
XLA Ops:
  0.6 4.0 %shard_map.86.refs_0_ = bf16[8,928,128]{2,1,0:T(8,128)(2,1)} custom-call(bf16[1,2686976]{1,0:T(2,128)(2,1)} %pool.3), custom_call_target="tpu_custom_call" | custom-call | bytes 8388608 | tf_op jit(solution)/shard_map/pallas_call | solution.py:316
  4.7 5.5 %all-to-all-start = ((bf16[8,928,128]{2,1,0:T(8,128)(2,1)}), bf16[8,928,128]{2,1,0:T(8,128)(2,1)}, u32[]{:S(2)}, u32[]{:S(2)}) async-start(bf16[8,928,128]{2,1,0:T(8,128)(2,1)} %shard_map.86.refs_0_), calls=%async_computation | async-start | bytes 3801088 | tf_op jit(solution)/shard_map/all_to_all | solution.py:742
  10.3 0.3 shard_map.88
  10.5 0.6 collective-permute-start.2
  11.2 3.2 %collective-permute-start = (bf16[64,1024]{1,0:T(8,128)(2,1)S(1)}, bf16[64,1024]{1,0:T(8,128)(2,1)S(1)}, u32[]{:S(2)}, u32[]{:S(2)}) collective-permute-start(bf16[64,1024]{1,0:T(8,128)(2,1)S(1)} %constant_dynamic-update-slice_fusion), channel_id=1, source_target_pairs={{0,8},{1,9},{2,10},{3,11},{4,12},{5,13},{6,14},{7,15},{8,0},{9,1},... | collective-permute-start | bytes 393224 | tf_op jit(solution)/shard_map/ppermute | solution.py:711
  14.3 1.5 collective-permute-start.1
  15.9 2.6 %shard_map.87 = bf16[8,384,128]{2,1,0:T(8,128)(2,1)} custom-call(bf16[1,2686976]{1,0:T(2,128)(2,1)} %pool.3, bf16[8,928,128]{2,1,0:T(8,128)(2,1)} %shard_map.86.refs_0_), custom_call_target="tpu_custom_call" | custom-call | bytes 8388608 | tf_op jit(solution)/shard_map/pallas_call | solution.py:316
  18.5 16.0 %collective-permute-done = bf16[64,1024]{1,0:T(8,128)(2,1)S(1)} collective-permute-done((bf16[64,1024]{1,0:T(8,128)(2,1)S(1)}, bf16[64,1024]{1,0:T(8,128)(2,1)S(1)}, u32[]{:S(2)}, u32[]{:S(2)}) %collective-permute-start) | collective-permute-done | bytes 131104 | tf_op jit(solution)/shard_map/ppermute | solution.py:711
  34.5 0.7 pad_maximum_fusion.7
  35.3 1.5 all-to-all-done.spread
  36.8 2.0 %shard_map.89 = (bf16[960,128]{1,0:T(8,128)(2,1)S(1)}, bf16[960,128]{1,0:T(8,128)(2,1)S(1)}, bf16[960,128]{1,0:T(8,128)(2,1)S(1)}, bf16[960,128]{1,0:T(8,128)(2,1)S(1)}) custom-call(s32[2]{0:T(128)S(1)} %copy-done.3, s32[2]{0:T(128)S(1)} %collective-permute-done.1.there, s32[16]{0:T(128)S(1)} %copy-done.4, bf16[8,928,128]{2,1,0:T(8,128)(2,1)} %all-to-all-done.spread), custom_call_target="tpu_custom_call" | custom-call | bytes 2097152 | tf_op jit(solution)/shard_map/pallas_call | solution.py:363
  38.8 2.0 %collective-permute-start.3 = (bf16[960,128]{1,0:T(8,128)(2,1)S(1)}, bf16[960,128]{1,0:T(8,128)(2,1)S(1)}, u32[]{:S(2)}, u32[]{:S(2)}) collective-permute-start(bf16[960,128]{1,0:T(8,128)(2,1)S(1)} %get-tuple-element.37), channel_id=1, source_target_pairs={{0,16},{1,17},{2,18},{3,19},{4,20},{5,21},{6,22},{7,23},{8,24},{9,... | collective-permute-start | bytes 737288 | tf_op jit(solution)/shard_map/ppermute | solution.py:711
  40.8 5.8 %collective-permute-done.3.refs_2_ = bf16[960,128]{1,0:T(8,128)(2,1)S(1)} collective-permute-done((bf16[960,128]{1,0:T(8,128)(2,1)S(1)}, bf16[960,128]{1,0:T(8,128)(2,1)S(1)}, u32[]{:S(2)}, u32[]{:S(2)}) %collective-permute-start.3) | collective-permute-done | bytes 245792 | tf_op jit(solution)/shard_map/ppermute | solution.py:711
  46.6 5.6 %all-to-all-start.1 = ((bf16[8,384,128]{2,1,0:T(8,128)(2,1)}), bf16[8,384,128]{2,1,0:T(8,128)(2,1)S(1)}, u32[]{:S(2)}, u32[]{:S(2)}) async-start(bf16[8,384,128]{2,1,0:T(8,128)(2,1)} %shard_map.87), calls=%async_computation.1 | async-start | bytes 1572864 | tf_op jit(solution)/shard_map/all_to_all | solution.py:750
  52.2 0.8 pad_maximum_fusion.8
  53.0 0.8 pad_maximum_fusion.10
  53.8 2.0 %collective-permute-start.7 = (bf16[2,64,1024]{2,1,0:T(8,128)(2,1)}, bf16[2,64,1024]{2,1,0:T(8,128)(2,1)S(1)}, u32[]{:S(2)}, u32[]{:S(2)}) collective-permute-start(bf16[2,64,1024]{2,1,0:T(8,128)(2,1)} %get-tuple-element.49), channel_id=1, source_target_pairs={{0,2},{1,3},{2,0},{3,1},{4,6},{5,7},{6,4},{7,5},{8,10},{9,11},{10,... | collective-permute-start | bytes 786440 | tf_op jit(solution)/shard_map/ppermute | solution.py:711
  55.8 1.5 collective-permute-start.8
  57.3 0.1 collective-permute-start.5
  57.3 3.8 %collective-permute-start.6 = (bf16[960,128]{1,0:T(8,128)(2,1)S(1)}, bf16[960,128]{1,0:T(8,128)(2,1)S(1)}, u32[]{:S(2)}, u32[]{:S(2)}) collective-permute-start(bf16[960,128]{1,0:T(8,128)(2,1)S(1)} %get-tuple-element.41), channel_id=1, source_target_pairs={{0,24},{1,25},{2,26},{3,27},{4,28},{5,29},{6,30},{7,31},{8,16},{9,... | collective-permute-start | bytes 737288 | tf_op jit(solution)/shard_map/ppermute | solution.py:711
  61.1 17.3 %collective-permute-done.5.refs_1_ = bf16[960,128]{1,0:T(8,128)(2,1)S(1)} collective-permute-done((bf16[960,128]{1,0:T(8,128)(2,1)S(1)}, bf16[960,128]{1,0:T(8,128)(2,1)S(1)}, u32[]{:S(2)}, u32[]{:S(2)}) %collective-permute-start.5) | collective-permute-done | bytes 245792 | tf_op jit(solution)/shard_map/ppermute | solution.py:711
  78.5 5.1 %collective-permute-done.6.refs_3_ = bf16[960,128]{1,0:T(8,128)(2,1)S(1)} collective-permute-done((bf16[960,128]{1,0:T(8,128)(2,1)S(1)}, bf16[960,128]{1,0:T(8,128)(2,1)S(1)}, u32[]{:S(2)}, u32[]{:S(2)}) %collective-permute-start.6) | collective-permute-done | bytes 245792 | tf_op jit(solution)/shard_map/ppermute | solution.py:711
  83.5 1.0 shard_map.90
  84.5 1.2 shard_map.91
  85.7 0.8 collective-permute-done.9.refs_3_
  86.5 0.4 shard_map.92
  86.9 3.4 %collective-permute-start.12 = (bf16[2,64,192]{2,1,0:T(8,128)(2,1)S(1)}, bf16[2,64,192]{2,1,0:T(8,128)(2,1)S(1)}, u32[]{:S(2)}, u32[]{:S(2)}) collective-permute-start(bf16[2,64,192]{2,1,0:T(8,128)(2,1)S(1)} %get-tuple-element.55), channel_id=1, source_target_pairs={{0,6},{1,7},{2,4},{3,5},{4,2},{5,3},{6,0},{7,1},{8,14},{9,15},{10,... | collective-permute-start | bytes 147464 | tf_op jit(solution)/shard_map/ppermute | solution.py:711
  90.4 0.6 collective-permute-start.10
  91.0 1.9 %collective-permute-start.4 = (bf16[2,64,1024]{2,1,0:T(8,128)(2,1)S(1)}, bf16[2,64,1024]{2,1,0:T(8,128)(2,1)S(1)}, u32[]{:S(2)}, u32[]{:S(2)}) collective-permute-start(bf16[2,64,1024]{2,1,0:T(8,128)(2,1)S(1)} %copy-done.6), channel_id=1, source_target_pairs={{0,4},{1,5},{2,6},{3,7},{4,0},{5,1},{6,2},{7,3},{8,12},{9,13},{10,... | collective-permute-start | bytes 786440 | tf_op jit(solution)/shard_map/ppermute | solution.py:711
  93.0 2.4 %collective-permute-done.11 = bf16[2,64,192]{2,1,0:T(8,128)(2,1)S(1)} collective-permute-done((bf16[2,64,192]{2,1,0:T(8,128)(2,1)S(1)}, bf16[2,64,192]{2,1,0:T(8,128)(2,1)S(1)}, u32[]{:S(2)}, u32[]{:S(2)}) %collective-permute-start.11) | collective-permute-done | bytes 49184 | tf_op jit(solution)/shard_map/ppermute | solution.py:711
  95.5 0.1 collective-permute-start.13
  95.5 3.8 %collective-permute-done.4 = bf16[2,64,1024]{2,1,0:T(8,128)(2,1)S(1)} collective-permute-done((bf16[2,64,1024]{2,1,0:T(8,128)(2,1)S(1)}, bf16[2,64,1024]{2,1,0:T(8,128)(2,1)S(1)}, u32[]{:S(2)}, u32[]{:S(2)}) %collective-permute-start.4) | collective-permute-done | bytes 262176 | tf_op jit(solution)/shard_map/ppermute | solution.py:711
  99.3 1.0 pad_maximum_fusion.2
  100.4 1.1 collective-permute-start.14
  101.5 0.1 slice_bitcast_fusion.1
  101.6 2.6 %collective-permute-start.15 = (bf16[64,128]{1,0:T(8,128)(2,1)S(1)}, bf16[64,128]{1,0:T(8,128)(2,1)S(1)}, u32[]{:S(2)}, u32[]{:S(2)}) collective-permute-start(bf16[64,128]{1,0:T(8,128)(2,1)S(1)} %get-tuple-element.81), channel_id=1, source_target_pairs={{0,8},{1,9},{2,10},{3,11},{4,12},{5,13},{6,14},{7,15},{8,0},{9,1},... | collective-permute-start | bytes 49160 | tf_op jit(solution)/shard_map/ppermute | solution.py:711
  104.2 0.3 collective-permute-start.24
  104.5 4.2 %collective-permute-done.15 = bf16[64,128]{1,0:T(8,128)(2,1)S(1)} collective-permute-done((bf16[64,128]{1,0:T(8,128)(2,1)S(1)}, bf16[64,128]{1,0:T(8,128)(2,1)S(1)}, u32[]{:S(2)}, u32[]{:S(2)}) %collective-permute-start.15) | collective-permute-done | bytes 16416 | tf_op jit(solution)/shard_map/ppermute | solution.py:711
  108.7 2.0 %collective-permute-start.17 = (bf16[2,64,128]{2,1,0:T(8,128)(2,1)S(1)}, bf16[2,64,128]{2,1,0:T(8,128)(2,1)S(1)}, u32[]{:S(2)}, u32[]{:S(2)}) collective-permute-start(bf16[2,64,128]{2,1,0:T(8,128)(2,1)S(1)} %get-tuple-element.79), channel_id=1, source_target_pairs={{0,4},{1,5},{2,6},{3,7},{4,0},{5,1},{6,2},{7,3},{8,12},{9,13},{10,... | collective-permute-start | bytes 98312 | tf_op jit(solution)/shard_map/ppermute | solution.py:711
  110.7 1.5 collective-permute-start.16
  112.2 3.2 %collective-permute-done.18 = bf16[2,64,128]{2,1,0:T(8,128)(2,1)S(1)} collective-permute-done((bf16[2,64,128]{2,1,0:T(8,128)(2,1)S(1)}, bf16[2,64,128]{2,1,0:T(8,128)(2,1)S(1)}, u32[]{:S(2)}, u32[]{:S(2)}) %collective-permute-start.18) | collective-permute-done | bytes 32800 | tf_op jit(solution)/shard_map/ppermute | solution.py:711
  115.4 0.1 collective-permute-start.20
  115.5 0.6 shard_map.94
  116.1 0.6 collective-permute-start.25
  116.7 0.1 pad_maximum_fusion
  116.8 0.1 copy.9
  116.9 0.3 collective-permute-start.19
  117.2 2.8 %collective-permute-done.21 = bf16[2,192,128]{2,1,0:T(8,128)(2,1)S(1)} collective-permute-done((bf16[2,192,128]{2,1,0:T(8,128)(2,1)S(1)}, bf16[2,192,128]{2,1,0:T(8,128)(2,1)S(1)}, u32[]{:S(2)}, u32[]{:S(2)}) %collective-permute-start.21) | collective-permute-done | bytes 98336 | tf_op jit(solution)/shard_map/ppermute | solution.py:711
  120.0 1.1 collective-permute-start.22
  121.1 0.3 collective-permute-done.25
  121.4 2.1 %collective-permute-start.26 = (bf16[2,384,128]{2,1,0:T(8,128)(2,1)S(1)}, bf16[2,384,128]{2,1,0:T(8,128)(2,1)S(1)}, u32[]{:S(2)}, u32[]{:S(2)}) collective-permute-start(bf16[2,384,128]{2,1,0:T(8,128)(2,1)S(1)} %pad_maximum_fusion.14), channel_id=1, source_target_pairs={{0,4},{1,5},{2,6},{3,7},{4,0},{5,1},{6,2},{7,3},{8,12},{9,13},{10,... | collective-permute-start | bytes 589832 | tf_op jit(solution)/shard_map/ppermute | solution.py:711
  123.5 0.7 pad_maximum_fusion.12.all_rank
  124.2 1.5 collective-permute-done.22
  125.8 0.1 collective-permute-start.23
  125.9 2.4 %collective-permute-done.26 = bf16[2,384,128]{2,1,0:T(8,128)(2,1)S(1)} collective-permute-done((bf16[2,384,128]{2,1,0:T(8,128)(2,1)S(1)}, bf16[2,384,128]{2,1,0:T(8,128)(2,1)S(1)}, u32[]{:S(2)}, u32[]{:S(2)}) %collective-permute-start.26) | collective-permute-done | bytes 196640 | tf_op jit(solution)/shard_map/ppermute | solution.py:711
  128.3 1.1 collective-permute-start.27
  129.4 1.9 %fusion = (f32[1024,64]{1,0:T(8,128)S(1)}, f32[1024,64]{1,0:T(8,128)S(1)}, f32[1024,64]{1,0:T(8,128)S(1)}) fusion(f32[64]{0:T(128)S(1)} %multiply_power_fusion, f32[1024]{0:T(1024)S(1)} %iota_convert_fusion), kind=kLoop, calls=%fused_computation.17 | loop fusion | flops 131072 | bytes 790784 | tf_op jit(solution)/shard_map/neg | solution.py:787
  131.3 1.3 pad_maximum_fusion.3
  132.6 5.9 %collective-permute-done.27 = bf16[2,2,384,128]{3,2,1,0:T(8,128)(2,1)S(1)} collective-permute-done((bf16[2,2,384,128]{3,2,1,0:T(8,128)(2,1)S(1)}, bf16[2,2,384,128]{3,2,1,0:T(8,128)(2,1)S(1)}, u32[]{:S(2)}, u32[]{:S(2)}) %collective-permute-start.27) | collective-permute-done | bytes 393248 | tf_op jit(solution)/shard_map/ppermute | solution.py:711
  138.5 0.1 pad_maximum_fusion.1
  138.8 1.0 copy-done.11
  139.8 10.7 %shard_map.93.attended = bf16[64,4096]{1,0:T(8,128)(2,1)} custom-call(bf16[64,4096]{1,0:T(8,128)(2,1)} %query_block.1, bf16[4,2,64,1024]{3,2,1,0:T(8,128)(2,1)} %bitcast.45, bf16[4,2,64,1024]{3,2,1,0:T(8,128)(2,1)} %copy-done.11, bf16[4,2,64,1024]{3,2,1,0:T(8,128)(2,1)} %bitcast.46, bf16[4,2,64,1024]{3,2,1,0:T(8,128)(2,1)} %copy-done.11, ...), custom_call_target="tpu_custom_call" | custom-call | flops 12884901888 | bytes 10485760 | tf_op jit(solution)/shard_map/pallas_call | solution.py:635
  150.6 1.0 copy-done.2
  151.6 3.0 %shard_map.95 = bf16[64,8192]{1,0:T(8,128)(2,1)} custom-call(bf16[64,4096]{1,0:T(8,128)(2,1)S(1)} %copy-done.2, bf16[4,2,384,128]{3,2,1,0:T(8,128)(2,1)S(1)} %bitcast.39, bf16[4,2,384,128]{3,2,1,0:T(8,128)(2,1)S(1)} %collective-permute-done.28.other), custom_call_target="tpu_custom_call" | custom-call | flops 134217728 | bytes 4194304 | tf_op jit(solution)/shard_map/pallas_call | solution.py:696
  (62 shorter events, 0.7 us)
Async XLA Ops:
  4.7 5.5 %copy-start = (bf16[8,928,128]{2,1,0:T(8,128)(2,1)S(1)}, bf16[8,928,128]{2,1,0:T(8,128)(2,1)}, u32[]{:S(2)}) copy-start(bf16[8,928,128]{2,1,0:T(8,128)(2,1)} %shard_map.86.refs_0_) | copy-start | bytes 5701636
  4.7 5.5 %copy-start.1 = (bf16[64,8192]{1,0:T(8,128)(2,1)S(1)}, bf16[64,8192]{1,0:T(8,128)(2,1)}, u32[]{:S(2)}) copy-start(bf16[64,8192]{1,0:T(8,128)(2,1)} %rows.1) | copy-start | bytes 3145732
  4.7 32.1 %all-to-all-start = ((bf16[8,928,128]{2,1,0:T(8,128)(2,1)}), bf16[8,928,128]{2,1,0:T(8,128)(2,1)}, u32[]{:S(2)}, u32[]{:S(2)}) async-start(bf16[8,928,128]{2,1,0:T(8,128)(2,1)} %shard_map.86.refs_0_), calls=%async_computation | async-start | bytes 3801088 | tf_op jit(solution)/shard_map/all_to_all | solution.py:742
  10.2 0.9 copy-start.9
  10.2 0.9 copy-start.10
  10.2 4.1 %copy-start.3 = (s32[2]{0:T(128)S(1)}, s32[2]{0:T(128)}, u32[]{:S(2)}) copy-start(s32[2]{0:T(128)} %here.7) | copy-start | bytes 28
  10.5 24.7 %collective-permute-start.2 = (bf16[4,64,1024]{2,1,0:T(8,128)(2,1)S(1)}, bf16[4,64,1024]{2,1,0:T(8,128)(2,1)S(1)}, u32[]{:S(2)}, u32[]{:S(2)}) collective-permute-start(bf16[4,64,1024]{2,1,0:T(8,128)(2,1)S(1)} %get-tuple-element.35), channel_id=1, source_target_pairs={{0,1},{1,0},{2,3},{3,2},{4,5},{5,4},{6,7},{7,6},{8,9},{9,8},{10,11... | collective-permute-start | bytes 1572872 | tf_op jit(solution)/shard_map/ppermute | solution.py:711
  11.1 25.6 %copy-start.4 = (s32[16]{0:T(128)S(1)}, s32[16]{0:T(128)}, u32[]{:S(2)}) copy-start(s32[16]{0:T(128)} %owner.7) | copy-start | bytes 196
  11.2 23.4 %collective-permute-start = (bf16[64,1024]{1,0:T(8,128)(2,1)S(1)}, bf16[64,1024]{1,0:T(8,128)(2,1)S(1)}, u32[]{:S(2)}, u32[]{:S(2)}) collective-permute-start(bf16[64,1024]{1,0:T(8,128)(2,1)S(1)} %constant_dynamic-update-slice_fusion), channel_id=1, source_target_pairs={{0,8},{1,9},{2,10},{3,11},{4,12},{5,13},{6,14},{7,15},{8,0},{9,1},... | collective-permute-start | bytes 393224 | tf_op jit(solution)/shard_map/ppermute | solution.py:711
  14.3 22.4 %collective-permute-start.1 = (s32[2]{0:T(128)S(1)}, s32[2]{0:T(128)S(1)}, u32[]{:S(2)}, u32[]{:S(2)}) collective-permute-start(s32[2]{0:T(128)S(1)} %copy-done.3), channel_id=1, source_target_pairs={{0,16},{1,17},{2,18},{3,19},{4,20},{5,21},{6,22},{7,23},{8,24},{9,... | collective-permute-start | bytes 32 | tf_op jit(solution)/shard_map/ppermute | solution.py:711
  38.8 7.8 %collective-permute-start.3 = (bf16[960,128]{1,0:T(8,128)(2,1)S(1)}, bf16[960,128]{1,0:T(8,128)(2,1)S(1)}, u32[]{:S(2)}, u32[]{:S(2)}) collective-permute-start(bf16[960,128]{1,0:T(8,128)(2,1)S(1)} %get-tuple-element.37), channel_id=1, source_target_pairs={{0,16},{1,17},{2,18},{3,19},{4,20},{5,21},{6,22},{7,23},{8,24},{9,... | collective-permute-start | bytes 737288 | tf_op jit(solution)/shard_map/ppermute | solution.py:711
  46.6 37.9 %all-to-all-start.1 = ((bf16[8,384,128]{2,1,0:T(8,128)(2,1)}), bf16[8,384,128]{2,1,0:T(8,128)(2,1)S(1)}, u32[]{:S(2)}, u32[]{:S(2)}) async-start(bf16[8,384,128]{2,1,0:T(8,128)(2,1)} %shard_map.87), calls=%async_computation.1 | async-start | bytes 1572864 | tf_op jit(solution)/shard_map/all_to_all | solution.py:750
  53.8 37.3 %copy-start.6 = (bf16[2,64,1024]{2,1,0:T(8,128)(2,1)S(1)}, bf16[2,64,1024]{2,1,0:T(8,128)(2,1)}, u32[]{:S(2)}) copy-start(bf16[2,64,1024]{2,1,0:T(8,128)(2,1)} %pad_maximum_fusion.7) | copy-start | bytes 786436
  53.8 31.9 %collective-permute-start.7 = (bf16[2,64,1024]{2,1,0:T(8,128)(2,1)}, bf16[2,64,1024]{2,1,0:T(8,128)(2,1)S(1)}, u32[]{:S(2)}, u32[]{:S(2)}) collective-permute-start(bf16[2,64,1024]{2,1,0:T(8,128)(2,1)} %get-tuple-element.49), channel_id=1, source_target_pairs={{0,2},{1,3},{2,0},{3,1},{4,6},{5,7},{6,4},{7,5},{8,10},{9,11},{10,... | collective-permute-start | bytes 786440 | tf_op jit(solution)/shard_map/ppermute | solution.py:711
  55.8 29.9 %collective-permute-start.8 = (bf16[2,64,1024]{2,1,0:T(8,128)(2,1)}, bf16[2,64,1024]{2,1,0:T(8,128)(2,1)S(1)}, u32[]{:S(2)}, u32[]{:S(2)}) collective-permute-start(bf16[2,64,1024]{2,1,0:T(8,128)(2,1)} %get-tuple-element.50), channel_id=1, source_target_pairs={{0,4},{1,5},{2,6},{3,7},{4,0},{5,1},{6,2},{7,3},{8,12},{9,13},{10,... | collective-permute-start | bytes 786440 | tf_op jit(solution)/shard_map/ppermute | solution.py:711
  57.2 29.2 %collective-permute-start.9 = (bf16[2,64,1024]{2,1,0:T(8,128)(2,1)S(1)}, bf16[2,64,1024]{2,1,0:T(8,128)(2,1)S(1)}, u32[]{:S(2)}, u32[]{:S(2)}) collective-permute-start(bf16[2,64,1024]{2,1,0:T(8,128)(2,1)S(1)} %get-tuple-element.51), channel_id=1, source_target_pairs={{0,6},{1,7},{2,4},{3,5},{4,2},{5,3},{6,0},{7,1},{8,14},{9,15},{10,... | collective-permute-start | bytes 786440 | tf_op jit(solution)/shard_map/ppermute | solution.py:711
  57.3 21.2 %collective-permute-start.5 = (bf16[960,128]{1,0:T(8,128)(2,1)S(1)}, bf16[960,128]{1,0:T(8,128)(2,1)S(1)}, u32[]{:S(2)}, u32[]{:S(2)}) collective-permute-start(bf16[960,128]{1,0:T(8,128)(2,1)S(1)} %get-tuple-element.40), channel_id=1, source_target_pairs={{0,8},{1,9},{2,10},{3,11},{4,12},{5,13},{6,14},{7,15},{8,0},{9,1},... | collective-permute-start | bytes 737288 | tf_op jit(solution)/shard_map/ppermute | solution.py:711
  57.3 26.2 %collective-permute-start.6 = (bf16[960,128]{1,0:T(8,128)(2,1)S(1)}, bf16[960,128]{1,0:T(8,128)(2,1)S(1)}, u32[]{:S(2)}, u32[]{:S(2)}) collective-permute-start(bf16[960,128]{1,0:T(8,128)(2,1)S(1)} %get-tuple-element.41), channel_id=1, source_target_pairs={{0,24},{1,25},{2,26},{3,27},{4,28},{5,29},{6,30},{7,31},{8,16},{9,... | collective-permute-start | bytes 737288 | tf_op jit(solution)/shard_map/ppermute | solution.py:711
  86.9 6.1 %collective-permute-start.12 = (bf16[2,64,192]{2,1,0:T(8,128)(2,1)S(1)}, bf16[2,64,192]{2,1,0:T(8,128)(2,1)S(1)}, u32[]{:S(2)}, u32[]{:S(2)}) collective-permute-start(bf16[2,64,192]{2,1,0:T(8,128)(2,1)S(1)} %get-tuple-element.55), channel_id=1, source_target_pairs={{0,6},{1,7},{2,4},{3,5},{4,2},{5,3},{6,0},{7,1},{8,14},{9,15},{10,... | collective-permute-start | bytes 147464 | tf_op jit(solution)/shard_map/ppermute | solution.py:711
  90.4 5.0 %collective-permute-start.11 = (bf16[2,64,192]{2,1,0:T(8,128)(2,1)S(1)}, bf16[2,64,192]{2,1,0:T(8,128)(2,1)S(1)}, u32[]{:S(2)}, u32[]{:S(2)}) collective-permute-start(bf16[2,64,192]{2,1,0:T(8,128)(2,1)S(1)} %get-tuple-element.54), channel_id=1, source_target_pairs={{0,4},{1,5},{2,6},{3,7},{4,0},{5,1},{6,2},{7,3},{8,12},{9,13},{10,... | collective-permute-start | bytes 147464 | tf_op jit(solution)/shard_map/ppermute | solution.py:711
  90.4 5.0 %collective-permute-start.10 = (bf16[2,64,192]{2,1,0:T(8,128)(2,1)S(1)}, bf16[2,64,192]{2,1,0:T(8,128)(2,1)S(1)}, u32[]{:S(2)}, u32[]{:S(2)}) collective-permute-start(bf16[2,64,192]{2,1,0:T(8,128)(2,1)S(1)} %get-tuple-element.53), channel_id=1, source_target_pairs={{0,2},{1,3},{2,0},{3,1},{4,6},{5,7},{6,4},{7,5},{8,10},{9,11},{10,... | collective-permute-start | bytes 147464 | tf_op jit(solution)/shard_map/ppermute | solution.py:711
  91.0 8.3 %collective-permute-start.4 = (bf16[2,64,1024]{2,1,0:T(8,128)(2,1)S(1)}, bf16[2,64,1024]{2,1,0:T(8,128)(2,1)S(1)}, u32[]{:S(2)}, u32[]{:S(2)}) collective-permute-start(bf16[2,64,1024]{2,1,0:T(8,128)(2,1)S(1)} %copy-done.6), channel_id=1, source_target_pairs={{0,4},{1,5},{2,6},{3,7},{4,0},{5,1},{6,2},{7,3},{8,12},{9,13},{10,... | collective-permute-start | bytes 786440 | tf_op jit(solution)/shard_map/ppermute | solution.py:711
  95.5 4.9 %collective-permute-start.13 = (bf16[64,192]{1,0:T(8,128)(2,1)S(1)}, bf16[64,192]{1,0:T(8,128)(2,1)S(1)}, u32[]{:S(2)}, u32[]{:S(2)}) collective-permute-start(bf16[64,192]{1,0:T(8,128)(2,1)S(1)} %fusion.3), channel_id=1, source_target_pairs={{0,1},{1,0},{2,3},{3,2},{4,5},{5,4},{6,7},{7,6},{8,9},{9,8},{10,11... | collective-permute-start | bytes 73736 | tf_op jit(solution)/shard_map/ppermute | solution.py:711
  100.4 16.6 %copy-start.8 = (bf16[64,192]{1,0:T(8,128)(2,1)}, bf16[64,192]{1,0:T(8,128)(2,1)S(1)}, u32[]{:S(2)}) copy-start(bf16[64,192]{1,0:T(8,128)(2,1)S(1)} %fusion.2.own_rank) | copy-start | bytes 73732
  100.4 16.3 %collective-permute-start.14 = (bf16[2,2,64,1024]{3,2,1,0:T(8,128)(2,1)S(1)}, bf16[2,2,64,1024]{3,2,1,0:T(8,128)(2,1)S(1)}, u32[]{:S(2)}, u32[]{:S(2)}) collective-permute-start(bf16[2,2,64,1024]{3,2,1,0:T(8,128)(2,1)S(1)} %pad_maximum_fusion.2), channel_id=1, source_target_pairs={{0,2},{1,3},{2,0},{3,1},{4,6},{5,7},{6,4},{7,5},{8,10},{9,11},{10,... | collective-permute-start | bytes 1572872 | tf_op jit(solution)/shard_map/ppermute | solution.py:711
  101.6 7.1 %collective-permute-start.15 = (bf16[64,128]{1,0:T(8,128)(2,1)S(1)}, bf16[64,128]{1,0:T(8,128)(2,1)S(1)}, u32[]{:S(2)}, u32[]{:S(2)}) collective-permute-start(bf16[64,128]{1,0:T(8,128)(2,1)S(1)} %get-tuple-element.81), channel_id=1, source_target_pairs={{0,8},{1,9},{2,10},{3,11},{4,12},{5,13},{6,14},{7,15},{8,0},{9,1},... | collective-permute-start | bytes 49160 | tf_op jit(solution)/shard_map/ppermute | solution.py:711
  104.2 11.3 %collective-permute-start.24 = (bf16[2,384,128]{2,1,0:T(8,128)(2,1)S(1)}, bf16[2,384,128]{2,1,0:T(8,128)(2,1)S(1)}, u32[]{:S(2)}, u32[]{:S(2)}) collective-permute-start(bf16[2,384,128]{2,1,0:T(8,128)(2,1)S(1)} %get-tuple-element.62), channel_id=1, source_target_pairs={{0,8},{1,9},{2,10},{3,11},{4,12},{5,13},{6,14},{7,15},{8,0},{9,1},... | collective-permute-start | bytes 589832 | tf_op jit(solution)/shard_map/ppermute | solution.py:711
  108.7 6.7 %collective-permute-start.18 = (bf16[2,64,128]{2,1,0:T(8,128)(2,1)S(1)}, bf16[2,64,128]{2,1,0:T(8,128)(2,1)S(1)}, u32[]{:S(2)}, u32[]{:S(2)}) collective-permute-start(bf16[2,64,128]{2,1,0:T(8,128)(2,1)S(1)} %get-tuple-element.79), channel_id=1, source_target_pairs={{0,6},{1,7},{2,4},{3,5},{4,2},{5,3},{6,0},{7,1},{8,14},{9,15},{10,... | collective-permute-start | bytes 98312 | tf_op jit(solution)/shard_map/ppermute | solution.py:711
  108.7 6.7 %collective-permute-start.17 = (bf16[2,64,128]{2,1,0:T(8,128)(2,1)S(1)}, bf16[2,64,128]{2,1,0:T(8,128)(2,1)S(1)}, u32[]{:S(2)}, u32[]{:S(2)}) collective-permute-start(bf16[2,64,128]{2,1,0:T(8,128)(2,1)S(1)} %get-tuple-element.79), channel_id=1, source_target_pairs={{0,4},{1,5},{2,6},{3,7},{4,0},{5,1},{6,2},{7,3},{8,12},{9,13},{10,... | collective-permute-start | bytes 98312 | tf_op jit(solution)/shard_map/ppermute | solution.py:711
  110.7 4.7 %collective-permute-start.16 = (bf16[2,64,128]{2,1,0:T(8,128)(2,1)S(1)}, bf16[2,64,128]{2,1,0:T(8,128)(2,1)S(1)}, u32[]{:S(2)}, u32[]{:S(2)}) collective-permute-start(bf16[2,64,128]{2,1,0:T(8,128)(2,1)S(1)} %get-tuple-element.79), channel_id=1, source_target_pairs={{0,2},{1,3},{2,0},{3,1},{4,6},{5,7},{6,4},{7,5},{8,10},{9,11},{10,... | collective-permute-start | bytes 98312 | tf_op jit(solution)/shard_map/ppermute | solution.py:711
  115.4 4.6 %collective-permute-start.21 = (bf16[2,192,128]{2,1,0:T(8,128)(2,1)S(1)}, bf16[2,192,128]{2,1,0:T(8,128)(2,1)S(1)}, u32[]{:S(2)}, u32[]{:S(2)}) collective-permute-start(bf16[2,192,128]{2,1,0:T(8,128)(2,1)S(1)} %get-tuple-element.59), channel_id=1, source_target_pairs={{0,4},{1,5},{2,6},{3,7},{4,0},{5,1},{6,2},{7,3},{8,12},{9,13},{10,... | collective-permute-start | bytes 294920 | tf_op jit(solution)/shard_map/ppermute | solution.py:711
  115.4 8.1 %collective-permute-start.20 = (bf16[4,2,64,128]{3,2,1,0:T(8,128)(2,1)S(1)}, bf16[4,2,64,128]{3,2,1,0:T(8,128)(2,1)S(1)}, u32[]{:S(2)}, u32[]{:S(2)}) collective-permute-start(bf16[4,2,64,128]{3,2,1,0:T(8,128)(2,1)S(1)} %get-tuple-element.77), channel_id=1, source_target_pairs={{0,1},{1,0},{2,3},{3,2},{4,5},{5,4},{6,7},{7,6},{8,9},{9,8},{10,11... | collective-permute-start | bytes 393224 | tf_op jit(solution)/shard_map/ppermute | solution.py:711
  116.1 5.3 %collective-permute-start.25 = (bf16[384,128]{1,0:T(8,128)(2,1)S(1)}, bf16[384,128]{1,0:T(8,128)(2,1)S(1)}, u32[]{:S(2)}, u32[]{:S(2)}) collective-permute-start(bf16[384,128]{1,0:T(8,128)(2,1)S(1)} %get-tuple-element.65), channel_id=1, source_target_pairs={{0,16},{1,17},{2,18},{3,19},{4,20},{5,21},{6,22},{7,23},{8,24},{9,... | collective-permute-start | bytes 294920 | tf_op jit(solution)/shard_map/ppermute | solution.py:711
  116.9 14.3 %copy-start.5 = (bf16[2,2,2,64,1024]{4,3,2,1,0:T(8,128)(2,1)}, bf16[2,2,2,64,1024]{4,3,2,1,0:T(8,128)(2,1)S(1)}, u32[]{:S(2)}) copy-start(bf16[2,2,2,64,1024]{4,3,2,1,0:T(8,128)(2,1)S(1)} %copy.9) | copy-start | bytes 3145732
  116.9 21.8 %collective-permute-start.19 = (bf16[4,2,64,1024]{3,2,1,0:T(8,128)(2,1)S(1)}, bf16[4,2,64,1024]{3,2,1,0:T(8,128)(2,1)S(1)}, u32[]{:S(2)}, u32[]{:S(2)}) collective-permute-start(bf16[4,2,64,1024]{3,2,1,0:T(8,128)(2,1)S(1)} %bitcast.44), channel_id=1, source_target_pairs={{0,1},{1,0},{2,3},{3,2},{4,5},{5,4},{6,7},{7,6},{8,9},{9,8},{10,11... | collective-permute-start | bytes 3145736 | tf_op jit(solution)/shard_map/ppermute | solution.py:711
  120.0 5.7 %collective-permute-start.22 = (bf16[2,2,192,128]{3,2,1,0:T(8,128)(2,1)S(1)}, bf16[2,2,192,128]{3,2,1,0:T(8,128)(2,1)S(1)}, u32[]{:S(2)}, u32[]{:S(2)}) collective-permute-start(bf16[2,2,192,128]{3,2,1,0:T(8,128)(2,1)S(1)} %pad_maximum_fusion.13), channel_id=1, source_target_pairs={{0,2},{1,3},{2,0},{3,1},{4,6},{5,7},{6,4},{7,5},{8,10},{9,11},{10,... | collective-permute-start | bytes 589832 | tf_op jit(solution)/shard_map/ppermute | solution.py:711
  121.4 6.9 %collective-permute-start.26 = (bf16[2,384,128]{2,1,0:T(8,128)(2,1)S(1)}, bf16[2,384,128]{2,1,0:T(8,128)(2,1)S(1)}, u32[]{:S(2)}, u32[]{:S(2)}) collective-permute-start(bf16[2,384,128]{2,1,0:T(8,128)(2,1)S(1)} %pad_maximum_fusion.14), channel_id=1, source_target_pairs={{0,4},{1,5},{2,6},{3,7},{4,0},{5,1},{6,2},{7,3},{8,12},{9,13},{10,... | collective-permute-start | bytes 589832 | tf_op jit(solution)/shard_map/ppermute | solution.py:711
  125.8 6.8 %copy-start.7 = (bf16[2,2,2,192,128]{4,3,2,1,0:T(8,128)(2,1)}, bf16[2,2,2,192,128]{4,3,2,1,0:T(8,128)(2,1)S(1)}, u32[]{:S(2)}) copy-start(bf16[2,2,2,192,128]{4,3,2,1,0:T(8,128)(2,1)S(1)} %copy.10) | copy-start | bytes 1179652
  125.8 12.9 %collective-permute-start.23 = (bf16[4,2,192,128]{3,2,1,0:T(8,128)(2,1)S(1)}, bf16[4,2,192,128]{3,2,1,0:T(8,128)(2,1)S(1)}, u32[]{:S(2)}, u32[]{:S(2)}) collective-permute-start(bf16[4,2,192,128]{3,2,1,0:T(8,128)(2,1)S(1)} %bitcast.51), channel_id=1, source_target_pairs={{0,1},{1,0},{2,3},{3,2},{4,5},{5,4},{6,7},{7,6},{8,9},{9,8},{10,11... | collective-permute-start | bytes 1179656 | tf_op jit(solution)/shard_map/ppermute | solution.py:711
  128.3 10.2 %collective-permute-start.27 = (bf16[2,2,384,128]{3,2,1,0:T(8,128)(2,1)S(1)}, bf16[2,2,384,128]{3,2,1,0:T(8,128)(2,1)S(1)}, u32[]{:S(2)}, u32[]{:S(2)}) collective-permute-start(bf16[2,2,384,128]{3,2,1,0:T(8,128)(2,1)S(1)} %pad_maximum_fusion.6), channel_id=1, source_target_pairs={{0,2},{1,3},{2,0},{3,1},{4,6},{5,7},{6,4},{7,5},{8,10},{9,11},{10,... | collective-permute-start | bytes 1179656 | tf_op jit(solution)/shard_map/ppermute | solution.py:711
  138.7 11.9 %collective-permute-start.28 = (bf16[4,2,384,128]{3,2,1,0:T(8,128)(2,1)S(1)}, bf16[4,2,384,128]{3,2,1,0:T(8,128)(2,1)S(1)}, u32[]{:S(2)}, u32[]{:S(2)}) collective-permute-start(bf16[4,2,384,128]{3,2,1,0:T(8,128)(2,1)S(1)} %bitcast.38), channel_id=1, source_target_pairs={{0,1},{1,0},{2,3},{3,2},{4,5},{5,4},{6,7},{7,6},{8,9},{9,8},{10,11... | collective-permute-start | bytes 2359304 | tf_op jit(solution)/shard_map/ppermute | solution.py:711
  138.8 1.1 copy-start.12
  138.8 1.0 copy-start.11
  150.6 1.0 copy-start.2

commit v6 on v5

--- a/solution.py
+++ b/solution.py
@@ -665,7 +665,9 @@
     )(query_base, base[0], base[1], base[0], base[1], own_rank, all_rank, *ups, cosines, sines)
 
 
-def widen_kernel(attended, same, other, out_delta, down_out, up_out):
+def widen_kernel(attended_rows, same, other, out_delta, down_out, up_out, attended, sem):
+    fetch = pltpu.make_async_copy(attended_rows, attended, sem)
+    fetch.start()
     plane = lax.axis_index("groups")
     seat = lax.rem(lax.axis_index("ctx"), PIECES)
     for apart in range(PIECES):
@@ -680,6 +682,7 @@
             first = pl.multiple_of(place * UP_OUT_ROWS, UP_OUT_ROWS)
             up_out[pl.ds(first, UP_OUT_ROWS), :] = piece[DOWN_OUT_ROWS:]
     dot = partial(jnp.dot, preferred_element_type=jnp.float32)
+    fetch.wait()
     rank = dot(attended[...], down_out[...].astype(jnp.bfloat16))[:, :ADAPTER_RANK]
     rank = rank.astype(jnp.bfloat16)
     blocks = D // 128
@@ -692,19 +695,21 @@
         out_delta[:, first * 128 : (first + 4) * 128] = delta.astype(jnp.bfloat16)
 
 
-def widen(attended, pieces):
+def widen(attended, same, other):
     return pl.pallas_call(
         widen_kernel,
         out_shape=jax.ShapeDtypeStruct((attended.shape[0], D), jnp.bfloat16),
-        in_specs=[pl.BlockSpec(memory_space=pltpu.VMEM)] * 3,
+        in_specs=[pl.BlockSpec(memory_space=pl.ANY)] + [pl.BlockSpec(memory_space=pltpu.VMEM)] * 2,
         out_specs=pl.BlockSpec(memory_space=pltpu.VMEM),
         scratch_shapes=[
             pltpu.VMEM((QH * HEAD_SIZE, 128), jnp.float32),
             pltpu.VMEM((ADAPTER_RANK * D // 128, 128), jnp.float32),
+            pltpu.VMEM(attended.shape, attended.dtype),
+            pltpu.SemaphoreType.DMA,
         ],
-        compiler_params=pltpu.CompilerParams(vmem_limit_bytes=32 << 20),
+        compiler_params=pltpu.CompilerParams(vmem_limit_bytes=60 << 20),
         cost_estimate=pl.CostEstimate(flops=1 << 27, bytes_accessed=4 << 20, transcendentals=0),
-    )(attended, *pieces)
+    )(attended, same, other)
 
 
 def swap(block, mask):
@@ -718,6 +723,14 @@
     ctx = lax.axis_size("ctx")
     seq = ctx * tok_rows
     blocks = [list(range(PIECES)), list(range(PIECES, 2 * PIECES))]
+    half_dim = HEAD_SIZE // 2
+    frequency = rope_base ** (-(jnp.arange(half_dim, dtype=jnp.float32) * 2.0) / HEAD_SIZE)
+    angle = jnp.arange(seq, dtype=jnp.int32).astype(jnp.float32)[:, None] * frequency[None, :]
+    cosine = jnp.cos(angle)
+    sine = jnp.sin(angle)
+    cosines = jnp.concatenate([cosine, cosine], 1)
+    sines = jnp.concatenate([-sine, sine], 1)
+
     def after(block, *others):
         return lax.optimization_barrier((block, others))[0]
 
@@ -745,48 +758,38 @@
     arrived = exchange(sent)
     dealt = [after(jnp.stack([even[j], sibling[j]]), sent) for j in range(PIECES // 2)]
     dealt = [swap(block, 2 * j) if j else block for j, block in enumerate(dealt)]
-    base = along_z(after(base, arrived[2]))
-    packed_second = after(packed_second, arrived[2])
+    packed_second = after(packed_second, arrived[1])
     spread = lax.all_to_all(packed_second, "ctx", 0, 0, axis_index_groups=blocks)
 
-    near, far = pick(
-        after(spread, arrived[1]), stretch_adapter, elsewhere, adapter_owner, None
-    )
-    far = swap(far, PIECES)
-
     weight, ups = join(stretch_adapter, adapter_owner, arrived)
-    partial_sums = narrow(after(weight, near), dealt)
+    partial_sums = narrow(after(weight, cosines, sines), dealt)
     back = [swap(block, 2 * j) if j else block for j, block in enumerate(partial_sums)]
     back = sum(block.astype(jnp.float32) for block in back)
-    own_rank = back[0] + swap(back[1].astype(jnp.bfloat16), 1).astype(jnp.float32)
+    own_rank = swap(after(back[1].astype(jnp.bfloat16), spread), 1)
+    own_rank = back[0] + own_rank.astype(jnp.float32)
     own_rank = own_rank.astype(jnp.bfloat16)
     all_rank = own_rank[:, ADAPTER_RANK:]
+    base = along_z(after(base, *partial_sums))
     ups = along_z(after(ups, *partial_sums))
-    base = along_x(after(base, own_rank))
+    near, far = pick(spread, stretch_adapter, elsewhere, adapter_owner, None)
+    far = swap(far, PIECES)
     all_rank = jnp.stack([all_rank, swap(all_rank, PIECES)])
-    far = after(far, all_rank)
+    all_rank = after(all_rank, ups)
+    ups = along_x(after(ups, all_rank))
+    base = along_x(after(base, all_rank))
     own, across = settle(stretch_adapter, elsewhere, adapter_owner, near, far)
+    all_rank = jnp.stack([swap(all_rank, apart) if apart else all_rank for apart in (0, 2, 4, 6)])
+    all_rank = after(all_rank, across, ups)
+    base = after(base, all_rank)
     ends = jnp.stack([own, swap(across, 2 * PIECES)])
-    ups = along_x(after(ups, all_rank))
-    all_rank = jnp.stack([swap(all_rank, apart) if apart else all_rank for apart in (0, 2, 4, 6)])
-    ends = along_z(after(ends, all_rank))
-    base = after(base, all_rank)
-    ups = after(ups, all_rank)
     all_rank = jnp.stack([all_rank, swap(all_rank, 1)])
+    ends = jnp.stack([swap(ends, apart) if apart else ends for apart in (0, 2, 4, 6)])
     base = (base, swap(base, 1))
     ups = (ups, swap(ups, 1))
-    ends = along_x(after(ends, all_rank))
     ends = (ends, swap(ends, 1))
 
-    half_dim = HEAD_SIZE // 2
-    frequency = rope_base ** (-(jnp.arange(half_dim, dtype=jnp.float32) * 2.0) / HEAD_SIZE)
-    angle = jnp.arange(seq, dtype=jnp.int32).astype(jnp.float32)[:, None] * frequency[None, :]
-    cosine = jnp.cos(angle)
-    sine = jnp.sin(angle)
-    cosines = jnp.concatenate([cosine, cosine], 1)
-    sines = jnp.concatenate([-sine, sine], 1)
     attended = attend(query_base, base, own_rank, all_rank, ups, cosines, sines)
-    return attended, widen(attended, ends)
+    return attended, widen(attended, *ends)
 
 
 def shards(normed_input, query_base, key_base, value_base, adapter_pool, stretch_adapter, owner):

time: 155 us -> 158 us (1.019)
  waiting for transfers between devices: 73 us -> 76.7 us
  other arithmetic: 7.6 us -> 4.5 us
  Pallas kernels: 25.8 us -> 28.2 us
    ppermute x29 -> x30, waiting for transfers between devices: 71.5 us -> 74.5 us  [swap(): lax.ppermute(block, ('groups', 'ctx'), [(i, i ^ mask) for i in range(4 *...]
    pallas_call x1, Pallas kernels: 2.98 us -> 5.33 us  [widen(): pl.pallas_call(widen_kernel, out_shape=jax.ShapeDtypeStruct((attended.sha...]
    all_to_all x1, starting transfers between devices: 5.59 us -> 3.55 us  [direct_shards(): lax.all_to_all(packed_second, 'ctx', 0, 0, axis_index_groups=blocks)]
    ppermute x29 -> x30, starting transfers between devices: 33.5 us -> 34.4 us  [swap(): lax.ppermute(block, ('groups', 'ctx'), [(i, i ^ mask) for i in range(4 *...]
  transfers between devices with their start and end apart: 31 -> 32, of which waited for: 16 -> 18; matrix products, arithmetic and copies ran while one was open for 5% -> 3% of each run, Pallas kernels for 11% -> 11%
where the time goes in v6:
time: 158 us
  waiting for transfers between devices  76.7 us (49%)
  starting transfers between devices  43.5 us (28%)
  Pallas kernels  28.2 us (18%)
  other arithmetic  4.5 us (3%)
  local copies, waits for them, and re-layouts  3.91 us (2%)
    ppermute x30, waiting for transfers between devices, swap(): lax.ppermute(block, ('groups', 'ctx'), [(i, i ^ mask) for i in range(4 *...  74.5 us
    ppermute x30, starting transfers between devices, swap(): lax.ppermute(block, ('groups', 'ctx'), [(i, i ^ mask) for i in range(4 *...  34.4 us
    pallas_call x1, Pallas kernels, attend(): pl.pallas_call(attend_kernel, grid=(KEYVALUE_HEADS,), out_shape=jax.Shape...  10.7 us
    pallas_call x2, Pallas kernels, pack_row(): pl.pallas_call(partial(pack_kernel, sections), out_shape=jax.ShapeDtypeSt...  6.68 us
    all_to_all x1, starting transfers between devices, direct_shards(): spread = lax.all_to_all(packed, 'ctx', 0, 0, axis_index_groups=blocks)  5.5 us
    pallas_call x1, Pallas kernels, widen(): pl.pallas_call(widen_kernel, out_shape=jax.ShapeDtypeStruct((attended.sha...  5.33 us
    all_to_all x1, starting transfers between devices, direct_shards(): lax.all_to_all(packed_second, 'ctx', 0, 0, axis_index_groups=blocks)  3.55 us
  transfers between devices with their start and end apart: 32, of which 18 were waited for; matrix products, arithmetic and copies ran while one was open for 3% of the time, Pallas kernels for 11%

profile of v6, /device:TPU:0, one launch (start us, length us, event | category | flops | bytes accessed | tf_op | source)
XLA Modules:
  0.0 157.9 jit_solution(12708428973650680419)
XLA Ops:
  0.6 4.1 %shard_map.86.refs_0_ = bf16[8,928,128]{2,1,0:T(8,128)(2,1)} custom-call(bf16[1,2686976]{1,0:T(2,128)(2,1)} %pool.3), custom_call_target="tpu_custom_call" | custom-call | bytes 8388608 | tf_op jit(solution)/shard_map/pallas_call | solution.py:316
  4.7 5.5 %all-to-all-start = ((bf16[8,928,128]{2,1,0:T(8,128)(2,1)}), bf16[8,928,128]{2,1,0:T(8,128)(2,1)}, u32[]{:S(2)}, u32[]{:S(2)}) async-start(bf16[8,928,128]{2,1,0:T(8,128)(2,1)} %shard_map.86.refs_0_), calls=%async_computation | async-start | bytes 3801088 | tf_op jit(solution)/shard_map/all_to_all | solution.py:755
  10.3 0.3 shard_map.88
  10.6 0.6 collective-permute-start.2
  11.2 3.2 %collective-permute-start = (bf16[64,1024]{1,0:T(8,128)(2,1)S(1)}, bf16[64,1024]{1,0:T(8,128)(2,1)S(1)}, u32[]{:S(2)}, u32[]{:S(2)}) collective-permute-start(bf16[64,1024]{1,0:T(8,128)(2,1)S(1)} %constant_dynamic-update-slice_fusion), channel_id=1, source_target_pairs={{0,8},{1,9},{2,10},{3,11},{4,12},{5,13},{6,14},{7,15},{8,0},{9,1},... | collective-permute-start | bytes 393224 | tf_op jit(solution)/shard_map/ppermute | solution.py:716
  14.4 1.5 collective-permute-start.1
  15.9 2.6 %shard_map.87 = bf16[8,384,128]{2,1,0:T(8,128)(2,1)} custom-call(bf16[1,2686976]{1,0:T(2,128)(2,1)} %pool.3, bf16[8,928,128]{2,1,0:T(8,128)(2,1)} %shard_map.86.refs_0_), custom_call_target="tpu_custom_call" | custom-call | bytes 8388608 | tf_op jit(solution)/shard_map/pallas_call | solution.py:316
  18.5 16.0 %collective-permute-done = bf16[64,1024]{1,0:T(8,128)(2,1)S(1)} collective-permute-done((bf16[64,1024]{1,0:T(8,128)(2,1)S(1)}, bf16[64,1024]{1,0:T(8,128)(2,1)S(1)}, u32[]{:S(2)}, u32[]{:S(2)}) %collective-permute-start) | collective-permute-done | bytes 131104 | tf_op jit(solution)/shard_map/ppermute | solution.py:716
  34.6 2.2 %all-to-all-done.spread = bf16[8,928,128]{2,1,0:T(8,128)(2,1)} async-done(((bf16[8,928,128]{2,1,0:T(8,128)(2,1)}), bf16[8,928,128]{2,1,0:T(8,128)(2,1)}, u32[]{:S(2)}, u32[]{:S(2)}) %all-to-all-start) | async-done | bytes 1900576 | tf_op jit(solution)/shard_map/all_to_all | solution.py:755
  36.8 2.0 %shard_map.89 = (bf16[960,128]{1,0:T(8,128)(2,1)S(1)}, bf16[960,128]{1,0:T(8,128)(2,1)S(1)}, bf16[960,128]{1,0:T(8,128)(2,1)S(1)}, bf16[960,128]{1,0:T(8,128)(2,1)S(1)}) custom-call(s32[2]{0:T(128)S(1)} %copy-done.2, s32[2]{0:T(128)S(1)} %collective-permute-done.1.there, s32[16]{0:T(128)S(1)} %copy-done.3, bf16[8,928,128]{2,1,0:T(8,128)(2,1)} %all-to-all-done.spread), custom_call_target="tpu_custom_call" | custom-call | bytes 2097152 | tf_op jit(solution)/shard_map/pallas_call | solution.py:363
  38.8 1.3 collective-permute-start.3
  40.1 0.8 fusion.5
  40.9 11.6 %collective-permute-done.3.refs_1_ = bf16[960,128]{1,0:T(8,128)(2,1)S(1)} collective-permute-done((bf16[960,128]{1,0:T(8,128)(2,1)S(1)}, bf16[960,128]{1,0:T(8,128)(2,1)S(1)}, u32[]{:S(2)}, u32[]{:S(2)}) %collective-permute-start.3) | collective-permute-done | bytes 245792 | tf_op jit(solution)/shard_map/ppermute | solution.py:716
  52.5 3.5 %all-to-all-start.1 = ((bf16[8,384,128]{2,1,0:T(8,128)(2,1)}), bf16[8,384,128]{2,1,0:T(8,128)(2,1)S(1)}, u32[]{:S(2)}, u32[]{:S(2)}) async-start(bf16[8,384,128]{2,1,0:T(8,128)(2,1)} %shard_map.87), calls=%async_computation.1 | async-start | bytes 1572864 | tf_op jit(solution)/shard_map/all_to_all | solution.py:762
  56.3 2.0 %collective-permute-start.4 = (bf16[960,128]{1,0:T(8,128)(2,1)S(1)}, bf16[960,128]{1,0:T(8,128)(2,1)S(1)}, u32[]{:S(2)}, u32[]{:S(2)}) collective-permute-start(bf16[960,128]{1,0:T(8,128)(2,1)S(1)} %get-tuple-element.37), channel_id=1, source_target_pairs={{0,16},{1,17},{2,18},{3,19},{4,20},{5,21},{6,22},{7,23},{8,24},{9,... | collective-permute-start | bytes 737288 | tf_op jit(solution)/shard_map/ppermute | solution.py:716
  58.3 1.0 collective-permute-start.5
  59.3 2.0 %collective-permute-start.6 = (bf16[2,64,1024]{2,1,0:T(8,128)(2,1)S(1)}, bf16[2,64,1024]{2,1,0:T(8,128)(2,1)S(1)}, u32[]{:S(2)}, u32[]{:S(2)}) collective-permute-start(bf16[2,64,1024]{2,1,0:T(8,128)(2,1)S(1)} %get-tuple-element.43), channel_id=1, source_target_pairs={{0,2},{1,3},{2,0},{3,1},{4,6},{5,7},{6,4},{7,5},{8,10},{9,11},{10,... | collective-permute-start | bytes 786440 | tf_op jit(solution)/shard_map/ppermute | solution.py:716
  61.3 1.5 collective-permute-start.7
  62.8 1.9 %fusion = (f32[1024,64]{1,0:T(8,128)S(1)}, f32[1024,64]{1,0:T(8,128)S(1)}, f32[1024,64]{1,0:T(8,128)S(1)}) fusion(f32[64]{0:T(128)S(1)} %multiply_power_fusion, f32[1024]{0:T(1024)S(1)} %iota_convert_fusion), kind=kLoop, calls=%fused_computation.16 | loop fusion | flops 131072 | bytes 790784 | tf_op jit(solution)/shard_map/neg | solution.py:732
  64.7 1.3 pad_maximum_fusion.2
  66.0 4.1 %collective-permute-done.4.refs_2_ = bf16[960,128]{1,0:T(8,128)(2,1)S(1)} collective-permute-done((bf16[960,128]{1,0:T(8,128)(2,1)S(1)}, bf16[960,128]{1,0:T(8,128)(2,1)S(1)}, u32[]{:S(2)}, u32[]{:S(2)}) %collective-permute-start.4) | collective-permute-done | bytes 245792 | tf_op jit(solution)/shard_map/ppermute | solution.py:716
  70.1 0.9 collective-permute-done.5.refs_3_
  71.0 1.0 shard_map.90
  72.0 1.2 collective-permute-done.6.refs_1_
  73.2 5.8 %collective-permute-done.7.refs_2_ = bf16[2,64,1024]{2,1,0:T(8,128)(2,1)S(1)} collective-permute-done((bf16[2,64,1024]{2,1,0:T(8,128)(2,1)S(1)}, bf16[2,64,1024]{2,1,0:T(8,128)(2,1)S(1)}, u32[]{:S(2)}, u32[]{:S(2)}) %collective-permute-start.7) | collective-permute-done | bytes 262176 | tf_op jit(solution)/shard_map/ppermute | solution.py:716
  79.0 6.1 %collective-permute-done.8.refs_3_ = bf16[2,64,1024]{2,1,0:T(8,128)(2,1)S(1)} collective-permute-done((bf16[2,64,1024]{2,1,0:T(8,128)(2,1)S(1)}, bf16[2,64,1024]{2,1,0:T(8,128)(2,1)S(1)}, u32[]{:S(2)}, u32[]{:S(2)}) %collective-permute-start.8) | collective-permute-done | bytes 262176 | tf_op jit(solution)/shard_map/ppermute | solution.py:716
  85.1 0.5 shard_map.91
  85.6 0.4 collective-permute-start.12
  86.0 1.7 %collective-permute-start.11 = (bf16[2,64,192]{2,1,0:T(8,128)(2,1)S(1)}, bf16[2,64,192]{2,1,0:T(8,128)(2,1)S(1)}, u32[]{:S(2)}, u32[]{:S(2)}) collective-permute-start(bf16[2,64,192]{2,1,0:T(8,128)(2,1)S(1)} %get-tuple-element.48), channel_id=1, source_target_pairs={{0,4},{1,5},{2,6},{3,7},{4,0},{5,1},{6,2},{7,3},{8,12},{9,13},{10,... | collective-permute-start | bytes 147464 | tf_op jit(solution)/shard_map/ppermute | solution.py:716
  87.6 1.5 collective-permute-start.10
  89.1 0.5 collective-permute-start.9
  89.6 1.5 collective-permute-start.15
  91.2 0.7 collective-permute-done.10
  92.0 6.3 %collective-permute-done.15 = bf16[2,192,128]{2,1,0:T(8,128)(2,1)S(1)} collective-permute-done((bf16[2,192,128]{2,1,0:T(8,128)(2,1)S(1)}, bf16[2,192,128]{2,1,0:T(8,128)(2,1)S(1)}, u32[]{:S(2)}, u32[]{:S(2)}) %collective-permute-start.15) | collective-permute-done | bytes 98336 | tf_op jit(solution)/shard_map/ppermute | solution.py:716
  98.5 1.5 collective-permute-start.14
  100.1 3.1 %collective-permute-done.14 = bf16[64,128]{1,0:T(8,128)(2,1)S(1)} collective-permute-done((bf16[64,128]{1,0:T(8,128)(2,1)S(1)}, bf16[64,128]{1,0:T(8,128)(2,1)S(1)}, u32[]{:S(2)}, u32[]{:S(2)}) %collective-permute-start.14) | collective-permute-done | bytes 16416 | tf_op jit(solution)/shard_map/ppermute | solution.py:716
  103.2 1.5 collective-permute-start.16
  104.6 1.2 shard_map.92
  105.8 1.6 collective-permute-start.20
  107.4 0.6 collective-permute-start.21
  107.9 2.0 %collective-permute-start.19 = (bf16[2,64,128]{2,1,0:T(8,128)(2,1)S(1)}, bf16[2,64,128]{2,1,0:T(8,128)(2,1)S(1)}, u32[]{:S(2)}, u32[]{:S(2)}) collective-permute-start(bf16[2,64,128]{2,1,0:T(8,128)(2,1)S(1)} %pad_maximum_fusion.15), channel_id=1, source_target_pairs={{0,6},{1,7},{2,4},{3,5},{4,2},{5,3},{6,0},{7,1},{8,14},{9,15},{10,... | collective-permute-start | bytes 98312 | tf_op jit(solution)/shard_map/ppermute | solution.py:716
  109.9 1.0 collective-permute-start.18
  110.8 2.0 %collective-permute-done.19 = bf16[2,64,128]{2,1,0:T(8,128)(2,1)S(1)} collective-permute-done((bf16[2,64,128]{2,1,0:T(8,128)(2,1)S(1)}, bf16[2,64,128]{2,1,0:T(8,128)(2,1)S(1)}, u32[]{:S(2)}, u32[]{:S(2)}) %collective-permute-start.19) | collective-permute-done | bytes 32800 | tf_op jit(solution)/shard_map/ppermute | solution.py:716
  112.8 1.5 collective-permute-start.17
  114.3 1.3 collective-permute-done.18
  115.7 4.5 %collective-permute-done.17 = bf16[2,64,128]{2,1,0:T(8,128)(2,1)S(1)} collective-permute-done((bf16[2,64,128]{2,1,0:T(8,128)(2,1)S(1)}, bf16[2,64,128]{2,1,0:T(8,128)(2,1)S(1)}, u32[]{:S(2)}, u32[]{:S(2)}) %collective-permute-start.17) | collective-permute-done | bytes 32800 | tf_op jit(solution)/shard_map/ppermute | solution.py:716
  120.2 0.6 shard_map.93
  121.0 0.1 copy.9
  121.2 2.0 %collective-permute-start.25 = (bf16[384,128]{1,0:T(8,128)(2,1)S(1)}, bf16[384,128]{1,0:T(8,128)(2,1)S(1)}, u32[]{:S(2)}, u32[]{:S(2)}) collective-permute-start(bf16[384,128]{1,0:T(8,128)(2,1)S(1)} %get-tuple-element.59), channel_id=1, source_target_pairs={{0,16},{1,17},{2,18},{3,19},{4,20},{5,21},{6,22},{7,23},{8,24},{9,... | collective-permute-start | bytes 294920 | tf_op jit(solution)/shard_map/ppermute | solution.py:716
  123.3 0.2 collective-permute-start.23
  123.4 0.3 collective-permute-start.24
  123.8 2.9 %collective-permute-done.25 = bf16[384,128]{1,0:T(8,128)(2,1)S(1)} collective-permute-done((bf16[384,128]{1,0:T(8,128)(2,1)S(1)}, bf16[384,128]{1,0:T(8,128)(2,1)S(1)}, u32[]{:S(2)}, u32[]{:S(2)}) %collective-permute-start.25) | collective-permute-done | bytes 98336 | tf_op jit(solution)/shard_map/ppermute | solution.py:716
  126.7 2.5 %collective-permute-start.28 = (bf16[2,384,128]{2,1,0:T(8,128)(2,1)S(1)}, bf16[2,384,128]{2,1,0:T(8,128)(2,1)S(1)}, u32[]{:S(2)}, u32[]{:S(2)}) collective-permute-start(bf16[2,384,128]{2,1,0:T(8,128)(2,1)S(1)} %get-tuple-element.73), channel_id=1, source_target_pairs={{0,6},{1,7},{2,4},{3,5},{4,2},{5,3},{6,0},{7,1},{8,14},{9,15},{10,... | collective-permute-start | bytes 589832 | tf_op jit(solution)/shard_map/ppermute | solution.py:716
  129.2 0.8 collective-permute-start.27
  130.0 0.3 collective-permute-start.26
  130.2 0.7 pad_maximum_fusion.11.all_rank
  131.0 4.5 %collective-permute-done.28 = bf16[2,384,128]{2,1,0:T(8,128)(2,1)S(1)} collective-permute-done((bf16[2,384,128]{2,1,0:T(8,128)(2,1)S(1)}, bf16[2,384,128]{2,1,0:T(8,128)(2,1)S(1)}, u32[]{:S(2)}, u32[]{:S(2)}) %collective-permute-start.28) | collective-permute-done | bytes 196640 | tf_op jit(solution)/shard_map/ppermute | solution.py:716
  135.4 3.4 %collective-permute-done.27 = bf16[2,384,128]{2,1,0:T(8,128)(2,1)S(1)} collective-permute-done((bf16[2,384,128]{2,1,0:T(8,128)(2,1)S(1)}, bf16[2,384,128]{2,1,0:T(8,128)(2,1)S(1)}, u32[]{:S(2)}, u32[]{:S(2)}) %collective-permute-start.27) | collective-permute-done | bytes 196640 | tf_op jit(solution)/shard_map/ppermute | solution.py:716
  138.8 0.1 pad_maximum_fusion.1.same
  139.0 0.8 copy-done.16
  139.9 1.0 copy-done.15
  140.9 10.7 %shard_map.94.attended_rows = bf16[64,4096]{1,0:T(8,128)(2,1)} custom-call(bf16[64,4096]{1,0:T(8,128)(2,1)} %query_block.1, bf16[4,2,64,1024]{3,2,1,0:T(8,128)(2,1)} %bitcast.40, bf16[4,2,64,1024]{3,2,1,0:T(8,128)(2,1)} %copy-done.15, bf16[4,2,64,1024]{3,2,1,0:T(8,128)(2,1)} %bitcast.41, bf16[4,2,64,1024]{3,2,1,0:T(8,128)(2,1)} %copy-done.15, ...), custom_call_target="tpu_custom_call" | custom-call | flops 12884901888 | bytes 10485760 | tf_op jit(solution)/shard_map/pallas_call | solution.py:635
  151.6 0.9 copy-done.6
  152.5 5.3 %shard_map.95 = bf16[64,8192]{1,0:T(8,128)(2,1)} custom-call(bf16[64,4096]{1,0:T(8,128)(2,1)} %shard_map.94.attended_rows, bf16[4,2,384,128]{3,2,1,0:T(8,128)(2,1)} %copy-done.4, bf16[4,2,384,128]{3,2,1,0:T(8,128)(2,1)} %copy-done.6), custom_call_target="tpu_custom_call" | custom-call | flops 134217728 | bytes 4194304 | tf_op jit(solution)/shard_map/pallas_call | solution.py:699
  (70 shorter events, 1.0 us)
Async XLA Ops:
  4.7 5.5 %copy-start = (bf16[8,928,128]{2,1,0:T(8,128)(2,1)S(1)}, bf16[8,928,128]{2,1,0:T(8,128)(2,1)}, u32[]{:S(2)}) copy-start(bf16[8,928,128]{2,1,0:T(8,128)(2,1)} %shard_map.86.refs_0_) | copy-start | bytes 5701636
  4.7 5.5 %copy-start.1 = (bf16[64,8192]{1,0:T(8,128)(2,1)S(1)}, bf16[64,8192]{1,0:T(8,128)(2,1)}, u32[]{:S(2)}) copy-start(bf16[64,8192]{1,0:T(8,128)(2,1)} %rows.1) | copy-start | bytes 3145732
  4.7 32.1 %all-to-all-start = ((bf16[8,928,128]{2,1,0:T(8,128)(2,1)}), bf16[8,928,128]{2,1,0:T(8,128)(2,1)}, u32[]{:S(2)}, u32[]{:S(2)}) async-start(bf16[8,928,128]{2,1,0:T(8,128)(2,1)} %shard_map.86.refs_0_), calls=%async_computation | async-start | bytes 3801088 | tf_op jit(solution)/shard_map/all_to_all | solution.py:755
  10.2 0.9 copy-start.13
  10.2 0.9 copy-start.14
  10.3 4.1 %copy-start.2 = (s32[2]{0:T(128)S(1)}, s32[2]{0:T(128)}, u32[]{:S(2)}) copy-start(s32[2]{0:T(128)} %here.7) | copy-start | bytes 28
  10.6 24.0 %collective-permute-start.2 = (bf16[4,64,1024]{2,1,0:T(8,128)(2,1)S(1)}, bf16[4,64,1024]{2,1,0:T(8,128)(2,1)S(1)}, u32[]{:S(2)}, u32[]{:S(2)}) collective-permute-start(bf16[4,64,1024]{2,1,0:T(8,128)(2,1)S(1)} %get-tuple-element.33), channel_id=1, source_target_pairs={{0,1},{1,0},{2,3},{3,2},{4,5},{5,4},{6,7},{7,6},{8,9},{9,8},{10,11... | collective-permute-start | bytes 1572872 | tf_op jit(solution)/shard_map/ppermute | solution.py:716
  11.2 25.6 %copy-start.3 = (s32[16]{0:T(128)S(1)}, s32[16]{0:T(128)}, u32[]{:S(2)}) copy-start(s32[16]{0:T(128)} %owner.7) | copy-start | bytes 196
  11.2 23.4 %collective-permute-start = (bf16[64,1024]{1,0:T(8,128)(2,1)S(1)}, bf16[64,1024]{1,0:T(8,128)(2,1)S(1)}, u32[]{:S(2)}, u32[]{:S(2)}) collective-permute-start(bf16[64,1024]{1,0:T(8,128)(2,1)S(1)} %constant_dynamic-update-slice_fusion), channel_id=1, source_target_pairs={{0,8},{1,9},{2,10},{3,11},{4,12},{5,13},{6,14},{7,15},{8,0},{9,1},... | collective-permute-start | bytes 393224 | tf_op jit(solution)/shard_map/ppermute | solution.py:716
  14.4 22.4 %collective-permute-start.1 = (s32[2]{0:T(128)S(1)}, s32[2]{0:T(128)S(1)}, u32[]{:S(2)}, u32[]{:S(2)}) collective-permute-start(s32[2]{0:T(128)S(1)} %copy-done.2), channel_id=1, source_target_pairs={{0,16},{1,17},{2,18},{3,19},{4,20},{5,21},{6,22},{7,23},{8,24},{9,... | collective-permute-start | bytes 32 | tf_op jit(solution)/shard_map/ppermute | solution.py:716
  38.8 13.7 %collective-permute-start.3 = (bf16[960,128]{1,0:T(8,128)(2,1)S(1)}, bf16[960,128]{1,0:T(8,128)(2,1)S(1)}, u32[]{:S(2)}, u32[]{:S(2)}) collective-permute-start(bf16[960,128]{1,0:T(8,128)(2,1)S(1)} %get-tuple-element.36), channel_id=1, source_target_pairs={{0,8},{1,9},{2,10},{3,11},{4,12},{5,13},{6,14},{7,15},{8,0},{9,1},... | collective-permute-start | bytes 737288 | tf_op jit(solution)/shard_map/ppermute | solution.py:716
  40.9 15.2 %copy-start.9 = (bf16[1,64,1024]{2,1,0:T(8,128)(2,1)S(1)}, bf16[1,64,1024]{2,1,0:T(8,128)(2,1)}, u32[]{:S(2)}) copy-start(bf16[1,64,1024]{2,1,0:T(8,128)(2,1)} %get-tuple-element.66) | copy-start | bytes 393220
  40.9 15.2 %copy-start.10 = (bf16[1,64,1024]{2,1,0:T(8,128)(2,1)S(1)}, bf16[1,64,1024]{2,1,0:T(8,128)(2,1)}, u32[]{:S(2)}) copy-start(bf16[1,64,1024]{2,1,0:T(8,128)(2,1)} %get-tuple-element.67) | copy-start | bytes 393220
  40.9 15.3 %copy-start.7 = (bf16[1,64,1024]{2,1,0:T(8,128)(2,1)S(1)}, bf16[1,64,1024]{2,1,0:T(8,128)(2,1)}, u32[]{:S(2)}) copy-start(bf16[1,64,1024]{2,1,0:T(8,128)(2,1)} %get-tuple-element.64) | copy-start | bytes 393220
  40.9 15.3 %copy-start.8 = (bf16[1,64,1024]{2,1,0:T(8,128)(2,1)S(1)}, bf16[1,64,1024]{2,1,0:T(8,128)(2,1)}, u32[]{:S(2)}) copy-start(bf16[1,64,1024]{2,1,0:T(8,128)(2,1)} %get-tuple-element.65) | copy-start | bytes 393220
  52.5 39.5 %all-to-all-start.1 = ((bf16[8,384,128]{2,1,0:T(8,128)(2,1)}), bf16[8,384,128]{2,1,0:T(8,128)(2,1)S(1)}, u32[]{:S(2)}, u32[]{:S(2)}) async-start(bf16[8,384,128]{2,1,0:T(8,128)(2,1)} %shard_map.87), calls=%async_computation.1 | async-start | bytes 1572864 | tf_op jit(solution)/shard_map/all_to_all | solution.py:762
  56.3 13.8 %collective-permute-start.4 = (bf16[960,128]{1,0:T(8,128)(2,1)S(1)}, bf16[960,128]{1,0:T(8,128)(2,1)S(1)}, u32[]{:S(2)}, u32[]{:S(2)}) collective-permute-start(bf16[960,128]{1,0:T(8,128)(2,1)S(1)} %get-tuple-element.37), channel_id=1, source_target_pairs={{0,16},{1,17},{2,18},{3,19},{4,20},{5,21},{6,22},{7,23},{8,24},{9,... | collective-permute-start | bytes 737288 | tf_op jit(solution)/shard_map/ppermute | solution.py:716
  58.3 12.7 %collective-permute-start.5 = (bf16[960,128]{1,0:T(8,128)(2,1)S(1)}, bf16[960,128]{1,0:T(8,128)(2,1)S(1)}, u32[]{:S(2)}, u32[]{:S(2)}) collective-permute-start(bf16[960,128]{1,0:T(8,128)(2,1)S(1)} %get-tuple-element.38), channel_id=1, source_target_pairs={{0,24},{1,25},{2,26},{3,27},{4,28},{5,29},{6,30},{7,31},{8,16},{9,... | collective-permute-start | bytes 737288 | tf_op jit(solution)/shard_map/ppermute | solution.py:716
  59.3 14.0 %collective-permute-start.6 = (bf16[2,64,1024]{2,1,0:T(8,128)(2,1)S(1)}, bf16[2,64,1024]{2,1,0:T(8,128)(2,1)S(1)}, u32[]{:S(2)}, u32[]{:S(2)}) collective-permute-start(bf16[2,64,1024]{2,1,0:T(8,128)(2,1)S(1)} %get-tuple-element.43), channel_id=1, source_target_pairs={{0,2},{1,3},{2,0},{3,1},{4,6},{5,7},{6,4},{7,5},{8,10},{9,11},{10,... | collective-permute-start | bytes 786440 | tf_op jit(solution)/shard_map/ppermute | solution.py:716
  61.3 17.8 %collective-permute-start.7 = (bf16[2,64,1024]{2,1,0:T(8,128)(2,1)S(1)}, bf16[2,64,1024]{2,1,0:T(8,128)(2,1)S(1)}, u32[]{:S(2)}, u32[]{:S(2)}) collective-permute-start(bf16[2,64,1024]{2,1,0:T(8,128)(2,1)S(1)} %get-tuple-element.44), channel_id=1, source_target_pairs={{0,4},{1,5},{2,6},{3,7},{4,0},{5,1},{6,2},{7,3},{8,12},{9,13},{10,... | collective-permute-start | bytes 786440 | tf_op jit(solution)/shard_map/ppermute | solution.py:716
  62.8 22.3 %collective-permute-start.8 = (bf16[2,64,1024]{2,1,0:T(8,128)(2,1)S(1)}, bf16[2,64,1024]{2,1,0:T(8,128)(2,1)S(1)}, u32[]{:S(2)}, u32[]{:S(2)}) collective-permute-start(bf16[2,64,1024]{2,1,0:T(8,128)(2,1)S(1)} %get-tuple-element.45), channel_id=1, source_target_pairs={{0,6},{1,7},{2,4},{3,5},{4,2},{5,3},{6,0},{7,1},{8,14},{9,15},{10,... | collective-permute-start | bytes 786440 | tf_op jit(solution)/shard_map/ppermute | solution.py:716
  85.6 5.7 %collective-permute-start.12 = (bf16[2,64,192]{2,1,0:T(8,128)(2,1)S(1)}, bf16[2,64,192]{2,1,0:T(8,128)(2,1)S(1)}, u32[]{:S(2)}, u32[]{:S(2)}) collective-permute-start(bf16[2,64,192]{2,1,0:T(8,128)(2,1)S(1)} %get-tuple-element.49), channel_id=1, source_target_pairs={{0,6},{1,7},{2,4},{3,5},{4,2},{5,3},{6,0},{7,1},{8,14},{9,15},{10,... | collective-permute-start | bytes 147464 | tf_op jit(solution)/shard_map/ppermute | solution.py:716
  86.0 5.3 %collective-permute-start.11 = (bf16[2,64,192]{2,1,0:T(8,128)(2,1)S(1)}, bf16[2,64,192]{2,1,0:T(8,128)(2,1)S(1)}, u32[]{:S(2)}, u32[]{:S(2)}) collective-permute-start(bf16[2,64,192]{2,1,0:T(8,128)(2,1)S(1)} %get-tuple-element.48), channel_id=1, source_target_pairs={{0,4},{1,5},{2,6},{3,7},{4,0},{5,1},{6,2},{7,3},{8,12},{9,13},{10,... | collective-permute-start | bytes 147464 | tf_op jit(solution)/shard_map/ppermute | solution.py:716
  87.6 4.3 %collective-permute-start.10 = (bf16[2,64,192]{2,1,0:T(8,128)(2,1)S(1)}, bf16[2,64,192]{2,1,0:T(8,128)(2,1)S(1)}, u32[]{:S(2)}, u32[]{:S(2)}) collective-permute-start(bf16[2,64,192]{2,1,0:T(8,128)(2,1)S(1)} %get-tuple-element.47), channel_id=1, source_target_pairs={{0,2},{1,3},{2,0},{3,1},{4,6},{5,7},{6,4},{7,5},{8,10},{9,11},{10,... | collective-permute-start | bytes 147464 | tf_op jit(solution)/shard_map/ppermute | solution.py:716
  89.1 10.9 %collective-permute-start.9 = (bf16[2,64,1024]{2,1,0:T(8,128)(2,1)S(1)}, bf16[2,64,1024]{2,1,0:T(8,128)(2,1)S(1)}, u32[]{:S(2)}, u32[]{:S(2)}) collective-permute-start(bf16[2,64,1024]{2,1,0:T(8,128)(2,1)S(1)} %pad_maximum_fusion.6), channel_id=1, source_target_pairs={{0,4},{1,5},{2,6},{3,7},{4,0},{5,1},{6,2},{7,3},{8,12},{9,13},{10,... | collective-permute-start | bytes 786440 | tf_op jit(solution)/shard_map/ppermute | solution.py:716
  89.6 8.8 %collective-permute-start.15 = (bf16[2,192,128]{2,1,0:T(8,128)(2,1)S(1)}, bf16[2,192,128]{2,1,0:T(8,128)(2,1)S(1)}, u32[]{:S(2)}, u32[]{:S(2)}) collective-permute-start(bf16[2,192,128]{2,1,0:T(8,128)(2,1)S(1)} %get-tuple-element.54), channel_id=1, source_target_pairs={{0,4},{1,5},{2,6},{3,7},{4,0},{5,1},{6,2},{7,3},{8,12},{9,13},{10,... | collective-permute-start | bytes 294920 | tf_op jit(solution)/shard_map/ppermute | solution.py:716
  92.0 6.4 %collective-permute-start.13 = (bf16[64,192]{1,0:T(8,128)(2,1)S(1)}, bf16[64,192]{1,0:T(8,128)(2,1)S(1)}, u32[]{:S(2)}, u32[]{:S(2)}) collective-permute-start(bf16[64,192]{1,0:T(8,128)(2,1)S(1)} %fusion.3), channel_id=1, source_target_pairs={{0,1},{1,0},{2,3},{3,2},{4,5},{5,4},{6,7},{7,6},{8,9},{9,8},{10,11... | collective-permute-start | bytes 73736 | tf_op jit(solution)/shard_map/ppermute | solution.py:716
  98.4 22.5 %copy-start.12 = (bf16[64,192]{1,0:T(8,128)(2,1)}, bf16[64,192]{1,0:T(8,128)(2,1)S(1)}, u32[]{:S(2)}) copy-start(bf16[64,192]{1,0:T(8,128)(2,1)S(1)} %fusion.2.own_rank) | copy-start | bytes 73732
  98.5 4.6 %collective-permute-start.14 = (bf16[64,128]{1,0:T(8,128)(2,1)S(1)}, bf16[64,128]{1,0:T(8,128)(2,1)S(1)}, u32[]{:S(2)}, u32[]{:S(2)}) collective-permute-start(bf16[64,128]{1,0:T(8,128)(2,1)S(1)} %get-tuple-element.75), channel_id=1, source_target_pairs={{0,8},{1,9},{2,10},{3,11},{4,12},{5,13},{6,14},{7,15},{8,0},{9,1},... | collective-permute-start | bytes 49160 | tf_op jit(solution)/shard_map/ppermute | solution.py:716
  103.2 17.7 %collective-permute-start.16 = (bf16[2,2,64,1024]{3,2,1,0:T(8,128)(2,1)S(1)}, bf16[2,2,64,1024]{3,2,1,0:T(8,128)(2,1)S(1)}, u32[]{:S(2)}, u32[]{:S(2)}) collective-permute-start(bf16[2,2,64,1024]{3,2,1,0:T(8,128)(2,1)S(1)} %pad_maximum_fusion.4), channel_id=1, source_target_pairs={{0,2},{1,3},{2,0},{3,1},{4,6},{5,7},{6,4},{7,5},{8,10},{9,11},{10,... | collective-permute-start | bytes 1572872 | tf_op jit(solution)/shard_map/ppermute | solution.py:716
  105.8 14.4 %collective-permute-start.20 = (bf16[2,384,128]{2,1,0:T(8,128)(2,1)S(1)}, bf16[2,384,128]{2,1,0:T(8,128)(2,1)S(1)}, u32[]{:S(2)}, u32[]{:S(2)}) collective-permute-start(bf16[2,384,128]{2,1,0:T(8,128)(2,1)S(1)} %get-tuple-element.58), channel_id=1, source_target_pairs={{0,8},{1,9},{2,10},{3,11},{4,12},{5,13},{6,14},{7,15},{8,0},{9,1},... | collective-permute-start | bytes 589832 | tf_op jit(solution)/shard_map/ppermute | solution.py:716
  107.4 13.4 %collective-permute-start.21 = (bf16[2,2,192,128]{3,2,1,0:T(8,128)(2,1)S(1)}, bf16[2,2,192,128]{3,2,1,0:T(8,128)(2,1)S(1)}, u32[]{:S(2)}, u32[]{:S(2)}) collective-permute-start(bf16[2,2,192,128]{3,2,1,0:T(8,128)(2,1)S(1)} %pad_maximum_fusion.12), channel_id=1, source_target_pairs={{0,2},{1,3},{2,0},{3,1},{4,6},{5,7},{6,4},{7,5},{8,10},{9,11},{10,... | collective-permute-start | bytes 589832 | tf_op jit(solution)/shard_map/ppermute | solution.py:716
  107.9 4.9 %collective-permute-start.19 = (bf16[2,64,128]{2,1,0:T(8,128)(2,1)S(1)}, bf16[2,64,128]{2,1,0:T(8,128)(2,1)S(1)}, u32[]{:S(2)}, u32[]{:S(2)}) collective-permute-start(bf16[2,64,128]{2,1,0:T(8,128)(2,1)S(1)} %pad_maximum_fusion.15), channel_id=1, source_target_pairs={{0,6},{1,7},{2,4},{3,5},{4,2},{5,3},{6,0},{7,1},{8,14},{9,15},{10,... | collective-permute-start | bytes 98312 | tf_op jit(solution)/shard_map/ppermute | solution.py:716
  109.9 5.8 %collective-permute-start.18 = (bf16[2,64,128]{2,1,0:T(8,128)(2,1)S(1)}, bf16[2,64,128]{2,1,0:T(8,128)(2,1)S(1)}, u32[]{:S(2)}, u32[]{:S(2)}) collective-permute-start(bf16[2,64,128]{2,1,0:T(8,128)(2,1)S(1)} %pad_maximum_fusion.15), channel_id=1, source_target_pairs={{0,4},{1,5},{2,6},{3,7},{4,0},{5,1},{6,2},{7,3},{8,12},{9,13},{10,... | collective-permute-start | bytes 98312 | tf_op jit(solution)/shard_map/ppermute | solution.py:716
  112.8 7.3 %collective-permute-start.17 = (bf16[2,64,128]{2,1,0:T(8,128)(2,1)S(1)}, bf16[2,64,128]{2,1,0:T(8,128)(2,1)S(1)}, u32[]{:S(2)}, u32[]{:S(2)}) collective-permute-start(bf16[2,64,128]{2,1,0:T(8,128)(2,1)S(1)} %pad_maximum_fusion.15), channel_id=1, source_target_pairs={{0,2},{1,3},{2,0},{3,1},{4,6},{5,7},{6,4},{7,5},{8,10},{9,11},{10,... | collective-permute-start | bytes 98312 | tf_op jit(solution)/shard_map/ppermute | solution.py:716
  120.9 2.5 %copy-start.11 = (bf16[2,2,2,192,128]{4,3,2,1,0:T(8,128)(2,1)}, bf16[2,2,2,192,128]{4,3,2,1,0:T(8,128)(2,1)S(1)}, u32[]{:S(2)}) copy-start(bf16[2,2,2,192,128]{4,3,2,1,0:T(8,128)(2,1)S(1)} %copy.10) | copy-start | bytes 1179652
  121.1 18.7 %copy-start.5 = (bf16[2,2,2,64,1024]{4,3,2,1,0:T(8,128)(2,1)}, bf16[2,2,2,64,1024]{4,3,2,1,0:T(8,128)(2,1)S(1)}, u32[]{:S(2)}) copy-start(bf16[2,2,2,64,1024]{4,3,2,1,0:T(8,128)(2,1)S(1)} %copy.9) | copy-start | bytes 3145732
  121.1 18.7 %collective-permute-start.22 = (bf16[4,2,64,1024]{3,2,1,0:T(8,128)(2,1)S(1)}, bf16[4,2,64,1024]{3,2,1,0:T(8,128)(2,1)S(1)}, u32[]{:S(2)}, u32[]{:S(2)}) collective-permute-start(bf16[4,2,64,1024]{3,2,1,0:T(8,128)(2,1)S(1)} %bitcast.39), channel_id=1, source_target_pairs={{0,1},{1,0},{2,3},{3,2},{4,5},{5,4},{6,7},{7,6},{8,9},{9,8},{10,11... | collective-permute-start | bytes 3145736 | tf_op jit(solution)/shard_map/ppermute | solution.py:716
  121.2 5.4 %collective-permute-start.25 = (bf16[384,128]{1,0:T(8,128)(2,1)S(1)}, bf16[384,128]{1,0:T(8,128)(2,1)S(1)}, u32[]{:S(2)}, u32[]{:S(2)}) collective-permute-start(bf16[384,128]{1,0:T(8,128)(2,1)S(1)} %get-tuple-element.59), channel_id=1, source_target_pairs={{0,16},{1,17},{2,18},{3,19},{4,20},{5,21},{6,22},{7,23},{8,24},{9,... | collective-permute-start | bytes 294920 | tf_op jit(solution)/shard_map/ppermute | solution.py:716
  123.3 6.7 %collective-permute-start.23 = (bf16[4,2,64,128]{3,2,1,0:T(8,128)(2,1)S(1)}, bf16[4,2,64,128]{3,2,1,0:T(8,128)(2,1)S(1)}, u32[]{:S(2)}, u32[]{:S(2)}) collective-permute-start(bf16[4,2,64,128]{3,2,1,0:T(8,128)(2,1)S(1)} %pad_maximum_fusion.14), channel_id=1, source_target_pairs={{0,1},{1,0},{2,3},{3,2},{4,5},{5,4},{6,7},{7,6},{8,9},{9,8},{10,11... | collective-permute-start | bytes 393224 | tf_op jit(solution)/shard_map/ppermute | solution.py:716
  123.4 15.6 %collective-permute-start.24 = (bf16[4,2,192,128]{3,2,1,0:T(8,128)(2,1)S(1)}, bf16[4,2,192,128]{3,2,1,0:T(8,128)(2,1)S(1)}, u32[]{:S(2)}, u32[]{:S(2)}) collective-permute-start(bf16[4,2,192,128]{3,2,1,0:T(8,128)(2,1)S(1)} %bitcast.46), channel_id=1, source_target_pairs={{0,1},{1,0},{2,3},{3,2},{4,5},{5,4},{6,7},{7,6},{8,9},{9,8},{10,11... | collective-permute-start | bytes 1179656 | tf_op jit(solution)/shard_map/ppermute | solution.py:716
  126.7 8.8 %collective-permute-start.28 = (bf16[2,384,128]{2,1,0:T(8,128)(2,1)S(1)}, bf16[2,384,128]{2,1,0:T(8,128)(2,1)S(1)}, u32[]{:S(2)}, u32[]{:S(2)}) collective-permute-start(bf16[2,384,128]{2,1,0:T(8,128)(2,1)S(1)} %get-tuple-element.73), channel_id=1, source_target_pairs={{0,6},{1,7},{2,4},{3,5},{4,2},{5,3},{6,0},{7,1},{8,14},{9,15},{10,... | collective-permute-start | bytes 589832 | tf_op jit(solution)/shard_map/ppermute | solution.py:716
  129.2 9.6 %collective-permute-start.27 = (bf16[2,384,128]{2,1,0:T(8,128)(2,1)S(1)}, bf16[2,384,128]{2,1,0:T(8,128)(2,1)S(1)}, u32[]{:S(2)}, u32[]{:S(2)}) collective-permute-start(bf16[2,384,128]{2,1,0:T(8,128)(2,1)S(1)} %get-tuple-element.73), channel_id=1, source_target_pairs={{0,4},{1,5},{2,6},{3,7},{4,0},{5,1},{6,2},{7,3},{8,12},{9,13},{10,... | collective-permute-start | bytes 589832 | tf_op jit(solution)/shard_map/ppermute | solution.py:716
  130.0 8.8 %collective-permute-start.26 = (bf16[2,384,128]{2,1,0:T(8,128)(2,1)S(1)}, bf16[2,384,128]{2,1,0:T(8,128)(2,1)S(1)}, u32[]{:S(2)}, u32[]{:S(2)}) collective-permute-start(bf16[2,384,128]{2,1,0:T(8,128)(2,1)S(1)} %get-tuple-element.73), channel_id=1, source_target_pairs={{0,2},{1,3},{2,0},{3,1},{4,6},{5,7},{6,4},{7,5},{8,10},{9,11},{10,... | collective-permute-start | bytes 589832 | tf_op jit(solution)/shard_map/ppermute | solution.py:716
  138.9 12.7 %copy-start.4 = (bf16[4,2,384,128]{3,2,1,0:T(8,128)(2,1)}, bf16[4,2,384,128]{3,2,1,0:T(8,128)(2,1)S(1)}, u32[]{:S(2)}) copy-start(bf16[4,2,384,128]{3,2,1,0:T(8,128)(2,1)S(1)} %pad_maximum_fusion.1.same) | copy-start | bytes 2359300
  138.9 12.7 %collective-permute-start.29 = (bf16[4,2,384,128]{3,2,1,0:T(8,128)(2,1)S(1)}, bf16[4,2,384,128]{3,2,1,0:T(8,128)(2,1)S(1)}, u32[]{:S(2)}, u32[]{:S(2)}) collective-permute-start(bf16[4,2,384,128]{3,2,1,0:T(8,128)(2,1)S(1)} %pad_maximum_fusion.1.same), channel_id=1, source_target_pairs={{0,1},{1,0},{2,3},{3,2},{4,5},{5,4},{6,7},{7,6},{8,9},{9,8},{10,11... | collective-permute-start | bytes 2359304 | tf_op jit(solution)/shard_map/ppermute | solution.py:716
  139.0 0.8 copy-start.16
  139.9 1.0 copy-start.15
  151.6 0.9 copy-start.6

commit v7 on v6

--- a/solution.py
+++ b/solution.py
@@ -468,7 +468,7 @@
             pltpu.VMEM((depth, 128), jnp.float32),
         ],
         compiler_params=pltpu.CompilerParams(vmem_limit_bytes=16 << 20),
-        cost_estimate=pl.CostEstimate(flops=0, bytes_accessed=16 << 20, transcendentals=0),
+        cost_estimate=pl.CostEstimate(flops=0, bytes_accessed=96 << 20, transcendentals=0),
     )(here, owner, *arrived)
 
 
@@ -665,9 +665,7 @@
     )(query_base, base[0], base[1], base[0], base[1], own_rank, all_rank, *ups, cosines, sines)
 
 
-def widen_kernel(attended_rows, same, other, out_delta, down_out, up_out, attended, sem):
-    fetch = pltpu.make_async_copy(attended_rows, attended, sem)
-    fetch.start()
+def widen_kernel(attended, same, other, out_delta, down_out, up_out):
     plane = lax.axis_index("groups")
     seat = lax.rem(lax.axis_index("ctx"), PIECES)
     for apart in range(PIECES):
@@ -682,7 +680,6 @@
             first = pl.multiple_of(place * UP_OUT_ROWS, UP_OUT_ROWS)
             up_out[pl.ds(first, UP_OUT_ROWS), :] = piece[DOWN_OUT_ROWS:]
     dot = partial(jnp.dot, preferred_element_type=jnp.float32)
-    fetch.wait()
     rank = dot(attended[...], down_out[...].astype(jnp.bfloat16))[:, :ADAPTER_RANK]
     rank = rank.astype(jnp.bfloat16)
     blocks = D // 128
@@ -699,15 +696,13 @@
     return pl.pallas_call(
         widen_kernel,
         out_shape=jax.ShapeDtypeStruct((attended.shape[0], D), jnp.bfloat16),
-        in_specs=[pl.BlockSpec(memory_space=pl.ANY)] + [pl.BlockSpec(memory_space=pltpu.VMEM)] * 2,
+        in_specs=[pl.BlockSpec(memory_space=pltpu.VMEM)] * 3,
         out_specs=pl.BlockSpec(memory_space=pltpu.VMEM),
         scratch_shapes=[
             pltpu.VMEM((QH * HEAD_SIZE, 128), jnp.float32),
             pltpu.VMEM((ADAPTER_RANK * D // 128, 128), jnp.float32),
-            pltpu.VMEM(attended.shape, attended.dtype),
-            pltpu.SemaphoreType.DMA,
         ],
-        compiler_params=pltpu.CompilerParams(vmem_limit_bytes=60 << 20),
+        compiler_params=pltpu.CompilerParams(vmem_limit_bytes=32 << 20),
         cost_estimate=pl.CostEstimate(flops=1 << 27, bytes_accessed=4 << 20, transcendentals=0),
     )(attended, same, other)
 
@@ -750,7 +745,7 @@
     even, odd = deal(normed_input, packed)
     sibling = swap(odd, 1)
     base = jnp.concatenate([key_base, value_base], 1)
-    base = jnp.stack([base, swap(base, PIECES)])
+    base = along_x(along_z(jnp.stack([base, swap(base, PIECES)])))
 
     spread = lax.all_to_all(packed, "ctx", 0, 0, axis_index_groups=blocks)
     spread = after(spread, packed_second, sibling, base)
@@ -758,33 +753,33 @@
     arrived = exchange(sent)
     dealt = [after(jnp.stack([even[j], sibling[j]]), sent) for j in range(PIECES // 2)]
     dealt = [swap(block, 2 * j) if j else block for j, block in enumerate(dealt)]
-    packed_second = after(packed_second, arrived[1])
+    packed_second = after(packed_second, sent)
     spread = lax.all_to_all(packed_second, "ctx", 0, 0, axis_index_groups=blocks)
 
     weight, ups = join(stretch_adapter, adapter_owner, arrived)
-    partial_sums = narrow(after(weight, cosines, sines), dealt)
+    partial_sums = narrow(after(weight, spread, cosines, sines), dealt)
     back = [swap(block, 2 * j) if j else block for j, block in enumerate(partial_sums)]
     back = sum(block.astype(jnp.float32) for block in back)
-    own_rank = swap(after(back[1].astype(jnp.bfloat16), spread), 1)
+    own_rank = swap(back[1].astype(jnp.bfloat16), 1)
     own_rank = back[0] + own_rank.astype(jnp.float32)
     own_rank = own_rank.astype(jnp.bfloat16)
-    all_rank = own_rank[:, ADAPTER_RANK:]
-    base = along_z(after(base, *partial_sums))
     ups = along_z(after(ups, *partial_sums))
-    near, far = pick(spread, stretch_adapter, elsewhere, adapter_owner, None)
+    near, far = pick(
+        after(spread, *partial_sums), stretch_adapter, elsewhere, adapter_owner, None
+    )
     far = swap(far, PIECES)
+    base = after(base, *partial_sums)
+    base = (base, swap(base, 1))
+    all_rank = after(own_rank[:, ADAPTER_RANK:], ups)
     all_rank = jnp.stack([all_rank, swap(all_rank, PIECES)])
-    all_rank = after(all_rank, ups)
+    own, across = settle(stretch_adapter, elsewhere, adapter_owner, near, far)
+    all_rank = after(all_rank, across)
     ups = along_x(after(ups, all_rank))
-    base = along_x(after(base, all_rank))
-    own, across = settle(stretch_adapter, elsewhere, adapter_owner, near, far)
+    ends = jnp.stack([own, swap(across, 2 * PIECES)])
     all_rank = jnp.stack([swap(all_rank, apart) if apart else all_rank for apart in (0, 2, 4, 6)])
-    all_rank = after(all_rank, across, ups)
-    base = after(base, all_rank)
-    ends = jnp.stack([own, swap(across, 2 * PIECES)])
+    all_rank = after(all_rank, ups, ends)
+    ends = jnp.stack([swap(ends, apart) if apart else ends for apart in (0, 2, 4, 6)])
     all_rank = jnp.stack([all_rank, swap(all_rank, 1)])
-    ends = jnp.stack([swap(ends, apart) if apart else ends for apart in (0, 2, 4, 6)])
-    base = (base, swap(base, 1))
     ups = (ups, swap(ups, 1))
     ends = (ends, swap(ends, 1))
 

time: 158 us -> 160 us (1.013)
  starting transfers between devices: 43.5 us -> 49 us
  waiting for transfers between devices: 76.7 us -> 73.3 us
  Pallas kernels: 28.2 us -> 25.9 us
  other arithmetic: 4.5 us -> 6.28 us
    ppermute x30, starting transfers between devices: 34.4 us -> 40 us  [swap(): lax.ppermute(block, ('groups', 'ctx'), [(i, i ^ mask) for i in range(4 *...]
    pallas_call x1, Pallas kernels: 5.33 us -> 3 us  [widen(): pl.pallas_call(widen_kernel, out_shape=jax.ShapeDtypeStruct((attended.sha...]
    all_to_all x1, waiting for transfers between devices: 2.19 us -> 0.01 us  [direct_shards(): spread = lax.all_to_all(packed, 'ctx', 0, 0, axis_index_groups=blocks)]
  transfers between devices with their start and end apart: 32 -> 32, of which waited for: 18 -> 17; matrix products, arithmetic and copies ran while one was open for 3% -> 5% of each run, Pallas kernels for 11% -> 10%
where the time goes in v7:
time: 160 us
  waiting for transfers between devices  73.3 us (46%)
  starting transfers between devices  49 us (31%)
  Pallas kernels  25.9 us (16%)
  other arithmetic  6.28 us (4%)
  local copies, waits for them, and re-layouts  4.14 us (3%)
    ppermute x30, waiting for transfers between devices, swap(): lax.ppermute(block, ('groups', 'ctx'), [(i, i ^ mask) for i in range(4 *...  73.3 us
    ppermute x30, starting transfers between devices, swap(): lax.ppermute(block, ('groups', 'ctx'), [(i, i ^ mask) for i in range(4 *...  40 us
    pallas_call x1, Pallas kernels, attend(): pl.pallas_call(attend_kernel, grid=(KEYVALUE_HEADS,), out_shape=jax.Shape...  10.8 us
    pallas_call x2, Pallas kernels, pack_row(): pl.pallas_call(partial(pack_kernel, sections), out_shape=jax.ShapeDtypeSt...  6.68 us
    all_to_all x1, starting transfers between devices, direct_shards(): spread = lax.all_to_all(packed, 'ctx', 0, 0, axis_index_groups=blocks)  5.37 us
    all_to_all x1, starting transfers between devices, direct_shards(): lax.all_to_all(packed_second, 'ctx', 0, 0, axis_index_groups=blocks)  3.62 us
  transfers between devices with their start and end apart: 32, of which 17 were waited for; matrix products, arithmetic and copies ran while one was open for 5% of the time, Pallas kernels for 10%

profile of v7, /device:TPU:0, one launch (start us, length us, event | category | flops | bytes accessed | tf_op | source)
XLA Modules:
  0.0 159.7 jit_solution(3074569823948563930)
XLA Ops:
  0.6 4.0 %shard_map.86.refs_0_ = bf16[8,928,128]{2,1,0:T(8,128)(2,1)} custom-call(bf16[1,2686976]{1,0:T(2,128)(2,1)} %pool.3), custom_call_target="tpu_custom_call" | custom-call | bytes 8388608 | tf_op jit(solution)/shard_map/pallas_call | solution.py:316
  4.7 5.4 %all-to-all-start = ((bf16[8,928,128]{2,1,0:T(8,128)(2,1)}), bf16[8,928,128]{2,1,0:T(8,128)(2,1)}, u32[]{:S(2)}, u32[]{:S(2)}) async-start(bf16[8,928,128]{2,1,0:T(8,128)(2,1)} %shard_map.86.refs_0_), calls=%async_computation | async-start | bytes 3801088 | tf_op jit(solution)/shard_map/all_to_all | solution.py:750
  10.1 3.2 %collective-permute-start = (bf16[64,1024]{1,0:T(8,128)(2,1)S(1)}, bf16[64,1024]{1,0:T(8,128)(2,1)S(1)}, u32[]{:S(2)}, u32[]{:S(2)}) collective-permute-start(bf16[64,1024]{1,0:T(8,128)(2,1)S(1)} %constant_dynamic-update-slice_fusion), channel_id=1, source_target_pairs={{0,8},{1,9},{2,10},{3,11},{4,12},{5,13},{6,14},{7,15},{8,0},{9,1},... | collective-permute-start | bytes 393224 | tf_op jit(solution)/shard_map/ppermute | solution.py:711
  13.4 21.0 %collective-permute-done = bf16[64,1024]{1,0:T(8,128)(2,1)S(1)} collective-permute-done((bf16[64,1024]{1,0:T(8,128)(2,1)S(1)}, bf16[64,1024]{1,0:T(8,128)(2,1)S(1)}, u32[]{:S(2)}, u32[]{:S(2)}) %collective-permute-start) | collective-permute-done | bytes 131104 | tf_op jit(solution)/shard_map/ppermute | solution.py:711
  34.5 5.2 %collective-permute-start.1 = (bf16[2,64,1024]{2,1,0:T(8,128)(2,1)S(1)}, bf16[2,64,1024]{2,1,0:T(8,128)(2,1)S(1)}, u32[]{:S(2)}, u32[]{:S(2)}) collective-permute-start(bf16[2,64,1024]{2,1,0:T(8,128)(2,1)S(1)} %get-tuple-element.73), channel_id=1, source_target_pairs={{0,4},{1,5},{2,6},{3,7},{4,0},{5,1},{6,2},{7,3},{8,12},{9,13},{10,... | collective-permute-start | bytes 786440 | tf_op jit(solution)/shard_map/ppermute | solution.py:711
  39.6 6.1 %collective-permute-done.1 = bf16[2,64,1024]{2,1,0:T(8,128)(2,1)S(1)} collective-permute-done((bf16[2,64,1024]{2,1,0:T(8,128)(2,1)S(1)}, bf16[2,64,1024]{2,1,0:T(8,128)(2,1)S(1)}, u32[]{:S(2)}, u32[]{:S(2)}) %collective-permute-start.1) | collective-permute-done | bytes 262176 | tf_op jit(solution)/shard_map/ppermute | solution.py:711
  45.8 1.5 collective-permute-start.2
  47.4 0.3 shard_map.88
  47.6 0.1 collective-permute-start.4
  47.7 1.6 collective-permute-start.3
  49.3 2.6 %shard_map.87 = bf16[8,384,128]{2,1,0:T(8,128)(2,1)} custom-call(bf16[1,2686976]{1,0:T(2,128)(2,1)} %pool.3, bf16[8,928,128]{2,1,0:T(8,128)(2,1)} %shard_map.86.refs_0_), custom_call_target="tpu_custom_call" | custom-call | bytes 8388608 | tf_op jit(solution)/shard_map/pallas_call | solution.py:316
  51.9 6.9 %collective-permute-done.2 = bf16[2,2,64,1024]{3,2,1,0:T(8,128)(2,1)} collective-permute-done((bf16[2,2,64,1024]{3,2,1,0:T(8,128)(2,1)S(1)}, bf16[2,2,64,1024]{3,2,1,0:T(8,128)(2,1)}, u32[]{:S(2)}, u32[]{:S(2)}) %collective-permute-start.2) | collective-permute-done | bytes 524320 | tf_op jit(solution)/shard_map/ppermute | solution.py:711
  58.9 1.2 pad_maximum_fusion
  60.0 1.1 copy.9
  61.1 2.0 %shard_map.89 = (bf16[960,128]{1,0:T(8,128)(2,1)S(1)}, bf16[960,128]{1,0:T(8,128)(2,1)S(1)}, bf16[960,128]{1,0:T(8,128)(2,1)S(1)}, bf16[960,128]{1,0:T(8,128)(2,1)S(1)}) custom-call(s32[2]{0:T(128)S(1)} %copy-done.3, s32[2]{0:T(128)S(1)} %collective-permute-done.3.there, s32[16]{0:T(128)S(1)} %copy-done.4, bf16[8,928,128]{2,1,0:T(8,128)(2,1)} %all-to-all-done.spread), custom_call_target="tpu_custom_call" | custom-call | bytes 2097152 | tf_op jit(solution)/shard_map/pallas_call | solution.py:363
  63.1 3.6 %all-to-all-start.1 = ((bf16[8,384,128]{2,1,0:T(8,128)(2,1)}), bf16[8,384,128]{2,1,0:T(8,128)(2,1)S(1)}, u32[]{:S(2)}, u32[]{:S(2)}) async-start(bf16[8,384,128]{2,1,0:T(8,128)(2,1)} %shard_map.87), calls=%async_computation.1 | async-start | bytes 1572864 | tf_op jit(solution)/shard_map/all_to_all | solution.py:757
  66.9 0.3 collective-permute-start.5
  67.2 0.8 pad_maximum_fusion.7
  68.0 1.8 %collective-permute-start.6 = (bf16[960,128]{1,0:T(8,128)(2,1)S(1)}, bf16[960,128]{1,0:T(8,128)(2,1)S(1)}, u32[]{:S(2)}, u32[]{:S(2)}) collective-permute-start(bf16[960,128]{1,0:T(8,128)(2,1)S(1)} %get-tuple-element.36), channel_id=1, source_target_pairs={{0,16},{1,17},{2,18},{3,19},{4,20},{5,21},{6,22},{7,23},{8,24},{9,... | collective-permute-start | bytes 737288 | tf_op jit(solution)/shard_map/ppermute | solution.py:711
  69.8 2.3 %collective-permute-start.7 = (bf16[960,128]{1,0:T(8,128)(2,1)S(1)}, bf16[960,128]{1,0:T(8,128)(2,1)S(1)}, u32[]{:S(2)}, u32[]{:S(2)}) collective-permute-start(bf16[960,128]{1,0:T(8,128)(2,1)S(1)} %get-tuple-element.37), channel_id=1, source_target_pairs={{0,24},{1,25},{2,26},{3,27},{4,28},{5,29},{6,30},{7,31},{8,16},{9,... | collective-permute-start | bytes 737288 | tf_op jit(solution)/shard_map/ppermute | solution.py:711
  72.1 2.9 %collective-permute-start.10 = (bf16[2,64,1024]{2,1,0:T(8,128)(2,1)S(1)}, bf16[2,64,1024]{2,1,0:T(8,128)(2,1)S(1)}, u32[]{:S(2)}, u32[]{:S(2)}) collective-permute-start(bf16[2,64,1024]{2,1,0:T(8,128)(2,1)S(1)} %get-tuple-element.45), channel_id=1, source_target_pairs={{0,6},{1,7},{2,4},{3,5},{4,2},{5,3},{6,0},{7,1},{8,14},{9,15},{10,... | collective-permute-start | bytes 786440 | tf_op jit(solution)/shard_map/ppermute | solution.py:711
  75.0 0.6 collective-permute-start.9
  75.6 6.2 %collective-permute-done.5.refs_1_ = bf16[960,128]{1,0:T(8,128)(2,1)S(1)} collective-permute-done((bf16[960,128]{1,0:T(8,128)(2,1)S(1)}, bf16[960,128]{1,0:T(8,128)(2,1)S(1)}, u32[]{:S(2)}, u32[]{:S(2)}) %collective-permute-start.5) | collective-permute-done | bytes 245792 | tf_op jit(solution)/shard_map/ppermute | solution.py:711
  81.8 1.9 %collective-permute-start.8 = (bf16[2,64,1024]{2,1,0:T(8,128)(2,1)}, bf16[2,64,1024]{2,1,0:T(8,128)(2,1)S(1)}, u32[]{:S(2)}, u32[]{:S(2)}) collective-permute-start(bf16[2,64,1024]{2,1,0:T(8,128)(2,1)} %get-tuple-element.43), channel_id=1, source_target_pairs={{0,2},{1,3},{2,0},{3,1},{4,6},{5,7},{6,4},{7,5},{8,10},{9,11},{10,... | collective-permute-start | bytes 786440 | tf_op jit(solution)/shard_map/ppermute | solution.py:711
  83.7 1.9 %fusion = (f32[1024,64]{1,0:T(8,128)S(1)}, f32[1024,64]{1,0:T(8,128)S(1)}, f32[1024,64]{1,0:T(8,128)S(1)}) fusion(f32[64]{0:T(128)S(1)} %multiply_power_fusion, f32[1024]{0:T(1024)S(1)} %iota_convert_fusion), kind=kLoop, calls=%fused_computation.16 | loop fusion | flops 131072 | bytes 790784 | tf_op jit(solution)/shard_map/neg | solution.py:727
  85.6 1.3 pad_maximum_fusion.3
  87.0 6.1 %collective-permute-done.7.refs_3_ = bf16[960,128]{1,0:T(8,128)(2,1)S(1)} collective-permute-done((bf16[960,128]{1,0:T(8,128)(2,1)S(1)}, bf16[960,128]{1,0:T(8,128)(2,1)S(1)}, u32[]{:S(2)}, u32[]{:S(2)}) %collective-permute-start.7) | collective-permute-done | bytes 245792 | tf_op jit(solution)/shard_map/ppermute | solution.py:711
  93.1 1.0 shard_map.90
  94.1 2.0 %collective-permute-done.10.refs_3_ = bf16[2,64,1024]{2,1,0:T(8,128)(2,1)S(1)} collective-permute-done((bf16[2,64,1024]{2,1,0:T(8,128)(2,1)S(1)}, bf16[2,64,1024]{2,1,0:T(8,128)(2,1)S(1)}, u32[]{:S(2)}, u32[]{:S(2)}) %collective-permute-start.10) | collective-permute-done | bytes 262176 | tf_op jit(solution)/shard_map/ppermute | solution.py:711
  96.0 4.2 %collective-permute-done.9.refs_2_ = bf16[2,64,1024]{2,1,0:T(8,128)(2,1)S(1)} collective-permute-done((bf16[2,64,1024]{2,1,0:T(8,128)(2,1)S(1)}, bf16[2,64,1024]{2,1,0:T(8,128)(2,1)S(1)}, u32[]{:S(2)}, u32[]{:S(2)}) %collective-permute-start.9) | collective-permute-done | bytes 262176 | tf_op jit(solution)/shard_map/ppermute | solution.py:711
  100.3 0.4 shard_map.91
  100.7 1.5 collective-permute-start.12
  102.3 0.6 collective-permute-start.13
  102.8 1.5 collective-permute-start.14
  104.3 0.8 collective-permute-done.12
  105.1 1.5 collective-permute-done.13
  106.5 1.5 collective-permute-done.14
  108.1 1.2 shard_map.92
  109.3 0.2 collective-permute-start.18
  109.5 1.6 collective-permute-start.16
  111.0 0.1 collective-permute-start.11
  111.1 0.1 slice.51
  111.2 5.4 %collective-permute-done.16 = bf16[2,192,128]{2,1,0:T(8,128)(2,1)S(1)} collective-permute-done((bf16[2,192,128]{2,1,0:T(8,128)(2,1)S(1)}, bf16[2,192,128]{2,1,0:T(8,128)(2,1)S(1)}, u32[]{:S(2)}, u32[]{:S(2)}) %collective-permute-start.16) | collective-permute-done | bytes 98336 | tf_op jit(solution)/shard_map/ppermute | solution.py:711
  116.6 4.6 %collective-permute-start.17 = (bf16[64,128]{1,0:T(8,128)(2,1)S(1)}, bf16[64,128]{1,0:T(8,128)(2,1)S(1)}, u32[]{:S(2)}, u32[]{:S(2)}) collective-permute-start(bf16[64,128]{1,0:T(8,128)(2,1)S(1)} %slice.51), channel_id=1, source_target_pairs={{0,8},{1,9},{2,10},{3,11},{4,12},{5,13},{6,14},{7,15},{8,0},{9,1},... | collective-permute-start | bytes 49160 | tf_op jit(solution)/shard_map/ppermute | solution.py:711
  121.3 0.5 collective-permute-done.18.far
  121.8 0.6 shard_map.93
  122.4 1.6 collective-permute-start.23
  124.0 0.8 collective-permute-start.22
  124.8 1.3 collective-permute-start.19
  126.1 1.0 collective-permute-done.23
  127.1 1.2 collective-permute-start.21
  128.3 3.1 %collective-permute-done.19 = bf16[2,64,128]{2,1,0:T(8,128)(2,1)S(1)} collective-permute-done((bf16[2,64,128]{2,1,0:T(8,128)(2,1)S(1)}, bf16[2,64,128]{2,1,0:T(8,128)(2,1)S(1)}, u32[]{:S(2)}, u32[]{:S(2)}) %collective-permute-start.19) | collective-permute-done | bytes 32800 | tf_op jit(solution)/shard_map/ppermute | solution.py:711
  131.4 0.7 collective-permute-start.26
  132.1 2.8 %collective-permute-start.28 = (bf16[2,384,128]{2,1,0:T(8,128)(2,1)S(1)}, bf16[2,384,128]{2,1,0:T(8,128)(2,1)S(1)}, u32[]{:S(2)}, u32[]{:S(2)}) collective-permute-start(bf16[2,384,128]{2,1,0:T(8,128)(2,1)S(1)} %get-tuple-element.75), channel_id=1, source_target_pairs={{0,6},{1,7},{2,4},{3,5},{4,2},{5,3},{6,0},{7,1},{8,14},{9,15},{10,... | collective-permute-start | bytes 589832 | tf_op jit(solution)/shard_map/ppermute | solution.py:711
  135.1 3.9 %collective-permute-done.26 = bf16[2,384,128]{2,1,0:T(8,128)(2,1)S(1)} collective-permute-done((bf16[2,384,128]{2,1,0:T(8,128)(2,1)S(1)}, bf16[2,384,128]{2,1,0:T(8,128)(2,1)S(1)}, u32[]{:S(2)}, u32[]{:S(2)}) %collective-permute-start.26) | collective-permute-done | bytes 196640 | tf_op jit(solution)/shard_map/ppermute | solution.py:711
  139.0 0.2 collective-permute-done.27
  139.2 2.9 %collective-permute-done.28 = bf16[2,384,128]{2,1,0:T(8,128)(2,1)S(1)} collective-permute-done((bf16[2,384,128]{2,1,0:T(8,128)(2,1)S(1)}, bf16[2,384,128]{2,1,0:T(8,128)(2,1)S(1)}, u32[]{:S(2)}, u32[]{:S(2)}) %collective-permute-start.28) | collective-permute-done | bytes 196640 | tf_op jit(solution)/shard_map/ppermute | solution.py:711
  142.1 0.1 pad_maximum_fusion.1.same
  142.3 0.7 pad_maximum_fusion.11.all_rank
  143.0 0.8 copy-done.10
  143.8 1.0 copy-done.9
  144.8 10.8 %shard_map.94.attended = bf16[64,4096]{1,0:T(8,128)(2,1)} custom-call(bf16[64,4096]{1,0:T(8,128)(2,1)} %query_block.1, bf16[4,2,64,1024]{3,2,1,0:T(8,128)(2,1)} %bitcast.40, bf16[4,2,64,1024]{3,2,1,0:T(8,128)(2,1)} %copy-done.9, bf16[4,2,64,1024]{3,2,1,0:T(8,128)(2,1)} %bitcast.41, bf16[4,2,64,1024]{3,2,1,0:T(8,128)(2,1)} %copy-done.9, ...), custom_call_target="tpu_custom_call" | custom-call | flops 12884901888 | bytes 10485760 | tf_op jit(solution)/shard_map/pallas_call | solution.py:635
  155.6 1.0 copy-done.2
  156.7 3.0 %shard_map.95 = bf16[64,8192]{1,0:T(8,128)(2,1)} custom-call(bf16[64,4096]{1,0:T(8,128)(2,1)S(1)} %copy-done.2, bf16[4,2,384,128]{3,2,1,0:T(8,128)(2,1)S(1)} %pad_maximum_fusion.1.same, bf16[4,2,384,128]{3,2,1,0:T(8,128)(2,1)S(1)} %collective-permute-done.29.other), custom_call_target="tpu_custom_call" | custom-call | flops 134217728 | bytes 4194304 | tf_op jit(solution)/shard_map/pallas_call | solution.py:696
  (58 shorter events, 0.7 us)
Async XLA Ops:
  4.7 5.4 %copy-start.7 = (bf16[64,512]{1,0:T(8,128)(2,1)S(1)}, bf16[64,512]{1,0:T(8,128)(2,1)}, u32[]{:S(2)}) copy-start(bf16[64,512]{1,0:T(8,128)(2,1)} %param.9) | copy-start | bytes 196612
  4.7 5.4 %copy-start.8 = (bf16[64,512]{1,0:T(8,128)(2,1)S(1)}, bf16[64,512]{1,0:T(8,128)(2,1)}, u32[]{:S(2)}) copy-start(bf16[64,512]{1,0:T(8,128)(2,1)} %param.10) | copy-start | bytes 196612
  4.7 42.7 %copy-start.1 = (bf16[64,8192]{1,0:T(8,128)(2,1)S(1)}, bf16[64,8192]{1,0:T(8,128)(2,1)}, u32[]{:S(2)}) copy-start(bf16[64,8192]{1,0:T(8,128)(2,1)} %rows.1) | copy-start | bytes 3145732
  4.7 56.4 %all-to-all-start = ((bf16[8,928,128]{2,1,0:T(8,128)(2,1)}), bf16[8,928,128]{2,1,0:T(8,128)(2,1)}, u32[]{:S(2)}, u32[]{:S(2)}) async-start(bf16[8,928,128]{2,1,0:T(8,128)(2,1)} %shard_map.86.refs_0_), calls=%async_computation | async-start | bytes 3801088 | tf_op jit(solution)/shard_map/all_to_all | solution.py:750
  10.1 37.3 %copy-start = (bf16[8,928,128]{2,1,0:T(8,128)(2,1)S(1)}, bf16[8,928,128]{2,1,0:T(8,128)(2,1)}, u32[]{:S(2)}) copy-start(bf16[8,928,128]{2,1,0:T(8,128)(2,1)} %shard_map.86.refs_0_) | copy-start | bytes 5701636
  10.1 24.3 %collective-permute-start = (bf16[64,1024]{1,0:T(8,128)(2,1)S(1)}, bf16[64,1024]{1,0:T(8,128)(2,1)S(1)}, u32[]{:S(2)}, u32[]{:S(2)}) collective-permute-start(bf16[64,1024]{1,0:T(8,128)(2,1)S(1)} %constant_dynamic-update-slice_fusion), channel_id=1, source_target_pairs={{0,8},{1,9},{2,10},{3,11},{4,12},{5,13},{6,14},{7,15},{8,0},{9,1},... | collective-permute-start | bytes 393224 | tf_op jit(solution)/shard_map/ppermute | solution.py:711
  34.5 11.3 %collective-permute-start.1 = (bf16[2,64,1024]{2,1,0:T(8,128)(2,1)S(1)}, bf16[2,64,1024]{2,1,0:T(8,128)(2,1)S(1)}, u32[]{:S(2)}, u32[]{:S(2)}) collective-permute-start(bf16[2,64,1024]{2,1,0:T(8,128)(2,1)S(1)} %get-tuple-element.73), channel_id=1, source_target_pairs={{0,4},{1,5},{2,6},{3,7},{4,0},{5,1},{6,2},{7,3},{8,12},{9,13},{10,... | collective-permute-start | bytes 786440 | tf_op jit(solution)/shard_map/ppermute | solution.py:711
  45.7 2.0 %copy-start.3 = (s32[2]{0:T(128)S(1)}, s32[2]{0:T(128)}, u32[]{:S(2)}) copy-start(s32[2]{0:T(128)} %here.7) | copy-start | bytes 28
  45.8 13.1 %collective-permute-start.2 = (bf16[2,2,64,1024]{3,2,1,0:T(8,128)(2,1)S(1)}, bf16[2,2,64,1024]{3,2,1,0:T(8,128)(2,1)}, u32[]{:S(2)}, u32[]{:S(2)}) collective-permute-start(bf16[2,2,64,1024]{3,2,1,0:T(8,128)(2,1)S(1)} %get-tuple-element.71), channel_id=1, source_target_pairs={{0,2},{1,3},{2,0},{3,1},{4,6},{5,7},{6,4},{7,5},{8,10},{9,11},{10,... | collective-permute-start | bytes 1572872 | tf_op jit(solution)/shard_map/ppermute | solution.py:711
  47.6 13.5 %collective-permute-start.4 = (bf16[4,64,1024]{2,1,0:T(8,128)(2,1)S(1)}, bf16[4,64,1024]{2,1,0:T(8,128)(2,1)S(1)}, u32[]{:S(2)}, u32[]{:S(2)}) collective-permute-start(bf16[4,64,1024]{2,1,0:T(8,128)(2,1)S(1)} %get-tuple-element.32), channel_id=1, source_target_pairs={{0,1},{1,0},{2,3},{3,2},{4,5},{5,4},{6,7},{7,6},{8,9},{9,8},{10,11... | collective-permute-start | bytes 1572872 | tf_op jit(solution)/shard_map/ppermute | solution.py:711
  47.7 13.4 %collective-permute-start.3 = (s32[2]{0:T(128)S(1)}, s32[2]{0:T(128)S(1)}, u32[]{:S(2)}, u32[]{:S(2)}) collective-permute-start(s32[2]{0:T(128)S(1)} %copy-done.3), channel_id=1, source_target_pairs={{0,16},{1,17},{2,18},{3,19},{4,20},{5,21},{6,22},{7,23},{8,24},{9,... | collective-permute-start | bytes 32 | tf_op jit(solution)/shard_map/ppermute | solution.py:711
  58.9 2.3 %copy-start.4 = (s32[16]{0:T(128)S(1)}, s32[16]{0:T(128)}, u32[]{:S(2)}) copy-start(s32[16]{0:T(128)} %owner.7) | copy-start | bytes 196
  63.1 30.9 %all-to-all-start.1 = ((bf16[8,384,128]{2,1,0:T(8,128)(2,1)}), bf16[8,384,128]{2,1,0:T(8,128)(2,1)S(1)}, u32[]{:S(2)}, u32[]{:S(2)}) async-start(bf16[8,384,128]{2,1,0:T(8,128)(2,1)} %shard_map.87), calls=%async_computation.1 | async-start | bytes 1572864 | tf_op jit(solution)/shard_map/all_to_all | solution.py:757
  66.9 15.0 %collective-permute-start.5 = (bf16[960,128]{1,0:T(8,128)(2,1)S(1)}, bf16[960,128]{1,0:T(8,128)(2,1)S(1)}, u32[]{:S(2)}, u32[]{:S(2)}) collective-permute-start(bf16[960,128]{1,0:T(8,128)(2,1)S(1)} %get-tuple-element.35), channel_id=1, source_target_pairs={{0,8},{1,9},{2,10},{3,11},{4,12},{5,13},{6,14},{7,15},{8,0},{9,1},... | collective-permute-start | bytes 737288 | tf_op jit(solution)/shard_map/ppermute | solution.py:711
  68.0 19.0 %collective-permute-start.6 = (bf16[960,128]{1,0:T(8,128)(2,1)S(1)}, bf16[960,128]{1,0:T(8,128)(2,1)S(1)}, u32[]{:S(2)}, u32[]{:S(2)}) collective-permute-start(bf16[960,128]{1,0:T(8,128)(2,1)S(1)} %get-tuple-element.36), channel_id=1, source_target_pairs={{0,16},{1,17},{2,18},{3,19},{4,20},{5,21},{6,22},{7,23},{8,24},{9,... | collective-permute-start | bytes 737288 | tf_op jit(solution)/shard_map/ppermute | solution.py:711
  69.8 23.3 %collective-permute-start.7 = (bf16[960,128]{1,0:T(8,128)(2,1)S(1)}, bf16[960,128]{1,0:T(8,128)(2,1)S(1)}, u32[]{:S(2)}, u32[]{:S(2)}) collective-permute-start(bf16[960,128]{1,0:T(8,128)(2,1)S(1)} %get-tuple-element.37), channel_id=1, source_target_pairs={{0,24},{1,25},{2,26},{3,27},{4,28},{5,29},{6,30},{7,31},{8,16},{9,... | collective-permute-start | bytes 737288 | tf_op jit(solution)/shard_map/ppermute | solution.py:711
  72.1 23.9 %collective-permute-start.10 = (bf16[2,64,1024]{2,1,0:T(8,128)(2,1)S(1)}, bf16[2,64,1024]{2,1,0:T(8,128)(2,1)S(1)}, u32[]{:S(2)}, u32[]{:S(2)}) collective-permute-start(bf16[2,64,1024]{2,1,0:T(8,128)(2,1)S(1)} %get-tuple-element.45), channel_id=1, source_target_pairs={{0,6},{1,7},{2,4},{3,5},{4,2},{5,3},{6,0},{7,1},{8,14},{9,15},{10,... | collective-permute-start | bytes 786440 | tf_op jit(solution)/shard_map/ppermute | solution.py:711
  75.0 25.2 %collective-permute-start.9 = (bf16[2,64,1024]{2,1,0:T(8,128)(2,1)S(1)}, bf16[2,64,1024]{2,1,0:T(8,128)(2,1)S(1)}, u32[]{:S(2)}, u32[]{:S(2)}) collective-permute-start(bf16[2,64,1024]{2,1,0:T(8,128)(2,1)S(1)} %get-tuple-element.44), channel_id=1, source_target_pairs={{0,4},{1,5},{2,6},{3,7},{4,0},{5,1},{6,2},{7,3},{8,12},{9,13},{10,... | collective-permute-start | bytes 786440 | tf_op jit(solution)/shard_map/ppermute | solution.py:711
  81.8 18.4 %collective-permute-start.8 = (bf16[2,64,1024]{2,1,0:T(8,128)(2,1)}, bf16[2,64,1024]{2,1,0:T(8,128)(2,1)S(1)}, u32[]{:S(2)}, u32[]{:S(2)}) collective-permute-start(bf16[2,64,1024]{2,1,0:T(8,128)(2,1)} %get-tuple-element.43), channel_id=1, source_target_pairs={{0,2},{1,3},{2,0},{3,1},{4,6},{5,7},{6,4},{7,5},{8,10},{9,11},{10,... | collective-permute-start | bytes 786440 | tf_op jit(solution)/shard_map/ppermute | solution.py:711
  100.7 4.3 %collective-permute-start.12 = (bf16[2,64,192]{2,1,0:T(8,128)(2,1)S(1)}, bf16[2,64,192]{2,1,0:T(8,128)(2,1)S(1)}, u32[]{:S(2)}, u32[]{:S(2)}) collective-permute-start(bf16[2,64,192]{2,1,0:T(8,128)(2,1)S(1)} %get-tuple-element.47), channel_id=1, source_target_pairs={{0,2},{1,3},{2,0},{3,1},{4,6},{5,7},{6,4},{7,5},{8,10},{9,11},{10,... | collective-permute-start | bytes 147464 | tf_op jit(solution)/shard_map/ppermute | solution.py:711
  102.3 4.3 %collective-permute-start.13 = (bf16[2,64,192]{2,1,0:T(8,128)(2,1)S(1)}, bf16[2,64,192]{2,1,0:T(8,128)(2,1)S(1)}, u32[]{:S(2)}, u32[]{:S(2)}) collective-permute-start(bf16[2,64,192]{2,1,0:T(8,128)(2,1)S(1)} %get-tuple-element.48), channel_id=1, source_target_pairs={{0,4},{1,5},{2,6},{3,7},{4,0},{5,1},{6,2},{7,3},{8,12},{9,13},{10,... | collective-permute-start | bytes 147464 | tf_op jit(solution)/shard_map/ppermute | solution.py:711
  102.8 5.2 %collective-permute-start.14 = (bf16[2,64,192]{2,1,0:T(8,128)(2,1)S(1)}, bf16[2,64,192]{2,1,0:T(8,128)(2,1)S(1)}, u32[]{:S(2)}, u32[]{:S(2)}) collective-permute-start(bf16[2,64,192]{2,1,0:T(8,128)(2,1)S(1)} %get-tuple-element.49), channel_id=1, source_target_pairs={{0,6},{1,7},{2,4},{3,5},{4,2},{5,3},{6,0},{7,1},{8,14},{9,15},{10,... | collective-permute-start | bytes 147464 | tf_op jit(solution)/shard_map/ppermute | solution.py:711
  108.0 3.1 %collective-permute-start.15 = (bf16[64,192]{1,0:T(8,128)(2,1)S(1)}, bf16[64,192]{1,0:T(8,128)(2,1)S(1)}, u32[]{:S(2)}, u32[]{:S(2)}) collective-permute-start(bf16[64,192]{1,0:T(8,128)(2,1)S(1)} %fusion.3), channel_id=1, source_target_pairs={{0,1},{1,0},{2,3},{3,2},{4,5},{5,4},{6,7},{7,6},{8,9},{9,8},{10,11... | collective-permute-start | bytes 73736 | tf_op jit(solution)/shard_map/ppermute | solution.py:711
  109.3 12.5 %collective-permute-start.18 = (bf16[2,384,128]{2,1,0:T(8,128)(2,1)S(1)}, bf16[2,384,128]{2,1,0:T(8,128)(2,1)S(1)}, u32[]{:S(2)}, u32[]{:S(2)}) collective-permute-start(bf16[2,384,128]{2,1,0:T(8,128)(2,1)S(1)} %get-tuple-element.56), channel_id=1, source_target_pairs={{0,8},{1,9},{2,10},{3,11},{4,12},{5,13},{6,14},{7,15},{8,0},{9,1},... | collective-permute-start | bytes 589832 | tf_op jit(solution)/shard_map/ppermute | solution.py:711
  109.5 7.1 %collective-permute-start.16 = (bf16[2,192,128]{2,1,0:T(8,128)(2,1)S(1)}, bf16[2,192,128]{2,1,0:T(8,128)(2,1)S(1)}, u32[]{:S(2)}, u32[]{:S(2)}) collective-permute-start(bf16[2,192,128]{2,1,0:T(8,128)(2,1)S(1)} %get-tuple-element.52), channel_id=1, source_target_pairs={{0,4},{1,5},{2,6},{3,7},{4,0},{5,1},{6,2},{7,3},{8,12},{9,13},{10,... | collective-permute-start | bytes 294920 | tf_op jit(solution)/shard_map/ppermute | solution.py:711
  111.0 32.0 %collective-permute-start.11 = (bf16[4,2,64,1024]{3,2,1,0:T(8,128)(2,1)}, bf16[4,2,64,1024]{3,2,1,0:T(8,128)(2,1)S(1)}, u32[]{:S(2)}, u32[]{:S(2)}) collective-permute-start(bf16[4,2,64,1024]{3,2,1,0:T(8,128)(2,1)} %bitcast.39), channel_id=1, source_target_pairs={{0,1},{1,0},{2,3},{3,2},{4,5},{5,4},{6,7},{7,6},{8,9},{9,8},{10,11... | collective-permute-start | bytes 3145736 | tf_op jit(solution)/shard_map/ppermute | solution.py:711
  111.1 31.0 %copy-start.6 = (bf16[64,192]{1,0:T(8,128)(2,1)}, bf16[64,192]{1,0:T(8,128)(2,1)S(1)}, u32[]{:S(2)}) copy-start(bf16[64,192]{1,0:T(8,128)(2,1)S(1)} %fusion.2.own_rank) | copy-start | bytes 73732
  116.6 7.4 %collective-permute-start.17 = (bf16[64,128]{1,0:T(8,128)(2,1)S(1)}, bf16[64,128]{1,0:T(8,128)(2,1)S(1)}, u32[]{:S(2)}, u32[]{:S(2)}) collective-permute-start(bf16[64,128]{1,0:T(8,128)(2,1)S(1)} %slice.51), channel_id=1, source_target_pairs={{0,8},{1,9},{2,10},{3,11},{4,12},{5,13},{6,14},{7,15},{8,0},{9,1},... | collective-permute-start | bytes 49160 | tf_op jit(solution)/shard_map/ppermute | solution.py:711
  122.4 4.7 %collective-permute-start.23 = (bf16[384,128]{1,0:T(8,128)(2,1)S(1)}, bf16[384,128]{1,0:T(8,128)(2,1)S(1)}, u32[]{:S(2)}, u32[]{:S(2)}) collective-permute-start(bf16[384,128]{1,0:T(8,128)(2,1)S(1)} %get-tuple-element.57), channel_id=1, source_target_pairs={{0,16},{1,17},{2,18},{3,19},{4,20},{5,21},{6,22},{7,23},{8,24},{9,... | collective-permute-start | bytes 294920 | tf_op jit(solution)/shard_map/ppermute | solution.py:711
  124.0 8.1 %collective-permute-start.22 = (bf16[2,2,192,128]{3,2,1,0:T(8,128)(2,1)S(1)}, bf16[2,2,192,128]{3,2,1,0:T(8,128)(2,1)S(1)}, u32[]{:S(2)}, u32[]{:S(2)}) collective-permute-start(bf16[2,2,192,128]{3,2,1,0:T(8,128)(2,1)S(1)} %pad_maximum_fusion.12), channel_id=1, source_target_pairs={{0,2},{1,3},{2,0},{3,1},{4,6},{5,7},{6,4},{7,5},{8,10},{9,11},{10,... | collective-permute-start | bytes 589832 | tf_op jit(solution)/shard_map/ppermute | solution.py:711
  124.8 6.6 %collective-permute-start.19 = (bf16[2,64,128]{2,1,0:T(8,128)(2,1)S(1)}, bf16[2,64,128]{2,1,0:T(8,128)(2,1)S(1)}, u32[]{:S(2)}, u32[]{:S(2)}) collective-permute-start(bf16[2,64,128]{2,1,0:T(8,128)(2,1)S(1)} %pad_maximum_fusion.15), channel_id=1, source_target_pairs={{0,2},{1,3},{2,0},{3,1},{4,6},{5,7},{6,4},{7,5},{8,10},{9,11},{10,... | collective-permute-start | bytes 98312 | tf_op jit(solution)/shard_map/ppermute | solution.py:711
  126.1 6.0 %collective-permute-start.20 = (bf16[2,64,128]{2,1,0:T(8,128)(2,1)S(1)}, bf16[2,64,128]{2,1,0:T(8,128)(2,1)S(1)}, u32[]{:S(2)}, u32[]{:S(2)}) collective-permute-start(bf16[2,64,128]{2,1,0:T(8,128)(2,1)S(1)} %pad_maximum_fusion.15), channel_id=1, source_target_pairs={{0,4},{1,5},{2,6},{3,7},{4,0},{5,1},{6,2},{7,3},{8,12},{9,13},{10,... | collective-permute-start | bytes 98312 | tf_op jit(solution)/shard_map/ppermute | solution.py:711
  127.1 7.9 %collective-permute-start.21 = (bf16[2,64,128]{2,1,0:T(8,128)(2,1)S(1)}, bf16[2,64,128]{2,1,0:T(8,128)(2,1)S(1)}, u32[]{:S(2)}, u32[]{:S(2)}) collective-permute-start(bf16[2,64,128]{2,1,0:T(8,128)(2,1)S(1)} %pad_maximum_fusion.15), channel_id=1, source_target_pairs={{0,6},{1,7},{2,4},{3,5},{4,2},{5,3},{6,0},{7,1},{8,14},{9,15},{10,... | collective-permute-start | bytes 98312 | tf_op jit(solution)/shard_map/ppermute | solution.py:711
  131.4 7.6 %collective-permute-start.26 = (bf16[2,384,128]{2,1,0:T(8,128)(2,1)S(1)}, bf16[2,384,128]{2,1,0:T(8,128)(2,1)S(1)}, u32[]{:S(2)}, u32[]{:S(2)}) collective-permute-start(bf16[2,384,128]{2,1,0:T(8,128)(2,1)S(1)} %get-tuple-element.75), channel_id=1, source_target_pairs={{0,2},{1,3},{2,0},{3,1},{4,6},{5,7},{6,4},{7,5},{8,10},{9,11},{10,... | collective-permute-start | bytes 589832 | tf_op jit(solution)/shard_map/ppermute | solution.py:711
  132.1 7.1 %collective-permute-start.27 = (bf16[2,384,128]{2,1,0:T(8,128)(2,1)S(1)}, bf16[2,384,128]{2,1,0:T(8,128)(2,1)S(1)}, u32[]{:S(2)}, u32[]{:S(2)}) collective-permute-start(bf16[2,384,128]{2,1,0:T(8,128)(2,1)S(1)} %get-tuple-element.75), channel_id=1, source_target_pairs={{0,4},{1,5},{2,6},{3,7},{4,0},{5,1},{6,2},{7,3},{8,12},{9,13},{10,... | collective-permute-start | bytes 589832 | tf_op jit(solution)/shard_map/ppermute | solution.py:711
  132.1 10.0 %collective-permute-start.28 = (bf16[2,384,128]{2,1,0:T(8,128)(2,1)S(1)}, bf16[2,384,128]{2,1,0:T(8,128)(2,1)S(1)}, u32[]{:S(2)}, u32[]{:S(2)}) collective-permute-start(bf16[2,384,128]{2,1,0:T(8,128)(2,1)S(1)} %get-tuple-element.75), channel_id=1, source_target_pairs={{0,6},{1,7},{2,4},{3,5},{4,2},{5,3},{6,0},{7,1},{8,14},{9,15},{10,... | collective-permute-start | bytes 589832 | tf_op jit(solution)/shard_map/ppermute | solution.py:711
  134.9 8.1 %copy-start.5 = (bf16[2,2,2,192,128]{4,3,2,1,0:T(8,128)(2,1)}, bf16[2,2,2,192,128]{4,3,2,1,0:T(8,128)(2,1)S(1)}, u32[]{:S(2)}) copy-start(bf16[2,2,2,192,128]{4,3,2,1,0:T(8,128)(2,1)S(1)} %copy.10) | copy-start | bytes 1179652
  135.0 8.1 %collective-permute-start.25 = (bf16[4,2,192,128]{3,2,1,0:T(8,128)(2,1)S(1)}, bf16[4,2,192,128]{3,2,1,0:T(8,128)(2,1)S(1)}, u32[]{:S(2)}, u32[]{:S(2)}) collective-permute-start(bf16[4,2,192,128]{3,2,1,0:T(8,128)(2,1)S(1)} %bitcast.44), channel_id=1, source_target_pairs={{0,1},{1,0},{2,3},{3,2},{4,5},{5,4},{6,7},{7,6},{8,9},{9,8},{10,11... | collective-permute-start | bytes 1179656 | tf_op jit(solution)/shard_map/ppermute | solution.py:711
  139.0 3.3 %collective-permute-start.24 = (bf16[4,2,64,128]{3,2,1,0:T(8,128)(2,1)S(1)}, bf16[4,2,64,128]{3,2,1,0:T(8,128)(2,1)S(1)}, u32[]{:S(2)}, u32[]{:S(2)}) collective-permute-start(bf16[4,2,64,128]{3,2,1,0:T(8,128)(2,1)S(1)} %pad_maximum_fusion.14), channel_id=1, source_target_pairs={{0,1},{1,0},{2,3},{3,2},{4,5},{5,4},{6,7},{7,6},{8,9},{9,8},{10,11... | collective-permute-start | bytes 393224 | tf_op jit(solution)/shard_map/ppermute | solution.py:711
  142.2 13.4 %collective-permute-start.29 = (bf16[4,2,384,128]{3,2,1,0:T(8,128)(2,1)S(1)}, bf16[4,2,384,128]{3,2,1,0:T(8,128)(2,1)S(1)}, u32[]{:S(2)}, u32[]{:S(2)}) collective-permute-start(bf16[4,2,384,128]{3,2,1,0:T(8,128)(2,1)S(1)} %pad_maximum_fusion.1.same), channel_id=1, source_target_pairs={{0,1},{1,0},{2,3},{3,2},{4,5},{5,4},{6,7},{7,6},{8,9},{9,8},{10,11... | collective-permute-start | bytes 2359304 | tf_op jit(solution)/shard_map/ppermute | solution.py:711
  143.0 0.8 copy-start.10
  143.8 1.0 copy-start.9
  155.6 1.0 copy-start.2

commit v8 on v7

--- a/solution.py
+++ b/solution.py
@@ -526,6 +526,7 @@
 
 
 def attend_kernel(
+    first_head,
     query_block,
     key_same,
     key_other,
@@ -537,20 +538,17 @@
     up_other,
     cosines,
     sines,
-    attended,
-    flat_query,
-    flat_keyval,
-    keys,
-    values,
+    *refs,
 ):
-    step = pl.program_id(0)
+    attended, flat_query, flat_keyval, keys, values = refs[-5:]
+    step = pl.program_id(0) + first_head
     rows = query_block.shape[0]
     base = lax.axis_index("ctx") * rows
     half = lax.axis_index("ctx") // PIECES
     seat = lax.rem(lax.axis_index("ctx"), PIECES)
     dot = partial(jnp.dot, preferred_element_type=jnp.float32)
 
-    @pl.when(step == 0)
+    @pl.when(pl.program_id(0) == 0)
     def _():
         for apart in range(PIECES):
             ups = up_other if apart % 2 else up_same
@@ -620,7 +618,7 @@
             attended[:, span] = result[place * rows : (place + 1) * rows]
 
 
-def attend(query_base, base, own_rank, all_rank, ups, cosines, sines):
+def attend(first_head, heads, before, query_base, base, own_rank, all_rank, ups, cosines, sines):
     rows = query_base.shape[0]
     seq = 4 * PIECES // 2 * rows
     width = GROUP * HEAD_SIZE
@@ -628,16 +626,19 @@
     def whole(shape):
         return pl.BlockSpec(shape, lambda h: (0,) * len(shape))
 
-    key_spec = pl.BlockSpec((PIECES // 2, 2, rows, HEAD_SIZE), lambda h: (0, 0, 0, h))
+    key_spec = pl.BlockSpec((PIECES // 2, 2, rows, HEAD_SIZE), lambda h: (0, 0, 0, h + first_head))
     value_spec = pl.BlockSpec(
-        (PIECES // 2, 2, rows, HEAD_SIZE), lambda h: (0, 0, 0, h + KEYVALUE_HEADS)
-    )
+        (PIECES // 2, 2, rows, HEAD_SIZE), lambda h: (0, 0, 0, h + first_head + KEYVALUE_HEADS)
+    )
+    operands = (query_base, base[0], base[1], base[0], base[1], own_rank, all_rank, *ups)
+    operands += (cosines, sines) + (() if before is None else (before,))
+    query_spec = pl.BlockSpec((rows, width), lambda h: (0, h + first_head))
     return pl.pallas_call(
-        attend_kernel,
-        grid=(KEYVALUE_HEADS,),
+        partial(attend_kernel, first_head),
+        grid=(heads,),
         out_shape=jax.ShapeDtypeStruct((rows, QH * HEAD_SIZE), jnp.bfloat16),
         in_specs=[
-            pl.BlockSpec((rows, width), lambda h: (0, h)),
+            query_spec,
             key_spec,
             key_spec,
             value_spec,
@@ -648,8 +649,10 @@
             whole(ups[1].shape),
             whole(cosines.shape),
             whole(sines.shape),
-        ],
-        out_specs=pl.BlockSpec((rows, width), lambda h: (0, h)),
+        ]
+        + [pl.BlockSpec(memory_space=pl.ANY)] * (len(operands) - 11),
+        out_specs=query_spec,
+        input_output_aliases={} if before is None else {len(operands) - 1: 0},
         scratch_shapes=[
             pltpu.VMEM((2 * PIECES * QUERY_ROWS, 128), jnp.float32),
             pltpu.VMEM((2, 2 * PIECES * KEYVAL_ROWS, 128), jnp.float32),
@@ -658,11 +661,11 @@
         ],
         compiler_params=pltpu.CompilerParams(vmem_limit_bytes=60 << 20),
         cost_estimate=pl.CostEstimate(
-            flops=48 * rows * QH * seq * HEAD_SIZE,
+            flops=12 * heads * rows * QH * seq * HEAD_SIZE,
             bytes_accessed=10 << 20,
-            transcendentals=rows * QH * seq,
+            transcendentals=heads * rows * GROUP * seq,
         ),
-    )(query_base, base[0], base[1], base[0], base[1], own_rank, all_rank, *ups, cosines, sines)
+    )(*operands)
 
 
 def widen_kernel(attended, same, other, out_delta, down_out, up_out):
@@ -745,46 +748,50 @@
     even, odd = deal(normed_input, packed)
     sibling = swap(odd, 1)
     base = jnp.concatenate([key_base, value_base], 1)
-    base = along_x(along_z(jnp.stack([base, swap(base, PIECES)])))
+    base = jnp.stack([base, swap(base, PIECES)])
+    packed = after(packed, base)
 
     spread = lax.all_to_all(packed, "ctx", 0, 0, axis_index_groups=blocks)
-    spread = after(spread, packed_second, sibling, base)
+    spread = after(spread, packed_second, sibling)
     sent = pick(spread, stretch_adapter, elsewhere, adapter_owner, (896, KEYVAL_ROWS))
     arrived = exchange(sent)
     dealt = [after(jnp.stack([even[j], sibling[j]]), sent) for j in range(PIECES // 2)]
     dealt = [swap(block, 2 * j) if j else block for j, block in enumerate(dealt)]
-    packed_second = after(packed_second, sent)
+    base = along_z(after(base, sent))
+
+    weight, ups = join(stretch_adapter, adapter_owner, arrived)
+    partial_sums = narrow(after(weight, base, cosines, sines), dealt)
+    packed_second = after(packed_second, *partial_sums)
     spread = lax.all_to_all(packed_second, "ctx", 0, 0, axis_index_groups=blocks)
-
-    weight, ups = join(stretch_adapter, adapter_owner, arrived)
-    partial_sums = narrow(after(weight, spread, cosines, sines), dealt)
     back = [swap(block, 2 * j) if j else block for j, block in enumerate(partial_sums)]
     back = sum(block.astype(jnp.float32) for block in back)
     own_rank = swap(back[1].astype(jnp.bfloat16), 1)
     own_rank = back[0] + own_rank.astype(jnp.float32)
     own_rank = own_rank.astype(jnp.bfloat16)
     ups = along_z(after(ups, *partial_sums))
-    near, far = pick(
-        after(spread, *partial_sums), stretch_adapter, elsewhere, adapter_owner, None
-    )
+    base = along_x(base)
+    all_rank = after(own_rank[:, ADAPTER_RANK:], ups)
+    near, far = pick(after(spread, all_rank), stretch_adapter, elsewhere, adapter_owner, None)
     far = swap(far, PIECES)
-    base = after(base, *partial_sums)
-    base = (base, swap(base, 1))
-    all_rank = after(own_rank[:, ADAPTER_RANK:], ups)
     all_rank = jnp.stack([all_rank, swap(all_rank, PIECES)])
+    all_rank = after(all_rank, base)
+    ups = along_x(after(ups, all_rank))
+    base = (base, swap(after(base, all_rank), 1))
+    all_rank = jnp.stack([swap(all_rank, apart) if apart else all_rank for apart in (0, 2, 4, 6)])
+    all_rank = after(all_rank, ups, near)
+    ups = (ups, swap(ups, 1))
+    all_rank = jnp.stack([all_rank, swap(all_rank, 1)])
+
+    far = after(far, all_rank)
     own, across = settle(stretch_adapter, elsewhere, adapter_owner, near, far)
-    all_rank = after(all_rank, across)
-    ups = along_x(after(ups, all_rank))
     ends = jnp.stack([own, swap(across, 2 * PIECES)])
-    all_rank = jnp.stack([swap(all_rank, apart) if apart else all_rank for apart in (0, 2, 4, 6)])
-    all_rank = after(all_rank, ups, ends)
+    shared = (query_base, base, own_rank, all_rank, ups, cosines, sines)
+    attended = attend(0, 1, None, *shared)
+    ends = after(ends, attended)
     ends = jnp.stack([swap(ends, apart) if apart else ends for apart in (0, 2, 4, 6)])
-    all_rank = jnp.stack([all_rank, swap(all_rank, 1)])
-    ups = (ups, swap(ups, 1))
-    ends = (ends, swap(ends, 1))
-
-    attended = attend(query_base, base, own_rank, all_rank, ups, cosines, sines)
-    return attended, widen(attended, *ends)
+    attended = attend(1, KEYVALUE_HEADS - 1, attended, *shared)
+    ends = after(ends, attended)
+    return attended, widen(attended, ends, swap(ends, 1))
 
 
 def shards(normed_input, query_base, key_base, value_base, adapter_pool, stretch_adapter, owner):

time: 160 us -> 158 us (0.988)
  starting transfers between devices: 49 us -> 45.8 us
  Pallas kernels: 25.9 us -> 28.5 us
    ppermute x30, waiting for transfers between devices: 73.3 us -> 56.4 us  [swap(): lax.ppermute(block, ('groups', 'ctx'), [(i, i ^ mask) for i in range(4 *...]
    all_to_all x1, waiting for transfers between devices: 0.01 us -> 15.4 us  [direct_shards(): spread = lax.all_to_all(packed, 'ctx', 0, 0, axis_index_groups=blocks)]
    ppermute x30, starting transfers between devices: 40 us -> 37.6 us  [swap(): lax.ppermute(block, ('groups', 'ctx'), [(i, i ^ mask) for i in range(4 *...]
    pallas_call x1 -> x2, Pallas kernels: 10.8 us -> 13.2 us  [attend(): pl.pallas_call(partial(attend_kernel, first_head), grid=(heads,), out_sha...]
  transfers between devices with their start and end apart: 32 -> 32, of which waited for: 17 -> 14; matrix products, arithmetic and copies ran while one was open for 5% -> 5% of each run, Pallas kernels for 10% -> 15%
where the time goes in v8:
time: 158 us
  waiting for transfers between devices  71.8 us (45%)
  starting transfers between devices  45.8 us (29%)
  Pallas kernels  28.5 us (18%)
  other arithmetic  5.23 us (3%)
  local copies, waits for them, and re-layouts  5.22 us (3%)
    ppermute x30, waiting for transfers between devices, swap(): lax.ppermute(block, ('groups', 'ctx'), [(i, i ^ mask) for i in range(4 *...  56.4 us
    ppermute x30, starting transfers between devices, swap(): lax.ppermute(block, ('groups', 'ctx'), [(i, i ^ mask) for i in range(4 *...  37.6 us
    all_to_all x1, waiting for transfers between devices, direct_shards(): spread = lax.all_to_all(packed, 'ctx', 0, 0, axis_index_groups=blocks)  15.4 us
    pallas_call x2, Pallas kernels, attend(): pl.pallas_call(partial(attend_kernel, first_head), grid=(heads,), out_sha...  13.2 us
    pallas_call x2, Pallas kernels, pack_row(): pl.pallas_call(partial(pack_kernel, sections), out_shape=jax.ShapeDtypeSt...  6.68 us
    all_to_all x1, starting transfers between devices, direct_shards(): spread = lax.all_to_all(packed, 'ctx', 0, 0, axis_index_groups=blocks)  4.59 us
    all_to_all x1, starting transfers between devices, direct_shards(): lax.all_to_all(packed_second, 'ctx', 0, 0, axis_index_groups=blocks)  3.56 us
  transfers between devices with their start and end apart: 32, of which 14 were waited for; matrix products, arithmetic and copies ran while one was open for 5% of the time, Pallas kernels for 15%

profile of v8, /device:TPU:0, one launch (start us, length us, event | category | flops | bytes accessed | tf_op | source)
XLA Modules:
  0.0 157.5 jit_solution(168427551625143362)
XLA Ops:
  0.6 0.8 constant_dynamic-update-slice_fusion.1
  1.5 0.8 constant_dynamic-update-slice_fusion
  2.3 4.0 %collective-permute-start = (bf16[64,1024]{1,0:T(8,128)(2,1)S(1)}, bf16[64,1024]{1,0:T(8,128)(2,1)S(1)}, u32[]{:S(2)}, u32[]{:S(2)}) collective-permute-start(bf16[64,1024]{1,0:T(8,128)(2,1)S(1)} %constant_dynamic-update-slice_fusion), channel_id=1, source_target_pairs={{0,8},{1,9},{2,10},{3,11},{4,12},{5,13},{6,14},{7,15},{8,0},{9,1},... | collective-permute-start | bytes 393224 | tf_op jit(solution)/shard_map/ppermute | solution.py:714
  6.4 4.0 %shard_map.86.refs_0_ = bf16[8,928,128]{2,1,0:T(8,128)(2,1)} custom-call(bf16[1,2686976]{1,0:T(2,128)(2,1)} %pool.3), custom_call_target="tpu_custom_call" | custom-call | bytes 8388608 | tf_op jit(solution)/shard_map/pallas_call | solution.py:316
  10.4 2.3 %collective-permute-done = bf16[64,1024]{1,0:T(8,128)(2,1)S(1)} collective-permute-done((bf16[64,1024]{1,0:T(8,128)(2,1)S(1)}, bf16[64,1024]{1,0:T(8,128)(2,1)S(1)}, u32[]{:S(2)}, u32[]{:S(2)}) %collective-permute-start) | collective-permute-done | bytes 131104 | tf_op jit(solution)/shard_map/ppermute | solution.py:714
  12.7 0.7 pad_maximum_fusion.6
  13.4 4.6 %all-to-all-start = ((bf16[8,928,128]{2,1,0:T(8,128)(2,1)}), bf16[8,928,128]{2,1,0:T(8,128)(2,1)}, u32[]{:S(2)}, u32[]{:S(2)}) async-start(bf16[8,928,128]{2,1,0:T(8,128)(2,1)} %shard_map.86.refs_0_), calls=%async_computation | async-start | bytes 3801088 | tf_op jit(solution)/shard_map/all_to_all | solution.py:754
  18.0 1.6 %collective-permute-start.1 = (s32[2]{0:T(128)S(1)}, s32[2]{0:T(128)S(1)}, u32[]{:S(2)}, u32[]{:S(2)}) collective-permute-start(s32[2]{0:T(128)S(1)} %copy-done.3), channel_id=1, source_target_pairs={{0,16},{1,17},{2,18},{3,19},{4,20},{5,21},{6,22},{7,23},{8,24},{9,... | collective-permute-start | bytes 32 | tf_op jit(solution)/shard_map/ppermute | solution.py:714
  19.6 0.3 shard_map.88
  19.9 0.1 collective-permute-start.2
  20.0 2.7 %shard_map.87 = bf16[8,384,128]{2,1,0:T(8,128)(2,1)} custom-call(bf16[1,2686976]{1,0:T(2,128)(2,1)} %pool.3, bf16[8,928,128]{2,1,0:T(8,128)(2,1)} %shard_map.86.refs_0_), custom_call_target="tpu_custom_call" | custom-call | bytes 8388608 | tf_op jit(solution)/shard_map/pallas_call | solution.py:316
  22.7 0.8 fusion.5
  23.5 1.9 %fusion = (f32[1024,64]{1,0:T(8,128)S(1)}, f32[1024,64]{1,0:T(8,128)S(1)}, f32[1024,64]{1,0:T(8,128)S(1)}) fusion(f32[64]{0:T(128)S(1)} %multiply_power_fusion, f32[1024]{0:T(1024)S(1)} %iota_convert_fusion), kind=kLoop, calls=%fused_computation.16 | loop fusion | flops 131072 | bytes 790784 | tf_op jit(solution)/shard_map/neg | solution.py:730
  25.4 0.7 fusion.6
  26.2 15.4 %all-to-all-done.spread = bf16[8,928,128]{2,1,0:T(8,128)(2,1)} async-done(((bf16[8,928,128]{2,1,0:T(8,128)(2,1)}), bf16[8,928,128]{2,1,0:T(8,128)(2,1)}, u32[]{:S(2)}, u32[]{:S(2)}) %all-to-all-start) | async-done | bytes 1900576 | tf_op jit(solution)/shard_map/all_to_all | solution.py:754
  41.6 2.0 %shard_map.89 = (bf16[960,128]{1,0:T(8,128)(2,1)S(1)}, bf16[960,128]{1,0:T(8,128)(2,1)S(1)}, bf16[960,128]{1,0:T(8,128)(2,1)S(1)}, bf16[960,128]{1,0:T(8,128)(2,1)S(1)}) custom-call(s32[2]{0:T(128)S(1)} %copy-done.3, s32[2]{0:T(128)S(1)} %collective-permute-done.1.there, s32[16]{0:T(128)S(1)} %copy-done.4, bf16[8,928,128]{2,1,0:T(8,128)(2,1)} %all-to-all-done.spread), custom_call_target="tpu_custom_call" | custom-call | bytes 2097152 | tf_op jit(solution)/shard_map/pallas_call | solution.py:363
  43.6 2.1 %collective-permute-start.5 = (bf16[960,128]{1,0:T(8,128)(2,1)S(1)}, bf16[960,128]{1,0:T(8,128)(2,1)S(1)}, u32[]{:S(2)}, u32[]{:S(2)}) collective-permute-start(bf16[960,128]{1,0:T(8,128)(2,1)S(1)} %get-tuple-element.41), channel_id=1, source_target_pairs={{0,8},{1,9},{2,10},{3,11},{4,12},{5,13},{6,14},{7,15},{8,0},{9,1},... | collective-permute-start | bytes 737288 | tf_op jit(solution)/shard_map/ppermute | solution.py:714
  45.7 1.5 collective-permute-start.6
  47.3 0.9 collective-permute-start.7
  48.2 1.5 collective-permute-start.3
  49.7 0.6 collective-permute-start.8
  50.3 12.4 %collective-permute-done.5.refs_1_ = bf16[960,128]{1,0:T(8,128)(2,1)S(1)} collective-permute-done((bf16[960,128]{1,0:T(8,128)(2,1)S(1)}, bf16[960,128]{1,0:T(8,128)(2,1)S(1)}, u32[]{:S(2)}, u32[]{:S(2)}) %collective-permute-start.5) | collective-permute-done | bytes 245792 | tf_op jit(solution)/shard_map/ppermute | solution.py:714
  62.7 1.0 collective-permute-start.10
  63.8 1.8 %collective-permute-start.9 = (bf16[2,64,1024]{2,1,0:T(8,128)(2,1)S(1)}, bf16[2,64,1024]{2,1,0:T(8,128)(2,1)S(1)}, u32[]{:S(2)}, u32[]{:S(2)}) collective-permute-start(bf16[2,64,1024]{2,1,0:T(8,128)(2,1)S(1)} %get-tuple-element.50), channel_id=1, source_target_pairs={{0,4},{1,5},{2,6},{3,7},{4,0},{5,1},{6,2},{7,3},{8,12},{9,13},{10,... | collective-permute-start | bytes 786440 | tf_op jit(solution)/shard_map/ppermute | solution.py:714
  65.6 1.3 pad_maximum_fusion.3
  66.9 2.0 %collective-permute-done.7.refs_3_ = bf16[960,128]{1,0:T(8,128)(2,1)S(1)} collective-permute-done((bf16[960,128]{1,0:T(8,128)(2,1)S(1)}, bf16[960,128]{1,0:T(8,128)(2,1)S(1)}, u32[]{:S(2)}, u32[]{:S(2)}) %collective-permute-start.7) | collective-permute-done | bytes 245792 | tf_op jit(solution)/shard_map/ppermute | solution.py:714
  69.0 1.0 shard_map.90
  70.0 4.4 %collective-permute-done.10.refs_3_ = bf16[2,64,1024]{2,1,0:T(8,128)(2,1)S(1)} collective-permute-done((bf16[2,64,1024]{2,1,0:T(8,128)(2,1)S(1)}, bf16[2,64,1024]{2,1,0:T(8,128)(2,1)S(1)}, u32[]{:S(2)}, u32[]{:S(2)}) %collective-permute-start.10) | collective-permute-done | bytes 262176 | tf_op jit(solution)/shard_map/ppermute | solution.py:714
  74.4 4.6 %collective-permute-done.9.refs_2_ = bf16[2,64,1024]{2,1,0:T(8,128)(2,1)S(1)} collective-permute-done((bf16[2,64,1024]{2,1,0:T(8,128)(2,1)S(1)}, bf16[2,64,1024]{2,1,0:T(8,128)(2,1)S(1)}, u32[]{:S(2)}, u32[]{:S(2)}) %collective-permute-start.9) | collective-permute-done | bytes 262176 | tf_op jit(solution)/shard_map/ppermute | solution.py:714
  79.1 0.5 shard_map.91
  79.5 1.5 collective-permute-start.11
  81.1 2.0 %collective-permute-start.13 = (bf16[2,64,192]{2,1,0:T(8,128)(2,1)S(1)}, bf16[2,64,192]{2,1,0:T(8,128)(2,1)S(1)}, u32[]{:S(2)}, u32[]{:S(2)}) collective-permute-start(bf16[2,64,192]{2,1,0:T(8,128)(2,1)S(1)} %get-tuple-element.55), channel_id=1, source_target_pairs={{0,6},{1,7},{2,4},{3,5},{4,2},{5,3},{6,0},{7,1},{8,14},{9,15},{10,... | collective-permute-start | bytes 147464 | tf_op jit(solution)/shard_map/ppermute | solution.py:714
  83.1 1.4 collective-permute-start.4
  84.6 0.9 collective-permute-done.12
  85.5 1.0 collective-permute-done.13
  86.6 3.6 %all-to-all-start.1 = ((bf16[8,384,128]{2,1,0:T(8,128)(2,1)}), bf16[8,384,128]{2,1,0:T(8,128)(2,1)S(1)}, u32[]{:S(2)}, u32[]{:S(2)}) async-start(bf16[8,384,128]{2,1,0:T(8,128)(2,1)} %shard_map.87), calls=%async_computation.1 | async-start | bytes 1572864 | tf_op jit(solution)/shard_map/all_to_all | solution.py:765
  90.2 1.9 %collective-permute-start.15 = (bf16[2,192,128]{2,1,0:T(8,128)(2,1)S(1)}, bf16[2,192,128]{2,1,0:T(8,128)(2,1)S(1)}, u32[]{:S(2)}, u32[]{:S(2)}) collective-permute-start(bf16[2,192,128]{2,1,0:T(8,128)(2,1)S(1)} %get-tuple-element.57), channel_id=1, source_target_pairs={{0,4},{1,5},{2,6},{3,7},{4,0},{5,1},{6,2},{7,3},{8,12},{9,13},{10,... | collective-permute-start | bytes 294920 | tf_op jit(solution)/shard_map/ppermute | solution.py:714
  92.2 11.8 %collective-permute-done.15 = bf16[2,192,128]{2,1,0:T(8,128)(2,1)S(1)} collective-permute-done((bf16[2,192,128]{2,1,0:T(8,128)(2,1)S(1)}, bf16[2,192,128]{2,1,0:T(8,128)(2,1)S(1)}, u32[]{:S(2)}, u32[]{:S(2)}) %collective-permute-start.15) | collective-permute-done | bytes 98336 | tf_op jit(solution)/shard_map/ppermute | solution.py:714
  104.1 2.4 %collective-permute-start.16 = (bf16[64,128]{1,0:T(8,128)(2,1)S(1)}, bf16[64,128]{1,0:T(8,128)(2,1)S(1)}, u32[]{:S(2)}, u32[]{:S(2)}) collective-permute-start(bf16[64,128]{1,0:T(8,128)(2,1)S(1)} %slice.51), channel_id=1, source_target_pairs={{0,8},{1,9},{2,10},{3,11},{4,12},{5,13},{6,14},{7,15},{8,0},{9,1},... | collective-permute-start | bytes 49160 | tf_op jit(solution)/shard_map/ppermute | solution.py:714
  106.4 2.3 %collective-permute-done.16 = bf16[64,128]{1,0:T(8,128)(2,1)S(1)} collective-permute-done((bf16[64,128]{1,0:T(8,128)(2,1)S(1)}, bf16[64,128]{1,0:T(8,128)(2,1)S(1)}, u32[]{:S(2)}, u32[]{:S(2)}) %collective-permute-start.16) | collective-permute-done | bytes 16416 | tf_op jit(solution)/shard_map/ppermute | solution.py:714
  108.8 0.1 pad_maximum_fusion
  108.9 1.1 copy.10
  110.0 1.5 collective-permute-start.21
  111.4 0.2 collective-permute-start.20
  111.7 1.8 %collective-permute-start.19 = (bf16[2,64,128]{2,1,0:T(8,128)(2,1)S(1)}, bf16[2,64,128]{2,1,0:T(8,128)(2,1)S(1)}, u32[]{:S(2)}, u32[]{:S(2)}) collective-permute-start(bf16[2,64,128]{2,1,0:T(8,128)(2,1)S(1)} %pad_maximum_fusion.15), channel_id=1, source_target_pairs={{0,4},{1,5},{2,6},{3,7},{4,0},{5,1},{6,2},{7,3},{8,12},{9,13},{10,... | collective-permute-start | bytes 98312 | tf_op jit(solution)/shard_map/ppermute | solution.py:714
  113.5 1.5 collective-permute-start.18
  114.9 3.4 %collective-permute-done.21 = bf16[2,2,192,128]{3,2,1,0:T(8,128)(2,1)S(1)} collective-permute-done((bf16[2,2,192,128]{3,2,1,0:T(8,128)(2,1)S(1)}, bf16[2,2,192,128]{3,2,1,0:T(8,128)(2,1)S(1)}, u32[]{:S(2)}, u32[]{:S(2)}) %collective-permute-start.21) | collective-permute-done | bytes 196640 | tf_op jit(solution)/shard_map/ppermute | solution.py:714
  118.5 0.2 collective-permute-done.18
  118.7 1.2 shard_map.92
  119.9 0.4 collective-permute-start.22
  120.3 2.3 %collective-permute-start.24 = (bf16[2,384,128]{2,1,0:T(8,128)(2,1)S(1)}, bf16[2,384,128]{2,1,0:T(8,128)(2,1)S(1)}, u32[]{:S(2)}, u32[]{:S(2)}) collective-permute-start(bf16[2,384,128]{2,1,0:T(8,128)(2,1)S(1)} %get-tuple-element.66), channel_id=1, source_target_pairs={{0,8},{1,9},{2,10},{3,11},{4,12},{5,13},{6,14},{7,15},{8,0},{9,1},... | collective-permute-start | bytes 589832 | tf_op jit(solution)/shard_map/ppermute | solution.py:714
  122.6 0.7 pad_maximum_fusion.11.all_rank
  123.4 8.7 %collective-permute-done.24.far = bf16[2,384,128]{2,1,0:T(8,128)(2,1)S(1)} collective-permute-done((bf16[2,384,128]{2,1,0:T(8,128)(2,1)S(1)}, bf16[2,384,128]{2,1,0:T(8,128)(2,1)S(1)}, u32[]{:S(2)}, u32[]{:S(2)}) %collective-permute-start.24) | collective-permute-done | bytes 196640 | tf_op jit(solution)/shard_map/ppermute | solution.py:714
  132.0 0.8 shard_map.95
  132.8 1.7 %collective-permute-start.25 = (bf16[384,128]{1,0:T(8,128)(2,1)S(1)}, bf16[384,128]{1,0:T(8,128)(2,1)S(1)}, u32[]{:S(2)}, u32[]{:S(2)}) collective-permute-start(bf16[384,128]{1,0:T(8,128)(2,1)S(1)} %get-tuple-element.69), channel_id=1, source_target_pairs={{0,16},{1,17},{2,18},{3,19},{4,20},{5,21},{6,22},{7,23},{8,24},{9,... | collective-permute-start | bytes 294920 | tf_op jit(solution)/shard_map/ppermute | solution.py:714
  134.5 0.8 copy-done.13
  135.3 4.5 %shard_map.93.refs_0_ = bf16[64,4096]{1,0:T(8,128)(2,1)} custom-call(bf16[64,4096]{1,0:T(8,128)(2,1)} %query_block.3, bf16[4,2,64,1024]{3,2,1,0:T(8,128)(2,1)} %bitcast.6.key_same.value_same, bf16[4,2,64,1024]{3,2,1,0:T(8,128)(2,1)} %collective-permute-done.17.key_other.value_other, bf16[4,2,64,1024]{3,2,1,0:T(8,128)(2,1)} %bitcast.6.key_same.value_same, ...), custom_call_target="tpu_custom_call" | custom-call | flops 3221225472 | bytes 10485760 | tf_op jit(solution)/shard_map/pallas_call | solution.py:636
  139.8 0.7 collective-permute-start.28
  140.5 2.4 %collective-permute-start.27 = (bf16[2,384,128]{2,1,0:T(8,128)(2,1)S(1)}, bf16[2,384,128]{2,1,0:T(8,128)(2,1)S(1)}, u32[]{:S(2)}, u32[]{:S(2)}) collective-permute-start(bf16[2,384,128]{2,1,0:T(8,128)(2,1)S(1)} %pad_maximum_fusion.13), channel_id=1, source_target_pairs={{0,4},{1,5},{2,6},{3,7},{4,0},{5,1},{6,2},{7,3},{8,12},{9,13},{10,... | collective-permute-start | bytes 589832 | tf_op jit(solution)/shard_map/ppermute | solution.py:714
  142.9 0.4 collective-permute-start.26
  143.3 8.7 %shard_map.94.attended = bf16[64,4096]{1,0:T(8,128)(2,1)} custom-call(bf16[64,4096]{1,0:T(8,128)(2,1)} %query_block.3, bf16[4,2,64,1024]{3,2,1,0:T(8,128)(2,1)} %bitcast.6.key_same.value_same, bf16[4,2,64,1024]{3,2,1,0:T(8,128)(2,1)} %collective-permute-done.17.key_other.value_other, ...), custom_call_target="tpu_custom_call", output_to_operand_aliasing={{}: (11, {})} | custom-call | flops 9663676416 | bytes 10485760 | tf_op jit(solution)/shard_map/pallas_call | solution.py:636
  152.1 0.1 pad_maximum_fusion.1.same
  152.2 2.3 %collective-permute-done.29.other = bf16[4,2,384,128]{3,2,1,0:T(8,128)(2,1)S(1)} collective-permute-done((bf16[4,2,384,128]{3,2,1,0:T(8,128)(2,1)S(1)}, bf16[4,2,384,128]{3,2,1,0:T(8,128)(2,1)S(1)}, u32[]{:S(2)}, u32[]{:S(2)}) %collective-permute-start.29) | collective-permute-done | bytes 786464 | tf_op jit(solution)/shard_map/ppermute | solution.py:714
  154.5 3.0 %shard_map.96 = bf16[64,8192]{1,0:T(8,128)(2,1)} custom-call(bf16[64,4096]{1,0:T(8,128)(2,1)S(1)} %copy-done.2, bf16[4,2,384,128]{3,2,1,0:T(8,128)(2,1)S(1)} %pad_maximum_fusion.1.same, bf16[4,2,384,128]{3,2,1,0:T(8,128)(2,1)S(1)} %collective-permute-done.29.other), custom_call_target="tpu_custom_call" | custom-call | flops 134217728 | bytes 4194304 | tf_op jit(solution)/shard_map/pallas_call | solution.py:699
  (65 shorter events, 0.8 us)
Async XLA Ops:
  2.3 10.3 %collective-permute-start = (bf16[64,1024]{1,0:T(8,128)(2,1)S(1)}, bf16[64,1024]{1,0:T(8,128)(2,1)S(1)}, u32[]{:S(2)}, u32[]{:S(2)}) collective-permute-start(bf16[64,1024]{1,0:T(8,128)(2,1)S(1)} %constant_dynamic-update-slice_fusion), channel_id=1, source_target_pairs={{0,8},{1,9},{2,10},{3,11},{4,12},{5,13},{6,14},{7,15},{8,0},{9,1},... | collective-permute-start | bytes 393224 | tf_op jit(solution)/shard_map/ppermute | solution.py:714
  13.4 4.6 %copy-start.3 = (s32[2]{0:T(128)S(1)}, s32[2]{0:T(128)}, u32[]{:S(2)}) copy-start(s32[2]{0:T(128)} %here.7) | copy-start | bytes 28
  13.4 6.3 %copy-start = (bf16[8,928,128]{2,1,0:T(8,128)(2,1)S(1)}, bf16[8,928,128]{2,1,0:T(8,128)(2,1)}, u32[]{:S(2)}) copy-start(bf16[8,928,128]{2,1,0:T(8,128)(2,1)} %shard_map.86.refs_0_) | copy-start | bytes 5701636
  13.4 6.3 %copy-start.1 = (bf16[64,8192]{1,0:T(8,128)(2,1)S(1)}, bf16[64,8192]{1,0:T(8,128)(2,1)}, u32[]{:S(2)}) copy-start(bf16[64,8192]{1,0:T(8,128)(2,1)} %rows.1) | copy-start | bytes 3145732
  13.4 28.2 %all-to-all-start = ((bf16[8,928,128]{2,1,0:T(8,128)(2,1)}), bf16[8,928,128]{2,1,0:T(8,128)(2,1)}, u32[]{:S(2)}, u32[]{:S(2)}) async-start(bf16[8,928,128]{2,1,0:T(8,128)(2,1)} %shard_map.86.refs_0_), calls=%async_computation | async-start | bytes 3801088 | tf_op jit(solution)/shard_map/all_to_all | solution.py:754
  18.0 23.6 %collective-permute-start.1 = (s32[2]{0:T(128)S(1)}, s32[2]{0:T(128)S(1)}, u32[]{:S(2)}, u32[]{:S(2)}) collective-permute-start(s32[2]{0:T(128)S(1)} %copy-done.3), channel_id=1, source_target_pairs={{0,16},{1,17},{2,18},{3,19},{4,20},{5,21},{6,22},{7,23},{8,24},{9,... | collective-permute-start | bytes 32 | tf_op jit(solution)/shard_map/ppermute | solution.py:714
  19.9 5.5 %collective-permute-start.2 = (bf16[4,64,1024]{2,1,0:T(8,128)(2,1)S(1)}, bf16[4,64,1024]{2,1,0:T(8,128)(2,1)S(1)}, u32[]{:S(2)}, u32[]{:S(2)}) collective-permute-start(bf16[4,64,1024]{2,1,0:T(8,128)(2,1)S(1)} %get-tuple-element.38), channel_id=1, source_target_pairs={{0,1},{1,0},{2,3},{3,2},{4,5},{5,4},{6,7},{7,6},{8,9},{9,8},{10,11... | collective-permute-start | bytes 1572872 | tf_op jit(solution)/shard_map/ppermute | solution.py:714
  22.7 18.9 %copy-start.4 = (s32[16]{0:T(128)S(1)}, s32[16]{0:T(128)}, u32[]{:S(2)}) copy-start(s32[16]{0:T(128)} %owner.7) | copy-start | bytes 196
  25.4 22.8 %copy-start.5 = (bf16[2,64,1024]{2,1,0:T(8,128)(2,1)S(1)}, bf16[2,64,1024]{2,1,0:T(8,128)(2,1)}, u32[]{:S(2)}) copy-start(bf16[2,64,1024]{2,1,0:T(8,128)(2,1)} %pad_maximum_fusion.6) | copy-start | bytes 786436
  25.4 21.8 %copy-start.7 = (bf16[1,64,1024]{2,1,0:T(8,128)(2,1)S(1)}, bf16[1,64,1024]{2,1,0:T(8,128)(2,1)}, u32[]{:S(2)}) copy-start(bf16[1,64,1024]{2,1,0:T(8,128)(2,1)} %get-tuple-element.72) | copy-start | bytes 393220
  25.4 24.2 %copy-start.6 = (bf16[1,64,1024]{2,1,0:T(8,128)(2,1)S(1)}, bf16[1,64,1024]{2,1,0:T(8,128)(2,1)}, u32[]{:S(2)}) copy-start(bf16[1,64,1024]{2,1,0:T(8,128)(2,1)} %get-tuple-element.75) | copy-start | bytes 393220
  26.2 21.1 %copy-start.8 = (bf16[1,64,1024]{2,1,0:T(8,128)(2,1)S(1)}, bf16[1,64,1024]{2,1,0:T(8,128)(2,1)}, u32[]{:S(2)}) copy-start(bf16[1,64,1024]{2,1,0:T(8,128)(2,1)} %get-tuple-element.73) | copy-start | bytes 393220
  26.2 21.1 %copy-start.9 = (bf16[1,64,1024]{2,1,0:T(8,128)(2,1)S(1)}, bf16[1,64,1024]{2,1,0:T(8,128)(2,1)}, u32[]{:S(2)}) copy-start(bf16[1,64,1024]{2,1,0:T(8,128)(2,1)} %get-tuple-element.76) | copy-start | bytes 393220
  26.2 21.1 %copy-start.10 = (bf16[1,64,1024]{2,1,0:T(8,128)(2,1)S(1)}, bf16[1,64,1024]{2,1,0:T(8,128)(2,1)}, u32[]{:S(2)}) copy-start(bf16[1,64,1024]{2,1,0:T(8,128)(2,1)} %get-tuple-element.77) | copy-start | bytes 393220
  43.6 19.1 %collective-permute-start.5 = (bf16[960,128]{1,0:T(8,128)(2,1)S(1)}, bf16[960,128]{1,0:T(8,128)(2,1)S(1)}, u32[]{:S(2)}, u32[]{:S(2)}) collective-permute-start(bf16[960,128]{1,0:T(8,128)(2,1)S(1)} %get-tuple-element.41), channel_id=1, source_target_pairs={{0,8},{1,9},{2,10},{3,11},{4,12},{5,13},{6,14},{7,15},{8,0},{9,1},... | collective-permute-start | bytes 737288 | tf_op jit(solution)/shard_map/ppermute | solution.py:714
  45.7 18.0 %collective-permute-start.6 = (bf16[960,128]{1,0:T(8,128)(2,1)S(1)}, bf16[960,128]{1,0:T(8,128)(2,1)S(1)}, u32[]{:S(2)}, u32[]{:S(2)}) collective-permute-start(bf16[960,128]{1,0:T(8,128)(2,1)S(1)} %get-tuple-element.42), channel_id=1, source_target_pairs={{0,16},{1,17},{2,18},{3,19},{4,20},{5,21},{6,22},{7,23},{8,24},{9,... | collective-permute-start | bytes 737288 | tf_op jit(solution)/shard_map/ppermute | solution.py:714
  47.3 21.6 %collective-permute-start.7 = (bf16[960,128]{1,0:T(8,128)(2,1)S(1)}, bf16[960,128]{1,0:T(8,128)(2,1)S(1)}, u32[]{:S(2)}, u32[]{:S(2)}) collective-permute-start(bf16[960,128]{1,0:T(8,128)(2,1)S(1)} %get-tuple-element.43), channel_id=1, source_target_pairs={{0,24},{1,25},{2,26},{3,27},{4,28},{5,29},{6,30},{7,31},{8,16},{9,... | collective-permute-start | bytes 737288 | tf_op jit(solution)/shard_map/ppermute | solution.py:714
  48.2 21.7 %collective-permute-start.3 = (bf16[2,64,1024]{2,1,0:T(8,128)(2,1)S(1)}, bf16[2,64,1024]{2,1,0:T(8,128)(2,1)S(1)}, u32[]{:S(2)}, u32[]{:S(2)}) collective-permute-start(bf16[2,64,1024]{2,1,0:T(8,128)(2,1)S(1)} %copy-done.5), channel_id=1, source_target_pairs={{0,4},{1,5},{2,6},{3,7},{4,0},{5,1},{6,2},{7,3},{8,12},{9,13},{10,... | collective-permute-start | bytes 786440 | tf_op jit(solution)/shard_map/ppermute | solution.py:714
  49.7 20.3 %collective-permute-start.8 = (bf16[2,64,1024]{2,1,0:T(8,128)(2,1)S(1)}, bf16[2,64,1024]{2,1,0:T(8,128)(2,1)S(1)}, u32[]{:S(2)}, u32[]{:S(2)}) collective-permute-start(bf16[2,64,1024]{2,1,0:T(8,128)(2,1)S(1)} %get-tuple-element.49), channel_id=1, source_target_pairs={{0,2},{1,3},{2,0},{3,1},{4,6},{5,7},{6,4},{7,5},{8,10},{9,11},{10,... | collective-permute-start | bytes 786440 | tf_op jit(solution)/shard_map/ppermute | solution.py:714
  62.7 11.7 %collective-permute-start.10 = (bf16[2,64,1024]{2,1,0:T(8,128)(2,1)S(1)}, bf16[2,64,1024]{2,1,0:T(8,128)(2,1)S(1)}, u32[]{:S(2)}, u32[]{:S(2)}) collective-permute-start(bf16[2,64,1024]{2,1,0:T(8,128)(2,1)S(1)} %get-tuple-element.51), channel_id=1, source_target_pairs={{0,6},{1,7},{2,4},{3,5},{4,2},{5,3},{6,0},{7,1},{8,14},{9,15},{10,... | collective-permute-start | bytes 786440 | tf_op jit(solution)/shard_map/ppermute | solution.py:714
  63.8 15.3 %collective-permute-start.9 = (bf16[2,64,1024]{2,1,0:T(8,128)(2,1)S(1)}, bf16[2,64,1024]{2,1,0:T(8,128)(2,1)S(1)}, u32[]{:S(2)}, u32[]{:S(2)}) collective-permute-start(bf16[2,64,1024]{2,1,0:T(8,128)(2,1)S(1)} %get-tuple-element.50), channel_id=1, source_target_pairs={{0,4},{1,5},{2,6},{3,7},{4,0},{5,1},{6,2},{7,3},{8,12},{9,13},{10,... | collective-permute-start | bytes 786440 | tf_op jit(solution)/shard_map/ppermute | solution.py:714
  79.5 5.0 %collective-permute-start.11 = (bf16[2,64,192]{2,1,0:T(8,128)(2,1)S(1)}, bf16[2,64,192]{2,1,0:T(8,128)(2,1)S(1)}, u32[]{:S(2)}, u32[]{:S(2)}) collective-permute-start(bf16[2,64,192]{2,1,0:T(8,128)(2,1)S(1)} %get-tuple-element.53), channel_id=1, source_target_pairs={{0,2},{1,3},{2,0},{3,1},{4,6},{5,7},{6,4},{7,5},{8,10},{9,11},{10,... | collective-permute-start | bytes 147464 | tf_op jit(solution)/shard_map/ppermute | solution.py:714
  81.1 4.4 %collective-permute-start.12 = (bf16[2,64,192]{2,1,0:T(8,128)(2,1)S(1)}, bf16[2,64,192]{2,1,0:T(8,128)(2,1)S(1)}, u32[]{:S(2)}, u32[]{:S(2)}) collective-permute-start(bf16[2,64,192]{2,1,0:T(8,128)(2,1)S(1)} %get-tuple-element.54), channel_id=1, source_target_pairs={{0,4},{1,5},{2,6},{3,7},{4,0},{5,1},{6,2},{7,3},{8,12},{9,13},{10,... | collective-permute-start | bytes 147464 | tf_op jit(solution)/shard_map/ppermute | solution.py:714
  81.1 5.4 %collective-permute-start.13 = (bf16[2,64,192]{2,1,0:T(8,128)(2,1)S(1)}, bf16[2,64,192]{2,1,0:T(8,128)(2,1)S(1)}, u32[]{:S(2)}, u32[]{:S(2)}) collective-permute-start(bf16[2,64,192]{2,1,0:T(8,128)(2,1)S(1)} %get-tuple-element.55), channel_id=1, source_target_pairs={{0,6},{1,7},{2,4},{3,5},{4,2},{5,3},{6,0},{7,1},{8,14},{9,15},{10,... | collective-permute-start | bytes 147464 | tf_op jit(solution)/shard_map/ppermute | solution.py:714
  83.1 25.7 %collective-permute-start.4 = (bf16[2,2,64,1024]{3,2,1,0:T(8,128)(2,1)S(1)}, bf16[2,2,64,1024]{3,2,1,0:T(8,128)(2,1)S(1)}, u32[]{:S(2)}, u32[]{:S(2)}) collective-permute-start(bf16[2,2,64,1024]{3,2,1,0:T(8,128)(2,1)S(1)} %get-tuple-element.81), channel_id=1, source_target_pairs={{0,2},{1,3},{2,0},{3,1},{4,6},{5,7},{6,4},{7,5},{8,10},{9,11},{10,... | collective-permute-start | bytes 1572872 | tf_op jit(solution)/shard_map/ppermute | solution.py:714
  86.5 5.6 %collective-permute-start.14 = (bf16[64,192]{1,0:T(8,128)(2,1)S(1)}, bf16[64,192]{1,0:T(8,128)(2,1)S(1)}, u32[]{:S(2)}, u32[]{:S(2)}) collective-permute-start(bf16[64,192]{1,0:T(8,128)(2,1)S(1)} %fusion.3), channel_id=1, source_target_pairs={{0,1},{1,0},{2,3},{3,2},{4,5},{5,4},{6,7},{7,6},{8,9},{9,8},{10,11... | collective-permute-start | bytes 73736 | tf_op jit(solution)/shard_map/ppermute | solution.py:714
  86.6 32.1 %all-to-all-start.1 = ((bf16[8,384,128]{2,1,0:T(8,128)(2,1)}), bf16[8,384,128]{2,1,0:T(8,128)(2,1)S(1)}, u32[]{:S(2)}, u32[]{:S(2)}) async-start(bf16[8,384,128]{2,1,0:T(8,128)(2,1)} %shard_map.87), calls=%async_computation.1 | async-start | bytes 1572864 | tf_op jit(solution)/shard_map/all_to_all | solution.py:765
  90.2 13.8 %collective-permute-start.15 = (bf16[2,192,128]{2,1,0:T(8,128)(2,1)S(1)}, bf16[2,192,128]{2,1,0:T(8,128)(2,1)S(1)}, u32[]{:S(2)}, u32[]{:S(2)}) collective-permute-start(bf16[2,192,128]{2,1,0:T(8,128)(2,1)S(1)} %get-tuple-element.57), channel_id=1, source_target_pairs={{0,4},{1,5},{2,6},{3,7},{4,0},{5,1},{6,2},{7,3},{8,12},{9,13},{10,... | collective-permute-start | bytes 294920 | tf_op jit(solution)/shard_map/ppermute | solution.py:714
  92.2 17.8 %copy-start.12 = (bf16[64,192]{1,0:T(8,128)(2,1)}, bf16[64,192]{1,0:T(8,128)(2,1)S(1)}, u32[]{:S(2)}) copy-start(bf16[64,192]{1,0:T(8,128)(2,1)S(1)} %fusion.2.own_rank) | copy-start | bytes 73732
  104.1 4.7 %collective-permute-start.16 = (bf16[64,128]{1,0:T(8,128)(2,1)S(1)}, bf16[64,128]{1,0:T(8,128)(2,1)S(1)}, u32[]{:S(2)}, u32[]{:S(2)}) collective-permute-start(bf16[64,128]{1,0:T(8,128)(2,1)S(1)} %slice.51), channel_id=1, source_target_pairs={{0,8},{1,9},{2,10},{3,11},{4,12},{5,13},{6,14},{7,15},{8,0},{9,1},... | collective-permute-start | bytes 49160 | tf_op jit(solution)/shard_map/ppermute | solution.py:714
  110.0 24.5 %collective-permute-start.17 = (bf16[4,2,64,1024]{3,2,1,0:T(8,128)(2,1)}, bf16[4,2,64,1024]{3,2,1,0:T(8,128)(2,1)}, u32[]{:S(2)}, u32[]{:S(2)}) collective-permute-start(bf16[4,2,64,1024]{3,2,1,0:T(8,128)(2,1)} %bitcast.6.key_same.value_same), channel_id=1, source_target_pairs={{0,1},{1,0},{2,3},{3,2},{4,5},{5,4},{6,7},{7,6},{8,9},{9,8},{10,11... | collective-permute-start | bytes 3145736 | tf_op jit(solution)/shard_map/ppermute | solution.py:714
  110.0 8.4 %collective-permute-start.21 = (bf16[2,2,192,128]{3,2,1,0:T(8,128)(2,1)S(1)}, bf16[2,2,192,128]{3,2,1,0:T(8,128)(2,1)S(1)}, u32[]{:S(2)}, u32[]{:S(2)}) collective-permute-start(bf16[2,2,192,128]{3,2,1,0:T(8,128)(2,1)S(1)} %pad_maximum_fusion.12), channel_id=1, source_target_pairs={{0,2},{1,3},{2,0},{3,1},{4,6},{5,7},{6,4},{7,5},{8,10},{9,11},{10,... | collective-permute-start | bytes 589832 | tf_op jit(solution)/shard_map/ppermute | solution.py:714
  111.4 7.1 %collective-permute-start.20 = (bf16[2,64,128]{2,1,0:T(8,128)(2,1)S(1)}, bf16[2,64,128]{2,1,0:T(8,128)(2,1)S(1)}, u32[]{:S(2)}, u32[]{:S(2)}) collective-permute-start(bf16[2,64,128]{2,1,0:T(8,128)(2,1)S(1)} %pad_maximum_fusion.15), channel_id=1, source_target_pairs={{0,6},{1,7},{2,4},{3,5},{4,2},{5,3},{6,0},{7,1},{8,14},{9,15},{10,... | collective-permute-start | bytes 98312 | tf_op jit(solution)/shard_map/ppermute | solution.py:714
  111.7 6.9 %collective-permute-start.19 = (bf16[2,64,128]{2,1,0:T(8,128)(2,1)S(1)}, bf16[2,64,128]{2,1,0:T(8,128)(2,1)S(1)}, u32[]{:S(2)}, u32[]{:S(2)}) collective-permute-start(bf16[2,64,128]{2,1,0:T(8,128)(2,1)S(1)} %pad_maximum_fusion.15), channel_id=1, source_target_pairs={{0,4},{1,5},{2,6},{3,7},{4,0},{5,1},{6,2},{7,3},{8,12},{9,13},{10,... | collective-permute-start | bytes 98312 | tf_op jit(solution)/shard_map/ppermute | solution.py:714
  113.5 5.2 %collective-permute-start.18 = (bf16[2,64,128]{2,1,0:T(8,128)(2,1)S(1)}, bf16[2,64,128]{2,1,0:T(8,128)(2,1)S(1)}, u32[]{:S(2)}, u32[]{:S(2)}) collective-permute-start(bf16[2,64,128]{2,1,0:T(8,128)(2,1)S(1)} %pad_maximum_fusion.15), channel_id=1, source_target_pairs={{0,2},{1,3},{2,0},{3,1},{4,6},{5,7},{6,4},{7,5},{8,10},{9,11},{10,... | collective-permute-start | bytes 98312 | tf_op jit(solution)/shard_map/ppermute | solution.py:714
  118.4 16.1 %copy-start.11 = (bf16[2,2,2,192,128]{4,3,2,1,0:T(8,128)(2,1)}, bf16[2,2,2,192,128]{4,3,2,1,0:T(8,128)(2,1)S(1)}, u32[]{:S(2)}) copy-start(bf16[2,2,2,192,128]{4,3,2,1,0:T(8,128)(2,1)S(1)} %copy.11) | copy-start | bytes 1179652
  118.4 16.1 %collective-permute-start.23 = (bf16[4,2,192,128]{3,2,1,0:T(8,128)(2,1)S(1)}, bf16[4,2,192,128]{3,2,1,0:T(8,128)(2,1)S(1)}, u32[]{:S(2)}, u32[]{:S(2)}) collective-permute-start(bf16[4,2,192,128]{3,2,1,0:T(8,128)(2,1)S(1)} %bitcast.42), channel_id=1, source_target_pairs={{0,1},{1,0},{2,3},{3,2},{4,5},{5,4},{6,7},{7,6},{8,9},{9,8},{10,11... | collective-permute-start | bytes 1179656 | tf_op jit(solution)/shard_map/ppermute | solution.py:714
  119.9 2.7 %collective-permute-start.22 = (bf16[4,2,64,128]{3,2,1,0:T(8,128)(2,1)S(1)}, bf16[4,2,64,128]{3,2,1,0:T(8,128)(2,1)S(1)}, u32[]{:S(2)}, u32[]{:S(2)}) collective-permute-start(bf16[4,2,64,128]{3,2,1,0:T(8,128)(2,1)S(1)} %pad_maximum_fusion.14), channel_id=1, source_target_pairs={{0,1},{1,0},{2,3},{3,2},{4,5},{5,4},{6,7},{7,6},{8,9},{9,8},{10,11... | collective-permute-start | bytes 393224 | tf_op jit(solution)/shard_map/ppermute | solution.py:714
  120.3 11.8 %collective-permute-start.24 = (bf16[2,384,128]{2,1,0:T(8,128)(2,1)S(1)}, bf16[2,384,128]{2,1,0:T(8,128)(2,1)S(1)}, u32[]{:S(2)}, u32[]{:S(2)}) collective-permute-start(bf16[2,384,128]{2,1,0:T(8,128)(2,1)S(1)} %get-tuple-element.66), channel_id=1, source_target_pairs={{0,8},{1,9},{2,10},{3,11},{4,12},{5,13},{6,14},{7,15},{8,0},{9,1},... | collective-permute-start | bytes 589832 | tf_op jit(solution)/shard_map/ppermute | solution.py:714
  132.8 6.9 %collective-permute-start.25 = (bf16[384,128]{1,0:T(8,128)(2,1)S(1)}, bf16[384,128]{1,0:T(8,128)(2,1)S(1)}, u32[]{:S(2)}, u32[]{:S(2)}) collective-permute-start(bf16[384,128]{1,0:T(8,128)(2,1)S(1)} %get-tuple-element.69), channel_id=1, source_target_pairs={{0,16},{1,17},{2,18},{3,19},{4,20},{5,21},{6,22},{7,23},{8,24},{9,... | collective-permute-start | bytes 294920 | tf_op jit(solution)/shard_map/ppermute | solution.py:714
  134.5 0.8 copy-start.13
  139.8 12.3 %collective-permute-start.28 = (bf16[2,384,128]{2,1,0:T(8,128)(2,1)S(1)}, bf16[2,384,128]{2,1,0:T(8,128)(2,1)S(1)}, u32[]{:S(2)}, u32[]{:S(2)}) collective-permute-start(bf16[2,384,128]{2,1,0:T(8,128)(2,1)S(1)} %pad_maximum_fusion.13), channel_id=1, source_target_pairs={{0,6},{1,7},{2,4},{3,5},{4,2},{5,3},{6,0},{7,1},{8,14},{9,15},{10,... | collective-permute-start | bytes 589832 | tf_op jit(solution)/shard_map/ppermute | solution.py:714
  140.5 11.5 %collective-permute-start.27 = (bf16[2,384,128]{2,1,0:T(8,128)(2,1)S(1)}, bf16[2,384,128]{2,1,0:T(8,128)(2,1)S(1)}, u32[]{:S(2)}, u32[]{:S(2)}) collective-permute-start(bf16[2,384,128]{2,1,0:T(8,128)(2,1)S(1)} %pad_maximum_fusion.13), channel_id=1, source_target_pairs={{0,4},{1,5},{2,6},{3,7},{4,0},{5,1},{6,2},{7,3},{8,12},{9,13},{10,... | collective-permute-start | bytes 589832 | tf_op jit(solution)/shard_map/ppermute | solution.py:714
  142.9 9.1 %collective-permute-start.26 = (bf16[2,384,128]{2,1,0:T(8,128)(2,1)S(1)}, bf16[2,384,128]{2,1,0:T(8,128)(2,1)S(1)}, u32[]{:S(2)}, u32[]{:S(2)}) collective-permute-start(bf16[2,384,128]{2,1,0:T(8,128)(2,1)S(1)} %pad_maximum_fusion.13), channel_id=1, source_target_pairs={{0,2},{1,3},{2,0},{3,1},{4,6},{5,7},{6,4},{7,5},{8,10},{9,11},{10,... | collective-permute-start | bytes 589832 | tf_op jit(solution)/shard_map/ppermute | solution.py:714
  152.0 2.5 %copy-start.2 = (bf16[64,4096]{1,0:T(8,128)(2,1)S(1)}, bf16[64,4096]{1,0:T(8,128)(2,1)}, u32[]{:S(2)}) copy-start(bf16[64,4096]{1,0:T(8,128)(2,1)} %shard_map.94.attended) | copy-start | bytes 1572868
  152.2 2.4 %collective-permute-start.29 = (bf16[4,2,384,128]{3,2,1,0:T(8,128)(2,1)S(1)}, bf16[4,2,384,128]{3,2,1,0:T(8,128)(2,1)S(1)}, u32[]{:S(2)}, u32[]{:S(2)}) collective-permute-start(bf16[4,2,384,128]{3,2,1,0:T(8,128)(2,1)S(1)} %pad_maximum_fusion.1.same), channel_id=1, source_target_pairs={{0,1},{1,0},{2,3},{3,2},{4,5},{5,4},{6,7},{7,6},{8,9},{9,8},{10,11... | collective-permute-start | bytes 2359304 | tf_op jit(solution)/shard_map/ppermute | solution.py:714

commit v9 on v8

--- a/solution.py
+++ b/solution.py
@@ -264,10 +264,10 @@
 
 PIECES = 8
 GROUP = QH // KEYVALUE_HEADS
-FIRST = ((0, 12288), (12288, 2048), (14336, 512))
-SECOND = ((14848, 2048), (16896, 4096))
+SECTIONS = ((0, 12288), (12288, 2048), (14336, 512), (14848, 2048), (16896, 4096))
 DOWN_ROWS, QUERY_ROWS, KEYVAL_ROWS, DOWN_OUT_ROWS, UP_OUT_ROWS = 768, 128, 32, 128, 256
 UP_ROWS = QUERY_ROWS + 2 * KEYVAL_ROWS
+FIRST_ROWS = DOWN_ROWS + QUERY_ROWS + KEYVAL_ROWS
 
 
 def pack_kernel(sections, pool, *refs):
@@ -327,48 +327,46 @@
     )(pool, *after)
 
 
-def pick_kernel(mirrored, here, there, owner, spread, *refs):
-    sems = refs[-1]
-    outs = refs[:4] if len(refs) > 3 else [refs[flip % 2].at[flip // 2] for flip in range(4)]
+def pick_kernel(here, there, owner, spread, *refs):
+    outs, lasts, sems = refs[:4], refs[4:6], refs[6]
     half = lax.axis_index("ctx") // PIECES
-    rows = spread.shape[1]
+    last = spread.shape[1] - FIRST_ROWS
     copies = []
     for flip, out in enumerate(outs):
         wishes = there if flip >= 2 else here
         block = half ^ (flip & 1)
         row = lax.rem(owner[wishes[block]], PIECES)
-        copies.append(
-            pltpu.make_async_copy(spread.at[row], out.at[pl.ds(0, rows)], sems.at[flip, 0])
+        mirrored = lax.rem(owner[wishes[1 - block]], PIECES)
+        pairs = (
+            (spread.at[row, pl.ds(0, FIRST_ROWS)], out.at[pl.ds(0, FIRST_ROWS)]),
+            (
+                spread.at[mirrored, pl.ds(FIRST_ROWS - KEYVAL_ROWS, KEYVAL_ROWS)],
+                out.at[pl.ds(FIRST_ROWS, KEYVAL_ROWS)],
+            ),
+            (spread.at[row, pl.ds(FIRST_ROWS, last)], lasts[flip % 2].at[flip // 2]),
         )
-        if mirrored is not None:
-            first, count = mirrored
-            row = lax.rem(owner[wishes[1 - block]], PIECES)
-            copies.append(
-                pltpu.make_async_copy(
-                    spread.at[row, pl.ds(first, count)],
-                    out.at[pl.ds(rows, count)],
-                    sems.at[flip, 1],
-                )
-            )
+        for number, (source, target) in enumerate(pairs):
+            copies.append(pltpu.make_async_copy(source, target, sems.at[flip, number]))
     for copy in copies:
         copy.start()
     for copy in copies:
         copy.wait()
 
 
-def pick(spread, here, there, owner, mirrored):
-    rows = spread.shape[1] + (mirrored[1] if mirrored else 0)
-    shape, count = ((rows, 128), 4) if mirrored else ((2, rows, 128), 2)
-    slab = jax.ShapeDtypeStruct(shape, jnp.bfloat16)
-    return pl.pallas_call(
-        partial(pick_kernel, mirrored),
-        out_shape=(slab,) * count,
+def pick(spread, here, there, owner):
+    last = spread.shape[1] - FIRST_ROWS
+    first_shape = jax.ShapeDtypeStruct((FIRST_ROWS + KEYVAL_ROWS, 128), jnp.bfloat16)
+    last_shape = jax.ShapeDtypeStruct((2, last, 128), jnp.bfloat16)
+    outs = pl.pallas_call(
+        pick_kernel,
+        out_shape=(first_shape,) * 4 + (last_shape,) * 2,
         in_specs=[pl.BlockSpec(memory_space=pltpu.SMEM)] * 3 + [pl.BlockSpec(memory_space=pl.ANY)],
-        out_specs=(pl.BlockSpec(memory_space=pltpu.VMEM),) * count,
-        scratch_shapes=[pltpu.SemaphoreType.DMA((4, 2))],
+        out_specs=(pl.BlockSpec(memory_space=pltpu.VMEM),) * 6,
+        scratch_shapes=[pltpu.SemaphoreType.DMA((4, 3))],
         compiler_params=pltpu.CompilerParams(vmem_limit_bytes=16 << 20),
-        cost_estimate=pl.CostEstimate(flops=0, bytes_accessed=2 << 20, transcendentals=0),
+        cost_estimate=pl.CostEstimate(flops=0, bytes_accessed=3 << 20, transcendentals=0),
     )(here, there, owner, spread)
+    return outs[:4], outs[4], outs[5]
 
 
 def deal_kernel(rows, even, odd, sems):
@@ -733,7 +731,8 @@
         return lax.optimization_barrier((block, others))[0]
 
     def exchange(sent):
-        return [swap(block, flip * PIECES) if flip else block for flip, block in enumerate(sent)]
+        across = swap(sent[2], 2 * PIECES)
+        return [sent[0], swap(sent[1], PIECES), across, swap(sent[3], 3 * PIECES)]
 
     def along_z(block):
         return jnp.stack([block, swap(block, 4)])
@@ -743,48 +742,45 @@
         return quad.reshape((PIECES // 2,) + pair.shape[1:])
 
     elsewhere = swap(stretch_adapter, 2 * PIECES)
-    packed = pack_row(adapter_pool, FIRST)
-    packed_second = pack_row(adapter_pool, SECOND, packed)
+    packed = pack_row(adapter_pool, SECTIONS)
     even, odd = deal(normed_input, packed)
     sibling = swap(odd, 1)
     base = jnp.concatenate([key_base, value_base], 1)
     base = jnp.stack([base, swap(base, PIECES)])
-    packed = after(packed, base)
 
     spread = lax.all_to_all(packed, "ctx", 0, 0, axis_index_groups=blocks)
-    spread = after(spread, packed_second, sibling)
-    sent = pick(spread, stretch_adapter, elsewhere, adapter_owner, (896, KEYVAL_ROWS))
+    spread = after(spread, sibling, base, cosines, sines)
+    sent, near, far = pick(spread, stretch_adapter, elsewhere, adapter_owner)
     arrived = exchange(sent)
     dealt = [after(jnp.stack([even[j], sibling[j]]), sent) for j in range(PIECES // 2)]
     dealt = [swap(block, 2 * j) if j else block for j, block in enumerate(dealt)]
-    base = along_z(after(base, sent))
 
     weight, ups = join(stretch_adapter, adapter_owner, arrived)
-    partial_sums = narrow(after(weight, base, cosines, sines), dealt)
-    packed_second = after(packed_second, *partial_sums)
-    spread = lax.all_to_all(packed_second, "ctx", 0, 0, axis_index_groups=blocks)
+    far = swap(after(far, weight), PIECES)
+    partial_sums = narrow(weight, dealt)
     back = [swap(block, 2 * j) if j else block for j, block in enumerate(partial_sums)]
     back = sum(block.astype(jnp.float32) for block in back)
-    own_rank = swap(back[1].astype(jnp.bfloat16), 1)
+    own_rank = swap(after(back[1].astype(jnp.bfloat16), far), 1)
     own_rank = back[0] + own_rank.astype(jnp.float32)
     own_rank = own_rank.astype(jnp.bfloat16)
     ups = along_z(after(ups, *partial_sums))
-    base = along_x(base)
-    all_rank = after(own_rank[:, ADAPTER_RANK:], ups)
-    near, far = pick(after(spread, all_rank), stretch_adapter, elsewhere, adapter_owner, None)
-    far = swap(far, PIECES)
+    base = along_z(after(base, *partial_sums))
+    all_rank = own_rank[:, ADAPTER_RANK:]
+    base = along_x(after(base, own_rank))
+    own, across = settle(
+        stretch_adapter, elsewhere, adapter_owner, near, after(far, own_rank)
+    )
+    ends = jnp.stack([own, swap(across, 2 * PIECES)])
     all_rank = jnp.stack([all_rank, swap(all_rank, PIECES)])
-    all_rank = after(all_rank, base)
+    all_rank = after(all_rank, ups)
     ups = along_x(after(ups, all_rank))
-    base = (base, swap(after(base, all_rank), 1))
     all_rank = jnp.stack([swap(all_rank, apart) if apart else all_rank for apart in (0, 2, 4, 6)])
-    all_rank = after(all_rank, ups, near)
+    base = after(base, all_rank)
+    base = (base, swap(base, 1))
+    all_rank = after(all_rank, ups, ends)
     ups = (ups, swap(ups, 1))
     all_rank = jnp.stack([all_rank, swap(all_rank, 1)])
 
-    far = after(far, all_rank)
-    own, across = settle(stretch_adapter, elsewhere, adapter_owner, near, far)
-    ends = jnp.stack([own, swap(across, 2 * PIECES)])
     shared = (query_base, base, own_rank, all_rank, ups, cosines, sines)
     attended = attend(0, 1, None, *shared)
     ends = after(ends, attended)

time: 158 us -> 143 us (0.905)
  waiting for transfers between devices: 71.8 us -> 62.6 us
  Pallas kernels: 28.5 us -> 25.9 us
    all_to_all x1, waiting for transfers between devices: 15.4 us -> 2.14 us  [direct_shards(): spread = lax.all_to_all(packed, 'ctx', 0, 0, axis_index_groups=blocks)]
    ppermute x30, waiting for transfers between devices: 56.4 us -> 60.4 us  [swap(): lax.ppermute(block, ('groups', 'ctx'), [(i, i ^ mask) for i in range(4 *...]
    all_to_all x1 -> x0, starting transfers between devices: 3.56 us -> none  [direct_shards(): lax.all_to_all(packed_second, 'ctx', 0, 0, axis_index_groups=blocks)]
    unnamed x29 -> x23, local copies, waits for them, and re-layouts: 1.66 us -> 3.53 us
    ppermute x30, starting transfers between devices: 37.6 us -> 39.2 us  [swap(): lax.ppermute(block, ('groups', 'ctx'), [(i, i ^ mask) for i in range(4 *...]
    pallas_call x2 -> x1, Pallas kernels: 6.68 us -> 5.16 us  [pack_row(): pl.pallas_call(partial(pack_kernel, sections), out_shape=jax.ShapeDtypeSt...]
  transfers between devices with their start and end apart: 32 -> 31, of which waited for: 14 -> 16; matrix products, arithmetic and copies ran while one was open for 5% -> 3% of each run, Pallas kernels for 15% -> 8%
where the time goes in v9:
time: 143 us; the launch traced here: 142 us
  waiting for transfers between devices  62.6 us (44%)
  starting transfers between devices  44.8 us (31%)
  Pallas kernels  25.9 us (18%)
  other arithmetic  4.49 us (3%)
  local copies, waits for them, and re-layouts  3.78 us (3%)
    ppermute x30, waiting for transfers between devices, swap(): lax.ppermute(block, ('groups', 'ctx'), [(i, i ^ mask) for i in range(4 *...  60.4 us
    ppermute x30, starting transfers between devices, swap(): lax.ppermute(block, ('groups', 'ctx'), [(i, i ^ mask) for i in range(4 *...  39.2 us
    pallas_call x2, Pallas kernels, attend(): pl.pallas_call(partial(attend_kernel, first_head), grid=(heads,), out_sha...  13.2 us
    all_to_all x1, starting transfers between devices, direct_shards(): spread = lax.all_to_all(packed, 'ctx', 0, 0, axis_index_groups=blocks)  5.5 us
    pallas_call x1, Pallas kernels, pack_row(): pl.pallas_call(partial(pack_kernel, sections), out_shape=jax.ShapeDtypeSt...  5.16 us
    unnamed x23, local copies, waits for them, and re-layouts  3.53 us
    pallas_call x1, Pallas kernels, widen(): pl.pallas_call(widen_kernel, out_shape=jax.ShapeDtypeStruct((attended.sha...  2.98 us
  transfers between devices with their start and end apart: 31, of which 16 were waited for; matrix products, arithmetic and copies ran while one was open for 3% of the time, Pallas kernels for 8%

profile of v9, /device:TPU:0, one launch (start us, length us, event | category | flops | bytes accessed | tf_op | source)
XLA Modules:
  0.0 142.4 jit_solution(6205376630160570797)
XLA Ops:
  0.6 5.2 %shard_map.86.refs_0_ = bf16[8,1312,128]{2,1,0:T(8,128)(2,1)} custom-call(bf16[1,2686976]{1,0:T(2,128)(2,1)} %pool.1), custom_call_target="tpu_custom_call" | custom-call | bytes 8388608 | tf_op jit(solution)/shard_map/pallas_call | solution.py:316
  5.8 5.5 %all-to-all-start = ((bf16[8,1312,128]{2,1,0:T(8,128)(2,1)}), bf16[8,1312,128]{2,1,0:T(8,128)(2,1)}, u32[]{:S(2)}, u32[]{:S(2)}) async-start(bf16[8,1312,128]{2,1,0:T(8,128)(2,1)} %shard_map.86.refs_0_), calls=%async_computation | async-start | bytes 5373952 | tf_op jit(solution)/shard_map/all_to_all | solution.py:751
  11.3 2.2 %collective-permute-start.1 = (s32[2]{0:T(128)S(1)}, s32[2]{0:T(128)S(1)}, u32[]{:S(2)}, u32[]{:S(2)}) collective-permute-start(s32[2]{0:T(128)S(1)} %copy-done.3), channel_id=1, source_target_pairs={{0,16},{1,17},{2,18},{3,19},{4,20},{5,21},{6,22},{7,23},{8,24},{9,... | collective-permute-start | bytes 32 | tf_op jit(solution)/shard_map/ppermute | solution.py:712
  13.5 1.2 copy-done.1
  14.8 0.3 shard_map.87
  15.0 0.1 collective-permute-start.2
  15.1 0.5 copy-done.8
  15.7 2.6 %collective-permute-start = (bf16[64,1024]{1,0:T(8,128)(2,1)S(1)}, bf16[64,1024]{1,0:T(8,128)(2,1)S(1)}, u32[]{:S(2)}, u32[]{:S(2)}) collective-permute-start(bf16[64,1024]{1,0:T(8,128)(2,1)S(1)} %constant_dynamic-update-slice_fusion), channel_id=1, source_target_pairs={{0,8},{1,9},{2,10},{3,11},{4,12},{5,13},{6,14},{7,15},{8,0},{9,1},... | collective-permute-start | bytes 393224 | tf_op jit(solution)/shard_map/ppermute | solution.py:712
  18.4 1.9 %fusion = (f32[1024,64]{1,0:T(8,128)S(1)}, f32[1024,64]{1,0:T(8,128)S(1)}, f32[1024,64]{1,0:T(8,128)S(1)}) fusion(f32[64]{0:T(128)S(1)} %multiply_power_fusion, f32[1024]{0:T(1024)S(1)} %iota_convert_fusion), kind=kLoop, calls=%fused_computation.16 | loop fusion | flops 131072 | bytes 790784 | tf_op jit(solution)/shard_map/neg | solution.py:728
  20.3 1.3 pad_maximum_fusion.2
  21.6 22.5 %collective-permute-done = bf16[64,1024]{1,0:T(8,128)(2,1)S(1)} collective-permute-done((bf16[64,1024]{1,0:T(8,128)(2,1)S(1)}, bf16[64,1024]{1,0:T(8,128)(2,1)S(1)}, u32[]{:S(2)}, u32[]{:S(2)}) %collective-permute-start) | collective-permute-done | bytes 131104 | tf_op jit(solution)/shard_map/ppermute | solution.py:712
  44.2 2.1 %all-to-all-done.spread = bf16[8,1312,128]{2,1,0:T(8,128)(2,1)} async-done(((bf16[8,1312,128]{2,1,0:T(8,128)(2,1)}), bf16[8,1312,128]{2,1,0:T(8,128)(2,1)}, u32[]{:S(2)}, u32[]{:S(2)}) %all-to-all-start) | async-done | bytes 2687008 | tf_op jit(solution)/shard_map/all_to_all | solution.py:751
  46.3 2.1 %shard_map.88 = (bf16[960,128]{1,0:T(8,128)(2,1)S(1)}, bf16[960,128]{1,0:T(8,128)(2,1)S(1)}, bf16[960,128]{1,0:T(8,128)(2,1)S(1)}, bf16[960,128]{1,0:T(8,128)(2,...) custom-call(s32[2]{0:T(128)S(1)} %copy-done.3, s32[2]{0:T(128)S(1)} %collective-permute-done.1.there, ...), custom_call_target="tpu_custom_call" | custom-call | bytes 3145728 | tf_op jit(solution)/shard_map/pallas_call | solution.py:360
  48.4 1.3 collective-permute-start.3
  49.9 1.7 %collective-permute-start.6 = (bf16[2,64,1024]{2,1,0:T(8,128)(2,1)S(1)}, bf16[2,64,1024]{2,1,0:T(8,128)(2,1)S(1)}, u32[]{:S(2)}, u32[]{:S(2)}) collective-permute-start(bf16[2,64,1024]{2,1,0:T(8,128)(2,1)S(1)} %get-tuple-element.44), channel_id=1, source_target_pairs={{0,2},{1,3},{2,0},{3,1},{4,6},{5,7},{6,4},{7,5},{8,10},{9,11},{10,... | collective-permute-start | bytes 786440 | tf_op jit(solution)/shard_map/ppermute | solution.py:712
  51.5 2.2 %collective-permute-start.7 = (bf16[2,64,1024]{2,1,0:T(8,128)(2,1)S(1)}, bf16[2,64,1024]{2,1,0:T(8,128)(2,1)S(1)}, u32[]{:S(2)}, u32[]{:S(2)}) collective-permute-start(bf16[2,64,1024]{2,1,0:T(8,128)(2,1)S(1)} %get-tuple-element.45), channel_id=1, source_target_pairs={{0,4},{1,5},{2,6},{3,7},{4,0},{5,1},{6,2},{7,3},{8,12},{9,13},{10,... | collective-permute-start | bytes 786440 | tf_op jit(solution)/shard_map/ppermute | solution.py:712
  53.8 1.7 %collective-permute-start.4 = (bf16[960,128]{1,0:T(8,128)(2,1)S(1)}, bf16[960,128]{1,0:T(8,128)(2,1)S(1)}, u32[]{:S(2)}, u32[]{:S(2)}) collective-permute-start(bf16[960,128]{1,0:T(8,128)(2,1)S(1)} %get-tuple-element.39), channel_id=1, source_target_pairs={{0,16},{1,17},{2,18},{3,19},{4,20},{5,21},{6,22},{7,23},{8,24},{9,... | collective-permute-start | bytes 737288 | tf_op jit(solution)/shard_map/ppermute | solution.py:712
  55.4 6.7 %collective-permute-done.3.refs_1_ = bf16[960,128]{1,0:T(8,128)(2,1)S(1)} collective-permute-done((bf16[960,128]{1,0:T(8,128)(2,1)S(1)}, bf16[960,128]{1,0:T(8,128)(2,1)S(1)}, u32[]{:S(2)}, u32[]{:S(2)}) %collective-permute-start.3) | collective-permute-done | bytes 245792 | tf_op jit(solution)/shard_map/ppermute | solution.py:712
  62.2 1.0 collective-permute-start.5
  63.2 8.4 %collective-permute-done.5.refs_3_ = bf16[960,128]{1,0:T(8,128)(2,1)S(1)} collective-permute-done((bf16[960,128]{1,0:T(8,128)(2,1)S(1)}, bf16[960,128]{1,0:T(8,128)(2,1)S(1)}, u32[]{:S(2)}, u32[]{:S(2)}) %collective-permute-start.5) | collective-permute-done | bytes 245792 | tf_op jit(solution)/shard_map/ppermute | solution.py:712
  71.7 1.0 shard_map.89
  72.6 1.1 collective-permute-done.8.refs_3_
  73.8 0.4 shard_map.90
  74.2 5.7 %collective-permute-start.12 = (bf16[2,64,192]{2,1,0:T(8,128)(2,1)S(1)}, bf16[2,64,192]{2,1,0:T(8,128)(2,1)S(1)}, u32[]{:S(2)}, u32[]{:S(2)}) collective-permute-start(bf16[2,64,192]{2,1,0:T(8,128)(2,1)S(1)} %get-tuple-element.50), channel_id=1, source_target_pairs={{0,6},{1,7},{2,4},{3,5},{4,2},{5,3},{6,0},{7,1},{8,14},{9,15},{10,... | collective-permute-start | bytes 147464 | tf_op jit(solution)/shard_map/ppermute | solution.py:712
  79.9 0.6 collective-permute-start.10
  80.5 2.8 %collective-permute-start.13 = (bf16[2,384,128]{2,1,0:T(8,128)(2,1)S(1)}, bf16[2,384,128]{2,1,0:T(8,128)(2,1)S(1)}, u32[]{:S(2)}, u32[]{:S(2)}) collective-permute-start(bf16[2,384,128]{2,1,0:T(8,128)(2,1)S(1)} %get-tuple-element.53), channel_id=1, source_target_pairs={{0,8},{1,9},{2,10},{3,11},{4,12},{5,13},{6,14},{7,15},{8,0},{9,1},... | collective-permute-start | bytes 589832 | tf_op jit(solution)/shard_map/ppermute | solution.py:712
  83.3 2.0 %collective-permute-start.9 = (bf16[2,64,1024]{2,1,0:T(8,128)(2,1)S(1)}, bf16[2,64,1024]{2,1,0:T(8,128)(2,1)S(1)}, u32[]{:S(2)}, u32[]{:S(2)}) collective-permute-start(bf16[2,64,1024]{2,1,0:T(8,128)(2,1)S(1)} %pad_maximum_fusion.6), channel_id=1, source_target_pairs={{0,4},{1,5},{2,6},{3,7},{4,0},{5,1},{6,2},{7,3},{8,12},{9,13},{10,... | collective-permute-start | bytes 786440 | tf_op jit(solution)/shard_map/ppermute | solution.py:712
  85.3 0.3 collective-permute-done.11
  85.7 5.6 %collective-permute-done.13.far = bf16[2,384,128]{2,1,0:T(8,128)(2,1)S(1)} collective-permute-done((bf16[2,384,128]{2,1,0:T(8,128)(2,1)S(1)}, bf16[2,384,128]{2,1,0:T(8,128)(2,1)S(1)}, u32[]{:S(2)}, u32[]{:S(2)}) %collective-permute-start.13) | collective-permute-done | bytes 196640 | tf_op jit(solution)/shard_map/ppermute | solution.py:712
  91.3 0.7 collective-permute-start.17
  92.0 0.5 collective-permute-done.14
  92.6 0.8 collective-permute-done.9
  93.4 1.3 collective-permute-start.15
  94.7 0.1 slice_bitcast_fusion.1
  94.7 2.1 %collective-permute-start.16 = (bf16[64,128]{1,0:T(8,128)(2,1)S(1)}, bf16[64,128]{1,0:T(8,128)(2,1)S(1)}, u32[]{:S(2)}, u32[]{:S(2)}) collective-permute-start(bf16[64,128]{1,0:T(8,128)(2,1)S(1)} %get-tuple-element.77), channel_id=1, source_target_pairs={{0,8},{1,9},{2,10},{3,11},{4,12},{5,13},{6,14},{7,15},{8,0},{9,1},... | collective-permute-start | bytes 49160 | tf_op jit(solution)/shard_map/ppermute | solution.py:712
  96.8 2.6 %collective-permute-done.16 = bf16[64,128]{1,0:T(8,128)(2,1)S(1)} collective-permute-done((bf16[64,128]{1,0:T(8,128)(2,1)S(1)}, bf16[64,128]{1,0:T(8,128)(2,1)S(1)}, u32[]{:S(2)}, u32[]{:S(2)}) %collective-permute-start.16) | collective-permute-done | bytes 16416 | tf_op jit(solution)/shard_map/ppermute | solution.py:712
  99.4 1.7 %collective-permute-start.20 = (bf16[2,64,128]{2,1,0:T(8,128)(2,1)S(1)}, bf16[2,64,128]{2,1,0:T(8,128)(2,1)S(1)}, u32[]{:S(2)}, u32[]{:S(2)}) collective-permute-start(bf16[2,64,128]{2,1,0:T(8,128)(2,1)S(1)} %pad_maximum_fusion.15), channel_id=1, source_target_pairs={{0,6},{1,7},{2,4},{3,5},{4,2},{5,3},{6,0},{7,1},{8,14},{9,15},{10,... | collective-permute-start | bytes 98312 | tf_op jit(solution)/shard_map/ppermute | solution.py:712
  101.0 0.6 collective-permute-start.19
  101.7 1.2 collective-permute-start.18
  102.9 1.4 %collective-permute-done.20 = bf16[2,64,128]{2,1,0:T(8,128)(2,1)S(1)} collective-permute-done((bf16[2,64,128]{2,1,0:T(8,128)(2,1)S(1)}, bf16[2,64,128]{2,1,0:T(8,128)(2,1)S(1)}, u32[]{:S(2)}, u32[]{:S(2)}) %collective-permute-start.20) | collective-permute-done | bytes 32800 | tf_op jit(solution)/shard_map/ppermute | solution.py:712
  104.3 0.7 collective-permute-done.19
  105.0 3.1 %collective-permute-done.18 = bf16[2,64,128]{2,1,0:T(8,128)(2,1)S(1)} collective-permute-done((bf16[2,64,128]{2,1,0:T(8,128)(2,1)S(1)}, bf16[2,64,128]{2,1,0:T(8,128)(2,1)S(1)}, u32[]{:S(2)}, u32[]{:S(2)}) %collective-permute-start.18) | collective-permute-done | bytes 32800 | tf_op jit(solution)/shard_map/ppermute | solution.py:712
  108.1 0.1 pad_maximum_fusion
  108.2 0.1 copy.10
  108.3 0.1 collective-permute-start.21
  108.4 1.3 collective-permute-start.22
  109.7 0.8 shard_map.91
  110.5 2.3 %collective-permute-start.23 = (bf16[384,128]{1,0:T(8,128)(2,1)S(1)}, bf16[384,128]{1,0:T(8,128)(2,1)S(1)}, u32[]{:S(2)}, u32[]{:S(2)}) collective-permute-start(bf16[384,128]{1,0:T(8,128)(2,1)S(1)} %get-tuple-element.64), channel_id=1, source_target_pairs={{0,16},{1,17},{2,18},{3,19},{4,20},{5,21},{6,22},{7,23},{8,24},{9,... | collective-permute-start | bytes 294920 | tf_op jit(solution)/shard_map/ppermute | solution.py:712
  112.8 3.0 %collective-permute-done.22 = bf16[2,2,192,128]{3,2,1,0:T(8,128)(2,1)S(1)} collective-permute-done((bf16[2,2,192,128]{3,2,1,0:T(8,128)(2,1)S(1)}, bf16[2,2,192,128]{3,2,1,0:T(8,128)(2,1)S(1)}, u32[]{:S(2)}, u32[]{:S(2)}) %collective-permute-start.22) | collective-permute-done | bytes 196640 | tf_op jit(solution)/shard_map/ppermute | solution.py:712
  115.8 0.1 collective-permute-start.25
  115.9 0.5 collective-permute-start.24
  116.5 1.3 collective-permute-done.24
  117.8 0.7 pad_maximum_fusion.11.all_rank
  118.6 0.7 copy-done.10
  119.3 4.5 %shard_map.92.refs_0_ = bf16[64,4096]{1,0:T(8,128)(2,1)} custom-call(bf16[64,4096]{1,0:T(8,128)(2,1)} %query_block.3, bf16[4,2,64,1024]{3,2,1,0:T(8,128)(2,1)} %bitcast.39, bf16[4,2,64,1024]{3,2,1,0:T(8,128)(2,1)} %collective-permute-done.21.key_other.value_other, bf16[4,2,64,1024]{3,2,1,0:T(8,128)(2,1)} %bitcast.40, ...), custom_call_target="tpu_custom_call" | custom-call | flops 3221225472 | bytes 10485760 | tf_op jit(solution)/shard_map/pallas_call | solution.py:634
  123.8 1.5 %collective-permute-start.28 = (bf16[2,384,128]{2,1,0:T(8,128)(2,1)S(1)}, bf16[2,384,128]{2,1,0:T(8,128)(2,1)S(1)}, u32[]{:S(2)}, u32[]{:S(2)}) collective-permute-start(bf16[2,384,128]{2,1,0:T(8,128)(2,1)S(1)} %pad_maximum_fusion.13), channel_id=1, source_target_pairs={{0,6},{1,7},{2,4},{3,5},{4,2},{5,3},{6,0},{7,1},{8,14},{9,15},{10,... | collective-permute-start | bytes 589832 | tf_op jit(solution)/shard_map/ppermute | solution.py:712
  125.3 1.1 collective-permute-start.27
  126.4 0.8 collective-permute-start.26
  127.2 8.7 %shard_map.93.attended = bf16[64,4096]{1,0:T(8,128)(2,1)} custom-call(bf16[64,4096]{1,0:T(8,128)(2,1)} %query_block.3, bf16[4,2,64,1024]{3,2,1,0:T(8,128)(2,1)} %bitcast.41, bf16[4,2,64,1024]{3,2,1,0:T(8,128)(2,1)} %collective-permute-done.21.key_other.value_other, bf16[4,2,64,1024]{3,2,1,0:T(8,128)(2,1)} %bitcast.42, ...), custom_call_target="tpu_custom_call", output_to_operand_aliasing={{}: (11, {})} | custom-call | flops 9663676416 | bytes 10485760 | tf_op jit(solution)/shard_map/pallas_call | solution.py:634
  136.0 0.1 pad_maximum_fusion.1.same
  136.1 0.1 collective-permute-start.29
  136.2 2.3 %collective-permute-done.29.other = bf16[4,2,384,128]{3,2,1,0:T(8,128)(2,1)S(1)} collective-permute-done((bf16[4,2,384,128]{3,2,1,0:T(8,128)(2,1)S(1)}, bf16[4,2,384,128]{3,2,1,0:T(8,128)(2,1)S(1)}, u32[]{:S(2)}, u32[]{:S(2)}) %collective-permute-start.29) | collective-permute-done | bytes 786464 | tf_op jit(solution)/shard_map/ppermute | solution.py:712
  138.4 1.0 copy-done.2
  139.5 3.0 %shard_map.94 = bf16[64,8192]{1,0:T(8,128)(2,1)} custom-call(bf16[64,4096]{1,0:T(8,128)(2,1)S(1)} %copy-done.2, bf16[4,2,384,128]{3,2,1,0:T(8,128)(2,1)S(1)} %pad_maximum_fusion.1.same, bf16[4,2,384,128]{3,2,1,0:T(8,128)(2,1)S(1)} %collective-permute-done.29.other), custom_call_target="tpu_custom_call" | custom-call | flops 134217728 | bytes 4194304 | tf_op jit(solution)/shard_map/pallas_call | solution.py:697
  (55 shorter events, 0.6 us)
Async XLA Ops:
  5.8 5.5 %copy-start.3 = (s32[2]{0:T(128)S(1)}, s32[2]{0:T(128)}, u32[]{:S(2)}) copy-start(s32[2]{0:T(128)} %here.5) | copy-start | bytes 28
  5.8 7.7 %copy-start = (bf16[8,1312,128]{2,1,0:T(8,128)(2,1)S(1)}, bf16[8,1312,128]{2,1,0:T(8,128)(2,1)}, u32[]{:S(2)}) copy-start(bf16[8,1312,128]{2,1,0:T(8,128)(2,1)} %shard_map.86.refs_0_) | copy-start | bytes 8060932
  5.8 40.5 %all-to-all-start = ((bf16[8,1312,128]{2,1,0:T(8,128)(2,1)}), bf16[8,1312,128]{2,1,0:T(8,128)(2,1)}, u32[]{:S(2)}, u32[]{:S(2)}) async-start(bf16[8,1312,128]{2,1,0:T(8,128)(2,1)} %shard_map.86.refs_0_), calls=%async_computation | async-start | bytes 5373952 | tf_op jit(solution)/shard_map/all_to_all | solution.py:751
  11.3 35.0 %collective-permute-start.1 = (s32[2]{0:T(128)S(1)}, s32[2]{0:T(128)S(1)}, u32[]{:S(2)}, u32[]{:S(2)}) collective-permute-start(s32[2]{0:T(128)S(1)} %copy-done.3), channel_id=1, source_target_pairs={{0,16},{1,17},{2,18},{3,19},{4,20},{5,21},{6,22},{7,23},{8,24},{9,... | collective-permute-start | bytes 32 | tf_op jit(solution)/shard_map/ppermute | solution.py:712
  13.5 1.2 copy-start.1
  14.8 0.8 copy-start.8
  14.8 0.9 copy-start.9
  15.0 29.1 %collective-permute-start.2 = (bf16[4,64,1024]{2,1,0:T(8,128)(2,1)S(1)}, bf16[4,64,1024]{2,1,0:T(8,128)(2,1)S(1)}, u32[]{:S(2)}, u32[]{:S(2)}) collective-permute-start(bf16[4,64,1024]{2,1,0:T(8,128)(2,1)S(1)} %get-tuple-element.35), channel_id=1, source_target_pairs={{0,1},{1,0},{2,3},{3,2},{4,5},{5,4},{6,7},{7,6},{8,9},{9,8},{10,11... | collective-permute-start | bytes 1572872 | tf_op jit(solution)/shard_map/ppermute | solution.py:712
  15.7 28.4 %collective-permute-start = (bf16[64,1024]{1,0:T(8,128)(2,1)S(1)}, bf16[64,1024]{1,0:T(8,128)(2,1)S(1)}, u32[]{:S(2)}, u32[]{:S(2)}) collective-permute-start(bf16[64,1024]{1,0:T(8,128)(2,1)S(1)} %constant_dynamic-update-slice_fusion), channel_id=1, source_target_pairs={{0,8},{1,9},{2,10},{3,11},{4,12},{5,13},{6,14},{7,15},{8,0},{9,1},... | collective-permute-start | bytes 393224 | tf_op jit(solution)/shard_map/ppermute | solution.py:712
  18.4 27.9 %copy-start.4 = (s32[16]{0:T(128)S(1)}, s32[16]{0:T(128)}, u32[]{:S(2)}) copy-start(s32[16]{0:T(128)} %owner.5) | copy-start | bytes 196
  48.4 13.8 %collective-permute-start.3 = (bf16[960,128]{1,0:T(8,128)(2,1)S(1)}, bf16[960,128]{1,0:T(8,128)(2,1)S(1)}, u32[]{:S(2)}, u32[]{:S(2)}) collective-permute-start(bf16[960,128]{1,0:T(8,128)(2,1)S(1)} %get-tuple-element.38), channel_id=1, source_target_pairs={{0,8},{1,9},{2,10},{3,11},{4,12},{5,13},{6,14},{7,15},{8,0},{9,1},... | collective-permute-start | bytes 737288 | tf_op jit(solution)/shard_map/ppermute | solution.py:712
  49.9 22.8 %collective-permute-start.6 = (bf16[2,64,1024]{2,1,0:T(8,128)(2,1)S(1)}, bf16[2,64,1024]{2,1,0:T(8,128)(2,1)S(1)}, u32[]{:S(2)}, u32[]{:S(2)}) collective-permute-start(bf16[2,64,1024]{2,1,0:T(8,128)(2,1)S(1)} %get-tuple-element.44), channel_id=1, source_target_pairs={{0,2},{1,3},{2,0},{3,1},{4,6},{5,7},{6,4},{7,5},{8,10},{9,11},{10,... | collective-permute-start | bytes 786440 | tf_op jit(solution)/shard_map/ppermute | solution.py:712
  51.5 21.1 %collective-permute-start.7 = (bf16[2,64,1024]{2,1,0:T(8,128)(2,1)S(1)}, bf16[2,64,1024]{2,1,0:T(8,128)(2,1)S(1)}, u32[]{:S(2)}, u32[]{:S(2)}) collective-permute-start(bf16[2,64,1024]{2,1,0:T(8,128)(2,1)S(1)} %get-tuple-element.45), channel_id=1, source_target_pairs={{0,4},{1,5},{2,6},{3,7},{4,0},{5,1},{6,2},{7,3},{8,12},{9,13},{10,... | collective-permute-start | bytes 786440 | tf_op jit(solution)/shard_map/ppermute | solution.py:712
  53.8 20.0 %collective-permute-start.8 = (bf16[2,64,1024]{2,1,0:T(8,128)(2,1)S(1)}, bf16[2,64,1024]{2,1,0:T(8,128)(2,1)S(1)}, u32[]{:S(2)}, u32[]{:S(2)}) collective-permute-start(bf16[2,64,1024]{2,1,0:T(8,128)(2,1)S(1)} %get-tuple-element.46), channel_id=1, source_target_pairs={{0,6},{1,7},{2,4},{3,5},{4,2},{5,3},{6,0},{7,1},{8,14},{9,15},{10,... | collective-permute-start | bytes 786440 | tf_op jit(solution)/shard_map/ppermute | solution.py:712
  53.8 9.4 %collective-permute-start.4 = (bf16[960,128]{1,0:T(8,128)(2,1)S(1)}, bf16[960,128]{1,0:T(8,128)(2,1)S(1)}, u32[]{:S(2)}, u32[]{:S(2)}) collective-permute-start(bf16[960,128]{1,0:T(8,128)(2,1)S(1)} %get-tuple-element.39), channel_id=1, source_target_pairs={{0,16},{1,17},{2,18},{3,19},{4,20},{5,21},{6,22},{7,23},{8,24},{9,... | collective-permute-start | bytes 737288 | tf_op jit(solution)/shard_map/ppermute | solution.py:712
  62.2 9.5 %collective-permute-start.5 = (bf16[960,128]{1,0:T(8,128)(2,1)S(1)}, bf16[960,128]{1,0:T(8,128)(2,1)S(1)}, u32[]{:S(2)}, u32[]{:S(2)}) collective-permute-start(bf16[960,128]{1,0:T(8,128)(2,1)S(1)} %get-tuple-element.40), channel_id=1, source_target_pairs={{0,24},{1,25},{2,26},{3,27},{4,28},{5,29},{6,30},{7,31},{8,16},{9,... | collective-permute-start | bytes 737288 | tf_op jit(solution)/shard_map/ppermute | solution.py:712
  74.2 11.1 %collective-permute-start.12 = (bf16[2,64,192]{2,1,0:T(8,128)(2,1)S(1)}, bf16[2,64,192]{2,1,0:T(8,128)(2,1)S(1)}, u32[]{:S(2)}, u32[]{:S(2)}) collective-permute-start(bf16[2,64,192]{2,1,0:T(8,128)(2,1)S(1)} %get-tuple-element.50), channel_id=1, source_target_pairs={{0,6},{1,7},{2,4},{3,5},{4,2},{5,3},{6,0},{7,1},{8,14},{9,15},{10,... | collective-permute-start | bytes 147464 | tf_op jit(solution)/shard_map/ppermute | solution.py:712
  79.9 5.8 %collective-permute-start.11 = (bf16[2,64,192]{2,1,0:T(8,128)(2,1)S(1)}, bf16[2,64,192]{2,1,0:T(8,128)(2,1)S(1)}, u32[]{:S(2)}, u32[]{:S(2)}) collective-permute-start(bf16[2,64,192]{2,1,0:T(8,128)(2,1)S(1)} %get-tuple-element.49), channel_id=1, source_target_pairs={{0,4},{1,5},{2,6},{3,7},{4,0},{5,1},{6,2},{7,3},{8,12},{9,13},{10,... | collective-permute-start | bytes 147464 | tf_op jit(solution)/shard_map/ppermute | solution.py:712
  79.9 5.8 %collective-permute-start.10 = (bf16[2,64,192]{2,1,0:T(8,128)(2,1)S(1)}, bf16[2,64,192]{2,1,0:T(8,128)(2,1)S(1)}, u32[]{:S(2)}, u32[]{:S(2)}) collective-permute-start(bf16[2,64,192]{2,1,0:T(8,128)(2,1)S(1)} %get-tuple-element.48), channel_id=1, source_target_pairs={{0,2},{1,3},{2,0},{3,1},{4,6},{5,7},{6,4},{7,5},{8,10},{9,11},{10,... | collective-permute-start | bytes 147464 | tf_op jit(solution)/shard_map/ppermute | solution.py:712
  80.5 10.8 %collective-permute-start.13 = (bf16[2,384,128]{2,1,0:T(8,128)(2,1)S(1)}, bf16[2,384,128]{2,1,0:T(8,128)(2,1)S(1)}, u32[]{:S(2)}, u32[]{:S(2)}) collective-permute-start(bf16[2,384,128]{2,1,0:T(8,128)(2,1)S(1)} %get-tuple-element.53), channel_id=1, source_target_pairs={{0,8},{1,9},{2,10},{3,11},{4,12},{5,13},{6,14},{7,15},{8,0},{9,1},... | collective-permute-start | bytes 589832 | tf_op jit(solution)/shard_map/ppermute | solution.py:712
  83.3 10.1 %collective-permute-start.9 = (bf16[2,64,1024]{2,1,0:T(8,128)(2,1)S(1)}, bf16[2,64,1024]{2,1,0:T(8,128)(2,1)S(1)}, u32[]{:S(2)}, u32[]{:S(2)}) collective-permute-start(bf16[2,64,1024]{2,1,0:T(8,128)(2,1)S(1)} %pad_maximum_fusion.6), channel_id=1, source_target_pairs={{0,4},{1,5},{2,6},{3,7},{4,0},{5,1},{6,2},{7,3},{8,12},{9,13},{10,... | collective-permute-start | bytes 786440 | tf_op jit(solution)/shard_map/ppermute | solution.py:712
  91.3 1.2 collective-permute-start.14
  91.3 5.4 %collective-permute-start.17 = (bf16[2,192,128]{2,1,0:T(8,128)(2,1)S(1)}, bf16[2,192,128]{2,1,0:T(8,128)(2,1)S(1)}, u32[]{:S(2)}, u32[]{:S(2)}) collective-permute-start(bf16[2,192,128]{2,1,0:T(8,128)(2,1)S(1)} %get-tuple-element.57), channel_id=1, source_target_pairs={{0,4},{1,5},{2,6},{3,7},{4,0},{5,1},{6,2},{7,3},{8,12},{9,13},{10,... | collective-permute-start | bytes 294920 | tf_op jit(solution)/shard_map/ppermute | solution.py:712
  92.6 15.8 %copy-start.7 = (bf16[64,192]{1,0:T(8,128)(2,1)}, bf16[64,192]{1,0:T(8,128)(2,1)S(1)}, u32[]{:S(2)}) copy-start(bf16[64,192]{1,0:T(8,128)(2,1)S(1)} %fusion.2.own_rank) | copy-start | bytes 73732
  93.4 14.7 %collective-permute-start.15 = (bf16[2,2,64,1024]{3,2,1,0:T(8,128)(2,1)S(1)}, bf16[2,2,64,1024]{3,2,1,0:T(8,128)(2,1)S(1)}, u32[]{:S(2)}, u32[]{:S(2)}) collective-permute-start(bf16[2,2,64,1024]{3,2,1,0:T(8,128)(2,1)S(1)} %pad_maximum_fusion.4), channel_id=1, source_target_pairs={{0,2},{1,3},{2,0},{3,1},{4,6},{5,7},{6,4},{7,5},{8,10},{9,11},{10,... | collective-permute-start | bytes 1572872 | tf_op jit(solution)/shard_map/ppermute | solution.py:712
  94.7 4.6 %collective-permute-start.16 = (bf16[64,128]{1,0:T(8,128)(2,1)S(1)}, bf16[64,128]{1,0:T(8,128)(2,1)S(1)}, u32[]{:S(2)}, u32[]{:S(2)}) collective-permute-start(bf16[64,128]{1,0:T(8,128)(2,1)S(1)} %get-tuple-element.77), channel_id=1, source_target_pairs={{0,8},{1,9},{2,10},{3,11},{4,12},{5,13},{6,14},{7,15},{8,0},{9,1},... | collective-permute-start | bytes 49160 | tf_op jit(solution)/shard_map/ppermute | solution.py:712
  99.4 4.9 %collective-permute-start.20 = (bf16[2,64,128]{2,1,0:T(8,128)(2,1)S(1)}, bf16[2,64,128]{2,1,0:T(8,128)(2,1)S(1)}, u32[]{:S(2)}, u32[]{:S(2)}) collective-permute-start(bf16[2,64,128]{2,1,0:T(8,128)(2,1)S(1)} %pad_maximum_fusion.15), channel_id=1, source_target_pairs={{0,6},{1,7},{2,4},{3,5},{4,2},{5,3},{6,0},{7,1},{8,14},{9,15},{10,... | collective-permute-start | bytes 98312 | tf_op jit(solution)/shard_map/ppermute | solution.py:712
  101.0 3.9 %collective-permute-start.19 = (bf16[2,64,128]{2,1,0:T(8,128)(2,1)S(1)}, bf16[2,64,128]{2,1,0:T(8,128)(2,1)S(1)}, u32[]{:S(2)}, u32[]{:S(2)}) collective-permute-start(bf16[2,64,128]{2,1,0:T(8,128)(2,1)S(1)} %pad_maximum_fusion.15), channel_id=1, source_target_pairs={{0,4},{1,5},{2,6},{3,7},{4,0},{5,1},{6,2},{7,3},{8,12},{9,13},{10,... | collective-permute-start | bytes 98312 | tf_op jit(solution)/shard_map/ppermute | solution.py:712
  101.7 6.4 %collective-permute-start.18 = (bf16[2,64,128]{2,1,0:T(8,128)(2,1)S(1)}, bf16[2,64,128]{2,1,0:T(8,128)(2,1)S(1)}, u32[]{:S(2)}, u32[]{:S(2)}) collective-permute-start(bf16[2,64,128]{2,1,0:T(8,128)(2,1)S(1)} %pad_maximum_fusion.15), channel_id=1, source_target_pairs={{0,2},{1,3},{2,0},{3,1},{4,6},{5,7},{6,4},{7,5},{8,10},{9,11},{10,... | collective-permute-start | bytes 98312 | tf_op jit(solution)/shard_map/ppermute | solution.py:712
  108.3 10.2 %copy-start.5 = (bf16[2,2,2,64,1024]{4,3,2,1,0:T(8,128)(2,1)}, bf16[2,2,2,64,1024]{4,3,2,1,0:T(8,128)(2,1)S(1)}, u32[]{:S(2)}) copy-start(bf16[2,2,2,64,1024]{4,3,2,1,0:T(8,128)(2,1)S(1)} %copy.10) | copy-start | bytes 3145732
  108.3 10.2 %collective-permute-start.21 = (bf16[4,2,64,1024]{3,2,1,0:T(8,128)(2,1)S(1)}, bf16[4,2,64,1024]{3,2,1,0:T(8,128)(2,1)}, u32[]{:S(2)}, u32[]{:S(2)}) collective-permute-start(bf16[4,2,64,1024]{3,2,1,0:T(8,128)(2,1)S(1)} %bitcast.38), channel_id=1, source_target_pairs={{0,1},{1,0},{2,3},{3,2},{4,5},{5,4},{6,7},{7,6},{8,9},{9,8},{10,11... | collective-permute-start | bytes 3145736 | tf_op jit(solution)/shard_map/ppermute | solution.py:712
  108.4 7.3 %collective-permute-start.22 = (bf16[2,2,192,128]{3,2,1,0:T(8,128)(2,1)S(1)}, bf16[2,2,192,128]{3,2,1,0:T(8,128)(2,1)S(1)}, u32[]{:S(2)}, u32[]{:S(2)}) collective-permute-start(bf16[2,2,192,128]{3,2,1,0:T(8,128)(2,1)S(1)} %pad_maximum_fusion.12), channel_id=1, source_target_pairs={{0,2},{1,3},{2,0},{3,1},{4,6},{5,7},{6,4},{7,5},{8,10},{9,11},{10,... | collective-permute-start | bytes 589832 | tf_op jit(solution)/shard_map/ppermute | solution.py:712
  110.5 5.4 %collective-permute-start.23 = (bf16[384,128]{1,0:T(8,128)(2,1)S(1)}, bf16[384,128]{1,0:T(8,128)(2,1)S(1)}, u32[]{:S(2)}, u32[]{:S(2)}) collective-permute-start(bf16[384,128]{1,0:T(8,128)(2,1)S(1)} %get-tuple-element.64), channel_id=1, source_target_pairs={{0,16},{1,17},{2,18},{3,19},{4,20},{5,21},{6,22},{7,23},{8,24},{9,... | collective-permute-start | bytes 294920 | tf_op jit(solution)/shard_map/ppermute | solution.py:712
  115.8 2.7 %copy-start.6 = (bf16[2,2,2,192,128]{4,3,2,1,0:T(8,128)(2,1)}, bf16[2,2,2,192,128]{4,3,2,1,0:T(8,128)(2,1)S(1)}, u32[]{:S(2)}) copy-start(bf16[2,2,2,192,128]{4,3,2,1,0:T(8,128)(2,1)S(1)} %copy.11) | copy-start | bytes 1179652
  115.8 2.7 %collective-permute-start.25 = (bf16[4,2,192,128]{3,2,1,0:T(8,128)(2,1)S(1)}, bf16[4,2,192,128]{3,2,1,0:T(8,128)(2,1)S(1)}, u32[]{:S(2)}, u32[]{:S(2)}) collective-permute-start(bf16[4,2,192,128]{3,2,1,0:T(8,128)(2,1)S(1)} %bitcast.48), channel_id=1, source_target_pairs={{0,1},{1,0},{2,3},{3,2},{4,5},{5,4},{6,7},{7,6},{8,9},{9,8},{10,11... | collective-permute-start | bytes 1179656 | tf_op jit(solution)/shard_map/ppermute | solution.py:712
  115.9 1.9 %collective-permute-start.24 = (bf16[4,2,64,128]{3,2,1,0:T(8,128)(2,1)S(1)}, bf16[4,2,64,128]{3,2,1,0:T(8,128)(2,1)S(1)}, u32[]{:S(2)}, u32[]{:S(2)}) collective-permute-start(bf16[4,2,64,128]{3,2,1,0:T(8,128)(2,1)S(1)} %pad_maximum_fusion.14), channel_id=1, source_target_pairs={{0,1},{1,0},{2,3},{3,2},{4,5},{5,4},{6,7},{7,6},{8,9},{9,8},{10,11... | collective-permute-start | bytes 393224 | tf_op jit(solution)/shard_map/ppermute | solution.py:712
  118.5 0.7 copy-start.10
  123.8 12.2 %collective-permute-start.28 = (bf16[2,384,128]{2,1,0:T(8,128)(2,1)S(1)}, bf16[2,384,128]{2,1,0:T(8,128)(2,1)S(1)}, u32[]{:S(2)}, u32[]{:S(2)}) collective-permute-start(bf16[2,384,128]{2,1,0:T(8,128)(2,1)S(1)} %pad_maximum_fusion.13), channel_id=1, source_target_pairs={{0,6},{1,7},{2,4},{3,5},{4,2},{5,3},{6,0},{7,1},{8,14},{9,15},{10,... | collective-permute-start | bytes 589832 | tf_op jit(solution)/shard_map/ppermute | solution.py:712
  125.3 10.7 %collective-permute-start.27 = (bf16[2,384,128]{2,1,0:T(8,128)(2,1)S(1)}, bf16[2,384,128]{2,1,0:T(8,128)(2,1)S(1)}, u32[]{:S(2)}, u32[]{:S(2)}) collective-permute-start(bf16[2,384,128]{2,1,0:T(8,128)(2,1)S(1)} %pad_maximum_fusion.13), channel_id=1, source_target_pairs={{0,4},{1,5},{2,6},{3,7},{4,0},{5,1},{6,2},{7,3},{8,12},{9,13},{10,... | collective-permute-start | bytes 589832 | tf_op jit(solution)/shard_map/ppermute | solution.py:712
  126.4 9.5 %collective-permute-start.26 = (bf16[2,384,128]{2,1,0:T(8,128)(2,1)S(1)}, bf16[2,384,128]{2,1,0:T(8,128)(2,1)S(1)}, u32[]{:S(2)}, u32[]{:S(2)}) collective-permute-start(bf16[2,384,128]{2,1,0:T(8,128)(2,1)S(1)} %pad_maximum_fusion.13), channel_id=1, source_target_pairs={{0,2},{1,3},{2,0},{3,1},{4,6},{5,7},{6,4},{7,5},{8,10},{9,11},{10,... | collective-permute-start | bytes 589832 | tf_op jit(solution)/shard_map/ppermute | solution.py:712
  136.1 2.4 %collective-permute-start.29 = (bf16[4,2,384,128]{3,2,1,0:T(8,128)(2,1)S(1)}, bf16[4,2,384,128]{3,2,1,0:T(8,128)(2,1)S(1)}, u32[]{:S(2)}, u32[]{:S(2)}) collective-permute-start(bf16[4,2,384,128]{3,2,1,0:T(8,128)(2,1)S(1)} %pad_maximum_fusion.1.same), channel_id=1, source_target_pairs={{0,1},{1,0},{2,3},{3,2},{4,5},{5,4},{6,7},{7,6},{8,9},{9,8},{10,11... | collective-permute-start | bytes 2359304 | tf_op jit(solution)/shard_map/ppermute | solution.py:712
  138.4 1.0 copy-start.2

commit v10 on v9

--- a/solution.py
+++ b/solution.py
@@ -666,7 +666,9 @@
     )(*operands)
 
 
-def widen_kernel(attended, same, other, out_delta, down_out, up_out):
+def widen_kernel(attended_rows, same, other, out_delta, down_out, up_out, attended, sem):
+    fetch = pltpu.make_async_copy(attended_rows, attended, sem)
+    fetch.start()
     plane = lax.axis_index("groups")
     seat = lax.rem(lax.axis_index("ctx"), PIECES)
     for apart in range(PIECES):
@@ -681,6 +683,7 @@
             first = pl.multiple_of(place * UP_OUT_ROWS, UP_OUT_ROWS)
             up_out[pl.ds(first, UP_OUT_ROWS), :] = piece[DOWN_OUT_ROWS:]
     dot = partial(jnp.dot, preferred_element_type=jnp.float32)
+    fetch.wait()
     rank = dot(attended[...], down_out[...].astype(jnp.bfloat16))[:, :ADAPTER_RANK]
     rank = rank.astype(jnp.bfloat16)
     blocks = D // 128
@@ -697,11 +700,13 @@
     return pl.pallas_call(
         widen_kernel,
         out_shape=jax.ShapeDtypeStruct((attended.shape[0], D), jnp.bfloat16),
-        in_specs=[pl.BlockSpec(memory_space=pltpu.VMEM)] * 3,
+        in_specs=[pl.BlockSpec(memory_space=pl.ANY)] + [pl.BlockSpec(memory_space=pltpu.VMEM)] * 2,
         out_specs=pl.BlockSpec(memory_space=pltpu.VMEM),
         scratch_shapes=[
             pltpu.VMEM((QH * HEAD_SIZE, 128), jnp.float32),
             pltpu.VMEM((ADAPTER_RANK * D // 128, 128), jnp.float32),
+            pltpu.VMEM(attended.shape, attended.dtype),
+            pltpu.SemaphoreType.DMA,
         ],
         compiler_params=pltpu.CompilerParams(vmem_limit_bytes=32 << 20),
         cost_estimate=pl.CostEstimate(flops=1 << 27, bytes_accessed=4 << 20, transcendentals=0),
@@ -756,34 +761,31 @@
     dealt = [swap(block, 2 * j) if j else block for j, block in enumerate(dealt)]
 
     weight, ups = join(stretch_adapter, adapter_owner, arrived)
-    far = swap(after(far, weight), PIECES)
-    partial_sums = narrow(weight, dealt)
+    base = along_z(after(base, arrived[1]))
+    partial_sums = narrow(after(weight, base), dealt)
     back = [swap(block, 2 * j) if j else block for j, block in enumerate(partial_sums)]
     back = sum(block.astype(jnp.float32) for block in back)
-    own_rank = swap(after(back[1].astype(jnp.bfloat16), far), 1)
+    ups = along_z(after(ups, *partial_sums))
+    own_rank = swap(after(back[1].astype(jnp.bfloat16), ups), 1)
     own_rank = back[0] + own_rank.astype(jnp.float32)
     own_rank = own_rank.astype(jnp.bfloat16)
-    ups = along_z(after(ups, *partial_sums))
-    base = along_z(after(base, *partial_sums))
+    base = along_x(after(base, *partial_sums))
     all_rank = own_rank[:, ADAPTER_RANK:]
-    base = along_x(after(base, own_rank))
-    own, across = settle(
-        stretch_adapter, elsewhere, adapter_owner, near, after(far, own_rank)
-    )
-    ends = jnp.stack([own, swap(across, 2 * PIECES)])
+    ups = along_x(after(ups, own_rank))
     all_rank = jnp.stack([all_rank, swap(all_rank, PIECES)])
     all_rank = after(all_rank, ups)
-    ups = along_x(after(ups, all_rank))
+    far = swap(after(far, all_rank), PIECES)
     all_rank = jnp.stack([swap(all_rank, apart) if apart else all_rank for apart in (0, 2, 4, 6)])
     base = after(base, all_rank)
     base = (base, swap(base, 1))
-    all_rank = after(all_rank, ups, ends)
-    ups = (ups, swap(ups, 1))
+    ups = (ups, swap(after(ups, all_rank), 1))
     all_rank = jnp.stack([all_rank, swap(all_rank, 1)])
 
     shared = (query_base, base, own_rank, all_rank, ups, cosines, sines)
     attended = attend(0, 1, None, *shared)
-    ends = after(ends, attended)
+    far = after(far, attended)
+    own, across = settle(stretch_adapter, elsewhere, adapter_owner, near, far)
+    ends = jnp.stack([own, swap(across, 2 * PIECES)])
     ends = jnp.stack([swap(ends, apart) if apart else ends for apart in (0, 2, 4, 6)])
     attended = attend(1, KEYVALUE_HEADS - 1, attended, *shared)
     ends = after(ends, attended)

time: 143 us -> 163 us (1.14)
  waiting for transfers between devices: 62.6 us -> 88.9 us
  starting transfers between devices: 44.8 us -> 36.9 us
    ppermute x30, waiting for transfers between devices: 60.4 us -> 86.7 us  [swap(): lax.ppermute(block, ('groups', 'ctx'), [(i, i ^ mask) for i in range(4 *...]
    ppermute x30, starting transfers between devices: 39.2 us -> 31.4 us  [swap(): lax.ppermute(block, ('groups', 'ctx'), [(i, i ^ mask) for i in range(4 *...]
    unnamed x23 -> x25, local copies, waits for them, and re-layouts: 3.53 us -> 4.53 us
  transfers between devices with their start and end apart: 31 -> 31, of which waited for: 16 -> 19; matrix products, arithmetic and copies ran while one was open for 3% -> 3% of each run, Pallas kernels for 8% -> 9%
where the time goes in v10:
time: 163 us; the launch traced here: 162 us
  waiting for transfers between devices  88.9 us (55%)
  starting transfers between devices  36.9 us (23%)
  Pallas kernels  26 us (16%)
  local copies, waits for them, and re-layouts  4.78 us (3%)
  other arithmetic  4.51 us (3%)
    ppermute x30, waiting for transfers between devices, swap(): lax.ppermute(block, ('groups', 'ctx'), [(i, i ^ mask) for i in range(4 *...  86.7 us
    ppermute x30, starting transfers between devices, swap(): lax.ppermute(block, ('groups', 'ctx'), [(i, i ^ mask) for i in range(4 *...  31.4 us
    pallas_call x2, Pallas kernels, attend(): pl.pallas_call(partial(attend_kernel, first_head), grid=(heads,), out_sha...  13.2 us
    all_to_all x1, starting transfers between devices, direct_shards(): spread = lax.all_to_all(packed, 'ctx', 0, 0, axis_index_groups=blocks)  5.5 us
    pallas_call x1, Pallas kernels, pack_row(): pl.pallas_call(partial(pack_kernel, sections), out_shape=jax.ShapeDtypeSt...  5.15 us
    unnamed x25, local copies, waits for them, and re-layouts  4.53 us
  transfers between devices with their start and end apart: 31, of which 19 were waited for; matrix products, arithmetic and copies ran while one was open for 3% of the time, Pallas kernels for 9%

profile of v10, /device:TPU:0, one launch (start us, length us, event | category | flops | bytes accessed | tf_op | source)
XLA Modules:
  0.0 162.2 jit_solution(14740011007598485225)
XLA Ops:
  0.6 5.1 %shard_map.86.refs_0_ = bf16[8,1312,128]{2,1,0:T(8,128)(2,1)} custom-call(bf16[1,2686976]{1,0:T(2,128)(2,1)} %pool.1), custom_call_target="tpu_custom_call" | custom-call | bytes 8388608 | tf_op jit(solution)/shard_map/pallas_call | solution.py:316
  5.8 5.5 %all-to-all-start = ((bf16[8,1312,128]{2,1,0:T(8,128)(2,1)}), bf16[8,1312,128]{2,1,0:T(8,128)(2,1)}, u32[]{:S(2)}, u32[]{:S(2)}) async-start(bf16[8,1312,128]{2,1,0:T(8,128)(2,1)} %shard_map.86.refs_0_), calls=%async_computation | async-start | bytes 5373952 | tf_op jit(solution)/shard_map/all_to_all | solution.py:756
  11.3 2.2 %collective-permute-start.1 = (s32[2]{0:T(128)S(1)}, s32[2]{0:T(128)S(1)}, u32[]{:S(2)}, u32[]{:S(2)}) collective-permute-start(s32[2]{0:T(128)S(1)} %copy-done.3), channel_id=1, source_target_pairs={{0,16},{1,17},{2,18},{3,19},{4,20},{5,21},{6,22},{7,23},{8,24},{9,... | collective-permute-start | bytes 32 | tf_op jit(solution)/shard_map/ppermute | solution.py:717
  13.6 1.2 copy-done.1
  14.8 0.3 shard_map.87
  15.1 0.1 collective-permute-start.2
  15.2 0.5 copy-done.8
  15.7 2.6 %collective-permute-start = (bf16[64,1024]{1,0:T(8,128)(2,1)S(1)}, bf16[64,1024]{1,0:T(8,128)(2,1)S(1)}, u32[]{:S(2)}, u32[]{:S(2)}) collective-permute-start(bf16[64,1024]{1,0:T(8,128)(2,1)S(1)} %constant_dynamic-update-slice_fusion), channel_id=1, source_target_pairs={{0,8},{1,9},{2,10},{3,11},{4,12},{5,13},{6,14},{7,15},{8,0},{9,1},... | collective-permute-start | bytes 393224 | tf_op jit(solution)/shard_map/ppermute | solution.py:717
  18.4 1.9 %fusion = (f32[1024,64]{1,0:T(8,128)S(1)}, f32[1024,64]{1,0:T(8,128)S(1)}, f32[1024,64]{1,0:T(8,128)S(1)}) fusion(f32[64]{0:T(128)S(1)} %multiply_power_fusion, f32[1024]{0:T(1024)S(1)} %iota_convert_fusion), kind=kLoop, calls=%fused_computation.16 | loop fusion | flops 131072 | bytes 790784 | tf_op jit(solution)/shard_map/neg | solution.py:733
  20.3 1.3 pad_maximum_fusion.2
  21.6 22.4 %collective-permute-done = bf16[64,1024]{1,0:T(8,128)(2,1)S(1)} collective-permute-done((bf16[64,1024]{1,0:T(8,128)(2,1)S(1)}, bf16[64,1024]{1,0:T(8,128)(2,1)S(1)}, u32[]{:S(2)}, u32[]{:S(2)}) %collective-permute-start) | collective-permute-done | bytes 131104 | tf_op jit(solution)/shard_map/ppermute | solution.py:717
  44.1 2.2 %all-to-all-done.spread = bf16[8,1312,128]{2,1,0:T(8,128)(2,1)} async-done(((bf16[8,1312,128]{2,1,0:T(8,128)(2,1)}), bf16[8,1312,128]{2,1,0:T(8,128)(2,1)}, u32[]{:S(2)}, u32[]{:S(2)}) %all-to-all-start) | async-done | bytes 2687008 | tf_op jit(solution)/shard_map/all_to_all | solution.py:756
  46.3 2.1 %shard_map.88 = (bf16[960,128]{1,0:T(8,128)(2,1)S(1)}, bf16[960,128]{1,0:T(8,128)(2,1)S(1)}, bf16[960,128]{1,0:T(8,128)(2,1)S(1)}, bf16[960,128]{1,0:T(8,128)(2,...) custom-call(s32[2]{0:T(128)S(1)} %copy-done.3, s32[2]{0:T(128)S(1)} %collective-permute-done.1.there, ...), custom_call_target="tpu_custom_call" | custom-call | bytes 3145728 | tf_op jit(solution)/shard_map/pallas_call | solution.py:360
  48.4 1.3 collective-permute-start.3
  49.7 2.1 %collective-permute-start.5 = (bf16[960,128]{1,0:T(8,128)(2,1)S(1)}, bf16[960,128]{1,0:T(8,128)(2,1)S(1)}, u32[]{:S(2)}, u32[]{:S(2)}) collective-permute-start(bf16[960,128]{1,0:T(8,128)(2,1)S(1)} %get-tuple-element.40), channel_id=1, source_target_pairs={{0,16},{1,17},{2,18},{3,19},{4,20},{5,21},{6,22},{7,23},{8,24},{9,... | collective-permute-start | bytes 737288 | tf_op jit(solution)/shard_map/ppermute | solution.py:717
  51.9 1.2 collective-permute-start.6
  53.1 15.7 %collective-permute-done.3.refs_1_ = bf16[960,128]{1,0:T(8,128)(2,1)S(1)} collective-permute-done((bf16[960,128]{1,0:T(8,128)(2,1)S(1)}, bf16[960,128]{1,0:T(8,128)(2,1)S(1)}, u32[]{:S(2)}, u32[]{:S(2)}) %collective-permute-start.3) | collective-permute-done | bytes 245792 | tf_op jit(solution)/shard_map/ppermute | solution.py:717
  68.9 1.5 collective-permute-start.7
  70.4 2.0 %collective-permute-start.8 = (bf16[2,64,1024]{2,1,0:T(8,128)(2,1)S(1)}, bf16[2,64,1024]{2,1,0:T(8,128)(2,1)S(1)}, u32[]{:S(2)}, u32[]{:S(2)}) collective-permute-start(bf16[2,64,1024]{2,1,0:T(8,128)(2,1)S(1)} %get-tuple-element.47), channel_id=1, source_target_pairs={{0,4},{1,5},{2,6},{3,7},{4,0},{5,1},{6,2},{7,3},{8,12},{9,13},{10,... | collective-permute-start | bytes 786440 | tf_op jit(solution)/shard_map/ppermute | solution.py:717
  72.4 1.8 %collective-permute-done.6.refs_3_ = bf16[960,128]{1,0:T(8,128)(2,1)S(1)} collective-permute-done((bf16[960,128]{1,0:T(8,128)(2,1)S(1)}, bf16[960,128]{1,0:T(8,128)(2,1)S(1)}, u32[]{:S(2)}, u32[]{:S(2)}) %collective-permute-start.6) | collective-permute-done | bytes 245792 | tf_op jit(solution)/shard_map/ppermute | solution.py:717
  74.3 1.0 shard_map.89
  75.2 3.1 %collective-permute-done.4 = bf16[2,64,1024]{2,1,0:T(8,128)(2,1)S(1)} collective-permute-done((bf16[2,64,1024]{2,1,0:T(8,128)(2,1)S(1)}, bf16[2,64,1024]{2,1,0:T(8,128)(2,1)S(1)}, u32[]{:S(2)}, u32[]{:S(2)}) %collective-permute-start.4) | collective-permute-done | bytes 262176 | tf_op jit(solution)/shard_map/ppermute | solution.py:717
  78.4 5.6 %collective-permute-done.8.refs_2_ = bf16[2,64,1024]{2,1,0:T(8,128)(2,1)S(1)} collective-permute-done((bf16[2,64,1024]{2,1,0:T(8,128)(2,1)S(1)}, bf16[2,64,1024]{2,1,0:T(8,128)(2,1)S(1)}, u32[]{:S(2)}, u32[]{:S(2)}) %collective-permute-start.8) | collective-permute-done | bytes 262176 | tf_op jit(solution)/shard_map/ppermute | solution.py:717
  83.9 6.4 %collective-permute-done.9.refs_3_ = bf16[2,64,1024]{2,1,0:T(8,128)(2,1)S(1)} collective-permute-done((bf16[2,64,1024]{2,1,0:T(8,128)(2,1)S(1)}, bf16[2,64,1024]{2,1,0:T(8,128)(2,1)S(1)}, u32[]{:S(2)}, u32[]{:S(2)}) %collective-permute-start.9) | collective-permute-done | bytes 262176 | tf_op jit(solution)/shard_map/ppermute | solution.py:717
  90.3 0.5 shard_map.90
  90.8 0.1 collective-permute-start.13
  90.8 2.1 %collective-permute-start.12 = (bf16[2,64,192]{2,1,0:T(8,128)(2,1)S(1)}, bf16[2,64,192]{2,1,0:T(8,128)(2,1)S(1)}, u32[]{:S(2)}, u32[]{:S(2)}) collective-permute-start(bf16[2,64,192]{2,1,0:T(8,128)(2,1)S(1)} %get-tuple-element.51), channel_id=1, source_target_pairs={{0,4},{1,5},{2,6},{3,7},{4,0},{5,1},{6,2},{7,3},{8,12},{9,13},{10,... | collective-permute-start | bytes 147464 | tf_op jit(solution)/shard_map/ppermute | solution.py:717
  92.9 1.4 collective-permute-start.11
  94.3 2.4 %collective-permute-done.13 = bf16[2,64,192]{2,1,0:T(8,128)(2,1)S(1)} collective-permute-done((bf16[2,64,192]{2,1,0:T(8,128)(2,1)S(1)}, bf16[2,64,192]{2,1,0:T(8,128)(2,1)S(1)}, u32[]{:S(2)}, u32[]{:S(2)}) %collective-permute-start.13) | collective-permute-done | bytes 49184 | tf_op jit(solution)/shard_map/ppermute | solution.py:717
  96.7 0.6 collective-permute-done.11
  97.3 1.6 collective-permute-done.14
  99.0 0.9 collective-permute-start.10
  100.0 0.3 collective-permute-done.15
  100.3 1.0 collective-permute-start.17
  101.2 0.1 slice_bitcast_fusion.1
  101.3 1.3 collective-permute-start.16
  102.6 3.4 %collective-permute-done.16 = bf16[64,128]{1,0:T(8,128)(2,1)S(1)} collective-permute-done((bf16[64,128]{1,0:T(8,128)(2,1)S(1)}, bf16[64,128]{1,0:T(8,128)(2,1)S(1)}, u32[]{:S(2)}, u32[]{:S(2)}) %collective-permute-start.16) | collective-permute-done | bytes 16416 | tf_op jit(solution)/shard_map/ppermute | solution.py:717
  106.0 11.6 %collective-permute-done.17 = bf16[2,2,192,128]{3,2,1,0:T(8,128)(2,1)S(1)} collective-permute-done((bf16[2,2,192,128]{3,2,1,0:T(8,128)(2,1)S(1)}, bf16[2,2,192,128]{3,2,1,0:T(8,128)(2,1)S(1)}, u32[]{:S(2)}, u32[]{:S(2)}) %collective-permute-start.17) | collective-permute-done | bytes 196640 | tf_op jit(solution)/shard_map/ppermute | solution.py:717
  117.7 0.7 collective-permute-start.20
  118.4 1.7 %collective-permute-start.19 = (bf16[2,64,128]{2,1,0:T(8,128)(2,1)S(1)}, bf16[2,64,128]{2,1,0:T(8,128)(2,1)S(1)}, u32[]{:S(2)}, u32[]{:S(2)}) collective-permute-start(bf16[2,64,128]{2,1,0:T(8,128)(2,1)S(1)} %pad_maximum_fusion.15), channel_id=1, source_target_pairs={{0,4},{1,5},{2,6},{3,7},{4,0},{5,1},{6,2},{7,3},{8,12},{9,13},{10,... | collective-permute-start | bytes 98312 | tf_op jit(solution)/shard_map/ppermute | solution.py:717
  120.1 1.2 collective-permute-start.18
  121.2 1.3 collective-permute-done.20
  122.6 1.4 collective-permute-done.18
  124.0 0.1 pad_maximum_fusion
  124.2 0.1 collective-permute-start.21
  124.3 0.5 collective-permute-start.23
  124.8 0.1 collective-permute-start.22
  124.9 1.3 collective-permute-start.24
  126.2 1.5 collective-permute-done.22
  127.7 0.7 pad_maximum_fusion.11.all_rank
  128.5 0.7 copy-done.11
  129.2 1.0 copy-done.10
  130.2 4.5 %shard_map.91.refs_0_ = bf16[64,4096]{1,0:T(8,128)(2,1)} custom-call(bf16[64,4096]{1,0:T(8,128)(2,1)} %query_block.3, bf16[4,2,64,1024]{3,2,1,0:T(8,128)(2,1)} %bitcast.41, bf16[4,2,64,1024]{3,2,1,0:T(8,128)(2,1)} %copy-done.10, bf16[4,2,64,1024]{3,2,1,0:T(8,128)(2,1)} %bitcast.42, bf16[4,2,64,1024]{3,2,1,0:T(8,128)(2,1)} %copy-done.10, ...), custom_call_target="tpu_custom_call" | custom-call | flops 3221225472 | bytes 10485760 | tf_op jit(solution)/shard_map/pallas_call | solution.py:634
  134.7 2.4 %collective-permute-done.24.far = bf16[2,384,128]{2,1,0:T(8,128)(2,1)S(1)} collective-permute-done((bf16[2,384,128]{2,1,0:T(8,128)(2,1)S(1)}, bf16[2,384,128]{2,1,0:T(8,128)(2,1)S(1)}, u32[]{:S(2)}, u32[]{:S(2)}) %collective-permute-start.24) | collective-permute-done | bytes 196640 | tf_op jit(solution)/shard_map/ppermute | solution.py:717
  137.0 0.8 shard_map.93
  137.8 2.3 %collective-permute-start.25 = (bf16[384,128]{1,0:T(8,128)(2,1)S(1)}, bf16[384,128]{1,0:T(8,128)(2,1)S(1)}, u32[]{:S(2)}, u32[]{:S(2)}) collective-permute-start(bf16[384,128]{1,0:T(8,128)(2,1)S(1)} %get-tuple-element.66), channel_id=1, source_target_pairs={{0,16},{1,17},{2,18},{3,19},{4,20},{5,21},{6,22},{7,23},{8,24},{9,... | collective-permute-start | bytes 294920 | tf_op jit(solution)/shard_map/ppermute | solution.py:717
  140.1 3.0 %collective-permute-done.25 = bf16[384,128]{1,0:T(8,128)(2,1)S(1)} collective-permute-done((bf16[384,128]{1,0:T(8,128)(2,1)S(1)}, bf16[384,128]{1,0:T(8,128)(2,1)S(1)}, u32[]{:S(2)}, u32[]{:S(2)}) %collective-permute-start.25) | collective-permute-done | bytes 98336 | tf_op jit(solution)/shard_map/ppermute | solution.py:717
  143.2 2.5 %collective-permute-start.27 = (bf16[2,384,128]{2,1,0:T(8,128)(2,1)S(1)}, bf16[2,384,128]{2,1,0:T(8,128)(2,1)S(1)}, u32[]{:S(2)}, u32[]{:S(2)}) collective-permute-start(bf16[2,384,128]{2,1,0:T(8,128)(2,1)S(1)} %get-tuple-element.77), channel_id=1, source_target_pairs={{0,4},{1,5},{2,6},{3,7},{4,0},{5,1},{6,2},{7,3},{8,12},{9,13},{10,... | collective-permute-start | bytes 589832 | tf_op jit(solution)/shard_map/ppermute | solution.py:717
  145.7 1.0 collective-permute-start.26
  146.7 8.7 %shard_map.92.attended_rows = bf16[64,4096]{1,0:T(8,128)(2,1)} custom-call(bf16[64,4096]{1,0:T(8,128)(2,1)} %query_block.3, bf16[4,2,64,1024]{3,2,1,0:T(8,128)(2,1)} %bitcast.43, bf16[4,2,64,1024]{3,2,1,0:T(8,128)(2,1)} %copy-done.10, bf16[4,2,64,1024]{3,2,1,0:T(8,128)(2,1)} %bitcast.44, ...), custom_call_target="tpu_custom_call", output_to_operand_aliasing={{}: (11, {})} | custom-call | flops 9663676416 | bytes 10485760 | tf_op jit(solution)/shard_map/pallas_call | solution.py:634
  155.5 0.1 pad_maximum_fusion.1.same
  155.6 2.3 %collective-permute-done.29.other = bf16[4,2,384,128]{3,2,1,0:T(8,128)(2,1)S(1)} collective-permute-done((bf16[4,2,384,128]{3,2,1,0:T(8,128)(2,1)S(1)}, bf16[4,2,384,128]{3,2,1,0:T(8,128)(2,1)S(1)}, u32[]{:S(2)}, u32[]{:S(2)}) %collective-permute-start.29) | collective-permute-done | bytes 786464 | tf_op jit(solution)/shard_map/ppermute | solution.py:717
  157.9 1.0 copy-done.2
  159.0 3.1 %shard_map.94 = bf16[64,8192]{1,0:T(8,128)(2,1)} custom-call(bf16[64,4096]{1,0:T(8,128)(2,1)S(1)} %copy-done.2, bf16[4,2,384,128]{3,2,1,0:T(8,128)(2,1)S(1)} %pad_maximum_fusion.1.same, bf16[4,2,384,128]{3,2,1,0:T(8,128)(2,1)S(1)} %collective-permute-done.29.other), custom_call_target="tpu_custom_call" | custom-call | flops 134217728 | bytes 4194304 | tf_op jit(solution)/shard_map/pallas_call | solution.py:700
  (57 shorter events, 0.8 us)
Async XLA Ops:
  5.8 5.5 %copy-start.3 = (s32[2]{0:T(128)S(1)}, s32[2]{0:T(128)}, u32[]{:S(2)}) copy-start(s32[2]{0:T(128)} %here.5) | copy-start | bytes 28
  5.8 7.8 %copy-start = (bf16[8,1312,128]{2,1,0:T(8,128)(2,1)S(1)}, bf16[8,1312,128]{2,1,0:T(8,128)(2,1)}, u32[]{:S(2)}) copy-start(bf16[8,1312,128]{2,1,0:T(8,128)(2,1)} %shard_map.86.refs_0_) | copy-start | bytes 8060932
  5.8 40.5 %all-to-all-start = ((bf16[8,1312,128]{2,1,0:T(8,128)(2,1)}), bf16[8,1312,128]{2,1,0:T(8,128)(2,1)}, u32[]{:S(2)}, u32[]{:S(2)}) async-start(bf16[8,1312,128]{2,1,0:T(8,128)(2,1)} %shard_map.86.refs_0_), calls=%async_computation | async-start | bytes 5373952 | tf_op jit(solution)/shard_map/all_to_all | solution.py:756
  11.3 35.0 %collective-permute-start.1 = (s32[2]{0:T(128)S(1)}, s32[2]{0:T(128)S(1)}, u32[]{:S(2)}, u32[]{:S(2)}) collective-permute-start(s32[2]{0:T(128)S(1)} %copy-done.3), channel_id=1, source_target_pairs={{0,16},{1,17},{2,18},{3,19},{4,20},{5,21},{6,22},{7,23},{8,24},{9,... | collective-permute-start | bytes 32 | tf_op jit(solution)/shard_map/ppermute | solution.py:717
  13.6 1.2 copy-start.1
  14.8 0.8 copy-start.8
  14.8 0.9 copy-start.9
  15.1 29.0 %collective-permute-start.2 = (bf16[4,64,1024]{2,1,0:T(8,128)(2,1)S(1)}, bf16[4,64,1024]{2,1,0:T(8,128)(2,1)S(1)}, u32[]{:S(2)}, u32[]{:S(2)}) collective-permute-start(bf16[4,64,1024]{2,1,0:T(8,128)(2,1)S(1)} %get-tuple-element.35), channel_id=1, source_target_pairs={{0,1},{1,0},{2,3},{3,2},{4,5},{5,4},{6,7},{7,6},{8,9},{9,8},{10,11... | collective-permute-start | bytes 1572872 | tf_op jit(solution)/shard_map/ppermute | solution.py:717
  15.7 28.4 %collective-permute-start = (bf16[64,1024]{1,0:T(8,128)(2,1)S(1)}, bf16[64,1024]{1,0:T(8,128)(2,1)S(1)}, u32[]{:S(2)}, u32[]{:S(2)}) collective-permute-start(bf16[64,1024]{1,0:T(8,128)(2,1)S(1)} %constant_dynamic-update-slice_fusion), channel_id=1, source_target_pairs={{0,8},{1,9},{2,10},{3,11},{4,12},{5,13},{6,14},{7,15},{8,0},{9,1},... | collective-permute-start | bytes 393224 | tf_op jit(solution)/shard_map/ppermute | solution.py:717
  18.3 28.0 %copy-start.4 = (s32[16]{0:T(128)S(1)}, s32[16]{0:T(128)}, u32[]{:S(2)}) copy-start(s32[16]{0:T(128)} %owner.5) | copy-start | bytes 196
  48.4 20.4 %collective-permute-start.3 = (bf16[960,128]{1,0:T(8,128)(2,1)S(1)}, bf16[960,128]{1,0:T(8,128)(2,1)S(1)}, u32[]{:S(2)}, u32[]{:S(2)}) collective-permute-start(bf16[960,128]{1,0:T(8,128)(2,1)S(1)} %get-tuple-element.37), channel_id=1, source_target_pairs={{0,8},{1,9},{2,10},{3,11},{4,12},{5,13},{6,14},{7,15},{8,0},{9,1},... | collective-permute-start | bytes 737288 | tf_op jit(solution)/shard_map/ppermute | solution.py:717
  49.7 22.7 %collective-permute-start.5 = (bf16[960,128]{1,0:T(8,128)(2,1)S(1)}, bf16[960,128]{1,0:T(8,128)(2,1)S(1)}, u32[]{:S(2)}, u32[]{:S(2)}) collective-permute-start(bf16[960,128]{1,0:T(8,128)(2,1)S(1)} %get-tuple-element.40), channel_id=1, source_target_pairs={{0,16},{1,17},{2,18},{3,19},{4,20},{5,21},{6,22},{7,23},{8,24},{9,... | collective-permute-start | bytes 737288 | tf_op jit(solution)/shard_map/ppermute | solution.py:717
  51.9 22.4 %collective-permute-start.6 = (bf16[960,128]{1,0:T(8,128)(2,1)S(1)}, bf16[960,128]{1,0:T(8,128)(2,1)S(1)}, u32[]{:S(2)}, u32[]{:S(2)}) collective-permute-start(bf16[960,128]{1,0:T(8,128)(2,1)S(1)} %get-tuple-element.41), channel_id=1, source_target_pairs={{0,24},{1,25},{2,26},{3,27},{4,28},{5,29},{6,30},{7,31},{8,16},{9,... | collective-permute-start | bytes 737288 | tf_op jit(solution)/shard_map/ppermute | solution.py:717
  68.8 9.5 %collective-permute-start.4 = (bf16[2,64,1024]{2,1,0:T(8,128)(2,1)S(1)}, bf16[2,64,1024]{2,1,0:T(8,128)(2,1)S(1)}, u32[]{:S(2)}, u32[]{:S(2)}) collective-permute-start(bf16[2,64,1024]{2,1,0:T(8,128)(2,1)S(1)} %pad_maximum_fusion.6), channel_id=1, source_target_pairs={{0,4},{1,5},{2,6},{3,7},{4,0},{5,1},{6,2},{7,3},{8,12},{9,13},{10,... | collective-permute-start | bytes 786440 | tf_op jit(solution)/shard_map/ppermute | solution.py:717
  68.9 9.5 %collective-permute-start.7 = (bf16[2,64,1024]{2,1,0:T(8,128)(2,1)S(1)}, bf16[2,64,1024]{2,1,0:T(8,128)(2,1)S(1)}, u32[]{:S(2)}, u32[]{:S(2)}) collective-permute-start(bf16[2,64,1024]{2,1,0:T(8,128)(2,1)S(1)} %get-tuple-element.46), channel_id=1, source_target_pairs={{0,2},{1,3},{2,0},{3,1},{4,6},{5,7},{6,4},{7,5},{8,10},{9,11},{10,... | collective-permute-start | bytes 786440 | tf_op jit(solution)/shard_map/ppermute | solution.py:717
  70.4 13.5 %collective-permute-start.8 = (bf16[2,64,1024]{2,1,0:T(8,128)(2,1)S(1)}, bf16[2,64,1024]{2,1,0:T(8,128)(2,1)S(1)}, u32[]{:S(2)}, u32[]{:S(2)}) collective-permute-start(bf16[2,64,1024]{2,1,0:T(8,128)(2,1)S(1)} %get-tuple-element.47), channel_id=1, source_target_pairs={{0,4},{1,5},{2,6},{3,7},{4,0},{5,1},{6,2},{7,3},{8,12},{9,13},{10,... | collective-permute-start | bytes 786440 | tf_op jit(solution)/shard_map/ppermute | solution.py:717
  72.4 17.9 %collective-permute-start.9 = (bf16[2,64,1024]{2,1,0:T(8,128)(2,1)S(1)}, bf16[2,64,1024]{2,1,0:T(8,128)(2,1)S(1)}, u32[]{:S(2)}, u32[]{:S(2)}) collective-permute-start(bf16[2,64,1024]{2,1,0:T(8,128)(2,1)S(1)} %get-tuple-element.48), channel_id=1, source_target_pairs={{0,6},{1,7},{2,4},{3,5},{4,2},{5,3},{6,0},{7,1},{8,14},{9,15},{10,... | collective-permute-start | bytes 786440 | tf_op jit(solution)/shard_map/ppermute | solution.py:717
  90.8 5.9 %collective-permute-start.13 = (bf16[2,64,192]{2,1,0:T(8,128)(2,1)S(1)}, bf16[2,64,192]{2,1,0:T(8,128)(2,1)S(1)}, u32[]{:S(2)}, u32[]{:S(2)}) collective-permute-start(bf16[2,64,192]{2,1,0:T(8,128)(2,1)S(1)} %get-tuple-element.52), channel_id=1, source_target_pairs={{0,6},{1,7},{2,4},{3,5},{4,2},{5,3},{6,0},{7,1},{8,14},{9,15},{10,... | collective-permute-start | bytes 147464 | tf_op jit(solution)/shard_map/ppermute | solution.py:717
  90.8 5.8 %collective-permute-start.12 = (bf16[2,64,192]{2,1,0:T(8,128)(2,1)S(1)}, bf16[2,64,192]{2,1,0:T(8,128)(2,1)S(1)}, u32[]{:S(2)}, u32[]{:S(2)}) collective-permute-start(bf16[2,64,192]{2,1,0:T(8,128)(2,1)S(1)} %get-tuple-element.51), channel_id=1, source_target_pairs={{0,4},{1,5},{2,6},{3,7},{4,0},{5,1},{6,2},{7,3},{8,12},{9,13},{10,... | collective-permute-start | bytes 147464 | tf_op jit(solution)/shard_map/ppermute | solution.py:717
  92.9 4.4 %collective-permute-start.11 = (bf16[2,64,192]{2,1,0:T(8,128)(2,1)S(1)}, bf16[2,64,192]{2,1,0:T(8,128)(2,1)S(1)}, u32[]{:S(2)}, u32[]{:S(2)}) collective-permute-start(bf16[2,64,192]{2,1,0:T(8,128)(2,1)S(1)} %get-tuple-element.50), channel_id=1, source_target_pairs={{0,2},{1,3},{2,0},{3,1},{4,6},{5,7},{6,4},{7,5},{8,10},{9,11},{10,... | collective-permute-start | bytes 147464 | tf_op jit(solution)/shard_map/ppermute | solution.py:717
  94.3 4.6 %collective-permute-start.14 = (bf16[2,192,128]{2,1,0:T(8,128)(2,1)S(1)}, bf16[2,192,128]{2,1,0:T(8,128)(2,1)S(1)}, u32[]{:S(2)}, u32[]{:S(2)}) collective-permute-start(bf16[2,192,128]{2,1,0:T(8,128)(2,1)S(1)} %get-tuple-element.55), channel_id=1, source_target_pairs={{0,4},{1,5},{2,6},{3,7},{4,0},{5,1},{6,2},{7,3},{8,12},{9,13},{10,... | collective-permute-start | bytes 294920 | tf_op jit(solution)/shard_map/ppermute | solution.py:717
  99.0 1.3 collective-permute-start.15
  99.0 25.0 %collective-permute-start.10 = (bf16[2,2,64,1024]{3,2,1,0:T(8,128)(2,1)S(1)}, bf16[2,2,64,1024]{3,2,1,0:T(8,128)(2,1)S(1)}, u32[]{:S(2)}, u32[]{:S(2)}) collective-permute-start(bf16[2,2,64,1024]{3,2,1,0:T(8,128)(2,1)S(1)} %pad_maximum_fusion.4), channel_id=1, source_target_pairs={{0,2},{1,3},{2,0},{3,1},{4,6},{5,7},{6,4},{7,5},{8,10},{9,11},{10,... | collective-permute-start | bytes 1572872 | tf_op jit(solution)/shard_map/ppermute | solution.py:717
  100.2 24.0 %copy-start.7 = (bf16[64,192]{1,0:T(8,128)(2,1)}, bf16[64,192]{1,0:T(8,128)(2,1)S(1)}, u32[]{:S(2)}) copy-start(bf16[64,192]{1,0:T(8,128)(2,1)S(1)} %fusion.2.own_rank) | copy-start | bytes 73732
  100.3 17.3 %collective-permute-start.17 = (bf16[2,2,192,128]{3,2,1,0:T(8,128)(2,1)S(1)}, bf16[2,2,192,128]{3,2,1,0:T(8,128)(2,1)S(1)}, u32[]{:S(2)}, u32[]{:S(2)}) collective-permute-start(bf16[2,2,192,128]{3,2,1,0:T(8,128)(2,1)S(1)} %pad_maximum_fusion.12), channel_id=1, source_target_pairs={{0,2},{1,3},{2,0},{3,1},{4,6},{5,7},{6,4},{7,5},{8,10},{9,11},{10,... | collective-permute-start | bytes 589832 | tf_op jit(solution)/shard_map/ppermute | solution.py:717
  101.3 4.6 %collective-permute-start.16 = (bf16[64,128]{1,0:T(8,128)(2,1)S(1)}, bf16[64,128]{1,0:T(8,128)(2,1)S(1)}, u32[]{:S(2)}, u32[]{:S(2)}) collective-permute-start(bf16[64,128]{1,0:T(8,128)(2,1)S(1)} %get-tuple-element.81), channel_id=1, source_target_pairs={{0,8},{1,9},{2,10},{3,11},{4,12},{5,13},{6,14},{7,15},{8,0},{9,1},... | collective-permute-start | bytes 49160 | tf_op jit(solution)/shard_map/ppermute | solution.py:717
  117.7 10.8 %copy-start.6 = (bf16[2,2,2,192,128]{4,3,2,1,0:T(8,128)(2,1)}, bf16[2,2,2,192,128]{4,3,2,1,0:T(8,128)(2,1)S(1)}, u32[]{:S(2)}) copy-start(bf16[2,2,2,192,128]{4,3,2,1,0:T(8,128)(2,1)S(1)} %copy.11) | copy-start | bytes 1179652
  117.7 4.9 %collective-permute-start.20 = (bf16[2,64,128]{2,1,0:T(8,128)(2,1)S(1)}, bf16[2,64,128]{2,1,0:T(8,128)(2,1)S(1)}, u32[]{:S(2)}, u32[]{:S(2)}) collective-permute-start(bf16[2,64,128]{2,1,0:T(8,128)(2,1)S(1)} %pad_maximum_fusion.15), channel_id=1, source_target_pairs={{0,6},{1,7},{2,4},{3,5},{4,2},{5,3},{6,0},{7,1},{8,14},{9,15},{10,... | collective-permute-start | bytes 98312 | tf_op jit(solution)/shard_map/ppermute | solution.py:717
  118.4 4.2 %collective-permute-start.19 = (bf16[2,64,128]{2,1,0:T(8,128)(2,1)S(1)}, bf16[2,64,128]{2,1,0:T(8,128)(2,1)S(1)}, u32[]{:S(2)}, u32[]{:S(2)}) collective-permute-start(bf16[2,64,128]{2,1,0:T(8,128)(2,1)S(1)} %pad_maximum_fusion.15), channel_id=1, source_target_pairs={{0,4},{1,5},{2,6},{3,7},{4,0},{5,1},{6,2},{7,3},{8,12},{9,13},{10,... | collective-permute-start | bytes 98312 | tf_op jit(solution)/shard_map/ppermute | solution.py:717
  120.1 3.9 %collective-permute-start.18 = (bf16[2,64,128]{2,1,0:T(8,128)(2,1)S(1)}, bf16[2,64,128]{2,1,0:T(8,128)(2,1)S(1)}, u32[]{:S(2)}, u32[]{:S(2)}) collective-permute-start(bf16[2,64,128]{2,1,0:T(8,128)(2,1)S(1)} %pad_maximum_fusion.15), channel_id=1, source_target_pairs={{0,2},{1,3},{2,0},{3,1},{4,6},{5,7},{6,4},{7,5},{8,10},{9,11},{10,... | collective-permute-start | bytes 98312 | tf_op jit(solution)/shard_map/ppermute | solution.py:717
  124.2 4.2 %copy-start.5 = (bf16[2,2,2,64,1024]{4,3,2,1,0:T(8,128)(2,1)}, bf16[2,2,2,64,1024]{4,3,2,1,0:T(8,128)(2,1)S(1)}, u32[]{:S(2)}) copy-start(bf16[2,2,2,64,1024]{4,3,2,1,0:T(8,128)(2,1)S(1)} %copy.10) | copy-start | bytes 3145732
  124.2 4.2 %collective-permute-start.21 = (bf16[4,2,64,1024]{3,2,1,0:T(8,128)(2,1)S(1)}, bf16[4,2,64,1024]{3,2,1,0:T(8,128)(2,1)S(1)}, u32[]{:S(2)}, u32[]{:S(2)}) collective-permute-start(bf16[4,2,64,1024]{3,2,1,0:T(8,128)(2,1)S(1)} %bitcast.40), channel_id=1, source_target_pairs={{0,1},{1,0},{2,3},{3,2},{4,5},{5,4},{6,7},{7,6},{8,9},{9,8},{10,11... | collective-permute-start | bytes 3145736 | tf_op jit(solution)/shard_map/ppermute | solution.py:717
  124.3 4.1 %collective-permute-start.23 = (bf16[4,2,192,128]{3,2,1,0:T(8,128)(2,1)S(1)}, bf16[4,2,192,128]{3,2,1,0:T(8,128)(2,1)S(1)}, u32[]{:S(2)}, u32[]{:S(2)}) collective-permute-start(bf16[4,2,192,128]{3,2,1,0:T(8,128)(2,1)S(1)} %bitcast.48), channel_id=1, source_target_pairs={{0,1},{1,0},{2,3},{3,2},{4,5},{5,4},{6,7},{7,6},{8,9},{9,8},{10,11... | collective-permute-start | bytes 1179656 | tf_op jit(solution)/shard_map/ppermute | solution.py:717
  124.8 2.9 %collective-permute-start.22 = (bf16[4,2,64,128]{3,2,1,0:T(8,128)(2,1)S(1)}, bf16[4,2,64,128]{3,2,1,0:T(8,128)(2,1)S(1)}, u32[]{:S(2)}, u32[]{:S(2)}) collective-permute-start(bf16[4,2,64,128]{3,2,1,0:T(8,128)(2,1)S(1)} %get-tuple-element.79), channel_id=1, source_target_pairs={{0,1},{1,0},{2,3},{3,2},{4,5},{5,4},{6,7},{7,6},{8,9},{9,8},{10,11... | collective-permute-start | bytes 393224 | tf_op jit(solution)/shard_map/ppermute | solution.py:717
  124.9 12.1 %collective-permute-start.24 = (bf16[2,384,128]{2,1,0:T(8,128)(2,1)S(1)}, bf16[2,384,128]{2,1,0:T(8,128)(2,1)S(1)}, u32[]{:S(2)}, u32[]{:S(2)}) collective-permute-start(bf16[2,384,128]{2,1,0:T(8,128)(2,1)S(1)} %get-tuple-element.63), channel_id=1, source_target_pairs={{0,8},{1,9},{2,10},{3,11},{4,12},{5,13},{6,14},{7,15},{8,0},{9,1},... | collective-permute-start | bytes 589832 | tf_op jit(solution)/shard_map/ppermute | solution.py:717
  128.5 0.7 copy-start.11
  129.2 1.0 copy-start.10
  137.8 5.3 %collective-permute-start.25 = (bf16[384,128]{1,0:T(8,128)(2,1)S(1)}, bf16[384,128]{1,0:T(8,128)(2,1)S(1)}, u32[]{:S(2)}, u32[]{:S(2)}) collective-permute-start(bf16[384,128]{1,0:T(8,128)(2,1)S(1)} %get-tuple-element.66), channel_id=1, source_target_pairs={{0,16},{1,17},{2,18},{3,19},{4,20},{5,21},{6,22},{7,23},{8,24},{9,... | collective-permute-start | bytes 294920 | tf_op jit(solution)/shard_map/ppermute | solution.py:717
  143.2 12.3 %collective-permute-start.28 = (bf16[2,384,128]{2,1,0:T(8,128)(2,1)S(1)}, bf16[2,384,128]{2,1,0:T(8,128)(2,1)S(1)}, u32[]{:S(2)}, u32[]{:S(2)}) collective-permute-start(bf16[2,384,128]{2,1,0:T(8,128)(2,1)S(1)} %get-tuple-element.77), channel_id=1, source_target_pairs={{0,6},{1,7},{2,4},{3,5},{4,2},{5,3},{6,0},{7,1},{8,14},{9,15},{10,... | collective-permute-start | bytes 589832 | tf_op jit(solution)/shard_map/ppermute | solution.py:717
  143.2 12.2 %collective-permute-start.27 = (bf16[2,384,128]{2,1,0:T(8,128)(2,1)S(1)}, bf16[2,384,128]{2,1,0:T(8,128)(2,1)S(1)}, u32[]{:S(2)}, u32[]{:S(2)}) collective-permute-start(bf16[2,384,128]{2,1,0:T(8,128)(2,1)S(1)} %get-tuple-element.77), channel_id=1, source_target_pairs={{0,4},{1,5},{2,6},{3,7},{4,0},{5,1},{6,2},{7,3},{8,12},{9,13},{10,... | collective-permute-start | bytes 589832 | tf_op jit(solution)/shard_map/ppermute | solution.py:717
  145.7 9.7 %collective-permute-start.26 = (bf16[2,384,128]{2,1,0:T(8,128)(2,1)S(1)}, bf16[2,384,128]{2,1,0:T(8,128)(2,1)S(1)}, u32[]{:S(2)}, u32[]{:S(2)}) collective-permute-start(bf16[2,384,128]{2,1,0:T(8,128)(2,1)S(1)} %get-tuple-element.77), channel_id=1, source_target_pairs={{0,2},{1,3},{2,0},{3,1},{4,6},{5,7},{6,4},{7,5},{8,10},{9,11},{10,... | collective-permute-start | bytes 589832 | tf_op jit(solution)/shard_map/ppermute | solution.py:717
  155.6 2.4 %collective-permute-start.29 = (bf16[4,2,384,128]{3,2,1,0:T(8,128)(2,1)S(1)}, bf16[4,2,384,128]{3,2,1,0:T(8,128)(2,1)S(1)}, u32[]{:S(2)}, u32[]{:S(2)}) collective-permute-start(bf16[4,2,384,128]{3,2,1,0:T(8,128)(2,1)S(1)} %pad_maximum_fusion.1.same), channel_id=1, source_target_pairs={{0,1},{1,0},{2,3},{3,2},{4,5},{5,4},{6,7},{7,6},{8,9},{9,8},{10,11... | collective-permute-start | bytes 2359304 | tf_op jit(solution)/shard_map/ppermute | solution.py:717
  157.9 1.0 copy-start.2

commit v11 on v10

--- a/solution.py
+++ b/solution.py
@@ -761,24 +761,26 @@
     dealt = [swap(block, 2 * j) if j else block for j, block in enumerate(dealt)]
 
     weight, ups = join(stretch_adapter, adapter_owner, arrived)
-    base = along_z(after(base, arrived[1]))
-    partial_sums = narrow(after(weight, base), dealt)
+    partial_sums = narrow(weight, dealt)
     back = [swap(block, 2 * j) if j else block for j, block in enumerate(partial_sums)]
     back = sum(block.astype(jnp.float32) for block in back)
-    ups = along_z(after(ups, *partial_sums))
-    own_rank = swap(after(back[1].astype(jnp.bfloat16), ups), 1)
+    base = after(base, *partial_sums)
+    base = [base, swap(base, 2), swap(base, 4)]
+    own_rank = swap(after(back[1].astype(jnp.bfloat16), *base), 1)
     own_rank = back[0] + own_rank.astype(jnp.float32)
     own_rank = own_rank.astype(jnp.bfloat16)
-    base = along_x(after(base, *partial_sums))
+    base = jnp.stack(base + [swap(after(base[2], own_rank), 2)])
     all_rank = own_rank[:, ADAPTER_RANK:]
-    ups = along_x(after(ups, own_rank))
+    ups = along_z(after(ups, own_rank))
     all_rank = jnp.stack([all_rank, swap(all_rank, PIECES)])
     all_rank = after(all_rank, ups)
+    ups = along_x(after(ups, all_rank))
     far = swap(after(far, all_rank), PIECES)
     all_rank = jnp.stack([swap(all_rank, apart) if apart else all_rank for apart in (0, 2, 4, 6)])
     base = after(base, all_rank)
     base = (base, swap(base, 1))
-    ups = (ups, swap(after(ups, all_rank), 1))
+    all_rank = after(all_rank, ups)
+    ups = (ups, swap(ups, 1))
     all_rank = jnp.stack([all_rank, swap(all_rank, 1)])
 
     shared = (query_base, base, own_rank, all_rank, ups, cosines, sines)

time: 163 us -> 149 us (0.914)
  waiting for transfers between devices: 88.9 us -> 68.4 us
  starting transfers between devices: 36.9 us -> 45.3 us
    ppermute x30 -> x31, waiting for transfers between devices: 86.7 us -> 66.2 us  [swap(): lax.ppermute(block, ('groups', 'ctx'), [(i, i ^ mask) for i in range(4 *...]
    ppermute x30 -> x31, starting transfers between devices: 31.4 us -> 39.8 us  [swap(): lax.ppermute(block, ('groups', 'ctx'), [(i, i ^ mask) for i in range(4 *...]
    unnamed x25 -> x23, local copies, waits for them, and re-layouts: 4.53 us -> 3.52 us
  transfers between devices with their start and end apart: 31 -> 32, of which waited for: 19 -> 19; matrix products, arithmetic and copies ran while one was open for 3% -> 3% of each run, Pallas kernels for 9% -> 10%
where the time goes in v11:
time: 149 us
  waiting for transfers between devices  68.4 us (46%)
  starting transfers between devices  45.3 us (30%)
  Pallas kernels  26 us (17%)
  other arithmetic  4.49 us (3%)
  local copies, waits for them, and re-layouts  3.7 us (2%)
    ppermute x31, waiting for transfers between devices, swap(): lax.ppermute(block, ('groups', 'ctx'), [(i, i ^ mask) for i in range(4 *...  66.2 us
    ppermute x31, starting transfers between devices, swap(): lax.ppermute(block, ('groups', 'ctx'), [(i, i ^ mask) for i in range(4 *...  39.8 us
    pallas_call x2, Pallas kernels, attend(): pl.pallas_call(partial(attend_kernel, first_head), grid=(heads,), out_sha...  13.2 us
    all_to_all x1, starting transfers between devices, direct_shards(): spread = lax.all_to_all(packed, 'ctx', 0, 0, axis_index_groups=blocks)  5.5 us
    pallas_call x1, Pallas kernels, pack_row(): pl.pallas_call(partial(pack_kernel, sections), out_shape=jax.ShapeDtypeSt...  5.16 us
    unnamed x23, local copies, waits for them, and re-layouts  3.52 us
    pallas_call x1, Pallas kernels, widen(): pl.pallas_call(widen_kernel, out_shape=jax.ShapeDtypeStruct((attended.sha...  3.06 us
  transfers between devices with their start and end apart: 32, of which 19 were waited for; matrix products, arithmetic and copies ran while one was open for 3% of the time, Pallas kernels for 10%

profile of v11, /device:TPU:0, one launch (start us, length us, event | category | flops | bytes accessed | tf_op | source)
XLA Modules:
  0.0 149.0 jit_solution(6554119143695864517)
XLA Ops:
  0.6 5.2 %shard_map.86.refs_0_ = bf16[8,1312,128]{2,1,0:T(8,128)(2,1)} custom-call(bf16[1,2686976]{1,0:T(2,128)(2,1)} %pool.1), custom_call_target="tpu_custom_call" | custom-call | bytes 8388608 | tf_op jit(solution)/shard_map/pallas_call | solution.py:316
  5.8 5.5 %all-to-all-start = ((bf16[8,1312,128]{2,1,0:T(8,128)(2,1)}), bf16[8,1312,128]{2,1,0:T(8,128)(2,1)}, u32[]{:S(2)}, u32[]{:S(2)}) async-start(bf16[8,1312,128]{2,1,0:T(8,128)(2,1)} %shard_map.86.refs_0_), calls=%async_computation | async-start | bytes 5373952 | tf_op jit(solution)/shard_map/all_to_all | solution.py:756
  11.3 2.2 %collective-permute-start.1 = (s32[2]{0:T(128)S(1)}, s32[2]{0:T(128)S(1)}, u32[]{:S(2)}, u32[]{:S(2)}) collective-permute-start(s32[2]{0:T(128)S(1)} %copy-done.3), channel_id=1, source_target_pairs={{0,16},{1,17},{2,18},{3,19},{4,20},{5,21},{6,22},{7,23},{8,24},{9,... | collective-permute-start | bytes 32 | tf_op jit(solution)/shard_map/ppermute | solution.py:717
  13.6 1.2 copy-done.1
  14.8 0.3 shard_map.87
  15.1 0.1 collective-permute-start.2
  15.2 0.5 copy-done.8
  15.7 2.6 %collective-permute-start = (bf16[64,1024]{1,0:T(8,128)(2,1)S(1)}, bf16[64,1024]{1,0:T(8,128)(2,1)S(1)}, u32[]{:S(2)}, u32[]{:S(2)}) collective-permute-start(bf16[64,1024]{1,0:T(8,128)(2,1)S(1)} %constant_dynamic-update-slice_fusion), channel_id=1, source_target_pairs={{0,8},{1,9},{2,10},{3,11},{4,12},{5,13},{6,14},{7,15},{8,0},{9,1},... | collective-permute-start | bytes 393224 | tf_op jit(solution)/shard_map/ppermute | solution.py:717
  18.4 1.9 %fusion = (f32[1024,64]{1,0:T(8,128)S(1)}, f32[1024,64]{1,0:T(8,128)S(1)}, f32[1024,64]{1,0:T(8,128)S(1)}) fusion(f32[64]{0:T(128)S(1)} %multiply_power_fusion, f32[1024]{0:T(1024)S(1)} %iota_convert_fusion), kind=kLoop, calls=%fused_computation.15 | loop fusion | flops 131072 | bytes 790784 | tf_op jit(solution)/shard_map/neg | solution.py:733
  20.3 1.3 pad_maximum_fusion.2
  21.6 22.4 %collective-permute-done = bf16[64,1024]{1,0:T(8,128)(2,1)S(1)} collective-permute-done((bf16[64,1024]{1,0:T(8,128)(2,1)S(1)}, bf16[64,1024]{1,0:T(8,128)(2,1)S(1)}, u32[]{:S(2)}, u32[]{:S(2)}) %collective-permute-start) | collective-permute-done | bytes 131104 | tf_op jit(solution)/shard_map/ppermute | solution.py:717
  44.2 2.1 %all-to-all-done.spread = bf16[8,1312,128]{2,1,0:T(8,128)(2,1)} async-done(((bf16[8,1312,128]{2,1,0:T(8,128)(2,1)}), bf16[8,1312,128]{2,1,0:T(8,128)(2,1)}, u32[]{:S(2)}, u32[]{:S(2)}) %all-to-all-start) | async-done | bytes 2687008 | tf_op jit(solution)/shard_map/all_to_all | solution.py:756
  46.3 2.1 %shard_map.88 = (bf16[960,128]{1,0:T(8,128)(2,1)S(1)}, bf16[960,128]{1,0:T(8,128)(2,1)S(1)}, bf16[960,128]{1,0:T(8,128)(2,1)S(1)}, bf16[960,128]{1,0:T(8,128)(2,...) custom-call(s32[2]{0:T(128)S(1)} %copy-done.3, s32[2]{0:T(128)S(1)} %collective-permute-done.1.there, ...), custom_call_target="tpu_custom_call" | custom-call | bytes 3145728 | tf_op jit(solution)/shard_map/pallas_call | solution.py:360
  48.4 1.3 collective-permute-start.3
  49.9 1.7 %collective-permute-start.6 = (bf16[2,64,1024]{2,1,0:T(8,128)(2,1)S(1)}, bf16[2,64,1024]{2,1,0:T(8,128)(2,1)S(1)}, u32[]{:S(2)}, u32[]{:S(2)}) collective-permute-start(bf16[2,64,1024]{2,1,0:T(8,128)(2,1)S(1)} %get-tuple-element.43), channel_id=1, source_target_pairs={{0,2},{1,3},{2,0},{3,1},{4,6},{5,7},{6,4},{7,5},{8,10},{9,11},{10,... | collective-permute-start | bytes 786440 | tf_op jit(solution)/shard_map/ppermute | solution.py:717
  51.6 2.2 %collective-permute-start.7 = (bf16[2,64,1024]{2,1,0:T(8,128)(2,1)S(1)}, bf16[2,64,1024]{2,1,0:T(8,128)(2,1)S(1)}, u32[]{:S(2)}, u32[]{:S(2)}) collective-permute-start(bf16[2,64,1024]{2,1,0:T(8,128)(2,1)S(1)} %get-tuple-element.44), channel_id=1, source_target_pairs={{0,4},{1,5},{2,6},{3,7},{4,0},{5,1},{6,2},{7,3},{8,12},{9,13},{10,... | collective-permute-start | bytes 786440 | tf_op jit(solution)/shard_map/ppermute | solution.py:717
  53.8 1.7 %collective-permute-start.4 = (bf16[960,128]{1,0:T(8,128)(2,1)S(1)}, bf16[960,128]{1,0:T(8,128)(2,1)S(1)}, u32[]{:S(2)}, u32[]{:S(2)}) collective-permute-start(bf16[960,128]{1,0:T(8,128)(2,1)S(1)} %get-tuple-element.38), channel_id=1, source_target_pairs={{0,16},{1,17},{2,18},{3,19},{4,20},{5,21},{6,22},{7,23},{8,24},{9,... | collective-permute-start | bytes 737288 | tf_op jit(solution)/shard_map/ppermute | solution.py:717
  55.5 6.7 %collective-permute-done.3.refs_1_ = bf16[960,128]{1,0:T(8,128)(2,1)S(1)} collective-permute-done((bf16[960,128]{1,0:T(8,128)(2,1)S(1)}, bf16[960,128]{1,0:T(8,128)(2,1)S(1)}, u32[]{:S(2)}, u32[]{:S(2)}) %collective-permute-start.3) | collective-permute-done | bytes 245792 | tf_op jit(solution)/shard_map/ppermute | solution.py:717
  62.2 1.1 collective-permute-start.5
  63.2 8.4 %collective-permute-done.5.refs_3_ = bf16[960,128]{1,0:T(8,128)(2,1)S(1)} collective-permute-done((bf16[960,128]{1,0:T(8,128)(2,1)S(1)}, bf16[960,128]{1,0:T(8,128)(2,1)S(1)}, u32[]{:S(2)}, u32[]{:S(2)}) %collective-permute-start.5) | collective-permute-done | bytes 245792 | tf_op jit(solution)/shard_map/ppermute | solution.py:717
  71.7 1.0 shard_map.89
  72.6 1.1 collective-permute-done.8.refs_3_
  73.8 0.4 shard_map.90
  74.2 5.7 %collective-permute-start.13 = (bf16[2,64,192]{2,1,0:T(8,128)(2,1)S(1)}, bf16[2,64,192]{2,1,0:T(8,128)(2,1)S(1)}, u32[]{:S(2)}, u32[]{:S(2)}) collective-permute-start(bf16[2,64,192]{2,1,0:T(8,128)(2,1)S(1)} %get-tuple-element.49), channel_id=1, source_target_pairs={{0,6},{1,7},{2,4},{3,5},{4,2},{5,3},{6,0},{7,1},{8,14},{9,15},{10,... | collective-permute-start | bytes 147464 | tf_op jit(solution)/shard_map/ppermute | solution.py:717
  79.9 0.6 collective-permute-start.11
  80.6 1.4 collective-permute-start.9
  81.9 2.0 %collective-permute-start.10 = (bf16[2,64,1024]{2,1,0:T(8,128)(2,1)S(1)}, bf16[2,64,1024]{2,1,0:T(8,128)(2,1)S(1)}, u32[]{:S(2)}, u32[]{:S(2)}) collective-permute-start(bf16[2,64,1024]{2,1,0:T(8,128)(2,1)S(1)} %pad_maximum_fusion.5), channel_id=1, source_target_pairs={{0,4},{1,5},{2,6},{3,7},{4,0},{5,1},{6,2},{7,3},{8,12},{9,13},{10,... | collective-permute-start | bytes 786440 | tf_op jit(solution)/shard_map/ppermute | solution.py:717
  84.0 0.9 collective-permute-done.12
  84.8 0.1 collective-permute-done.11
  85.0 4.1 %collective-permute-done.9 = bf16[2,64,1024]{2,1,0:T(8,128)(2,1)S(1)} collective-permute-done((bf16[2,64,1024]{2,1,0:T(8,128)(2,1)S(1)}, bf16[2,64,1024]{2,1,0:T(8,128)(2,1)S(1)}, u32[]{:S(2)}, u32[]{:S(2)}) %collective-permute-start.9) | collective-permute-done | bytes 262176 | tf_op jit(solution)/shard_map/ppermute | solution.py:717
  89.2 1.2 collective-permute-done.14
  90.4 0.1 slice_bitcast_fusion.1
  90.5 2.6 %collective-permute-start.16 = (bf16[64,128]{1,0:T(8,128)(2,1)S(1)}, bf16[64,128]{1,0:T(8,128)(2,1)S(1)}, u32[]{:S(2)}, u32[]{:S(2)}) collective-permute-start(bf16[64,128]{1,0:T(8,128)(2,1)S(1)} %get-tuple-element.77), channel_id=1, source_target_pairs={{0,8},{1,9},{2,10},{3,11},{4,12},{5,13},{6,14},{7,15},{8,0},{9,1},... | collective-permute-start | bytes 49160 | tf_op jit(solution)/shard_map/ppermute | solution.py:717
  93.1 1.7 %collective-permute-start.17 = (bf16[2,192,128]{2,1,0:T(8,128)(2,1)S(1)}, bf16[2,192,128]{2,1,0:T(8,128)(2,1)S(1)}, u32[]{:S(2)}, u32[]{:S(2)}) collective-permute-start(bf16[2,192,128]{2,1,0:T(8,128)(2,1)S(1)} %get-tuple-element.54), channel_id=1, source_target_pairs={{0,4},{1,5},{2,6},{3,7},{4,0},{5,1},{6,2},{7,3},{8,12},{9,13},{10,... | collective-permute-start | bytes 294920 | tf_op jit(solution)/shard_map/ppermute | solution.py:717
  94.8 1.0 collective-permute-start.15
  95.8 1.9 %collective-permute-done.17 = bf16[2,192,128]{2,1,0:T(8,128)(2,1)S(1)} collective-permute-done((bf16[2,192,128]{2,1,0:T(8,128)(2,1)S(1)}, bf16[2,192,128]{2,1,0:T(8,128)(2,1)S(1)}, u32[]{:S(2)}, u32[]{:S(2)}) %collective-permute-start.17) | collective-permute-done | bytes 98336 | tf_op jit(solution)/shard_map/ppermute | solution.py:717
  97.7 2.2 %collective-permute-start.20 = (bf16[2,64,128]{2,1,0:T(8,128)(2,1)S(1)}, bf16[2,64,128]{2,1,0:T(8,128)(2,1)S(1)}, u32[]{:S(2)}, u32[]{:S(2)}) collective-permute-start(bf16[2,64,128]{2,1,0:T(8,128)(2,1)S(1)} %pad_maximum_fusion.14), channel_id=1, source_target_pairs={{0,6},{1,7},{2,4},{3,5},{4,2},{5,3},{6,0},{7,1},{8,14},{9,15},{10,... | collective-permute-start | bytes 98312 | tf_op jit(solution)/shard_map/ppermute | solution.py:717
  99.9 0.2 collective-permute-start.19
  100.2 1.1 collective-permute-start.18
  101.3 1.4 collective-permute-done.20
  102.7 1.2 collective-permute-done.19
  103.9 0.2 collective-permute-done.18
  104.1 0.1 pad_maximum_fusion.key_same.value_same
  104.3 0.1 collective-permute-start.21
  104.4 1.1 collective-permute-start.22
  105.5 6.2 %collective-permute-done.22 = bf16[2,2,192,128]{3,2,1,0:T(8,128)(2,1)S(1)} collective-permute-done((bf16[2,2,192,128]{3,2,1,0:T(8,128)(2,1)S(1)}, bf16[2,2,192,128]{3,2,1,0:T(8,128)(2,1)S(1)}, u32[]{:S(2)}, u32[]{:S(2)}) %collective-permute-start.22) | collective-permute-done | bytes 196640 | tf_op jit(solution)/shard_map/ppermute | solution.py:717
  111.9 0.5 collective-permute-start.23
  112.3 0.7 collective-permute-start.25
  113.0 0.7 collective-permute-done.23
  113.8 0.7 pad_maximum_fusion.10.all_rank
  114.5 0.7 copy-done.10
  115.2 4.5 %shard_map.91.refs_0_ = bf16[64,4096]{1,0:T(8,128)(2,1)} custom-call(bf16[64,4096]{1,0:T(8,128)(2,1)} %query_block.3, bf16[4,2,64,1024]{3,2,1,0:T(8,128)(2,1)} %copy-done.5, bf16[4,2,64,1024]{3,2,1,0:T(8,128)(2,1)} %collective-permute-done.21.key_other.value_other, bf16[4,2,64,1024]{3,2,1,0:T(8,128)(2,1)} %copy-done.5, ...), custom_call_target="tpu_custom_call" | custom-call | flops 3221225472 | bytes 10485760 | tf_op jit(solution)/shard_map/pallas_call | solution.py:634
  119.7 4.6 %collective-permute-done.25.far = bf16[2,384,128]{2,1,0:T(8,128)(2,1)S(1)} collective-permute-done((bf16[2,384,128]{2,1,0:T(8,128)(2,1)S(1)}, bf16[2,384,128]{2,1,0:T(8,128)(2,1)S(1)}, u32[]{:S(2)}, u32[]{:S(2)}) %collective-permute-start.25) | collective-permute-done | bytes 196640 | tf_op jit(solution)/shard_map/ppermute | solution.py:717
  124.3 0.8 shard_map.93
  125.1 2.2 %collective-permute-start.26 = (bf16[384,128]{1,0:T(8,128)(2,1)S(1)}, bf16[384,128]{1,0:T(8,128)(2,1)S(1)}, u32[]{:S(2)}, u32[]{:S(2)}) collective-permute-start(bf16[384,128]{1,0:T(8,128)(2,1)S(1)} %get-tuple-element.64), channel_id=1, source_target_pairs={{0,16},{1,17},{2,18},{3,19},{4,20},{5,21},{6,22},{7,23},{8,24},{9,... | collective-permute-start | bytes 294920 | tf_op jit(solution)/shard_map/ppermute | solution.py:717
  127.4 2.6 %collective-permute-done.26 = bf16[384,128]{1,0:T(8,128)(2,1)S(1)} collective-permute-done((bf16[384,128]{1,0:T(8,128)(2,1)S(1)}, bf16[384,128]{1,0:T(8,128)(2,1)S(1)}, u32[]{:S(2)}, u32[]{:S(2)}) %collective-permute-start.26) | collective-permute-done | bytes 98336 | tf_op jit(solution)/shard_map/ppermute | solution.py:717
  130.0 0.1 collective-permute-start.29
  130.1 2.6 %collective-permute-start.28 = (bf16[2,384,128]{2,1,0:T(8,128)(2,1)S(1)}, bf16[2,384,128]{2,1,0:T(8,128)(2,1)S(1)}, u32[]{:S(2)}, u32[]{:S(2)}) collective-permute-start(bf16[2,384,128]{2,1,0:T(8,128)(2,1)S(1)} %get-tuple-element.75), channel_id=1, source_target_pairs={{0,4},{1,5},{2,6},{3,7},{4,0},{5,1},{6,2},{7,3},{8,12},{9,13},{10,... | collective-permute-start | bytes 589832 | tf_op jit(solution)/shard_map/ppermute | solution.py:717
  132.7 0.8 collective-permute-start.27
  133.5 8.7 %shard_map.92.attended_rows = bf16[64,4096]{1,0:T(8,128)(2,1)} custom-call(bf16[64,4096]{1,0:T(8,128)(2,1)} %query_block.3, bf16[4,2,64,1024]{3,2,1,0:T(8,128)(2,1)} %copy-done.5, bf16[4,2,64,1024]{3,2,1,0:T(8,128)(2,1)} %collective-permute-done.21.key_other.value_other, bf16[4,2,64,1024]{3,2,1,0:T(8,128)(2,1)} %copy-done.5, ...), custom_call_target="tpu_custom_call", output_to_operand_aliasing={{}: (11, {})} | custom-call | flops 9663676416 | bytes 10485760 | tf_op jit(solution)/shard_map/pallas_call | solution.py:634
  142.3 0.1 pad_maximum_fusion.1.same
  142.5 2.3 %collective-permute-done.30.other = bf16[4,2,384,128]{3,2,1,0:T(8,128)(2,1)S(1)} collective-permute-done((bf16[4,2,384,128]{3,2,1,0:T(8,128)(2,1)S(1)}, bf16[4,2,384,128]{3,2,1,0:T(8,128)(2,1)S(1)}, u32[]{:S(2)}, u32[]{:S(2)}) %collective-permute-start.30) | collective-permute-done | bytes 786464 | tf_op jit(solution)/shard_map/ppermute | solution.py:717
  144.7 1.0 copy-done.2
  145.8 3.1 %shard_map.94 = bf16[64,8192]{1,0:T(8,128)(2,1)} custom-call(bf16[64,4096]{1,0:T(8,128)(2,1)S(1)} %copy-done.2, bf16[4,2,384,128]{3,2,1,0:T(8,128)(2,1)S(1)} %pad_maximum_fusion.1.same, bf16[4,2,384,128]{3,2,1,0:T(8,128)(2,1)S(1)} %collective-permute-done.30.other), custom_call_target="tpu_custom_call" | custom-call | flops 134217728 | bytes 4194304 | tf_op jit(solution)/shard_map/pallas_call | solution.py:700
  (55 shorter events, 0.7 us)
Async XLA Ops:
  5.8 5.5 %copy-start.3 = (s32[2]{0:T(128)S(1)}, s32[2]{0:T(128)}, u32[]{:S(2)}) copy-start(s32[2]{0:T(128)} %here.5) | copy-start | bytes 28
  5.8 7.8 %copy-start = (bf16[8,1312,128]{2,1,0:T(8,128)(2,1)S(1)}, bf16[8,1312,128]{2,1,0:T(8,128)(2,1)}, u32[]{:S(2)}) copy-start(bf16[8,1312,128]{2,1,0:T(8,128)(2,1)} %shard_map.86.refs_0_) | copy-start | bytes 8060932
  5.8 40.5 %all-to-all-start = ((bf16[8,1312,128]{2,1,0:T(8,128)(2,1)}), bf16[8,1312,128]{2,1,0:T(8,128)(2,1)}, u32[]{:S(2)}, u32[]{:S(2)}) async-start(bf16[8,1312,128]{2,1,0:T(8,128)(2,1)} %shard_map.86.refs_0_), calls=%async_computation | async-start | bytes 5373952 | tf_op jit(solution)/shard_map/all_to_all | solution.py:756
  11.3 35.0 %collective-permute-start.1 = (s32[2]{0:T(128)S(1)}, s32[2]{0:T(128)S(1)}, u32[]{:S(2)}, u32[]{:S(2)}) collective-permute-start(s32[2]{0:T(128)S(1)} %copy-done.3), channel_id=1, source_target_pairs={{0,16},{1,17},{2,18},{3,19},{4,20},{5,21},{6,22},{7,23},{8,24},{9,... | collective-permute-start | bytes 32 | tf_op jit(solution)/shard_map/ppermute | solution.py:717
  13.6 1.2 copy-start.1
  14.8 0.8 copy-start.8
  14.8 0.9 copy-start.9
  15.1 29.0 %collective-permute-start.2 = (bf16[4,64,1024]{2,1,0:T(8,128)(2,1)S(1)}, bf16[4,64,1024]{2,1,0:T(8,128)(2,1)S(1)}, u32[]{:S(2)}, u32[]{:S(2)}) collective-permute-start(bf16[4,64,1024]{2,1,0:T(8,128)(2,1)S(1)} %get-tuple-element.34), channel_id=1, source_target_pairs={{0,1},{1,0},{2,3},{3,2},{4,5},{5,4},{6,7},{7,6},{8,9},{9,8},{10,11... | collective-permute-start | bytes 1572872 | tf_op jit(solution)/shard_map/ppermute | solution.py:717
  15.7 28.4 %collective-permute-start = (bf16[64,1024]{1,0:T(8,128)(2,1)S(1)}, bf16[64,1024]{1,0:T(8,128)(2,1)S(1)}, u32[]{:S(2)}, u32[]{:S(2)}) collective-permute-start(bf16[64,1024]{1,0:T(8,128)(2,1)S(1)} %constant_dynamic-update-slice_fusion), channel_id=1, source_target_pairs={{0,8},{1,9},{2,10},{3,11},{4,12},{5,13},{6,14},{7,15},{8,0},{9,1},... | collective-permute-start | bytes 393224 | tf_op jit(solution)/shard_map/ppermute | solution.py:717
  18.4 27.9 %copy-start.4 = (s32[16]{0:T(128)S(1)}, s32[16]{0:T(128)}, u32[]{:S(2)}) copy-start(s32[16]{0:T(128)} %owner.5) | copy-start | bytes 196
  48.4 13.8 %collective-permute-start.3 = (bf16[960,128]{1,0:T(8,128)(2,1)S(1)}, bf16[960,128]{1,0:T(8,128)(2,1)S(1)}, u32[]{:S(2)}, u32[]{:S(2)}) collective-permute-start(bf16[960,128]{1,0:T(8,128)(2,1)S(1)} %get-tuple-element.37), channel_id=1, source_target_pairs={{0,8},{1,9},{2,10},{3,11},{4,12},{5,13},{6,14},{7,15},{8,0},{9,1},... | collective-permute-start | bytes 737288 | tf_op jit(solution)/shard_map/ppermute | solution.py:717
  49.9 22.8 %collective-permute-start.6 = (bf16[2,64,1024]{2,1,0:T(8,128)(2,1)S(1)}, bf16[2,64,1024]{2,1,0:T(8,128)(2,1)S(1)}, u32[]{:S(2)}, u32[]{:S(2)}) collective-permute-start(bf16[2,64,1024]{2,1,0:T(8,128)(2,1)S(1)} %get-tuple-element.43), channel_id=1, source_target_pairs={{0,2},{1,3},{2,0},{3,1},{4,6},{5,7},{6,4},{7,5},{8,10},{9,11},{10,... | collective-permute-start | bytes 786440 | tf_op jit(solution)/shard_map/ppermute | solution.py:717
  51.6 21.1 %collective-permute-start.7 = (bf16[2,64,1024]{2,1,0:T(8,128)(2,1)S(1)}, bf16[2,64,1024]{2,1,0:T(8,128)(2,1)S(1)}, u32[]{:S(2)}, u32[]{:S(2)}) collective-permute-start(bf16[2,64,1024]{2,1,0:T(8,128)(2,1)S(1)} %get-tuple-element.44), channel_id=1, source_target_pairs={{0,4},{1,5},{2,6},{3,7},{4,0},{5,1},{6,2},{7,3},{8,12},{9,13},{10,... | collective-permute-start | bytes 786440 | tf_op jit(solution)/shard_map/ppermute | solution.py:717
  53.8 20.0 %collective-permute-start.8 = (bf16[2,64,1024]{2,1,0:T(8,128)(2,1)S(1)}, bf16[2,64,1024]{2,1,0:T(8,128)(2,1)S(1)}, u32[]{:S(2)}, u32[]{:S(2)}) collective-permute-start(bf16[2,64,1024]{2,1,0:T(8,128)(2,1)S(1)} %get-tuple-element.45), channel_id=1, source_target_pairs={{0,6},{1,7},{2,4},{3,5},{4,2},{5,3},{6,0},{7,1},{8,14},{9,15},{10,... | collective-permute-start | bytes 786440 | tf_op jit(solution)/shard_map/ppermute | solution.py:717
  53.8 9.4 %collective-permute-start.4 = (bf16[960,128]{1,0:T(8,128)(2,1)S(1)}, bf16[960,128]{1,0:T(8,128)(2,1)S(1)}, u32[]{:S(2)}, u32[]{:S(2)}) collective-permute-start(bf16[960,128]{1,0:T(8,128)(2,1)S(1)} %get-tuple-element.38), channel_id=1, source_target_pairs={{0,16},{1,17},{2,18},{3,19},{4,20},{5,21},{6,22},{7,23},{8,24},{9,... | collective-permute-start | bytes 737288 | tf_op jit(solution)/shard_map/ppermute | solution.py:717
  62.2 9.5 %collective-permute-start.5 = (bf16[960,128]{1,0:T(8,128)(2,1)S(1)}, bf16[960,128]{1,0:T(8,128)(2,1)S(1)}, u32[]{:S(2)}, u32[]{:S(2)}) collective-permute-start(bf16[960,128]{1,0:T(8,128)(2,1)S(1)} %get-tuple-element.39), channel_id=1, source_target_pairs={{0,24},{1,25},{2,26},{3,27},{4,28},{5,29},{6,30},{7,31},{8,16},{9,... | collective-permute-start | bytes 737288 | tf_op jit(solution)/shard_map/ppermute | solution.py:717
  74.2 9.7 %collective-permute-start.13 = (bf16[2,64,192]{2,1,0:T(8,128)(2,1)S(1)}, bf16[2,64,192]{2,1,0:T(8,128)(2,1)S(1)}, u32[]{:S(2)}, u32[]{:S(2)}) collective-permute-start(bf16[2,64,192]{2,1,0:T(8,128)(2,1)S(1)} %get-tuple-element.49), channel_id=1, source_target_pairs={{0,6},{1,7},{2,4},{3,5},{4,2},{5,3},{6,0},{7,1},{8,14},{9,15},{10,... | collective-permute-start | bytes 147464 | tf_op jit(solution)/shard_map/ppermute | solution.py:717
  79.9 4.9 %collective-permute-start.12 = (bf16[2,64,192]{2,1,0:T(8,128)(2,1)S(1)}, bf16[2,64,192]{2,1,0:T(8,128)(2,1)S(1)}, u32[]{:S(2)}, u32[]{:S(2)}) collective-permute-start(bf16[2,64,192]{2,1,0:T(8,128)(2,1)S(1)} %get-tuple-element.48), channel_id=1, source_target_pairs={{0,4},{1,5},{2,6},{3,7},{4,0},{5,1},{6,2},{7,3},{8,12},{9,13},{10,... | collective-permute-start | bytes 147464 | tf_op jit(solution)/shard_map/ppermute | solution.py:717
  79.9 5.0 %collective-permute-start.11 = (bf16[2,64,192]{2,1,0:T(8,128)(2,1)S(1)}, bf16[2,64,192]{2,1,0:T(8,128)(2,1)S(1)}, u32[]{:S(2)}, u32[]{:S(2)}) collective-permute-start(bf16[2,64,192]{2,1,0:T(8,128)(2,1)S(1)} %get-tuple-element.47), channel_id=1, source_target_pairs={{0,2},{1,3},{2,0},{3,1},{4,6},{5,7},{6,4},{7,5},{8,10},{9,11},{10,... | collective-permute-start | bytes 147464 | tf_op jit(solution)/shard_map/ppermute | solution.py:717
  80.6 8.5 %collective-permute-start.9 = (bf16[2,64,1024]{2,1,0:T(8,128)(2,1)S(1)}, bf16[2,64,1024]{2,1,0:T(8,128)(2,1)S(1)}, u32[]{:S(2)}, u32[]{:S(2)}) collective-permute-start(bf16[2,64,1024]{2,1,0:T(8,128)(2,1)S(1)} %pad_maximum_fusion.5), channel_id=1, source_target_pairs={{0,2},{1,3},{2,0},{3,1},{4,6},{5,7},{6,4},{7,5},{8,10},{9,11},{10,... | collective-permute-start | bytes 786440 | tf_op jit(solution)/shard_map/ppermute | solution.py:717
  81.9 7.2 %collective-permute-start.10 = (bf16[2,64,1024]{2,1,0:T(8,128)(2,1)S(1)}, bf16[2,64,1024]{2,1,0:T(8,128)(2,1)S(1)}, u32[]{:S(2)}, u32[]{:S(2)}) collective-permute-start(bf16[2,64,1024]{2,1,0:T(8,128)(2,1)S(1)} %pad_maximum_fusion.5), channel_id=1, source_target_pairs={{0,4},{1,5},{2,6},{3,7},{4,0},{5,1},{6,2},{7,3},{8,12},{9,13},{10,... | collective-permute-start | bytes 786440 | tf_op jit(solution)/shard_map/ppermute | solution.py:717
  89.2 1.2 collective-permute-start.14
  90.4 24.1 %copy-start.7 = (bf16[64,192]{1,0:T(8,128)(2,1)}, bf16[64,192]{1,0:T(8,128)(2,1)S(1)}, u32[]{:S(2)}) copy-start(bf16[64,192]{1,0:T(8,128)(2,1)S(1)} %fusion.2.own_rank) | copy-start | bytes 73732
  90.5 5.3 %collective-permute-start.16 = (bf16[64,128]{1,0:T(8,128)(2,1)S(1)}, bf16[64,128]{1,0:T(8,128)(2,1)S(1)}, u32[]{:S(2)}, u32[]{:S(2)}) collective-permute-start(bf16[64,128]{1,0:T(8,128)(2,1)S(1)} %get-tuple-element.77), channel_id=1, source_target_pairs={{0,8},{1,9},{2,10},{3,11},{4,12},{5,13},{6,14},{7,15},{8,0},{9,1},... | collective-permute-start | bytes 49160 | tf_op jit(solution)/shard_map/ppermute | solution.py:717
  93.1 4.6 %collective-permute-start.17 = (bf16[2,192,128]{2,1,0:T(8,128)(2,1)S(1)}, bf16[2,192,128]{2,1,0:T(8,128)(2,1)S(1)}, u32[]{:S(2)}, u32[]{:S(2)}) collective-permute-start(bf16[2,192,128]{2,1,0:T(8,128)(2,1)S(1)} %get-tuple-element.54), channel_id=1, source_target_pairs={{0,4},{1,5},{2,6},{3,7},{4,0},{5,1},{6,2},{7,3},{8,12},{9,13},{10,... | collective-permute-start | bytes 294920 | tf_op jit(solution)/shard_map/ppermute | solution.py:717
  94.8 9.4 %collective-permute-start.15 = (bf16[2,64,1024]{2,1,0:T(8,128)(2,1)S(1)}, bf16[2,64,1024]{2,1,0:T(8,128)(2,1)S(1)}, u32[]{:S(2)}, u32[]{:S(2)}) collective-permute-start(bf16[2,64,1024]{2,1,0:T(8,128)(2,1)S(1)} %collective-permute-done.10), channel_id=1, source_target_pairs={{0,2},{1,3},{2,0},{3,1},{4,6},{5,7},{6,4},{7,5},{8,10},{9,11},{10,... | collective-permute-start | bytes 786440 | tf_op jit(solution)/shard_map/ppermute | solution.py:717
  97.7 5.0 %collective-permute-start.20 = (bf16[2,64,128]{2,1,0:T(8,128)(2,1)S(1)}, bf16[2,64,128]{2,1,0:T(8,128)(2,1)S(1)}, u32[]{:S(2)}, u32[]{:S(2)}) collective-permute-start(bf16[2,64,128]{2,1,0:T(8,128)(2,1)S(1)} %pad_maximum_fusion.14), channel_id=1, source_target_pairs={{0,6},{1,7},{2,4},{3,5},{4,2},{5,3},{6,0},{7,1},{8,14},{9,15},{10,... | collective-permute-start | bytes 98312 | tf_op jit(solution)/shard_map/ppermute | solution.py:717
  99.9 3.9 %collective-permute-start.19 = (bf16[2,64,128]{2,1,0:T(8,128)(2,1)S(1)}, bf16[2,64,128]{2,1,0:T(8,128)(2,1)S(1)}, u32[]{:S(2)}, u32[]{:S(2)}) collective-permute-start(bf16[2,64,128]{2,1,0:T(8,128)(2,1)S(1)} %pad_maximum_fusion.14), channel_id=1, source_target_pairs={{0,4},{1,5},{2,6},{3,7},{4,0},{5,1},{6,2},{7,3},{8,12},{9,13},{10,... | collective-permute-start | bytes 98312 | tf_op jit(solution)/shard_map/ppermute | solution.py:717
  100.2 3.9 %collective-permute-start.18 = (bf16[2,64,128]{2,1,0:T(8,128)(2,1)S(1)}, bf16[2,64,128]{2,1,0:T(8,128)(2,1)S(1)}, u32[]{:S(2)}, u32[]{:S(2)}) collective-permute-start(bf16[2,64,128]{2,1,0:T(8,128)(2,1)S(1)} %pad_maximum_fusion.14), channel_id=1, source_target_pairs={{0,2},{1,3},{2,0},{3,1},{4,6},{5,7},{6,4},{7,5},{8,10},{9,11},{10,... | collective-permute-start | bytes 98312 | tf_op jit(solution)/shard_map/ppermute | solution.py:717
  104.3 10.2 %copy-start.5 = (bf16[4,2,64,1024]{3,2,1,0:T(8,128)(2,1)}, bf16[4,2,64,1024]{3,2,1,0:T(8,128)(2,1)S(1)}, u32[]{:S(2)}) copy-start(bf16[4,2,64,1024]{3,2,1,0:T(8,128)(2,1)S(1)} %pad_maximum_fusion.key_same.value_same) | copy-start | bytes 3145732
  104.3 10.2 %collective-permute-start.21 = (bf16[4,2,64,1024]{3,2,1,0:T(8,128)(2,1)S(1)}, bf16[4,2,64,1024]{3,2,1,0:T(8,128)(2,1)}, u32[]{:S(2)}, u32[]{:S(2)}) collective-permute-start(bf16[4,2,64,1024]{3,2,1,0:T(8,128)(2,1)S(1)} %pad_maximum_fusion.key_same.value_same), channel_id=1, source_target_pairs={{0,1},{1,0},{2,3},{3,2},{4,5},{5,4},{6,7},{7,6},{8,9},{9,8},{10,11... | collective-permute-start | bytes 3145736 | tf_op jit(solution)/shard_map/ppermute | solution.py:717
  104.4 7.3 %collective-permute-start.22 = (bf16[2,2,192,128]{3,2,1,0:T(8,128)(2,1)S(1)}, bf16[2,2,192,128]{3,2,1,0:T(8,128)(2,1)S(1)}, u32[]{:S(2)}, u32[]{:S(2)}) collective-permute-start(bf16[2,2,192,128]{3,2,1,0:T(8,128)(2,1)S(1)} %pad_maximum_fusion.11), channel_id=1, source_target_pairs={{0,2},{1,3},{2,0},{3,1},{4,6},{5,7},{6,4},{7,5},{8,10},{9,11},{10,... | collective-permute-start | bytes 589832 | tf_op jit(solution)/shard_map/ppermute | solution.py:717
  111.8 2.7 %copy-start.6 = (bf16[2,2,2,192,128]{4,3,2,1,0:T(8,128)(2,1)}, bf16[2,2,2,192,128]{4,3,2,1,0:T(8,128)(2,1)S(1)}, u32[]{:S(2)}) copy-start(bf16[2,2,2,192,128]{4,3,2,1,0:T(8,128)(2,1)S(1)} %copy.10) | copy-start | bytes 1179652
  111.8 2.7 %collective-permute-start.24 = (bf16[4,2,192,128]{3,2,1,0:T(8,128)(2,1)S(1)}, bf16[4,2,192,128]{3,2,1,0:T(8,128)(2,1)S(1)}, u32[]{:S(2)}, u32[]{:S(2)}) collective-permute-start(bf16[4,2,192,128]{3,2,1,0:T(8,128)(2,1)S(1)} %bitcast.40), channel_id=1, source_target_pairs={{0,1},{1,0},{2,3},{3,2},{4,5},{5,4},{6,7},{7,6},{8,9},{9,8},{10,11... | collective-permute-start | bytes 1179656 | tf_op jit(solution)/shard_map/ppermute | solution.py:717
  111.9 1.9 %collective-permute-start.23 = (bf16[4,2,64,128]{3,2,1,0:T(8,128)(2,1)S(1)}, bf16[4,2,64,128]{3,2,1,0:T(8,128)(2,1)S(1)}, u32[]{:S(2)}, u32[]{:S(2)}) collective-permute-start(bf16[4,2,64,128]{3,2,1,0:T(8,128)(2,1)S(1)} %pad_maximum_fusion.13), channel_id=1, source_target_pairs={{0,1},{1,0},{2,3},{3,2},{4,5},{5,4},{6,7},{7,6},{8,9},{9,8},{10,11... | collective-permute-start | bytes 393224 | tf_op jit(solution)/shard_map/ppermute | solution.py:717
  112.3 12.0 %collective-permute-start.25 = (bf16[2,384,128]{2,1,0:T(8,128)(2,1)S(1)}, bf16[2,384,128]{2,1,0:T(8,128)(2,1)S(1)}, u32[]{:S(2)}, u32[]{:S(2)}) collective-permute-start(bf16[2,384,128]{2,1,0:T(8,128)(2,1)S(1)} %get-tuple-element.61), channel_id=1, source_target_pairs={{0,8},{1,9},{2,10},{3,11},{4,12},{5,13},{6,14},{7,15},{8,0},{9,1},... | collective-permute-start | bytes 589832 | tf_op jit(solution)/shard_map/ppermute | solution.py:717
  114.5 0.7 copy-start.10
  125.1 4.8 %collective-permute-start.26 = (bf16[384,128]{1,0:T(8,128)(2,1)S(1)}, bf16[384,128]{1,0:T(8,128)(2,1)S(1)}, u32[]{:S(2)}, u32[]{:S(2)}) collective-permute-start(bf16[384,128]{1,0:T(8,128)(2,1)S(1)} %get-tuple-element.64), channel_id=1, source_target_pairs={{0,16},{1,17},{2,18},{3,19},{4,20},{5,21},{6,22},{7,23},{8,24},{9,... | collective-permute-start | bytes 294920 | tf_op jit(solution)/shard_map/ppermute | solution.py:717
  130.0 12.3 %collective-permute-start.29 = (bf16[2,384,128]{2,1,0:T(8,128)(2,1)S(1)}, bf16[2,384,128]{2,1,0:T(8,128)(2,1)S(1)}, u32[]{:S(2)}, u32[]{:S(2)}) collective-permute-start(bf16[2,384,128]{2,1,0:T(8,128)(2,1)S(1)} %get-tuple-element.75), channel_id=1, source_target_pairs={{0,6},{1,7},{2,4},{3,5},{4,2},{5,3},{6,0},{7,1},{8,14},{9,15},{10,... | collective-permute-start | bytes 589832 | tf_op jit(solution)/shard_map/ppermute | solution.py:717
  130.1 12.2 %collective-permute-start.28 = (bf16[2,384,128]{2,1,0:T(8,128)(2,1)S(1)}, bf16[2,384,128]{2,1,0:T(8,128)(2,1)S(1)}, u32[]{:S(2)}, u32[]{:S(2)}) collective-permute-start(bf16[2,384,128]{2,1,0:T(8,128)(2,1)S(1)} %get-tuple-element.75), channel_id=1, source_target_pairs={{0,4},{1,5},{2,6},{3,7},{4,0},{5,1},{6,2},{7,3},{8,12},{9,13},{10,... | collective-permute-start | bytes 589832 | tf_op jit(solution)/shard_map/ppermute | solution.py:717
  132.7 9.5 %collective-permute-start.27 = (bf16[2,384,128]{2,1,0:T(8,128)(2,1)S(1)}, bf16[2,384,128]{2,1,0:T(8,128)(2,1)S(1)}, u32[]{:S(2)}, u32[]{:S(2)}) collective-permute-start(bf16[2,384,128]{2,1,0:T(8,128)(2,1)S(1)} %get-tuple-element.75), channel_id=1, source_target_pairs={{0,2},{1,3},{2,0},{3,1},{4,6},{5,7},{6,4},{7,5},{8,10},{9,11},{10,... | collective-permute-start | bytes 589832 | tf_op jit(solution)/shard_map/ppermute | solution.py:717
  142.4 2.4 %collective-permute-start.30 = (bf16[4,2,384,128]{3,2,1,0:T(8,128)(2,1)S(1)}, bf16[4,2,384,128]{3,2,1,0:T(8,128)(2,1)S(1)}, u32[]{:S(2)}, u32[]{:S(2)}) collective-permute-start(bf16[4,2,384,128]{3,2,1,0:T(8,128)(2,1)S(1)} %pad_maximum_fusion.1.same), channel_id=1, source_target_pairs={{0,1},{1,0},{2,3},{3,2},{4,5},{5,4},{6,7},{7,6},{8,9},{9,8},{10,11... | collective-permute-start | bytes 2359304 | tf_op jit(solution)/shard_map/ppermute | solution.py:717
  144.7 1.0 copy-start.2

commit v12 on v11

--- a/solution.py
+++ b/solution.py
@@ -300,12 +300,11 @@
             copy.wait()
 
         def chunk(index, inner):
-            line = buffers[slab, :, pl.ds(pl.multiple_of(index * 2048, 2048), 2048)]
-            block = line.astype(jnp.float32).reshape(16, 128).astype(jnp.bfloat16)
-            out[slab, pl.ds(pl.multiple_of(index * 16, 16), 16), :] = block
+            line = buffers[slab, :, pl.ds(pl.multiple_of(index * 4096, 4096), 4096)]
+            out[slab, pl.ds(pl.multiple_of(index * 32, 32), 32), :] = line.reshape(32, 128)
             return inner
 
-        lax.fori_loop(0, slab_rows // 16, chunk, 0, unroll=8)
+        lax.fori_loop(0, slab_rows // 32, chunk, 0, unroll=4)
         return carried
 
     lax.fori_loop(0, slabs, step, 0)
@@ -739,13 +738,6 @@
         across = swap(sent[2], 2 * PIECES)
         return [sent[0], swap(sent[1], PIECES), across, swap(sent[3], 3 * PIECES)]
 
-    def along_z(block):
-        return jnp.stack([block, swap(block, 4)])
-
-    def along_x(pair):
-        quad = jnp.stack([pair, swap(pair, 2)], 1)
-        return quad.reshape((PIECES // 2,) + pair.shape[1:])
-
     elsewhere = swap(stretch_adapter, 2 * PIECES)
     packed = pack_row(adapter_pool, SECTIONS)
     even, odd = deal(normed_input, packed)
@@ -761,33 +753,34 @@
     dealt = [swap(block, 2 * j) if j else block for j, block in enumerate(dealt)]
 
     weight, ups = join(stretch_adapter, adapter_owner, arrived)
+    far = swap(after(far, weight), PIECES)
     partial_sums = narrow(weight, dealt)
     back = [swap(block, 2 * j) if j else block for j, block in enumerate(partial_sums)]
     back = sum(block.astype(jnp.float32) for block in back)
     base = after(base, *partial_sums)
     base = [base, swap(base, 2), swap(base, 4)]
-    own_rank = swap(after(back[1].astype(jnp.bfloat16), *base), 1)
+    own_rank = swap(after(back[1].astype(jnp.bfloat16), far, *base), 1)
     own_rank = back[0] + own_rank.astype(jnp.float32)
     own_rank = own_rank.astype(jnp.bfloat16)
     base = jnp.stack(base + [swap(after(base[2], own_rank), 2)])
     all_rank = own_rank[:, ADAPTER_RANK:]
-    ups = along_z(after(ups, own_rank))
+    ups = jnp.stack([ups, swap(after(ups, own_rank), 2)])
     all_rank = jnp.stack([all_rank, swap(all_rank, PIECES)])
+    own, across = settle(stretch_adapter, elsewhere, adapter_owner, near, after(far, own_rank))
+    ends = jnp.stack([own, swap(across, 2 * PIECES)])
     all_rank = after(all_rank, ups)
-    ups = along_x(after(ups, all_rank))
-    far = swap(after(far, all_rank), PIECES)
+    ups = jnp.stack([ups, swap(after(ups, all_rank), 4)])
+    ups = ups.reshape((PIECES // 2,) + ups.shape[2:])
     all_rank = jnp.stack([swap(all_rank, apart) if apart else all_rank for apart in (0, 2, 4, 6)])
     base = after(base, all_rank)
     base = (base, swap(base, 1))
-    all_rank = after(all_rank, ups)
+    all_rank = after(all_rank, ups, across)
     ups = (ups, swap(ups, 1))
     all_rank = jnp.stack([all_rank, swap(all_rank, 1)])
 
     shared = (query_base, base, own_rank, all_rank, ups, cosines, sines)
     attended = attend(0, 1, None, *shared)
-    far = after(far, attended)
-    own, across = settle(stretch_adapter, elsewhere, adapter_owner, near, far)
-    ends = jnp.stack([own, swap(across, 2 * PIECES)])
+    ends = after(ends, attended)
     ends = jnp.stack([swap(ends, apart) if apart else ends for apart in (0, 2, 4, 6)])
     attended = attend(1, KEYVALUE_HEADS - 1, attended, *shared)
     ends = after(ends, attended)

time: 149 us -> 156 us (1.047)
  waiting for transfers between devices: 68.4 us -> 71.2 us
    ppermute x31, waiting for transfers between devices: 66.2 us -> 69.1 us  [swap(): lax.ppermute(block, ('groups', 'ctx'), [(i, i ^ mask) for i in range(4 *...]
    unnamed x23 -> x25, local copies, waits for them, and re-layouts: 3.52 us -> 4.52 us
  transfers between devices with their start and end apart: 32 -> 32, of which waited for: 19 -> 15; matrix products, arithmetic and copies ran while one was open for 3% -> 3% of each run, Pallas kernels for 10% -> 7%
where the time goes in v12:
time: 156 us; the launch traced here: 155 us
  waiting for transfers between devices  71.2 us (46%)
  starting transfers between devices  46.6 us (30%)
  Pallas kernels  27.3 us (18%)
  local copies, waits for them, and re-layouts  4.68 us (3%)
  other arithmetic  4.49 us (3%)
    ppermute x31, waiting for transfers between devices, swap(): lax.ppermute(block, ('groups', 'ctx'), [(i, i ^ mask) for i in range(4 *...  69.1 us
    ppermute x31, starting transfers between devices, swap(): lax.ppermute(block, ('groups', 'ctx'), [(i, i ^ mask) for i in range(4 *...  41.1 us
    pallas_call x2, Pallas kernels, attend(): pl.pallas_call(partial(attend_kernel, first_head), grid=(heads,), out_sha...  13.2 us
    pallas_call x1, Pallas kernels, pack_row(): pl.pallas_call(partial(pack_kernel, sections), out_shape=jax.ShapeDtypeSt...  6.53 us
    all_to_all x1, starting transfers between devices, direct_shards(): spread = lax.all_to_all(packed, 'ctx', 0, 0, axis_index_groups=blocks)  5.5 us
    unnamed x25, local copies, waits for them, and re-layouts  4.52 us
  transfers between devices with their start and end apart: 32, of which 15 were waited for; matrix products, arithmetic and copies ran while one was open for 3% of the time, Pallas kernels for 7%

profile of v12, /device:TPU:0, one launch (start us, length us, event | category | flops | bytes accessed | tf_op | source)
XLA Modules:
  0.0 155.4 jit_solution(598344502877617066)
XLA Ops:
  0.6 6.5 %shard_map.86.refs_0_ = bf16[8,1312,128]{2,1,0:T(8,128)(2,1)} custom-call(bf16[1,2686976]{1,0:T(2,128)(2,1)} %pool.1), custom_call_target="tpu_custom_call" | custom-call | bytes 8388608 | tf_op jit(solution)/shard_map/pallas_call | solution.py:315
  7.2 5.5 %all-to-all-start = ((bf16[8,1312,128]{2,1,0:T(8,128)(2,1)}), bf16[8,1312,128]{2,1,0:T(8,128)(2,1)}, u32[]{:S(2)}, u32[]{:S(2)}) async-start(bf16[8,1312,128]{2,1,0:T(8,128)(2,1)} %shard_map.86.refs_0_), calls=%async_computation | async-start | bytes 5373952 | tf_op jit(solution)/shard_map/all_to_all | solution.py:748
  12.7 2.2 %collective-permute-start.1 = (s32[2]{0:T(128)S(1)}, s32[2]{0:T(128)S(1)}, u32[]{:S(2)}, u32[]{:S(2)}) collective-permute-start(s32[2]{0:T(128)S(1)} %copy-done.3), channel_id=1, source_target_pairs={{0,16},{1,17},{2,18},{3,19},{4,20},{5,21},{6,22},{7,23},{8,24},{9,... | collective-permute-start | bytes 32 | tf_op jit(solution)/shard_map/ppermute | solution.py:716
  14.9 1.2 copy-done.1
  16.2 0.3 shard_map.87
  16.4 0.1 collective-permute-start.2
  16.5 0.5 copy-done.8
  17.0 0.0 copy-done.9
  17.0 2.6 %collective-permute-start = (bf16[64,1024]{1,0:T(8,128)(2,1)S(1)}, bf16[64,1024]{1,0:T(8,128)(2,1)S(1)}, u32[]{:S(2)}, u32[]{:S(2)}) collective-permute-start(bf16[64,1024]{1,0:T(8,128)(2,1)S(1)} %constant_dynamic-update-slice_fusion), channel_id=1, source_target_pairs={{0,8},{1,9},{2,10},{3,11},{4,12},{5,13},{6,14},{7,15},{8,0},{9,1},... | collective-permute-start | bytes 393224 | tf_op jit(solution)/shard_map/ppermute | solution.py:716
  19.8 1.9 %fusion = (f32[1024,64]{1,0:T(8,128)S(1)}, f32[1024,64]{1,0:T(8,128)S(1)}, f32[1024,64]{1,0:T(8,128)S(1)}) fusion(f32[64]{0:T(128)S(1)} %multiply_power_fusion, f32[1024]{0:T(1024)S(1)} %iota_convert_fusion), kind=kLoop, calls=%fused_computation.15 | loop fusion | flops 131072 | bytes 790784 | tf_op jit(solution)/shard_map/neg | solution.py:732
  21.7 1.3 pad_maximum_fusion.2
  23.0 22.4 %collective-permute-done = bf16[64,1024]{1,0:T(8,128)(2,1)S(1)} collective-permute-done((bf16[64,1024]{1,0:T(8,128)(2,1)S(1)}, bf16[64,1024]{1,0:T(8,128)(2,1)S(1)}, u32[]{:S(2)}, u32[]{:S(2)}) %collective-permute-start) | collective-permute-done | bytes 131104 | tf_op jit(solution)/shard_map/ppermute | solution.py:716
  45.5 2.1 %all-to-all-done.spread = bf16[8,1312,128]{2,1,0:T(8,128)(2,1)} async-done(((bf16[8,1312,128]{2,1,0:T(8,128)(2,1)}), bf16[8,1312,128]{2,1,0:T(8,128)(2,1)}, u32[]{:S(2)}, u32[]{:S(2)}) %all-to-all-start) | async-done | bytes 2687008 | tf_op jit(solution)/shard_map/all_to_all | solution.py:748
  47.7 2.1 %shard_map.88 = (bf16[960,128]{1,0:T(8,128)(2,1)S(1)}, bf16[960,128]{1,0:T(8,128)(2,1)S(1)}, bf16[960,128]{1,0:T(8,128)(2,1)S(1)}, bf16[960,128]{1,0:T(8,128)(2,...) custom-call(s32[2]{0:T(128)S(1)} %copy-done.3, s32[2]{0:T(128)S(1)} %collective-permute-done.1.there, ...), custom_call_target="tpu_custom_call" | custom-call | bytes 3145728 | tf_op jit(solution)/shard_map/pallas_call | solution.py:359
  49.8 1.3 collective-permute-start.3
  51.2 1.7 %collective-permute-start.6 = (bf16[2,64,1024]{2,1,0:T(8,128)(2,1)S(1)}, bf16[2,64,1024]{2,1,0:T(8,128)(2,1)S(1)}, u32[]{:S(2)}, u32[]{:S(2)}) collective-permute-start(bf16[2,64,1024]{2,1,0:T(8,128)(2,1)S(1)} %get-tuple-element.44), channel_id=1, source_target_pairs={{0,2},{1,3},{2,0},{3,1},{4,6},{5,7},{6,4},{7,5},{8,10},{9,11},{10,... | collective-permute-start | bytes 786440 | tf_op jit(solution)/shard_map/ppermute | solution.py:716
  52.9 2.3 %collective-permute-start.7 = (bf16[2,64,1024]{2,1,0:T(8,128)(2,1)S(1)}, bf16[2,64,1024]{2,1,0:T(8,128)(2,1)S(1)}, u32[]{:S(2)}, u32[]{:S(2)}) collective-permute-start(bf16[2,64,1024]{2,1,0:T(8,128)(2,1)S(1)} %get-tuple-element.45), channel_id=1, source_target_pairs={{0,4},{1,5},{2,6},{3,7},{4,0},{5,1},{6,2},{7,3},{8,12},{9,13},{10,... | collective-permute-start | bytes 786440 | tf_op jit(solution)/shard_map/ppermute | solution.py:716
  55.2 1.7 %collective-permute-start.4 = (bf16[960,128]{1,0:T(8,128)(2,1)S(1)}, bf16[960,128]{1,0:T(8,128)(2,1)S(1)}, u32[]{:S(2)}, u32[]{:S(2)}) collective-permute-start(bf16[960,128]{1,0:T(8,128)(2,1)S(1)} %get-tuple-element.39), channel_id=1, source_target_pairs={{0,16},{1,17},{2,18},{3,19},{4,20},{5,21},{6,22},{7,23},{8,24},{9,... | collective-permute-start | bytes 737288 | tf_op jit(solution)/shard_map/ppermute | solution.py:716
  56.8 6.7 %collective-permute-done.3.refs_1_ = bf16[960,128]{1,0:T(8,128)(2,1)S(1)} collective-permute-done((bf16[960,128]{1,0:T(8,128)(2,1)S(1)}, bf16[960,128]{1,0:T(8,128)(2,1)S(1)}, u32[]{:S(2)}, u32[]{:S(2)}) %collective-permute-start.3) | collective-permute-done | bytes 245792 | tf_op jit(solution)/shard_map/ppermute | solution.py:716
  63.6 1.1 collective-permute-start.5
  64.6 8.4 %collective-permute-done.5.refs_3_ = bf16[960,128]{1,0:T(8,128)(2,1)S(1)} collective-permute-done((bf16[960,128]{1,0:T(8,128)(2,1)S(1)}, bf16[960,128]{1,0:T(8,128)(2,1)S(1)}, u32[]{:S(2)}, u32[]{:S(2)}) %collective-permute-start.5) | collective-permute-done | bytes 245792 | tf_op jit(solution)/shard_map/ppermute | solution.py:716
  73.0 1.0 shard_map.89
  74.0 1.1 collective-permute-done.8.refs_3_
  75.1 0.4 shard_map.90
  75.6 5.7 %collective-permute-start.13 = (bf16[2,64,192]{2,1,0:T(8,128)(2,1)S(1)}, bf16[2,64,192]{2,1,0:T(8,128)(2,1)S(1)}, u32[]{:S(2)}, u32[]{:S(2)}) collective-permute-start(bf16[2,64,192]{2,1,0:T(8,128)(2,1)S(1)} %get-tuple-element.50), channel_id=1, source_target_pairs={{0,6},{1,7},{2,4},{3,5},{4,2},{5,3},{6,0},{7,1},{8,14},{9,15},{10,... | collective-permute-start | bytes 147464 | tf_op jit(solution)/shard_map/ppermute | solution.py:716
  81.3 0.6 collective-permute-start.11
  81.9 2.7 %collective-permute-start.14 = (bf16[2,384,128]{2,1,0:T(8,128)(2,1)S(1)}, bf16[2,384,128]{2,1,0:T(8,128)(2,1)S(1)}, u32[]{:S(2)}, u32[]{:S(2)}) collective-permute-start(bf16[2,384,128]{2,1,0:T(8,128)(2,1)S(1)} %get-tuple-element.53), channel_id=1, source_target_pairs={{0,8},{1,9},{2,10},{3,11},{4,12},{5,13},{6,14},{7,15},{8,0},{9,1},... | collective-permute-start | bytes 589832 | tf_op jit(solution)/shard_map/ppermute | solution.py:716
  84.7 1.2 collective-permute-start.9
  85.9 2.0 %collective-permute-start.10 = (bf16[2,64,1024]{2,1,0:T(8,128)(2,1)S(1)}, bf16[2,64,1024]{2,1,0:T(8,128)(2,1)S(1)}, u32[]{:S(2)}, u32[]{:S(2)}) collective-permute-start(bf16[2,64,1024]{2,1,0:T(8,128)(2,1)S(1)} %pad_maximum_fusion.5), channel_id=1, source_target_pairs={{0,4},{1,5},{2,6},{3,7},{4,0},{5,1},{6,2},{7,3},{8,12},{9,13},{10,... | collective-permute-start | bytes 786440 | tf_op jit(solution)/shard_map/ppermute | solution.py:716
  88.0 4.8 %collective-permute-done.14.far = bf16[2,384,128]{2,1,0:T(8,128)(2,1)S(1)} collective-permute-done((bf16[2,384,128]{2,1,0:T(8,128)(2,1)S(1)}, bf16[2,384,128]{2,1,0:T(8,128)(2,1)S(1)}, u32[]{:S(2)}, u32[]{:S(2)}) %collective-permute-start.14) | collective-permute-done | bytes 196640 | tf_op jit(solution)/shard_map/ppermute | solution.py:716
  92.7 2.1 %collective-permute-done.10 = bf16[2,64,1024]{2,1,0:T(8,128)(2,1)S(1)} collective-permute-done((bf16[2,64,1024]{2,1,0:T(8,128)(2,1)S(1)}, bf16[2,64,1024]{2,1,0:T(8,128)(2,1)S(1)}, u32[]{:S(2)}, u32[]{:S(2)}) %collective-permute-start.10) | collective-permute-done | bytes 262176 | tf_op jit(solution)/shard_map/ppermute | solution.py:716
  94.9 1.2 collective-permute-done.15
  96.1 0.1 slice_bitcast_fusion.1
  96.2 1.9 %collective-permute-start.17 = (bf16[64,128]{1,0:T(8,128)(2,1)S(1)}, bf16[64,128]{1,0:T(8,128)(2,1)S(1)}, u32[]{:S(2)}, u32[]{:S(2)}) collective-permute-start(bf16[64,128]{1,0:T(8,128)(2,1)S(1)} %get-tuple-element.79), channel_id=1, source_target_pairs={{0,8},{1,9},{2,10},{3,11},{4,12},{5,13},{6,14},{7,15},{8,0},{9,1},... | collective-permute-start | bytes 49160 | tf_op jit(solution)/shard_map/ppermute | solution.py:716
  98.0 1.2 collective-permute-start.16
  99.2 0.8 collective-permute-start.18
  100.1 0.8 collective-permute-done.17
  100.9 7.3 %collective-permute-done.18 = bf16[2,192,128]{2,1,0:T(8,128)(2,1)S(1)} collective-permute-done((bf16[2,192,128]{2,1,0:T(8,128)(2,1)S(1)}, bf16[2,192,128]{2,1,0:T(8,128)(2,1)S(1)}, u32[]{:S(2)}, u32[]{:S(2)}) %collective-permute-start.18) | collective-permute-done | bytes 98336 | tf_op jit(solution)/shard_map/ppermute | solution.py:716
  108.3 2.7 %collective-permute-start.21 = (bf16[2,64,128]{2,1,0:T(8,128)(2,1)S(1)}, bf16[2,64,128]{2,1,0:T(8,128)(2,1)S(1)}, u32[]{:S(2)}, u32[]{:S(2)}) collective-permute-start(bf16[2,64,128]{2,1,0:T(8,128)(2,1)S(1)} %pad_maximum_fusion.14), channel_id=1, source_target_pairs={{0,6},{1,7},{2,4},{3,5},{4,2},{5,3},{6,0},{7,1},{8,14},{9,15},{10,... | collective-permute-start | bytes 98312 | tf_op jit(solution)/shard_map/ppermute | solution.py:716
  111.0 0.8 collective-permute-start.19
  111.8 1.4 collective-permute-done.21
  113.2 1.7 %collective-permute-done.20 = bf16[2,64,128]{2,1,0:T(8,128)(2,1)S(1)} collective-permute-done((bf16[2,64,128]{2,1,0:T(8,128)(2,1)S(1)}, bf16[2,64,128]{2,1,0:T(8,128)(2,1)S(1)}, u32[]{:S(2)}, u32[]{:S(2)}) %collective-permute-start.20) | collective-permute-done | bytes 32800 | tf_op jit(solution)/shard_map/ppermute | solution.py:716
  115.0 0.1 pad_maximum_fusion.key_same.value_same
  115.1 0.1 collective-permute-start.22
  115.2 2.1 %collective-permute-start.23 = (bf16[2,2,192,128]{3,2,1,0:T(8,128)(2,1)S(1)}, bf16[2,2,192,128]{3,2,1,0:T(8,128)(2,1)S(1)}, u32[]{:S(2)}, u32[]{:S(2)}) collective-permute-start(bf16[2,2,192,128]{3,2,1,0:T(8,128)(2,1)S(1)} %get-tuple-element.60), channel_id=1, source_target_pairs={{0,4},{1,5},{2,6},{3,7},{4,0},{5,1},{6,2},{7,3},{8,12},{9,13},{10,... | collective-permute-start | bytes 589832 | tf_op jit(solution)/shard_map/ppermute | solution.py:716
  117.3 5.5 %collective-permute-done.23 = bf16[2,2,192,128]{3,2,1,0:T(8,128)(2,1)S(1)} collective-permute-done((bf16[2,2,192,128]{3,2,1,0:T(8,128)(2,1)S(1)}, bf16[2,2,192,128]{3,2,1,0:T(8,128)(2,1)S(1)}, u32[]{:S(2)}, u32[]{:S(2)}) %collective-permute-start.23) | collective-permute-done | bytes 196640 | tf_op jit(solution)/shard_map/ppermute | solution.py:716
  122.8 0.1 collective-permute-start.25
  122.9 0.8 shard_map.91
  123.7 2.3 %collective-permute-start.26 = (bf16[384,128]{1,0:T(8,128)(2,1)S(1)}, bf16[384,128]{1,0:T(8,128)(2,1)S(1)}, u32[]{:S(2)}, u32[]{:S(2)}) collective-permute-start(bf16[384,128]{1,0:T(8,128)(2,1)S(1)} %get-tuple-element.63), channel_id=1, source_target_pairs={{0,16},{1,17},{2,18},{3,19},{4,20},{5,21},{6,22},{7,23},{8,24},{9,... | collective-permute-start | bytes 294920 | tf_op jit(solution)/shard_map/ppermute | solution.py:716
  126.1 0.2 collective-permute-start.24
  126.3 3.2 %collective-permute-done.26 = bf16[384,128]{1,0:T(8,128)(2,1)S(1)} collective-permute-done((bf16[384,128]{1,0:T(8,128)(2,1)S(1)}, bf16[384,128]{1,0:T(8,128)(2,1)S(1)}, u32[]{:S(2)}, u32[]{:S(2)}) %collective-permute-start.26) | collective-permute-done | bytes 98336 | tf_op jit(solution)/shard_map/ppermute | solution.py:716
  129.5 0.7 pad_maximum_fusion.10.all_rank
  130.3 0.7 copy-done.11
  131.0 1.0 copy-done.10
  132.0 4.5 %shard_map.92.refs_0_ = bf16[64,4096]{1,0:T(8,128)(2,1)} custom-call(bf16[64,4096]{1,0:T(8,128)(2,1)} %query_block.3, bf16[4,2,64,1024]{3,2,1,0:T(8,128)(2,1)} %copy-done.5, bf16[4,2,64,1024]{3,2,1,0:T(8,128)(2,1)} %copy-done.10, bf16[4,2,64,1024]{3,2,1,0:T(8,128)(2,1)} %copy-done.5, bf16[4,2,64,1024]{3,2,1,0:T(8,128)(2,1)} %copy-done.10, ...), custom_call_target="tpu_custom_call" | custom-call | flops 3221225472 | bytes 10485760 | tf_op jit(solution)/shard_map/pallas_call | solution.py:633
  136.5 2.0 %collective-permute-start.29 = (bf16[2,384,128]{2,1,0:T(8,128)(2,1)S(1)}, bf16[2,384,128]{2,1,0:T(8,128)(2,1)S(1)}, u32[]{:S(2)}, u32[]{:S(2)}) collective-permute-start(bf16[2,384,128]{2,1,0:T(8,128)(2,1)S(1)} %pad_maximum_fusion.12), channel_id=1, source_target_pairs={{0,6},{1,7},{2,4},{3,5},{4,2},{5,3},{6,0},{7,1},{8,14},{9,15},{10,... | collective-permute-start | bytes 589832 | tf_op jit(solution)/shard_map/ppermute | solution.py:716
  138.5 0.3 collective-permute-start.28
  138.8 1.2 collective-permute-start.27
  140.0 8.7 %shard_map.93.attended_rows = bf16[64,4096]{1,0:T(8,128)(2,1)} custom-call(bf16[64,4096]{1,0:T(8,128)(2,1)} %query_block.3, bf16[4,2,64,1024]{3,2,1,0:T(8,128)(2,1)} %copy-done.5, bf16[4,2,64,1024]{3,2,1,0:T(8,128)(2,1)} %copy-done.10, bf16[4,2,64,1024]{3,2,1,0:T(8,128)(2,1)} %copy-done.5, ...), custom_call_target="tpu_custom_call", output_to_operand_aliasing={{}: (11, {})} | custom-call | flops 9663676416 | bytes 10485760 | tf_op jit(solution)/shard_map/pallas_call | solution.py:633
  148.7 0.1 pad_maximum_fusion.1.same
  148.8 0.1 collective-permute-start.30
  148.9 2.3 %collective-permute-done.30.other = bf16[4,2,384,128]{3,2,1,0:T(8,128)(2,1)S(1)} collective-permute-done((bf16[4,2,384,128]{3,2,1,0:T(8,128)(2,1)S(1)}, bf16[4,2,384,128]{3,2,1,0:T(8,128)(2,1)S(1)}, u32[]{:S(2)}, u32[]{:S(2)}) %collective-permute-start.30) | collective-permute-done | bytes 786464 | tf_op jit(solution)/shard_map/ppermute | solution.py:716
  151.2 1.0 copy-done.2
  152.2 3.1 %shard_map.94 = bf16[64,8192]{1,0:T(8,128)(2,1)} custom-call(bf16[64,4096]{1,0:T(8,128)(2,1)S(1)} %copy-done.2, bf16[4,2,384,128]{3,2,1,0:T(8,128)(2,1)S(1)} %pad_maximum_fusion.1.same, bf16[4,2,384,128]{3,2,1,0:T(8,128)(2,1)S(1)} %collective-permute-done.30.other), custom_call_target="tpu_custom_call" | custom-call | flops 134217728 | bytes 4194304 | tf_op jit(solution)/shard_map/pallas_call | solution.py:699
  (56 shorter events, 0.5 us)
Async XLA Ops:
  7.2 5.5 %copy-start.3 = (s32[2]{0:T(128)S(1)}, s32[2]{0:T(128)}, u32[]{:S(2)}) copy-start(s32[2]{0:T(128)} %here.5) | copy-start | bytes 28
  7.2 7.8 %copy-start = (bf16[8,1312,128]{2,1,0:T(8,128)(2,1)S(1)}, bf16[8,1312,128]{2,1,0:T(8,128)(2,1)}, u32[]{:S(2)}) copy-start(bf16[8,1312,128]{2,1,0:T(8,128)(2,1)} %shard_map.86.refs_0_) | copy-start | bytes 8060932
  7.2 40.5 %all-to-all-start = ((bf16[8,1312,128]{2,1,0:T(8,128)(2,1)}), bf16[8,1312,128]{2,1,0:T(8,128)(2,1)}, u32[]{:S(2)}, u32[]{:S(2)}) async-start(bf16[8,1312,128]{2,1,0:T(8,128)(2,1)} %shard_map.86.refs_0_), calls=%async_computation | async-start | bytes 5373952 | tf_op jit(solution)/shard_map/all_to_all | solution.py:748
  12.7 35.0 %collective-permute-start.1 = (s32[2]{0:T(128)S(1)}, s32[2]{0:T(128)S(1)}, u32[]{:S(2)}, u32[]{:S(2)}) collective-permute-start(s32[2]{0:T(128)S(1)} %copy-done.3), channel_id=1, source_target_pairs={{0,16},{1,17},{2,18},{3,19},{4,20},{5,21},{6,22},{7,23},{8,24},{9,... | collective-permute-start | bytes 32 | tf_op jit(solution)/shard_map/ppermute | solution.py:716
  14.9 1.2 copy-start.1
  16.2 0.8 copy-start.8
  16.2 0.9 copy-start.9
  16.4 29.0 %collective-permute-start.2 = (bf16[4,64,1024]{2,1,0:T(8,128)(2,1)S(1)}, bf16[4,64,1024]{2,1,0:T(8,128)(2,1)S(1)}, u32[]{:S(2)}, u32[]{:S(2)}) collective-permute-start(bf16[4,64,1024]{2,1,0:T(8,128)(2,1)S(1)} %get-tuple-element.35), channel_id=1, source_target_pairs={{0,1},{1,0},{2,3},{3,2},{4,5},{5,4},{6,7},{7,6},{8,9},{9,8},{10,11... | collective-permute-start | bytes 1572872 | tf_op jit(solution)/shard_map/ppermute | solution.py:716
  17.0 28.4 %collective-permute-start = (bf16[64,1024]{1,0:T(8,128)(2,1)S(1)}, bf16[64,1024]{1,0:T(8,128)(2,1)S(1)}, u32[]{:S(2)}, u32[]{:S(2)}) collective-permute-start(bf16[64,1024]{1,0:T(8,128)(2,1)S(1)} %constant_dynamic-update-slice_fusion), channel_id=1, source_target_pairs={{0,8},{1,9},{2,10},{3,11},{4,12},{5,13},{6,14},{7,15},{8,0},{9,1},... | collective-permute-start | bytes 393224 | tf_op jit(solution)/shard_map/ppermute | solution.py:716
  19.7 27.9 %copy-start.4 = (s32[16]{0:T(128)S(1)}, s32[16]{0:T(128)}, u32[]{:S(2)}) copy-start(s32[16]{0:T(128)} %owner.5) | copy-start | bytes 196
  49.8 13.8 %collective-permute-start.3 = (bf16[960,128]{1,0:T(8,128)(2,1)S(1)}, bf16[960,128]{1,0:T(8,128)(2,1)S(1)}, u32[]{:S(2)}, u32[]{:S(2)}) collective-permute-start(bf16[960,128]{1,0:T(8,128)(2,1)S(1)} %get-tuple-element.38), channel_id=1, source_target_pairs={{0,8},{1,9},{2,10},{3,11},{4,12},{5,13},{6,14},{7,15},{8,0},{9,1},... | collective-permute-start | bytes 737288 | tf_op jit(solution)/shard_map/ppermute | solution.py:716
  51.2 22.8 %collective-permute-start.6 = (bf16[2,64,1024]{2,1,0:T(8,128)(2,1)S(1)}, bf16[2,64,1024]{2,1,0:T(8,128)(2,1)S(1)}, u32[]{:S(2)}, u32[]{:S(2)}) collective-permute-start(bf16[2,64,1024]{2,1,0:T(8,128)(2,1)S(1)} %get-tuple-element.44), channel_id=1, source_target_pairs={{0,2},{1,3},{2,0},{3,1},{4,6},{5,7},{6,4},{7,5},{8,10},{9,11},{10,... | collective-permute-start | bytes 786440 | tf_op jit(solution)/shard_map/ppermute | solution.py:716
  52.9 21.1 %collective-permute-start.7 = (bf16[2,64,1024]{2,1,0:T(8,128)(2,1)S(1)}, bf16[2,64,1024]{2,1,0:T(8,128)(2,1)S(1)}, u32[]{:S(2)}, u32[]{:S(2)}) collective-permute-start(bf16[2,64,1024]{2,1,0:T(8,128)(2,1)S(1)} %get-tuple-element.45), channel_id=1, source_target_pairs={{0,4},{1,5},{2,6},{3,7},{4,0},{5,1},{6,2},{7,3},{8,12},{9,13},{10,... | collective-permute-start | bytes 786440 | tf_op jit(solution)/shard_map/ppermute | solution.py:716
  55.2 20.0 %collective-permute-start.8 = (bf16[2,64,1024]{2,1,0:T(8,128)(2,1)S(1)}, bf16[2,64,1024]{2,1,0:T(8,128)(2,1)S(1)}, u32[]{:S(2)}, u32[]{:S(2)}) collective-permute-start(bf16[2,64,1024]{2,1,0:T(8,128)(2,1)S(1)} %get-tuple-element.46), channel_id=1, source_target_pairs={{0,6},{1,7},{2,4},{3,5},{4,2},{5,3},{6,0},{7,1},{8,14},{9,15},{10,... | collective-permute-start | bytes 786440 | tf_op jit(solution)/shard_map/ppermute | solution.py:716
  55.2 9.4 %collective-permute-start.4 = (bf16[960,128]{1,0:T(8,128)(2,1)S(1)}, bf16[960,128]{1,0:T(8,128)(2,1)S(1)}, u32[]{:S(2)}, u32[]{:S(2)}) collective-permute-start(bf16[960,128]{1,0:T(8,128)(2,1)S(1)} %get-tuple-element.39), channel_id=1, source_target_pairs={{0,16},{1,17},{2,18},{3,19},{4,20},{5,21},{6,22},{7,23},{8,24},{9,... | collective-permute-start | bytes 737288 | tf_op jit(solution)/shard_map/ppermute | solution.py:716
  63.6 9.5 %collective-permute-start.5 = (bf16[960,128]{1,0:T(8,128)(2,1)S(1)}, bf16[960,128]{1,0:T(8,128)(2,1)S(1)}, u32[]{:S(2)}, u32[]{:S(2)}) collective-permute-start(bf16[960,128]{1,0:T(8,128)(2,1)S(1)} %get-tuple-element.40), channel_id=1, source_target_pairs={{0,24},{1,25},{2,26},{3,27},{4,28},{5,29},{6,30},{7,31},{8,16},{9,... | collective-permute-start | bytes 737288 | tf_op jit(solution)/shard_map/ppermute | solution.py:716
  75.6 10.3 %collective-permute-start.13 = (bf16[2,64,192]{2,1,0:T(8,128)(2,1)S(1)}, bf16[2,64,192]{2,1,0:T(8,128)(2,1)S(1)}, u32[]{:S(2)}, u32[]{:S(2)}) collective-permute-start(bf16[2,64,192]{2,1,0:T(8,128)(2,1)S(1)} %get-tuple-element.50), channel_id=1, source_target_pairs={{0,6},{1,7},{2,4},{3,5},{4,2},{5,3},{6,0},{7,1},{8,14},{9,15},{10,... | collective-permute-start | bytes 147464 | tf_op jit(solution)/shard_map/ppermute | solution.py:716
  81.3 6.6 %collective-permute-start.12 = (bf16[2,64,192]{2,1,0:T(8,128)(2,1)S(1)}, bf16[2,64,192]{2,1,0:T(8,128)(2,1)S(1)}, u32[]{:S(2)}, u32[]{:S(2)}) collective-permute-start(bf16[2,64,192]{2,1,0:T(8,128)(2,1)S(1)} %get-tuple-element.49), channel_id=1, source_target_pairs={{0,4},{1,5},{2,6},{3,7},{4,0},{5,1},{6,2},{7,3},{8,12},{9,13},{10,... | collective-permute-start | bytes 147464 | tf_op jit(solution)/shard_map/ppermute | solution.py:716
  81.3 6.6 %collective-permute-start.11 = (bf16[2,64,192]{2,1,0:T(8,128)(2,1)S(1)}, bf16[2,64,192]{2,1,0:T(8,128)(2,1)S(1)}, u32[]{:S(2)}, u32[]{:S(2)}) collective-permute-start(bf16[2,64,192]{2,1,0:T(8,128)(2,1)S(1)} %get-tuple-element.48), channel_id=1, source_target_pairs={{0,2},{1,3},{2,0},{3,1},{4,6},{5,7},{6,4},{7,5},{8,10},{9,11},{10,... | collective-permute-start | bytes 147464 | tf_op jit(solution)/shard_map/ppermute | solution.py:716
  81.9 10.8 %collective-permute-start.14 = (bf16[2,384,128]{2,1,0:T(8,128)(2,1)S(1)}, bf16[2,384,128]{2,1,0:T(8,128)(2,1)S(1)}, u32[]{:S(2)}, u32[]{:S(2)}) collective-permute-start(bf16[2,384,128]{2,1,0:T(8,128)(2,1)S(1)} %get-tuple-element.53), channel_id=1, source_target_pairs={{0,8},{1,9},{2,10},{3,11},{4,12},{5,13},{6,14},{7,15},{8,0},{9,1},... | collective-permute-start | bytes 589832 | tf_op jit(solution)/shard_map/ppermute | solution.py:716
  84.7 8.1 %collective-permute-start.9 = (bf16[2,64,1024]{2,1,0:T(8,128)(2,1)S(1)}, bf16[2,64,1024]{2,1,0:T(8,128)(2,1)S(1)}, u32[]{:S(2)}, u32[]{:S(2)}) collective-permute-start(bf16[2,64,1024]{2,1,0:T(8,128)(2,1)S(1)} %pad_maximum_fusion.5), channel_id=1, source_target_pairs={{0,2},{1,3},{2,0},{3,1},{4,6},{5,7},{6,4},{7,5},{8,10},{9,11},{10,... | collective-permute-start | bytes 786440 | tf_op jit(solution)/shard_map/ppermute | solution.py:716
  85.9 9.0 %collective-permute-start.10 = (bf16[2,64,1024]{2,1,0:T(8,128)(2,1)S(1)}, bf16[2,64,1024]{2,1,0:T(8,128)(2,1)S(1)}, u32[]{:S(2)}, u32[]{:S(2)}) collective-permute-start(bf16[2,64,1024]{2,1,0:T(8,128)(2,1)S(1)} %pad_maximum_fusion.5), channel_id=1, source_target_pairs={{0,4},{1,5},{2,6},{3,7},{4,0},{5,1},{6,2},{7,3},{8,12},{9,13},{10,... | collective-permute-start | bytes 786440 | tf_op jit(solution)/shard_map/ppermute | solution.py:716
  94.9 1.2 collective-permute-start.15
  96.1 34.2 %copy-start.7 = (bf16[64,192]{1,0:T(8,128)(2,1)}, bf16[64,192]{1,0:T(8,128)(2,1)S(1)}, u32[]{:S(2)}) copy-start(bf16[64,192]{1,0:T(8,128)(2,1)S(1)} %fusion.2.own_rank) | copy-start | bytes 73732
  96.2 4.7 %collective-permute-start.17 = (bf16[64,128]{1,0:T(8,128)(2,1)S(1)}, bf16[64,128]{1,0:T(8,128)(2,1)S(1)}, u32[]{:S(2)}, u32[]{:S(2)}) collective-permute-start(bf16[64,128]{1,0:T(8,128)(2,1)S(1)} %get-tuple-element.79), channel_id=1, source_target_pairs={{0,8},{1,9},{2,10},{3,11},{4,12},{5,13},{6,14},{7,15},{8,0},{9,1},... | collective-permute-start | bytes 49160 | tf_op jit(solution)/shard_map/ppermute | solution.py:716
  98.0 16.9 %collective-permute-start.16 = (bf16[2,64,1024]{2,1,0:T(8,128)(2,1)S(1)}, bf16[2,64,1024]{2,1,0:T(8,128)(2,1)S(1)}, u32[]{:S(2)}, u32[]{:S(2)}) collective-permute-start(bf16[2,64,1024]{2,1,0:T(8,128)(2,1)S(1)} %collective-permute-done.10), channel_id=1, source_target_pairs={{0,2},{1,3},{2,0},{3,1},{4,6},{5,7},{6,4},{7,5},{8,10},{9,11},{10,... | collective-permute-start | bytes 786440 | tf_op jit(solution)/shard_map/ppermute | solution.py:716
  99.2 9.0 %collective-permute-start.18 = (bf16[2,192,128]{2,1,0:T(8,128)(2,1)S(1)}, bf16[2,192,128]{2,1,0:T(8,128)(2,1)S(1)}, u32[]{:S(2)}, u32[]{:S(2)}) collective-permute-start(bf16[2,192,128]{2,1,0:T(8,128)(2,1)S(1)} %get-tuple-element.57), channel_id=1, source_target_pairs={{0,2},{1,3},{2,0},{3,1},{4,6},{5,7},{6,4},{7,5},{8,10},{9,11},{10,... | collective-permute-start | bytes 294920 | tf_op jit(solution)/shard_map/ppermute | solution.py:716
  108.3 4.9 %collective-permute-start.21 = (bf16[2,64,128]{2,1,0:T(8,128)(2,1)S(1)}, bf16[2,64,128]{2,1,0:T(8,128)(2,1)S(1)}, u32[]{:S(2)}, u32[]{:S(2)}) collective-permute-start(bf16[2,64,128]{2,1,0:T(8,128)(2,1)S(1)} %pad_maximum_fusion.14), channel_id=1, source_target_pairs={{0,6},{1,7},{2,4},{3,5},{4,2},{5,3},{6,0},{7,1},{8,14},{9,15},{10,... | collective-permute-start | bytes 98312 | tf_op jit(solution)/shard_map/ppermute | solution.py:716
  111.0 3.9 %collective-permute-start.20 = (bf16[2,64,128]{2,1,0:T(8,128)(2,1)S(1)}, bf16[2,64,128]{2,1,0:T(8,128)(2,1)S(1)}, u32[]{:S(2)}, u32[]{:S(2)}) collective-permute-start(bf16[2,64,128]{2,1,0:T(8,128)(2,1)S(1)} %pad_maximum_fusion.14), channel_id=1, source_target_pairs={{0,4},{1,5},{2,6},{3,7},{4,0},{5,1},{6,2},{7,3},{8,12},{9,13},{10,... | collective-permute-start | bytes 98312 | tf_op jit(solution)/shard_map/ppermute | solution.py:716
  111.0 3.9 %collective-permute-start.19 = (bf16[2,64,128]{2,1,0:T(8,128)(2,1)S(1)}, bf16[2,64,128]{2,1,0:T(8,128)(2,1)S(1)}, u32[]{:S(2)}, u32[]{:S(2)}) collective-permute-start(bf16[2,64,128]{2,1,0:T(8,128)(2,1)S(1)} %pad_maximum_fusion.14), channel_id=1, source_target_pairs={{0,2},{1,3},{2,0},{3,1},{4,6},{5,7},{6,4},{7,5},{8,10},{9,11},{10,... | collective-permute-start | bytes 98312 | tf_op jit(solution)/shard_map/ppermute | solution.py:716
  115.1 15.2 %copy-start.5 = (bf16[4,2,64,1024]{3,2,1,0:T(8,128)(2,1)}, bf16[4,2,64,1024]{3,2,1,0:T(8,128)(2,1)S(1)}, u32[]{:S(2)}) copy-start(bf16[4,2,64,1024]{3,2,1,0:T(8,128)(2,1)S(1)} %pad_maximum_fusion.key_same.value_same) | copy-start | bytes 3145732
  115.1 15.2 %collective-permute-start.22 = (bf16[4,2,64,1024]{3,2,1,0:T(8,128)(2,1)S(1)}, bf16[4,2,64,1024]{3,2,1,0:T(8,128)(2,1)S(1)}, u32[]{:S(2)}, u32[]{:S(2)}) collective-permute-start(bf16[4,2,64,1024]{3,2,1,0:T(8,128)(2,1)S(1)} %pad_maximum_fusion.key_same.value_same), channel_id=1, source_target_pairs={{0,1},{1,0},{2,3},{3,2},{4,5},{5,4},{6,7},{7,6},{8,9},{9,8},{10,11... | collective-permute-start | bytes 3145736 | tf_op jit(solution)/shard_map/ppermute | solution.py:716
  115.2 7.6 %collective-permute-start.23 = (bf16[2,2,192,128]{3,2,1,0:T(8,128)(2,1)S(1)}, bf16[2,2,192,128]{3,2,1,0:T(8,128)(2,1)S(1)}, u32[]{:S(2)}, u32[]{:S(2)}) collective-permute-start(bf16[2,2,192,128]{3,2,1,0:T(8,128)(2,1)S(1)} %get-tuple-element.60), channel_id=1, source_target_pairs={{0,4},{1,5},{2,6},{3,7},{4,0},{5,1},{6,2},{7,3},{8,12},{9,13},{10,... | collective-permute-start | bytes 589832 | tf_op jit(solution)/shard_map/ppermute | solution.py:716
  122.8 7.5 %copy-start.6 = (bf16[2,2,2,192,128]{4,3,2,1,0:T(8,128)(2,1)}, bf16[2,2,2,192,128]{4,3,2,1,0:T(8,128)(2,1)S(1)}, u32[]{:S(2)}) copy-start(bf16[2,2,2,192,128]{4,3,2,1,0:T(8,128)(2,1)S(1)} %pad_maximum_fusion.4) | copy-start | bytes 1179652
  122.8 7.4 %collective-permute-start.25 = (bf16[4,2,192,128]{3,2,1,0:T(8,128)(2,1)S(1)}, bf16[4,2,192,128]{3,2,1,0:T(8,128)(2,1)S(1)}, u32[]{:S(2)}, u32[]{:S(2)}) collective-permute-start(bf16[4,2,192,128]{3,2,1,0:T(8,128)(2,1)S(1)} %bitcast.40), channel_id=1, source_target_pairs={{0,1},{1,0},{2,3},{3,2},{4,5},{5,4},{6,7},{7,6},{8,9},{9,8},{10,11... | collective-permute-start | bytes 1179656 | tf_op jit(solution)/shard_map/ppermute | solution.py:716
  123.7 5.8 %collective-permute-start.26 = (bf16[384,128]{1,0:T(8,128)(2,1)S(1)}, bf16[384,128]{1,0:T(8,128)(2,1)S(1)}, u32[]{:S(2)}, u32[]{:S(2)}) collective-permute-start(bf16[384,128]{1,0:T(8,128)(2,1)S(1)} %get-tuple-element.63), channel_id=1, source_target_pairs={{0,16},{1,17},{2,18},{3,19},{4,20},{5,21},{6,22},{7,23},{8,24},{9,... | collective-permute-start | bytes 294920 | tf_op jit(solution)/shard_map/ppermute | solution.py:716
  126.1 3.5 %collective-permute-start.24 = (bf16[4,2,64,128]{3,2,1,0:T(8,128)(2,1)S(1)}, bf16[4,2,64,128]{3,2,1,0:T(8,128)(2,1)S(1)}, u32[]{:S(2)}, u32[]{:S(2)}) collective-permute-start(bf16[4,2,64,128]{3,2,1,0:T(8,128)(2,1)S(1)} %pad_maximum_fusion.13), channel_id=1, source_target_pairs={{0,1},{1,0},{2,3},{3,2},{4,5},{5,4},{6,7},{7,6},{8,9},{9,8},{10,11... | collective-permute-start | bytes 393224 | tf_op jit(solution)/shard_map/ppermute | solution.py:716
  130.3 0.7 copy-start.11
  131.0 1.0 copy-start.10
  136.5 12.2 %collective-permute-start.29 = (bf16[2,384,128]{2,1,0:T(8,128)(2,1)S(1)}, bf16[2,384,128]{2,1,0:T(8,128)(2,1)S(1)}, u32[]{:S(2)}, u32[]{:S(2)}) collective-permute-start(bf16[2,384,128]{2,1,0:T(8,128)(2,1)S(1)} %pad_maximum_fusion.12), channel_id=1, source_target_pairs={{0,6},{1,7},{2,4},{3,5},{4,2},{5,3},{6,0},{7,1},{8,14},{9,15},{10,... | collective-permute-start | bytes 589832 | tf_op jit(solution)/shard_map/ppermute | solution.py:716
  138.5 10.2 %collective-permute-start.28 = (bf16[2,384,128]{2,1,0:T(8,128)(2,1)S(1)}, bf16[2,384,128]{2,1,0:T(8,128)(2,1)S(1)}, u32[]{:S(2)}, u32[]{:S(2)}) collective-permute-start(bf16[2,384,128]{2,1,0:T(8,128)(2,1)S(1)} %pad_maximum_fusion.12), channel_id=1, source_target_pairs={{0,4},{1,5},{2,6},{3,7},{4,0},{5,1},{6,2},{7,3},{8,12},{9,13},{10,... | collective-permute-start | bytes 589832 | tf_op jit(solution)/shard_map/ppermute | solution.py:716
  138.8 9.9 %collective-permute-start.27 = (bf16[2,384,128]{2,1,0:T(8,128)(2,1)S(1)}, bf16[2,384,128]{2,1,0:T(8,128)(2,1)S(1)}, u32[]{:S(2)}, u32[]{:S(2)}) collective-permute-start(bf16[2,384,128]{2,1,0:T(8,128)(2,1)S(1)} %pad_maximum_fusion.12), channel_id=1, source_target_pairs={{0,2},{1,3},{2,0},{3,1},{4,6},{5,7},{6,4},{7,5},{8,10},{9,11},{10,... | collective-permute-start | bytes 589832 | tf_op jit(solution)/shard_map/ppermute | solution.py:716
  148.8 2.4 %collective-permute-start.30 = (bf16[4,2,384,128]{3,2,1,0:T(8,128)(2,1)S(1)}, bf16[4,2,384,128]{3,2,1,0:T(8,128)(2,1)S(1)}, u32[]{:S(2)}, u32[]{:S(2)}) collective-permute-start(bf16[4,2,384,128]{3,2,1,0:T(8,128)(2,1)S(1)} %pad_maximum_fusion.1.same), channel_id=1, source_target_pairs={{0,1},{1,0},{2,3},{3,2},{4,5},{5,4},{6,7},{7,6},{8,9},{9,8},{10,11... | collective-permute-start | bytes 2359304 | tf_op jit(solution)/shard_map/ppermute | solution.py:716
  151.2 1.0 copy-start.2

commit v13 on v9

--- a/solution.py
+++ b/solution.py
@@ -531,9 +531,8 @@
     value_same,
     value_other,
     own_rank,
-    all_rank,
-    up_same,
-    up_other,
+    rows_same,
+    rows_other,
     cosines,
     sines,
     *refs,
@@ -549,9 +548,10 @@
     @pl.when(pl.program_id(0) == 0)
     def _():
         for apart in range(PIECES):
-            ups = up_other if apart % 2 else up_same
+            source = rows_other if apart % 2 else rows_same
             for position in range(2):
-                piece = ups[apart // 2, position].astype(jnp.float32)
+                begin = PIECES * rows + (apart // 2 * 2 + position) * UP_ROWS
+                piece = source[begin : begin + UP_ROWS, :].astype(jnp.float32)
                 place = (seat ^ apart) * 2 + position
                 first = pl.multiple_of(place * QUERY_ROWS, QUERY_ROWS)
                 flat_query[pl.ds(first, QUERY_ROWS), :] = piece[:QUERY_ROWS]
@@ -573,7 +573,12 @@
         key_up = up(flat_keyval.at[side], step, heads)
         value_up = up(flat_keyval.at[side], step + KEYVALUE_HEADS, heads)
         for core in range(2):
-            rank = all_rank[core, :, side].reshape(PIECES // 2 * rows, 2 * ADAPTER_RANK)
+            source = rows_other if core else rows_same
+            rank = [
+                source[(2 * chip + side) * rows : (2 * chip + side + 1) * rows, :]
+                for chip in range(PIECES // 2)
+            ]
+            rank = jnp.concatenate(rank, 0)
             key_delta = adapter_scale * dot(rank[:, :ADAPTER_RANK], key_up)
             value_delta = adapter_scale * dot(rank[:, ADAPTER_RANK:], value_up)
             for chip in range(PIECES // 2):
@@ -590,6 +595,8 @@
     cosine = cosines[here, :]
     sine = sines[here, :]
     taken = GROUP // 2
+    limit = lax.broadcasted_iota(jnp.int32, (rows, 1), 0) + base
+    limit = jnp.concatenate([limit] * taken, 0)
     for first in range(0, GROUP, taken):
         weight = [up(flat_query, step * GROUP + first + head, QH) for head in range(taken)]
         deltas = adapter_scale * dot(own_rank[:, :ADAPTER_RANK], jnp.concatenate(weight, 1))
@@ -604,9 +611,8 @@
         scores = lax.dot_general(
             queries, keys[...], (((1,), (1,)), ((), ())), preferred_element_type=jnp.float32
         )
-        row = lax.broadcasted_iota(jnp.int32, scores.shape, 0)
         column = lax.broadcasted_iota(jnp.int32, scores.shape, 1)
-        scores = jnp.where(column <= base + lax.rem(row, rows), scores, mask_floor)
+        scores = jnp.where(column <= limit, scores, mask_floor)
         scores = scores - jnp.max(scores, axis=-1, keepdims=True)
         weights = jnp.exp2(scores * (HEAD_SIZE ** (-0.5) * math.log2(math.e)))
         divisor = jnp.sum(weights, axis=-1, keepdims=True)
@@ -616,7 +622,7 @@
             attended[:, span] = result[place * rows : (place + 1) * rows]
 
 
-def attend(first_head, heads, before, query_base, base, own_rank, all_rank, ups, cosines, sines):
+def attend(first_head, heads, before, query_base, base, own_rank, gathered, cosines, sines):
     rows = query_base.shape[0]
     seq = 4 * PIECES // 2 * rows
     width = GROUP * HEAD_SIZE
@@ -628,7 +634,7 @@
     value_spec = pl.BlockSpec(
         (PIECES // 2, 2, rows, HEAD_SIZE), lambda h: (0, 0, 0, h + first_head + KEYVALUE_HEADS)
     )
-    operands = (query_base, base[0], base[1], base[0], base[1], own_rank, all_rank, *ups)
+    operands = (query_base, base[0], base[1], base[0], base[1], own_rank, *gathered)
     operands += (cosines, sines) + (() if before is None else (before,))
     query_spec = pl.BlockSpec((rows, width), lambda h: (0, h + first_head))
     return pl.pallas_call(
@@ -642,13 +648,12 @@
             value_spec,
             value_spec,
             whole(own_rank.shape),
-            whole(all_rank.shape),
-            whole(ups[0].shape),
-            whole(ups[1].shape),
+            whole(gathered[0].shape),
+            whole(gathered[1].shape),
             whole(cosines.shape),
             whole(sines.shape),
         ]
-        + [pl.BlockSpec(memory_space=pl.ANY)] * (len(operands) - 11),
+        + [pl.BlockSpec(memory_space=pl.ANY)] * (len(operands) - 10),
         out_specs=query_spec,
         input_output_aliases={} if before is None else {len(operands) - 1: 0},
         scratch_shapes=[
@@ -777,11 +782,11 @@
     all_rank = jnp.stack([swap(all_rank, apart) if apart else all_rank for apart in (0, 2, 4, 6)])
     base = after(base, all_rank)
     base = (base, swap(base, 1))
-    all_rank = after(all_rank, ups, ends)
-    ups = (ups, swap(ups, 1))
-    all_rank = jnp.stack([all_rank, swap(all_rank, 1)])
-
-    shared = (query_base, base, own_rank, all_rank, ups, cosines, sines)
+    gathered = jnp.concatenate([all_rank.reshape(-1, 128), ups.reshape(-1, 128)])
+    gathered = after(gathered, ends)
+    gathered = (gathered, swap(gathered, 1))
+
+    shared = (query_base, base, own_rank, gathered, cosines, sines)
     attended = attend(0, 1, None, *shared)
     ends = after(ends, attended)
     ends = jnp.stack([swap(ends, apart) if apart else ends for apart in (0, 2, 4, 6)])

time: 143 us -> 140 us (0.979)
  waiting for transfers between devices: 62.6 us -> 60.6 us
    ppermute x30 -> x29, waiting for transfers between devices: 60.4 us -> 58.4 us  [swap(): lax.ppermute(block, ('groups', 'ctx'), [(i, i ^ mask) for i in range(4 *...]
    ppermute x30 -> x29, starting transfers between devices: 39.2 us -> 37.9 us  [swap(): lax.ppermute(block, ('groups', 'ctx'), [(i, i ^ mask) for i in range(4 *...]
    unnamed x23 -> x25, local copies, waits for them, and re-layouts: 3.53 us -> 4.56 us
  transfers between devices with their start and end apart: 31 -> 30, of which waited for: 16 -> 15; matrix products, arithmetic and copies ran while one was open for 3% -> 3% of each run, Pallas kernels for 8% -> 8%
where the time goes in v13:
time: 140 us; the launch traced here: 139 us
  waiting for transfers between devices  60.6 us (43%)
  starting transfers between devices  43.4 us (31%)
  Pallas kernels  25.6 us (18%)
  local copies, waits for them, and re-layouts  4.82 us (3%)
  other arithmetic  3.8 us (3%)
    ppermute x29, waiting for transfers between devices, swap(): lax.ppermute(block, ('groups', 'ctx'), [(i, i ^ mask) for i in range(4 *...  58.4 us
    ppermute x29, starting transfers between devices, swap(): lax.ppermute(block, ('groups', 'ctx'), [(i, i ^ mask) for i in range(4 *...  37.9 us
    pallas_call x2, Pallas kernels, attend(): pl.pallas_call(partial(attend_kernel, first_head), grid=(heads,), out_sha...  12.9 us
    all_to_all x1, starting transfers between devices, direct_shards(): spread = lax.all_to_all(packed, 'ctx', 0, 0, axis_index_groups=blocks)  5.5 us
    pallas_call x1, Pallas kernels, pack_row(): pl.pallas_call(partial(pack_kernel, sections), out_shape=jax.ShapeDtypeSt...  5.16 us
    unnamed x25, local copies, waits for them, and re-layouts  4.56 us
    pallas_call x1, Pallas kernels, widen(): pl.pallas_call(widen_kernel, out_shape=jax.ShapeDtypeStruct((attended.sha...  2.98 us
  transfers between devices with their start and end apart: 30, of which 15 were waited for; matrix products, arithmetic and copies ran while one was open for 3% of the time, Pallas kernels for 8%

profile of v13, /device:TPU:0, one launch (start us, length us, event | category | flops | bytes accessed | tf_op | source)
XLA Modules:
  0.0 139.1 jit_solution(5318126773910444114)
XLA Ops:
  0.6 5.2 %shard_map.86.refs_0_ = bf16[8,1312,128]{2,1,0:T(8,128)(2,1)} custom-call(bf16[1,2686976]{1,0:T(2,128)(2,1)} %pool.1), custom_call_target="tpu_custom_call" | custom-call | bytes 8388608 | tf_op jit(solution)/shard_map/pallas_call | solution.py:316
  5.8 5.5 %all-to-all-start = ((bf16[8,1312,128]{2,1,0:T(8,128)(2,1)}), bf16[8,1312,128]{2,1,0:T(8,128)(2,1)}, u32[]{:S(2)}, u32[]{:S(2)}) async-start(bf16[8,1312,128]{2,1,0:T(8,128)(2,1)} %shard_map.86.refs_0_), calls=%async_computation | async-start | bytes 5373952 | tf_op jit(solution)/shard_map/all_to_all | solution.py:756
  11.3 2.2 %collective-permute-start.1 = (s32[2]{0:T(128)S(1)}, s32[2]{0:T(128)S(1)}, u32[]{:S(2)}, u32[]{:S(2)}) collective-permute-start(s32[2]{0:T(128)S(1)} %copy-done.3), channel_id=1, source_target_pairs={{0,16},{1,17},{2,18},{3,19},{4,20},{5,21},{6,22},{7,23},{8,24},{9,... | collective-permute-start | bytes 32 | tf_op jit(solution)/shard_map/ppermute | solution.py:717
  13.5 1.2 copy-done.1
  14.8 0.3 shard_map.87
  15.0 0.1 collective-permute-start.2
  15.1 0.5 copy-done.8
  15.6 0.0 copy-done.9
  15.7 2.6 %collective-permute-start = (bf16[64,1024]{1,0:T(8,128)(2,1)S(1)}, bf16[64,1024]{1,0:T(8,128)(2,1)S(1)}, u32[]{:S(2)}, u32[]{:S(2)}) collective-permute-start(bf16[64,1024]{1,0:T(8,128)(2,1)S(1)} %constant_dynamic-update-slice_fusion), channel_id=1, source_target_pairs={{0,8},{1,9},{2,10},{3,11},{4,12},{5,13},{6,14},{7,15},{8,0},{9,1},... | collective-permute-start | bytes 393224 | tf_op jit(solution)/shard_map/ppermute | solution.py:717
  18.4 1.9 %fusion = (f32[1024,64]{1,0:T(8,128)S(1)}, f32[1024,64]{1,0:T(8,128)S(1)}, f32[1024,64]{1,0:T(8,128)S(1)}) fusion(f32[64]{0:T(128)S(1)} %multiply_power_fusion, f32[1024]{0:T(1024)S(1)} %iota_convert_fusion), kind=kLoop, calls=%fused_computation.16 | loop fusion | flops 131072 | bytes 790784 | tf_op jit(solution)/shard_map/neg | solution.py:733
  20.3 1.3 pad_maximum_fusion.2
  21.6 22.5 %collective-permute-done = bf16[64,1024]{1,0:T(8,128)(2,1)S(1)} collective-permute-done((bf16[64,1024]{1,0:T(8,128)(2,1)S(1)}, bf16[64,1024]{1,0:T(8,128)(2,1)S(1)}, u32[]{:S(2)}, u32[]{:S(2)}) %collective-permute-start) | collective-permute-done | bytes 131104 | tf_op jit(solution)/shard_map/ppermute | solution.py:717
  44.2 2.1 %all-to-all-done.spread = bf16[8,1312,128]{2,1,0:T(8,128)(2,1)} async-done(((bf16[8,1312,128]{2,1,0:T(8,128)(2,1)}), bf16[8,1312,128]{2,1,0:T(8,128)(2,1)}, u32[]{:S(2)}, u32[]{:S(2)}) %all-to-all-start) | async-done | bytes 2687008 | tf_op jit(solution)/shard_map/all_to_all | solution.py:756
  46.3 2.1 %shard_map.88 = (bf16[960,128]{1,0:T(8,128)(2,1)S(1)}, bf16[960,128]{1,0:T(8,128)(2,1)S(1)}, bf16[960,128]{1,0:T(8,128)(2,1)S(1)}, bf16[960,128]{1,0:T(8,128)(2,...) custom-call(s32[2]{0:T(128)S(1)} %copy-done.3, s32[2]{0:T(128)S(1)} %collective-permute-done.1.there, ...), custom_call_target="tpu_custom_call" | custom-call | bytes 3145728 | tf_op jit(solution)/shard_map/pallas_call | solution.py:360
  48.4 1.3 collective-permute-start.3
  49.9 1.7 %collective-permute-start.6 = (bf16[2,64,1024]{2,1,0:T(8,128)(2,1)S(1)}, bf16[2,64,1024]{2,1,0:T(8,128)(2,1)S(1)}, u32[]{:S(2)}, u32[]{:S(2)}) collective-permute-start(bf16[2,64,1024]{2,1,0:T(8,128)(2,1)S(1)} %get-tuple-element.44), channel_id=1, source_target_pairs={{0,2},{1,3},{2,0},{3,1},{4,6},{5,7},{6,4},{7,5},{8,10},{9,11},{10,... | collective-permute-start | bytes 786440 | tf_op jit(solution)/shard_map/ppermute | solution.py:717
  51.5 2.2 %collective-permute-start.7 = (bf16[2,64,1024]{2,1,0:T(8,128)(2,1)S(1)}, bf16[2,64,1024]{2,1,0:T(8,128)(2,1)S(1)}, u32[]{:S(2)}, u32[]{:S(2)}) collective-permute-start(bf16[2,64,1024]{2,1,0:T(8,128)(2,1)S(1)} %get-tuple-element.45), channel_id=1, source_target_pairs={{0,4},{1,5},{2,6},{3,7},{4,0},{5,1},{6,2},{7,3},{8,12},{9,13},{10,... | collective-permute-start | bytes 786440 | tf_op jit(solution)/shard_map/ppermute | solution.py:717
  53.8 1.7 %collective-permute-start.4 = (bf16[960,128]{1,0:T(8,128)(2,1)S(1)}, bf16[960,128]{1,0:T(8,128)(2,1)S(1)}, u32[]{:S(2)}, u32[]{:S(2)}) collective-permute-start(bf16[960,128]{1,0:T(8,128)(2,1)S(1)} %get-tuple-element.39), channel_id=1, source_target_pairs={{0,16},{1,17},{2,18},{3,19},{4,20},{5,21},{6,22},{7,23},{8,24},{9,... | collective-permute-start | bytes 737288 | tf_op jit(solution)/shard_map/ppermute | solution.py:717
  55.4 6.7 %collective-permute-done.3.refs_1_ = bf16[960,128]{1,0:T(8,128)(2,1)S(1)} collective-permute-done((bf16[960,128]{1,0:T(8,128)(2,1)S(1)}, bf16[960,128]{1,0:T(8,128)(2,1)S(1)}, u32[]{:S(2)}, u32[]{:S(2)}) %collective-permute-start.3) | collective-permute-done | bytes 245792 | tf_op jit(solution)/shard_map/ppermute | solution.py:717
  62.2 1.0 collective-permute-start.5
  63.2 8.4 %collective-permute-done.5.refs_3_ = bf16[960,128]{1,0:T(8,128)(2,1)S(1)} collective-permute-done((bf16[960,128]{1,0:T(8,128)(2,1)S(1)}, bf16[960,128]{1,0:T(8,128)(2,1)S(1)}, u32[]{:S(2)}, u32[]{:S(2)}) %collective-permute-start.5) | collective-permute-done | bytes 245792 | tf_op jit(solution)/shard_map/ppermute | solution.py:717
  71.7 1.0 shard_map.89
  72.6 1.1 collective-permute-done.8.refs_3_
  73.8 0.4 shard_map.90
  74.2 5.7 %collective-permute-start.12 = (bf16[2,64,192]{2,1,0:T(8,128)(2,1)S(1)}, bf16[2,64,192]{2,1,0:T(8,128)(2,1)S(1)}, u32[]{:S(2)}, u32[]{:S(2)}) collective-permute-start(bf16[2,64,192]{2,1,0:T(8,128)(2,1)S(1)} %get-tuple-element.50), channel_id=1, source_target_pairs={{0,6},{1,7},{2,4},{3,5},{4,2},{5,3},{6,0},{7,1},{8,14},{9,15},{10,... | collective-permute-start | bytes 147464 | tf_op jit(solution)/shard_map/ppermute | solution.py:717
  79.9 0.6 collective-permute-start.10
  80.5 2.8 %collective-permute-start.13 = (bf16[2,384,128]{2,1,0:T(8,128)(2,1)S(1)}, bf16[2,384,128]{2,1,0:T(8,128)(2,1)S(1)}, u32[]{:S(2)}, u32[]{:S(2)}) collective-permute-start(bf16[2,384,128]{2,1,0:T(8,128)(2,1)S(1)} %get-tuple-element.53), channel_id=1, source_target_pairs={{0,8},{1,9},{2,10},{3,11},{4,12},{5,13},{6,14},{7,15},{8,0},{9,1},... | collective-permute-start | bytes 589832 | tf_op jit(solution)/shard_map/ppermute | solution.py:717
  83.3 2.0 %collective-permute-start.9 = (bf16[2,64,1024]{2,1,0:T(8,128)(2,1)S(1)}, bf16[2,64,1024]{2,1,0:T(8,128)(2,1)S(1)}, u32[]{:S(2)}, u32[]{:S(2)}) collective-permute-start(bf16[2,64,1024]{2,1,0:T(8,128)(2,1)S(1)} %pad_maximum_fusion.7), channel_id=1, source_target_pairs={{0,4},{1,5},{2,6},{3,7},{4,0},{5,1},{6,2},{7,3},{8,12},{9,13},{10,... | collective-permute-start | bytes 786440 | tf_op jit(solution)/shard_map/ppermute | solution.py:717
  85.3 0.3 collective-permute-done.11
  85.7 5.6 %collective-permute-done.13.far = bf16[2,384,128]{2,1,0:T(8,128)(2,1)S(1)} collective-permute-done((bf16[2,384,128]{2,1,0:T(8,128)(2,1)S(1)}, bf16[2,384,128]{2,1,0:T(8,128)(2,1)S(1)}, u32[]{:S(2)}, u32[]{:S(2)}) %collective-permute-start.13) | collective-permute-done | bytes 196640 | tf_op jit(solution)/shard_map/ppermute | solution.py:717
  91.4 0.7 collective-permute-start.17
  92.0 0.5 collective-permute-done.14
  92.6 0.8 collective-permute-done.9
  93.4 0.1 pad_maximum_fusion.4
  93.4 1.3 collective-permute-start.15
  94.7 0.1 slice_bitcast_fusion.1
  94.7 2.1 %collective-permute-start.16 = (bf16[64,128]{1,0:T(8,128)(2,1)S(1)}, bf16[64,128]{1,0:T(8,128)(2,1)S(1)}, u32[]{:S(2)}, u32[]{:S(2)}) collective-permute-start(bf16[64,128]{1,0:T(8,128)(2,1)S(1)} %get-tuple-element.77), channel_id=1, source_target_pairs={{0,8},{1,9},{2,10},{3,11},{4,12},{5,13},{6,14},{7,15},{8,0},{9,1},... | collective-permute-start | bytes 49160 | tf_op jit(solution)/shard_map/ppermute | solution.py:717
  96.8 2.6 %collective-permute-done.16 = bf16[64,128]{1,0:T(8,128)(2,1)S(1)} collective-permute-done((bf16[64,128]{1,0:T(8,128)(2,1)S(1)}, bf16[64,128]{1,0:T(8,128)(2,1)S(1)}, u32[]{:S(2)}, u32[]{:S(2)}) %collective-permute-start.16) | collective-permute-done | bytes 16416 | tf_op jit(solution)/shard_map/ppermute | solution.py:717
  99.4 1.7 %collective-permute-start.20 = (bf16[2,64,128]{2,1,0:T(8,128)(2,1)S(1)}, bf16[2,64,128]{2,1,0:T(8,128)(2,1)S(1)}, u32[]{:S(2)}, u32[]{:S(2)}) collective-permute-start(bf16[2,64,128]{2,1,0:T(8,128)(2,1)S(1)} %pad_maximum_fusion.15), channel_id=1, source_target_pairs={{0,6},{1,7},{2,4},{3,5},{4,2},{5,3},{6,0},{7,1},{8,14},{9,15},{10,... | collective-permute-start | bytes 98312 | tf_op jit(solution)/shard_map/ppermute | solution.py:717
  101.0 0.6 collective-permute-start.19
  101.7 1.2 collective-permute-start.18
  102.9 0.8 shard_map.91
  103.7 1.7 %collective-permute-start.23 = (bf16[384,128]{1,0:T(8,128)(2,1)S(1)}, bf16[384,128]{1,0:T(8,128)(2,1)S(1)}, u32[]{:S(2)}, u32[]{:S(2)}) collective-permute-start(bf16[384,128]{1,0:T(8,128)(2,1)S(1)} %get-tuple-element.64), channel_id=1, source_target_pairs={{0,16},{1,17},{2,18},{3,19},{4,20},{5,21},{6,22},{7,23},{8,24},{9,... | collective-permute-start | bytes 294920 | tf_op jit(solution)/shard_map/ppermute | solution.py:717
  105.4 1.0 collective-permute-start.22
  106.4 3.3 %collective-permute-done.18 = bf16[2,64,128]{2,1,0:T(8,128)(2,1)S(1)} collective-permute-done((bf16[2,64,128]{2,1,0:T(8,128)(2,1)S(1)}, bf16[2,64,128]{2,1,0:T(8,128)(2,1)S(1)}, u32[]{:S(2)}, u32[]{:S(2)}) %collective-permute-start.18) | collective-permute-done | bytes 32800 | tf_op jit(solution)/shard_map/ppermute | solution.py:717
  109.8 0.1 pad_maximum_fusion
  109.9 0.1 copy.10
  110.0 0.1 collective-permute-start.21
  110.1 2.2 %collective-permute-done.22 = bf16[2,2,192,128]{3,2,1,0:T(8,128)(2,1)S(1)} collective-permute-done((bf16[2,2,192,128]{3,2,1,0:T(8,128)(2,1)S(1)}, bf16[2,2,192,128]{3,2,1,0:T(8,128)(2,1)S(1)}, u32[]{:S(2)}, u32[]{:S(2)}) %collective-permute-start.22) | collective-permute-done | bytes 196640 | tf_op jit(solution)/shard_map/ppermute | solution.py:717
  112.5 0.1 collective-permute-start.24
  112.5 1.9 %collective-permute-done.24.rows_other = bf16[2048,128]{1,0:T(8,128)(2,1)S(1)} collective-permute-done((bf16[2048,128]{1,0:T(8,128)(2,1)S(1)}, bf16[2048,128]{1,0:T(8,128)(2,1)S(1)}, u32[]{:S(2)}, u32[]{:S(2)}) %collective-permute-start.24) | collective-permute-done | bytes 524320 | tf_op jit(solution)/shard_map/ppermute | solution.py:717
  114.5 0.8 copy-done.11
  115.2 1.0 copy-done.10
  116.2 4.4 %shard_map.92.refs_0_ = bf16[64,4096]{1,0:T(8,128)(2,1)} custom-call(bf16[64,4096]{1,0:T(8,128)(2,1)} %query_block.3, bf16[4,2,64,1024]{3,2,1,0:T(8,128)(2,1)} %bitcast.39, bf16[4,2,64,1024]{3,2,1,0:T(8,128)(2,1)} %copy-done.10, bf16[4,2,64,1024]{3,2,1,0:T(8,128)(2,1)} %bitcast.40, bf16[4,2,64,1024]{3,2,1,0:T(8,128)(2,1)} %copy-done.10, ...), custom_call_target="tpu_custom_call" | custom-call | flops 3221225472 | bytes 10485760 | tf_op jit(solution)/shard_map/pallas_call | solution.py:640
  120.6 1.5 %collective-permute-start.27 = (bf16[2,384,128]{2,1,0:T(8,128)(2,1)S(1)}, bf16[2,384,128]{2,1,0:T(8,128)(2,1)S(1)}, u32[]{:S(2)}, u32[]{:S(2)}) collective-permute-start(bf16[2,384,128]{2,1,0:T(8,128)(2,1)S(1)} %pad_maximum_fusion.13), channel_id=1, source_target_pairs={{0,6},{1,7},{2,4},{3,5},{4,2},{5,3},{6,0},{7,1},{8,14},{9,15},{10,... | collective-permute-start | bytes 589832 | tf_op jit(solution)/shard_map/ppermute | solution.py:717
  122.1 1.1 collective-permute-start.26
  123.3 0.8 collective-permute-start.25
  124.1 8.5 %shard_map.93.attended = bf16[64,4096]{1,0:T(8,128)(2,1)} custom-call(bf16[64,4096]{1,0:T(8,128)(2,1)} %query_block.3, bf16[4,2,64,1024]{3,2,1,0:T(8,128)(2,1)} %bitcast.41, bf16[4,2,64,1024]{3,2,1,0:T(8,128)(2,1)} %copy-done.10, bf16[4,2,64,1024]{3,2,1,0:T(8,128)(2,1)} %bitcast.42, ...), custom_call_target="tpu_custom_call", output_to_operand_aliasing={{}: (10, {})} | custom-call | flops 9663676416 | bytes 10485760 | tf_op jit(solution)/shard_map/pallas_call | solution.py:640
  132.6 0.1 collective-permute-done.25
  132.7 0.1 pad_maximum_fusion.1.same
  132.8 0.1 collective-permute-start.28
  132.8 2.3 %collective-permute-done.28.other = bf16[4,2,384,128]{3,2,1,0:T(8,128)(2,1)S(1)} collective-permute-done((bf16[4,2,384,128]{3,2,1,0:T(8,128)(2,1)S(1)}, bf16[4,2,384,128]{3,2,1,0:T(8,128)(2,1)S(1)}, u32[]{:S(2)}, u32[]{:S(2)}) %collective-permute-start.28) | collective-permute-done | bytes 786464 | tf_op jit(solution)/shard_map/ppermute | solution.py:717
  135.1 1.0 copy-done.2
  136.2 3.0 %shard_map.94 = bf16[64,8192]{1,0:T(8,128)(2,1)} custom-call(bf16[64,4096]{1,0:T(8,128)(2,1)S(1)} %copy-done.2, bf16[4,2,384,128]{3,2,1,0:T(8,128)(2,1)S(1)} %pad_maximum_fusion.1.same, bf16[4,2,384,128]{3,2,1,0:T(8,128)(2,1)S(1)} %collective-permute-done.28.other), custom_call_target="tpu_custom_call" | custom-call | flops 134217728 | bytes 4194304 | tf_op jit(solution)/shard_map/pallas_call | solution.py:702
  (55 shorter events, 0.5 us)
Async XLA Ops:
  5.8 5.5 %copy-start.3 = (s32[2]{0:T(128)S(1)}, s32[2]{0:T(128)}, u32[]{:S(2)}) copy-start(s32[2]{0:T(128)} %here.5) | copy-start | bytes 28
  5.8 7.7 %copy-start = (bf16[8,1312,128]{2,1,0:T(8,128)(2,1)S(1)}, bf16[8,1312,128]{2,1,0:T(8,128)(2,1)}, u32[]{:S(2)}) copy-start(bf16[8,1312,128]{2,1,0:T(8,128)(2,1)} %shard_map.86.refs_0_) | copy-start | bytes 8060932
  5.8 40.5 %all-to-all-start = ((bf16[8,1312,128]{2,1,0:T(8,128)(2,1)}), bf16[8,1312,128]{2,1,0:T(8,128)(2,1)}, u32[]{:S(2)}, u32[]{:S(2)}) async-start(bf16[8,1312,128]{2,1,0:T(8,128)(2,1)} %shard_map.86.refs_0_), calls=%async_computation | async-start | bytes 5373952 | tf_op jit(solution)/shard_map/all_to_all | solution.py:756
  11.3 35.0 %collective-permute-start.1 = (s32[2]{0:T(128)S(1)}, s32[2]{0:T(128)S(1)}, u32[]{:S(2)}, u32[]{:S(2)}) collective-permute-start(s32[2]{0:T(128)S(1)} %copy-done.3), channel_id=1, source_target_pairs={{0,16},{1,17},{2,18},{3,19},{4,20},{5,21},{6,22},{7,23},{8,24},{9,... | collective-permute-start | bytes 32 | tf_op jit(solution)/shard_map/ppermute | solution.py:717
  13.5 1.2 copy-start.1
  14.8 0.8 copy-start.8
  14.8 0.9 copy-start.9
  15.0 29.1 %collective-permute-start.2 = (bf16[4,64,1024]{2,1,0:T(8,128)(2,1)S(1)}, bf16[4,64,1024]{2,1,0:T(8,128)(2,1)S(1)}, u32[]{:S(2)}, u32[]{:S(2)}) collective-permute-start(bf16[4,64,1024]{2,1,0:T(8,128)(2,1)S(1)} %get-tuple-element.35), channel_id=1, source_target_pairs={{0,1},{1,0},{2,3},{3,2},{4,5},{5,4},{6,7},{7,6},{8,9},{9,8},{10,11... | collective-permute-start | bytes 1572872 | tf_op jit(solution)/shard_map/ppermute | solution.py:717
  15.7 28.4 %collective-permute-start = (bf16[64,1024]{1,0:T(8,128)(2,1)S(1)}, bf16[64,1024]{1,0:T(8,128)(2,1)S(1)}, u32[]{:S(2)}, u32[]{:S(2)}) collective-permute-start(bf16[64,1024]{1,0:T(8,128)(2,1)S(1)} %constant_dynamic-update-slice_fusion), channel_id=1, source_target_pairs={{0,8},{1,9},{2,10},{3,11},{4,12},{5,13},{6,14},{7,15},{8,0},{9,1},... | collective-permute-start | bytes 393224 | tf_op jit(solution)/shard_map/ppermute | solution.py:717
  18.4 27.9 %copy-start.4 = (s32[16]{0:T(128)S(1)}, s32[16]{0:T(128)}, u32[]{:S(2)}) copy-start(s32[16]{0:T(128)} %owner.5) | copy-start | bytes 196
  48.4 13.8 %collective-permute-start.3 = (bf16[960,128]{1,0:T(8,128)(2,1)S(1)}, bf16[960,128]{1,0:T(8,128)(2,1)S(1)}, u32[]{:S(2)}, u32[]{:S(2)}) collective-permute-start(bf16[960,128]{1,0:T(8,128)(2,1)S(1)} %get-tuple-element.38), channel_id=1, source_target_pairs={{0,8},{1,9},{2,10},{3,11},{4,12},{5,13},{6,14},{7,15},{8,0},{9,1},... | collective-permute-start | bytes 737288 | tf_op jit(solution)/shard_map/ppermute | solution.py:717
  49.9 22.8 %collective-permute-start.6 = (bf16[2,64,1024]{2,1,0:T(8,128)(2,1)S(1)}, bf16[2,64,1024]{2,1,0:T(8,128)(2,1)S(1)}, u32[]{:S(2)}, u32[]{:S(2)}) collective-permute-start(bf16[2,64,1024]{2,1,0:T(8,128)(2,1)S(1)} %get-tuple-element.44), channel_id=1, source_target_pairs={{0,2},{1,3},{2,0},{3,1},{4,6},{5,7},{6,4},{7,5},{8,10},{9,11},{10,... | collective-permute-start | bytes 786440 | tf_op jit(solution)/shard_map/ppermute | solution.py:717
  51.5 21.1 %collective-permute-start.7 = (bf16[2,64,1024]{2,1,0:T(8,128)(2,1)S(1)}, bf16[2,64,1024]{2,1,0:T(8,128)(2,1)S(1)}, u32[]{:S(2)}, u32[]{:S(2)}) collective-permute-start(bf16[2,64,1024]{2,1,0:T(8,128)(2,1)S(1)} %get-tuple-element.45), channel_id=1, source_target_pairs={{0,4},{1,5},{2,6},{3,7},{4,0},{5,1},{6,2},{7,3},{8,12},{9,13},{10,... | collective-permute-start | bytes 786440 | tf_op jit(solution)/shard_map/ppermute | solution.py:717
  53.8 20.0 %collective-permute-start.8 = (bf16[2,64,1024]{2,1,0:T(8,128)(2,1)S(1)}, bf16[2,64,1024]{2,1,0:T(8,128)(2,1)S(1)}, u32[]{:S(2)}, u32[]{:S(2)}) collective-permute-start(bf16[2,64,1024]{2,1,0:T(8,128)(2,1)S(1)} %get-tuple-element.46), channel_id=1, source_target_pairs={{0,6},{1,7},{2,4},{3,5},{4,2},{5,3},{6,0},{7,1},{8,14},{9,15},{10,... | collective-permute-start | bytes 786440 | tf_op jit(solution)/shard_map/ppermute | solution.py:717
  53.8 9.4 %collective-permute-start.4 = (bf16[960,128]{1,0:T(8,128)(2,1)S(1)}, bf16[960,128]{1,0:T(8,128)(2,1)S(1)}, u32[]{:S(2)}, u32[]{:S(2)}) collective-permute-start(bf16[960,128]{1,0:T(8,128)(2,1)S(1)} %get-tuple-element.39), channel_id=1, source_target_pairs={{0,16},{1,17},{2,18},{3,19},{4,20},{5,21},{6,22},{7,23},{8,24},{9,... | collective-permute-start | bytes 737288 | tf_op jit(solution)/shard_map/ppermute | solution.py:717
  62.2 9.5 %collective-permute-start.5 = (bf16[960,128]{1,0:T(8,128)(2,1)S(1)}, bf16[960,128]{1,0:T(8,128)(2,1)S(1)}, u32[]{:S(2)}, u32[]{:S(2)}) collective-permute-start(bf16[960,128]{1,0:T(8,128)(2,1)S(1)} %get-tuple-element.40), channel_id=1, source_target_pairs={{0,24},{1,25},{2,26},{3,27},{4,28},{5,29},{6,30},{7,31},{8,16},{9,... | collective-permute-start | bytes 737288 | tf_op jit(solution)/shard_map/ppermute | solution.py:717
  74.2 11.1 %collective-permute-start.12 = (bf16[2,64,192]{2,1,0:T(8,128)(2,1)S(1)}, bf16[2,64,192]{2,1,0:T(8,128)(2,1)S(1)}, u32[]{:S(2)}, u32[]{:S(2)}) collective-permute-start(bf16[2,64,192]{2,1,0:T(8,128)(2,1)S(1)} %get-tuple-element.50), channel_id=1, source_target_pairs={{0,6},{1,7},{2,4},{3,5},{4,2},{5,3},{6,0},{7,1},{8,14},{9,15},{10,... | collective-permute-start | bytes 147464 | tf_op jit(solution)/shard_map/ppermute | solution.py:717
  79.9 5.8 %collective-permute-start.11 = (bf16[2,64,192]{2,1,0:T(8,128)(2,1)S(1)}, bf16[2,64,192]{2,1,0:T(8,128)(2,1)S(1)}, u32[]{:S(2)}, u32[]{:S(2)}) collective-permute-start(bf16[2,64,192]{2,1,0:T(8,128)(2,1)S(1)} %get-tuple-element.49), channel_id=1, source_target_pairs={{0,4},{1,5},{2,6},{3,7},{4,0},{5,1},{6,2},{7,3},{8,12},{9,13},{10,... | collective-permute-start | bytes 147464 | tf_op jit(solution)/shard_map/ppermute | solution.py:717
  79.9 5.8 %collective-permute-start.10 = (bf16[2,64,192]{2,1,0:T(8,128)(2,1)S(1)}, bf16[2,64,192]{2,1,0:T(8,128)(2,1)S(1)}, u32[]{:S(2)}, u32[]{:S(2)}) collective-permute-start(bf16[2,64,192]{2,1,0:T(8,128)(2,1)S(1)} %get-tuple-element.48), channel_id=1, source_target_pairs={{0,2},{1,3},{2,0},{3,1},{4,6},{5,7},{6,4},{7,5},{8,10},{9,11},{10,... | collective-permute-start | bytes 147464 | tf_op jit(solution)/shard_map/ppermute | solution.py:717
  80.5 10.8 %collective-permute-start.13 = (bf16[2,384,128]{2,1,0:T(8,128)(2,1)S(1)}, bf16[2,384,128]{2,1,0:T(8,128)(2,1)S(1)}, u32[]{:S(2)}, u32[]{:S(2)}) collective-permute-start(bf16[2,384,128]{2,1,0:T(8,128)(2,1)S(1)} %get-tuple-element.53), channel_id=1, source_target_pairs={{0,8},{1,9},{2,10},{3,11},{4,12},{5,13},{6,14},{7,15},{8,0},{9,1},... | collective-permute-start | bytes 589832 | tf_op jit(solution)/shard_map/ppermute | solution.py:717
  83.3 10.1 %collective-permute-start.9 = (bf16[2,64,1024]{2,1,0:T(8,128)(2,1)S(1)}, bf16[2,64,1024]{2,1,0:T(8,128)(2,1)S(1)}, u32[]{:S(2)}, u32[]{:S(2)}) collective-permute-start(bf16[2,64,1024]{2,1,0:T(8,128)(2,1)S(1)} %pad_maximum_fusion.7), channel_id=1, source_target_pairs={{0,4},{1,5},{2,6},{3,7},{4,0},{5,1},{6,2},{7,3},{8,12},{9,13},{10,... | collective-permute-start | bytes 786440 | tf_op jit(solution)/shard_map/ppermute | solution.py:717
  91.3 1.2 collective-permute-start.14
  91.4 5.4 %collective-permute-start.17 = (bf16[2,192,128]{2,1,0:T(8,128)(2,1)S(1)}, bf16[2,192,128]{2,1,0:T(8,128)(2,1)S(1)}, u32[]{:S(2)}, u32[]{:S(2)}) collective-permute-start(bf16[2,192,128]{2,1,0:T(8,128)(2,1)S(1)} %get-tuple-element.57), channel_id=1, source_target_pairs={{0,4},{1,5},{2,6},{3,7},{4,0},{5,1},{6,2},{7,3},{8,12},{9,13},{10,... | collective-permute-start | bytes 294920 | tf_op jit(solution)/shard_map/ppermute | solution.py:717
  92.6 17.4 %copy-start.7 = (bf16[64,192]{1,0:T(8,128)(2,1)}, bf16[64,192]{1,0:T(8,128)(2,1)S(1)}, u32[]{:S(2)}) copy-start(bf16[64,192]{1,0:T(8,128)(2,1)S(1)} %fusion.2.own_rank) | copy-start | bytes 73732
  93.4 16.4 %collective-permute-start.15 = (bf16[2,2,64,1024]{3,2,1,0:T(8,128)(2,1)S(1)}, bf16[2,2,64,1024]{3,2,1,0:T(8,128)(2,1)S(1)}, u32[]{:S(2)}, u32[]{:S(2)}) collective-permute-start(bf16[2,2,64,1024]{3,2,1,0:T(8,128)(2,1)S(1)} %pad_maximum_fusion.4), channel_id=1, source_target_pairs={{0,2},{1,3},{2,0},{3,1},{4,6},{5,7},{6,4},{7,5},{8,10},{9,11},{10,... | collective-permute-start | bytes 1572872 | tf_op jit(solution)/shard_map/ppermute | solution.py:717
  94.7 4.6 %collective-permute-start.16 = (bf16[64,128]{1,0:T(8,128)(2,1)S(1)}, bf16[64,128]{1,0:T(8,128)(2,1)S(1)}, u32[]{:S(2)}, u32[]{:S(2)}) collective-permute-start(bf16[64,128]{1,0:T(8,128)(2,1)S(1)} %get-tuple-element.77), channel_id=1, source_target_pairs={{0,8},{1,9},{2,10},{3,11},{4,12},{5,13},{6,14},{7,15},{8,0},{9,1},... | collective-permute-start | bytes 49160 | tf_op jit(solution)/shard_map/ppermute | solution.py:717
  99.4 6.0 %collective-permute-start.20 = (bf16[2,64,128]{2,1,0:T(8,128)(2,1)S(1)}, bf16[2,64,128]{2,1,0:T(8,128)(2,1)S(1)}, u32[]{:S(2)}, u32[]{:S(2)}) collective-permute-start(bf16[2,64,128]{2,1,0:T(8,128)(2,1)S(1)} %pad_maximum_fusion.15), channel_id=1, source_target_pairs={{0,6},{1,7},{2,4},{3,5},{4,2},{5,3},{6,0},{7,1},{8,14},{9,15},{10,... | collective-permute-start | bytes 98312 | tf_op jit(solution)/shard_map/ppermute | solution.py:717
  101.0 5.4 %collective-permute-start.19 = (bf16[2,64,128]{2,1,0:T(8,128)(2,1)S(1)}, bf16[2,64,128]{2,1,0:T(8,128)(2,1)S(1)}, u32[]{:S(2)}, u32[]{:S(2)}) collective-permute-start(bf16[2,64,128]{2,1,0:T(8,128)(2,1)S(1)} %pad_maximum_fusion.15), channel_id=1, source_target_pairs={{0,4},{1,5},{2,6},{3,7},{4,0},{5,1},{6,2},{7,3},{8,12},{9,13},{10,... | collective-permute-start | bytes 98312 | tf_op jit(solution)/shard_map/ppermute | solution.py:717
  101.7 8.0 %collective-permute-start.18 = (bf16[2,64,128]{2,1,0:T(8,128)(2,1)S(1)}, bf16[2,64,128]{2,1,0:T(8,128)(2,1)S(1)}, u32[]{:S(2)}, u32[]{:S(2)}) collective-permute-start(bf16[2,64,128]{2,1,0:T(8,128)(2,1)S(1)} %pad_maximum_fusion.15), channel_id=1, source_target_pairs={{0,2},{1,3},{2,0},{3,1},{4,6},{5,7},{6,4},{7,5},{8,10},{9,11},{10,... | collective-permute-start | bytes 98312 | tf_op jit(solution)/shard_map/ppermute | solution.py:717
  103.7 6.4 %collective-permute-start.23 = (bf16[384,128]{1,0:T(8,128)(2,1)S(1)}, bf16[384,128]{1,0:T(8,128)(2,1)S(1)}, u32[]{:S(2)}, u32[]{:S(2)}) collective-permute-start(bf16[384,128]{1,0:T(8,128)(2,1)S(1)} %get-tuple-element.64), channel_id=1, source_target_pairs={{0,16},{1,17},{2,18},{3,19},{4,20},{5,21},{6,22},{7,23},{8,24},{9,... | collective-permute-start | bytes 294920 | tf_op jit(solution)/shard_map/ppermute | solution.py:717
  105.4 6.9 %collective-permute-start.22 = (bf16[2,2,192,128]{3,2,1,0:T(8,128)(2,1)S(1)}, bf16[2,2,192,128]{3,2,1,0:T(8,128)(2,1)S(1)}, u32[]{:S(2)}, u32[]{:S(2)}) collective-permute-start(bf16[2,2,192,128]{3,2,1,0:T(8,128)(2,1)S(1)} %pad_maximum_fusion.12), channel_id=1, source_target_pairs={{0,2},{1,3},{2,0},{3,1},{4,6},{5,7},{6,4},{7,5},{8,10},{9,11},{10,... | collective-permute-start | bytes 589832 | tf_op jit(solution)/shard_map/ppermute | solution.py:717
  110.0 4.5 %copy-start.5 = (bf16[2,2,2,64,1024]{4,3,2,1,0:T(8,128)(2,1)}, bf16[2,2,2,64,1024]{4,3,2,1,0:T(8,128)(2,1)S(1)}, u32[]{:S(2)}) copy-start(bf16[2,2,2,64,1024]{4,3,2,1,0:T(8,128)(2,1)S(1)} %copy.10) | copy-start | bytes 3145732
  110.0 4.5 %collective-permute-start.21 = (bf16[4,2,64,1024]{3,2,1,0:T(8,128)(2,1)S(1)}, bf16[4,2,64,1024]{3,2,1,0:T(8,128)(2,1)S(1)}, u32[]{:S(2)}, u32[]{:S(2)}) collective-permute-start(bf16[4,2,64,1024]{3,2,1,0:T(8,128)(2,1)S(1)} %bitcast.38), channel_id=1, source_target_pairs={{0,1},{1,0},{2,3},{3,2},{4,5},{5,4},{6,7},{7,6},{8,9},{9,8},{10,11... | collective-permute-start | bytes 3145736 | tf_op jit(solution)/shard_map/ppermute | solution.py:717
  112.4 2.0 %copy-start.6 = (bf16[2048,128]{1,0:T(8,128)(2,1)}, bf16[2048,128]{1,0:T(8,128)(2,1)S(1)}, u32[]{:S(2)}) copy-start(bf16[2048,128]{1,0:T(8,128)(2,1)S(1)} %pad_maximum_fusion.5.rows_same) | copy-start | bytes 1572868
  112.5 2.0 %collective-permute-start.24 = (bf16[2048,128]{1,0:T(8,128)(2,1)S(1)}, bf16[2048,128]{1,0:T(8,128)(2,1)S(1)}, u32[]{:S(2)}, u32[]{:S(2)}) collective-permute-start(bf16[2048,128]{1,0:T(8,128)(2,1)S(1)} %pad_maximum_fusion.5.rows_same), channel_id=1, source_target_pairs={{0,1},{1,0},{2,3},{3,2},{4,5},{5,4},{6,7},{7,6},{8,9},{9,8},{10,11... | collective-permute-start | bytes 1572872 | tf_op jit(solution)/shard_map/ppermute | solution.py:717
  114.4 0.8 copy-start.11
  115.2 1.0 copy-start.10
  120.6 12.0 %collective-permute-start.27 = (bf16[2,384,128]{2,1,0:T(8,128)(2,1)S(1)}, bf16[2,384,128]{2,1,0:T(8,128)(2,1)S(1)}, u32[]{:S(2)}, u32[]{:S(2)}) collective-permute-start(bf16[2,384,128]{2,1,0:T(8,128)(2,1)S(1)} %pad_maximum_fusion.13), channel_id=1, source_target_pairs={{0,6},{1,7},{2,4},{3,5},{4,2},{5,3},{6,0},{7,1},{8,14},{9,15},{10,... | collective-permute-start | bytes 589832 | tf_op jit(solution)/shard_map/ppermute | solution.py:717
  122.1 10.5 %collective-permute-start.26 = (bf16[2,384,128]{2,1,0:T(8,128)(2,1)S(1)}, bf16[2,384,128]{2,1,0:T(8,128)(2,1)S(1)}, u32[]{:S(2)}, u32[]{:S(2)}) collective-permute-start(bf16[2,384,128]{2,1,0:T(8,128)(2,1)S(1)} %pad_maximum_fusion.13), channel_id=1, source_target_pairs={{0,4},{1,5},{2,6},{3,7},{4,0},{5,1},{6,2},{7,3},{8,12},{9,13},{10,... | collective-permute-start | bytes 589832 | tf_op jit(solution)/shard_map/ppermute | solution.py:717
  123.3 9.4 %collective-permute-start.25 = (bf16[2,384,128]{2,1,0:T(8,128)(2,1)S(1)}, bf16[2,384,128]{2,1,0:T(8,128)(2,1)S(1)}, u32[]{:S(2)}, u32[]{:S(2)}) collective-permute-start(bf16[2,384,128]{2,1,0:T(8,128)(2,1)S(1)} %pad_maximum_fusion.13), channel_id=1, source_target_pairs={{0,2},{1,3},{2,0},{3,1},{4,6},{5,7},{6,4},{7,5},{8,10},{9,11},{10,... | collective-permute-start | bytes 589832 | tf_op jit(solution)/shard_map/ppermute | solution.py:717
  132.8 2.4 %collective-permute-start.28 = (bf16[4,2,384,128]{3,2,1,0:T(8,128)(2,1)S(1)}, bf16[4,2,384,128]{3,2,1,0:T(8,128)(2,1)S(1)}, u32[]{:S(2)}, u32[]{:S(2)}) collective-permute-start(bf16[4,2,384,128]{3,2,1,0:T(8,128)(2,1)S(1)} %pad_maximum_fusion.1.same), channel_id=1, source_target_pairs={{0,1},{1,0},{2,3},{3,2},{4,5},{5,4},{6,7},{7,6},{8,9},{9,8},{10,11... | collective-permute-start | bytes 2359304 | tf_op jit(solution)/shard_map/ppermute | solution.py:717
  135.1 1.0 copy-start.2

commit v14 on v13

--- a/solution.py
+++ b/solution.py
@@ -594,7 +594,7 @@
     here = pl.ds(pl.multiple_of(base, rows), rows)
     cosine = cosines[here, :]
     sine = sines[here, :]
-    taken = GROUP // 2
+    taken = GROUP
     limit = lax.broadcasted_iota(jnp.int32, (rows, 1), 0) + base
     limit = jnp.concatenate([limit] * taken, 0)
     for first in range(0, GROUP, taken):
@@ -614,7 +614,7 @@
         column = lax.broadcasted_iota(jnp.int32, scores.shape, 1)
         scores = jnp.where(column <= limit, scores, mask_floor)
         scores = scores - jnp.max(scores, axis=-1, keepdims=True)
-        weights = jnp.exp2(scores * (HEAD_SIZE ** (-0.5) * math.log2(math.e)))
+        weights = jnp.exp(scores * HEAD_SIZE ** (-0.5))
         divisor = jnp.sum(weights, axis=-1, keepdims=True)
         result = (dot(weights.astype(jnp.bfloat16), values[...]) / divisor).astype(jnp.bfloat16)
         for place in range(taken):
@@ -662,7 +662,7 @@
             pltpu.VMEM((seq, HEAD_SIZE), jnp.bfloat16),
             pltpu.VMEM((seq, HEAD_SIZE), jnp.bfloat16),
         ],
-        compiler_params=pltpu.CompilerParams(vmem_limit_bytes=60 << 20),
+        compiler_params=pltpu.CompilerParams(vmem_limit_bytes=32 << 20),
         cost_estimate=pl.CostEstimate(
             flops=12 * heads * rows * QH * seq * HEAD_SIZE,
             bytes_accessed=10 << 20,

time: 140 us -> 136 us (0.971)
  Pallas kernels: 25.6 us -> 23.2 us
  waiting for transfers between devices: 60.6 us -> 62.4 us
  local copies, waits for them, and re-layouts: 4.82 us -> 3.09 us
    pallas_call x2, Pallas kernels: 12.9 us -> 10.5 us  [attend(): pl.pallas_call(partial(attend_kernel, first_head), grid=(heads,), out_sha...]
    ppermute x29, waiting for transfers between devices: 58.4 us -> 60.3 us  [swap(): lax.ppermute(block, ('groups', 'ctx'), [(i, i ^ mask) for i in range(4 *...]
    unnamed x25 -> x17, local copies, waits for them, and re-layouts: 4.56 us -> 2.79 us
  transfers between devices with their start and end apart: 30 -> 30, of which waited for: 15 -> 16; matrix products, arithmetic and copies ran while one was open for 3% -> 2% of each run, Pallas kernels for 8% -> 7%
where the time goes in v14:
time: 136 us
  waiting for transfers between devices  62.4 us (46%)
  starting transfers between devices  43.4 us (32%)
  Pallas kernels  23.2 us (17%)
  local copies, waits for them, and re-layouts  3.09 us (2%)
  other arithmetic  2.81 us (2%)
    ppermute x29, waiting for transfers between devices, swap(): lax.ppermute(block, ('groups', 'ctx'), [(i, i ^ mask) for i in range(4 *...  60.3 us
    ppermute x29, starting transfers between devices, swap(): lax.ppermute(block, ('groups', 'ctx'), [(i, i ^ mask) for i in range(4 *...  37.9 us
    pallas_call x2, Pallas kernels, attend(): pl.pallas_call(partial(attend_kernel, first_head), grid=(heads,), out_sha...  10.5 us
    all_to_all x1, starting transfers between devices, direct_shards(): spread = lax.all_to_all(packed, 'ctx', 0, 0, axis_index_groups=blocks)  5.5 us
    pallas_call x1, Pallas kernels, pack_row(): pl.pallas_call(partial(pack_kernel, sections), out_shape=jax.ShapeDtypeSt...  5.16 us
    pallas_call x1, Pallas kernels, widen(): pl.pallas_call(widen_kernel, out_shape=jax.ShapeDtypeStruct((attended.sha...  2.98 us
    unnamed x17, local copies, waits for them, and re-layouts  2.79 us
  transfers between devices with their start and end apart: 30, of which 16 were waited for; matrix products, arithmetic and copies ran while one was open for 2% of the time, Pallas kernels for 7%

profile of v14, /device:TPU:0, one launch (start us, length us, event | category | flops | bytes accessed | tf_op | source)
XLA Modules:
  0.0 135.8 jit_solution(8828969509455043943)
XLA Ops:
  0.6 5.2 %shard_map.86.refs_0_ = bf16[8,1312,128]{2,1,0:T(8,128)(2,1)} custom-call(bf16[1,2686976]{1,0:T(2,128)(2,1)} %pool.1), custom_call_target="tpu_custom_call" | custom-call | bytes 8388608 | tf_op jit(solution)/shard_map/pallas_call | solution.py:316
  5.8 0.0 copy-start.3
  5.8 5.5 %all-to-all-start = ((bf16[8,1312,128]{2,1,0:T(8,128)(2,1)}), bf16[8,1312,128]{2,1,0:T(8,128)(2,1)}, u32[]{:S(2)}, u32[]{:S(2)}) async-start(bf16[8,1312,128]{2,1,0:T(8,128)(2,1)} %shard_map.86.refs_0_), calls=%async_computation | async-start | bytes 5373952 | tf_op jit(solution)/shard_map/all_to_all | solution.py:756
  11.3 2.2 %collective-permute-start.1 = (s32[2]{0:T(128)S(1)}, s32[2]{0:T(128)S(1)}, u32[]{:S(2)}, u32[]{:S(2)}) collective-permute-start(s32[2]{0:T(128)S(1)} %copy-done.3), channel_id=1, source_target_pairs={{0,16},{1,17},{2,18},{3,19},{4,20},{5,21},{6,22},{7,23},{8,24},{9,... | collective-permute-start | bytes 32 | tf_op jit(solution)/shard_map/ppermute | solution.py:717
  13.6 1.2 copy-done.1
  14.8 0.3 shard_map.87
  15.1 0.1 collective-permute-start.2
  15.1 0.5 copy-done.6
  15.6 0.0 copy-done.7
  15.7 2.6 %collective-permute-start = (bf16[64,1024]{1,0:T(8,128)(2,1)S(1)}, bf16[64,1024]{1,0:T(8,128)(2,1)S(1)}, u32[]{:S(2)}, u32[]{:S(2)}) collective-permute-start(bf16[64,1024]{1,0:T(8,128)(2,1)S(1)} %constant_dynamic-update-slice_fusion), channel_id=1, source_target_pairs={{0,8},{1,9},{2,10},{3,11},{4,12},{5,13},{6,14},{7,15},{8,0},{9,1},... | collective-permute-start | bytes 393224 | tf_op jit(solution)/shard_map/ppermute | solution.py:717
  18.4 1.9 %fusion = (f32[1024,64]{1,0:T(8,128)S(1)}, f32[1024,64]{1,0:T(8,128)S(1)}, f32[1024,64]{1,0:T(8,128)S(1)}) fusion(f32[64]{0:T(128)S(1)} %multiply_power_fusion, f32[1024]{0:T(1024)S(1)} %iota_convert_fusion), kind=kLoop, calls=%fused_computation.16 | loop fusion | flops 131072 | bytes 790784 | tf_op jit(solution)/shard_map/neg | solution.py:733
  20.3 0.3 pad_maximum_fusion.2
  20.6 23.5 %collective-permute-done = bf16[64,1024]{1,0:T(8,128)(2,1)S(1)} collective-permute-done((bf16[64,1024]{1,0:T(8,128)(2,1)S(1)}, bf16[64,1024]{1,0:T(8,128)(2,1)S(1)}, u32[]{:S(2)}, u32[]{:S(2)}) %collective-permute-start) | collective-permute-done | bytes 131104 | tf_op jit(solution)/shard_map/ppermute | solution.py:717
  44.2 2.1 %all-to-all-done.spread = bf16[8,1312,128]{2,1,0:T(8,128)(2,1)} async-done(((bf16[8,1312,128]{2,1,0:T(8,128)(2,1)}), bf16[8,1312,128]{2,1,0:T(8,128)(2,1)}, u32[]{:S(2)}, u32[]{:S(2)}) %all-to-all-start) | async-done | bytes 2687008 | tf_op jit(solution)/shard_map/all_to_all | solution.py:756
  46.3 2.1 %shard_map.88 = (bf16[960,128]{1,0:T(8,128)(2,1)S(1)}, bf16[960,128]{1,0:T(8,128)(2,1)S(1)}, bf16[960,128]{1,0:T(8,128)(2,1)S(1)}, bf16[960,128]{1,0:T(8,128)(2,...) custom-call(s32[2]{0:T(128)S(1)} %copy-done.3, s32[2]{0:T(128)S(1)} %collective-permute-done.1.there, ...), custom_call_target="tpu_custom_call" | custom-call | bytes 3145728 | tf_op jit(solution)/shard_map/pallas_call | solution.py:360
  48.4 1.3 collective-permute-start.3
  49.9 1.7 %collective-permute-start.6 = (bf16[2,64,1024]{2,1,0:T(8,128)(2,1)S(1)}, bf16[2,64,1024]{2,1,0:T(8,128)(2,1)S(1)}, u32[]{:S(2)}, u32[]{:S(2)}) collective-permute-start(bf16[2,64,1024]{2,1,0:T(8,128)(2,1)S(1)} %get-tuple-element.44), channel_id=1, source_target_pairs={{0,2},{1,3},{2,0},{3,1},{4,6},{5,7},{6,4},{7,5},{8,10},{9,11},{10,... | collective-permute-start | bytes 786440 | tf_op jit(solution)/shard_map/ppermute | solution.py:717
  51.5 2.2 %collective-permute-start.7 = (bf16[2,64,1024]{2,1,0:T(8,128)(2,1)S(1)}, bf16[2,64,1024]{2,1,0:T(8,128)(2,1)S(1)}, u32[]{:S(2)}, u32[]{:S(2)}) collective-permute-start(bf16[2,64,1024]{2,1,0:T(8,128)(2,1)S(1)} %get-tuple-element.45), channel_id=1, source_target_pairs={{0,4},{1,5},{2,6},{3,7},{4,0},{5,1},{6,2},{7,3},{8,12},{9,13},{10,... | collective-permute-start | bytes 786440 | tf_op jit(solution)/shard_map/ppermute | solution.py:717
  53.8 1.7 %collective-permute-start.4 = (bf16[960,128]{1,0:T(8,128)(2,1)S(1)}, bf16[960,128]{1,0:T(8,128)(2,1)S(1)}, u32[]{:S(2)}, u32[]{:S(2)}) collective-permute-start(bf16[960,128]{1,0:T(8,128)(2,1)S(1)} %get-tuple-element.39), channel_id=1, source_target_pairs={{0,16},{1,17},{2,18},{3,19},{4,20},{5,21},{6,22},{7,23},{8,24},{9,... | collective-permute-start | bytes 737288 | tf_op jit(solution)/shard_map/ppermute | solution.py:717
  55.4 6.7 %collective-permute-done.3.refs_1_ = bf16[960,128]{1,0:T(8,128)(2,1)S(1)} collective-permute-done((bf16[960,128]{1,0:T(8,128)(2,1)S(1)}, bf16[960,128]{1,0:T(8,128)(2,1)S(1)}, u32[]{:S(2)}, u32[]{:S(2)}) %collective-permute-start.3) | collective-permute-done | bytes 245792 | tf_op jit(solution)/shard_map/ppermute | solution.py:717
  62.2 1.0 collective-permute-start.5
  63.2 8.4 %collective-permute-done.5.refs_3_ = bf16[960,128]{1,0:T(8,128)(2,1)S(1)} collective-permute-done((bf16[960,128]{1,0:T(8,128)(2,1)S(1)}, bf16[960,128]{1,0:T(8,128)(2,1)S(1)}, u32[]{:S(2)}, u32[]{:S(2)}) %collective-permute-start.5) | collective-permute-done | bytes 245792 | tf_op jit(solution)/shard_map/ppermute | solution.py:717
  71.7 1.0 shard_map.89
  72.6 1.1 collective-permute-done.8.refs_3_
  73.8 0.4 shard_map.90
  74.2 5.7 %collective-permute-start.12 = (bf16[2,64,192]{2,1,0:T(8,128)(2,1)S(1)}, bf16[2,64,192]{2,1,0:T(8,128)(2,1)S(1)}, u32[]{:S(2)}, u32[]{:S(2)}) collective-permute-start(bf16[2,64,192]{2,1,0:T(8,128)(2,1)S(1)} %get-tuple-element.50), channel_id=1, source_target_pairs={{0,6},{1,7},{2,4},{3,5},{4,2},{5,3},{6,0},{7,1},{8,14},{9,15},{10,... | collective-permute-start | bytes 147464 | tf_op jit(solution)/shard_map/ppermute | solution.py:717
  79.9 0.6 collective-permute-start.10
  80.6 2.7 %collective-permute-start.13 = (bf16[2,384,128]{2,1,0:T(8,128)(2,1)S(1)}, bf16[2,384,128]{2,1,0:T(8,128)(2,1)S(1)}, u32[]{:S(2)}, u32[]{:S(2)}) collective-permute-start(bf16[2,384,128]{2,1,0:T(8,128)(2,1)S(1)} %get-tuple-element.53), channel_id=1, source_target_pairs={{0,8},{1,9},{2,10},{3,11},{4,12},{5,13},{6,14},{7,15},{8,0},{9,1},... | collective-permute-start | bytes 589832 | tf_op jit(solution)/shard_map/ppermute | solution.py:717
  83.3 2.0 %collective-permute-start.9 = (bf16[2,64,1024]{2,1,0:T(8,128)(2,1)S(1)}, bf16[2,64,1024]{2,1,0:T(8,128)(2,1)S(1)}, u32[]{:S(2)}, u32[]{:S(2)}) collective-permute-start(bf16[2,64,1024]{2,1,0:T(8,128)(2,1)S(1)} %pad_maximum_fusion.7), channel_id=1, source_target_pairs={{0,4},{1,5},{2,6},{3,7},{4,0},{5,1},{6,2},{7,3},{8,12},{9,13},{10,... | collective-permute-start | bytes 786440 | tf_op jit(solution)/shard_map/ppermute | solution.py:717
  85.3 0.3 collective-permute-done.11
  85.7 5.6 %collective-permute-done.13.far = bf16[2,384,128]{2,1,0:T(8,128)(2,1)S(1)} collective-permute-done((bf16[2,384,128]{2,1,0:T(8,128)(2,1)S(1)}, bf16[2,384,128]{2,1,0:T(8,128)(2,1)S(1)}, u32[]{:S(2)}, u32[]{:S(2)}) %collective-permute-start.13) | collective-permute-done | bytes 196640 | tf_op jit(solution)/shard_map/ppermute | solution.py:717
  91.4 0.7 collective-permute-start.17
  92.0 0.5 collective-permute-done.14
  92.6 0.8 collective-permute-done.9
  93.4 0.1 pad_maximum_fusion.4
  93.4 1.3 collective-permute-start.15
  94.7 0.1 slice_bitcast_fusion.1
  94.7 2.0 %collective-permute-start.16 = (bf16[64,128]{1,0:T(8,128)(2,1)S(1)}, bf16[64,128]{1,0:T(8,128)(2,1)S(1)}, u32[]{:S(2)}, u32[]{:S(2)}) collective-permute-start(bf16[64,128]{1,0:T(8,128)(2,1)S(1)} %get-tuple-element.77), channel_id=1, source_target_pairs={{0,8},{1,9},{2,10},{3,11},{4,12},{5,13},{6,14},{7,15},{8,0},{9,1},... | collective-permute-start | bytes 49160 | tf_op jit(solution)/shard_map/ppermute | solution.py:717
  96.8 2.6 %collective-permute-done.16 = bf16[64,128]{1,0:T(8,128)(2,1)S(1)} collective-permute-done((bf16[64,128]{1,0:T(8,128)(2,1)S(1)}, bf16[64,128]{1,0:T(8,128)(2,1)S(1)}, u32[]{:S(2)}, u32[]{:S(2)}) %collective-permute-start.16) | collective-permute-done | bytes 16416 | tf_op jit(solution)/shard_map/ppermute | solution.py:717
  99.4 1.7 %collective-permute-start.20 = (bf16[2,64,128]{2,1,0:T(8,128)(2,1)S(1)}, bf16[2,64,128]{2,1,0:T(8,128)(2,1)S(1)}, u32[]{:S(2)}, u32[]{:S(2)}) collective-permute-start(bf16[2,64,128]{2,1,0:T(8,128)(2,1)S(1)} %pad_maximum_fusion.15), channel_id=1, source_target_pairs={{0,6},{1,7},{2,4},{3,5},{4,2},{5,3},{6,0},{7,1},{8,14},{9,15},{10,... | collective-permute-start | bytes 98312 | tf_op jit(solution)/shard_map/ppermute | solution.py:717
  101.1 0.6 collective-permute-start.19
  101.7 1.2 collective-permute-start.18
  102.9 0.8 shard_map.91
  103.7 1.8 %collective-permute-start.23 = (bf16[384,128]{1,0:T(8,128)(2,1)S(1)}, bf16[384,128]{1,0:T(8,128)(2,1)S(1)}, u32[]{:S(2)}, u32[]{:S(2)}) collective-permute-start(bf16[384,128]{1,0:T(8,128)(2,1)S(1)} %get-tuple-element.64), channel_id=1, source_target_pairs={{0,16},{1,17},{2,18},{3,19},{4,20},{5,21},{6,22},{7,23},{8,24},{9,... | collective-permute-start | bytes 294920 | tf_op jit(solution)/shard_map/ppermute | solution.py:717
  105.4 1.0 collective-permute-start.22
  106.4 3.3 %collective-permute-done.18 = bf16[2,64,128]{2,1,0:T(8,128)(2,1)S(1)} collective-permute-done((bf16[2,64,128]{2,1,0:T(8,128)(2,1)S(1)}, bf16[2,64,128]{2,1,0:T(8,128)(2,1)S(1)}, u32[]{:S(2)}, u32[]{:S(2)}) %collective-permute-start.18) | collective-permute-done | bytes 32800 | tf_op jit(solution)/shard_map/ppermute | solution.py:717
  109.8 0.1 pad_maximum_fusion
  109.9 0.1 copy.10
  110.0 0.1 collective-permute-start.21
  110.1 2.2 %collective-permute-done.22 = bf16[2,2,192,128]{3,2,1,0:T(8,128)(2,1)S(1)} collective-permute-done((bf16[2,2,192,128]{3,2,1,0:T(8,128)(2,1)S(1)}, bf16[2,2,192,128]{3,2,1,0:T(8,128)(2,1)S(1)}, u32[]{:S(2)}, u32[]{:S(2)}) %collective-permute-start.22) | collective-permute-done | bytes 196640 | tf_op jit(solution)/shard_map/ppermute | solution.py:717
  112.4 0.1 collective-permute-start.24
  112.5 1.9 %collective-permute-done.24.rows_other = bf16[2048,128]{1,0:T(8,128)(2,1)S(1)} collective-permute-done((bf16[2048,128]{1,0:T(8,128)(2,1)S(1)}, bf16[2048,128]{1,0:T(8,128)(2,1)S(1)}, u32[]{:S(2)}, u32[]{:S(2)}) %collective-permute-start.24) | collective-permute-done | bytes 524320 | tf_op jit(solution)/shard_map/ppermute | solution.py:717
  114.4 2.9 %shard_map.92.refs_0_ = bf16[64,4096]{1,0:T(8,128)(2,1)} custom-call(bf16[64,4096]{1,0:T(8,128)(2,1)S(1)} %copy-done.5, bf16[4,2,64,1024]{3,2,1,0:T(8,128)(2,1)S(1)} %bitcast.35, bf16[4,2,64,1024]{3,2,1,0:T(8,128)(2,1)S(1)} %collective-permute-done.21.key_other.value_other, bf16[4,2,64,1024]{3,2,1,0:T(8,128)(2,1)S(1)} %bitcast.36, ...), custom_call_target="tpu_custom_call" | custom-call | flops 3221225472 | bytes 10485760 | tf_op jit(solution)/shard_map/pallas_call | solution.py:640
  117.3 1.6 %collective-permute-start.27 = (bf16[2,384,128]{2,1,0:T(8,128)(2,1)S(1)}, bf16[2,384,128]{2,1,0:T(8,128)(2,1)S(1)}, u32[]{:S(2)}, u32[]{:S(2)}) collective-permute-start(bf16[2,384,128]{2,1,0:T(8,128)(2,1)S(1)} %pad_maximum_fusion.13), channel_id=1, source_target_pairs={{0,6},{1,7},{2,4},{3,5},{4,2},{5,3},{6,0},{7,1},{8,14},{9,15},{10,... | collective-permute-start | bytes 589832 | tf_op jit(solution)/shard_map/ppermute | solution.py:717
  118.9 1.1 collective-permute-start.26
  120.0 0.8 collective-permute-start.25
  120.8 7.6 %shard_map.93.attended = bf16[64,4096]{1,0:T(8,128)(2,1)} custom-call(bf16[64,4096]{1,0:T(8,128)(2,1)S(1)} %copy-done.5, bf16[4,2,64,1024]{3,2,1,0:T(8,128)(2,1)S(1)} %bitcast.37, bf16[4,2,64,1024]{3,2,1,0:T(8,128)(2,1)S(1)} %collective-permute-done.21.key_other.value_other, bf16[4,2,64,1024]{3,2,1,0:T(8,128)(2,1)S(1)} %bitcast.38, ...), custom_call_target="tpu_custom_call", output_to_operand_aliasing={{}: (10, {})} | custom-call | flops 9663676416 | bytes 10485760 | tf_op jit(solution)/shard_map/pallas_call | solution.py:640
  128.4 0.8 collective-permute-done.26
  129.2 0.2 collective-permute-done.25
  129.4 0.1 pad_maximum_fusion.1.same
  129.5 0.1 collective-permute-start.28
  129.6 2.3 %collective-permute-done.28.other = bf16[4,2,384,128]{3,2,1,0:T(8,128)(2,1)S(1)} collective-permute-done((bf16[4,2,384,128]{3,2,1,0:T(8,128)(2,1)S(1)}, bf16[4,2,384,128]{3,2,1,0:T(8,128)(2,1)S(1)}, u32[]{:S(2)}, u32[]{:S(2)}) %collective-permute-start.28) | collective-permute-done | bytes 786464 | tf_op jit(solution)/shard_map/ppermute | solution.py:717
  131.8 1.0 copy-done.2
  132.9 3.0 %shard_map.94 = bf16[64,8192]{1,0:T(8,128)(2,1)} custom-call(bf16[64,4096]{1,0:T(8,128)(2,1)S(1)} %copy-done.2, bf16[4,2,384,128]{3,2,1,0:T(8,128)(2,1)S(1)} %pad_maximum_fusion.1.same, bf16[4,2,384,128]{3,2,1,0:T(8,128)(2,1)S(1)} %collective-permute-done.28.other), custom_call_target="tpu_custom_call" | custom-call | flops 134217728 | bytes 4194304 | tf_op jit(solution)/shard_map/pallas_call | solution.py:702
  (47 shorter events, 0.5 us)
Async XLA Ops:
  5.8 5.5 %copy-start.3 = (s32[2]{0:T(128)S(1)}, s32[2]{0:T(128)}, u32[]{:S(2)}) copy-start(s32[2]{0:T(128)} %here.5) | copy-start | bytes 28
  5.8 7.7 %copy-start = (bf16[8,1312,128]{2,1,0:T(8,128)(2,1)S(1)}, bf16[8,1312,128]{2,1,0:T(8,128)(2,1)}, u32[]{:S(2)}) copy-start(bf16[8,1312,128]{2,1,0:T(8,128)(2,1)} %shard_map.86.refs_0_) | copy-start | bytes 8060932
  5.8 40.5 %all-to-all-start = ((bf16[8,1312,128]{2,1,0:T(8,128)(2,1)}), bf16[8,1312,128]{2,1,0:T(8,128)(2,1)}, u32[]{:S(2)}, u32[]{:S(2)}) async-start(bf16[8,1312,128]{2,1,0:T(8,128)(2,1)} %shard_map.86.refs_0_), calls=%async_computation | async-start | bytes 5373952 | tf_op jit(solution)/shard_map/all_to_all | solution.py:756
  11.3 35.0 %collective-permute-start.1 = (s32[2]{0:T(128)S(1)}, s32[2]{0:T(128)S(1)}, u32[]{:S(2)}, u32[]{:S(2)}) collective-permute-start(s32[2]{0:T(128)S(1)} %copy-done.3), channel_id=1, source_target_pairs={{0,16},{1,17},{2,18},{3,19},{4,20},{5,21},{6,22},{7,23},{8,24},{9,... | collective-permute-start | bytes 32 | tf_op jit(solution)/shard_map/ppermute | solution.py:717
  13.6 1.2 copy-start.1
  14.8 0.8 copy-start.6
  14.8 0.9 copy-start.7
  15.1 29.0 %collective-permute-start.2 = (bf16[4,64,1024]{2,1,0:T(8,128)(2,1)S(1)}, bf16[4,64,1024]{2,1,0:T(8,128)(2,1)S(1)}, u32[]{:S(2)}, u32[]{:S(2)}) collective-permute-start(bf16[4,64,1024]{2,1,0:T(8,128)(2,1)S(1)} %get-tuple-element.35), channel_id=1, source_target_pairs={{0,1},{1,0},{2,3},{3,2},{4,5},{5,4},{6,7},{7,6},{8,9},{9,8},{10,11... | collective-permute-start | bytes 1572872 | tf_op jit(solution)/shard_map/ppermute | solution.py:717
  15.7 28.4 %collective-permute-start = (bf16[64,1024]{1,0:T(8,128)(2,1)S(1)}, bf16[64,1024]{1,0:T(8,128)(2,1)S(1)}, u32[]{:S(2)}, u32[]{:S(2)}) collective-permute-start(bf16[64,1024]{1,0:T(8,128)(2,1)S(1)} %constant_dynamic-update-slice_fusion), channel_id=1, source_target_pairs={{0,8},{1,9},{2,10},{3,11},{4,12},{5,13},{6,14},{7,15},{8,0},{9,1},... | collective-permute-start | bytes 393224 | tf_op jit(solution)/shard_map/ppermute | solution.py:717
  18.4 27.9 %copy-start.4 = (s32[16]{0:T(128)S(1)}, s32[16]{0:T(128)}, u32[]{:S(2)}) copy-start(s32[16]{0:T(128)} %owner.5) | copy-start | bytes 196
  48.4 13.8 %collective-permute-start.3 = (bf16[960,128]{1,0:T(8,128)(2,1)S(1)}, bf16[960,128]{1,0:T(8,128)(2,1)S(1)}, u32[]{:S(2)}, u32[]{:S(2)}) collective-permute-start(bf16[960,128]{1,0:T(8,128)(2,1)S(1)} %get-tuple-element.38), channel_id=1, source_target_pairs={{0,8},{1,9},{2,10},{3,11},{4,12},{5,13},{6,14},{7,15},{8,0},{9,1},... | collective-permute-start | bytes 737288 | tf_op jit(solution)/shard_map/ppermute | solution.py:717
  49.9 22.8 %collective-permute-start.6 = (bf16[2,64,1024]{2,1,0:T(8,128)(2,1)S(1)}, bf16[2,64,1024]{2,1,0:T(8,128)(2,1)S(1)}, u32[]{:S(2)}, u32[]{:S(2)}) collective-permute-start(bf16[2,64,1024]{2,1,0:T(8,128)(2,1)S(1)} %get-tuple-element.44), channel_id=1, source_target_pairs={{0,2},{1,3},{2,0},{3,1},{4,6},{5,7},{6,4},{7,5},{8,10},{9,11},{10,... | collective-permute-start | bytes 786440 | tf_op jit(solution)/shard_map/ppermute | solution.py:717
  51.5 21.1 %collective-permute-start.7 = (bf16[2,64,1024]{2,1,0:T(8,128)(2,1)S(1)}, bf16[2,64,1024]{2,1,0:T(8,128)(2,1)S(1)}, u32[]{:S(2)}, u32[]{:S(2)}) collective-permute-start(bf16[2,64,1024]{2,1,0:T(8,128)(2,1)S(1)} %get-tuple-element.45), channel_id=1, source_target_pairs={{0,4},{1,5},{2,6},{3,7},{4,0},{5,1},{6,2},{7,3},{8,12},{9,13},{10,... | collective-permute-start | bytes 786440 | tf_op jit(solution)/shard_map/ppermute | solution.py:717
  53.8 20.0 %collective-permute-start.8 = (bf16[2,64,1024]{2,1,0:T(8,128)(2,1)S(1)}, bf16[2,64,1024]{2,1,0:T(8,128)(2,1)S(1)}, u32[]{:S(2)}, u32[]{:S(2)}) collective-permute-start(bf16[2,64,1024]{2,1,0:T(8,128)(2,1)S(1)} %get-tuple-element.46), channel_id=1, source_target_pairs={{0,6},{1,7},{2,4},{3,5},{4,2},{5,3},{6,0},{7,1},{8,14},{9,15},{10,... | collective-permute-start | bytes 786440 | tf_op jit(solution)/shard_map/ppermute | solution.py:717
  53.8 9.4 %collective-permute-start.4 = (bf16[960,128]{1,0:T(8,128)(2,1)S(1)}, bf16[960,128]{1,0:T(8,128)(2,1)S(1)}, u32[]{:S(2)}, u32[]{:S(2)}) collective-permute-start(bf16[960,128]{1,0:T(8,128)(2,1)S(1)} %get-tuple-element.39), channel_id=1, source_target_pairs={{0,16},{1,17},{2,18},{3,19},{4,20},{5,21},{6,22},{7,23},{8,24},{9,... | collective-permute-start | bytes 737288 | tf_op jit(solution)/shard_map/ppermute | solution.py:717
  62.2 9.5 %collective-permute-start.5 = (bf16[960,128]{1,0:T(8,128)(2,1)S(1)}, bf16[960,128]{1,0:T(8,128)(2,1)S(1)}, u32[]{:S(2)}, u32[]{:S(2)}) collective-permute-start(bf16[960,128]{1,0:T(8,128)(2,1)S(1)} %get-tuple-element.40), channel_id=1, source_target_pairs={{0,24},{1,25},{2,26},{3,27},{4,28},{5,29},{6,30},{7,31},{8,16},{9,... | collective-permute-start | bytes 737288 | tf_op jit(solution)/shard_map/ppermute | solution.py:717
  74.2 11.1 %collective-permute-start.12 = (bf16[2,64,192]{2,1,0:T(8,128)(2,1)S(1)}, bf16[2,64,192]{2,1,0:T(8,128)(2,1)S(1)}, u32[]{:S(2)}, u32[]{:S(2)}) collective-permute-start(bf16[2,64,192]{2,1,0:T(8,128)(2,1)S(1)} %get-tuple-element.50), channel_id=1, source_target_pairs={{0,6},{1,7},{2,4},{3,5},{4,2},{5,3},{6,0},{7,1},{8,14},{9,15},{10,... | collective-permute-start | bytes 147464 | tf_op jit(solution)/shard_map/ppermute | solution.py:717
  79.9 5.7 %collective-permute-start.11 = (bf16[2,64,192]{2,1,0:T(8,128)(2,1)S(1)}, bf16[2,64,192]{2,1,0:T(8,128)(2,1)S(1)}, u32[]{:S(2)}, u32[]{:S(2)}) collective-permute-start(bf16[2,64,192]{2,1,0:T(8,128)(2,1)S(1)} %get-tuple-element.49), channel_id=1, source_target_pairs={{0,4},{1,5},{2,6},{3,7},{4,0},{5,1},{6,2},{7,3},{8,12},{9,13},{10,... | collective-permute-start | bytes 147464 | tf_op jit(solution)/shard_map/ppermute | solution.py:717
  79.9 5.7 %collective-permute-start.10 = (bf16[2,64,192]{2,1,0:T(8,128)(2,1)S(1)}, bf16[2,64,192]{2,1,0:T(8,128)(2,1)S(1)}, u32[]{:S(2)}, u32[]{:S(2)}) collective-permute-start(bf16[2,64,192]{2,1,0:T(8,128)(2,1)S(1)} %get-tuple-element.48), channel_id=1, source_target_pairs={{0,2},{1,3},{2,0},{3,1},{4,6},{5,7},{6,4},{7,5},{8,10},{9,11},{10,... | collective-permute-start | bytes 147464 | tf_op jit(solution)/shard_map/ppermute | solution.py:717
  80.6 10.8 %collective-permute-start.13 = (bf16[2,384,128]{2,1,0:T(8,128)(2,1)S(1)}, bf16[2,384,128]{2,1,0:T(8,128)(2,1)S(1)}, u32[]{:S(2)}, u32[]{:S(2)}) collective-permute-start(bf16[2,384,128]{2,1,0:T(8,128)(2,1)S(1)} %get-tuple-element.53), channel_id=1, source_target_pairs={{0,8},{1,9},{2,10},{3,11},{4,12},{5,13},{6,14},{7,15},{8,0},{9,1},... | collective-permute-start | bytes 589832 | tf_op jit(solution)/shard_map/ppermute | solution.py:717
  83.3 10.1 %collective-permute-start.9 = (bf16[2,64,1024]{2,1,0:T(8,128)(2,1)S(1)}, bf16[2,64,1024]{2,1,0:T(8,128)(2,1)S(1)}, u32[]{:S(2)}, u32[]{:S(2)}) collective-permute-start(bf16[2,64,1024]{2,1,0:T(8,128)(2,1)S(1)} %pad_maximum_fusion.7), channel_id=1, source_target_pairs={{0,4},{1,5},{2,6},{3,7},{4,0},{5,1},{6,2},{7,3},{8,12},{9,13},{10,... | collective-permute-start | bytes 786440 | tf_op jit(solution)/shard_map/ppermute | solution.py:717
  91.4 1.2 collective-permute-start.14
  91.4 5.4 %collective-permute-start.17 = (bf16[2,192,128]{2,1,0:T(8,128)(2,1)S(1)}, bf16[2,192,128]{2,1,0:T(8,128)(2,1)S(1)}, u32[]{:S(2)}, u32[]{:S(2)}) collective-permute-start(bf16[2,192,128]{2,1,0:T(8,128)(2,1)S(1)} %get-tuple-element.57), channel_id=1, source_target_pairs={{0,4},{1,5},{2,6},{3,7},{4,0},{5,1},{6,2},{7,3},{8,12},{9,13},{10,... | collective-permute-start | bytes 294920 | tf_op jit(solution)/shard_map/ppermute | solution.py:717
  93.4 16.4 %collective-permute-start.15 = (bf16[2,2,64,1024]{3,2,1,0:T(8,128)(2,1)S(1)}, bf16[2,2,64,1024]{3,2,1,0:T(8,128)(2,1)S(1)}, u32[]{:S(2)}, u32[]{:S(2)}) collective-permute-start(bf16[2,2,64,1024]{3,2,1,0:T(8,128)(2,1)S(1)} %pad_maximum_fusion.4), channel_id=1, source_target_pairs={{0,2},{1,3},{2,0},{3,1},{4,6},{5,7},{6,4},{7,5},{8,10},{9,11},{10,... | collective-permute-start | bytes 1572872 | tf_op jit(solution)/shard_map/ppermute | solution.py:717
  94.7 4.6 %collective-permute-start.16 = (bf16[64,128]{1,0:T(8,128)(2,1)S(1)}, bf16[64,128]{1,0:T(8,128)(2,1)S(1)}, u32[]{:S(2)}, u32[]{:S(2)}) collective-permute-start(bf16[64,128]{1,0:T(8,128)(2,1)S(1)} %get-tuple-element.77), channel_id=1, source_target_pairs={{0,8},{1,9},{2,10},{3,11},{4,12},{5,13},{6,14},{7,15},{8,0},{9,1},... | collective-permute-start | bytes 49160 | tf_op jit(solution)/shard_map/ppermute | solution.py:717
  99.4 6.0 %collective-permute-start.20 = (bf16[2,64,128]{2,1,0:T(8,128)(2,1)S(1)}, bf16[2,64,128]{2,1,0:T(8,128)(2,1)S(1)}, u32[]{:S(2)}, u32[]{:S(2)}) collective-permute-start(bf16[2,64,128]{2,1,0:T(8,128)(2,1)S(1)} %pad_maximum_fusion.15), channel_id=1, source_target_pairs={{0,6},{1,7},{2,4},{3,5},{4,2},{5,3},{6,0},{7,1},{8,14},{9,15},{10,... | collective-permute-start | bytes 98312 | tf_op jit(solution)/shard_map/ppermute | solution.py:717
  101.1 5.4 %collective-permute-start.19 = (bf16[2,64,128]{2,1,0:T(8,128)(2,1)S(1)}, bf16[2,64,128]{2,1,0:T(8,128)(2,1)S(1)}, u32[]{:S(2)}, u32[]{:S(2)}) collective-permute-start(bf16[2,64,128]{2,1,0:T(8,128)(2,1)S(1)} %pad_maximum_fusion.15), channel_id=1, source_target_pairs={{0,4},{1,5},{2,6},{3,7},{4,0},{5,1},{6,2},{7,3},{8,12},{9,13},{10,... | collective-permute-start | bytes 98312 | tf_op jit(solution)/shard_map/ppermute | solution.py:717
  101.7 8.0 %collective-permute-start.18 = (bf16[2,64,128]{2,1,0:T(8,128)(2,1)S(1)}, bf16[2,64,128]{2,1,0:T(8,128)(2,1)S(1)}, u32[]{:S(2)}, u32[]{:S(2)}) collective-permute-start(bf16[2,64,128]{2,1,0:T(8,128)(2,1)S(1)} %pad_maximum_fusion.15), channel_id=1, source_target_pairs={{0,2},{1,3},{2,0},{3,1},{4,6},{5,7},{6,4},{7,5},{8,10},{9,11},{10,... | collective-permute-start | bytes 98312 | tf_op jit(solution)/shard_map/ppermute | solution.py:717
  103.7 6.4 %collective-permute-start.23 = (bf16[384,128]{1,0:T(8,128)(2,1)S(1)}, bf16[384,128]{1,0:T(8,128)(2,1)S(1)}, u32[]{:S(2)}, u32[]{:S(2)}) collective-permute-start(bf16[384,128]{1,0:T(8,128)(2,1)S(1)} %get-tuple-element.64), channel_id=1, source_target_pairs={{0,16},{1,17},{2,18},{3,19},{4,20},{5,21},{6,22},{7,23},{8,24},{9,... | collective-permute-start | bytes 294920 | tf_op jit(solution)/shard_map/ppermute | solution.py:717
  105.4 6.9 %collective-permute-start.22 = (bf16[2,2,192,128]{3,2,1,0:T(8,128)(2,1)S(1)}, bf16[2,2,192,128]{3,2,1,0:T(8,128)(2,1)S(1)}, u32[]{:S(2)}, u32[]{:S(2)}) collective-permute-start(bf16[2,2,192,128]{3,2,1,0:T(8,128)(2,1)S(1)} %pad_maximum_fusion.12), channel_id=1, source_target_pairs={{0,2},{1,3},{2,0},{3,1},{4,6},{5,7},{6,4},{7,5},{8,10},{9,11},{10,... | collective-permute-start | bytes 589832 | tf_op jit(solution)/shard_map/ppermute | solution.py:717
  109.9 4.5 %copy-start.5 = (bf16[64,4096]{1,0:T(8,128)(2,1)S(1)}, bf16[64,4096]{1,0:T(8,128)(2,1)}, u32[]{:S(2)}) copy-start(bf16[64,4096]{1,0:T(8,128)(2,1)} %query_block.3) | copy-start | bytes 1572868
  110.0 4.4 %collective-permute-start.21 = (bf16[4,2,64,1024]{3,2,1,0:T(8,128)(2,1)S(1)}, bf16[4,2,64,1024]{3,2,1,0:T(8,128)(2,1)S(1)}, u32[]{:S(2)}, u32[]{:S(2)}) collective-permute-start(bf16[4,2,64,1024]{3,2,1,0:T(8,128)(2,1)S(1)} %bitcast.34), channel_id=1, source_target_pairs={{0,1},{1,0},{2,3},{3,2},{4,5},{5,4},{6,7},{7,6},{8,9},{9,8},{10,11... | collective-permute-start | bytes 3145736 | tf_op jit(solution)/shard_map/ppermute | solution.py:717
  112.4 2.0 %collective-permute-start.24 = (bf16[2048,128]{1,0:T(8,128)(2,1)S(1)}, bf16[2048,128]{1,0:T(8,128)(2,1)S(1)}, u32[]{:S(2)}, u32[]{:S(2)}) collective-permute-start(bf16[2048,128]{1,0:T(8,128)(2,1)S(1)} %pad_maximum_fusion.5.rows_same), channel_id=1, source_target_pairs={{0,1},{1,0},{2,3},{3,2},{4,5},{5,4},{6,7},{7,6},{8,9},{9,8},{10,11... | collective-permute-start | bytes 1572872 | tf_op jit(solution)/shard_map/ppermute | solution.py:717
  117.3 11.1 %collective-permute-start.27 = (bf16[2,384,128]{2,1,0:T(8,128)(2,1)S(1)}, bf16[2,384,128]{2,1,0:T(8,128)(2,1)S(1)}, u32[]{:S(2)}, u32[]{:S(2)}) collective-permute-start(bf16[2,384,128]{2,1,0:T(8,128)(2,1)S(1)} %pad_maximum_fusion.13), channel_id=1, source_target_pairs={{0,6},{1,7},{2,4},{3,5},{4,2},{5,3},{6,0},{7,1},{8,14},{9,15},{10,... | collective-permute-start | bytes 589832 | tf_op jit(solution)/shard_map/ppermute | solution.py:717
  118.9 10.3 %collective-permute-start.26 = (bf16[2,384,128]{2,1,0:T(8,128)(2,1)S(1)}, bf16[2,384,128]{2,1,0:T(8,128)(2,1)S(1)}, u32[]{:S(2)}, u32[]{:S(2)}) collective-permute-start(bf16[2,384,128]{2,1,0:T(8,128)(2,1)S(1)} %pad_maximum_fusion.13), channel_id=1, source_target_pairs={{0,4},{1,5},{2,6},{3,7},{4,0},{5,1},{6,2},{7,3},{8,12},{9,13},{10,... | collective-permute-start | bytes 589832 | tf_op jit(solution)/shard_map/ppermute | solution.py:717
  120.0 9.3 %collective-permute-start.25 = (bf16[2,384,128]{2,1,0:T(8,128)(2,1)S(1)}, bf16[2,384,128]{2,1,0:T(8,128)(2,1)S(1)}, u32[]{:S(2)}, u32[]{:S(2)}) collective-permute-start(bf16[2,384,128]{2,1,0:T(8,128)(2,1)S(1)} %pad_maximum_fusion.13), channel_id=1, source_target_pairs={{0,2},{1,3},{2,0},{3,1},{4,6},{5,7},{6,4},{7,5},{8,10},{9,11},{10,... | collective-permute-start | bytes 589832 | tf_op jit(solution)/shard_map/ppermute | solution.py:717
  129.5 2.4 %collective-permute-start.28 = (bf16[4,2,384,128]{3,2,1,0:T(8,128)(2,1)S(1)}, bf16[4,2,384,128]{3,2,1,0:T(8,128)(2,1)S(1)}, u32[]{:S(2)}, u32[]{:S(2)}) collective-permute-start(bf16[4,2,384,128]{3,2,1,0:T(8,128)(2,1)S(1)} %pad_maximum_fusion.1.same), channel_id=1, source_target_pairs={{0,1},{1,0},{2,3},{3,2},{4,5},{5,4},{6,7},{7,6},{8,9},{9,8},{10,11... | collective-permute-start | bytes 2359304 | tf_op jit(solution)/shard_map/ppermute | solution.py:717
  131.8 1.0 copy-start.2

commit v15 on v14

--- a/solution.py
+++ b/solution.py
@@ -764,8 +764,9 @@
     far = swap(after(far, weight), PIECES)
     partial_sums = narrow(weight, dealt)
     back = [swap(block, 2 * j) if j else block for j, block in enumerate(partial_sums)]
+    back = after(back, far)
     back = sum(block.astype(jnp.float32) for block in back)
-    own_rank = swap(after(back[1].astype(jnp.bfloat16), far), 1)
+    own_rank = swap(back[1].astype(jnp.bfloat16), 1)
     own_rank = back[0] + own_rank.astype(jnp.float32)
     own_rank = own_rank.astype(jnp.bfloat16)
     ups = along_z(after(ups, *partial_sums))

time: 136 us -> 138 us (1.015)
  waiting for transfers between devices: 62.4 us -> 74.2 us
  starting transfers between devices: 43.4 us -> 33.3 us
    ppermute x29, waiting for transfers between devices: 60.3 us -> 72.1 us  [swap(): lax.ppermute(block, ('groups', 'ctx'), [(i, i ^ mask) for i in range(4 *...]
    ppermute x29, starting transfers between devices: 37.9 us -> 27.8 us  [swap(): lax.ppermute(block, ('groups', 'ctx'), [(i, i ^ mask) for i in range(4 *...]
  transfers between devices with their start and end apart: 30 -> 30, of which waited for: 16 -> 17; matrix products, arithmetic and copies ran while one was open for 2% -> 2% of each run, Pallas kernels for 7% -> 7%
where the time goes in v15:
time: 138 us; the launch traced here: 137 us
  waiting for transfers between devices  74.2 us (54%)
  starting transfers between devices  33.3 us (24%)
  Pallas kernels  23.2 us (17%)
  local copies, waits for them, and re-layouts  3.05 us (2%)
  other arithmetic  2.8 us (2%)
    ppermute x29, waiting for transfers between devices, swap(): lax.ppermute(block, ('groups', 'ctx'), [(i, i ^ mask) for i in range(4 *...  72.1 us
    ppermute x29, starting transfers between devices, swap(): lax.ppermute(block, ('groups', 'ctx'), [(i, i ^ mask) for i in range(4 *...  27.8 us
    pallas_call x2, Pallas kernels, attend(): pl.pallas_call(partial(attend_kernel, first_head), grid=(heads,), out_sha...  10.5 us
    all_to_all x1, starting transfers between devices, direct_shards(): spread = lax.all_to_all(packed, 'ctx', 0, 0, axis_index_groups=blocks)  5.5 us
    pallas_call x1, Pallas kernels, pack_row(): pl.pallas_call(partial(pack_kernel, sections), out_shape=jax.ShapeDtypeSt...  5.16 us
    pallas_call x1, Pallas kernels, widen(): pl.pallas_call(widen_kernel, out_shape=jax.ShapeDtypeStruct((attended.sha...  2.98 us
    unnamed x17, local copies, waits for them, and re-layouts  2.79 us
  transfers between devices with their start and end apart: 30, of which 17 were waited for; matrix products, arithmetic and copies ran while one was open for 2% of the time, Pallas kernels for 7%

profile of v15, /device:TPU:0, one launch (start us, length us, event | category | flops | bytes accessed | tf_op | source)
XLA Modules:
  0.0 137.5 jit_solution(3067774585233018984)
XLA Ops:
  0.6 5.2 %shard_map.86.refs_0_ = bf16[8,1312,128]{2,1,0:T(8,128)(2,1)} custom-call(bf16[1,2686976]{1,0:T(2,128)(2,1)} %pool.1), custom_call_target="tpu_custom_call" | custom-call | bytes 8388608 | tf_op jit(solution)/shard_map/pallas_call | solution.py:316
  5.8 5.5 %all-to-all-start = ((bf16[8,1312,128]{2,1,0:T(8,128)(2,1)}), bf16[8,1312,128]{2,1,0:T(8,128)(2,1)}, u32[]{:S(2)}, u32[]{:S(2)}) async-start(bf16[8,1312,128]{2,1,0:T(8,128)(2,1)} %shard_map.86.refs_0_), calls=%async_computation | async-start | bytes 5373952 | tf_op jit(solution)/shard_map/all_to_all | solution.py:756
  11.3 2.2 %collective-permute-start.1 = (s32[2]{0:T(128)S(1)}, s32[2]{0:T(128)S(1)}, u32[]{:S(2)}, u32[]{:S(2)}) collective-permute-start(s32[2]{0:T(128)S(1)} %copy-done.3), channel_id=1, source_target_pairs={{0,16},{1,17},{2,18},{3,19},{4,20},{5,21},{6,22},{7,23},{8,24},{9,... | collective-permute-start | bytes 32 | tf_op jit(solution)/shard_map/ppermute | solution.py:717
  13.6 1.2 copy-done.1
  14.8 0.3 shard_map.87
  15.1 0.1 collective-permute-start.2
  15.1 0.5 copy-done.6
  15.6 0.0 copy-done.7
  15.7 2.6 %collective-permute-start = (bf16[64,1024]{1,0:T(8,128)(2,1)S(1)}, bf16[64,1024]{1,0:T(8,128)(2,1)S(1)}, u32[]{:S(2)}, u32[]{:S(2)}) collective-permute-start(bf16[64,1024]{1,0:T(8,128)(2,1)S(1)} %constant_dynamic-update-slice_fusion), channel_id=1, source_target_pairs={{0,8},{1,9},{2,10},{3,11},{4,12},{5,13},{6,14},{7,15},{8,0},{9,1},... | collective-permute-start | bytes 393224 | tf_op jit(solution)/shard_map/ppermute | solution.py:717
  18.4 0.0 copy-start.4
  18.4 1.9 %fusion = (f32[1024,64]{1,0:T(8,128)S(1)}, f32[1024,64]{1,0:T(8,128)S(1)}, f32[1024,64]{1,0:T(8,128)S(1)}) fusion(f32[64]{0:T(128)S(1)} %multiply_power_fusion, f32[1024]{0:T(1024)S(1)} %iota_convert_fusion), kind=kLoop, calls=%fused_computation.16 | loop fusion | flops 131072 | bytes 790784 | tf_op jit(solution)/shard_map/neg | solution.py:733
  20.3 0.3 pad_maximum_fusion.2
  20.6 23.5 %collective-permute-done = bf16[64,1024]{1,0:T(8,128)(2,1)S(1)} collective-permute-done((bf16[64,1024]{1,0:T(8,128)(2,1)S(1)}, bf16[64,1024]{1,0:T(8,128)(2,1)S(1)}, u32[]{:S(2)}, u32[]{:S(2)}) %collective-permute-start) | collective-permute-done | bytes 131104 | tf_op jit(solution)/shard_map/ppermute | solution.py:717
  44.2 2.1 %all-to-all-done.spread = bf16[8,1312,128]{2,1,0:T(8,128)(2,1)} async-done(((bf16[8,1312,128]{2,1,0:T(8,128)(2,1)}), bf16[8,1312,128]{2,1,0:T(8,128)(2,1)}, u32[]{:S(2)}, u32[]{:S(2)}) %all-to-all-start) | async-done | bytes 2687008 | tf_op jit(solution)/shard_map/all_to_all | solution.py:756
  46.3 2.1 %shard_map.88 = (bf16[960,128]{1,0:T(8,128)(2,1)S(1)}, bf16[960,128]{1,0:T(8,128)(2,1)S(1)}, bf16[960,128]{1,0:T(8,128)(2,1)S(1)}, bf16[960,128]{1,0:T(8,128)(2,...) custom-call(s32[2]{0:T(128)S(1)} %copy-done.3, s32[2]{0:T(128)S(1)} %collective-permute-done.1.there, ...), custom_call_target="tpu_custom_call" | custom-call | bytes 3145728 | tf_op jit(solution)/shard_map/pallas_call | solution.py:360
  48.4 1.3 collective-permute-start.3
  49.8 2.1 %collective-permute-start.4 = (bf16[960,128]{1,0:T(8,128)(2,1)S(1)}, bf16[960,128]{1,0:T(8,128)(2,1)S(1)}, u32[]{:S(2)}, u32[]{:S(2)}) collective-permute-start(bf16[960,128]{1,0:T(8,128)(2,1)S(1)} %get-tuple-element.42), channel_id=1, source_target_pairs={{0,16},{1,17},{2,18},{3,19},{4,20},{5,21},{6,22},{7,23},{8,24},{9,... | collective-permute-start | bytes 737288 | tf_op jit(solution)/shard_map/ppermute | solution.py:717
  51.9 1.2 collective-permute-start.5
  53.1 1.5 %collective-permute-start.6 = (bf16[2,64,1024]{2,1,0:T(8,128)(2,1)S(1)}, bf16[2,64,1024]{2,1,0:T(8,128)(2,1)S(1)}, u32[]{:S(2)}, u32[]{:S(2)}) collective-permute-start(bf16[2,64,1024]{2,1,0:T(8,128)(2,1)S(1)} %get-tuple-element.47), channel_id=1, source_target_pairs={{0,2},{1,3},{2,0},{3,1},{4,6},{5,7},{6,4},{7,5},{8,10},{9,11},{10,... | collective-permute-start | bytes 786440 | tf_op jit(solution)/shard_map/ppermute | solution.py:717
  54.7 3.0 %collective-permute-start.7 = (bf16[2,64,1024]{2,1,0:T(8,128)(2,1)S(1)}, bf16[2,64,1024]{2,1,0:T(8,128)(2,1)S(1)}, u32[]{:S(2)}, u32[]{:S(2)}) collective-permute-start(bf16[2,64,1024]{2,1,0:T(8,128)(2,1)S(1)} %get-tuple-element.48), channel_id=1, source_target_pairs={{0,4},{1,5},{2,6},{3,7},{4,0},{5,1},{6,2},{7,3},{8,12},{9,13},{10,... | collective-permute-start | bytes 786440 | tf_op jit(solution)/shard_map/ppermute | solution.py:717
  57.7 11.1 %collective-permute-done.3.refs_1_ = bf16[960,128]{1,0:T(8,128)(2,1)S(1)} collective-permute-done((bf16[960,128]{1,0:T(8,128)(2,1)S(1)}, bf16[960,128]{1,0:T(8,128)(2,1)S(1)}, u32[]{:S(2)}, u32[]{:S(2)}) %collective-permute-start.3) | collective-permute-done | bytes 245792 | tf_op jit(solution)/shard_map/ppermute | solution.py:717
  68.8 5.5 %collective-permute-done.5.refs_3_ = bf16[960,128]{1,0:T(8,128)(2,1)S(1)} collective-permute-done((bf16[960,128]{1,0:T(8,128)(2,1)S(1)}, bf16[960,128]{1,0:T(8,128)(2,1)S(1)}, u32[]{:S(2)}, u32[]{:S(2)}) %collective-permute-start.5) | collective-permute-done | bytes 245792 | tf_op jit(solution)/shard_map/ppermute | solution.py:717
  74.3 1.0 shard_map.89
  75.2 0.1 collective-permute-start.13
  75.3 4.8 %collective-permute-done.8.refs_3_ = bf16[2,64,1024]{2,1,0:T(8,128)(2,1)S(1)} collective-permute-done((bf16[2,64,1024]{2,1,0:T(8,128)(2,1)S(1)}, bf16[2,64,1024]{2,1,0:T(8,128)(2,1)S(1)}, u32[]{:S(2)}, u32[]{:S(2)}) %collective-permute-start.8) | collective-permute-done | bytes 262176 | tf_op jit(solution)/shard_map/ppermute | solution.py:717
  80.1 0.5 shard_map.90
  80.6 0.7 collective-permute-start.10
  81.3 2.8 %collective-permute-start.12 = (bf16[2,64,192]{2,1,0:T(8,128)(2,1)S(1)}, bf16[2,64,192]{2,1,0:T(8,128)(2,1)S(1)}, u32[]{:S(2)}, u32[]{:S(2)}) collective-permute-start(bf16[2,64,192]{2,1,0:T(8,128)(2,1)S(1)} %get-tuple-element.53), channel_id=1, source_target_pairs={{0,6},{1,7},{2,4},{3,5},{4,2},{5,3},{6,0},{7,1},{8,14},{9,15},{10,... | collective-permute-start | bytes 147464 | tf_op jit(solution)/shard_map/ppermute | solution.py:717
  84.1 0.8 collective-permute-done.10
  84.9 2.5 %collective-permute-done.11 = bf16[2,64,192]{2,1,0:T(8,128)(2,1)S(1)} collective-permute-done((bf16[2,64,192]{2,1,0:T(8,128)(2,1)S(1)}, bf16[2,64,192]{2,1,0:T(8,128)(2,1)S(1)}, u32[]{:S(2)}, u32[]{:S(2)}) %collective-permute-start.11) | collective-permute-done | bytes 49184 | tf_op jit(solution)/shard_map/ppermute | solution.py:717
  87.4 2.3 %collective-permute-done.12 = bf16[2,64,192]{2,1,0:T(8,128)(2,1)S(1)} collective-permute-done((bf16[2,64,192]{2,1,0:T(8,128)(2,1)S(1)}, bf16[2,64,192]{2,1,0:T(8,128)(2,1)S(1)}, u32[]{:S(2)}, u32[]{:S(2)}) %collective-permute-start.12) | collective-permute-done | bytes 49184 | tf_op jit(solution)/shard_map/ppermute | solution.py:717
  89.8 0.1 collective-permute-start.14
  89.8 0.1 collective-permute-start.17
  89.9 1.1 collective-permute-done.14
  91.1 3.4 %collective-permute-done.9 = bf16[2,64,1024]{2,1,0:T(8,128)(2,1)S(1)} collective-permute-done((bf16[2,64,1024]{2,1,0:T(8,128)(2,1)S(1)}, bf16[2,64,1024]{2,1,0:T(8,128)(2,1)S(1)}, u32[]{:S(2)}, u32[]{:S(2)}) %collective-permute-start.9) | collective-permute-done | bytes 262176 | tf_op jit(solution)/shard_map/ppermute | solution.py:717
  94.4 0.1 pad_maximum_fusion.4
  94.5 1.5 %collective-permute-start.15 = (bf16[2,2,64,1024]{3,2,1,0:T(8,128)(2,1)S(1)}, bf16[2,2,64,1024]{3,2,1,0:T(8,128)(2,1)S(1)}, u32[]{:S(2)}, u32[]{:S(2)}) collective-permute-start(bf16[2,2,64,1024]{3,2,1,0:T(8,128)(2,1)S(1)} %pad_maximum_fusion.4), channel_id=1, source_target_pairs={{0,2},{1,3},{2,0},{3,1},{4,6},{5,7},{6,4},{7,5},{8,10},{9,11},{10,... | collective-permute-start | bytes 1572872 | tf_op jit(solution)/shard_map/ppermute | solution.py:717
  96.0 0.1 slice_bitcast_fusion.1
  96.1 0.0 collective-permute-start.16
  96.1 0.3 collective-permute-done.17
  96.5 4.3 %collective-permute-done.16 = bf16[64,128]{1,0:T(8,128)(2,1)S(1)} collective-permute-done((bf16[64,128]{1,0:T(8,128)(2,1)S(1)}, bf16[64,128]{1,0:T(8,128)(2,1)S(1)}, u32[]{:S(2)}, u32[]{:S(2)}) %collective-permute-start.16) | collective-permute-done | bytes 16416 | tf_op jit(solution)/shard_map/ppermute | solution.py:717
  100.7 2.0 %collective-permute-start.19 = (bf16[2,64,128]{2,1,0:T(8,128)(2,1)S(1)}, bf16[2,64,128]{2,1,0:T(8,128)(2,1)S(1)}, u32[]{:S(2)}, u32[]{:S(2)}) collective-permute-start(bf16[2,64,128]{2,1,0:T(8,128)(2,1)S(1)} %pad_maximum_fusion.15), channel_id=1, source_target_pairs={{0,4},{1,5},{2,6},{3,7},{4,0},{5,1},{6,2},{7,3},{8,12},{9,13},{10,... | collective-permute-start | bytes 98312 | tf_op jit(solution)/shard_map/ppermute | solution.py:717
  102.8 1.5 %collective-permute-start.18 = (bf16[2,64,128]{2,1,0:T(8,128)(2,1)S(1)}, bf16[2,64,128]{2,1,0:T(8,128)(2,1)S(1)}, u32[]{:S(2)}, u32[]{:S(2)}) collective-permute-start(bf16[2,64,128]{2,1,0:T(8,128)(2,1)S(1)} %pad_maximum_fusion.15), channel_id=1, source_target_pairs={{0,2},{1,3},{2,0},{3,1},{4,6},{5,7},{6,4},{7,5},{8,10},{9,11},{10,... | collective-permute-start | bytes 98312 | tf_op jit(solution)/shard_map/ppermute | solution.py:717
  104.2 0.8 shard_map.91
  105.0 1.1 collective-permute-start.23
  106.1 0.1 collective-permute-start.22
  106.2 4.5 %collective-permute-done.18 = bf16[2,64,128]{2,1,0:T(8,128)(2,1)S(1)} collective-permute-done((bf16[2,64,128]{2,1,0:T(8,128)(2,1)S(1)}, bf16[2,64,128]{2,1,0:T(8,128)(2,1)S(1)}, u32[]{:S(2)}, u32[]{:S(2)}) %collective-permute-start.18) | collective-permute-done | bytes 32800 | tf_op jit(solution)/shard_map/ppermute | solution.py:717
  110.8 0.1 pad_maximum_fusion
  110.9 0.1 copy.10
  111.0 0.1 collective-permute-start.21
  111.1 2.8 %collective-permute-done.22 = bf16[2,2,192,128]{3,2,1,0:T(8,128)(2,1)S(1)} collective-permute-done((bf16[2,2,192,128]{3,2,1,0:T(8,128)(2,1)S(1)}, bf16[2,2,192,128]{3,2,1,0:T(8,128)(2,1)S(1)}, u32[]{:S(2)}, u32[]{:S(2)}) %collective-permute-start.22) | collective-permute-done | bytes 196640 | tf_op jit(solution)/shard_map/ppermute | solution.py:717
  114.1 0.1 collective-permute-start.24
  114.1 1.9 %collective-permute-done.24.rows_other = bf16[2048,128]{1,0:T(8,128)(2,1)S(1)} collective-permute-done((bf16[2048,128]{1,0:T(8,128)(2,1)S(1)}, bf16[2048,128]{1,0:T(8,128)(2,1)S(1)}, u32[]{:S(2)}, u32[]{:S(2)}) %collective-permute-start.24) | collective-permute-done | bytes 524320 | tf_op jit(solution)/shard_map/ppermute | solution.py:717
  116.0 2.9 %shard_map.92.refs_0_ = bf16[64,4096]{1,0:T(8,128)(2,1)} custom-call(bf16[64,4096]{1,0:T(8,128)(2,1)S(1)} %copy-done.5, bf16[4,2,64,1024]{3,2,1,0:T(8,128)(2,1)S(1)} %bitcast.35, bf16[4,2,64,1024]{3,2,1,0:T(8,128)(2,1)S(1)} %collective-permute-done.21.key_other.value_other, bf16[4,2,64,1024]{3,2,1,0:T(8,128)(2,1)S(1)} %bitcast.36, ...), custom_call_target="tpu_custom_call" | custom-call | flops 3221225472 | bytes 10485760 | tf_op jit(solution)/shard_map/pallas_call | solution.py:640
  118.9 0.4 collective-permute-start.27
  119.4 2.5 %collective-permute-start.26 = (bf16[2,384,128]{2,1,0:T(8,128)(2,1)S(1)}, bf16[2,384,128]{2,1,0:T(8,128)(2,1)S(1)}, u32[]{:S(2)}, u32[]{:S(2)}) collective-permute-start(bf16[2,384,128]{2,1,0:T(8,128)(2,1)S(1)} %pad_maximum_fusion.13), channel_id=1, source_target_pairs={{0,4},{1,5},{2,6},{3,7},{4,0},{5,1},{6,2},{7,3},{8,12},{9,13},{10,... | collective-permute-start | bytes 589832 | tf_op jit(solution)/shard_map/ppermute | solution.py:717
  121.8 0.6 collective-permute-start.25
  122.4 7.6 %shard_map.93.attended = bf16[64,4096]{1,0:T(8,128)(2,1)} custom-call(bf16[64,4096]{1,0:T(8,128)(2,1)S(1)} %copy-done.5, bf16[4,2,64,1024]{3,2,1,0:T(8,128)(2,1)S(1)} %bitcast.37, bf16[4,2,64,1024]{3,2,1,0:T(8,128)(2,1)S(1)} %collective-permute-done.21.key_other.value_other, bf16[4,2,64,1024]{3,2,1,0:T(8,128)(2,1)S(1)} %bitcast.38, ...), custom_call_target="tpu_custom_call", output_to_operand_aliasing={{}: (10, {})} | custom-call | flops 9663676416 | bytes 10485760 | tf_op jit(solution)/shard_map/pallas_call | solution.py:640
  130.0 1.0 collective-permute-done.26
  131.0 0.1 pad_maximum_fusion.1.same
  131.1 0.1 collective-permute-start.28
  131.2 2.3 %collective-permute-done.28.other = bf16[4,2,384,128]{3,2,1,0:T(8,128)(2,1)S(1)} collective-permute-done((bf16[4,2,384,128]{3,2,1,0:T(8,128)(2,1)S(1)}, bf16[4,2,384,128]{3,2,1,0:T(8,128)(2,1)S(1)}, u32[]{:S(2)}, u32[]{:S(2)}) %collective-permute-start.28) | collective-permute-done | bytes 786464 | tf_op jit(solution)/shard_map/ppermute | solution.py:717
  133.5 1.0 copy-done.2
  134.5 3.0 %shard_map.94 = bf16[64,8192]{1,0:T(8,128)(2,1)} custom-call(bf16[64,4096]{1,0:T(8,128)(2,1)S(1)} %copy-done.2, bf16[4,2,384,128]{3,2,1,0:T(8,128)(2,1)S(1)} %pad_maximum_fusion.1.same, bf16[4,2,384,128]{3,2,1,0:T(8,128)(2,1)S(1)} %collective-permute-done.28.other), custom_call_target="tpu_custom_call" | custom-call | flops 134217728 | bytes 4194304 | tf_op jit(solution)/shard_map/pallas_call | solution.py:702
  (47 shorter events, 0.5 us)
Async XLA Ops:
  5.8 5.5 %copy-start.3 = (s32[2]{0:T(128)S(1)}, s32[2]{0:T(128)}, u32[]{:S(2)}) copy-start(s32[2]{0:T(128)} %here.5) | copy-start | bytes 28
  5.8 7.7 %copy-start = (bf16[8,1312,128]{2,1,0:T(8,128)(2,1)S(1)}, bf16[8,1312,128]{2,1,0:T(8,128)(2,1)}, u32[]{:S(2)}) copy-start(bf16[8,1312,128]{2,1,0:T(8,128)(2,1)} %shard_map.86.refs_0_) | copy-start | bytes 8060932
  5.8 40.5 %all-to-all-start = ((bf16[8,1312,128]{2,1,0:T(8,128)(2,1)}), bf16[8,1312,128]{2,1,0:T(8,128)(2,1)}, u32[]{:S(2)}, u32[]{:S(2)}) async-start(bf16[8,1312,128]{2,1,0:T(8,128)(2,1)} %shard_map.86.refs_0_), calls=%async_computation | async-start | bytes 5373952 | tf_op jit(solution)/shard_map/all_to_all | solution.py:756
  11.3 35.0 %collective-permute-start.1 = (s32[2]{0:T(128)S(1)}, s32[2]{0:T(128)S(1)}, u32[]{:S(2)}, u32[]{:S(2)}) collective-permute-start(s32[2]{0:T(128)S(1)} %copy-done.3), channel_id=1, source_target_pairs={{0,16},{1,17},{2,18},{3,19},{4,20},{5,21},{6,22},{7,23},{8,24},{9,... | collective-permute-start | bytes 32 | tf_op jit(solution)/shard_map/ppermute | solution.py:717
  13.6 1.2 copy-start.1
  14.8 0.8 copy-start.6
  14.8 0.9 copy-start.7
  15.1 29.0 %collective-permute-start.2 = (bf16[4,64,1024]{2,1,0:T(8,128)(2,1)S(1)}, bf16[4,64,1024]{2,1,0:T(8,128)(2,1)S(1)}, u32[]{:S(2)}, u32[]{:S(2)}) collective-permute-start(bf16[4,64,1024]{2,1,0:T(8,128)(2,1)S(1)} %get-tuple-element.38), channel_id=1, source_target_pairs={{0,1},{1,0},{2,3},{3,2},{4,5},{5,4},{6,7},{7,6},{8,9},{9,8},{10,11... | collective-permute-start | bytes 1572872 | tf_op jit(solution)/shard_map/ppermute | solution.py:717
  15.7 28.4 %collective-permute-start = (bf16[64,1024]{1,0:T(8,128)(2,1)S(1)}, bf16[64,1024]{1,0:T(8,128)(2,1)S(1)}, u32[]{:S(2)}, u32[]{:S(2)}) collective-permute-start(bf16[64,1024]{1,0:T(8,128)(2,1)S(1)} %constant_dynamic-update-slice_fusion), channel_id=1, source_target_pairs={{0,8},{1,9},{2,10},{3,11},{4,12},{5,13},{6,14},{7,15},{8,0},{9,1},... | collective-permute-start | bytes 393224 | tf_op jit(solution)/shard_map/ppermute | solution.py:717
  18.4 27.9 %copy-start.4 = (s32[16]{0:T(128)S(1)}, s32[16]{0:T(128)}, u32[]{:S(2)}) copy-start(s32[16]{0:T(128)} %owner.5) | copy-start | bytes 196
  48.4 20.4 %collective-permute-start.3 = (bf16[960,128]{1,0:T(8,128)(2,1)S(1)}, bf16[960,128]{1,0:T(8,128)(2,1)S(1)}, u32[]{:S(2)}, u32[]{:S(2)}) collective-permute-start(bf16[960,128]{1,0:T(8,128)(2,1)S(1)} %get-tuple-element.41), channel_id=1, source_target_pairs={{0,8},{1,9},{2,10},{3,11},{4,12},{5,13},{6,14},{7,15},{8,0},{9,1},... | collective-permute-start | bytes 737288 | tf_op jit(solution)/shard_map/ppermute | solution.py:717
  49.8 19.0 %collective-permute-start.4 = (bf16[960,128]{1,0:T(8,128)(2,1)S(1)}, bf16[960,128]{1,0:T(8,128)(2,1)S(1)}, u32[]{:S(2)}, u32[]{:S(2)}) collective-permute-start(bf16[960,128]{1,0:T(8,128)(2,1)S(1)} %get-tuple-element.42), channel_id=1, source_target_pairs={{0,16},{1,17},{2,18},{3,19},{4,20},{5,21},{6,22},{7,23},{8,24},{9,... | collective-permute-start | bytes 737288 | tf_op jit(solution)/shard_map/ppermute | solution.py:717
  51.9 22.4 %collective-permute-start.5 = (bf16[960,128]{1,0:T(8,128)(2,1)S(1)}, bf16[960,128]{1,0:T(8,128)(2,1)S(1)}, u32[]{:S(2)}, u32[]{:S(2)}) collective-permute-start(bf16[960,128]{1,0:T(8,128)(2,1)S(1)} %get-tuple-element.43), channel_id=1, source_target_pairs={{0,24},{1,25},{2,26},{3,27},{4,28},{5,29},{6,30},{7,31},{8,16},{9,... | collective-permute-start | bytes 737288 | tf_op jit(solution)/shard_map/ppermute | solution.py:717
  53.1 22.2 %collective-permute-start.6 = (bf16[2,64,1024]{2,1,0:T(8,128)(2,1)S(1)}, bf16[2,64,1024]{2,1,0:T(8,128)(2,1)S(1)}, u32[]{:S(2)}, u32[]{:S(2)}) collective-permute-start(bf16[2,64,1024]{2,1,0:T(8,128)(2,1)S(1)} %get-tuple-element.47), channel_id=1, source_target_pairs={{0,2},{1,3},{2,0},{3,1},{4,6},{5,7},{6,4},{7,5},{8,10},{9,11},{10,... | collective-permute-start | bytes 786440 | tf_op jit(solution)/shard_map/ppermute | solution.py:717
  54.7 20.6 %collective-permute-start.7 = (bf16[2,64,1024]{2,1,0:T(8,128)(2,1)S(1)}, bf16[2,64,1024]{2,1,0:T(8,128)(2,1)S(1)}, u32[]{:S(2)}, u32[]{:S(2)}) collective-permute-start(bf16[2,64,1024]{2,1,0:T(8,128)(2,1)S(1)} %get-tuple-element.48), channel_id=1, source_target_pairs={{0,4},{1,5},{2,6},{3,7},{4,0},{5,1},{6,2},{7,3},{8,12},{9,13},{10,... | collective-permute-start | bytes 786440 | tf_op jit(solution)/shard_map/ppermute | solution.py:717
  68.8 11.3 %collective-permute-start.8 = (bf16[2,64,1024]{2,1,0:T(8,128)(2,1)S(1)}, bf16[2,64,1024]{2,1,0:T(8,128)(2,1)S(1)}, u32[]{:S(2)}, u32[]{:S(2)}) collective-permute-start(bf16[2,64,1024]{2,1,0:T(8,128)(2,1)S(1)} %get-tuple-element.49), channel_id=1, source_target_pairs={{0,6},{1,7},{2,4},{3,5},{4,2},{5,3},{6,0},{7,1},{8,14},{9,15},{10,... | collective-permute-start | bytes 786440 | tf_op jit(solution)/shard_map/ppermute | solution.py:717
  75.2 14.5 %collective-permute-start.13 = (bf16[2,384,128]{2,1,0:T(8,128)(2,1)S(1)}, bf16[2,384,128]{2,1,0:T(8,128)(2,1)S(1)}, u32[]{:S(2)}, u32[]{:S(2)}) collective-permute-start(bf16[2,384,128]{2,1,0:T(8,128)(2,1)S(1)} %get-tuple-element.56), channel_id=1, source_target_pairs={{0,8},{1,9},{2,10},{3,11},{4,12},{5,13},{6,14},{7,15},{8,0},{9,1},... | collective-permute-start | bytes 589832 | tf_op jit(solution)/shard_map/ppermute | solution.py:717
  80.6 4.3 %collective-permute-start.10 = (bf16[2,64,192]{2,1,0:T(8,128)(2,1)S(1)}, bf16[2,64,192]{2,1,0:T(8,128)(2,1)S(1)}, u32[]{:S(2)}, u32[]{:S(2)}) collective-permute-start(bf16[2,64,192]{2,1,0:T(8,128)(2,1)S(1)} %get-tuple-element.51), channel_id=1, source_target_pairs={{0,2},{1,3},{2,0},{3,1},{4,6},{5,7},{6,4},{7,5},{8,10},{9,11},{10,... | collective-permute-start | bytes 147464 | tf_op jit(solution)/shard_map/ppermute | solution.py:717
  81.3 6.1 %collective-permute-start.11 = (bf16[2,64,192]{2,1,0:T(8,128)(2,1)S(1)}, bf16[2,64,192]{2,1,0:T(8,128)(2,1)S(1)}, u32[]{:S(2)}, u32[]{:S(2)}) collective-permute-start(bf16[2,64,192]{2,1,0:T(8,128)(2,1)S(1)} %get-tuple-element.52), channel_id=1, source_target_pairs={{0,4},{1,5},{2,6},{3,7},{4,0},{5,1},{6,2},{7,3},{8,12},{9,13},{10,... | collective-permute-start | bytes 147464 | tf_op jit(solution)/shard_map/ppermute | solution.py:717
  81.3 8.4 %collective-permute-start.12 = (bf16[2,64,192]{2,1,0:T(8,128)(2,1)S(1)}, bf16[2,64,192]{2,1,0:T(8,128)(2,1)S(1)}, u32[]{:S(2)}, u32[]{:S(2)}) collective-permute-start(bf16[2,64,192]{2,1,0:T(8,128)(2,1)S(1)} %get-tuple-element.53), channel_id=1, source_target_pairs={{0,6},{1,7},{2,4},{3,5},{4,2},{5,3},{6,0},{7,1},{8,14},{9,15},{10,... | collective-permute-start | bytes 147464 | tf_op jit(solution)/shard_map/ppermute | solution.py:717
  84.1 10.3 %collective-permute-start.9 = (bf16[2,64,1024]{2,1,0:T(8,128)(2,1)S(1)}, bf16[2,64,1024]{2,1,0:T(8,128)(2,1)S(1)}, u32[]{:S(2)}, u32[]{:S(2)}) collective-permute-start(bf16[2,64,1024]{2,1,0:T(8,128)(2,1)S(1)} %pad_maximum_fusion.7), channel_id=1, source_target_pairs={{0,4},{1,5},{2,6},{3,7},{4,0},{5,1},{6,2},{7,3},{8,12},{9,13},{10,... | collective-permute-start | bytes 786440 | tf_op jit(solution)/shard_map/ppermute | solution.py:717
  89.8 1.3 collective-permute-start.14
  89.8 6.6 %collective-permute-start.17 = (bf16[2,192,128]{2,1,0:T(8,128)(2,1)S(1)}, bf16[2,192,128]{2,1,0:T(8,128)(2,1)S(1)}, u32[]{:S(2)}, u32[]{:S(2)}) collective-permute-start(bf16[2,192,128]{2,1,0:T(8,128)(2,1)S(1)} %get-tuple-element.63), channel_id=1, source_target_pairs={{0,4},{1,5},{2,6},{3,7},{4,0},{5,1},{6,2},{7,3},{8,12},{9,13},{10,... | collective-permute-start | bytes 294920 | tf_op jit(solution)/shard_map/ppermute | solution.py:717
  94.5 16.3 %collective-permute-start.15 = (bf16[2,2,64,1024]{3,2,1,0:T(8,128)(2,1)S(1)}, bf16[2,2,64,1024]{3,2,1,0:T(8,128)(2,1)S(1)}, u32[]{:S(2)}, u32[]{:S(2)}) collective-permute-start(bf16[2,2,64,1024]{3,2,1,0:T(8,128)(2,1)S(1)} %pad_maximum_fusion.4), channel_id=1, source_target_pairs={{0,2},{1,3},{2,0},{3,1},{4,6},{5,7},{6,4},{7,5},{8,10},{9,11},{10,... | collective-permute-start | bytes 1572872 | tf_op jit(solution)/shard_map/ppermute | solution.py:717
  96.1 4.6 %collective-permute-start.16 = (bf16[64,128]{1,0:T(8,128)(2,1)S(1)}, bf16[64,128]{1,0:T(8,128)(2,1)S(1)}, u32[]{:S(2)}, u32[]{:S(2)}) collective-permute-start(bf16[64,128]{1,0:T(8,128)(2,1)S(1)} %get-tuple-element.83), channel_id=1, source_target_pairs={{0,8},{1,9},{2,10},{3,11},{4,12},{5,13},{6,14},{7,15},{8,0},{9,1},... | collective-permute-start | bytes 49160 | tf_op jit(solution)/shard_map/ppermute | solution.py:717
  100.7 5.4 %collective-permute-start.20 = (bf16[2,64,128]{2,1,0:T(8,128)(2,1)S(1)}, bf16[2,64,128]{2,1,0:T(8,128)(2,1)S(1)}, u32[]{:S(2)}, u32[]{:S(2)}) collective-permute-start(bf16[2,64,128]{2,1,0:T(8,128)(2,1)S(1)} %pad_maximum_fusion.15), channel_id=1, source_target_pairs={{0,6},{1,7},{2,4},{3,5},{4,2},{5,3},{6,0},{7,1},{8,14},{9,15},{10,... | collective-permute-start | bytes 98312 | tf_op jit(solution)/shard_map/ppermute | solution.py:717
  100.7 5.5 %collective-permute-start.19 = (bf16[2,64,128]{2,1,0:T(8,128)(2,1)S(1)}, bf16[2,64,128]{2,1,0:T(8,128)(2,1)S(1)}, u32[]{:S(2)}, u32[]{:S(2)}) collective-permute-start(bf16[2,64,128]{2,1,0:T(8,128)(2,1)S(1)} %pad_maximum_fusion.15), channel_id=1, source_target_pairs={{0,4},{1,5},{2,6},{3,7},{4,0},{5,1},{6,2},{7,3},{8,12},{9,13},{10,... | collective-permute-start | bytes 98312 | tf_op jit(solution)/shard_map/ppermute | solution.py:717
  102.8 8.0 %collective-permute-start.18 = (bf16[2,64,128]{2,1,0:T(8,128)(2,1)S(1)}, bf16[2,64,128]{2,1,0:T(8,128)(2,1)S(1)}, u32[]{:S(2)}, u32[]{:S(2)}) collective-permute-start(bf16[2,64,128]{2,1,0:T(8,128)(2,1)S(1)} %pad_maximum_fusion.15), channel_id=1, source_target_pairs={{0,2},{1,3},{2,0},{3,1},{4,6},{5,7},{6,4},{7,5},{8,10},{9,11},{10,... | collective-permute-start | bytes 98312 | tf_op jit(solution)/shard_map/ppermute | solution.py:717
  105.0 6.0 %collective-permute-start.23 = (bf16[384,128]{1,0:T(8,128)(2,1)S(1)}, bf16[384,128]{1,0:T(8,128)(2,1)S(1)}, u32[]{:S(2)}, u32[]{:S(2)}) collective-permute-start(bf16[384,128]{1,0:T(8,128)(2,1)S(1)} %get-tuple-element.70), channel_id=1, source_target_pairs={{0,16},{1,17},{2,18},{3,19},{4,20},{5,21},{6,22},{7,23},{8,24},{9,... | collective-permute-start | bytes 294920 | tf_op jit(solution)/shard_map/ppermute | solution.py:717
  106.1 7.8 %collective-permute-start.22 = (bf16[2,2,192,128]{3,2,1,0:T(8,128)(2,1)S(1)}, bf16[2,2,192,128]{3,2,1,0:T(8,128)(2,1)S(1)}, u32[]{:S(2)}, u32[]{:S(2)}) collective-permute-start(bf16[2,2,192,128]{3,2,1,0:T(8,128)(2,1)S(1)} %pad_maximum_fusion.12), channel_id=1, source_target_pairs={{0,2},{1,3},{2,0},{3,1},{4,6},{5,7},{6,4},{7,5},{8,10},{9,11},{10,... | collective-permute-start | bytes 589832 | tf_op jit(solution)/shard_map/ppermute | solution.py:717
  110.9 5.1 %copy-start.5 = (bf16[64,4096]{1,0:T(8,128)(2,1)S(1)}, bf16[64,4096]{1,0:T(8,128)(2,1)}, u32[]{:S(2)}) copy-start(bf16[64,4096]{1,0:T(8,128)(2,1)} %query_block.3) | copy-start | bytes 1572868
  111.0 5.0 %collective-permute-start.21 = (bf16[4,2,64,1024]{3,2,1,0:T(8,128)(2,1)S(1)}, bf16[4,2,64,1024]{3,2,1,0:T(8,128)(2,1)S(1)}, u32[]{:S(2)}, u32[]{:S(2)}) collective-permute-start(bf16[4,2,64,1024]{3,2,1,0:T(8,128)(2,1)S(1)} %bitcast.34), channel_id=1, source_target_pairs={{0,1},{1,0},{2,3},{3,2},{4,5},{5,4},{6,7},{7,6},{8,9},{9,8},{10,11... | collective-permute-start | bytes 3145736 | tf_op jit(solution)/shard_map/ppermute | solution.py:717
  114.1 2.0 %collective-permute-start.24 = (bf16[2048,128]{1,0:T(8,128)(2,1)S(1)}, bf16[2048,128]{1,0:T(8,128)(2,1)S(1)}, u32[]{:S(2)}, u32[]{:S(2)}) collective-permute-start(bf16[2048,128]{1,0:T(8,128)(2,1)S(1)} %pad_maximum_fusion.5.rows_same), channel_id=1, source_target_pairs={{0,1},{1,0},{2,3},{3,2},{4,5},{5,4},{6,7},{7,6},{8,9},{9,8},{10,11... | collective-permute-start | bytes 1572872 | tf_op jit(solution)/shard_map/ppermute | solution.py:717
  118.9 11.1 %collective-permute-start.27 = (bf16[2,384,128]{2,1,0:T(8,128)(2,1)S(1)}, bf16[2,384,128]{2,1,0:T(8,128)(2,1)S(1)}, u32[]{:S(2)}, u32[]{:S(2)}) collective-permute-start(bf16[2,384,128]{2,1,0:T(8,128)(2,1)S(1)} %pad_maximum_fusion.13), channel_id=1, source_target_pairs={{0,6},{1,7},{2,4},{3,5},{4,2},{5,3},{6,0},{7,1},{8,14},{9,15},{10,... | collective-permute-start | bytes 589832 | tf_op jit(solution)/shard_map/ppermute | solution.py:717
  119.4 11.7 %collective-permute-start.26 = (bf16[2,384,128]{2,1,0:T(8,128)(2,1)S(1)}, bf16[2,384,128]{2,1,0:T(8,128)(2,1)S(1)}, u32[]{:S(2)}, u32[]{:S(2)}) collective-permute-start(bf16[2,384,128]{2,1,0:T(8,128)(2,1)S(1)} %pad_maximum_fusion.13), channel_id=1, source_target_pairs={{0,4},{1,5},{2,6},{3,7},{4,0},{5,1},{6,2},{7,3},{8,12},{9,13},{10,... | collective-permute-start | bytes 589832 | tf_op jit(solution)/shard_map/ppermute | solution.py:717
  121.8 9.2 %collective-permute-start.25 = (bf16[2,384,128]{2,1,0:T(8,128)(2,1)S(1)}, bf16[2,384,128]{2,1,0:T(8,128)(2,1)S(1)}, u32[]{:S(2)}, u32[]{:S(2)}) collective-permute-start(bf16[2,384,128]{2,1,0:T(8,128)(2,1)S(1)} %pad_maximum_fusion.13), channel_id=1, source_target_pairs={{0,2},{1,3},{2,0},{3,1},{4,6},{5,7},{6,4},{7,5},{8,10},{9,11},{10,... | collective-permute-start | bytes 589832 | tf_op jit(solution)/shard_map/ppermute | solution.py:717
  131.1 2.4 %collective-permute-start.28 = (bf16[4,2,384,128]{3,2,1,0:T(8,128)(2,1)S(1)}, bf16[4,2,384,128]{3,2,1,0:T(8,128)(2,1)S(1)}, u32[]{:S(2)}, u32[]{:S(2)}) collective-permute-start(bf16[4,2,384,128]{3,2,1,0:T(8,128)(2,1)S(1)} %pad_maximum_fusion.1.same), channel_id=1, source_target_pairs={{0,1},{1,0},{2,3},{3,2},{4,5},{5,4},{6,7},{7,6},{8,9},{9,8},{10,11... | collective-permute-start | bytes 2359304 | tf_op jit(solution)/shard_map/ppermute | solution.py:717
  133.5 1.0 copy-start.2

commit v16 on v15

--- a/solution.py
+++ b/solution.py
@@ -422,7 +422,8 @@
 
 
 def join_kernel(here, owner, *refs):
-    arrived, (weight, ups), (flat, left, right) = refs[:4], refs[4:6], refs[6:]
+    (across, own, mirror, both), (weight, ups), (flat, left, right) = refs[:4], refs[4:6], refs[6:]
+    arrived = (own, mirror, across, both)
     half = lax.axis_index("ctx") // PIECES
     split = DOWN_ROWS + QUERY_ROWS + KEYVAL_ROWS
 
@@ -467,7 +468,7 @@
         ],
         compiler_params=pltpu.CompilerParams(vmem_limit_bytes=16 << 20),
         cost_estimate=pl.CostEstimate(flops=0, bytes_accessed=96 << 20, transcendentals=0),
-    )(here, owner, *arrived)
+    )(here, owner, arrived[2], arrived[0], arrived[1], arrived[3])
 
 
 def settle_kernel(here, there, owner, near, far, own, across):

time: 138 us -> 136 us (0.986)
  waiting for transfers between devices: 74.2 us -> 67.5 us
  starting transfers between devices: 33.3 us -> 37.8 us
    ppermute x29, waiting for transfers between devices: 72.1 us -> 65.4 us  [swap(): lax.ppermute(block, ('groups', 'ctx'), [(i, i ^ mask) for i in range(4 *...]
    ppermute x29, starting transfers between devices: 27.8 us -> 32.3 us  [swap(): lax.ppermute(block, ('groups', 'ctx'), [(i, i ^ mask) for i in range(4 *...]
where the time goes in v16:
time: 136 us; the launch traced here: 135 us
  waiting for transfers between devices  67.5 us (50%)
  starting transfers between devices  37.8 us (28%)
  Pallas kernels  23.2 us (17%)
  local copies, waits for them, and re-layouts  3.05 us (2%)
  other arithmetic  2.8 us (2%)
    ppermute x29, waiting for transfers between devices, swap(): lax.ppermute(block, ('groups', 'ctx'), [(i, i ^ mask) for i in range(4 *...  65.4 us
    ppermute x29, starting transfers between devices, swap(): lax.ppermute(block, ('groups', 'ctx'), [(i, i ^ mask) for i in range(4 *...  32.3 us
    pallas_call x2, Pallas kernels, attend(): pl.pallas_call(partial(attend_kernel, first_head), grid=(heads,), out_sha...  10.5 us
    all_to_all x1, starting transfers between devices, direct_shards(): spread = lax.all_to_all(packed, 'ctx', 0, 0, axis_index_groups=blocks)  5.5 us
    pallas_call x1, Pallas kernels, pack_row(): pl.pallas_call(partial(pack_kernel, sections), out_shape=jax.ShapeDtypeSt...  5.16 us
    pallas_call x1, Pallas kernels, widen(): pl.pallas_call(widen_kernel, out_shape=jax.ShapeDtypeStruct((attended.sha...  2.98 us
    unnamed x17, local copies, waits for them, and re-layouts  2.79 us
  transfers between devices with their start and end apart: 30, of which 17 were waited for; matrix products, arithmetic and copies ran while one was open for 2% of the time, Pallas kernels for 7%

profile of v16, /device:TPU:0, one launch (start us, length us, event | category | flops | bytes accessed | tf_op | source)
XLA Modules:
  0.0 135.3 jit_solution(6438607313543006662)
XLA Ops:
  0.6 5.2 %shard_map.86.refs_0_ = bf16[8,1312,128]{2,1,0:T(8,128)(2,1)} custom-call(bf16[1,2686976]{1,0:T(2,128)(2,1)} %pool.1), custom_call_target="tpu_custom_call" | custom-call | bytes 8388608 | tf_op jit(solution)/shard_map/pallas_call | solution.py:316
  5.8 5.5 %all-to-all-start = ((bf16[8,1312,128]{2,1,0:T(8,128)(2,1)}), bf16[8,1312,128]{2,1,0:T(8,128)(2,1)}, u32[]{:S(2)}, u32[]{:S(2)}) async-start(bf16[8,1312,128]{2,1,0:T(8,128)(2,1)} %shard_map.86.refs_0_), calls=%async_computation | async-start | bytes 5373952 | tf_op jit(solution)/shard_map/all_to_all | solution.py:757
  11.3 2.2 %collective-permute-start.1 = (s32[2]{0:T(128)S(1)}, s32[2]{0:T(128)S(1)}, u32[]{:S(2)}, u32[]{:S(2)}) collective-permute-start(s32[2]{0:T(128)S(1)} %copy-done.3), channel_id=1, source_target_pairs={{0,16},{1,17},{2,18},{3,19},{4,20},{5,21},{6,22},{7,23},{8,24},{9,... | collective-permute-start | bytes 32 | tf_op jit(solution)/shard_map/ppermute | solution.py:718
  13.6 1.2 copy-done.1
  14.8 0.3 shard_map.87
  15.1 0.1 collective-permute-start.2
  15.1 0.5 copy-done.6
  15.7 2.6 %collective-permute-start = (bf16[64,1024]{1,0:T(8,128)(2,1)S(1)}, bf16[64,1024]{1,0:T(8,128)(2,1)S(1)}, u32[]{:S(2)}, u32[]{:S(2)}) collective-permute-start(bf16[64,1024]{1,0:T(8,128)(2,1)S(1)} %constant_dynamic-update-slice_fusion), channel_id=1, source_target_pairs={{0,8},{1,9},{2,10},{3,11},{4,12},{5,13},{6,14},{7,15},{8,0},{9,1},... | collective-permute-start | bytes 393224 | tf_op jit(solution)/shard_map/ppermute | solution.py:718
  18.4 1.9 %fusion = (f32[1024,64]{1,0:T(8,128)S(1)}, f32[1024,64]{1,0:T(8,128)S(1)}, f32[1024,64]{1,0:T(8,128)S(1)}) fusion(f32[64]{0:T(128)S(1)} %multiply_power_fusion, f32[1024]{0:T(1024)S(1)} %iota_convert_fusion), kind=kLoop, calls=%fused_computation.16 | loop fusion | flops 131072 | bytes 790784 | tf_op jit(solution)/shard_map/neg | solution.py:734
  20.3 0.3 pad_maximum_fusion.2
  20.6 23.5 %collective-permute-done = bf16[64,1024]{1,0:T(8,128)(2,1)S(1)} collective-permute-done((bf16[64,1024]{1,0:T(8,128)(2,1)S(1)}, bf16[64,1024]{1,0:T(8,128)(2,1)S(1)}, u32[]{:S(2)}, u32[]{:S(2)}) %collective-permute-start) | collective-permute-done | bytes 131104 | tf_op jit(solution)/shard_map/ppermute | solution.py:718
  44.2 2.1 %all-to-all-done.spread = bf16[8,1312,128]{2,1,0:T(8,128)(2,1)} async-done(((bf16[8,1312,128]{2,1,0:T(8,128)(2,1)}), bf16[8,1312,128]{2,1,0:T(8,128)(2,1)}, u32[]{:S(2)}, u32[]{:S(2)}) %all-to-all-start) | async-done | bytes 2687008 | tf_op jit(solution)/shard_map/all_to_all | solution.py:757
  46.3 2.1 %shard_map.88 = (bf16[960,128]{1,0:T(8,128)(2,1)S(1)}, bf16[960,128]{1,0:T(8,128)(2,1)S(1)}, bf16[960,128]{1,0:T(8,128)(2,1)S(1)}, bf16[960,128]{1,0:T(8,128)(2,...) custom-call(s32[2]{0:T(128)S(1)} %copy-done.3, s32[2]{0:T(128)S(1)} %collective-permute-done.1.there, ...), custom_call_target="tpu_custom_call" | custom-call | bytes 3145728 | tf_op jit(solution)/shard_map/pallas_call | solution.py:360
  48.4 2.1 %collective-permute-start.3 = (bf16[960,128]{1,0:T(8,128)(2,1)S(1)}, bf16[960,128]{1,0:T(8,128)(2,1)S(1)}, u32[]{:S(2)}, u32[]{:S(2)}) collective-permute-start(bf16[960,128]{1,0:T(8,128)(2,1)S(1)} %get-tuple-element.40), channel_id=1, source_target_pairs={{0,16},{1,17},{2,18},{3,19},{4,20},{5,21},{6,22},{7,23},{8,24},{9,... | collective-permute-start | bytes 737288 | tf_op jit(solution)/shard_map/ppermute | solution.py:718
  50.6 1.3 collective-permute-start.4
  51.9 1.1 collective-permute-start.5
  53.1 1.5 %collective-permute-start.6 = (bf16[2,64,1024]{2,1,0:T(8,128)(2,1)S(1)}, bf16[2,64,1024]{2,1,0:T(8,128)(2,1)S(1)}, u32[]{:S(2)}, u32[]{:S(2)}) collective-permute-start(bf16[2,64,1024]{2,1,0:T(8,128)(2,1)S(1)} %get-tuple-element.47), channel_id=1, source_target_pairs={{0,2},{1,3},{2,0},{3,1},{4,6},{5,7},{6,4},{7,5},{8,10},{9,11},{10,... | collective-permute-start | bytes 786440 | tf_op jit(solution)/shard_map/ppermute | solution.py:718
  54.6 3.0 %collective-permute-start.7 = (bf16[2,64,1024]{2,1,0:T(8,128)(2,1)S(1)}, bf16[2,64,1024]{2,1,0:T(8,128)(2,1)S(1)}, u32[]{:S(2)}, u32[]{:S(2)}) collective-permute-start(bf16[2,64,1024]{2,1,0:T(8,128)(2,1)S(1)} %get-tuple-element.48), channel_id=1, source_target_pairs={{0,4},{1,5},{2,6},{3,7},{4,0},{5,1},{6,2},{7,3},{8,12},{9,13},{10,... | collective-permute-start | bytes 786440 | tf_op jit(solution)/shard_map/ppermute | solution.py:718
  57.7 2.3 %collective-permute-start.8 = (bf16[2,64,1024]{2,1,0:T(8,128)(2,1)S(1)}, bf16[2,64,1024]{2,1,0:T(8,128)(2,1)S(1)}, u32[]{:S(2)}, u32[]{:S(2)}) collective-permute-start(bf16[2,64,1024]{2,1,0:T(8,128)(2,1)S(1)} %get-tuple-element.49), channel_id=1, source_target_pairs={{0,6},{1,7},{2,4},{3,5},{4,2},{5,3},{6,0},{7,1},{8,14},{9,15},{10,... | collective-permute-start | bytes 786440 | tf_op jit(solution)/shard_map/ppermute | solution.py:718
  60.0 11.1 %collective-permute-done.4.refs_2_ = bf16[960,128]{1,0:T(8,128)(2,1)S(1)} collective-permute-done((bf16[960,128]{1,0:T(8,128)(2,1)S(1)}, bf16[960,128]{1,0:T(8,128)(2,1)S(1)}, u32[]{:S(2)}, u32[]{:S(2)}) %collective-permute-start.4) | collective-permute-done | bytes 245792 | tf_op jit(solution)/shard_map/ppermute | solution.py:718
  71.1 3.3 %collective-permute-done.5.refs_3_ = bf16[960,128]{1,0:T(8,128)(2,1)S(1)} collective-permute-done((bf16[960,128]{1,0:T(8,128)(2,1)S(1)}, bf16[960,128]{1,0:T(8,128)(2,1)S(1)}, u32[]{:S(2)}, u32[]{:S(2)}) %collective-permute-start.5) | collective-permute-done | bytes 245792 | tf_op jit(solution)/shard_map/ppermute | solution.py:718
  74.4 1.0 shard_map.89
  75.4 0.1 collective-permute-start.13
  75.5 1.2 collective-permute-done.8.refs_3_
  76.7 0.4 shard_map.90
  77.2 1.6 %collective-permute-start.10 = (bf16[2,64,192]{2,1,0:T(8,128)(2,1)S(1)}, bf16[2,64,192]{2,1,0:T(8,128)(2,1)S(1)}, u32[]{:S(2)}, u32[]{:S(2)}) collective-permute-start(bf16[2,64,192]{2,1,0:T(8,128)(2,1)S(1)} %get-tuple-element.51), channel_id=1, source_target_pairs={{0,2},{1,3},{2,0},{3,1},{4,6},{5,7},{6,4},{7,5},{8,10},{9,11},{10,... | collective-permute-start | bytes 147464 | tf_op jit(solution)/shard_map/ppermute | solution.py:718
  78.7 1.6 %collective-permute-start.11 = (bf16[2,64,192]{2,1,0:T(8,128)(2,1)S(1)}, bf16[2,64,192]{2,1,0:T(8,128)(2,1)S(1)}, u32[]{:S(2)}, u32[]{:S(2)}) collective-permute-start(bf16[2,64,192]{2,1,0:T(8,128)(2,1)S(1)} %get-tuple-element.52), channel_id=1, source_target_pairs={{0,4},{1,5},{2,6},{3,7},{4,0},{5,1},{6,2},{7,3},{8,12},{9,13},{10,... | collective-permute-start | bytes 147464 | tf_op jit(solution)/shard_map/ppermute | solution.py:718
  80.3 0.4 collective-permute-start.12
  80.7 1.7 %collective-permute-start.9 = (bf16[2,64,1024]{2,1,0:T(8,128)(2,1)S(1)}, bf16[2,64,1024]{2,1,0:T(8,128)(2,1)S(1)}, u32[]{:S(2)}, u32[]{:S(2)}) collective-permute-start(bf16[2,64,1024]{2,1,0:T(8,128)(2,1)S(1)} %pad_maximum_fusion.7), channel_id=1, source_target_pairs={{0,4},{1,5},{2,6},{3,7},{4,0},{5,1},{6,2},{7,3},{8,12},{9,13},{10,... | collective-permute-start | bytes 786440 | tf_op jit(solution)/shard_map/ppermute | solution.py:718
  82.4 4.3 %collective-permute-done.11 = bf16[2,64,192]{2,1,0:T(8,128)(2,1)S(1)} collective-permute-done((bf16[2,64,192]{2,1,0:T(8,128)(2,1)S(1)}, bf16[2,64,192]{2,1,0:T(8,128)(2,1)S(1)}, u32[]{:S(2)}, u32[]{:S(2)}) %collective-permute-start.11) | collective-permute-done | bytes 49184 | tf_op jit(solution)/shard_map/ppermute | solution.py:718
  86.8 1.8 %collective-permute-done.12 = bf16[2,64,192]{2,1,0:T(8,128)(2,1)S(1)} collective-permute-done((bf16[2,64,192]{2,1,0:T(8,128)(2,1)S(1)}, bf16[2,64,192]{2,1,0:T(8,128)(2,1)S(1)}, u32[]{:S(2)}, u32[]{:S(2)}) %collective-permute-start.12) | collective-permute-done | bytes 49184 | tf_op jit(solution)/shard_map/ppermute | solution.py:718
  88.6 0.1 collective-permute-start.14
  88.7 0.1 collective-permute-start.17
  88.7 1.1 collective-permute-done.14
  89.9 3.9 %collective-permute-done.9 = bf16[2,64,1024]{2,1,0:T(8,128)(2,1)S(1)} collective-permute-done((bf16[2,64,1024]{2,1,0:T(8,128)(2,1)S(1)}, bf16[2,64,1024]{2,1,0:T(8,128)(2,1)S(1)}, u32[]{:S(2)}, u32[]{:S(2)}) %collective-permute-start.9) | collective-permute-done | bytes 262176 | tf_op jit(solution)/shard_map/ppermute | solution.py:718
  93.8 0.8 collective-permute-start.15
  94.6 0.1 slice_bitcast_fusion.1
  94.7 0.2 collective-permute-start.16
  94.9 0.2 collective-permute-done.17
  95.0 4.3 %collective-permute-done.16 = bf16[64,128]{1,0:T(8,128)(2,1)S(1)} collective-permute-done((bf16[64,128]{1,0:T(8,128)(2,1)S(1)}, bf16[64,128]{1,0:T(8,128)(2,1)S(1)}, u32[]{:S(2)}, u32[]{:S(2)}) %collective-permute-start.16) | collective-permute-done | bytes 16416 | tf_op jit(solution)/shard_map/ppermute | solution.py:718
  99.3 0.3 collective-permute-start.20
  99.6 2.6 %collective-permute-start.19 = (bf16[2,64,128]{2,1,0:T(8,128)(2,1)S(1)}, bf16[2,64,128]{2,1,0:T(8,128)(2,1)S(1)}, u32[]{:S(2)}, u32[]{:S(2)}) collective-permute-start(bf16[2,64,128]{2,1,0:T(8,128)(2,1)S(1)} %pad_maximum_fusion.15), channel_id=1, source_target_pairs={{0,4},{1,5},{2,6},{3,7},{4,0},{5,1},{6,2},{7,3},{8,12},{9,13},{10,... | collective-permute-start | bytes 98312 | tf_op jit(solution)/shard_map/ppermute | solution.py:718
  102.2 0.6 collective-permute-start.18
  102.8 0.8 shard_map.91
  103.6 1.7 %collective-permute-start.23 = (bf16[384,128]{1,0:T(8,128)(2,1)S(1)}, bf16[384,128]{1,0:T(8,128)(2,1)S(1)}, u32[]{:S(2)}, u32[]{:S(2)}) collective-permute-start(bf16[384,128]{1,0:T(8,128)(2,1)S(1)} %get-tuple-element.70), channel_id=1, source_target_pairs={{0,16},{1,17},{2,18},{3,19},{4,20},{5,21},{6,22},{7,23},{8,24},{9,... | collective-permute-start | bytes 294920 | tf_op jit(solution)/shard_map/ppermute | solution.py:718
  105.3 0.6 collective-permute-start.22
  105.9 3.7 %collective-permute-done.18 = bf16[2,64,128]{2,1,0:T(8,128)(2,1)S(1)} collective-permute-done((bf16[2,64,128]{2,1,0:T(8,128)(2,1)S(1)}, bf16[2,64,128]{2,1,0:T(8,128)(2,1)S(1)}, u32[]{:S(2)}, u32[]{:S(2)}) %collective-permute-start.18) | collective-permute-done | bytes 32800 | tf_op jit(solution)/shard_map/ppermute | solution.py:718
  109.7 0.1 pad_maximum_fusion
  109.8 0.1 copy.10
  109.9 0.1 collective-permute-start.21
  110.0 1.8 %collective-permute-done.22 = bf16[2,2,192,128]{3,2,1,0:T(8,128)(2,1)S(1)} collective-permute-done((bf16[2,2,192,128]{3,2,1,0:T(8,128)(2,1)S(1)}, bf16[2,2,192,128]{3,2,1,0:T(8,128)(2,1)S(1)}, u32[]{:S(2)}, u32[]{:S(2)}) %collective-permute-start.22) | collective-permute-done | bytes 196640 | tf_op jit(solution)/shard_map/ppermute | solution.py:718
  111.9 0.1 collective-permute-start.24
  111.9 1.9 %collective-permute-done.24.rows_other = bf16[2048,128]{1,0:T(8,128)(2,1)S(1)} collective-permute-done((bf16[2048,128]{1,0:T(8,128)(2,1)S(1)}, bf16[2048,128]{1,0:T(8,128)(2,1)S(1)}, u32[]{:S(2)}, u32[]{:S(2)}) %collective-permute-start.24) | collective-permute-done | bytes 524320 | tf_op jit(solution)/shard_map/ppermute | solution.py:718
  113.8 2.9 %shard_map.92.refs_0_ = bf16[64,4096]{1,0:T(8,128)(2,1)} custom-call(bf16[64,4096]{1,0:T(8,128)(2,1)S(1)} %copy-done.5, bf16[4,2,64,1024]{3,2,1,0:T(8,128)(2,1)S(1)} %bitcast.35, bf16[4,2,64,1024]{3,2,1,0:T(8,128)(2,1)S(1)} %collective-permute-done.21.key_other.value_other, bf16[4,2,64,1024]{3,2,1,0:T(8,128)(2,1)S(1)} %bitcast.36, ...), custom_call_target="tpu_custom_call" | custom-call | flops 3221225472 | bytes 10485760 | tf_op jit(solution)/shard_map/pallas_call | solution.py:641
  116.7 2.1 %collective-permute-start.26 = (bf16[2,384,128]{2,1,0:T(8,128)(2,1)S(1)}, bf16[2,384,128]{2,1,0:T(8,128)(2,1)S(1)}, u32[]{:S(2)}, u32[]{:S(2)}) collective-permute-start(bf16[2,384,128]{2,1,0:T(8,128)(2,1)S(1)} %pad_maximum_fusion.13), channel_id=1, source_target_pairs={{0,4},{1,5},{2,6},{3,7},{4,0},{5,1},{6,2},{7,3},{8,12},{9,13},{10,... | collective-permute-start | bytes 589832 | tf_op jit(solution)/shard_map/ppermute | solution.py:718
  118.8 1.4 %collective-permute-start.25 = (bf16[2,384,128]{2,1,0:T(8,128)(2,1)S(1)}, bf16[2,384,128]{2,1,0:T(8,128)(2,1)S(1)}, u32[]{:S(2)}, u32[]{:S(2)}) collective-permute-start(bf16[2,384,128]{2,1,0:T(8,128)(2,1)S(1)} %pad_maximum_fusion.13), channel_id=1, source_target_pairs={{0,2},{1,3},{2,0},{3,1},{4,6},{5,7},{6,4},{7,5},{8,10},{9,11},{10,... | collective-permute-start | bytes 589832 | tf_op jit(solution)/shard_map/ppermute | solution.py:718
  120.2 7.6 %shard_map.93.attended = bf16[64,4096]{1,0:T(8,128)(2,1)} custom-call(bf16[64,4096]{1,0:T(8,128)(2,1)S(1)} %copy-done.5, bf16[4,2,64,1024]{3,2,1,0:T(8,128)(2,1)S(1)} %bitcast.37, bf16[4,2,64,1024]{3,2,1,0:T(8,128)(2,1)S(1)} %collective-permute-done.21.key_other.value_other, bf16[4,2,64,1024]{3,2,1,0:T(8,128)(2,1)S(1)} %bitcast.38, ...), custom_call_target="tpu_custom_call", output_to_operand_aliasing={{}: (10, {})} | custom-call | flops 9663676416 | bytes 10485760 | tf_op jit(solution)/shard_map/pallas_call | solution.py:641
  127.8 0.2 collective-permute-done.26
  128.0 0.8 collective-permute-done.25
  128.8 0.1 pad_maximum_fusion.1.same
  128.9 0.1 collective-permute-start.28
  129.0 2.3 %collective-permute-done.28.other = bf16[4,2,384,128]{3,2,1,0:T(8,128)(2,1)S(1)} collective-permute-done((bf16[4,2,384,128]{3,2,1,0:T(8,128)(2,1)S(1)}, bf16[4,2,384,128]{3,2,1,0:T(8,128)(2,1)S(1)}, u32[]{:S(2)}, u32[]{:S(2)}) %collective-permute-start.28) | collective-permute-done | bytes 786464 | tf_op jit(solution)/shard_map/ppermute | solution.py:718
  131.2 1.0 copy-done.2
  132.3 3.0 %shard_map.94 = bf16[64,8192]{1,0:T(8,128)(2,1)} custom-call(bf16[64,4096]{1,0:T(8,128)(2,1)S(1)} %copy-done.2, bf16[4,2,384,128]{3,2,1,0:T(8,128)(2,1)S(1)} %pad_maximum_fusion.1.same, bf16[4,2,384,128]{3,2,1,0:T(8,128)(2,1)S(1)} %collective-permute-done.28.other), custom_call_target="tpu_custom_call" | custom-call | flops 134217728 | bytes 4194304 | tf_op jit(solution)/shard_map/pallas_call | solution.py:703
  (47 shorter events, 0.6 us)
Async XLA Ops:
  5.8 5.5 %copy-start.3 = (s32[2]{0:T(128)S(1)}, s32[2]{0:T(128)}, u32[]{:S(2)}) copy-start(s32[2]{0:T(128)} %here.5) | copy-start | bytes 28
  5.8 7.7 %copy-start = (bf16[8,1312,128]{2,1,0:T(8,128)(2,1)S(1)}, bf16[8,1312,128]{2,1,0:T(8,128)(2,1)}, u32[]{:S(2)}) copy-start(bf16[8,1312,128]{2,1,0:T(8,128)(2,1)} %shard_map.86.refs_0_) | copy-start | bytes 8060932
  5.8 40.5 %all-to-all-start = ((bf16[8,1312,128]{2,1,0:T(8,128)(2,1)}), bf16[8,1312,128]{2,1,0:T(8,128)(2,1)}, u32[]{:S(2)}, u32[]{:S(2)}) async-start(bf16[8,1312,128]{2,1,0:T(8,128)(2,1)} %shard_map.86.refs_0_), calls=%async_computation | async-start | bytes 5373952 | tf_op jit(solution)/shard_map/all_to_all | solution.py:757
  11.3 35.0 %collective-permute-start.1 = (s32[2]{0:T(128)S(1)}, s32[2]{0:T(128)S(1)}, u32[]{:S(2)}, u32[]{:S(2)}) collective-permute-start(s32[2]{0:T(128)S(1)} %copy-done.3), channel_id=1, source_target_pairs={{0,16},{1,17},{2,18},{3,19},{4,20},{5,21},{6,22},{7,23},{8,24},{9,... | collective-permute-start | bytes 32 | tf_op jit(solution)/shard_map/ppermute | solution.py:718
  13.6 1.2 copy-start.1
  14.8 0.8 copy-start.6
  14.8 0.9 copy-start.7
  15.1 29.0 %collective-permute-start.2 = (bf16[4,64,1024]{2,1,0:T(8,128)(2,1)S(1)}, bf16[4,64,1024]{2,1,0:T(8,128)(2,1)S(1)}, u32[]{:S(2)}, u32[]{:S(2)}) collective-permute-start(bf16[4,64,1024]{2,1,0:T(8,128)(2,1)S(1)} %get-tuple-element.38), channel_id=1, source_target_pairs={{0,1},{1,0},{2,3},{3,2},{4,5},{5,4},{6,7},{7,6},{8,9},{9,8},{10,11... | collective-permute-start | bytes 1572872 | tf_op jit(solution)/shard_map/ppermute | solution.py:718
  15.7 28.4 %collective-permute-start = (bf16[64,1024]{1,0:T(8,128)(2,1)S(1)}, bf16[64,1024]{1,0:T(8,128)(2,1)S(1)}, u32[]{:S(2)}, u32[]{:S(2)}) collective-permute-start(bf16[64,1024]{1,0:T(8,128)(2,1)S(1)} %constant_dynamic-update-slice_fusion), channel_id=1, source_target_pairs={{0,8},{1,9},{2,10},{3,11},{4,12},{5,13},{6,14},{7,15},{8,0},{9,1},... | collective-permute-start | bytes 393224 | tf_op jit(solution)/shard_map/ppermute | solution.py:718
  18.4 27.9 %copy-start.4 = (s32[16]{0:T(128)S(1)}, s32[16]{0:T(128)}, u32[]{:S(2)}) copy-start(s32[16]{0:T(128)} %owner.5) | copy-start | bytes 196
  48.4 9.2 %collective-permute-start.3 = (bf16[960,128]{1,0:T(8,128)(2,1)S(1)}, bf16[960,128]{1,0:T(8,128)(2,1)S(1)}, u32[]{:S(2)}, u32[]{:S(2)}) collective-permute-start(bf16[960,128]{1,0:T(8,128)(2,1)S(1)} %get-tuple-element.40), channel_id=1, source_target_pairs={{0,16},{1,17},{2,18},{3,19},{4,20},{5,21},{6,22},{7,23},{8,24},{9,... | collective-permute-start | bytes 737288 | tf_op jit(solution)/shard_map/ppermute | solution.py:718
  50.6 20.5 %collective-permute-start.4 = (bf16[960,128]{1,0:T(8,128)(2,1)S(1)}, bf16[960,128]{1,0:T(8,128)(2,1)S(1)}, u32[]{:S(2)}, u32[]{:S(2)}) collective-permute-start(bf16[960,128]{1,0:T(8,128)(2,1)S(1)} %get-tuple-element.42), channel_id=1, source_target_pairs={{0,8},{1,9},{2,10},{3,11},{4,12},{5,13},{6,14},{7,15},{8,0},{9,1},... | collective-permute-start | bytes 737288 | tf_op jit(solution)/shard_map/ppermute | solution.py:718
  51.9 22.5 %collective-permute-start.5 = (bf16[960,128]{1,0:T(8,128)(2,1)S(1)}, bf16[960,128]{1,0:T(8,128)(2,1)S(1)}, u32[]{:S(2)}, u32[]{:S(2)}) collective-permute-start(bf16[960,128]{1,0:T(8,128)(2,1)S(1)} %get-tuple-element.43), channel_id=1, source_target_pairs={{0,24},{1,25},{2,26},{3,27},{4,28},{5,29},{6,30},{7,31},{8,16},{9,... | collective-permute-start | bytes 737288 | tf_op jit(solution)/shard_map/ppermute | solution.py:718
  53.1 22.4 %collective-permute-start.6 = (bf16[2,64,1024]{2,1,0:T(8,128)(2,1)S(1)}, bf16[2,64,1024]{2,1,0:T(8,128)(2,1)S(1)}, u32[]{:S(2)}, u32[]{:S(2)}) collective-permute-start(bf16[2,64,1024]{2,1,0:T(8,128)(2,1)S(1)} %get-tuple-element.47), channel_id=1, source_target_pairs={{0,2},{1,3},{2,0},{3,1},{4,6},{5,7},{6,4},{7,5},{8,10},{9,11},{10,... | collective-permute-start | bytes 786440 | tf_op jit(solution)/shard_map/ppermute | solution.py:718
  54.6 20.8 %collective-permute-start.7 = (bf16[2,64,1024]{2,1,0:T(8,128)(2,1)S(1)}, bf16[2,64,1024]{2,1,0:T(8,128)(2,1)S(1)}, u32[]{:S(2)}, u32[]{:S(2)}) collective-permute-start(bf16[2,64,1024]{2,1,0:T(8,128)(2,1)S(1)} %get-tuple-element.48), channel_id=1, source_target_pairs={{0,4},{1,5},{2,6},{3,7},{4,0},{5,1},{6,2},{7,3},{8,12},{9,13},{10,... | collective-permute-start | bytes 786440 | tf_op jit(solution)/shard_map/ppermute | solution.py:718
  57.7 19.0 %collective-permute-start.8 = (bf16[2,64,1024]{2,1,0:T(8,128)(2,1)S(1)}, bf16[2,64,1024]{2,1,0:T(8,128)(2,1)S(1)}, u32[]{:S(2)}, u32[]{:S(2)}) collective-permute-start(bf16[2,64,1024]{2,1,0:T(8,128)(2,1)S(1)} %get-tuple-element.49), channel_id=1, source_target_pairs={{0,6},{1,7},{2,4},{3,5},{4,2},{5,3},{6,0},{7,1},{8,14},{9,15},{10,... | collective-permute-start | bytes 786440 | tf_op jit(solution)/shard_map/ppermute | solution.py:718
  75.4 13.1 %collective-permute-start.13 = (bf16[2,384,128]{2,1,0:T(8,128)(2,1)S(1)}, bf16[2,384,128]{2,1,0:T(8,128)(2,1)S(1)}, u32[]{:S(2)}, u32[]{:S(2)}) collective-permute-start(bf16[2,384,128]{2,1,0:T(8,128)(2,1)S(1)} %get-tuple-element.56), channel_id=1, source_target_pairs={{0,8},{1,9},{2,10},{3,11},{4,12},{5,13},{6,14},{7,15},{8,0},{9,1},... | collective-permute-start | bytes 589832 | tf_op jit(solution)/shard_map/ppermute | solution.py:718
  77.2 5.3 %collective-permute-start.10 = (bf16[2,64,192]{2,1,0:T(8,128)(2,1)S(1)}, bf16[2,64,192]{2,1,0:T(8,128)(2,1)S(1)}, u32[]{:S(2)}, u32[]{:S(2)}) collective-permute-start(bf16[2,64,192]{2,1,0:T(8,128)(2,1)S(1)} %get-tuple-element.51), channel_id=1, source_target_pairs={{0,2},{1,3},{2,0},{3,1},{4,6},{5,7},{6,4},{7,5},{8,10},{9,11},{10,... | collective-permute-start | bytes 147464 | tf_op jit(solution)/shard_map/ppermute | solution.py:718
  78.7 8.1 %collective-permute-start.11 = (bf16[2,64,192]{2,1,0:T(8,128)(2,1)S(1)}, bf16[2,64,192]{2,1,0:T(8,128)(2,1)S(1)}, u32[]{:S(2)}, u32[]{:S(2)}) collective-permute-start(bf16[2,64,192]{2,1,0:T(8,128)(2,1)S(1)} %get-tuple-element.52), channel_id=1, source_target_pairs={{0,4},{1,5},{2,6},{3,7},{4,0},{5,1},{6,2},{7,3},{8,12},{9,13},{10,... | collective-permute-start | bytes 147464 | tf_op jit(solution)/shard_map/ppermute | solution.py:718
  80.3 8.2 %collective-permute-start.12 = (bf16[2,64,192]{2,1,0:T(8,128)(2,1)S(1)}, bf16[2,64,192]{2,1,0:T(8,128)(2,1)S(1)}, u32[]{:S(2)}, u32[]{:S(2)}) collective-permute-start(bf16[2,64,192]{2,1,0:T(8,128)(2,1)S(1)} %get-tuple-element.53), channel_id=1, source_target_pairs={{0,6},{1,7},{2,4},{3,5},{4,2},{5,3},{6,0},{7,1},{8,14},{9,15},{10,... | collective-permute-start | bytes 147464 | tf_op jit(solution)/shard_map/ppermute | solution.py:718
  80.7 13.1 %collective-permute-start.9 = (bf16[2,64,1024]{2,1,0:T(8,128)(2,1)S(1)}, bf16[2,64,1024]{2,1,0:T(8,128)(2,1)S(1)}, u32[]{:S(2)}, u32[]{:S(2)}) collective-permute-start(bf16[2,64,1024]{2,1,0:T(8,128)(2,1)S(1)} %pad_maximum_fusion.7), channel_id=1, source_target_pairs={{0,4},{1,5},{2,6},{3,7},{4,0},{5,1},{6,2},{7,3},{8,12},{9,13},{10,... | collective-permute-start | bytes 786440 | tf_op jit(solution)/shard_map/ppermute | solution.py:718
  88.6 1.3 collective-permute-start.14
  88.7 6.4 %collective-permute-start.17 = (bf16[2,192,128]{2,1,0:T(8,128)(2,1)S(1)}, bf16[2,192,128]{2,1,0:T(8,128)(2,1)S(1)}, u32[]{:S(2)}, u32[]{:S(2)}) collective-permute-start(bf16[2,192,128]{2,1,0:T(8,128)(2,1)S(1)} %get-tuple-element.63), channel_id=1, source_target_pairs={{0,4},{1,5},{2,6},{3,7},{4,0},{5,1},{6,2},{7,3},{8,12},{9,13},{10,... | collective-permute-start | bytes 294920 | tf_op jit(solution)/shard_map/ppermute | solution.py:718
  93.8 15.8 %collective-permute-start.15 = (bf16[2,2,64,1024]{3,2,1,0:T(8,128)(2,1)S(1)}, bf16[2,2,64,1024]{3,2,1,0:T(8,128)(2,1)S(1)}, u32[]{:S(2)}, u32[]{:S(2)}) collective-permute-start(bf16[2,2,64,1024]{3,2,1,0:T(8,128)(2,1)S(1)} %pad_maximum_fusion.4), channel_id=1, source_target_pairs={{0,2},{1,3},{2,0},{3,1},{4,6},{5,7},{6,4},{7,5},{8,10},{9,11},{10,... | collective-permute-start | bytes 1572872 | tf_op jit(solution)/shard_map/ppermute | solution.py:718
  94.7 4.6 %collective-permute-start.16 = (bf16[64,128]{1,0:T(8,128)(2,1)S(1)}, bf16[64,128]{1,0:T(8,128)(2,1)S(1)}, u32[]{:S(2)}, u32[]{:S(2)}) collective-permute-start(bf16[64,128]{1,0:T(8,128)(2,1)S(1)} %get-tuple-element.83), channel_id=1, source_target_pairs={{0,8},{1,9},{2,10},{3,11},{4,12},{5,13},{6,14},{7,15},{8,0},{9,1},... | collective-permute-start | bytes 49160 | tf_op jit(solution)/shard_map/ppermute | solution.py:718
  99.3 6.0 %collective-permute-start.20 = (bf16[2,64,128]{2,1,0:T(8,128)(2,1)S(1)}, bf16[2,64,128]{2,1,0:T(8,128)(2,1)S(1)}, u32[]{:S(2)}, u32[]{:S(2)}) collective-permute-start(bf16[2,64,128]{2,1,0:T(8,128)(2,1)S(1)} %pad_maximum_fusion.15), channel_id=1, source_target_pairs={{0,6},{1,7},{2,4},{3,5},{4,2},{5,3},{6,0},{7,1},{8,14},{9,15},{10,... | collective-permute-start | bytes 98312 | tf_op jit(solution)/shard_map/ppermute | solution.py:718
  99.6 6.3 %collective-permute-start.19 = (bf16[2,64,128]{2,1,0:T(8,128)(2,1)S(1)}, bf16[2,64,128]{2,1,0:T(8,128)(2,1)S(1)}, u32[]{:S(2)}, u32[]{:S(2)}) collective-permute-start(bf16[2,64,128]{2,1,0:T(8,128)(2,1)S(1)} %pad_maximum_fusion.15), channel_id=1, source_target_pairs={{0,4},{1,5},{2,6},{3,7},{4,0},{5,1},{6,2},{7,3},{8,12},{9,13},{10,... | collective-permute-start | bytes 98312 | tf_op jit(solution)/shard_map/ppermute | solution.py:718
  102.2 7.4 %collective-permute-start.18 = (bf16[2,64,128]{2,1,0:T(8,128)(2,1)S(1)}, bf16[2,64,128]{2,1,0:T(8,128)(2,1)S(1)}, u32[]{:S(2)}, u32[]{:S(2)}) collective-permute-start(bf16[2,64,128]{2,1,0:T(8,128)(2,1)S(1)} %pad_maximum_fusion.15), channel_id=1, source_target_pairs={{0,2},{1,3},{2,0},{3,1},{4,6},{5,7},{6,4},{7,5},{8,10},{9,11},{10,... | collective-permute-start | bytes 98312 | tf_op jit(solution)/shard_map/ppermute | solution.py:718
  103.6 6.3 %collective-permute-start.23 = (bf16[384,128]{1,0:T(8,128)(2,1)S(1)}, bf16[384,128]{1,0:T(8,128)(2,1)S(1)}, u32[]{:S(2)}, u32[]{:S(2)}) collective-permute-start(bf16[384,128]{1,0:T(8,128)(2,1)S(1)} %get-tuple-element.70), channel_id=1, source_target_pairs={{0,16},{1,17},{2,18},{3,19},{4,20},{5,21},{6,22},{7,23},{8,24},{9,... | collective-permute-start | bytes 294920 | tf_op jit(solution)/shard_map/ppermute | solution.py:718
  105.3 6.4 %collective-permute-start.22 = (bf16[2,2,192,128]{3,2,1,0:T(8,128)(2,1)S(1)}, bf16[2,2,192,128]{3,2,1,0:T(8,128)(2,1)S(1)}, u32[]{:S(2)}, u32[]{:S(2)}) collective-permute-start(bf16[2,2,192,128]{3,2,1,0:T(8,128)(2,1)S(1)} %pad_maximum_fusion.12), channel_id=1, source_target_pairs={{0,2},{1,3},{2,0},{3,1},{4,6},{5,7},{6,4},{7,5},{8,10},{9,11},{10,... | collective-permute-start | bytes 589832 | tf_op jit(solution)/shard_map/ppermute | solution.py:718
  109.8 4.1 %copy-start.5 = (bf16[64,4096]{1,0:T(8,128)(2,1)S(1)}, bf16[64,4096]{1,0:T(8,128)(2,1)}, u32[]{:S(2)}) copy-start(bf16[64,4096]{1,0:T(8,128)(2,1)} %query_block.3) | copy-start | bytes 1572868
  109.9 4.0 %collective-permute-start.21 = (bf16[4,2,64,1024]{3,2,1,0:T(8,128)(2,1)S(1)}, bf16[4,2,64,1024]{3,2,1,0:T(8,128)(2,1)S(1)}, u32[]{:S(2)}, u32[]{:S(2)}) collective-permute-start(bf16[4,2,64,1024]{3,2,1,0:T(8,128)(2,1)S(1)} %bitcast.34), channel_id=1, source_target_pairs={{0,1},{1,0},{2,3},{3,2},{4,5},{5,4},{6,7},{7,6},{8,9},{9,8},{10,11... | collective-permute-start | bytes 3145736 | tf_op jit(solution)/shard_map/ppermute | solution.py:718
  111.9 2.0 %collective-permute-start.24 = (bf16[2048,128]{1,0:T(8,128)(2,1)S(1)}, bf16[2048,128]{1,0:T(8,128)(2,1)S(1)}, u32[]{:S(2)}, u32[]{:S(2)}) collective-permute-start(bf16[2048,128]{1,0:T(8,128)(2,1)S(1)} %pad_maximum_fusion.5.rows_same), channel_id=1, source_target_pairs={{0,1},{1,0},{2,3},{3,2},{4,5},{5,4},{6,7},{7,6},{8,9},{9,8},{10,11... | collective-permute-start | bytes 1572872 | tf_op jit(solution)/shard_map/ppermute | solution.py:718
  116.7 11.1 %collective-permute-start.27 = (bf16[2,384,128]{2,1,0:T(8,128)(2,1)S(1)}, bf16[2,384,128]{2,1,0:T(8,128)(2,1)S(1)}, u32[]{:S(2)}, u32[]{:S(2)}) collective-permute-start(bf16[2,384,128]{2,1,0:T(8,128)(2,1)S(1)} %pad_maximum_fusion.13), channel_id=1, source_target_pairs={{0,6},{1,7},{2,4},{3,5},{4,2},{5,3},{6,0},{7,1},{8,14},{9,15},{10,... | collective-permute-start | bytes 589832 | tf_op jit(solution)/shard_map/ppermute | solution.py:718
  116.7 11.3 %collective-permute-start.26 = (bf16[2,384,128]{2,1,0:T(8,128)(2,1)S(1)}, bf16[2,384,128]{2,1,0:T(8,128)(2,1)S(1)}, u32[]{:S(2)}, u32[]{:S(2)}) collective-permute-start(bf16[2,384,128]{2,1,0:T(8,128)(2,1)S(1)} %pad_maximum_fusion.13), channel_id=1, source_target_pairs={{0,4},{1,5},{2,6},{3,7},{4,0},{5,1},{6,2},{7,3},{8,12},{9,13},{10,... | collective-permute-start | bytes 589832 | tf_op jit(solution)/shard_map/ppermute | solution.py:718
  118.8 9.9 %collective-permute-start.25 = (bf16[2,384,128]{2,1,0:T(8,128)(2,1)S(1)}, bf16[2,384,128]{2,1,0:T(8,128)(2,1)S(1)}, u32[]{:S(2)}, u32[]{:S(2)}) collective-permute-start(bf16[2,384,128]{2,1,0:T(8,128)(2,1)S(1)} %pad_maximum_fusion.13), channel_id=1, source_target_pairs={{0,2},{1,3},{2,0},{3,1},{4,6},{5,7},{6,4},{7,5},{8,10},{9,11},{10,... | collective-permute-start | bytes 589832 | tf_op jit(solution)/shard_map/ppermute | solution.py:718
  128.9 2.4 %collective-permute-start.28 = (bf16[4,2,384,128]{3,2,1,0:T(8,128)(2,1)S(1)}, bf16[4,2,384,128]{3,2,1,0:T(8,128)(2,1)S(1)}, u32[]{:S(2)}, u32[]{:S(2)}) collective-permute-start(bf16[4,2,384,128]{3,2,1,0:T(8,128)(2,1)S(1)} %pad_maximum_fusion.1.same), channel_id=1, source_target_pairs={{0,1},{1,0},{2,3},{3,2},{4,5},{5,4},{6,7},{7,6},{8,9},{9,8},{10,11... | collective-permute-start | bytes 2359304 | tf_op jit(solution)/shard_map/ppermute | solution.py:718
  131.2 1.0 copy-start.2

commit v17 on v16

--- a/solution.py
+++ b/solution.py
@@ -767,13 +767,14 @@
     back = [swap(block, 2 * j) if j else block for j, block in enumerate(partial_sums)]
     back = after(back, far)
     back = sum(block.astype(jnp.float32) for block in back)
-    own_rank = swap(back[1].astype(jnp.bfloat16), 1)
+    base = after(base, *partial_sums)
+    base = [base, swap(base, 2), swap(base, 4)]
+    own_rank = swap(after(back[1].astype(jnp.bfloat16), *base), 1)
     own_rank = back[0] + own_rank.astype(jnp.float32)
     own_rank = own_rank.astype(jnp.bfloat16)
     ups = along_z(after(ups, *partial_sums))
-    base = along_z(after(base, *partial_sums))
     all_rank = own_rank[:, ADAPTER_RANK:]
-    base = along_x(after(base, own_rank))
+    base = jnp.stack(base + [swap(after(base[2], own_rank), 2)])
     own, across = settle(
         stretch_adapter, elsewhere, adapter_owner, near, after(far, own_rank)
     )

time: 136 us -> 135 us (level)
  waiting for transfers between devices: 67.5 us -> 64.2 us
  starting transfers between devices: 37.8 us -> 40.5 us
    ppermute x29 -> x30, waiting for transfers between devices: 65.4 us -> 62.1 us  [swap(): lax.ppermute(block, ('groups', 'ctx'), [(i, i ^ mask) for i in range(4 *...]
    ppermute x29 -> x30, starting transfers between devices: 32.3 us -> 35 us  [swap(): lax.ppermute(block, ('groups', 'ctx'), [(i, i ^ mask) for i in range(4 *...]
  transfers between devices with their start and end apart: 30 -> 31, of which waited for: 17 -> 19; matrix products, arithmetic and copies ran while one was open for 2% -> 2% of each run, Pallas kernels for 7% -> 7%
where the time goes in v17:
time: 135 us
  waiting for transfers between devices  64.2 us (48%)
  starting transfers between devices  40.5 us (30%)
  Pallas kernels  23.2 us (17%)
  local copies, waits for them, and re-layouts  2.98 us (2%)
  other arithmetic  2.79 us (2%)
    ppermute x30, waiting for transfers between devices, swap(): lax.ppermute(block, ('groups', 'ctx'), [(i, i ^ mask) for i in range(4 *...  62.1 us
    ppermute x30, starting transfers between devices, swap(): lax.ppermute(block, ('groups', 'ctx'), [(i, i ^ mask) for i in range(4 *...  35 us
    pallas_call x2, Pallas kernels, attend(): pl.pallas_call(partial(attend_kernel, first_head), grid=(heads,), out_sha...  10.5 us
    all_to_all x1, starting transfers between devices, direct_shards(): spread = lax.all_to_all(packed, 'ctx', 0, 0, axis_index_groups=blocks)  5.5 us
    pallas_call x1, Pallas kernels, pack_row(): pl.pallas_call(partial(pack_kernel, sections), out_shape=jax.ShapeDtypeSt...  5.15 us
    pallas_call x1, Pallas kernels, widen(): pl.pallas_call(widen_kernel, out_shape=jax.ShapeDtypeStruct((attended.sha...  2.98 us
    unnamed x17, local copies, waits for them, and re-layouts  2.79 us
  transfers between devices with their start and end apart: 31, of which 19 were waited for; matrix products, arithmetic and copies ran while one was open for 2% of the time, Pallas kernels for 7%

profile of v17, /device:TPU:0, one launch (start us, length us, event | category | flops | bytes accessed | tf_op | source)
XLA Modules:
  0.0 134.6 jit_solution(11522418780108745587)
XLA Ops:
  0.6 5.2 %shard_map.86.refs_0_ = bf16[8,1312,128]{2,1,0:T(8,128)(2,1)} custom-call(bf16[1,2686976]{1,0:T(2,128)(2,1)} %pool.1), custom_call_target="tpu_custom_call" | custom-call | bytes 8388608 | tf_op jit(solution)/shard_map/pallas_call | solution.py:316
  5.8 5.5 %all-to-all-start = ((bf16[8,1312,128]{2,1,0:T(8,128)(2,1)}), bf16[8,1312,128]{2,1,0:T(8,128)(2,1)}, u32[]{:S(2)}, u32[]{:S(2)}) async-start(bf16[8,1312,128]{2,1,0:T(8,128)(2,1)} %shard_map.86.refs_0_), calls=%async_computation | async-start | bytes 5373952 | tf_op jit(solution)/shard_map/all_to_all | solution.py:757
  11.3 2.2 %collective-permute-start.1 = (s32[2]{0:T(128)S(1)}, s32[2]{0:T(128)S(1)}, u32[]{:S(2)}, u32[]{:S(2)}) collective-permute-start(s32[2]{0:T(128)S(1)} %copy-done.3), channel_id=1, source_target_pairs={{0,16},{1,17},{2,18},{3,19},{4,20},{5,21},{6,22},{7,23},{8,24},{9,... | collective-permute-start | bytes 32 | tf_op jit(solution)/shard_map/ppermute | solution.py:718
  13.5 1.2 copy-done.1
  14.8 0.3 shard_map.87
  15.0 0.1 collective-permute-start.2
  15.1 0.5 copy-done.6
  15.6 2.6 %collective-permute-start = (bf16[64,1024]{1,0:T(8,128)(2,1)S(1)}, bf16[64,1024]{1,0:T(8,128)(2,1)S(1)}, u32[]{:S(2)}, u32[]{:S(2)}) collective-permute-start(bf16[64,1024]{1,0:T(8,128)(2,1)S(1)} %constant_dynamic-update-slice_fusion), channel_id=1, source_target_pairs={{0,8},{1,9},{2,10},{3,11},{4,12},{5,13},{6,14},{7,15},{8,0},{9,1},... | collective-permute-start | bytes 393224 | tf_op jit(solution)/shard_map/ppermute | solution.py:718
  18.4 1.9 %fusion = (f32[1024,64]{1,0:T(8,128)S(1)}, f32[1024,64]{1,0:T(8,128)S(1)}, f32[1024,64]{1,0:T(8,128)S(1)}) fusion(f32[64]{0:T(128)S(1)} %multiply_power_fusion, f32[1024]{0:T(1024)S(1)} %iota_convert_fusion), kind=kLoop, calls=%fused_computation.15 | loop fusion | flops 131072 | bytes 790784 | tf_op jit(solution)/shard_map/neg | solution.py:734
  20.3 0.3 pad_maximum_fusion.2
  20.6 23.5 %collective-permute-done = bf16[64,1024]{1,0:T(8,128)(2,1)S(1)} collective-permute-done((bf16[64,1024]{1,0:T(8,128)(2,1)S(1)}, bf16[64,1024]{1,0:T(8,128)(2,1)S(1)}, u32[]{:S(2)}, u32[]{:S(2)}) %collective-permute-start) | collective-permute-done | bytes 131104 | tf_op jit(solution)/shard_map/ppermute | solution.py:718
  44.1 2.1 %all-to-all-done.spread = bf16[8,1312,128]{2,1,0:T(8,128)(2,1)} async-done(((bf16[8,1312,128]{2,1,0:T(8,128)(2,1)}), bf16[8,1312,128]{2,1,0:T(8,128)(2,1)}, u32[]{:S(2)}, u32[]{:S(2)}) %all-to-all-start) | async-done | bytes 2687008 | tf_op jit(solution)/shard_map/all_to_all | solution.py:757
  46.3 2.1 %shard_map.88 = (bf16[960,128]{1,0:T(8,128)(2,1)S(1)}, bf16[960,128]{1,0:T(8,128)(2,1)S(1)}, bf16[960,128]{1,0:T(8,128)(2,1)S(1)}, bf16[960,128]{1,0:T(8,128)(2,...) custom-call(s32[2]{0:T(128)S(1)} %copy-done.3, s32[2]{0:T(128)S(1)} %collective-permute-done.1.there, ...), custom_call_target="tpu_custom_call" | custom-call | bytes 3145728 | tf_op jit(solution)/shard_map/pallas_call | solution.py:360
  48.4 2.1 %collective-permute-start.3 = (bf16[960,128]{1,0:T(8,128)(2,1)S(1)}, bf16[960,128]{1,0:T(8,128)(2,1)S(1)}, u32[]{:S(2)}, u32[]{:S(2)}) collective-permute-start(bf16[960,128]{1,0:T(8,128)(2,1)S(1)} %get-tuple-element.41), channel_id=1, source_target_pairs={{0,16},{1,17},{2,18},{3,19},{4,20},{5,21},{6,22},{7,23},{8,24},{9,... | collective-permute-start | bytes 737288 | tf_op jit(solution)/shard_map/ppermute | solution.py:718
  50.6 1.3 collective-permute-start.4
  51.9 1.1 collective-permute-start.5
  53.1 1.5 %collective-permute-start.6 = (bf16[2,64,1024]{2,1,0:T(8,128)(2,1)S(1)}, bf16[2,64,1024]{2,1,0:T(8,128)(2,1)S(1)}, u32[]{:S(2)}, u32[]{:S(2)}) collective-permute-start(bf16[2,64,1024]{2,1,0:T(8,128)(2,1)S(1)} %get-tuple-element.48), channel_id=1, source_target_pairs={{0,2},{1,3},{2,0},{3,1},{4,6},{5,7},{6,4},{7,5},{8,10},{9,11},{10,... | collective-permute-start | bytes 786440 | tf_op jit(solution)/shard_map/ppermute | solution.py:718
  54.6 3.0 %collective-permute-start.7 = (bf16[2,64,1024]{2,1,0:T(8,128)(2,1)S(1)}, bf16[2,64,1024]{2,1,0:T(8,128)(2,1)S(1)}, u32[]{:S(2)}, u32[]{:S(2)}) collective-permute-start(bf16[2,64,1024]{2,1,0:T(8,128)(2,1)S(1)} %get-tuple-element.49), channel_id=1, source_target_pairs={{0,4},{1,5},{2,6},{3,7},{4,0},{5,1},{6,2},{7,3},{8,12},{9,13},{10,... | collective-permute-start | bytes 786440 | tf_op jit(solution)/shard_map/ppermute | solution.py:718
  57.7 2.3 %collective-permute-start.8 = (bf16[2,64,1024]{2,1,0:T(8,128)(2,1)S(1)}, bf16[2,64,1024]{2,1,0:T(8,128)(2,1)S(1)}, u32[]{:S(2)}, u32[]{:S(2)}) collective-permute-start(bf16[2,64,1024]{2,1,0:T(8,128)(2,1)S(1)} %get-tuple-element.50), channel_id=1, source_target_pairs={{0,6},{1,7},{2,4},{3,5},{4,2},{5,3},{6,0},{7,1},{8,14},{9,15},{10,... | collective-permute-start | bytes 786440 | tf_op jit(solution)/shard_map/ppermute | solution.py:718
  60.0 11.1 %collective-permute-done.4.refs_2_ = bf16[960,128]{1,0:T(8,128)(2,1)S(1)} collective-permute-done((bf16[960,128]{1,0:T(8,128)(2,1)S(1)}, bf16[960,128]{1,0:T(8,128)(2,1)S(1)}, u32[]{:S(2)}, u32[]{:S(2)}) %collective-permute-start.4) | collective-permute-done | bytes 245792 | tf_op jit(solution)/shard_map/ppermute | solution.py:718
  71.1 3.3 %collective-permute-done.5.refs_3_ = bf16[960,128]{1,0:T(8,128)(2,1)S(1)} collective-permute-done((bf16[960,128]{1,0:T(8,128)(2,1)S(1)}, bf16[960,128]{1,0:T(8,128)(2,1)S(1)}, u32[]{:S(2)}, u32[]{:S(2)}) %collective-permute-start.5) | collective-permute-done | bytes 245792 | tf_op jit(solution)/shard_map/ppermute | solution.py:718
  74.4 1.0 shard_map.89
  75.4 0.1 collective-permute-start.14
  75.5 1.2 collective-permute-done.8.refs_3_
  76.7 0.4 shard_map.90
  77.1 1.6 %collective-permute-start.11 = (bf16[2,64,192]{2,1,0:T(8,128)(2,1)S(1)}, bf16[2,64,192]{2,1,0:T(8,128)(2,1)S(1)}, u32[]{:S(2)}, u32[]{:S(2)}) collective-permute-start(bf16[2,64,192]{2,1,0:T(8,128)(2,1)S(1)} %get-tuple-element.52), channel_id=1, source_target_pairs={{0,2},{1,3},{2,0},{3,1},{4,6},{5,7},{6,4},{7,5},{8,10},{9,11},{10,... | collective-permute-start | bytes 147464 | tf_op jit(solution)/shard_map/ppermute | solution.py:718
  78.7 1.6 %collective-permute-start.12 = (bf16[2,64,192]{2,1,0:T(8,128)(2,1)S(1)}, bf16[2,64,192]{2,1,0:T(8,128)(2,1)S(1)}, u32[]{:S(2)}, u32[]{:S(2)}) collective-permute-start(bf16[2,64,192]{2,1,0:T(8,128)(2,1)S(1)} %get-tuple-element.53), channel_id=1, source_target_pairs={{0,4},{1,5},{2,6},{3,7},{4,0},{5,1},{6,2},{7,3},{8,12},{9,13},{10,... | collective-permute-start | bytes 147464 | tf_op jit(solution)/shard_map/ppermute | solution.py:718
  80.3 0.4 collective-permute-start.13
  80.7 1.5 %collective-permute-start.9 = (bf16[2,64,1024]{2,1,0:T(8,128)(2,1)S(1)}, bf16[2,64,1024]{2,1,0:T(8,128)(2,1)S(1)}, u32[]{:S(2)}, u32[]{:S(2)}) collective-permute-start(bf16[2,64,1024]{2,1,0:T(8,128)(2,1)S(1)} %pad_maximum_fusion.6), channel_id=1, source_target_pairs={{0,2},{1,3},{2,0},{3,1},{4,6},{5,7},{6,4},{7,5},{8,10},{9,11},{10,... | collective-permute-start | bytes 786440 | tf_op jit(solution)/shard_map/ppermute | solution.py:718
  82.2 1.6 %collective-permute-start.10 = (bf16[2,64,1024]{2,1,0:T(8,128)(2,1)S(1)}, bf16[2,64,1024]{2,1,0:T(8,128)(2,1)S(1)}, u32[]{:S(2)}, u32[]{:S(2)}) collective-permute-start(bf16[2,64,1024]{2,1,0:T(8,128)(2,1)S(1)} %pad_maximum_fusion.6), channel_id=1, source_target_pairs={{0,4},{1,5},{2,6},{3,7},{4,0},{5,1},{6,2},{7,3},{8,12},{9,13},{10,... | collective-permute-start | bytes 786440 | tf_op jit(solution)/shard_map/ppermute | solution.py:718
  83.8 3.0 %collective-permute-done.12 = bf16[2,64,192]{2,1,0:T(8,128)(2,1)S(1)} collective-permute-done((bf16[2,64,192]{2,1,0:T(8,128)(2,1)S(1)}, bf16[2,64,192]{2,1,0:T(8,128)(2,1)S(1)}, u32[]{:S(2)}, u32[]{:S(2)}) %collective-permute-start.12) | collective-permute-done | bytes 49184 | tf_op jit(solution)/shard_map/ppermute | solution.py:718
  86.8 1.8 %collective-permute-done.13 = bf16[2,64,192]{2,1,0:T(8,128)(2,1)S(1)} collective-permute-done((bf16[2,64,192]{2,1,0:T(8,128)(2,1)S(1)}, bf16[2,64,192]{2,1,0:T(8,128)(2,1)S(1)}, u32[]{:S(2)}, u32[]{:S(2)}) %collective-permute-start.13) | collective-permute-done | bytes 49184 | tf_op jit(solution)/shard_map/ppermute | solution.py:718
  88.6 0.5 collective-permute-done.9
  89.1 3.8 %collective-permute-done.10 = bf16[2,64,1024]{2,1,0:T(8,128)(2,1)S(1)} collective-permute-done((bf16[2,64,1024]{2,1,0:T(8,128)(2,1)S(1)}, bf16[2,64,1024]{2,1,0:T(8,128)(2,1)S(1)}, u32[]{:S(2)}, u32[]{:S(2)}) %collective-permute-start.10) | collective-permute-done | bytes 262176 | tf_op jit(solution)/shard_map/ppermute | solution.py:718
  92.9 1.2 collective-permute-done.15
  94.1 0.1 slice_bitcast_fusion.1
  94.2 0.8 collective-permute-start.16
  95.0 1.4 %collective-permute-start.17 = (bf16[64,128]{1,0:T(8,128)(2,1)S(1)}, bf16[64,128]{1,0:T(8,128)(2,1)S(1)}, u32[]{:S(2)}, u32[]{:S(2)}) collective-permute-start(bf16[64,128]{1,0:T(8,128)(2,1)S(1)} %get-tuple-element.85), channel_id=1, source_target_pairs={{0,8},{1,9},{2,10},{3,11},{4,12},{5,13},{6,14},{7,15},{8,0},{9,1},... | collective-permute-start | bytes 49160 | tf_op jit(solution)/shard_map/ppermute | solution.py:718
  96.4 1.7 %collective-permute-done.18 = bf16[2,192,128]{2,1,0:T(8,128)(2,1)S(1)} collective-permute-done((bf16[2,192,128]{2,1,0:T(8,128)(2,1)S(1)}, bf16[2,192,128]{2,1,0:T(8,128)(2,1)S(1)}, u32[]{:S(2)}, u32[]{:S(2)}) %collective-permute-start.18) | collective-permute-done | bytes 98336 | tf_op jit(solution)/shard_map/ppermute | solution.py:718
  98.1 1.5 %collective-permute-done.17 = bf16[64,128]{1,0:T(8,128)(2,1)S(1)} collective-permute-done((bf16[64,128]{1,0:T(8,128)(2,1)S(1)}, bf16[64,128]{1,0:T(8,128)(2,1)S(1)}, u32[]{:S(2)}, u32[]{:S(2)}) %collective-permute-start.17) | collective-permute-done | bytes 16416 | tf_op jit(solution)/shard_map/ppermute | solution.py:718
  99.7 1.5 %collective-permute-start.21 = (bf16[2,64,128]{2,1,0:T(8,128)(2,1)S(1)}, bf16[2,64,128]{2,1,0:T(8,128)(2,1)S(1)}, u32[]{:S(2)}, u32[]{:S(2)}) collective-permute-start(bf16[2,64,128]{2,1,0:T(8,128)(2,1)S(1)} %pad_maximum_fusion.14), channel_id=1, source_target_pairs={{0,6},{1,7},{2,4},{3,5},{4,2},{5,3},{6,0},{7,1},{8,14},{9,15},{10,... | collective-permute-start | bytes 98312 | tf_op jit(solution)/shard_map/ppermute | solution.py:718
  101.1 1.2 collective-permute-start.20
  102.3 0.8 collective-permute-start.19
  103.1 0.8 shard_map.91
  103.9 1.5 %collective-permute-start.24 = (bf16[384,128]{1,0:T(8,128)(2,1)S(1)}, bf16[384,128]{1,0:T(8,128)(2,1)S(1)}, u32[]{:S(2)}, u32[]{:S(2)}) collective-permute-start(bf16[384,128]{1,0:T(8,128)(2,1)S(1)} %get-tuple-element.72), channel_id=1, source_target_pairs={{0,16},{1,17},{2,18},{3,19},{4,20},{5,21},{6,22},{7,23},{8,24},{9,... | collective-permute-start | bytes 294920 | tf_op jit(solution)/shard_map/ppermute | solution.py:718
  105.4 1.0 collective-permute-start.23
  106.4 0.2 collective-permute-done.19
  106.6 0.1 pad_maximum_fusion.key_same.value_same
  106.8 0.1 collective-permute-start.22
  106.9 1.8 %collective-permute-done.24 = bf16[384,128]{1,0:T(8,128)(2,1)S(1)} collective-permute-done((bf16[384,128]{1,0:T(8,128)(2,1)S(1)}, bf16[384,128]{1,0:T(8,128)(2,1)S(1)}, u32[]{:S(2)}, u32[]{:S(2)}) %collective-permute-start.24) | collective-permute-done | bytes 98336 | tf_op jit(solution)/shard_map/ppermute | solution.py:718
  108.6 2.4 %collective-permute-done.23 = bf16[2,2,192,128]{3,2,1,0:T(8,128)(2,1)S(1)} collective-permute-done((bf16[2,2,192,128]{3,2,1,0:T(8,128)(2,1)S(1)}, bf16[2,2,192,128]{3,2,1,0:T(8,128)(2,1)S(1)}, u32[]{:S(2)}, u32[]{:S(2)}) %collective-permute-start.23) | collective-permute-done | bytes 196640 | tf_op jit(solution)/shard_map/ppermute | solution.py:718
  111.3 1.9 %collective-permute-done.25.rows_other = bf16[2048,128]{1,0:T(8,128)(2,1)S(1)} collective-permute-done((bf16[2048,128]{1,0:T(8,128)(2,1)S(1)}, bf16[2048,128]{1,0:T(8,128)(2,1)S(1)}, u32[]{:S(2)}, u32[]{:S(2)}) %collective-permute-start.25) | collective-permute-done | bytes 524320 | tf_op jit(solution)/shard_map/ppermute | solution.py:718
  113.2 2.9 %shard_map.92.refs_0_ = bf16[64,4096]{1,0:T(8,128)(2,1)} custom-call(bf16[64,4096]{1,0:T(8,128)(2,1)S(1)} %copy-done.5, bf16[4,2,64,1024]{3,2,1,0:T(8,128)(2,1)S(1)} %pad_maximum_fusion.key_same.value_same, bf16[4,2,64,1024]{3,2,1,0:T(8,128)(2,1)S(1)} %collective-permute-done.22.key_other.value_other, ...), custom_call_target="tpu_custom_call" | custom-call | flops 3221225472 | bytes 10485760 | tf_op jit(solution)/shard_map/pallas_call | solution.py:641
  116.1 1.3 collective-permute-start.28
  117.3 1.2 collective-permute-start.27
  118.5 1.0 collective-permute-start.26
  119.6 7.6 %shard_map.93.attended = bf16[64,4096]{1,0:T(8,128)(2,1)} custom-call(bf16[64,4096]{1,0:T(8,128)(2,1)S(1)} %copy-done.5, bf16[4,2,64,1024]{3,2,1,0:T(8,128)(2,1)S(1)} %pad_maximum_fusion.key_same.value_same, bf16[4,2,64,1024]{3,2,1,0:T(8,128)(2,1)S(1)} %collective-permute-done.22.key_other.value_other, ...), custom_call_target="tpu_custom_call", output_to_operand_aliasing={{}: (10, {})} | custom-call | flops 9663676416 | bytes 10485760 | tf_op jit(solution)/shard_map/pallas_call | solution.py:641
  127.2 0.6 collective-permute-done.27
  127.7 0.4 collective-permute-done.26
  128.1 0.1 pad_maximum_fusion.1.same
  128.2 0.1 collective-permute-start.29
  128.3 2.3 %collective-permute-done.29.other = bf16[4,2,384,128]{3,2,1,0:T(8,128)(2,1)S(1)} collective-permute-done((bf16[4,2,384,128]{3,2,1,0:T(8,128)(2,1)S(1)}, bf16[4,2,384,128]{3,2,1,0:T(8,128)(2,1)S(1)}, u32[]{:S(2)}, u32[]{:S(2)}) %collective-permute-start.29) | collective-permute-done | bytes 786464 | tf_op jit(solution)/shard_map/ppermute | solution.py:718
  130.6 1.0 copy-done.2
  131.6 3.0 %shard_map.94 = bf16[64,8192]{1,0:T(8,128)(2,1)} custom-call(bf16[64,4096]{1,0:T(8,128)(2,1)S(1)} %copy-done.2, bf16[4,2,384,128]{3,2,1,0:T(8,128)(2,1)S(1)} %pad_maximum_fusion.1.same, bf16[4,2,384,128]{3,2,1,0:T(8,128)(2,1)S(1)} %collective-permute-done.29.other), custom_call_target="tpu_custom_call" | custom-call | flops 134217728 | bytes 4194304 | tf_op jit(solution)/shard_map/pallas_call | solution.py:703
  (47 shorter events, 0.6 us)
Async XLA Ops:
  5.8 5.5 %copy-start.3 = (s32[2]{0:T(128)S(1)}, s32[2]{0:T(128)}, u32[]{:S(2)}) copy-start(s32[2]{0:T(128)} %here.5) | copy-start | bytes 28
  5.8 7.7 %copy-start = (bf16[8,1312,128]{2,1,0:T(8,128)(2,1)S(1)}, bf16[8,1312,128]{2,1,0:T(8,128)(2,1)}, u32[]{:S(2)}) copy-start(bf16[8,1312,128]{2,1,0:T(8,128)(2,1)} %shard_map.86.refs_0_) | copy-start | bytes 8060932
  5.8 40.5 %all-to-all-start = ((bf16[8,1312,128]{2,1,0:T(8,128)(2,1)}), bf16[8,1312,128]{2,1,0:T(8,128)(2,1)}, u32[]{:S(2)}, u32[]{:S(2)}) async-start(bf16[8,1312,128]{2,1,0:T(8,128)(2,1)} %shard_map.86.refs_0_), calls=%async_computation | async-start | bytes 5373952 | tf_op jit(solution)/shard_map/all_to_all | solution.py:757
  11.3 35.0 %collective-permute-start.1 = (s32[2]{0:T(128)S(1)}, s32[2]{0:T(128)S(1)}, u32[]{:S(2)}, u32[]{:S(2)}) collective-permute-start(s32[2]{0:T(128)S(1)} %copy-done.3), channel_id=1, source_target_pairs={{0,16},{1,17},{2,18},{3,19},{4,20},{5,21},{6,22},{7,23},{8,24},{9,... | collective-permute-start | bytes 32 | tf_op jit(solution)/shard_map/ppermute | solution.py:718
  13.5 1.2 copy-start.1
  14.8 0.8 copy-start.6
  14.8 0.9 copy-start.7
  15.0 29.1 %collective-permute-start.2 = (bf16[4,64,1024]{2,1,0:T(8,128)(2,1)S(1)}, bf16[4,64,1024]{2,1,0:T(8,128)(2,1)S(1)}, u32[]{:S(2)}, u32[]{:S(2)}) collective-permute-start(bf16[4,64,1024]{2,1,0:T(8,128)(2,1)S(1)} %get-tuple-element.39), channel_id=1, source_target_pairs={{0,1},{1,0},{2,3},{3,2},{4,5},{5,4},{6,7},{7,6},{8,9},{9,8},{10,11... | collective-permute-start | bytes 1572872 | tf_op jit(solution)/shard_map/ppermute | solution.py:718
  15.6 28.4 %collective-permute-start = (bf16[64,1024]{1,0:T(8,128)(2,1)S(1)}, bf16[64,1024]{1,0:T(8,128)(2,1)S(1)}, u32[]{:S(2)}, u32[]{:S(2)}) collective-permute-start(bf16[64,1024]{1,0:T(8,128)(2,1)S(1)} %constant_dynamic-update-slice_fusion), channel_id=1, source_target_pairs={{0,8},{1,9},{2,10},{3,11},{4,12},{5,13},{6,14},{7,15},{8,0},{9,1},... | collective-permute-start | bytes 393224 | tf_op jit(solution)/shard_map/ppermute | solution.py:718
  18.3 28.0 %copy-start.4 = (s32[16]{0:T(128)S(1)}, s32[16]{0:T(128)}, u32[]{:S(2)}) copy-start(s32[16]{0:T(128)} %owner.5) | copy-start | bytes 196
  48.4 9.2 %collective-permute-start.3 = (bf16[960,128]{1,0:T(8,128)(2,1)S(1)}, bf16[960,128]{1,0:T(8,128)(2,1)S(1)}, u32[]{:S(2)}, u32[]{:S(2)}) collective-permute-start(bf16[960,128]{1,0:T(8,128)(2,1)S(1)} %get-tuple-element.41), channel_id=1, source_target_pairs={{0,16},{1,17},{2,18},{3,19},{4,20},{5,21},{6,22},{7,23},{8,24},{9,... | collective-permute-start | bytes 737288 | tf_op jit(solution)/shard_map/ppermute | solution.py:718
  50.6 20.5 %collective-permute-start.4 = (bf16[960,128]{1,0:T(8,128)(2,1)S(1)}, bf16[960,128]{1,0:T(8,128)(2,1)S(1)}, u32[]{:S(2)}, u32[]{:S(2)}) collective-permute-start(bf16[960,128]{1,0:T(8,128)(2,1)S(1)} %get-tuple-element.43), channel_id=1, source_target_pairs={{0,8},{1,9},{2,10},{3,11},{4,12},{5,13},{6,14},{7,15},{8,0},{9,1},... | collective-permute-start | bytes 737288 | tf_op jit(solution)/shard_map/ppermute | solution.py:718
  51.9 22.5 %collective-permute-start.5 = (bf16[960,128]{1,0:T(8,128)(2,1)S(1)}, bf16[960,128]{1,0:T(8,128)(2,1)S(1)}, u32[]{:S(2)}, u32[]{:S(2)}) collective-permute-start(bf16[960,128]{1,0:T(8,128)(2,1)S(1)} %get-tuple-element.44), channel_id=1, source_target_pairs={{0,24},{1,25},{2,26},{3,27},{4,28},{5,29},{6,30},{7,31},{8,16},{9,... | collective-permute-start | bytes 737288 | tf_op jit(solution)/shard_map/ppermute | solution.py:718
  53.1 22.4 %collective-permute-start.6 = (bf16[2,64,1024]{2,1,0:T(8,128)(2,1)S(1)}, bf16[2,64,1024]{2,1,0:T(8,128)(2,1)S(1)}, u32[]{:S(2)}, u32[]{:S(2)}) collective-permute-start(bf16[2,64,1024]{2,1,0:T(8,128)(2,1)S(1)} %get-tuple-element.48), channel_id=1, source_target_pairs={{0,2},{1,3},{2,0},{3,1},{4,6},{5,7},{6,4},{7,5},{8,10},{9,11},{10,... | collective-permute-start | bytes 786440 | tf_op jit(solution)/shard_map/ppermute | solution.py:718
  54.6 20.8 %collective-permute-start.7 = (bf16[2,64,1024]{2,1,0:T(8,128)(2,1)S(1)}, bf16[2,64,1024]{2,1,0:T(8,128)(2,1)S(1)}, u32[]{:S(2)}, u32[]{:S(2)}) collective-permute-start(bf16[2,64,1024]{2,1,0:T(8,128)(2,1)S(1)} %get-tuple-element.49), channel_id=1, source_target_pairs={{0,4},{1,5},{2,6},{3,7},{4,0},{5,1},{6,2},{7,3},{8,12},{9,13},{10,... | collective-permute-start | bytes 786440 | tf_op jit(solution)/shard_map/ppermute | solution.py:718
  57.7 19.0 %collective-permute-start.8 = (bf16[2,64,1024]{2,1,0:T(8,128)(2,1)S(1)}, bf16[2,64,1024]{2,1,0:T(8,128)(2,1)S(1)}, u32[]{:S(2)}, u32[]{:S(2)}) collective-permute-start(bf16[2,64,1024]{2,1,0:T(8,128)(2,1)S(1)} %get-tuple-element.50), channel_id=1, source_target_pairs={{0,6},{1,7},{2,4},{3,5},{4,2},{5,3},{6,0},{7,1},{8,14},{9,15},{10,... | collective-permute-start | bytes 786440 | tf_op jit(solution)/shard_map/ppermute | solution.py:718
  75.4 13.2 %collective-permute-start.14 = (bf16[2,384,128]{2,1,0:T(8,128)(2,1)S(1)}, bf16[2,384,128]{2,1,0:T(8,128)(2,1)S(1)}, u32[]{:S(2)}, u32[]{:S(2)}) collective-permute-start(bf16[2,384,128]{2,1,0:T(8,128)(2,1)S(1)} %get-tuple-element.57), channel_id=1, source_target_pairs={{0,8},{1,9},{2,10},{3,11},{4,12},{5,13},{6,14},{7,15},{8,0},{9,1},... | collective-permute-start | bytes 589832 | tf_op jit(solution)/shard_map/ppermute | solution.py:718
  77.1 5.0 %collective-permute-start.11 = (bf16[2,64,192]{2,1,0:T(8,128)(2,1)S(1)}, bf16[2,64,192]{2,1,0:T(8,128)(2,1)S(1)}, u32[]{:S(2)}, u32[]{:S(2)}) collective-permute-start(bf16[2,64,192]{2,1,0:T(8,128)(2,1)S(1)} %get-tuple-element.52), channel_id=1, source_target_pairs={{0,2},{1,3},{2,0},{3,1},{4,6},{5,7},{6,4},{7,5},{8,10},{9,11},{10,... | collective-permute-start | bytes 147464 | tf_op jit(solution)/shard_map/ppermute | solution.py:718
  78.7 8.1 %collective-permute-start.12 = (bf16[2,64,192]{2,1,0:T(8,128)(2,1)S(1)}, bf16[2,64,192]{2,1,0:T(8,128)(2,1)S(1)}, u32[]{:S(2)}, u32[]{:S(2)}) collective-permute-start(bf16[2,64,192]{2,1,0:T(8,128)(2,1)S(1)} %get-tuple-element.53), channel_id=1, source_target_pairs={{0,4},{1,5},{2,6},{3,7},{4,0},{5,1},{6,2},{7,3},{8,12},{9,13},{10,... | collective-permute-start | bytes 147464 | tf_op jit(solution)/shard_map/ppermute | solution.py:718
  80.3 8.2 %collective-permute-start.13 = (bf16[2,64,192]{2,1,0:T(8,128)(2,1)S(1)}, bf16[2,64,192]{2,1,0:T(8,128)(2,1)S(1)}, u32[]{:S(2)}, u32[]{:S(2)}) collective-permute-start(bf16[2,64,192]{2,1,0:T(8,128)(2,1)S(1)} %get-tuple-element.54), channel_id=1, source_target_pairs={{0,6},{1,7},{2,4},{3,5},{4,2},{5,3},{6,0},{7,1},{8,14},{9,15},{10,... | collective-permute-start | bytes 147464 | tf_op jit(solution)/shard_map/ppermute | solution.py:718
  80.7 8.4 %collective-permute-start.9 = (bf16[2,64,1024]{2,1,0:T(8,128)(2,1)S(1)}, bf16[2,64,1024]{2,1,0:T(8,128)(2,1)S(1)}, u32[]{:S(2)}, u32[]{:S(2)}) collective-permute-start(bf16[2,64,1024]{2,1,0:T(8,128)(2,1)S(1)} %pad_maximum_fusion.6), channel_id=1, source_target_pairs={{0,2},{1,3},{2,0},{3,1},{4,6},{5,7},{6,4},{7,5},{8,10},{9,11},{10,... | collective-permute-start | bytes 786440 | tf_op jit(solution)/shard_map/ppermute | solution.py:718
  82.2 10.7 %collective-permute-start.10 = (bf16[2,64,1024]{2,1,0:T(8,128)(2,1)S(1)}, bf16[2,64,1024]{2,1,0:T(8,128)(2,1)S(1)}, u32[]{:S(2)}, u32[]{:S(2)}) collective-permute-start(bf16[2,64,1024]{2,1,0:T(8,128)(2,1)S(1)} %pad_maximum_fusion.6), channel_id=1, source_target_pairs={{0,4},{1,5},{2,6},{3,7},{4,0},{5,1},{6,2},{7,3},{8,12},{9,13},{10,... | collective-permute-start | bytes 786440 | tf_op jit(solution)/shard_map/ppermute | solution.py:718
  92.9 1.2 collective-permute-start.15
  92.9 5.2 %collective-permute-start.18 = (bf16[2,192,128]{2,1,0:T(8,128)(2,1)S(1)}, bf16[2,192,128]{2,1,0:T(8,128)(2,1)S(1)}, u32[]{:S(2)}, u32[]{:S(2)}) collective-permute-start(bf16[2,192,128]{2,1,0:T(8,128)(2,1)S(1)} %get-tuple-element.65), channel_id=1, source_target_pairs={{0,4},{1,5},{2,6},{3,7},{4,0},{5,1},{6,2},{7,3},{8,12},{9,13},{10,... | collective-permute-start | bytes 294920 | tf_op jit(solution)/shard_map/ppermute | solution.py:718
  94.2 12.4 %collective-permute-start.16 = (bf16[2,64,1024]{2,1,0:T(8,128)(2,1)S(1)}, bf16[2,64,1024]{2,1,0:T(8,128)(2,1)S(1)}, u32[]{:S(2)}, u32[]{:S(2)}) collective-permute-start(bf16[2,64,1024]{2,1,0:T(8,128)(2,1)S(1)} %collective-permute-done.10), channel_id=1, source_target_pairs={{0,2},{1,3},{2,0},{3,1},{4,6},{5,7},{6,4},{7,5},{8,10},{9,11},{10,... | collective-permute-start | bytes 786440 | tf_op jit(solution)/shard_map/ppermute | solution.py:718
  95.0 4.6 %collective-permute-start.17 = (bf16[64,128]{1,0:T(8,128)(2,1)S(1)}, bf16[64,128]{1,0:T(8,128)(2,1)S(1)}, u32[]{:S(2)}, u32[]{:S(2)}) collective-permute-start(bf16[64,128]{1,0:T(8,128)(2,1)S(1)} %get-tuple-element.85), channel_id=1, source_target_pairs={{0,8},{1,9},{2,10},{3,11},{4,12},{5,13},{6,14},{7,15},{8,0},{9,1},... | collective-permute-start | bytes 49160 | tf_op jit(solution)/shard_map/ppermute | solution.py:718
  99.7 5.8 %collective-permute-start.21 = (bf16[2,64,128]{2,1,0:T(8,128)(2,1)S(1)}, bf16[2,64,128]{2,1,0:T(8,128)(2,1)S(1)}, u32[]{:S(2)}, u32[]{:S(2)}) collective-permute-start(bf16[2,64,128]{2,1,0:T(8,128)(2,1)S(1)} %pad_maximum_fusion.14), channel_id=1, source_target_pairs={{0,6},{1,7},{2,4},{3,5},{4,2},{5,3},{6,0},{7,1},{8,14},{9,15},{10,... | collective-permute-start | bytes 98312 | tf_op jit(solution)/shard_map/ppermute | solution.py:718
  101.1 5.3 %collective-permute-start.20 = (bf16[2,64,128]{2,1,0:T(8,128)(2,1)S(1)}, bf16[2,64,128]{2,1,0:T(8,128)(2,1)S(1)}, u32[]{:S(2)}, u32[]{:S(2)}) collective-permute-start(bf16[2,64,128]{2,1,0:T(8,128)(2,1)S(1)} %pad_maximum_fusion.14), channel_id=1, source_target_pairs={{0,4},{1,5},{2,6},{3,7},{4,0},{5,1},{6,2},{7,3},{8,12},{9,13},{10,... | collective-permute-start | bytes 98312 | tf_op jit(solution)/shard_map/ppermute | solution.py:718
  102.3 4.3 %collective-permute-start.19 = (bf16[2,64,128]{2,1,0:T(8,128)(2,1)S(1)}, bf16[2,64,128]{2,1,0:T(8,128)(2,1)S(1)}, u32[]{:S(2)}, u32[]{:S(2)}) collective-permute-start(bf16[2,64,128]{2,1,0:T(8,128)(2,1)S(1)} %pad_maximum_fusion.14), channel_id=1, source_target_pairs={{0,2},{1,3},{2,0},{3,1},{4,6},{5,7},{6,4},{7,5},{8,10},{9,11},{10,... | collective-permute-start | bytes 98312 | tf_op jit(solution)/shard_map/ppermute | solution.py:718
  103.9 4.7 %collective-permute-start.24 = (bf16[384,128]{1,0:T(8,128)(2,1)S(1)}, bf16[384,128]{1,0:T(8,128)(2,1)S(1)}, u32[]{:S(2)}, u32[]{:S(2)}) collective-permute-start(bf16[384,128]{1,0:T(8,128)(2,1)S(1)} %get-tuple-element.72), channel_id=1, source_target_pairs={{0,16},{1,17},{2,18},{3,19},{4,20},{5,21},{6,22},{7,23},{8,24},{9,... | collective-permute-start | bytes 294920 | tf_op jit(solution)/shard_map/ppermute | solution.py:718
  105.4 5.7 %collective-permute-start.23 = (bf16[2,2,192,128]{3,2,1,0:T(8,128)(2,1)S(1)}, bf16[2,2,192,128]{3,2,1,0:T(8,128)(2,1)S(1)}, u32[]{:S(2)}, u32[]{:S(2)}) collective-permute-start(bf16[2,2,192,128]{3,2,1,0:T(8,128)(2,1)S(1)} %pad_maximum_fusion.11), channel_id=1, source_target_pairs={{0,2},{1,3},{2,0},{3,1},{4,6},{5,7},{6,4},{7,5},{8,10},{9,11},{10,... | collective-permute-start | bytes 589832 | tf_op jit(solution)/shard_map/ppermute | solution.py:718
  106.6 6.6 %copy-start.5 = (bf16[64,4096]{1,0:T(8,128)(2,1)S(1)}, bf16[64,4096]{1,0:T(8,128)(2,1)}, u32[]{:S(2)}) copy-start(bf16[64,4096]{1,0:T(8,128)(2,1)} %query_block.3) | copy-start | bytes 1572868
  106.8 6.4 %collective-permute-start.22 = (bf16[4,2,64,1024]{3,2,1,0:T(8,128)(2,1)S(1)}, bf16[4,2,64,1024]{3,2,1,0:T(8,128)(2,1)S(1)}, u32[]{:S(2)}, u32[]{:S(2)}) collective-permute-start(bf16[4,2,64,1024]{3,2,1,0:T(8,128)(2,1)S(1)} %pad_maximum_fusion.key_same.value_same), channel_id=1, source_target_pairs={{0,1},{1,0},{2,3},{3,2},{4,5},{5,4},{6,7},{7,6},{8,9},{9,8},{10,11... | collective-permute-start | bytes 3145736 | tf_op jit(solution)/shard_map/ppermute | solution.py:718
  111.2 2.0 %collective-permute-start.25 = (bf16[2048,128]{1,0:T(8,128)(2,1)S(1)}, bf16[2048,128]{1,0:T(8,128)(2,1)S(1)}, u32[]{:S(2)}, u32[]{:S(2)}) collective-permute-start(bf16[2048,128]{1,0:T(8,128)(2,1)S(1)} %pad_maximum_fusion.4.rows_same), channel_id=1, source_target_pairs={{0,1},{1,0},{2,3},{3,2},{4,5},{5,4},{6,7},{7,6},{8,9},{9,8},{10,11... | collective-permute-start | bytes 1572872 | tf_op jit(solution)/shard_map/ppermute | solution.py:718
  116.1 11.1 %collective-permute-start.28 = (bf16[2,384,128]{2,1,0:T(8,128)(2,1)S(1)}, bf16[2,384,128]{2,1,0:T(8,128)(2,1)S(1)}, u32[]{:S(2)}, u32[]{:S(2)}) collective-permute-start(bf16[2,384,128]{2,1,0:T(8,128)(2,1)S(1)} %pad_maximum_fusion.12), channel_id=1, source_target_pairs={{0,6},{1,7},{2,4},{3,5},{4,2},{5,3},{6,0},{7,1},{8,14},{9,15},{10,... | collective-permute-start | bytes 589832 | tf_op jit(solution)/shard_map/ppermute | solution.py:718
  117.3 10.4 %collective-permute-start.27 = (bf16[2,384,128]{2,1,0:T(8,128)(2,1)S(1)}, bf16[2,384,128]{2,1,0:T(8,128)(2,1)S(1)}, u32[]{:S(2)}, u32[]{:S(2)}) collective-permute-start(bf16[2,384,128]{2,1,0:T(8,128)(2,1)S(1)} %pad_maximum_fusion.12), channel_id=1, source_target_pairs={{0,4},{1,5},{2,6},{3,7},{4,0},{5,1},{6,2},{7,3},{8,12},{9,13},{10,... | collective-permute-start | bytes 589832 | tf_op jit(solution)/shard_map/ppermute | solution.py:718
  118.5 9.6 %collective-permute-start.26 = (bf16[2,384,128]{2,1,0:T(8,128)(2,1)S(1)}, bf16[2,384,128]{2,1,0:T(8,128)(2,1)S(1)}, u32[]{:S(2)}, u32[]{:S(2)}) collective-permute-start(bf16[2,384,128]{2,1,0:T(8,128)(2,1)S(1)} %pad_maximum_fusion.12), channel_id=1, source_target_pairs={{0,2},{1,3},{2,0},{3,1},{4,6},{5,7},{6,4},{7,5},{8,10},{9,11},{10,... | collective-permute-start | bytes 589832 | tf_op jit(solution)/shard_map/ppermute | solution.py:718
  128.2 2.4 %collective-permute-start.29 = (bf16[4,2,384,128]{3,2,1,0:T(8,128)(2,1)S(1)}, bf16[4,2,384,128]{3,2,1,0:T(8,128)(2,1)S(1)}, u32[]{:S(2)}, u32[]{:S(2)}) collective-permute-start(bf16[4,2,384,128]{3,2,1,0:T(8,128)(2,1)S(1)} %pad_maximum_fusion.1.same), channel_id=1, source_target_pairs={{0,1},{1,0},{2,3},{3,2},{4,5},{5,4},{6,7},{7,6},{8,9},{9,8},{10,11... | collective-permute-start | bytes 2359304 | tf_op jit(solution)/shard_map/ppermute | solution.py:718
  130.6 1.0 copy-start.2

commit v18 on v17

--- a/solution.py
+++ b/solution.py
@@ -769,17 +769,17 @@
     back = sum(block.astype(jnp.float32) for block in back)
     base = after(base, *partial_sums)
     base = [base, swap(base, 2), swap(base, 4)]
-    own_rank = swap(after(back[1].astype(jnp.bfloat16), *base), 1)
+    own_rank = swap(after(back[1].astype(jnp.bfloat16), base[1]), 1)
     own_rank = back[0] + own_rank.astype(jnp.float32)
     own_rank = own_rank.astype(jnp.bfloat16)
     ups = along_z(after(ups, *partial_sums))
     all_rank = own_rank[:, ADAPTER_RANK:]
-    base = jnp.stack(base + [swap(after(base[2], own_rank), 2)])
     own, across = settle(
         stretch_adapter, elsewhere, adapter_owner, near, after(far, own_rank)
     )
     ends = jnp.stack([own, swap(across, 2 * PIECES)])
     all_rank = jnp.stack([all_rank, swap(all_rank, PIECES)])
+    base = jnp.stack(base + [swap(after(base[2], all_rank), 2)])
     all_rank = after(all_rank, ups)
     ups = along_x(after(ups, all_rank))
     all_rank = jnp.stack([swap(all_rank, apart) if apart else all_rank for apart in (0, 2, 4, 6)])

time: 135 us -> 136 us (level)
  starting transfers between devices: 40.5 us -> 43 us
  waiting for transfers between devices: 64.2 us -> 62.8 us
    ppermute x30, starting transfers between devices: 35 us -> 37.5 us  [swap(): lax.ppermute(block, ('groups', 'ctx'), [(i, i ^ mask) for i in range(4 *...]
    ppermute x30, waiting for transfers between devices: 62.1 us -> 60.7 us  [swap(): lax.ppermute(block, ('groups', 'ctx'), [(i, i ^ mask) for i in range(4 *...]
  transfers between devices with their start and end apart: 31 -> 31, of which waited for: 19 -> 17; matrix products, arithmetic and copies ran while one was open for 2% -> 2% of each run, Pallas kernels for 7% -> 7%
where the time goes in v18:
time: 136 us
  waiting for transfers between devices  62.8 us (46%)
  starting transfers between devices  43 us (32%)
  Pallas kernels  23.2 us (17%)
  local copies, waits for them, and re-layouts  2.98 us (2%)
  other arithmetic  2.79 us (2%)
    ppermute x30, waiting for transfers between devices, swap(): lax.ppermute(block, ('groups', 'ctx'), [(i, i ^ mask) for i in range(4 *...  60.7 us
    ppermute x30, starting transfers between devices, swap(): lax.ppermute(block, ('groups', 'ctx'), [(i, i ^ mask) for i in range(4 *...  37.5 us
    pallas_call x2, Pallas kernels, attend(): pl.pallas_call(partial(attend_kernel, first_head), grid=(heads,), out_sha...  10.5 us
    all_to_all x1, starting transfers between devices, direct_shards(): spread = lax.all_to_all(packed, 'ctx', 0, 0, axis_index_groups=blocks)  5.5 us
    pallas_call x1, Pallas kernels, pack_row(): pl.pallas_call(partial(pack_kernel, sections), out_shape=jax.ShapeDtypeSt...  5.15 us
    pallas_call x1, Pallas kernels, widen(): pl.pallas_call(widen_kernel, out_shape=jax.ShapeDtypeStruct((attended.sha...  2.98 us
    unnamed x17, local copies, waits for them, and re-layouts  2.79 us
  transfers between devices with their start and end apart: 31, of which 17 were waited for; matrix products, arithmetic and copies ran while one was open for 2% of the time, Pallas kernels for 7%

profile of v18, /device:TPU:0, one launch (start us, length us, event | category | flops | bytes accessed | tf_op | source)
XLA Modules:
  0.0 135.7 jit_solution(15716359425822644752)
XLA Ops:
  0.6 5.2 %shard_map.86.refs_0_ = bf16[8,1312,128]{2,1,0:T(8,128)(2,1)} custom-call(bf16[1,2686976]{1,0:T(2,128)(2,1)} %pool.1), custom_call_target="tpu_custom_call" | custom-call | bytes 8388608 | tf_op jit(solution)/shard_map/pallas_call | solution.py:316
  5.8 5.5 %all-to-all-start = ((bf16[8,1312,128]{2,1,0:T(8,128)(2,1)}), bf16[8,1312,128]{2,1,0:T(8,128)(2,1)}, u32[]{:S(2)}, u32[]{:S(2)}) async-start(bf16[8,1312,128]{2,1,0:T(8,128)(2,1)} %shard_map.86.refs_0_), calls=%async_computation | async-start | bytes 5373952 | tf_op jit(solution)/shard_map/all_to_all | solution.py:757
  11.3 2.2 %collective-permute-start.1 = (s32[2]{0:T(128)S(1)}, s32[2]{0:T(128)S(1)}, u32[]{:S(2)}, u32[]{:S(2)}) collective-permute-start(s32[2]{0:T(128)S(1)} %copy-done.3), channel_id=1, source_target_pairs={{0,16},{1,17},{2,18},{3,19},{4,20},{5,21},{6,22},{7,23},{8,24},{9,... | collective-permute-start | bytes 32 | tf_op jit(solution)/shard_map/ppermute | solution.py:718
  13.5 1.2 copy-done.1
  14.8 0.3 shard_map.87
  15.0 0.1 collective-permute-start.2
  15.1 0.5 copy-done.6
  15.6 2.6 %collective-permute-start = (bf16[64,1024]{1,0:T(8,128)(2,1)S(1)}, bf16[64,1024]{1,0:T(8,128)(2,1)S(1)}, u32[]{:S(2)}, u32[]{:S(2)}) collective-permute-start(bf16[64,1024]{1,0:T(8,128)(2,1)S(1)} %constant_dynamic-update-slice_fusion), channel_id=1, source_target_pairs={{0,8},{1,9},{2,10},{3,11},{4,12},{5,13},{6,14},{7,15},{8,0},{9,1},... | collective-permute-start | bytes 393224 | tf_op jit(solution)/shard_map/ppermute | solution.py:718
  18.4 1.9 %fusion = (f32[1024,64]{1,0:T(8,128)S(1)}, f32[1024,64]{1,0:T(8,128)S(1)}, f32[1024,64]{1,0:T(8,128)S(1)}) fusion(f32[64]{0:T(128)S(1)} %multiply_power_fusion, f32[1024]{0:T(1024)S(1)} %iota_convert_fusion), kind=kLoop, calls=%fused_computation.15 | loop fusion | flops 131072 | bytes 790784 | tf_op jit(solution)/shard_map/neg | solution.py:734
  20.3 0.3 pad_maximum_fusion.2
  20.6 23.5 %collective-permute-done = bf16[64,1024]{1,0:T(8,128)(2,1)S(1)} collective-permute-done((bf16[64,1024]{1,0:T(8,128)(2,1)S(1)}, bf16[64,1024]{1,0:T(8,128)(2,1)S(1)}, u32[]{:S(2)}, u32[]{:S(2)}) %collective-permute-start) | collective-permute-done | bytes 131104 | tf_op jit(solution)/shard_map/ppermute | solution.py:718
  44.1 2.1 %all-to-all-done.spread = bf16[8,1312,128]{2,1,0:T(8,128)(2,1)} async-done(((bf16[8,1312,128]{2,1,0:T(8,128)(2,1)}), bf16[8,1312,128]{2,1,0:T(8,128)(2,1)}, u32[]{:S(2)}, u32[]{:S(2)}) %all-to-all-start) | async-done | bytes 2687008 | tf_op jit(solution)/shard_map/all_to_all | solution.py:757
  46.3 2.1 %shard_map.88 = (bf16[960,128]{1,0:T(8,128)(2,1)S(1)}, bf16[960,128]{1,0:T(8,128)(2,1)S(1)}, bf16[960,128]{1,0:T(8,128)(2,1)S(1)}, bf16[960,128]{1,0:T(8,128)(2,...) custom-call(s32[2]{0:T(128)S(1)} %copy-done.3, s32[2]{0:T(128)S(1)} %collective-permute-done.1.there, ...), custom_call_target="tpu_custom_call" | custom-call | bytes 3145728 | tf_op jit(solution)/shard_map/pallas_call | solution.py:360
  48.4 2.1 %collective-permute-start.3 = (bf16[960,128]{1,0:T(8,128)(2,1)S(1)}, bf16[960,128]{1,0:T(8,128)(2,1)S(1)}, u32[]{:S(2)}, u32[]{:S(2)}) collective-permute-start(bf16[960,128]{1,0:T(8,128)(2,1)S(1)} %get-tuple-element.41), channel_id=1, source_target_pairs={{0,16},{1,17},{2,18},{3,19},{4,20},{5,21},{6,22},{7,23},{8,24},{9,... | collective-permute-start | bytes 737288 | tf_op jit(solution)/shard_map/ppermute | solution.py:718
  50.6 1.3 collective-permute-start.4
  51.9 1.1 collective-permute-start.5
  53.1 1.5 %collective-permute-start.6 = (bf16[2,64,1024]{2,1,0:T(8,128)(2,1)S(1)}, bf16[2,64,1024]{2,1,0:T(8,128)(2,1)S(1)}, u32[]{:S(2)}, u32[]{:S(2)}) collective-permute-start(bf16[2,64,1024]{2,1,0:T(8,128)(2,1)S(1)} %get-tuple-element.48), channel_id=1, source_target_pairs={{0,2},{1,3},{2,0},{3,1},{4,6},{5,7},{6,4},{7,5},{8,10},{9,11},{10,... | collective-permute-start | bytes 786440 | tf_op jit(solution)/shard_map/ppermute | solution.py:718
  54.6 3.0 %collective-permute-start.7 = (bf16[2,64,1024]{2,1,0:T(8,128)(2,1)S(1)}, bf16[2,64,1024]{2,1,0:T(8,128)(2,1)S(1)}, u32[]{:S(2)}, u32[]{:S(2)}) collective-permute-start(bf16[2,64,1024]{2,1,0:T(8,128)(2,1)S(1)} %get-tuple-element.49), channel_id=1, source_target_pairs={{0,4},{1,5},{2,6},{3,7},{4,0},{5,1},{6,2},{7,3},{8,12},{9,13},{10,... | collective-permute-start | bytes 786440 | tf_op jit(solution)/shard_map/ppermute | solution.py:718
  57.7 2.3 %collective-permute-start.8 = (bf16[2,64,1024]{2,1,0:T(8,128)(2,1)S(1)}, bf16[2,64,1024]{2,1,0:T(8,128)(2,1)S(1)}, u32[]{:S(2)}, u32[]{:S(2)}) collective-permute-start(bf16[2,64,1024]{2,1,0:T(8,128)(2,1)S(1)} %get-tuple-element.50), channel_id=1, source_target_pairs={{0,6},{1,7},{2,4},{3,5},{4,2},{5,3},{6,0},{7,1},{8,14},{9,15},{10,... | collective-permute-start | bytes 786440 | tf_op jit(solution)/shard_map/ppermute | solution.py:718
  60.0 11.1 %collective-permute-done.4.refs_2_ = bf16[960,128]{1,0:T(8,128)(2,1)S(1)} collective-permute-done((bf16[960,128]{1,0:T(8,128)(2,1)S(1)}, bf16[960,128]{1,0:T(8,128)(2,1)S(1)}, u32[]{:S(2)}, u32[]{:S(2)}) %collective-permute-start.4) | collective-permute-done | bytes 245792 | tf_op jit(solution)/shard_map/ppermute | solution.py:718
  71.1 3.3 %collective-permute-done.5.refs_3_ = bf16[960,128]{1,0:T(8,128)(2,1)S(1)} collective-permute-done((bf16[960,128]{1,0:T(8,128)(2,1)S(1)}, bf16[960,128]{1,0:T(8,128)(2,1)S(1)}, u32[]{:S(2)}, u32[]{:S(2)}) %collective-permute-start.5) | collective-permute-done | bytes 245792 | tf_op jit(solution)/shard_map/ppermute | solution.py:718
  74.4 1.0 shard_map.89
  75.4 0.1 collective-permute-start.14
  75.5 1.2 collective-permute-done.8.refs_3_
  76.7 0.4 shard_map.90
  77.1 1.6 %collective-permute-start.11 = (bf16[2,64,192]{2,1,0:T(8,128)(2,1)S(1)}, bf16[2,64,192]{2,1,0:T(8,128)(2,1)S(1)}, u32[]{:S(2)}, u32[]{:S(2)}) collective-permute-start(bf16[2,64,192]{2,1,0:T(8,128)(2,1)S(1)} %get-tuple-element.52), channel_id=1, source_target_pairs={{0,2},{1,3},{2,0},{3,1},{4,6},{5,7},{6,4},{7,5},{8,10},{9,11},{10,... | collective-permute-start | bytes 147464 | tf_op jit(solution)/shard_map/ppermute | solution.py:718
  78.7 1.6 %collective-permute-start.12 = (bf16[2,64,192]{2,1,0:T(8,128)(2,1)S(1)}, bf16[2,64,192]{2,1,0:T(8,128)(2,1)S(1)}, u32[]{:S(2)}, u32[]{:S(2)}) collective-permute-start(bf16[2,64,192]{2,1,0:T(8,128)(2,1)S(1)} %get-tuple-element.53), channel_id=1, source_target_pairs={{0,4},{1,5},{2,6},{3,7},{4,0},{5,1},{6,2},{7,3},{8,12},{9,13},{10,... | collective-permute-start | bytes 147464 | tf_op jit(solution)/shard_map/ppermute | solution.py:718
  80.3 0.4 collective-permute-start.13
  80.7 1.5 %collective-permute-start.9 = (bf16[2,64,1024]{2,1,0:T(8,128)(2,1)S(1)}, bf16[2,64,1024]{2,1,0:T(8,128)(2,1)S(1)}, u32[]{:S(2)}, u32[]{:S(2)}) collective-permute-start(bf16[2,64,1024]{2,1,0:T(8,128)(2,1)S(1)} %pad_maximum_fusion.6), channel_id=1, source_target_pairs={{0,2},{1,3},{2,0},{3,1},{4,6},{5,7},{6,4},{7,5},{8,10},{9,11},{10,... | collective-permute-start | bytes 786440 | tf_op jit(solution)/shard_map/ppermute | solution.py:718
  82.2 4.4 %collective-permute-done.12 = bf16[2,64,192]{2,1,0:T(8,128)(2,1)S(1)} collective-permute-done((bf16[2,64,192]{2,1,0:T(8,128)(2,1)S(1)}, bf16[2,64,192]{2,1,0:T(8,128)(2,1)S(1)}, u32[]{:S(2)}, u32[]{:S(2)}) %collective-permute-start.12) | collective-permute-done | bytes 49184 | tf_op jit(solution)/shard_map/ppermute | solution.py:718
  86.6 1.2 collective-permute-done.13
  87.8 1.3 collective-permute-done.9
  89.1 1.1 collective-permute-start.10
  90.2 0.1 collective-permute-done.15
  90.3 0.1 slice_bitcast_fusion.1
  90.4 1.8 %collective-permute-start.16 = (bf16[64,128]{1,0:T(8,128)(2,1)S(1)}, bf16[64,128]{1,0:T(8,128)(2,1)S(1)}, u32[]{:S(2)}, u32[]{:S(2)}) collective-permute-start(bf16[64,128]{1,0:T(8,128)(2,1)S(1)} %get-tuple-element.85), channel_id=1, source_target_pairs={{0,8},{1,9},{2,10},{3,11},{4,12},{5,13},{6,14},{7,15},{8,0},{9,1},... | collective-permute-start | bytes 49160 | tf_op jit(solution)/shard_map/ppermute | solution.py:718
  92.2 1.2 collective-permute-start.18
  93.4 3.8 %collective-permute-done.16 = bf16[64,128]{1,0:T(8,128)(2,1)S(1)} collective-permute-done((bf16[64,128]{1,0:T(8,128)(2,1)S(1)}, bf16[64,128]{1,0:T(8,128)(2,1)S(1)}, u32[]{:S(2)}, u32[]{:S(2)}) %collective-permute-start.16) | collective-permute-done | bytes 16416 | tf_op jit(solution)/shard_map/ppermute | solution.py:718
  97.2 1.4 %collective-permute-done.10 = bf16[2,64,1024]{2,1,0:T(8,128)(2,1)S(1)} collective-permute-done((bf16[2,64,1024]{2,1,0:T(8,128)(2,1)S(1)}, bf16[2,64,1024]{2,1,0:T(8,128)(2,1)S(1)}, u32[]{:S(2)}, u32[]{:S(2)}) %collective-permute-start.10) | collective-permute-done | bytes 262176 | tf_op jit(solution)/shard_map/ppermute | solution.py:718
  98.6 1.4 %collective-permute-start.17 = (bf16[2,64,1024]{2,1,0:T(8,128)(2,1)S(1)}, bf16[2,64,1024]{2,1,0:T(8,128)(2,1)S(1)}, u32[]{:S(2)}, u32[]{:S(2)}) collective-permute-start(bf16[2,64,1024]{2,1,0:T(8,128)(2,1)S(1)} %collective-permute-done.10), channel_id=1, source_target_pairs={{0,2},{1,3},{2,0},{3,1},{4,6},{5,7},{6,4},{7,5},{8,10},{9,11},{10,... | collective-permute-start | bytes 786440 | tf_op jit(solution)/shard_map/ppermute | solution.py:718
  100.0 0.3 collective-permute-done.18
  100.3 2.0 %collective-permute-start.21 = (bf16[2,64,128]{2,1,0:T(8,128)(2,1)S(1)}, bf16[2,64,128]{2,1,0:T(8,128)(2,1)S(1)}, u32[]{:S(2)}, u32[]{:S(2)}) collective-permute-start(bf16[2,64,128]{2,1,0:T(8,128)(2,1)S(1)} %pad_maximum_fusion.14), channel_id=1, source_target_pairs={{0,6},{1,7},{2,4},{3,5},{4,2},{5,3},{6,0},{7,1},{8,14},{9,15},{10,... | collective-permute-start | bytes 98312 | tf_op jit(solution)/shard_map/ppermute | solution.py:718
  102.3 0.9 collective-permute-start.20
  103.2 0.6 collective-permute-start.19
  103.9 0.8 shard_map.91
  104.7 1.8 %collective-permute-start.24 = (bf16[384,128]{1,0:T(8,128)(2,1)S(1)}, bf16[384,128]{1,0:T(8,128)(2,1)S(1)}, u32[]{:S(2)}, u32[]{:S(2)}) collective-permute-start(bf16[384,128]{1,0:T(8,128)(2,1)S(1)} %get-tuple-element.72), channel_id=1, source_target_pairs={{0,16},{1,17},{2,18},{3,19},{4,20},{5,21},{6,22},{7,23},{8,24},{9,... | collective-permute-start | bytes 294920 | tf_op jit(solution)/shard_map/ppermute | solution.py:718
  106.5 1.4 %collective-permute-start.23 = (bf16[2,2,192,128]{3,2,1,0:T(8,128)(2,1)S(1)}, bf16[2,2,192,128]{3,2,1,0:T(8,128)(2,1)S(1)}, u32[]{:S(2)}, u32[]{:S(2)}) collective-permute-start(bf16[2,2,192,128]{3,2,1,0:T(8,128)(2,1)S(1)} %pad_maximum_fusion.11), channel_id=1, source_target_pairs={{0,2},{1,3},{2,0},{3,1},{4,6},{5,7},{6,4},{7,5},{8,10},{9,11},{10,... | collective-permute-start | bytes 589832 | tf_op jit(solution)/shard_map/ppermute | solution.py:718
  107.9 0.1 pad_maximum_fusion.key_same.value_same
  108.0 0.1 collective-permute-start.22
  108.1 1.2 collective-permute-done.24
  109.4 2.8 %collective-permute-done.23 = bf16[2,2,192,128]{3,2,1,0:T(8,128)(2,1)S(1)} collective-permute-done((bf16[2,2,192,128]{3,2,1,0:T(8,128)(2,1)S(1)}, bf16[2,2,192,128]{3,2,1,0:T(8,128)(2,1)S(1)}, u32[]{:S(2)}, u32[]{:S(2)}) %collective-permute-start.23) | collective-permute-done | bytes 196640 | tf_op jit(solution)/shard_map/ppermute | solution.py:718
  112.3 0.1 collective-permute-start.25
  112.3 1.9 %collective-permute-done.25.rows_other = bf16[2048,128]{1,0:T(8,128)(2,1)S(1)} collective-permute-done((bf16[2048,128]{1,0:T(8,128)(2,1)S(1)}, bf16[2048,128]{1,0:T(8,128)(2,1)S(1)}, u32[]{:S(2)}, u32[]{:S(2)}) %collective-permute-start.25) | collective-permute-done | bytes 524320 | tf_op jit(solution)/shard_map/ppermute | solution.py:718
  114.2 2.9 %shard_map.92.refs_0_ = bf16[64,4096]{1,0:T(8,128)(2,1)} custom-call(bf16[64,4096]{1,0:T(8,128)(2,1)S(1)} %copy-done.5, bf16[4,2,64,1024]{3,2,1,0:T(8,128)(2,1)S(1)} %pad_maximum_fusion.key_same.value_same, bf16[4,2,64,1024]{3,2,1,0:T(8,128)(2,1)S(1)} %collective-permute-done.22.key_other.value_other, ...), custom_call_target="tpu_custom_call" | custom-call | flops 3221225472 | bytes 10485760 | tf_op jit(solution)/shard_map/pallas_call | solution.py:641
  117.1 1.9 %collective-permute-start.28 = (bf16[2,384,128]{2,1,0:T(8,128)(2,1)S(1)}, bf16[2,384,128]{2,1,0:T(8,128)(2,1)S(1)}, u32[]{:S(2)}, u32[]{:S(2)}) collective-permute-start(bf16[2,384,128]{2,1,0:T(8,128)(2,1)S(1)} %pad_maximum_fusion.12), channel_id=1, source_target_pairs={{0,6},{1,7},{2,4},{3,5},{4,2},{5,3},{6,0},{7,1},{8,14},{9,15},{10,... | collective-permute-start | bytes 589832 | tf_op jit(solution)/shard_map/ppermute | solution.py:718
  119.0 0.9 collective-permute-start.27
  120.0 0.6 collective-permute-start.26
  120.6 7.6 %shard_map.93.attended = bf16[64,4096]{1,0:T(8,128)(2,1)} custom-call(bf16[64,4096]{1,0:T(8,128)(2,1)S(1)} %copy-done.5, bf16[4,2,64,1024]{3,2,1,0:T(8,128)(2,1)S(1)} %pad_maximum_fusion.key_same.value_same, bf16[4,2,64,1024]{3,2,1,0:T(8,128)(2,1)S(1)} %collective-permute-done.22.key_other.value_other, ...), custom_call_target="tpu_custom_call", output_to_operand_aliasing={{}: (10, {})} | custom-call | flops 9663676416 | bytes 10485760 | tf_op jit(solution)/shard_map/pallas_call | solution.py:641
  128.2 0.9 collective-permute-done.27
  129.2 0.1 pad_maximum_fusion.1.same
  129.3 0.1 collective-permute-start.29
  129.4 2.3 %collective-permute-done.29.other = bf16[4,2,384,128]{3,2,1,0:T(8,128)(2,1)S(1)} collective-permute-done((bf16[4,2,384,128]{3,2,1,0:T(8,128)(2,1)S(1)}, bf16[4,2,384,128]{3,2,1,0:T(8,128)(2,1)S(1)}, u32[]{:S(2)}, u32[]{:S(2)}) %collective-permute-start.29) | collective-permute-done | bytes 786464 | tf_op jit(solution)/shard_map/ppermute | solution.py:718
  131.6 1.0 copy-done.2
  132.7 3.0 %shard_map.94 = bf16[64,8192]{1,0:T(8,128)(2,1)} custom-call(bf16[64,4096]{1,0:T(8,128)(2,1)S(1)} %copy-done.2, bf16[4,2,384,128]{3,2,1,0:T(8,128)(2,1)S(1)} %pad_maximum_fusion.1.same, bf16[4,2,384,128]{3,2,1,0:T(8,128)(2,1)S(1)} %collective-permute-done.29.other), custom_call_target="tpu_custom_call" | custom-call | flops 134217728 | bytes 4194304 | tf_op jit(solution)/shard_map/pallas_call | solution.py:703
  (47 shorter events, 0.6 us)
Async XLA Ops:
  5.8 5.5 %copy-start.3 = (s32[2]{0:T(128)S(1)}, s32[2]{0:T(128)}, u32[]{:S(2)}) copy-start(s32[2]{0:T(128)} %here.5) | copy-start | bytes 28
  5.8 7.7 %copy-start = (bf16[8,1312,128]{2,1,0:T(8,128)(2,1)S(1)}, bf16[8,1312,128]{2,1,0:T(8,128)(2,1)}, u32[]{:S(2)}) copy-start(bf16[8,1312,128]{2,1,0:T(8,128)(2,1)} %shard_map.86.refs_0_) | copy-start | bytes 8060932
  5.8 40.5 %all-to-all-start = ((bf16[8,1312,128]{2,1,0:T(8,128)(2,1)}), bf16[8,1312,128]{2,1,0:T(8,128)(2,1)}, u32[]{:S(2)}, u32[]{:S(2)}) async-start(bf16[8,1312,128]{2,1,0:T(8,128)(2,1)} %shard_map.86.refs_0_), calls=%async_computation | async-start | bytes 5373952 | tf_op jit(solution)/shard_map/all_to_all | solution.py:757
  11.3 35.0 %collective-permute-start.1 = (s32[2]{0:T(128)S(1)}, s32[2]{0:T(128)S(1)}, u32[]{:S(2)}, u32[]{:S(2)}) collective-permute-start(s32[2]{0:T(128)S(1)} %copy-done.3), channel_id=1, source_target_pairs={{0,16},{1,17},{2,18},{3,19},{4,20},{5,21},{6,22},{7,23},{8,24},{9,... | collective-permute-start | bytes 32 | tf_op jit(solution)/shard_map/ppermute | solution.py:718
  13.5 1.2 copy-start.1
  14.8 0.8 copy-start.6
  14.8 0.9 copy-start.7
  15.0 29.1 %collective-permute-start.2 = (bf16[4,64,1024]{2,1,0:T(8,128)(2,1)S(1)}, bf16[4,64,1024]{2,1,0:T(8,128)(2,1)S(1)}, u32[]{:S(2)}, u32[]{:S(2)}) collective-permute-start(bf16[4,64,1024]{2,1,0:T(8,128)(2,1)S(1)} %get-tuple-element.39), channel_id=1, source_target_pairs={{0,1},{1,0},{2,3},{3,2},{4,5},{5,4},{6,7},{7,6},{8,9},{9,8},{10,11... | collective-permute-start | bytes 1572872 | tf_op jit(solution)/shard_map/ppermute | solution.py:718
  15.6 28.4 %collective-permute-start = (bf16[64,1024]{1,0:T(8,128)(2,1)S(1)}, bf16[64,1024]{1,0:T(8,128)(2,1)S(1)}, u32[]{:S(2)}, u32[]{:S(2)}) collective-permute-start(bf16[64,1024]{1,0:T(8,128)(2,1)S(1)} %constant_dynamic-update-slice_fusion), channel_id=1, source_target_pairs={{0,8},{1,9},{2,10},{3,11},{4,12},{5,13},{6,14},{7,15},{8,0},{9,1},... | collective-permute-start | bytes 393224 | tf_op jit(solution)/shard_map/ppermute | solution.py:718
  18.3 28.0 %copy-start.4 = (s32[16]{0:T(128)S(1)}, s32[16]{0:T(128)}, u32[]{:S(2)}) copy-start(s32[16]{0:T(128)} %owner.5) | copy-start | bytes 196
  48.4 9.2 %collective-permute-start.3 = (bf16[960,128]{1,0:T(8,128)(2,1)S(1)}, bf16[960,128]{1,0:T(8,128)(2,1)S(1)}, u32[]{:S(2)}, u32[]{:S(2)}) collective-permute-start(bf16[960,128]{1,0:T(8,128)(2,1)S(1)} %get-tuple-element.41), channel_id=1, source_target_pairs={{0,16},{1,17},{2,18},{3,19},{4,20},{5,21},{6,22},{7,23},{8,24},{9,... | collective-permute-start | bytes 737288 | tf_op jit(solution)/shard_map/ppermute | solution.py:718
  50.6 20.5 %collective-permute-start.4 = (bf16[960,128]{1,0:T(8,128)(2,1)S(1)}, bf16[960,128]{1,0:T(8,128)(2,1)S(1)}, u32[]{:S(2)}, u32[]{:S(2)}) collective-permute-start(bf16[960,128]{1,0:T(8,128)(2,1)S(1)} %get-tuple-element.43), channel_id=1, source_target_pairs={{0,8},{1,9},{2,10},{3,11},{4,12},{5,13},{6,14},{7,15},{8,0},{9,1},... | collective-permute-start | bytes 737288 | tf_op jit(solution)/shard_map/ppermute | solution.py:718
  51.9 22.5 %collective-permute-start.5 = (bf16[960,128]{1,0:T(8,128)(2,1)S(1)}, bf16[960,128]{1,0:T(8,128)(2,1)S(1)}, u32[]{:S(2)}, u32[]{:S(2)}) collective-permute-start(bf16[960,128]{1,0:T(8,128)(2,1)S(1)} %get-tuple-element.44), channel_id=1, source_target_pairs={{0,24},{1,25},{2,26},{3,27},{4,28},{5,29},{6,30},{7,31},{8,16},{9,... | collective-permute-start | bytes 737288 | tf_op jit(solution)/shard_map/ppermute | solution.py:718
  53.1 22.4 %collective-permute-start.6 = (bf16[2,64,1024]{2,1,0:T(8,128)(2,1)S(1)}, bf16[2,64,1024]{2,1,0:T(8,128)(2,1)S(1)}, u32[]{:S(2)}, u32[]{:S(2)}) collective-permute-start(bf16[2,64,1024]{2,1,0:T(8,128)(2,1)S(1)} %get-tuple-element.48), channel_id=1, source_target_pairs={{0,2},{1,3},{2,0},{3,1},{4,6},{5,7},{6,4},{7,5},{8,10},{9,11},{10,... | collective-permute-start | bytes 786440 | tf_op jit(solution)/shard_map/ppermute | solution.py:718
  54.6 20.8 %collective-permute-start.7 = (bf16[2,64,1024]{2,1,0:T(8,128)(2,1)S(1)}, bf16[2,64,1024]{2,1,0:T(8,128)(2,1)S(1)}, u32[]{:S(2)}, u32[]{:S(2)}) collective-permute-start(bf16[2,64,1024]{2,1,0:T(8,128)(2,1)S(1)} %get-tuple-element.49), channel_id=1, source_target_pairs={{0,4},{1,5},{2,6},{3,7},{4,0},{5,1},{6,2},{7,3},{8,12},{9,13},{10,... | collective-permute-start | bytes 786440 | tf_op jit(solution)/shard_map/ppermute | solution.py:718
  57.7 19.0 %collective-permute-start.8 = (bf16[2,64,1024]{2,1,0:T(8,128)(2,1)S(1)}, bf16[2,64,1024]{2,1,0:T(8,128)(2,1)S(1)}, u32[]{:S(2)}, u32[]{:S(2)}) collective-permute-start(bf16[2,64,1024]{2,1,0:T(8,128)(2,1)S(1)} %get-tuple-element.50), channel_id=1, source_target_pairs={{0,6},{1,7},{2,4},{3,5},{4,2},{5,3},{6,0},{7,1},{8,14},{9,15},{10,... | collective-permute-start | bytes 786440 | tf_op jit(solution)/shard_map/ppermute | solution.py:718
  75.4 12.4 %collective-permute-start.14 = (bf16[2,384,128]{2,1,0:T(8,128)(2,1)S(1)}, bf16[2,384,128]{2,1,0:T(8,128)(2,1)S(1)}, u32[]{:S(2)}, u32[]{:S(2)}) collective-permute-start(bf16[2,384,128]{2,1,0:T(8,128)(2,1)S(1)} %get-tuple-element.57), channel_id=1, source_target_pairs={{0,8},{1,9},{2,10},{3,11},{4,12},{5,13},{6,14},{7,15},{8,0},{9,1},... | collective-permute-start | bytes 589832 | tf_op jit(solution)/shard_map/ppermute | solution.py:718
  77.1 5.0 %collective-permute-start.11 = (bf16[2,64,192]{2,1,0:T(8,128)(2,1)S(1)}, bf16[2,64,192]{2,1,0:T(8,128)(2,1)S(1)}, u32[]{:S(2)}, u32[]{:S(2)}) collective-permute-start(bf16[2,64,192]{2,1,0:T(8,128)(2,1)S(1)} %get-tuple-element.52), channel_id=1, source_target_pairs={{0,2},{1,3},{2,0},{3,1},{4,6},{5,7},{6,4},{7,5},{8,10},{9,11},{10,... | collective-permute-start | bytes 147464 | tf_op jit(solution)/shard_map/ppermute | solution.py:718
  78.7 7.9 %collective-permute-start.12 = (bf16[2,64,192]{2,1,0:T(8,128)(2,1)S(1)}, bf16[2,64,192]{2,1,0:T(8,128)(2,1)S(1)}, u32[]{:S(2)}, u32[]{:S(2)}) collective-permute-start(bf16[2,64,192]{2,1,0:T(8,128)(2,1)S(1)} %get-tuple-element.53), channel_id=1, source_target_pairs={{0,4},{1,5},{2,6},{3,7},{4,0},{5,1},{6,2},{7,3},{8,12},{9,13},{10,... | collective-permute-start | bytes 147464 | tf_op jit(solution)/shard_map/ppermute | solution.py:718
  80.3 7.4 %collective-permute-start.13 = (bf16[2,64,192]{2,1,0:T(8,128)(2,1)S(1)}, bf16[2,64,192]{2,1,0:T(8,128)(2,1)S(1)}, u32[]{:S(2)}, u32[]{:S(2)}) collective-permute-start(bf16[2,64,192]{2,1,0:T(8,128)(2,1)S(1)} %get-tuple-element.54), channel_id=1, source_target_pairs={{0,6},{1,7},{2,4},{3,5},{4,2},{5,3},{6,0},{7,1},{8,14},{9,15},{10,... | collective-permute-start | bytes 147464 | tf_op jit(solution)/shard_map/ppermute | solution.py:718
  80.7 8.4 %collective-permute-start.9 = (bf16[2,64,1024]{2,1,0:T(8,128)(2,1)S(1)}, bf16[2,64,1024]{2,1,0:T(8,128)(2,1)S(1)}, u32[]{:S(2)}, u32[]{:S(2)}) collective-permute-start(bf16[2,64,1024]{2,1,0:T(8,128)(2,1)S(1)} %pad_maximum_fusion.6), channel_id=1, source_target_pairs={{0,2},{1,3},{2,0},{3,1},{4,6},{5,7},{6,4},{7,5},{8,10},{9,11},{10,... | collective-permute-start | bytes 786440 | tf_op jit(solution)/shard_map/ppermute | solution.py:718
  89.1 1.2 collective-permute-start.15
  89.1 9.5 %collective-permute-start.10 = (bf16[2,64,1024]{2,1,0:T(8,128)(2,1)S(1)}, bf16[2,64,1024]{2,1,0:T(8,128)(2,1)S(1)}, u32[]{:S(2)}, u32[]{:S(2)}) collective-permute-start(bf16[2,64,1024]{2,1,0:T(8,128)(2,1)S(1)} %pad_maximum_fusion.6), channel_id=1, source_target_pairs={{0,4},{1,5},{2,6},{3,7},{4,0},{5,1},{6,2},{7,3},{8,12},{9,13},{10,... | collective-permute-start | bytes 786440 | tf_op jit(solution)/shard_map/ppermute | solution.py:718
  90.4 6.8 %collective-permute-start.16 = (bf16[64,128]{1,0:T(8,128)(2,1)S(1)}, bf16[64,128]{1,0:T(8,128)(2,1)S(1)}, u32[]{:S(2)}, u32[]{:S(2)}) collective-permute-start(bf16[64,128]{1,0:T(8,128)(2,1)S(1)} %get-tuple-element.85), channel_id=1, source_target_pairs={{0,8},{1,9},{2,10},{3,11},{4,12},{5,13},{6,14},{7,15},{8,0},{9,1},... | collective-permute-start | bytes 49160 | tf_op jit(solution)/shard_map/ppermute | solution.py:718
  92.2 8.1 %collective-permute-start.18 = (bf16[2,192,128]{2,1,0:T(8,128)(2,1)S(1)}, bf16[2,192,128]{2,1,0:T(8,128)(2,1)S(1)}, u32[]{:S(2)}, u32[]{:S(2)}) collective-permute-start(bf16[2,192,128]{2,1,0:T(8,128)(2,1)S(1)} %get-tuple-element.65), channel_id=1, source_target_pairs={{0,4},{1,5},{2,6},{3,7},{4,0},{5,1},{6,2},{7,3},{8,12},{9,13},{10,... | collective-permute-start | bytes 294920 | tf_op jit(solution)/shard_map/ppermute | solution.py:718
  98.6 9.3 %collective-permute-start.17 = (bf16[2,64,1024]{2,1,0:T(8,128)(2,1)S(1)}, bf16[2,64,1024]{2,1,0:T(8,128)(2,1)S(1)}, u32[]{:S(2)}, u32[]{:S(2)}) collective-permute-start(bf16[2,64,1024]{2,1,0:T(8,128)(2,1)S(1)} %collective-permute-done.10), channel_id=1, source_target_pairs={{0,2},{1,3},{2,0},{3,1},{4,6},{5,7},{6,4},{7,5},{8,10},{9,11},{10,... | collective-permute-start | bytes 786440 | tf_op jit(solution)/shard_map/ppermute | solution.py:718
  100.3 6.1 %collective-permute-start.21 = (bf16[2,64,128]{2,1,0:T(8,128)(2,1)S(1)}, bf16[2,64,128]{2,1,0:T(8,128)(2,1)S(1)}, u32[]{:S(2)}, u32[]{:S(2)}) collective-permute-start(bf16[2,64,128]{2,1,0:T(8,128)(2,1)S(1)} %pad_maximum_fusion.14), channel_id=1, source_target_pairs={{0,6},{1,7},{2,4},{3,5},{4,2},{5,3},{6,0},{7,1},{8,14},{9,15},{10,... | collective-permute-start | bytes 98312 | tf_op jit(solution)/shard_map/ppermute | solution.py:718
  102.3 5.6 %collective-permute-start.20 = (bf16[2,64,128]{2,1,0:T(8,128)(2,1)S(1)}, bf16[2,64,128]{2,1,0:T(8,128)(2,1)S(1)}, u32[]{:S(2)}, u32[]{:S(2)}) collective-permute-start(bf16[2,64,128]{2,1,0:T(8,128)(2,1)S(1)} %pad_maximum_fusion.14), channel_id=1, source_target_pairs={{0,4},{1,5},{2,6},{3,7},{4,0},{5,1},{6,2},{7,3},{8,12},{9,13},{10,... | collective-permute-start | bytes 98312 | tf_op jit(solution)/shard_map/ppermute | solution.py:718
  103.2 4.6 %collective-permute-start.19 = (bf16[2,64,128]{2,1,0:T(8,128)(2,1)S(1)}, bf16[2,64,128]{2,1,0:T(8,128)(2,1)S(1)}, u32[]{:S(2)}, u32[]{:S(2)}) collective-permute-start(bf16[2,64,128]{2,1,0:T(8,128)(2,1)S(1)} %pad_maximum_fusion.14), channel_id=1, source_target_pairs={{0,2},{1,3},{2,0},{3,1},{4,6},{5,7},{6,4},{7,5},{8,10},{9,11},{10,... | collective-permute-start | bytes 98312 | tf_op jit(solution)/shard_map/ppermute | solution.py:718
  104.7 4.7 %collective-permute-start.24 = (bf16[384,128]{1,0:T(8,128)(2,1)S(1)}, bf16[384,128]{1,0:T(8,128)(2,1)S(1)}, u32[]{:S(2)}, u32[]{:S(2)}) collective-permute-start(bf16[384,128]{1,0:T(8,128)(2,1)S(1)} %get-tuple-element.72), channel_id=1, source_target_pairs={{0,16},{1,17},{2,18},{3,19},{4,20},{5,21},{6,22},{7,23},{8,24},{9,... | collective-permute-start | bytes 294920 | tf_op jit(solution)/shard_map/ppermute | solution.py:718
  106.5 5.7 %collective-permute-start.23 = (bf16[2,2,192,128]{3,2,1,0:T(8,128)(2,1)S(1)}, bf16[2,2,192,128]{3,2,1,0:T(8,128)(2,1)S(1)}, u32[]{:S(2)}, u32[]{:S(2)}) collective-permute-start(bf16[2,2,192,128]{3,2,1,0:T(8,128)(2,1)S(1)} %pad_maximum_fusion.11), channel_id=1, source_target_pairs={{0,2},{1,3},{2,0},{3,1},{4,6},{5,7},{6,4},{7,5},{8,10},{9,11},{10,... | collective-permute-start | bytes 589832 | tf_op jit(solution)/shard_map/ppermute | solution.py:718
  107.9 6.4 %copy-start.5 = (bf16[64,4096]{1,0:T(8,128)(2,1)S(1)}, bf16[64,4096]{1,0:T(8,128)(2,1)}, u32[]{:S(2)}) copy-start(bf16[64,4096]{1,0:T(8,128)(2,1)} %query_block.3) | copy-start | bytes 1572868
  108.0 6.2 %collective-permute-start.22 = (bf16[4,2,64,1024]{3,2,1,0:T(8,128)(2,1)S(1)}, bf16[4,2,64,1024]{3,2,1,0:T(8,128)(2,1)S(1)}, u32[]{:S(2)}, u32[]{:S(2)}) collective-permute-start(bf16[4,2,64,1024]{3,2,1,0:T(8,128)(2,1)S(1)} %pad_maximum_fusion.key_same.value_same), channel_id=1, source_target_pairs={{0,1},{1,0},{2,3},{3,2},{4,5},{5,4},{6,7},{7,6},{8,9},{9,8},{10,11... | collective-permute-start | bytes 3145736 | tf_op jit(solution)/shard_map/ppermute | solution.py:718
  112.3 2.0 %collective-permute-start.25 = (bf16[2048,128]{1,0:T(8,128)(2,1)S(1)}, bf16[2048,128]{1,0:T(8,128)(2,1)S(1)}, u32[]{:S(2)}, u32[]{:S(2)}) collective-permute-start(bf16[2048,128]{1,0:T(8,128)(2,1)S(1)} %pad_maximum_fusion.4.rows_same), channel_id=1, source_target_pairs={{0,1},{1,0},{2,3},{3,2},{4,5},{5,4},{6,7},{7,6},{8,9},{9,8},{10,11... | collective-permute-start | bytes 1572872 | tf_op jit(solution)/shard_map/ppermute | solution.py:718
  117.1 11.1 %collective-permute-start.28 = (bf16[2,384,128]{2,1,0:T(8,128)(2,1)S(1)}, bf16[2,384,128]{2,1,0:T(8,128)(2,1)S(1)}, u32[]{:S(2)}, u32[]{:S(2)}) collective-permute-start(bf16[2,384,128]{2,1,0:T(8,128)(2,1)S(1)} %pad_maximum_fusion.12), channel_id=1, source_target_pairs={{0,6},{1,7},{2,4},{3,5},{4,2},{5,3},{6,0},{7,1},{8,14},{9,15},{10,... | collective-permute-start | bytes 589832 | tf_op jit(solution)/shard_map/ppermute | solution.py:718
  119.0 10.1 %collective-permute-start.27 = (bf16[2,384,128]{2,1,0:T(8,128)(2,1)S(1)}, bf16[2,384,128]{2,1,0:T(8,128)(2,1)S(1)}, u32[]{:S(2)}, u32[]{:S(2)}) collective-permute-start(bf16[2,384,128]{2,1,0:T(8,128)(2,1)S(1)} %pad_maximum_fusion.12), channel_id=1, source_target_pairs={{0,4},{1,5},{2,6},{3,7},{4,0},{5,1},{6,2},{7,3},{8,12},{9,13},{10,... | collective-permute-start | bytes 589832 | tf_op jit(solution)/shard_map/ppermute | solution.py:718
  120.0 9.2 %collective-permute-start.26 = (bf16[2,384,128]{2,1,0:T(8,128)(2,1)S(1)}, bf16[2,384,128]{2,1,0:T(8,128)(2,1)S(1)}, u32[]{:S(2)}, u32[]{:S(2)}) collective-permute-start(bf16[2,384,128]{2,1,0:T(8,128)(2,1)S(1)} %pad_maximum_fusion.12), channel_id=1, source_target_pairs={{0,2},{1,3},{2,0},{3,1},{4,6},{5,7},{6,4},{7,5},{8,10},{9,11},{10,... | collective-permute-start | bytes 589832 | tf_op jit(solution)/shard_map/ppermute | solution.py:718
  129.3 2.4 %collective-permute-start.29 = (bf16[4,2,384,128]{3,2,1,0:T(8,128)(2,1)S(1)}, bf16[4,2,384,128]{3,2,1,0:T(8,128)(2,1)S(1)}, u32[]{:S(2)}, u32[]{:S(2)}) collective-permute-start(bf16[4,2,384,128]{3,2,1,0:T(8,128)(2,1)S(1)} %pad_maximum_fusion.1.same), channel_id=1, source_target_pairs={{0,1},{1,0},{2,3},{3,2},{4,5},{5,4},{6,7},{7,6},{8,9},{9,8},{10,11... | collective-permute-start | bytes 2359304 | tf_op jit(solution)/shard_map/ppermute | solution.py:718
  131.6 1.0 copy-start.2

commit v19 on v17

--- a/solution.py
+++ b/solution.py
@@ -791,8 +791,7 @@
 
     shared = (query_base, base, own_rank, gathered, cosines, sines)
     attended = attend(0, 1, None, *shared)
-    ends = after(ends, attended)
-    ends = jnp.stack([swap(ends, apart) if apart else ends for apart in (0, 2, 4, 6)])
+    ends = along_x(after(along_z(ends), attended))
     attended = attend(1, KEYVALUE_HEADS - 1, attended, *shared)
     ends = after(ends, attended)
     return attended, widen(attended, ends, swap(ends, 1))

time: 135 us -> 138 us (1.022)
  waiting for transfers between devices: 64.2 us -> 69.8 us
  starting transfers between devices: 40.5 us -> 38.9 us
    ppermute x30 -> x29, waiting for transfers between devices: 62.1 us -> 67.7 us  [swap(): lax.ppermute(block, ('groups', 'ctx'), [(i, i ^ mask) for i in range(4 *...]
    ppermute x30 -> x29, starting transfers between devices: 35 us -> 33.4 us  [swap(): lax.ppermute(block, ('groups', 'ctx'), [(i, i ^ mask) for i in range(4 *...]
  transfers between devices with their start and end apart: 31 -> 30, of which waited for: 19 -> 18; matrix products, arithmetic and copies ran while one was open for 2% -> 2% of each run, Pallas kernels for 7% -> 7%
where the time goes in v19:
time: 138 us
  waiting for transfers between devices  69.8 us (51%)
  starting transfers between devices  38.9 us (28%)
  Pallas kernels  23.2 us (17%)
  other arithmetic  2.81 us (2%)
  local copies, waits for them, and re-layouts  2 us (1%)
    ppermute x29, waiting for transfers between devices, swap(): lax.ppermute(block, ('groups', 'ctx'), [(i, i ^ mask) for i in range(4 *...  67.7 us
    ppermute x29, starting transfers between devices, swap(): lax.ppermute(block, ('groups', 'ctx'), [(i, i ^ mask) for i in range(4 *...  33.4 us
    pallas_call x2, Pallas kernels, attend(): pl.pallas_call(partial(attend_kernel, first_head), grid=(heads,), out_sha...  10.5 us
    all_to_all x1, starting transfers between devices, direct_shards(): spread = lax.all_to_all(packed, 'ctx', 0, 0, axis_index_groups=blocks)  5.5 us
    pallas_call x1, Pallas kernels, pack_row(): pl.pallas_call(partial(pack_kernel, sections), out_shape=jax.ShapeDtypeSt...  5.15 us
    pallas_call x1, Pallas kernels, widen(): pl.pallas_call(widen_kernel, out_shape=jax.ShapeDtypeStruct((attended.sha...  2.98 us
  transfers between devices with their start and end apart: 30, of which 18 were waited for; matrix products, arithmetic and copies ran while one was open for 2% of the time, Pallas kernels for 7%

profile of v19, /device:TPU:0, one launch (start us, length us, event | category | flops | bytes accessed | tf_op | source)
XLA Modules:
  0.0 137.7 jit_solution(250791758146912794)
XLA Ops:
  0.6 5.2 %shard_map.86.refs_0_ = bf16[8,1312,128]{2,1,0:T(8,128)(2,1)} custom-call(bf16[1,2686976]{1,0:T(2,128)(2,1)} %pool.1), custom_call_target="tpu_custom_call" | custom-call | bytes 8388608 | tf_op jit(solution)/shard_map/pallas_call | solution.py:316
  5.8 5.5 %all-to-all-start = ((bf16[8,1312,128]{2,1,0:T(8,128)(2,1)}), bf16[8,1312,128]{2,1,0:T(8,128)(2,1)}, u32[]{:S(2)}, u32[]{:S(2)}) async-start(bf16[8,1312,128]{2,1,0:T(8,128)(2,1)} %shard_map.86.refs_0_), calls=%async_computation | async-start | bytes 5373952 | tf_op jit(solution)/shard_map/all_to_all | solution.py:757
  11.3 2.2 %collective-permute-start.1 = (s32[2]{0:T(128)S(1)}, s32[2]{0:T(128)S(1)}, u32[]{:S(2)}, u32[]{:S(2)}) collective-permute-start(s32[2]{0:T(128)S(1)} %copy-done.3), channel_id=1, source_target_pairs={{0,16},{1,17},{2,18},{3,19},{4,20},{5,21},{6,22},{7,23},{8,24},{9,... | collective-permute-start | bytes 32 | tf_op jit(solution)/shard_map/ppermute | solution.py:718
  13.5 1.2 copy-done.1
  14.8 0.3 shard_map.87
  15.0 0.1 collective-permute-start.2
  15.1 0.5 copy-done.6
  15.6 0.0 copy-done.7
  15.6 2.6 %collective-permute-start = (bf16[64,1024]{1,0:T(8,128)(2,1)S(1)}, bf16[64,1024]{1,0:T(8,128)(2,1)S(1)}, u32[]{:S(2)}, u32[]{:S(2)}) collective-permute-start(bf16[64,1024]{1,0:T(8,128)(2,1)S(1)} %constant_dynamic-update-slice_fusion), channel_id=1, source_target_pairs={{0,8},{1,9},{2,10},{3,11},{4,12},{5,13},{6,14},{7,15},{8,0},{9,1},... | collective-permute-start | bytes 393224 | tf_op jit(solution)/shard_map/ppermute | solution.py:718
  18.4 1.9 %fusion = (f32[1024,64]{1,0:T(8,128)S(1)}, f32[1024,64]{1,0:T(8,128)S(1)}, f32[1024,64]{1,0:T(8,128)S(1)}) fusion(f32[64]{0:T(128)S(1)} %multiply_power_fusion, f32[1024]{0:T(1024)S(1)} %iota_convert_fusion), kind=kLoop, calls=%fused_computation.16 | loop fusion | flops 131072 | bytes 790784 | tf_op jit(solution)/shard_map/neg | solution.py:734
  20.3 0.3 pad_maximum_fusion.2
  20.6 23.5 %collective-permute-done = bf16[64,1024]{1,0:T(8,128)(2,1)S(1)} collective-permute-done((bf16[64,1024]{1,0:T(8,128)(2,1)S(1)}, bf16[64,1024]{1,0:T(8,128)(2,1)S(1)}, u32[]{:S(2)}, u32[]{:S(2)}) %collective-permute-start) | collective-permute-done | bytes 131104 | tf_op jit(solution)/shard_map/ppermute | solution.py:718
  44.1 2.1 %all-to-all-done.spread = bf16[8,1312,128]{2,1,0:T(8,128)(2,1)} async-done(((bf16[8,1312,128]{2,1,0:T(8,128)(2,1)}), bf16[8,1312,128]{2,1,0:T(8,128)(2,1)}, u32[]{:S(2)}, u32[]{:S(2)}) %all-to-all-start) | async-done | bytes 2687008 | tf_op jit(solution)/shard_map/all_to_all | solution.py:757
  46.3 2.1 %shard_map.88 = (bf16[960,128]{1,0:T(8,128)(2,1)S(1)}, bf16[960,128]{1,0:T(8,128)(2,1)S(1)}, bf16[960,128]{1,0:T(8,128)(2,1)S(1)}, bf16[960,128]{1,0:T(8,128)(2,...) custom-call(s32[2]{0:T(128)S(1)} %copy-done.3, s32[2]{0:T(128)S(1)} %collective-permute-done.1.there, ...), custom_call_target="tpu_custom_call" | custom-call | bytes 3145728 | tf_op jit(solution)/shard_map/pallas_call | solution.py:360
  48.4 2.1 %collective-permute-start.3 = (bf16[960,128]{1,0:T(8,128)(2,1)S(1)}, bf16[960,128]{1,0:T(8,128)(2,1)S(1)}, u32[]{:S(2)}, u32[]{:S(2)}) collective-permute-start(bf16[960,128]{1,0:T(8,128)(2,1)S(1)} %get-tuple-element.41), channel_id=1, source_target_pairs={{0,16},{1,17},{2,18},{3,19},{4,20},{5,21},{6,22},{7,23},{8,24},{9,... | collective-permute-start | bytes 737288 | tf_op jit(solution)/shard_map/ppermute | solution.py:718
  50.6 1.3 collective-permute-start.4
  51.9 1.1 collective-permute-start.5
  53.1 1.5 %collective-permute-start.6 = (bf16[2,64,1024]{2,1,0:T(8,128)(2,1)S(1)}, bf16[2,64,1024]{2,1,0:T(8,128)(2,1)S(1)}, u32[]{:S(2)}, u32[]{:S(2)}) collective-permute-start(bf16[2,64,1024]{2,1,0:T(8,128)(2,1)S(1)} %get-tuple-element.48), channel_id=1, source_target_pairs={{0,2},{1,3},{2,0},{3,1},{4,6},{5,7},{6,4},{7,5},{8,10},{9,11},{10,... | collective-permute-start | bytes 786440 | tf_op jit(solution)/shard_map/ppermute | solution.py:718
  54.6 3.0 %collective-permute-start.7 = (bf16[2,64,1024]{2,1,0:T(8,128)(2,1)S(1)}, bf16[2,64,1024]{2,1,0:T(8,128)(2,1)S(1)}, u32[]{:S(2)}, u32[]{:S(2)}) collective-permute-start(bf16[2,64,1024]{2,1,0:T(8,128)(2,1)S(1)} %get-tuple-element.49), channel_id=1, source_target_pairs={{0,4},{1,5},{2,6},{3,7},{4,0},{5,1},{6,2},{7,3},{8,12},{9,13},{10,... | collective-permute-start | bytes 786440 | tf_op jit(solution)/shard_map/ppermute | solution.py:718
  57.7 2.3 %collective-permute-start.8 = (bf16[2,64,1024]{2,1,0:T(8,128)(2,1)S(1)}, bf16[2,64,1024]{2,1,0:T(8,128)(2,1)S(1)}, u32[]{:S(2)}, u32[]{:S(2)}) collective-permute-start(bf16[2,64,1024]{2,1,0:T(8,128)(2,1)S(1)} %get-tuple-element.50), channel_id=1, source_target_pairs={{0,6},{1,7},{2,4},{3,5},{4,2},{5,3},{6,0},{7,1},{8,14},{9,15},{10,... | collective-permute-start | bytes 786440 | tf_op jit(solution)/shard_map/ppermute | solution.py:718
  60.0 11.1 %collective-permute-done.4.refs_2_ = bf16[960,128]{1,0:T(8,128)(2,1)S(1)} collective-permute-done((bf16[960,128]{1,0:T(8,128)(2,1)S(1)}, bf16[960,128]{1,0:T(8,128)(2,1)S(1)}, u32[]{:S(2)}, u32[]{:S(2)}) %collective-permute-start.4) | collective-permute-done | bytes 245792 | tf_op jit(solution)/shard_map/ppermute | solution.py:718
  71.1 3.3 %collective-permute-done.5.refs_3_ = bf16[960,128]{1,0:T(8,128)(2,1)S(1)} collective-permute-done((bf16[960,128]{1,0:T(8,128)(2,1)S(1)}, bf16[960,128]{1,0:T(8,128)(2,1)S(1)}, u32[]{:S(2)}, u32[]{:S(2)}) %collective-permute-start.5) | collective-permute-done | bytes 245792 | tf_op jit(solution)/shard_map/ppermute | solution.py:718
  74.4 1.0 shard_map.89
  75.4 0.1 collective-permute-start.14
  75.5 1.2 collective-permute-done.8.refs_3_
  76.7 0.4 shard_map.90
  77.1 1.6 %collective-permute-start.11 = (bf16[2,64,192]{2,1,0:T(8,128)(2,1)S(1)}, bf16[2,64,192]{2,1,0:T(8,128)(2,1)S(1)}, u32[]{:S(2)}, u32[]{:S(2)}) collective-permute-start(bf16[2,64,192]{2,1,0:T(8,128)(2,1)S(1)} %get-tuple-element.52), channel_id=1, source_target_pairs={{0,2},{1,3},{2,0},{3,1},{4,6},{5,7},{6,4},{7,5},{8,10},{9,11},{10,... | collective-permute-start | bytes 147464 | tf_op jit(solution)/shard_map/ppermute | solution.py:718
  78.7 1.6 %collective-permute-start.12 = (bf16[2,64,192]{2,1,0:T(8,128)(2,1)S(1)}, bf16[2,64,192]{2,1,0:T(8,128)(2,1)S(1)}, u32[]{:S(2)}, u32[]{:S(2)}) collective-permute-start(bf16[2,64,192]{2,1,0:T(8,128)(2,1)S(1)} %get-tuple-element.53), channel_id=1, source_target_pairs={{0,4},{1,5},{2,6},{3,7},{4,0},{5,1},{6,2},{7,3},{8,12},{9,13},{10,... | collective-permute-start | bytes 147464 | tf_op jit(solution)/shard_map/ppermute | solution.py:718
  80.3 0.4 collective-permute-start.13
  80.7 1.5 %collective-permute-start.9 = (bf16[2,64,1024]{2,1,0:T(8,128)(2,1)S(1)}, bf16[2,64,1024]{2,1,0:T(8,128)(2,1)S(1)}, u32[]{:S(2)}, u32[]{:S(2)}) collective-permute-start(bf16[2,64,1024]{2,1,0:T(8,128)(2,1)S(1)} %pad_maximum_fusion.7), channel_id=1, source_target_pairs={{0,2},{1,3},{2,0},{3,1},{4,6},{5,7},{6,4},{7,5},{8,10},{9,11},{10,... | collective-permute-start | bytes 786440 | tf_op jit(solution)/shard_map/ppermute | solution.py:718
  82.2 1.6 %collective-permute-start.10 = (bf16[2,64,1024]{2,1,0:T(8,128)(2,1)S(1)}, bf16[2,64,1024]{2,1,0:T(8,128)(2,1)S(1)}, u32[]{:S(2)}, u32[]{:S(2)}) collective-permute-start(bf16[2,64,1024]{2,1,0:T(8,128)(2,1)S(1)} %pad_maximum_fusion.7), channel_id=1, source_target_pairs={{0,4},{1,5},{2,6},{3,7},{4,0},{5,1},{6,2},{7,3},{8,12},{9,13},{10,... | collective-permute-start | bytes 786440 | tf_op jit(solution)/shard_map/ppermute | solution.py:718
  83.8 3.0 %collective-permute-done.12 = bf16[2,64,192]{2,1,0:T(8,128)(2,1)S(1)} collective-permute-done((bf16[2,64,192]{2,1,0:T(8,128)(2,1)S(1)}, bf16[2,64,192]{2,1,0:T(8,128)(2,1)S(1)}, u32[]{:S(2)}, u32[]{:S(2)}) %collective-permute-start.12) | collective-permute-done | bytes 49184 | tf_op jit(solution)/shard_map/ppermute | solution.py:718
  86.7 1.8 %collective-permute-done.13 = bf16[2,64,192]{2,1,0:T(8,128)(2,1)S(1)} collective-permute-done((bf16[2,64,192]{2,1,0:T(8,128)(2,1)S(1)}, bf16[2,64,192]{2,1,0:T(8,128)(2,1)S(1)}, u32[]{:S(2)}, u32[]{:S(2)}) %collective-permute-start.13) | collective-permute-done | bytes 49184 | tf_op jit(solution)/shard_map/ppermute | solution.py:718
  88.6 0.5 collective-permute-done.9
  89.1 3.8 %collective-permute-done.10 = bf16[2,64,1024]{2,1,0:T(8,128)(2,1)S(1)} collective-permute-done((bf16[2,64,1024]{2,1,0:T(8,128)(2,1)S(1)}, bf16[2,64,1024]{2,1,0:T(8,128)(2,1)S(1)}, u32[]{:S(2)}, u32[]{:S(2)}) %collective-permute-start.10) | collective-permute-done | bytes 262176 | tf_op jit(solution)/shard_map/ppermute | solution.py:718
  92.9 1.2 collective-permute-done.15
  94.1 0.1 slice_bitcast_fusion.1
  94.2 0.8 collective-permute-start.16
  95.0 1.4 %collective-permute-start.17 = (bf16[64,128]{1,0:T(8,128)(2,1)S(1)}, bf16[64,128]{1,0:T(8,128)(2,1)S(1)}, u32[]{:S(2)}, u32[]{:S(2)}) collective-permute-start(bf16[64,128]{1,0:T(8,128)(2,1)S(1)} %get-tuple-element.87), channel_id=1, source_target_pairs={{0,8},{1,9},{2,10},{3,11},{4,12},{5,13},{6,14},{7,15},{8,0},{9,1},... | collective-permute-start | bytes 49160 | tf_op jit(solution)/shard_map/ppermute | solution.py:718
  96.4 1.7 %collective-permute-done.18 = bf16[2,192,128]{2,1,0:T(8,128)(2,1)S(1)} collective-permute-done((bf16[2,192,128]{2,1,0:T(8,128)(2,1)S(1)}, bf16[2,192,128]{2,1,0:T(8,128)(2,1)S(1)}, u32[]{:S(2)}, u32[]{:S(2)}) %collective-permute-start.18) | collective-permute-done | bytes 98336 | tf_op jit(solution)/shard_map/ppermute | solution.py:718
  98.1 1.5 %collective-permute-done.17 = bf16[64,128]{1,0:T(8,128)(2,1)S(1)} collective-permute-done((bf16[64,128]{1,0:T(8,128)(2,1)S(1)}, bf16[64,128]{1,0:T(8,128)(2,1)S(1)}, u32[]{:S(2)}, u32[]{:S(2)}) %collective-permute-start.17) | collective-permute-done | bytes 16416 | tf_op jit(solution)/shard_map/ppermute | solution.py:718
  99.7 1.5 %collective-permute-start.21 = (bf16[2,64,128]{2,1,0:T(8,128)(2,1)S(1)}, bf16[2,64,128]{2,1,0:T(8,128)(2,1)S(1)}, u32[]{:S(2)}, u32[]{:S(2)}) collective-permute-start(bf16[2,64,128]{2,1,0:T(8,128)(2,1)S(1)} %pad_maximum_fusion.15), channel_id=1, source_target_pairs={{0,6},{1,7},{2,4},{3,5},{4,2},{5,3},{6,0},{7,1},{8,14},{9,15},{10,... | collective-permute-start | bytes 98312 | tf_op jit(solution)/shard_map/ppermute | solution.py:718
  101.1 1.2 collective-permute-start.20
  102.3 0.8 collective-permute-start.19
  103.1 0.8 shard_map.91
  103.9 1.5 %collective-permute-start.24 = (bf16[384,128]{1,0:T(8,128)(2,1)S(1)}, bf16[384,128]{1,0:T(8,128)(2,1)S(1)}, u32[]{:S(2)}, u32[]{:S(2)}) collective-permute-start(bf16[384,128]{1,0:T(8,128)(2,1)S(1)} %get-tuple-element.72), channel_id=1, source_target_pairs={{0,16},{1,17},{2,18},{3,19},{4,20},{5,21},{6,22},{7,23},{8,24},{9,... | collective-permute-start | bytes 294920 | tf_op jit(solution)/shard_map/ppermute | solution.py:718
  105.4 1.0 collective-permute-start.23
  106.4 0.2 collective-permute-done.19
  106.6 0.1 pad_maximum_fusion.key_same.value_same
  106.8 0.1 collective-permute-start.22
  106.9 1.8 %collective-permute-done.24 = bf16[384,128]{1,0:T(8,128)(2,1)S(1)} collective-permute-done((bf16[384,128]{1,0:T(8,128)(2,1)S(1)}, bf16[384,128]{1,0:T(8,128)(2,1)S(1)}, u32[]{:S(2)}, u32[]{:S(2)}) %collective-permute-start.24) | collective-permute-done | bytes 98336 | tf_op jit(solution)/shard_map/ppermute | solution.py:718
  108.7 2.4 %collective-permute-done.23 = bf16[2,2,192,128]{3,2,1,0:T(8,128)(2,1)S(1)} collective-permute-done((bf16[2,2,192,128]{3,2,1,0:T(8,128)(2,1)S(1)}, bf16[2,2,192,128]{3,2,1,0:T(8,128)(2,1)S(1)}, u32[]{:S(2)}, u32[]{:S(2)}) %collective-permute-start.23) | collective-permute-done | bytes 196640 | tf_op jit(solution)/shard_map/ppermute | solution.py:718
  111.2 0.1 collective-permute-start.25
  111.3 0.9 collective-permute-start.26
  112.2 6.4 %collective-permute-done.26 = bf16[2,384,128]{2,1,0:T(8,128)(2,1)S(1)} collective-permute-done((bf16[2,384,128]{2,1,0:T(8,128)(2,1)S(1)}, bf16[2,384,128]{2,1,0:T(8,128)(2,1)S(1)}, u32[]{:S(2)}, u32[]{:S(2)}) %collective-permute-start.26) | collective-permute-done | bytes 196640 | tf_op jit(solution)/shard_map/ppermute | solution.py:718
  118.7 2.9 %shard_map.92.refs_0_ = bf16[64,4096]{1,0:T(8,128)(2,1)} custom-call(bf16[64,4096]{1,0:T(8,128)(2,1)S(1)} %copy-done.5, bf16[4,2,64,1024]{3,2,1,0:T(8,128)(2,1)S(1)} %pad_maximum_fusion.key_same.value_same, bf16[4,2,64,1024]{3,2,1,0:T(8,128)(2,1)S(1)} %collective-permute-done.22.key_other.value_other, ...), custom_call_target="tpu_custom_call" | custom-call | flops 3221225472 | bytes 10485760 | tf_op jit(solution)/shard_map/pallas_call | solution.py:641
  121.6 1.0 collective-permute-start.27
  122.6 7.6 %shard_map.93.attended = bf16[64,4096]{1,0:T(8,128)(2,1)} custom-call(bf16[64,4096]{1,0:T(8,128)(2,1)S(1)} %copy-done.5, bf16[4,2,64,1024]{3,2,1,0:T(8,128)(2,1)S(1)} %pad_maximum_fusion.key_same.value_same, bf16[4,2,64,1024]{3,2,1,0:T(8,128)(2,1)S(1)} %collective-permute-done.22.key_other.value_other, ...), custom_call_target="tpu_custom_call", output_to_operand_aliasing={{}: (10, {})} | custom-call | flops 9663676416 | bytes 10485760 | tf_op jit(solution)/shard_map/pallas_call | solution.py:641
  130.2 2.1 %collective-permute-done.27 = bf16[2,2,384,128]{3,2,1,0:T(8,128)(2,1)S(1)} collective-permute-done((bf16[2,2,384,128]{3,2,1,0:T(8,128)(2,1)S(1)}, bf16[2,2,384,128]{3,2,1,0:T(8,128)(2,1)S(1)}, u32[]{:S(2)}, u32[]{:S(2)}) %collective-permute-start.27) | collective-permute-done | bytes 393248 | tf_op jit(solution)/shard_map/ppermute | solution.py:718
  132.2 0.1 pad_maximum_fusion.1
  132.3 0.1 copy.11
  132.4 0.1 collective-permute-start.28
  132.5 2.3 %collective-permute-done.28.other = bf16[4,2,384,128]{3,2,1,0:T(8,128)(2,1)S(1)} collective-permute-done((bf16[4,2,384,128]{3,2,1,0:T(8,128)(2,1)S(1)}, bf16[4,2,384,128]{3,2,1,0:T(8,128)(2,1)S(1)}, u32[]{:S(2)}, u32[]{:S(2)}) %collective-permute-start.28) | collective-permute-done | bytes 786464 | tf_op jit(solution)/shard_map/ppermute | solution.py:718
  134.7 3.0 %shard_map.94 = bf16[64,8192]{1,0:T(8,128)(2,1)} custom-call(bf16[64,4096]{1,0:T(8,128)(2,1)S(1)} %copy-done.2, bf16[4,2,384,128]{3,2,1,0:T(8,128)(2,1)S(1)} %bitcast.36, bf16[4,2,384,128]{3,2,1,0:T(8,128)(2,1)S(1)} %collective-permute-done.28.other), custom_call_target="tpu_custom_call" | custom-call | flops 134217728 | bytes 4194304 | tf_op jit(solution)/shard_map/pallas_call | solution.py:703
  (47 shorter events, 0.5 us)
Async XLA Ops:
  5.8 5.5 %copy-start.3 = (s32[2]{0:T(128)S(1)}, s32[2]{0:T(128)}, u32[]{:S(2)}) copy-start(s32[2]{0:T(128)} %here.5) | copy-start | bytes 28
  5.8 7.7 %copy-start = (bf16[8,1312,128]{2,1,0:T(8,128)(2,1)S(1)}, bf16[8,1312,128]{2,1,0:T(8,128)(2,1)}, u32[]{:S(2)}) copy-start(bf16[8,1312,128]{2,1,0:T(8,128)(2,1)} %shard_map.86.refs_0_) | copy-start | bytes 8060932
  5.8 40.5 %all-to-all-start = ((bf16[8,1312,128]{2,1,0:T(8,128)(2,1)}), bf16[8,1312,128]{2,1,0:T(8,128)(2,1)}, u32[]{:S(2)}, u32[]{:S(2)}) async-start(bf16[8,1312,128]{2,1,0:T(8,128)(2,1)} %shard_map.86.refs_0_), calls=%async_computation | async-start | bytes 5373952 | tf_op jit(solution)/shard_map/all_to_all | solution.py:757
  11.3 35.0 %collective-permute-start.1 = (s32[2]{0:T(128)S(1)}, s32[2]{0:T(128)S(1)}, u32[]{:S(2)}, u32[]{:S(2)}) collective-permute-start(s32[2]{0:T(128)S(1)} %copy-done.3), channel_id=1, source_target_pairs={{0,16},{1,17},{2,18},{3,19},{4,20},{5,21},{6,22},{7,23},{8,24},{9,... | collective-permute-start | bytes 32 | tf_op jit(solution)/shard_map/ppermute | solution.py:718
  13.5 1.2 copy-start.1
  14.8 0.8 copy-start.6
  14.8 0.9 copy-start.7
  15.0 29.1 %collective-permute-start.2 = (bf16[4,64,1024]{2,1,0:T(8,128)(2,1)S(1)}, bf16[4,64,1024]{2,1,0:T(8,128)(2,1)S(1)}, u32[]{:S(2)}, u32[]{:S(2)}) collective-permute-start(bf16[4,64,1024]{2,1,0:T(8,128)(2,1)S(1)} %get-tuple-element.39), channel_id=1, source_target_pairs={{0,1},{1,0},{2,3},{3,2},{4,5},{5,4},{6,7},{7,6},{8,9},{9,8},{10,11... | collective-permute-start | bytes 1572872 | tf_op jit(solution)/shard_map/ppermute | solution.py:718
  15.6 28.4 %collective-permute-start = (bf16[64,1024]{1,0:T(8,128)(2,1)S(1)}, bf16[64,1024]{1,0:T(8,128)(2,1)S(1)}, u32[]{:S(2)}, u32[]{:S(2)}) collective-permute-start(bf16[64,1024]{1,0:T(8,128)(2,1)S(1)} %constant_dynamic-update-slice_fusion), channel_id=1, source_target_pairs={{0,8},{1,9},{2,10},{3,11},{4,12},{5,13},{6,14},{7,15},{8,0},{9,1},... | collective-permute-start | bytes 393224 | tf_op jit(solution)/shard_map/ppermute | solution.py:718
  18.3 28.0 %copy-start.4 = (s32[16]{0:T(128)S(1)}, s32[16]{0:T(128)}, u32[]{:S(2)}) copy-start(s32[16]{0:T(128)} %owner.5) | copy-start | bytes 196
  48.4 9.2 %collective-permute-start.3 = (bf16[960,128]{1,0:T(8,128)(2,1)S(1)}, bf16[960,128]{1,0:T(8,128)(2,1)S(1)}, u32[]{:S(2)}, u32[]{:S(2)}) collective-permute-start(bf16[960,128]{1,0:T(8,128)(2,1)S(1)} %get-tuple-element.41), channel_id=1, source_target_pairs={{0,16},{1,17},{2,18},{3,19},{4,20},{5,21},{6,22},{7,23},{8,24},{9,... | collective-permute-start | bytes 737288 | tf_op jit(solution)/shard_map/ppermute | solution.py:718
  50.6 20.5 %collective-permute-start.4 = (bf16[960,128]{1,0:T(8,128)(2,1)S(1)}, bf16[960,128]{1,0:T(8,128)(2,1)S(1)}, u32[]{:S(2)}, u32[]{:S(2)}) collective-permute-start(bf16[960,128]{1,0:T(8,128)(2,1)S(1)} %get-tuple-element.43), channel_id=1, source_target_pairs={{0,8},{1,9},{2,10},{3,11},{4,12},{5,13},{6,14},{7,15},{8,0},{9,1},... | collective-permute-start | bytes 737288 | tf_op jit(solution)/shard_map/ppermute | solution.py:718
  51.9 22.5 %collective-permute-start.5 = (bf16[960,128]{1,0:T(8,128)(2,1)S(1)}, bf16[960,128]{1,0:T(8,128)(2,1)S(1)}, u32[]{:S(2)}, u32[]{:S(2)}) collective-permute-start(bf16[960,128]{1,0:T(8,128)(2,1)S(1)} %get-tuple-element.44), channel_id=1, source_target_pairs={{0,24},{1,25},{2,26},{3,27},{4,28},{5,29},{6,30},{7,31},{8,16},{9,... | collective-permute-start | bytes 737288 | tf_op jit(solution)/shard_map/ppermute | solution.py:718
  53.1 22.4 %collective-permute-start.6 = (bf16[2,64,1024]{2,1,0:T(8,128)(2,1)S(1)}, bf16[2,64,1024]{2,1,0:T(8,128)(2,1)S(1)}, u32[]{:S(2)}, u32[]{:S(2)}) collective-permute-start(bf16[2,64,1024]{2,1,0:T(8,128)(2,1)S(1)} %get-tuple-element.48), channel_id=1, source_target_pairs={{0,2},{1,3},{2,0},{3,1},{4,6},{5,7},{6,4},{7,5},{8,10},{9,11},{10,... | collective-permute-start | bytes 786440 | tf_op jit(solution)/shard_map/ppermute | solution.py:718
  54.6 20.8 %collective-permute-start.7 = (bf16[2,64,1024]{2,1,0:T(8,128)(2,1)S(1)}, bf16[2,64,1024]{2,1,0:T(8,128)(2,1)S(1)}, u32[]{:S(2)}, u32[]{:S(2)}) collective-permute-start(bf16[2,64,1024]{2,1,0:T(8,128)(2,1)S(1)} %get-tuple-element.49), channel_id=1, source_target_pairs={{0,4},{1,5},{2,6},{3,7},{4,0},{5,1},{6,2},{7,3},{8,12},{9,13},{10,... | collective-permute-start | bytes 786440 | tf_op jit(solution)/shard_map/ppermute | solution.py:718
  57.7 19.0 %collective-permute-start.8 = (bf16[2,64,1024]{2,1,0:T(8,128)(2,1)S(1)}, bf16[2,64,1024]{2,1,0:T(8,128)(2,1)S(1)}, u32[]{:S(2)}, u32[]{:S(2)}) collective-permute-start(bf16[2,64,1024]{2,1,0:T(8,128)(2,1)S(1)} %get-tuple-element.50), channel_id=1, source_target_pairs={{0,6},{1,7},{2,4},{3,5},{4,2},{5,3},{6,0},{7,1},{8,14},{9,15},{10,... | collective-permute-start | bytes 786440 | tf_op jit(solution)/shard_map/ppermute | solution.py:718
  75.4 13.2 %collective-permute-start.14 = (bf16[2,384,128]{2,1,0:T(8,128)(2,1)S(1)}, bf16[2,384,128]{2,1,0:T(8,128)(2,1)S(1)}, u32[]{:S(2)}, u32[]{:S(2)}) collective-permute-start(bf16[2,384,128]{2,1,0:T(8,128)(2,1)S(1)} %get-tuple-element.57), channel_id=1, source_target_pairs={{0,8},{1,9},{2,10},{3,11},{4,12},{5,13},{6,14},{7,15},{8,0},{9,1},... | collective-permute-start | bytes 589832 | tf_op jit(solution)/shard_map/ppermute | solution.py:718
  77.1 5.0 %collective-permute-start.11 = (bf16[2,64,192]{2,1,0:T(8,128)(2,1)S(1)}, bf16[2,64,192]{2,1,0:T(8,128)(2,1)S(1)}, u32[]{:S(2)}, u32[]{:S(2)}) collective-permute-start(bf16[2,64,192]{2,1,0:T(8,128)(2,1)S(1)} %get-tuple-element.52), channel_id=1, source_target_pairs={{0,2},{1,3},{2,0},{3,1},{4,6},{5,7},{6,4},{7,5},{8,10},{9,11},{10,... | collective-permute-start | bytes 147464 | tf_op jit(solution)/shard_map/ppermute | solution.py:718
  78.7 8.1 %collective-permute-start.12 = (bf16[2,64,192]{2,1,0:T(8,128)(2,1)S(1)}, bf16[2,64,192]{2,1,0:T(8,128)(2,1)S(1)}, u32[]{:S(2)}, u32[]{:S(2)}) collective-permute-start(bf16[2,64,192]{2,1,0:T(8,128)(2,1)S(1)} %get-tuple-element.53), channel_id=1, source_target_pairs={{0,4},{1,5},{2,6},{3,7},{4,0},{5,1},{6,2},{7,3},{8,12},{9,13},{10,... | collective-permute-start | bytes 147464 | tf_op jit(solution)/shard_map/ppermute | solution.py:718
  80.3 8.2 %collective-permute-start.13 = (bf16[2,64,192]{2,1,0:T(8,128)(2,1)S(1)}, bf16[2,64,192]{2,1,0:T(8,128)(2,1)S(1)}, u32[]{:S(2)}, u32[]{:S(2)}) collective-permute-start(bf16[2,64,192]{2,1,0:T(8,128)(2,1)S(1)} %get-tuple-element.54), channel_id=1, source_target_pairs={{0,6},{1,7},{2,4},{3,5},{4,2},{5,3},{6,0},{7,1},{8,14},{9,15},{10,... | collective-permute-start | bytes 147464 | tf_op jit(solution)/shard_map/ppermute | solution.py:718
  80.7 8.4 %collective-permute-start.9 = (bf16[2,64,1024]{2,1,0:T(8,128)(2,1)S(1)}, bf16[2,64,1024]{2,1,0:T(8,128)(2,1)S(1)}, u32[]{:S(2)}, u32[]{:S(2)}) collective-permute-start(bf16[2,64,1024]{2,1,0:T(8,128)(2,1)S(1)} %pad_maximum_fusion.7), channel_id=1, source_target_pairs={{0,2},{1,3},{2,0},{3,1},{4,6},{5,7},{6,4},{7,5},{8,10},{9,11},{10,... | collective-permute-start | bytes 786440 | tf_op jit(solution)/shard_map/ppermute | solution.py:718
  82.2 10.7 %collective-permute-start.10 = (bf16[2,64,1024]{2,1,0:T(8,128)(2,1)S(1)}, bf16[2,64,1024]{2,1,0:T(8,128)(2,1)S(1)}, u32[]{:S(2)}, u32[]{:S(2)}) collective-permute-start(bf16[2,64,1024]{2,1,0:T(8,128)(2,1)S(1)} %pad_maximum_fusion.7), channel_id=1, source_target_pairs={{0,4},{1,5},{2,6},{3,7},{4,0},{5,1},{6,2},{7,3},{8,12},{9,13},{10,... | collective-permute-start | bytes 786440 | tf_op jit(solution)/shard_map/ppermute | solution.py:718
  92.9 1.2 collective-permute-start.15
  92.9 5.2 %collective-permute-start.18 = (bf16[2,192,128]{2,1,0:T(8,128)(2,1)S(1)}, bf16[2,192,128]{2,1,0:T(8,128)(2,1)S(1)}, u32[]{:S(2)}, u32[]{:S(2)}) collective-permute-start(bf16[2,192,128]{2,1,0:T(8,128)(2,1)S(1)} %get-tuple-element.65), channel_id=1, source_target_pairs={{0,4},{1,5},{2,6},{3,7},{4,0},{5,1},{6,2},{7,3},{8,12},{9,13},{10,... | collective-permute-start | bytes 294920 | tf_op jit(solution)/shard_map/ppermute | solution.py:718
  94.2 12.4 %collective-permute-start.16 = (bf16[2,64,1024]{2,1,0:T(8,128)(2,1)S(1)}, bf16[2,64,1024]{2,1,0:T(8,128)(2,1)S(1)}, u32[]{:S(2)}, u32[]{:S(2)}) collective-permute-start(bf16[2,64,1024]{2,1,0:T(8,128)(2,1)S(1)} %collective-permute-done.10), channel_id=1, source_target_pairs={{0,2},{1,3},{2,0},{3,1},{4,6},{5,7},{6,4},{7,5},{8,10},{9,11},{10,... | collective-permute-start | bytes 786440 | tf_op jit(solution)/shard_map/ppermute | solution.py:718
  95.0 4.6 %collective-permute-start.17 = (bf16[64,128]{1,0:T(8,128)(2,1)S(1)}, bf16[64,128]{1,0:T(8,128)(2,1)S(1)}, u32[]{:S(2)}, u32[]{:S(2)}) collective-permute-start(bf16[64,128]{1,0:T(8,128)(2,1)S(1)} %get-tuple-element.87), channel_id=1, source_target_pairs={{0,8},{1,9},{2,10},{3,11},{4,12},{5,13},{6,14},{7,15},{8,0},{9,1},... | collective-permute-start | bytes 49160 | tf_op jit(solution)/shard_map/ppermute | solution.py:718
  99.7 5.8 %collective-permute-start.21 = (bf16[2,64,128]{2,1,0:T(8,128)(2,1)S(1)}, bf16[2,64,128]{2,1,0:T(8,128)(2,1)S(1)}, u32[]{:S(2)}, u32[]{:S(2)}) collective-permute-start(bf16[2,64,128]{2,1,0:T(8,128)(2,1)S(1)} %pad_maximum_fusion.15), channel_id=1, source_target_pairs={{0,6},{1,7},{2,4},{3,5},{4,2},{5,3},{6,0},{7,1},{8,14},{9,15},{10,... | collective-permute-start | bytes 98312 | tf_op jit(solution)/shard_map/ppermute | solution.py:718
  101.1 5.3 %collective-permute-start.20 = (bf16[2,64,128]{2,1,0:T(8,128)(2,1)S(1)}, bf16[2,64,128]{2,1,0:T(8,128)(2,1)S(1)}, u32[]{:S(2)}, u32[]{:S(2)}) collective-permute-start(bf16[2,64,128]{2,1,0:T(8,128)(2,1)S(1)} %pad_maximum_fusion.15), channel_id=1, source_target_pairs={{0,4},{1,5},{2,6},{3,7},{4,0},{5,1},{6,2},{7,3},{8,12},{9,13},{10,... | collective-permute-start | bytes 98312 | tf_op jit(solution)/shard_map/ppermute | solution.py:718
  102.3 4.3 %collective-permute-start.19 = (bf16[2,64,128]{2,1,0:T(8,128)(2,1)S(1)}, bf16[2,64,128]{2,1,0:T(8,128)(2,1)S(1)}, u32[]{:S(2)}, u32[]{:S(2)}) collective-permute-start(bf16[2,64,128]{2,1,0:T(8,128)(2,1)S(1)} %pad_maximum_fusion.15), channel_id=1, source_target_pairs={{0,2},{1,3},{2,0},{3,1},{4,6},{5,7},{6,4},{7,5},{8,10},{9,11},{10,... | collective-permute-start | bytes 98312 | tf_op jit(solution)/shard_map/ppermute | solution.py:718
  103.9 4.7 %collective-permute-start.24 = (bf16[384,128]{1,0:T(8,128)(2,1)S(1)}, bf16[384,128]{1,0:T(8,128)(2,1)S(1)}, u32[]{:S(2)}, u32[]{:S(2)}) collective-permute-start(bf16[384,128]{1,0:T(8,128)(2,1)S(1)} %get-tuple-element.72), channel_id=1, source_target_pairs={{0,16},{1,17},{2,18},{3,19},{4,20},{5,21},{6,22},{7,23},{8,24},{9,... | collective-permute-start | bytes 294920 | tf_op jit(solution)/shard_map/ppermute | solution.py:718
  105.4 5.7 %collective-permute-start.23 = (bf16[2,2,192,128]{3,2,1,0:T(8,128)(2,1)S(1)}, bf16[2,2,192,128]{3,2,1,0:T(8,128)(2,1)S(1)}, u32[]{:S(2)}, u32[]{:S(2)}) collective-permute-start(bf16[2,2,192,128]{3,2,1,0:T(8,128)(2,1)S(1)} %pad_maximum_fusion.12), channel_id=1, source_target_pairs={{0,2},{1,3},{2,0},{3,1},{4,6},{5,7},{6,4},{7,5},{8,10},{9,11},{10,... | collective-permute-start | bytes 589832 | tf_op jit(solution)/shard_map/ppermute | solution.py:718
  106.6 12.0 %copy-start.5 = (bf16[64,4096]{1,0:T(8,128)(2,1)S(1)}, bf16[64,4096]{1,0:T(8,128)(2,1)}, u32[]{:S(2)}) copy-start(bf16[64,4096]{1,0:T(8,128)(2,1)} %query_block.3) | copy-start | bytes 1572868
  106.8 11.9 %collective-permute-start.22 = (bf16[4,2,64,1024]{3,2,1,0:T(8,128)(2,1)S(1)}, bf16[4,2,64,1024]{3,2,1,0:T(8,128)(2,1)S(1)}, u32[]{:S(2)}, u32[]{:S(2)}) collective-permute-start(bf16[4,2,64,1024]{3,2,1,0:T(8,128)(2,1)S(1)} %pad_maximum_fusion.key_same.value_same), channel_id=1, source_target_pairs={{0,1},{1,0},{2,3},{3,2},{4,5},{5,4},{6,7},{7,6},{8,9},{9,8},{10,11... | collective-permute-start | bytes 3145736 | tf_op jit(solution)/shard_map/ppermute | solution.py:718
  111.2 7.4 %collective-permute-start.25 = (bf16[2048,128]{1,0:T(8,128)(2,1)S(1)}, bf16[2048,128]{1,0:T(8,128)(2,1)S(1)}, u32[]{:S(2)}, u32[]{:S(2)}) collective-permute-start(bf16[2048,128]{1,0:T(8,128)(2,1)S(1)} %pad_maximum_fusion.4.rows_same), channel_id=1, source_target_pairs={{0,1},{1,0},{2,3},{3,2},{4,5},{5,4},{6,7},{7,6},{8,9},{9,8},{10,11... | collective-permute-start | bytes 1572872 | tf_op jit(solution)/shard_map/ppermute | solution.py:718
  111.3 7.3 %collective-permute-start.26 = (bf16[2,384,128]{2,1,0:T(8,128)(2,1)S(1)}, bf16[2,384,128]{2,1,0:T(8,128)(2,1)S(1)}, u32[]{:S(2)}, u32[]{:S(2)}) collective-permute-start(bf16[2,384,128]{2,1,0:T(8,128)(2,1)S(1)} %get-tuple-element.85), channel_id=1, source_target_pairs={{0,4},{1,5},{2,6},{3,7},{4,0},{5,1},{6,2},{7,3},{8,12},{9,13},{10,... | collective-permute-start | bytes 589832 | tf_op jit(solution)/shard_map/ppermute | solution.py:718
  121.6 10.7 %collective-permute-start.27 = (bf16[2,2,384,128]{3,2,1,0:T(8,128)(2,1)S(1)}, bf16[2,2,384,128]{3,2,1,0:T(8,128)(2,1)S(1)}, u32[]{:S(2)}, u32[]{:S(2)}) collective-permute-start(bf16[2,2,384,128]{3,2,1,0:T(8,128)(2,1)S(1)} %pad_maximum_fusion.6), channel_id=1, source_target_pairs={{0,2},{1,3},{2,0},{3,1},{4,6},{5,7},{6,4},{7,5},{8,10},{9,11},{10,... | collective-permute-start | bytes 1179656 | tf_op jit(solution)/shard_map/ppermute | solution.py:718
  130.2 4.6 %copy-start.2 = (bf16[64,4096]{1,0:T(8,128)(2,1)S(1)}, bf16[64,4096]{1,0:T(8,128)(2,1)}, u32[]{:S(2)}) copy-start(bf16[64,4096]{1,0:T(8,128)(2,1)} %shard_map.93.attended) | copy-start | bytes 1572868
  132.4 2.4 %collective-permute-start.28 = (bf16[4,2,384,128]{3,2,1,0:T(8,128)(2,1)S(1)}, bf16[4,2,384,128]{3,2,1,0:T(8,128)(2,1)S(1)}, u32[]{:S(2)}, u32[]{:S(2)}) collective-permute-start(bf16[4,2,384,128]{3,2,1,0:T(8,128)(2,1)S(1)} %bitcast.35), channel_id=1, source_target_pairs={{0,1},{1,0},{2,3},{3,2},{4,5},{5,4},{6,7},{7,6},{8,9},{9,8},{10,11... | collective-permute-start | bytes 2359304 | tf_op jit(solution)/shard_map/ppermute | solution.py:718
